TPU v7x, 32 devices: a whole 2x2x4 slice. The times are simulated.
32 devices in a mesh: parts: 2 (over x), owner: 8 (over z, y), split: 2 (over core).
Axes of the slice: x: 2, y: 2, z: 4, core: 2. Of those that a mesh axis runs over, the one named last changes fastest.
Arguments:
- states: bfloat16 [16384, 1024], P(('parts', 'owner', 'split')), parts along dimension 0, may hold values from -6 to 6
- proj_weight: bfloat16 [1024, 768], replicated, may hold values from -0.1875 to 0.1875
- cluster_of: int32 [16384], P(('parts', 'owner', 'split')), parts along dimension 0, may hold values from 0 to 15, as said below
Outputs:
- score: float32 [16384], P(('parts', 'owner', 'split')), parts along dimension 0
There are 2 independent parts, one for each index of `parts`. A program takes and returns all parts, laid end to end along the dimension named above; an argument that names none is the same for every part. Nothing has to cross between parts.
Inputs may be any that keep to these rules, and one draw needn't show every extreme that they name: Call cluster_of // 2 a document's group. Among the 512 documents of one device (aligned blocks in order) at most 192 fall in any one group, and one group, the same for every device of a part, holds exactly 192 of them on every device.
All inputs are finite; a program needn't handle non-finite values. Where the computation divides by a largest or mean magnitude, that divisor is 1e-20 or more.
Results may differ from a plain program's by a relative error of at most 0.0003.
Values may be sent and summed in bfloat16 or wider, within the bound.
No kernel may reach another device: no remote copies, remote signals or barrier semaphores. Data moves between devices by JAX's collectives and lax.ppermute only.
A program may use at most 64 MiB of HBM per device.

v0:
```python
import math

import jax
import jax.numpy as jnp
from jax import lax
from jax.sharding import PartitionSpec as P

CLUS_OWN = 2


TAU = 0.05
THRESH = 0.2
EPS = 1e-06


def prepare(states, proj_weight):
    projected = jnp.dot(states, proj_weight, preferred_element_type=jnp.float32)
    unit = projected * lax.rsqrt(jnp.sum(projected * projected, axis=1, keepdims=True) + EPS)
    peak = jnp.max(jnp.abs(unit), axis=1).astype(jnp.bfloat16)
    quant = (unit / peak.astype(jnp.float32)[:, None]).astype(jnp.bfloat16)
    return (quant, peak)


def similarity_scores(
    own_quant, own_peak, own_cluster, own_index, col_quant, col_peak, col_cluster, col_index
):
    row_count = own_quant.shape[0]
    block = math.gcd(row_count, 768)
    col_scale = col_peak.astype(jnp.float32)

    def one_block(start):
        quant_rows = lax.dynamic_slice_in_dim(own_quant, start, block, 0)
        scale_rows = lax.dynamic_slice_in_dim(own_peak, start, block, 0).astype(jnp.float32)
        cluster_rows = lax.dynamic_slice_in_dim(own_cluster, start, block, 0)
        index_rows = lax.dynamic_slice_in_dim(own_index, start, block, 0)
        inner = lax.dot_general(
            quant_rows, col_quant, (((1,), (1,)), ((), ())), preferred_element_type=jnp.float32
        )
        cosine = inner * scale_rows[:, None] * col_scale[None, :]
        same = (cluster_rows[:, None] == col_cluster[None, :]) & (
            index_rows[:, None] != col_index[None, :]
        )
        weights = jnp.where(same, jnp.exp((cosine - THRESH) / TAU), jnp.zeros_like(cosine))
        return jnp.log(1.0 + jnp.sum(weights, axis=1))

    starts = jnp.arange(row_count // block, dtype=jnp.int32) * block
    return lax.map(one_block, starts).reshape(row_count)


def on_device(states, proj_weight, cluster_of):
    owners = lax.axis_size("owner")
    splits = lax.axis_size("split")
    half_index = lax.axis_index("split")
    doc_count = states.shape[0]
    capacity = 3 * doc_count // owners
    width = proj_weight.shape[1]
    slot_total = owners * capacity
    quant, peak = prepare(states, proj_weight)
    group_of = cluster_of // CLUS_OWN
    onehot = (group_of[:, None] == jnp.arange(owners, dtype=jnp.int32)[None, :]).astype(jnp.int32)
    before = jnp.cumsum(onehot, axis=0) - onehot
    target = group_of * capacity + jnp.sum(before * onehot, axis=1)
    quant_slots = (
        jnp.zeros((slot_total, width), jnp.bfloat16)
        .at[target]
        .set(quant)
        .reshape(owners, capacity, width)
    )
    peak_slots = (
        jnp.zeros((slot_total,), jnp.bfloat16).at[target].set(peak).reshape(owners, capacity)
    )
    cluster_slots = (
        jnp.full((slot_total,), -1, jnp.int32).at[target].set(cluster_of).reshape(owners, capacity)
    )
    positions = (
        jnp.arange(owners, dtype=jnp.int32)[:, None] * (splits * capacity)
        + jnp.arange(capacity, dtype=jnp.int32)[None, :]
    )
    own_index = (positions + half_index * capacity).reshape(slot_total)
    col_index = jnp.arange(splits * slot_total, dtype=jnp.int32)
    pair_quant, pair_peak, pair_cluster = (
        lax.all_gather(quant_slots, "split", axis=1, tiled=True),
        lax.all_gather(peak_slots, "split", axis=1, tiled=True),
        lax.all_gather(cluster_slots, "split", axis=1, tiled=True),
    )
    all_quant, all_peak, all_cluster = (
        lax.all_to_all(pair_quant, "owner", split_axis=0, concat_axis=0, tiled=True),
        lax.all_to_all(pair_peak, "owner", split_axis=0, concat_axis=0, tiled=True),
        lax.all_to_all(pair_cluster, "owner", split_axis=0, concat_axis=0, tiled=True),
    )
    own_quant = lax.dynamic_slice_in_dim(all_quant, half_index * capacity, capacity, 1)
    own_peak = lax.dynamic_slice_in_dim(all_peak, half_index * capacity, capacity, 1)
    own_cluster = lax.dynamic_slice_in_dim(all_cluster, half_index * capacity, capacity, 1)
    scores = similarity_scores(
        own_quant.reshape(slot_total, width),
        own_peak.reshape(slot_total),
        own_cluster.reshape(slot_total),
        own_index,
        all_quant.reshape(splits * slot_total, width),
        all_peak.reshape(splits * slot_total),
        all_cluster.reshape(splits * slot_total),
        col_index,
    )
    returned = lax.all_to_all(
        scores.reshape(owners, capacity), "owner", split_axis=0, concat_axis=0, tiled=True
    )
    return returned.reshape(slot_total)[target]


def solution(mesh):
    placed = (P(("parts", "owner", "split"), None), P(), P(("parts", "owner", "split")))
    return jax.shard_map(
        on_device,
        mesh=mesh,
        in_specs=placed,
        out_specs=P(("parts", "owner", "split")),
        check_vma=False,
    )
```

profile of v0, /device:TPU:0, one launch (start us, length us, event | category | flops | bytes accessed | tf_op | source)
XLA Modules:
  0.0 204.4 jit_solution(2253453384145952799)
XLA Ops:
  6.5 0.8 fusion.21
  7.3 0.7 add_select_fusion
  8.1 2.3 %multiply_reduce_fusion = (f32[512]{0:T(512)S(1)}, f32[512,768]{1,0:T(8,128)S(1)}) fusion(bf16[512,1024]{1,0:T(8,128)(2,1)} %param.5, bf16[1024,768]{1,0:T(8,128)(2,1)S(1)} %copy-done), kind=kOutput, calls=%fused_computation.14 | convolution fusion | flops 806092288 | bytes 4196352 | tf_op jit(solution)/shard_map/dot_general | solution.py:17
  10.4 0.3 abs_reduce_fusion
  10.7 1.1 reduce-window.6
  11.8 0.2 slice_reduce_fusion
  12.1 0.1 fusion.10
  12.2 4.4 %scatter_custom_fusion.1 = bf16[1536,768]{1,0:T(8,128)(2,1)} fusion(s32[512]{0:T(512)S(1)} %compare_select_fusion, bf16[]{:T(256)} %constant.82.clone.1, f32[512,768]{1,0:T(8,128)S(1)} %get-tuple-element.186, f32[512]{0:T(512)S(1)} %convert_element_type.39, f32[512]{0:T(512)S(1)} %add_rsqrt_fusion), kind=kCustom, calls=%fused_computation.15 | custom fusion | flops 1179648 | bytes 3936258 | tf_op jit(solution)/shard_map/scatter | solution.py:66
  16.6 3.8 %scatter_custom_fusion.2 = bf16[1536]{0:T(1024)(128)(2,1)S(1)} fusion(s32[512]{0:T(512)S(1)} %compare_select_fusion, bf16[512]{0:T(512)(128)(2,1)S(1)} %abs_reduce_fusion, bf16[]{:T(256)} %constant.82.clone.1), kind=kCustom, calls=%fused_computation.39 | custom fusion | bytes 3074 | tf_op jit(solution)/shard_map/scatter | solution.py:70
  20.5 1.9 all-gather.1
  22.5 0.5 broadcast.120
  23.0 0.6 reduce.7
  23.7 0.7 reshape.159
  24.4 7.1 %all-to-all-start.2 = ((bf16[8,2,192]{2,1,0:T(2,128)(2,1)}), bf16[8,2,192]{2,1,0:T(2,128)(2,1)S(1)}, u32[]{:S(2)}, u32[]{:S(2)}) async-start(bf16[8,2,192]{2,1,0:T(2,128)(2,1)} %reshape.159), calls=%async_computation.2 | async-start | bytes 16384 | tf_op jit(solution)/shard_map/all_to_all | solution.py:88
  31.5 2.4 %scatter_custom_fusion = s32[1536]{0:T(1024)S(1)} fusion(s32[512]{0:T(512)S(1)} %compare_select_fusion, s32[512]{0:T(512)S(1)} %copy-done.2, s32[]{:T(128)} %constant.84.clone.1), kind=kCustom, calls=%fused_computation.32 | custom fusion | bytes 6148 | tf_op jit(solution)/shard_map/scatter | solution.py:73
  34.0 1.8 all-gather
  35.9 2.1 %all-to-all-done.2 = bf16[8,2,192]{2,1,0:T(2,128)(2,1)S(1)} async-done(((bf16[8,2,192]{2,1,0:T(2,128)(2,1)}), bf16[8,2,192]{2,1,0:T(2,128)(2,1)S(1)}, u32[]{:S(2)}, u32[]{:S(2)}) %all-to-all-start.2) | async-done | bytes 6176 | tf_op jit(solution)/shard_map/all_to_all | solution.py:88
  38.0 10.3 %all_to_all.35 = s32[8,1,384]{2,1,0:T(1,128)S(1)} all-to-all(s32[8,1,384]{2,1,0:T(1,128)S(1)} %copy.8), channel_id=1, replica_groups=mesh['parts'=2,'owner'=8,'split'=2] {'owner'}, dimensions={0} | all-to-all | bytes 24576 | tf_op jit(solution)/shard_map/all_to_all | solution.py:89
  48.3 4.8 %all-to-all-start.1 = ((bf16[8,384,768]{2,1,0:T(8,128)(2,1)}), bf16[8,384,768]{2,1,0:T(8,128)(2,1)}, u32[]{:S(2)}, u32[]{:S(2)}) async-start(bf16[8,384,768]{2,1,0:T(8,128)(2,1)} %all-gather.4.cloned.1.call-done), calls=%async_computation.1 | async-start | bytes 9437184 | tf_op jit(solution)/shard_map/all_to_all | solution.py:87
  53.4 0.1 dynamic-slice_reduce_fusion
  53.6 0.1 dynamic-slice_reduce_fusion.1
  53.8 102.8 %all-to-all-done.1 = bf16[8,384,768]{2,1,0:T(8,128)(2,1)} async-done(((bf16[8,384,768]{2,1,0:T(8,128)(2,1)}), bf16[8,384,768]{2,1,0:T(8,128)(2,1)}, u32[]{:S(2)}, u32[]{:S(2)}) %all-to-all-start.1) | async-done | bytes 4718624 | tf_op jit(solution)/shard_map/all_to_all | solution.py:87
  156.5 3.3 %constant_dynamic-slice_fusion = bf16[8,192,768]{2,1,0:T(8,128)(2,1)} fusion(bf16[8,384,768]{2,1,0:T(8,128)(2,1)} %all-to-all-done.1, s32[]{:T(128)S(6)} %select_n.34), kind=kLoop, calls=%fused_computation.44 | loop fusion | bytes 4718596 | tf_op jit(solution)/shard_map/dynamic_slice | solution.py:91
  159.8 22.6 %while.14 = (s32[]{:T(128)}, f32[2,768]{1,0:T(2,128)S(1)}, s32[2]{0:T(128)S(1)}, s32[1536]{0:T(1024)S(1)}, s32[8,384]{1,0:T(8,128)}, /*index=5*/s32[1536]{0:T(10...) while((s32[]{:T(128)}, f32[2,768]{1,0:T(2,128)S(1)}, ...), condition=%wide.wide.region_10.11_spmd.clone, body=%wide.wide.region_8.10_spmd.clone.sunk | while | flops 3645113088 | bytes 5970631 | solution.py:47
  159.8 0.6 dynamic_slice.66
  162.5 8.4 %select_reduce_fusion.3 = f32[768]{0:T(1024)S(1)} fusion(bf16[3072,768]{1,0:T(8,128)(2,1)} %get-tuple-element.329, f32[3072]{0:T(1024)S(1)} %get-tuple-element.331, f32[768]{0:T(1024)S(1)} %dynamic-slice_convert_fusion.3, s32[768]{0:T(1024)S(1)} %dynamic_slice.67, s32[3072]{0:T(1024)S(1)} %get-tuple-element.332, s32[768]{0:T(1024)S(1)} %dynamic_slice.68, ...), kind=kOutput, calls=%fused_computation.6.clone.clone.1 | convolution fusion | flops 3645111552 | bytes 5935108 | tf_op jit(solution)/shard_map/while/body/eval_jaxpr/dot_general | solution.py:36
  171.1 0.6 dynamic_slice.66
  173.8 8.5 %select_reduce_fusion.3 = f32[768]{0:T(1024)S(1)} fusion(bf16[3072,768]{1,0:T(8,128)(2,1)} %get-tuple-element.329, f32[3072]{0:T(1024)S(1)} %get-tuple-element.331, f32[768]{0:T(1024)S(1)} %dynamic-slice_convert_fusion.3, s32[768]{0:T(1024)S(1)} %dynamic_slice.67, s32[3072]{0:T(1024)S(1)} %get-tuple-element.332, s32[768]{0:T(1024)S(1)} %dynamic_slice.68, ...), kind=kOutput, calls=%fused_computation.6.clone.clone.1 | convolution fusion | flops 3645111552 | bytes 5935108 | tf_op jit(solution)/shard_map/while/body/eval_jaxpr/dot_general | solution.py:36
  182.4 0.7 all_to_all.29
  183.1 3.6 %all-to-all-start.3 = ((f32[8,1,192]{2,1,0:T(1,128)}), f32[8,1,192]{2,1,0:T(1,128)S(1)}, u32[]{:S(2)}, u32[]{:S(2)}) async-start(f32[8,1,192]{2,1,0:T(1,128)} %all_to_all.29), calls=%async_computation.3 | async-start | bytes 16384 | tf_op jit(solution)/shard_map/all_to_all | solution.py:104
  186.7 6.5 %all-to-all-done.3 = f32[8,1,192]{2,1,0:T(1,128)S(1)} async-done(((f32[8,1,192]{2,1,0:T(1,128)}), f32[8,1,192]{2,1,0:T(1,128)S(1)}, u32[]{:S(2)}, u32[]{:S(2)}) %all-to-all-start.3) | async-done | bytes 6176 | tf_op jit(solution)/shard_map/all_to_all | solution.py:104
  193.3 4.3 %gather_fusion = f32[512]{0:T(512)} fusion(f32[1536]{0:T(1024)S(1)} %reshape.107, s32[1024]{0:T(1024)S(1)} %pad_clamp_fusion), kind=kCustom, calls=%fused_computation | custom fusion | bytes 6144 | tf_op jit(solution)/shard_map/gather | solution.py:107
  (48 shorter events, 1.6 us)
Async XLA Ops:
  6.5 1.5 copy-start
  6.5 41.8 %all-gather.4.cloned.1.call-start = ((), (), s32[]{:S(2)}) async-start(), calls=%async_computation.4 | async-start | bytes 7077888 | tf_op jit(solution)/shard_map/all_gather | solution.py:82
  8.0 4.2 %copy-start.2 = (s32[512]{0:T(512)S(1)}, s32[512]{0:T(512)}, u32[]{:S(2)}) copy-start(s32[512]{0:T(512)} %param.7) | copy-start | bytes 6148
  24.4 13.7 %all-to-all-start.2 = ((bf16[8,2,192]{2,1,0:T(2,128)(2,1)}), bf16[8,2,192]{2,1,0:T(2,128)(2,1)S(1)}, u32[]{:S(2)}, u32[]{:S(2)}) async-start(bf16[8,2,192]{2,1,0:T(2,128)(2,1)} %reshape.159), calls=%async_computation.2 | async-start | bytes 16384 | tf_op jit(solution)/shard_map/all_to_all | solution.py:88
  48.3 108.2 %all-to-all-start.1 = ((bf16[8,384,768]{2,1,0:T(8,128)(2,1)}), bf16[8,384,768]{2,1,0:T(8,128)(2,1)}, u32[]{:S(2)}, u32[]{:S(2)}) async-start(bf16[8,384,768]{2,1,0:T(8,128)(2,1)} %all-gather.4.cloned.1.call-done), calls=%async_computation.1 | async-start | bytes 9437184 | tf_op jit(solution)/shard_map/all_to_all | solution.py:87
  53.7 106.0 %copy-start.1 = (s32[8,1,384]{2,0,1:T(8,128)}, s32[8,1,384]{2,0,1:T(8,128)S(1)}, u32[]{:S(2)}) copy-start(s32[8,1,384]{2,0,1:T(8,128)S(1)} %copy.13) | copy-start | bytes 36868
  183.1 10.1 %all-to-all-start.3 = ((f32[8,1,192]{2,1,0:T(1,128)}), f32[8,1,192]{2,1,0:T(1,128)S(1)}, u32[]{:S(2)}, u32[]{:S(2)}) async-start(f32[8,1,192]{2,1,0:T(1,128)} %all_to_all.29), calls=%async_computation.3 | async-start | bytes 16384 | tf_op jit(solution)/shard_map/all_to_all | solution.py:104
Sparse Core Ops, SparseCore 0:
  16.7 17.1 all-gather.3
where the time goes:
time: 205 us; the launch traced here: 204 us
  waiting for transfers between devices  111 us (54%)
  matrix products  19.2 us (9%)
  local copies, waits for them, and re-layouts  18.5 us (9%)
  starting transfers between devices  15.5 us (8%)
  blocking collectives  14 us (7%)
  between operations  13.5 us (7%)
  other arithmetic  8.45 us (4%)
  loops' own time  3.88 us (2%)
    all_to_all x1, waiting for transfers between devices, on_device(): lax.all_to_all(pair_quant, 'owner', split_axis=0, concat_axis=0, tiled=True)  103 us
    dot_general x2, matrix products, one_block(): lax.dot_general(quant_rows, col_quant, (((1,), (1,)), ((), ())), preferre...  16.9 us
    all_to_all x1, blocking collectives, on_device(): lax.all_to_all(pair_cluster, 'owner', split_axis=0, concat_axis=0, tiled=...  10.3 us
    all_to_all x1, starting transfers between devices, on_device(): lax.all_to_all(pair_peak, 'owner', split_axis=0, concat_axis=0, tiled=True)  7.13 us
    all_to_all x1, waiting for transfers between devices, on_device(): lax.all_to_all(scores.reshape(owners, capacity), 'owner', split_axis=0, c...  6.51 us
    all_to_all x1, starting transfers between devices, on_device(): lax.all_to_all(pair_quant, 'owner', split_axis=0, concat_axis=0, tiled=True)  4.77 us
    scatter x1, other arithmetic, on_device(): quant_slots = jnp.zeros((slot_total, width), jnp.bfloat16).at[target].set...  4.36 us
    gather x1, local copies, waits for them, and re-layouts, on_device(): return returned.reshape(slot_total)[target]  4.27 us
  transfers between devices with their start and end apart: 4, of which 3 were waited for; matrix products, arithmetic and copies ran while one was open for 4% of the time, Pallas kernels for 0%

commit v1 on v0

--- a/solution.py
+++ b/solution.py
@@ -3,14 +3,21 @@
 import jax
 import jax.numpy as jnp
 from jax import lax
+from jax.experimental import pallas as pl
+from jax.experimental.pallas import tpu as pltpu
 from jax.sharding import PartitionSpec as P
 
 CLUS_OWN = 2
-
-
 TAU = 0.05
 THRESH = 0.2
 EPS = 1e-06
+LOG2E = math.log2(math.e)
+SCALE = LOG2E / TAU
+SHIFT = THRESH * LOG2E / TAU
+
+ROWS = 2
+F32 = jnp.float32
+BF16 = jnp.bfloat16
 
 
 def prepare(states, proj_weight):
@@ -47,7 +54,7 @@
     return lax.map(one_block, starts).reshape(row_count)
 
 
-def on_device(states, proj_weight, cluster_of):
+def owner_plan(states, proj_weight, cluster_of):
     owners = lax.axis_size("owner")
     splits = lax.axis_size("split")
     half_index = lax.axis_index("split")
@@ -78,19 +85,13 @@
     )
     own_index = (positions + half_index * capacity).reshape(slot_total)
     col_index = jnp.arange(splits * slot_total, dtype=jnp.int32)
-    pair_quant, pair_peak, pair_cluster = (
-        lax.all_gather(quant_slots, "split", axis=1, tiled=True),
-        lax.all_gather(peak_slots, "split", axis=1, tiled=True),
-        lax.all_gather(cluster_slots, "split", axis=1, tiled=True),
+    own_quant, own_peak, own_cluster = (
+        lax.all_to_all(a, "owner", split_axis=0, concat_axis=0, tiled=True)
+        for a in (quant_slots, peak_slots, cluster_slots)
     )
     all_quant, all_peak, all_cluster = (
-        lax.all_to_all(pair_quant, "owner", split_axis=0, concat_axis=0, tiled=True),
-        lax.all_to_all(pair_peak, "owner", split_axis=0, concat_axis=0, tiled=True),
-        lax.all_to_all(pair_cluster, "owner", split_axis=0, concat_axis=0, tiled=True),
-    )
-    own_quant = lax.dynamic_slice_in_dim(all_quant, half_index * capacity, capacity, 1)
-    own_peak = lax.dynamic_slice_in_dim(all_peak, half_index * capacity, capacity, 1)
-    own_cluster = lax.dynamic_slice_in_dim(all_cluster, half_index * capacity, capacity, 1)
+        lax.all_gather(a, "split", axis=1, tiled=True) for a in (own_quant, own_peak, own_cluster)
+    )
     scores = similarity_scores(
         own_quant.reshape(slot_total, width),
         own_peak.reshape(slot_total),
@@ -107,6 +108,282 @@
     return returned.reshape(slot_total)[target]
 
 
+def up(n, m):
+    return -(-n // m) * m
+
+
+def prep_kernel(hot, cl_ref, st_ref, w_ref, h_ref, n_ref, na_ref, nb_ref, meta_ref, slot_ref, quant, peaks):
+    docs = st_ref.shape[0]
+    half = na_ref.shape[0]
+    first = up(hot, 128)
+    lanes = meta_ref.shape[1]
+    tile = 128
+
+    cluster = cl_ref[...]
+    group = cluster // CLUS_OWN
+    kinds = lax.broadcasted_iota(jnp.int32, (8, docs), 0)
+    member = kinds == group
+    count = jnp.sum(member.astype(F32), axis=1, keepdims=True)
+    full = count == float(hot)
+    kind_col = lax.broadcasted_iota(jnp.int32, (8, 1), 0)
+    chosen = jnp.min(jnp.where(full, kind_col, 8), axis=0, keepdims=True)
+    doubt = jnp.where(jnp.sum(full.astype(F32), axis=0, keepdims=True) == 1.0, 0.0, 1.0)
+    in_hot = group == chosen
+
+    for t in range(docs // tile):
+        rows = slice(t * tile, (t + 1) * tile)
+        projected = jnp.dot(st_ref[rows, :], w_ref[...], preferred_element_type=F32)
+        unit = projected * lax.rsqrt(jnp.sum(projected * projected, axis=1, keepdims=True) + EPS)
+        peak = jnp.max(jnp.abs(unit), axis=1, keepdims=True).astype(BF16)
+        quant[rows, :] = (unit / peak.astype(F32)).astype(BF16)
+        peaks[rows, :] = jnp.broadcast_to(peak, (tile, 128))
+
+    ahead = (
+        lax.broadcasted_iota(jnp.int32, (docs, docs), 0) < lax.broadcasted_iota(jnp.int32, (docs, docs), 1)
+    ).astype(F32).astype(BF16)
+    hot_rows = jnp.broadcast_to(in_hot.astype(F32), (8, docs)).astype(BF16)
+    rank = jnp.dot(hot_rows, ahead, preferred_element_type=F32)[0:1, :].astype(jnp.int32)
+    place = lax.broadcasted_iota(jnp.int32, (1, docs), 1)
+    slot = jnp.where(in_hot, rank, first + place - rank)
+    slot_ref[...] = slot
+
+    sort = (lax.broadcasted_iota(jnp.int32, (lanes, docs), 0) == slot).astype(F32).astype(BF16)
+    sorted_h = jnp.dot(sort[:hot, :], quant[...], preferred_element_type=F32).astype(BF16)
+    sorted_n = jnp.dot(sort[first:first + docs - hot, :], quant[...], preferred_element_type=F32).astype(BF16)
+    h_ref[...] = sorted_h
+    n_ref[...] = sorted_n
+    na_ref[...] = sorted_n[:half]
+    nb_ref[...] = sorted_n[half:]
+
+    sorted_peak = jnp.dot(sort, peaks[...], preferred_element_type=F32).T[0:8, :]
+    sorted_cluster = lax.dot_general(
+        jnp.broadcast_to(cluster.astype(F32), (8, docs)).astype(BF16), sort, (((1,), (1,)), ((), ())),
+        preferred_element_type=F32,
+    )
+    field = lax.broadcasted_iota(jnp.int32, (8, lanes), 0)
+    meta_ref[...] = jnp.where(field == 0, sorted_peak, jnp.where(field == 1, sorted_cluster, doubt))
+
+
+def prep(hot, cluster_of, states, proj_weight):
+    docs, width = states.shape[0], proj_weight.shape[1]
+    rest = docs - hot
+    lanes = up(hot, 128) + up(rest, 128)
+    shape = jax.ShapeDtypeStruct
+    return pl.pallas_call(
+        lambda *refs: prep_kernel(hot, *refs),
+        out_shape=(
+            shape((hot, width), BF16),
+            shape((rest, width), BF16),
+            shape((rest // 2, width), BF16),
+            shape((rest // 2, width), BF16),
+            shape((8, lanes), F32),
+            shape((1, docs), jnp.int32),
+        ),
+        scratch_shapes=[pltpu.VMEM((docs, width), BF16), pltpu.VMEM((docs, 128), BF16)],
+        compiler_params=pltpu.CompilerParams(vmem_limit_bytes=48 * 2**20),
+        name="prep",
+    )(cluster_of.reshape(1, docs), states, proj_weight)
+
+
+def weights_of(moving, still, row_meta, still_meta, diagonal):
+    inner = lax.dot_general(moving, still, (((1,), (1,)), ((), ())), preferred_element_type=F32)
+    exponent = inner * (row_meta[:, 0:1] * SCALE) * still_meta[0:1, :] - SHIFT
+    same = row_meta[:, 1:2] == still_meta[1:2, :]
+    if diagonal:
+        same &= lax.broadcasted_iota(jnp.int32, inner.shape, 0) != lax.broadcasted_iota(jnp.int32, inner.shape, 1)
+    return jnp.where(same, jnp.exp2(exponent), 0.0)
+
+
+OWN = 3
+SUMS = 7
+
+
+def score_kernel(plan, geometry, *refs):
+    hot, rest, first, lanes = geometry
+    moving, stills = plan
+    place_ref, meta_ref, before_ref = refs[0:3]
+    at = 3
+    move_refs = refs[at:at + len(moving)]
+    at += len(moving)
+    still_refs = refs[at:at + len(stills)]
+    out_ref = refs[at + len(stills)]
+    out_ref[...] = before_ref[...]
+    z, y, c = place_ref[0], place_ref[1], place_ref[2]
+    columns = lax.axis_size("owner") // ROWS
+    start = {"h": 0, "n": first}
+    size = {"h": hot, "n": rest}
+
+    def device(target):
+        if target < OWN:
+            return ((lax.rem(z + target + 1, columns)) * ROWS + y) * 2 + c
+        other = target - OWN
+        return (z * ROWS + (1 - y if other // 2 else y)) * 2 + (1 - c if other % 2 else c)
+
+    for (kind, row, target, holders, meets), move_ref in zip(moving, move_refs):
+
+        def work(kind=kind, row=row, target=target, meets=meets, move_ref=move_ref):
+            count = move_ref.shape[0]
+            row_meta = meta_ref[device(target)].T[start[kind] + row:start[kind] + row + count, :]
+            total = jnp.zeros((count, 1), F32)
+            for index in meets:
+                still_kind, still_target = stills[index]
+                assert still_kind == kind
+                lane = slice(start[kind], start[kind] + size[kind])
+                weights = weights_of(
+                    move_ref[...], still_refs[index][...], row_meta, meta_ref[device(still_target)][:, lane],
+                    target == OWN and still_target == OWN,
+                )
+                total += jnp.sum(weights, axis=1, keepdims=True)
+                if target != OWN:
+                    out_ref[still_target, :, lane] += jnp.sum(weights, axis=0, keepdims=True)
+            spot = slice(start[kind] + row, start[kind] + row + count)
+            out_ref[target, :, spot] += jnp.broadcast_to(total, (count, 128)).T[0:1, :]
+
+        if holders is None:
+            work()
+        else:
+            held = z == holders[0]
+            for holder in holders[1:]:
+                held |= z == holder
+            pl.when(held)(work)
+
+
+def score(name, geometry, place, meta, before, moving, stills):
+    lanes = geometry[3]
+    plan = ([m[1:] for m in moving], [s[1:] for s in stills])
+    vmem = pl.BlockSpec(memory_space=pltpu.VMEM)
+    pairs = sum(m[0].shape[0] * sum(stills[i][0].shape[0] for i in m[5]) for m in moving)
+    width = moving[0][0].shape[1]
+    return pl.pallas_call(
+        lambda *refs: score_kernel(plan, geometry, *refs),
+        out_shape=jax.ShapeDtypeStruct((SUMS, 1, lanes), F32),
+        in_specs=[pl.BlockSpec(memory_space=pltpu.SMEM)] + [vmem] * (2 + len(moving) + len(stills)),
+        out_specs=vmem,
+        compiler_params=pltpu.CompilerParams(vmem_limit_bytes=48 * 2**20),
+        cost_estimate=pl.CostEstimate(
+            flops=2 * pairs * width, bytes_accessed=4 * 2**20, transcendentals=pairs
+        ),
+        name=name,
+    )(place, meta, before, *[m[0] for m in moving], *[s[0] for s in stills])
+
+
+def finish_kernel(slot_ref, *refs):
+    sums, out_ref = refs[:-1], refs[-1]
+    total = sums[0][...]
+    for ref in sums[1:]:
+        total += ref[...]
+    lanes, docs = total.shape[1], slot_ref.shape[1]
+    values = jnp.broadcast_to(jnp.log(1.0 + total), (8, lanes)).T[:, 0:1]
+    here = lax.broadcasted_iota(jnp.int32, (lanes, docs), 0) == slot_ref[...]
+    out_ref[...] = jnp.sum(jnp.where(here, values, 0.0), axis=0, keepdims=True)
+
+
+def finish(slot, sums):
+    return pl.pallas_call(
+        finish_kernel,
+        out_shape=jax.ShapeDtypeStruct(slot.shape, F32),
+        name="finish",
+    )(slot, *sums)
+
+
+def meeting_plan(states, proj_weight, cluster_of):
+    owners = lax.axis_size("owner")
+    columns = owners // ROWS
+    docs = states.shape[0]
+    hot = 3 * docs // owners
+    rest = docs - hot
+    first = up(hot, 128)
+    geometry = (hot, rest, first, first + up(rest, 128))
+
+    h, n, na, nb, meta, slot = prep(hot, cluster_of, states, proj_weight)
+    metas = lax.all_gather(meta, ("parts", "owner", "split"))
+    parts = lax.axis_size("parts")
+    doubt = jnp.max(metas[:, 2, 0]) > 0.0
+    meta = lax.dynamic_index_in_dim(
+        metas.reshape((parts, metas.shape[0] // parts) + metas.shape[1:]), lax.axis_index("parts"), 0, keepdims=False
+    )
+    owner = lax.axis_index("owner")
+    place = jnp.stack([owner // ROWS, owner % ROWS, lax.axis_index("split")]).astype(jnp.int32)
+
+    def hop(a, sources, step):
+        return lax.ppermute(
+            a, "owner", [(z * ROWS + y, (z + step) * ROWS + y) for z in sources for y in range(ROWS)]
+        )
+
+    def other_row(a):
+        return lax.ppermute(a, "owner", [(i, i ^ 1) for i in range(owners)])
+
+    def other_core(a):
+        return lax.ppermute(a, "split", [(0, 1), (1, 0)])
+
+    left1 = [hop(a, (2, 3), -1) for a in (na, nb)]
+    right1 = hop(h, (0, 1, 2), 1)
+    nc, hc = other_core(n), other_core(h)
+    ny, hy = other_row(n), other_row(h)
+    left2 = [hop(a, (2, 1), -1) for a in left1]
+    right2 = hop(right1, (1, 2), 1)
+    rightn = hop(n, (0,), 1)
+    left3 = [hop(a, (1,), -1) for a in left2]
+    right3 = hop(right2, (2,), 1)
+    nyc, hyc = other_core(ny), other_core(hy)
+
+    near = [(n, "n", 3), (nc, "n", 4), (h, "h", 3), (hc, "h", 4)]
+    far = [(ny, "n", 5), (nyc, "n", 6), (hy, "h", 5), (hyc, "h", 6)]
+    everything = near + far
+
+    sums = jnp.zeros((SUMS, 1, geometry[3]), F32)
+    sums = score(
+        "near", geometry, place, meta, sums,
+        [(n, "n", 0, OWN, None, (0, 1)), (h, "h", 0, OWN, None, (2, 3))],
+        near,
+    )
+    half = rest // 2
+    hop1 = [
+        (left1[0], "n", 0, 0, (1, 2)),
+        (left1[1], "n", half, 0, (1, 2)),
+        (right1, "h", 0, 2, (1, 2, 3)),
+    ]
+    sums = score(
+        "hop1_near", geometry, place, meta, sums, [m + ((0, 1) if m[1] == "n" else (2, 3),) for m in hop1], near
+    )
+    own = [(n, "n", 0, OWN, None), (h, "h", 0, OWN, None)]
+    sums = score(
+        "far", geometry, place, meta, sums, [m + ((0, 1) if m[1] == "n" else (2, 3),) for m in own + hop1], far
+    )
+    hop2 = [
+        (left2[0], "n", 0, 1, (0, 1)),
+        (left2[1], "n", half, 1, (0, 1)),
+        (right2, "h", 0, 1, (2, 3)),
+        (rightn, "n", 0, 2, (1,)),
+    ]
+    every = {"n": (0, 1, 4, 5), "h": (2, 3, 6, 7)}
+    sums = score("hop2", geometry, place, meta, sums, [m + (every[m[1]],) for m in hop2], everything)
+    hop3 = [
+        (left3[0], "n", 0, 2, (0,)),
+        (left3[1], "n", half, 2, (0,)),
+        (right3, "h", 0, 0, (3,)),
+    ]
+    sums = score("hop3", geometry, place, meta, sums, [m + (every[m[1]],) for m in hop3], everything)
+
+    def ahead(a, step):
+        return lax.ppermute(
+            a, "owner",
+            [(z * ROWS + y, (z + step) % columns * ROWS + y) for z in range(columns) for y in range(ROWS)],
+        )
+
+    across = lax.ppermute(sums[6], ("owner", "split"), [(i, i ^ 3) for i in range(2 * owners)])
+    back = [sums[OWN], other_core(sums[4]), other_row(sums[5]), across]
+    back += [ahead(sums[i], i + 1) for i in range(3)]
+    fast = finish(slot, back).reshape(docs)
+    return lax.cond(doubt, owner_plan, lambda *_: fast, states, proj_weight, cluster_of)
+
+
+def on_device(states, proj_weight, cluster_of):
+    if (lax.axis_size("owner"), lax.axis_size("split")) == (8, 2) and states.shape[0] == 512:
+        return meeting_plan(states, proj_weight, cluster_of)
+    return owner_plan(states, proj_weight, cluster_of)
+
+
 def solution(mesh):
     placed = (P(("parts", "owner", "split"), None), P(), P(("parts", "owner", "split")))
     return jax.shard_map(

time: 205 us -> 132 us (0.64)
  waiting for transfers between devices: 111 us -> 24.2 us
  blocking collectives: 14 us -> 47.9 us
  matrix products: 19.2 us -> 0 us
  local copies, waits for them, and re-layouts: 18.5 us -> 3.5 us
  Pallas kernels: 0 us -> 14.3 us
  starting transfers between devices: 15.5 us -> 25.6 us
  other arithmetic: 8.45 us -> 1.65 us
  loops' own time: 3.88 us -> 0.01 us
    all_to_all x3 -> x0, waiting for transfers between devices: 111 us -> none  [the longest x1 103 us: on_device(): lax.all_to_all(pair_quant, 'owner', split_axis=0, concat_axis=0, tiled=True)]
    all_gather x2 -> x1, blocking collectives: 3.74 us -> 47.9 us  [meeting_plan(): metas = lax.all_gather(meta, ('parts', 'owner', 'split'))]
    ppermute x0 -> x22, starting transfers between devices: none -> 25.6 us  [the longest x10 19.6 us: hop(): lax.ppermute(a, 'owner', [(z * ROWS + y, (z + step) * ROWS + y) for z in...]
    ppermute x0 -> x22, waiting for transfers between devices: none -> 24.2 us  [the longest x10 12.4 us: hop(): lax.ppermute(a, 'owner', [(z * ROWS + y, (z + step) * ROWS + y) for z in...]
    dot_general x3 -> x0, matrix products: 19.2 us -> none  [the longest x2 16.9 us: one_block(): lax.dot_general(quant_rows, col_quant, (((1,), (1,)), ((), ())), preferre...]
    all_to_all x3 -> x0, starting transfers between devices: 15.5 us -> none  [the longest x1 7.13 us: on_device(): lax.all_to_all(pair_peak, 'owner', split_axis=0, concat_axis=0, tiled=True)]
    pallas_call x0 -> x7, Pallas kernels: none -> 14.3 us  [the longest x5 9.25 us: score(): pl.pallas_call(lambda *refs: score_kernel(plan, geometry, *refs), out_sha...]
    all_to_all x1 -> x0, blocking collectives: 10.3 us -> none  [on_device(): lax.all_to_all(pair_cluster, 'owner', split_axis=0, concat_axis=0, tiled=...]
  transfers between devices with their start and end apart: 4 -> 22, of which waited for: 3 -> 5; matrix products, arithmetic and copies ran while one was open for 4% -> 2% of each run, Pallas kernels for 0% -> 5%
where the time goes in v1:
time: 132 us; the launch traced here: 131 us
  blocking collectives  47.9 us (36%)
  starting transfers between devices  25.6 us (19%)
  waiting for transfers between devices  24.2 us (18%)
  Pallas kernels  14.3 us (11%)
  between operations  14.3 us (11%)
  local copies, waits for them, and re-layouts  3.5 us (3%)
  other arithmetic  1.65 us (1%)
    all_gather x1, blocking collectives, meeting_plan(): metas = lax.all_gather(meta, ('parts', 'owner', 'split'))  47.9 us
    ppermute x10, starting transfers between devices, hop(): lax.ppermute(a, 'owner', [(z * ROWS + y, (z + step) * ROWS + y) for z in...  19.6 us
    ppermute x10, waiting for transfers between devices, hop(): lax.ppermute(a, 'owner', [(z * ROWS + y, (z + step) * ROWS + y) for z in...  12.4 us
    ppermute x3, waiting for transfers between devices, other_row(): return lax.ppermute(a, 'owner', [(i, i ^ 1) for i in range(owners)])  10.2 us
    pallas_call x5, Pallas kernels, score(): pl.pallas_call(lambda *refs: score_kernel(plan, geometry, *refs), out_sha...  9.25 us
    pallas_call x1, Pallas kernels, prep(): pl.pallas_call(lambda *refs: prep_kernel(hot, *refs), out_shape=(shape((h...  3.83 us
    ppermute x3, starting transfers between devices, other_row(): return lax.ppermute(a, 'owner', [(i, i ^ 1) for i in range(owners)])  3.11 us
  transfers between devices with their start and end apart: 22, of which 5 were waited for; matrix products, arithmetic and copies ran while one was open for 2% of the time, Pallas kernels for 5%

profile of v1, /device:TPU:0, one launch (start us, length us, event | category | flops | bytes accessed | tf_op | source)
XLA Modules:
  0.0 131.4 jit_solution(8638789534184533425)
XLA Ops:
  6.5 3.8 %prep.1 = (bf16[192,768]{1,0:T(8,128)(2,1)S(1)}, bf16[320,768]{1,0:T(8,128)(2,1)S(1)}, bf16[160,768]{1,0:T(8,128)(2,1)S(1)}, bf16[160,768]{1,0:T(8,128)(2,1)S(1)...) custom-call(s32[1,512]{1,0:T(1,128)} %bitcast.57, bf16[512,1024]{1,0:T(8,128)(2,1)} %refs_1_.1, bf16[1024,768]{1,0:T(8,128)(2,1)} %refs_2_.1), custom_call_target="tpu_custom_call" | custom-call | tf_op jit(solution)/shard_map/prep/pallas_call | solution.py:172
  10.4 0.7 collective-permute-start.2
  11.0 0.7 collective-permute-start.3
  11.7 3.0 %collective-permute-start.5 = (bf16[320,768]{1,0:T(8,128)(2,1)S(1)}, bf16[320,768]{1,0:T(8,128)(2,1)S(1)}, u32[]{:S(2)}, u32[]{:S(2)}) collective-permute-start(bf16[320,768]{1,0:T(8,128)(2,1)S(1)} %get-tuple-element.165.refs_3_.refs_5_.refs_6_.refs_7_), channel_id=1, source_target_pairs={{0,2},{2,0},{4,6},{6,4},{8,10},{10,8},{12,14},{14,12},{1,3},{3,1},... | collective-permute-start | bytes 1474568 | tf_op jit(solution)/shard_map/ppermute | solution.py:314
  14.8 5.1 %collective-permute-start.4 = (bf16[192,768]{1,0:T(8,128)(2,1)S(1)}, bf16[192,768]{1,0:T(8,128)(2,1)S(1)}, u32[]{:S(2)}, u32[]{:S(2)}) collective-permute-start(bf16[192,768]{1,0:T(8,128)(2,1)S(1)} %get-tuple-element.166.refs_4_.refs_7_.refs_8_.refs_9_), channel_id=1, source_target_pairs={{0,4},{2,6},{4,8},{6,10},{8,12},{10,14},{1,5},{3,7},{5,9},{7,11},{... | collective-permute-start | bytes 884744 | tf_op jit(solution)/shard_map/ppermute | solution.py:309
  20.1 1.3 collective-permute-start.9
  21.4 0.7 copy-done
  22.1 10.2 %collective-permute-done.7.refs_10_.refs_13_.refs_12_ = bf16[192,768]{1,0:T(8,128)(2,1)S(1)} collective-permute-done((bf16[192,768]{1,0:T(8,128)(2,1)S(1)}, bf16[192,768]{1,0:T(8,128)(2,1)S(1)}, u32[]{:S(2)}, u32[]{:S(2)}) %collective-permute-start.7) | collective-permute-done | bytes 294944 | tf_op jit(solution)/shard_map/ppermute | solution.py:314
  32.3 5.7 %collective-permute-start.12 = (bf16[320,768]{1,0:T(8,128)(2,1)S(1)}, bf16[320,768]{1,0:T(8,128)(2,1)}, u32[]{:S(2)}, u32[]{:S(2)}) collective-permute-start(bf16[320,768]{1,0:T(8,128)(2,1)S(1)} %get-tuple-element.165.refs_3_.refs_5_.refs_6_.refs_7_), channel_id=1, source_target_pairs={{0,4},{2,6},{1,5},{3,7},{16,20},{18,22},{17,21},{19,23}} | collective-permute-start | bytes 1474568 | tf_op jit(solution)/shard_map/ppermute | solution.py:309
  38.3 1.4 %collective-permute-start.11 = (bf16[192,768]{1,0:T(8,128)(2,1)S(1)}, bf16[192,768]{1,0:T(8,128)(2,1)}, u32[]{:S(2)}, u32[]{:S(2)}) collective-permute-start(bf16[192,768]{1,0:T(8,128)(2,1)S(1)} %collective-permute-done.4.refs_5_.refs_7_), channel_id=1, source_target_pairs={{4,8},{6,10},{8,12},{10,14},{5,9},{7,11},{9,13},{11,15},{20,24},{2... | collective-permute-start | bytes 884744 | tf_op jit(solution)/shard_map/ppermute | solution.py:309
  39.9 47.9 %all-gather.2 = f32[256,640]{1,0:T(8,128)} all-gather(f32[8,640]{1,0:T(8,128)S(1)} %get-tuple-element.163), channel_id=4, replica_groups=mesh['parts'=2,'owner'=8,'split'=2] {'parts','owner','split'}, dimensions={0}, use_global_device_ids=true | all-gather | bytes 675840 | tf_op jit(solution)/shard_map/all_gather | solution.py:299
  87.9 1.4 %collective-permute-start.10 = (bf16[160,768]{1,0:T(8,128)(2,1)}, bf16[160,768]{1,0:T(8,128)(2,1)S(1)}, u32[]{:S(2)}, u32[]{:S(2)}) collective-permute-start(bf16[160,768]{1,0:T(8,128)(2,1)} %copy-done.2), channel_id=1, source_target_pairs={{8,4},{10,6},{4,0},{6,2},{9,5},{11,7},{5,1},{7,3},{24,20},{26,22},... | collective-permute-start | bytes 737288 | tf_op jit(solution)/shard_map/ppermute | solution.py:309
  89.4 1.0 dynamic-slice_bitcast_fusion.refs_1_
  90.4 0.7 collective-permute-start.15
  91.1 1.6 %near.1.refs_2_ = f32[7,1,640]{2,1,0:T(1,128)S(1)} custom-call(s32[3]{0:T(128)S(1)} %pad_add_fusion.refs_0_, f32[16,8,640]{2,1,0:T(8,128)S(1)} %dynamic-slice_bitcast_fusion.refs_1_, f32[7,1,640]{2,1,0:T(1,128)S(1)} %broadcast_in_dim.5.refs_2_, bf16[320,768]{1,0:T(8,128)(2,1)S(1)} %get-tuple-element.165.refs_3_.refs_5_.refs_6_.refs_7_, ...), custom_call_target="tpu_custom_call" | custom-call | flops 427819008 | bytes 4194304 | tf_op jit(solution)/shard_map/near/pallas_call | solution.py:257
  92.7 5.6 %collective-permute-done.10.refs_4_ = bf16[160,768]{1,0:T(8,128)(2,1)S(1)} collective-permute-done((bf16[160,768]{1,0:T(8,128)(2,1)}, bf16[160,768]{1,0:T(8,128)(2,1)S(1)}, u32[]{:S(2)}, u32[]{:S(2)}) %collective-permute-start.10) | collective-permute-done | bytes 245792 | tf_op jit(solution)/shard_map/ppermute | solution.py:309
  98.3 1.3 collective-permute-start.13
  99.6 1.3 collective-permute-start.14
  100.9 0.6 hop1_near.1.refs_2_
  101.5 1.6 %far.1.refs_2_ = f32[7,1,640]{2,1,0:T(1,128)S(1)} custom-call(s32[3]{0:T(128)S(1)} %pad_add_fusion.refs_0_, f32[16,8,640]{2,1,0:T(8,128)S(1)} %dynamic-slice_bitcast_fusion.refs_1_, f32[7,1,640]{2,1,0:T(1,128)S(1)} %hop1_near.1.refs_2_, bf16[320,768]{1,0:T(8,128)(2,1)S(1)} %get-tuple-element.165.refs_3_.refs_5_.refs_6_.refs_7_, ...), custom_call_target="tpu_custom_call" | custom-call | flops 855638016 | bytes 4194304 | tf_op jit(solution)/shard_map/far/pallas_call | solution.py:257
  103.1 2.9 %hop2.1.refs_2_ = f32[7,1,640]{2,1,0:T(1,128)S(1)} custom-call(s32[3]{0:T(128)S(1)} %pad_add_fusion.refs_0_, f32[16,8,640]{2,1,0:T(8,128)S(1)} %dynamic-slice_bitcast_fusion.refs_1_, f32[7,1,640]{2,1,0:T(1,128)S(1)} %far.1.refs_2_, bf16[160,768]{1,0:T(8,128)(2,1)S(1)} %copy-done.6, bf16[160,768]{1,0:T(8,128)(2,1)S(1)} %collective-permute-done.10.refs_4_, ...), custom_call_target="tpu_custom_call" | custom-call | flops 1484783616 | bytes 4194304 | tf_op jit(solution)/shard_map/hop2/pallas_call | solution.py:257
  106.1 3.0 %collective-permute-done.13.refs_3_ = bf16[160,768]{1,0:T(8,128)(2,1)S(1)} collective-permute-done((bf16[160,768]{1,0:T(8,128)(2,1)S(1)}, bf16[160,768]{1,0:T(8,128)(2,1)S(1)}, u32[]{:S(2)}, u32[]{:S(2)}) %collective-permute-start.13) | collective-permute-done | bytes 245792 | tf_op jit(solution)/shard_map/ppermute | solution.py:309
  109.1 3.8 %collective-permute-done.14.refs_4_ = bf16[160,768]{1,0:T(8,128)(2,1)S(1)} collective-permute-done((bf16[160,768]{1,0:T(8,128)(2,1)S(1)}, bf16[160,768]{1,0:T(8,128)(2,1)S(1)}, u32[]{:S(2)}, u32[]{:S(2)}) %collective-permute-start.14) | collective-permute-done | bytes 245792 | tf_op jit(solution)/shard_map/ppermute | solution.py:309
  112.9 2.5 %hop3.1 = f32[7,1,640]{2,1,0:T(1,128)S(1)} custom-call(s32[3]{0:T(128)S(1)} %pad_add_fusion.refs_0_, f32[16,8,640]{2,1,0:T(8,128)S(1)} %dynamic-slice_bitcast_fusion.refs_1_, f32[7,1,640]{2,1,0:T(1,128)S(1)} %hop2.1.refs_2_, bf16[160,768]{1,0:T(8,128)(2,1)S(1)} %collective-permute-done.13.refs_3_, bf16[160,768]{1,0:T(8,128)(2,1)S(1)} %collective-permute-done.14.refs_4_, ...), custom_call_target="tpu_custom_call" | custom-call | flops 855638016 | bytes 4194304 | tf_op jit(solution)/shard_map/hop3/pallas_call | solution.py:257
  115.4 0.6 slice_bitcast_fusion
  116.2 1.8 %collective-permute-start.19 = (f32[1,640]{1,0:T(1,128)S(1)}, f32[1,640]{1,0:T(1,128)S(1)}, u32[]{:S(2)}, u32[]{:S(2)}) collective-permute-start(f32[1,640]{1,0:T(1,128)S(1)} %get-tuple-element.246), channel_id=1, source_target_pairs={{0,4},{2,6},{4,8},{6,10},{8,12},{10,14},{12,0},{14,2},{1,5},{3,7},... | collective-permute-start | bytes 7688 | tf_op jit(solution)/shard_map/ppermute | solution.py:369
  118.0 1.6 %collective-permute-done.21.refs_6_ = f32[1,640]{1,0:T(1,128)S(1)} collective-permute-done((f32[1,640]{1,0:T(1,128)S(1)}, f32[1,640]{1,0:T(1,128)S(1)}, u32[]{:S(2)}, u32[]{:S(2)}) %collective-permute-start.21) | collective-permute-done | bytes 2592 | tf_op jit(solution)/shard_map/ppermute | solution.py:369
  119.6 0.3 collective-permute-start.16
  119.9 1.6 %slice_reduce_fusion.1 = f32[]{:T(128)} fusion(f32[32,8,640]{2,1,0:T(8,128)} %bitcast.55), kind=kLoop, calls=%fused_computation.44 | loop fusion | flops 31 | bytes 132 | tf_op jit(solution)/shard_map/reduce_max | solution.py:301
  122.2 0.5 copy-done.12
  122.8 1.2 finish.1
  124.0 0.6 copy-done.17
  (56 shorter events, 1.1 us)
Async XLA Ops:
  10.4 77.5 %copy-start.4 = (s32[1,512]{1,0:T(1,128)}, s32[1,512]{1,0:T(1,128)S(1)}, u32[]{:S(2)}) copy-start(s32[1,512]{1,0:T(1,128)S(1)} %get-tuple-element.164.slot_ref) | copy-start | bytes 6148
  10.4 9.6 %collective-permute-start.2 = (bf16[160,768]{1,0:T(8,128)(2,1)S(1)}, bf16[160,768]{1,0:T(8,128)(2,1)S(1)}, u32[]{:S(2)}, u32[]{:S(2)}) collective-permute-start(bf16[160,768]{1,0:T(8,128)(2,1)S(1)} %get-tuple-element.167), channel_id=1, source_target_pairs={{8,4},{10,6},{12,8},{14,10},{9,5},{11,7},{13,9},{15,11},{24,20},{2... | collective-permute-start | bytes 737288 | tf_op jit(solution)/shard_map/ppermute | solution.py:309
  11.0 9.0 %collective-permute-start.3 = (bf16[160,768]{1,0:T(8,128)(2,1)S(1)}, bf16[160,768]{1,0:T(8,128)(2,1)S(1)}, u32[]{:S(2)}, u32[]{:S(2)}) collective-permute-start(bf16[160,768]{1,0:T(8,128)(2,1)S(1)} %get-tuple-element.168), channel_id=1, source_target_pairs={{8,4},{10,6},{12,8},{14,10},{9,5},{11,7},{13,9},{15,11},{24,20},{2... | collective-permute-start | bytes 737288 | tf_op jit(solution)/shard_map/ppermute | solution.py:309
  11.7 27.9 %collective-permute-start.5 = (bf16[320,768]{1,0:T(8,128)(2,1)S(1)}, bf16[320,768]{1,0:T(8,128)(2,1)S(1)}, u32[]{:S(2)}, u32[]{:S(2)}) collective-permute-start(bf16[320,768]{1,0:T(8,128)(2,1)S(1)} %get-tuple-element.165.refs_3_.refs_5_.refs_6_.refs_7_), channel_id=1, source_target_pairs={{0,2},{2,0},{4,6},{6,4},{8,10},{10,8},{12,14},{14,12},{1,3},{3,1},... | collective-permute-start | bytes 1474568 | tf_op jit(solution)/shard_map/ppermute | solution.py:314
  14.8 17.5 %collective-permute-start.7 = (bf16[192,768]{1,0:T(8,128)(2,1)S(1)}, bf16[192,768]{1,0:T(8,128)(2,1)S(1)}, u32[]{:S(2)}, u32[]{:S(2)}) collective-permute-start(bf16[192,768]{1,0:T(8,128)(2,1)S(1)} %get-tuple-element.166.refs_4_.refs_7_.refs_8_.refs_9_), channel_id=1, source_target_pairs={{0,2},{2,0},{4,6},{6,4},{8,10},{10,8},{12,14},{14,12},{1,3},{3,1},... | collective-permute-start | bytes 884744 | tf_op jit(solution)/shard_map/ppermute | solution.py:314
  14.8 17.5 %collective-permute-start.4 = (bf16[192,768]{1,0:T(8,128)(2,1)S(1)}, bf16[192,768]{1,0:T(8,128)(2,1)S(1)}, u32[]{:S(2)}, u32[]{:S(2)}) collective-permute-start(bf16[192,768]{1,0:T(8,128)(2,1)S(1)} %get-tuple-element.166.refs_4_.refs_7_.refs_8_.refs_9_), channel_id=1, source_target_pairs={{0,4},{2,6},{4,8},{6,10},{8,12},{10,14},{1,5},{3,7},{5,9},{7,11},{... | collective-permute-start | bytes 884744 | tf_op jit(solution)/shard_map/ppermute | solution.py:309
  20.0 18.0 %collective-permute-start.1 = (bf16[192,768]{1,0:T(8,128)(2,1)S(1)}, bf16[192,768]{1,0:T(8,128)(2,1)S(1)}, u32[]{:S(2)}, u32[]{:S(2)}) collective-permute-start(bf16[192,768]{1,0:T(8,128)(2,1)S(1)} %get-tuple-element.166.refs_4_.refs_7_.refs_8_.refs_9_), channel_id=1, source_target_pairs={{0,1},{1,0},{2,3},{3,2},{4,5},{5,4},{6,7},{7,6},{8,9},{9,8},{10,11... | collective-permute-start | bytes 884744 | tf_op jit(solution)/shard_map/ppermute | solution.py:317
  20.1 1.3 copy-start.2
  20.1 18.2 %collective-permute-start.9 = (bf16[160,768]{1,0:T(8,128)(2,1)S(1)}, bf16[160,768]{1,0:T(8,128)(2,1)S(1)}, u32[]{:S(2)}, u32[]{:S(2)}) collective-permute-start(bf16[160,768]{1,0:T(8,128)(2,1)S(1)} %collective-permute-done.2.refs_3_.refs_5_), channel_id=1, source_target_pairs={{8,4},{10,6},{4,0},{6,2},{9,5},{11,7},{5,1},{7,3},{24,20},{26,22},... | collective-permute-start | bytes 737288 | tf_op jit(solution)/shard_map/ppermute | solution.py:309
  21.4 0.7 copy-start
  32.3 55.5 %collective-permute-start = (bf16[320,768]{1,0:T(8,128)(2,1)S(1)}, bf16[320,768]{1,0:T(8,128)(2,1)S(1)}, u32[]{:S(2)}, u32[]{:S(2)}) collective-permute-start(bf16[320,768]{1,0:T(8,128)(2,1)S(1)} %get-tuple-element.165.refs_3_.refs_5_.refs_6_.refs_7_), channel_id=1, source_target_pairs={{0,1},{1,0},{2,3},{3,2},{4,5},{5,4},{6,7},{7,6},{8,9},{9,8},{10,11... | collective-permute-start | bytes 1474568 | tf_op jit(solution)/shard_map/ppermute | solution.py:317
  32.3 70.8 %collective-permute-start.12 = (bf16[320,768]{1,0:T(8,128)(2,1)S(1)}, bf16[320,768]{1,0:T(8,128)(2,1)}, u32[]{:S(2)}, u32[]{:S(2)}) collective-permute-start(bf16[320,768]{1,0:T(8,128)(2,1)S(1)} %get-tuple-element.165.refs_3_.refs_5_.refs_6_.refs_7_), channel_id=1, source_target_pairs={{0,4},{2,6},{1,5},{3,7},{16,20},{18,22},{17,21},{19,23}} | collective-permute-start | bytes 1474568 | tf_op jit(solution)/shard_map/ppermute | solution.py:309
  38.0 61.6 %collective-permute-start.8 = (bf16[192,768]{1,0:T(8,128)(2,1)S(1)}, bf16[192,768]{1,0:T(8,128)(2,1)S(1)}, u32[]{:S(2)}, u32[]{:S(2)}) collective-permute-start(bf16[192,768]{1,0:T(8,128)(2,1)S(1)} %collective-permute-done.7.refs_10_.refs_13_.refs_12_), channel_id=1, source_target_pairs={{0,1},{1,0},{2,3},{3,2},{4,5},{5,4},{6,7},{7,6},{8,9},{9,8},{10,11... | collective-permute-start | bytes 884744 | tf_op jit(solution)/shard_map/ppermute | solution.py:317
  38.3 49.6 %copy-start.5 = (bf16[160,768]{1,0:T(8,128)(2,1)}, bf16[160,768]{1,0:T(8,128)(2,1)S(1)}, u32[]{:S(2)}) copy-start(bf16[160,768]{1,0:T(8,128)(2,1)S(1)} %collective-permute-done.9.refs_3_) | copy-start | bytes 737284
  38.3 52.1 %collective-permute-start.11 = (bf16[192,768]{1,0:T(8,128)(2,1)S(1)}, bf16[192,768]{1,0:T(8,128)(2,1)}, u32[]{:S(2)}, u32[]{:S(2)}) collective-permute-start(bf16[192,768]{1,0:T(8,128)(2,1)S(1)} %collective-permute-done.4.refs_5_.refs_7_), channel_id=1, source_target_pairs={{4,8},{6,10},{8,12},{10,14},{5,9},{7,11},{9,13},{11,15},{20,24},{2... | collective-permute-start | bytes 884744 | tf_op jit(solution)/shard_map/ppermute | solution.py:309
  39.7 61.8 %collective-permute-start.6 = (bf16[320,768]{1,0:T(8,128)(2,1)S(1)}, bf16[320,768]{1,0:T(8,128)(2,1)S(1)}, u32[]{:S(2)}, u32[]{:S(2)}) collective-permute-start(bf16[320,768]{1,0:T(8,128)(2,1)S(1)} %collective-permute-done.5.refs_8_.refs_11_.refs_10_), channel_id=1, source_target_pairs={{0,1},{1,0},{2,3},{3,2},{4,5},{5,4},{6,7},{7,6},{8,9},{9,8},{10,11... | collective-permute-start | bytes 1474568 | tf_op jit(solution)/shard_map/ppermute | solution.py:317
  87.8 10.5 %copy-start.6 = (bf16[160,768]{1,0:T(8,128)(2,1)S(1)}, bf16[160,768]{1,0:T(8,128)(2,1)}, u32[]{:S(2)}) copy-start(bf16[160,768]{1,0:T(8,128)(2,1)} %copy-done.5) | copy-start | bytes 737284
  87.8 13.1 %copy-start.1 = (bf16[160,768]{1,0:T(8,128)(2,1)S(1)}, bf16[160,768]{1,0:T(8,128)(2,1)}, u32[]{:S(2)}) copy-start(bf16[160,768]{1,0:T(8,128)(2,1)} %copy-done) | copy-start | bytes 737284
  87.8 13.1 %copy-start.3 = (bf16[160,768]{1,0:T(8,128)(2,1)S(1)}, bf16[160,768]{1,0:T(8,128)(2,1)}, u32[]{:S(2)}) copy-start(bf16[160,768]{1,0:T(8,128)(2,1)} %copy-done.2) | copy-start | bytes 737284
  87.9 10.4 %collective-permute-start.10 = (bf16[160,768]{1,0:T(8,128)(2,1)}, bf16[160,768]{1,0:T(8,128)(2,1)S(1)}, u32[]{:S(2)}, u32[]{:S(2)}) collective-permute-start(bf16[160,768]{1,0:T(8,128)(2,1)} %copy-done.2), channel_id=1, source_target_pairs={{8,4},{10,6},{4,0},{6,2},{9,5},{11,7},{5,1},{7,3},{24,20},{26,22},... | collective-permute-start | bytes 737288 | tf_op jit(solution)/shard_map/ppermute | solution.py:309
  90.4 22.5 %collective-permute-start.15 = (bf16[192,768]{1,0:T(8,128)(2,1)}, bf16[192,768]{1,0:T(8,128)(2,1)S(1)}, u32[]{:S(2)}, u32[]{:S(2)}) collective-permute-start(bf16[192,768]{1,0:T(8,128)(2,1)} %collective-permute-done.11.refs_5_), channel_id=1, source_target_pairs={{8,12},{10,14},{9,13},{11,15},{24,28},{26,30},{25,29},{27,31}} | collective-permute-start | bytes 884744 | tf_op jit(solution)/shard_map/ppermute | solution.py:309
  98.3 10.8 %collective-permute-start.13 = (bf16[160,768]{1,0:T(8,128)(2,1)S(1)}, bf16[160,768]{1,0:T(8,128)(2,1)S(1)}, u32[]{:S(2)}, u32[]{:S(2)}) collective-permute-start(bf16[160,768]{1,0:T(8,128)(2,1)S(1)} %copy-done.6), channel_id=1, source_target_pairs={{4,0},{6,2},{5,1},{7,3},{20,16},{22,18},{21,17},{23,19}} | collective-permute-start | bytes 737288 | tf_op jit(solution)/shard_map/ppermute | solution.py:309
  99.6 13.3 %collective-permute-start.14 = (bf16[160,768]{1,0:T(8,128)(2,1)S(1)}, bf16[160,768]{1,0:T(8,128)(2,1)S(1)}, u32[]{:S(2)}, u32[]{:S(2)}) collective-permute-start(bf16[160,768]{1,0:T(8,128)(2,1)S(1)} %collective-permute-done.10.refs_4_), channel_id=1, source_target_pairs={{4,0},{6,2},{5,1},{7,3},{20,16},{22,18},{21,17},{23,19}} | collective-permute-start | bytes 737288 | tf_op jit(solution)/shard_map/ppermute | solution.py:309
  106.1 16.7 %copy-start.10 = (s32[512]{0:T(512)S(1)}, s32[512]{0:T(512)}, u32[]{:S(2)}) copy-start(s32[512]{0:T(512)} %param.9) | copy-start | bytes 6148
  116.0 3.6 %collective-permute-start.21 = (f32[1,640]{1,0:T(1,128)S(1)}, f32[1,640]{1,0:T(1,128)S(1)}, u32[]{:S(2)}, u32[]{:S(2)}) collective-permute-start(f32[1,640]{1,0:T(1,128)S(1)} %get-tuple-element.244), channel_id=1, source_target_pairs={{0,12},{2,14},{4,0},{6,2},{8,4},{10,6},{12,8},{14,10},{1,13},{3,15... | collective-permute-start | bytes 7688 | tf_op jit(solution)/shard_map/ppermute | solution.py:369
  116.0 6.1 %collective-permute-start.20 = (f32[1,640]{1,0:T(1,128)S(1)}, f32[1,640]{1,0:T(1,128)S(1)}, u32[]{:S(2)}, u32[]{:S(2)}) collective-permute-start(f32[1,640]{1,0:T(1,128)S(1)} %get-tuple-element.245), channel_id=1, source_target_pairs={{0,8},{2,10},{4,12},{6,14},{8,0},{10,2},{12,4},{14,6},{1,9},{3,11}... | collective-permute-start | bytes 7688 | tf_op jit(solution)/shard_map/ppermute | solution.py:369
  116.2 5.9 %collective-permute-start.19 = (f32[1,640]{1,0:T(1,128)S(1)}, f32[1,640]{1,0:T(1,128)S(1)}, u32[]{:S(2)}, u32[]{:S(2)}) collective-permute-start(f32[1,640]{1,0:T(1,128)S(1)} %get-tuple-element.246), channel_id=1, source_target_pairs={{0,4},{2,6},{4,8},{6,10},{8,12},{10,14},{12,0},{14,2},{1,5},{3,7},... | collective-permute-start | bytes 7688 | tf_op jit(solution)/shard_map/ppermute | solution.py:369
  118.0 4.1 %collective-permute-start.18 = (f32[1,640]{1,0:T(1,128)S(1)}, f32[1,640]{1,0:T(1,128)S(1)}, u32[]{:S(2)}, u32[]{:S(2)}) collective-permute-start(f32[1,640]{1,0:T(1,128)S(1)} %get-tuple-element.247), channel_id=1, source_target_pairs={{0,3},{1,2},{2,1},{3,0},{4,7},{5,6},{6,5},{7,4},{8,11},{9,10},{10,... | collective-permute-start | bytes 7688 | tf_op jit(solution)/shard_map/ppermute | solution.py:374
  118.0 4.1 %collective-permute-start.17 = (f32[1,640]{1,0:T(1,128)S(1)}, f32[1,640]{1,0:T(1,128)S(1)}, u32[]{:S(2)}, u32[]{:S(2)}) collective-permute-start(f32[1,640]{1,0:T(1,128)S(1)} %get-tuple-element.248), channel_id=1, source_target_pairs={{0,2},{2,0},{4,6},{6,4},{8,10},{10,8},{12,14},{14,12},{1,3},{3,1},... | collective-permute-start | bytes 7688 | tf_op jit(solution)/shard_map/ppermute | solution.py:314
  119.6 2.6 %copy-start.11 = (f32[1,640]{1,0:T(1,128)}, f32[1,640]{1,0:T(1,128)S(1)}, u32[]{:S(2)}) copy-start(f32[1,640]{1,0:T(1,128)S(1)} %collective-permute-done.21.refs_6_) | copy-start | bytes 7684
  119.6 2.6 %collective-permute-start.16 = (f32[1,640]{1,0:T(1,128)S(1)}, f32[1,640]{1,0:T(1,128)S(1)}, u32[]{:S(2)}, u32[]{:S(2)}) collective-permute-start(f32[1,640]{1,0:T(1,128)S(1)} %get-tuple-element.249), channel_id=1, source_target_pairs={{0,1},{1,0},{2,3},{3,2},{4,5},{5,4},{6,7},{7,6},{8,9},{9,8},{10,11... | collective-permute-start | bytes 7688 | tf_op jit(solution)/shard_map/ppermute | solution.py:317
  122.2 0.6 copy-start.15
  (5 other events, 2.9 us)

commit v2 on v0

--- a/solution.py
+++ b/solution.py
@@ -3,14 +3,21 @@
 import jax
 import jax.numpy as jnp
 from jax import lax
+from jax.experimental import pallas as pl
+from jax.experimental.pallas import tpu as pltpu
 from jax.sharding import PartitionSpec as P
 
 CLUS_OWN = 2
-
-
 TAU = 0.05
 THRESH = 0.2
 EPS = 1e-06
+LOG2E = math.log2(math.e)
+SCALE = LOG2E / TAU
+SHIFT = THRESH * LOG2E / TAU
+
+ROWS = 2
+F32 = jnp.float32
+BF16 = jnp.bfloat16
 
 
 def prepare(states, proj_weight):
@@ -47,7 +54,7 @@
     return lax.map(one_block, starts).reshape(row_count)
 
 
-def on_device(states, proj_weight, cluster_of):
+def owner_plan(states, proj_weight, cluster_of):
     owners = lax.axis_size("owner")
     splits = lax.axis_size("split")
     half_index = lax.axis_index("split")
@@ -78,19 +85,13 @@
     )
     own_index = (positions + half_index * capacity).reshape(slot_total)
     col_index = jnp.arange(splits * slot_total, dtype=jnp.int32)
-    pair_quant, pair_peak, pair_cluster = (
-        lax.all_gather(quant_slots, "split", axis=1, tiled=True),
-        lax.all_gather(peak_slots, "split", axis=1, tiled=True),
-        lax.all_gather(cluster_slots, "split", axis=1, tiled=True),
+    own_quant, own_peak, own_cluster = (
+        lax.all_to_all(a, "owner", split_axis=0, concat_axis=0, tiled=True)
+        for a in (quant_slots, peak_slots, cluster_slots)
     )
     all_quant, all_peak, all_cluster = (
-        lax.all_to_all(pair_quant, "owner", split_axis=0, concat_axis=0, tiled=True),
-        lax.all_to_all(pair_peak, "owner", split_axis=0, concat_axis=0, tiled=True),
-        lax.all_to_all(pair_cluster, "owner", split_axis=0, concat_axis=0, tiled=True),
-    )
-    own_quant = lax.dynamic_slice_in_dim(all_quant, half_index * capacity, capacity, 1)
-    own_peak = lax.dynamic_slice_in_dim(all_peak, half_index * capacity, capacity, 1)
-    own_cluster = lax.dynamic_slice_in_dim(all_cluster, half_index * capacity, capacity, 1)
+        lax.all_gather(a, "split", axis=1, tiled=True) for a in (own_quant, own_peak, own_cluster)
+    )
     scores = similarity_scores(
         own_quant.reshape(slot_total, width),
         own_peak.reshape(slot_total),
@@ -107,6 +108,287 @@
     return returned.reshape(slot_total)[target]
 
 
+def up(n, m):
+    return -(-n // m) * m
+
+
+META = 16
+
+
+def layout(docs, hot):
+    rest = docs - hot
+    first = up(rest, 128)
+    flag = first + hot
+    return rest, first, flag, up(flag + 1, 128)
+
+
+def prep_kernel(hot, cl_ref, st_ref, w_ref, q_ref, n_ref, na_ref, nb_ref, h_ref, slot_ref, vectors):
+    docs = st_ref.shape[0]
+    rest, first, flag, lanes = layout(docs, hot)
+    half = rest // 2
+    tile = 128
+
+    cluster = cl_ref[...]
+    group = cluster // CLUS_OWN
+    member = lax.broadcasted_iota(jnp.int32, (8, docs), 0) == group
+    full = jnp.sum(member.astype(F32), axis=1, keepdims=True) == float(hot)
+    chosen = jnp.min(
+        jnp.where(full, lax.broadcasted_iota(jnp.int32, (8, 1), 0), 8), axis=0, keepdims=True
+    )
+    doubt = jnp.where(jnp.sum(full.astype(F32), axis=0, keepdims=True) == 1.0, 0.0, 1.0)
+    in_hot = group == chosen
+
+    for t in range(docs // tile):
+        rows = slice(t * tile, (t + 1) * tile)
+        projected = jnp.dot(st_ref[rows, :], w_ref[...], preferred_element_type=F32)
+        norm = lax.rsqrt(jnp.sum(projected * projected, axis=1, keepdims=True) + EPS)
+        vectors[rows, :] = (projected * (norm * math.sqrt(SCALE))).astype(BF16)
+
+    ahead = (
+        lax.broadcasted_iota(jnp.int32, (docs, docs), 0) < lax.broadcasted_iota(jnp.int32, (docs, docs), 1)
+    ).astype(F32).astype(BF16)
+    hot_rows = jnp.broadcast_to(in_hot.astype(F32), (8, docs)).astype(BF16)
+    rank = jnp.dot(hot_rows, ahead, preferred_element_type=F32)[0:1, :].astype(jnp.int32)
+    place = lax.broadcasted_iota(jnp.int32, (1, docs), 1)
+    slot = jnp.where(in_hot, first + rank, place - rank)
+    slot_ref[...] = slot
+
+    sort = (lax.broadcasted_iota(jnp.int32, (lanes, docs), 0) == slot).astype(F32).astype(BF16)
+    cluster_rows = jnp.broadcast_to(cluster.astype(F32), (META, docs)).astype(BF16)
+    sorted_n = jnp.dot(sort[:rest, :], vectors[...], preferred_element_type=F32).astype(BF16)
+    sorted_h = jnp.dot(sort[first:flag, :], vectors[...], preferred_element_type=F32).astype(BF16)
+
+    def meta(ref, row, start, stop):
+        ids = lax.dot_general(
+            cluster_rows, sort[start:stop, :], (((1,), (1,)), ((), ())), preferred_element_type=F32
+        )
+        spot = lax.broadcasted_iota(jnp.int32, ids.shape, 1) + start
+        ids = jnp.where(spot == flag, doubt, ids)
+        ref[row:row + META, :] = jnp.zeros((META, ref.shape[1]), BF16)
+        ref[row:row + META, 0:stop - start] = ids.astype(BF16)
+
+    q_ref[:rest, :] = sorted_n
+    q_ref[rest:docs, :] = sorted_h
+    meta(q_ref, docs, 0, lanes)
+    n_ref[:rest, :] = sorted_n
+    meta(n_ref, rest, 0, rest)
+    na_ref[:half, :] = sorted_n[:half]
+    meta(na_ref, half, 0, half)
+    nb_ref[:half, :] = sorted_n[half:]
+    meta(nb_ref, half, half, rest)
+    h_ref[:hot, :] = sorted_h
+    meta(h_ref, hot, first, flag)
+
+
+def prep(hot, cluster_of, states, proj_weight):
+    docs, width = states.shape[0], proj_weight.shape[1]
+    rest = docs - hot
+    shape = jax.ShapeDtypeStruct
+    blocks = (docs, rest, rest // 2, rest // 2, hot)
+    return pl.pallas_call(
+        lambda *refs: prep_kernel(hot, *refs),
+        out_shape=tuple(shape((b + META, width), BF16) for b in blocks) + (shape((1, docs), jnp.int32),),
+        scratch_shapes=[pltpu.VMEM((docs, width), BF16)],
+        compiler_params=pltpu.CompilerParams(vmem_limit_bytes=48 * 2**20),
+        name="prep",
+    )(cluster_of.reshape(1, docs), states, proj_weight)
+
+
+OWN = 3
+SUMS = 7
+
+
+def score_kernel(plan, docs, hot, carries, flags, outs, *refs):
+    moving, stills = plan
+    rest, first, flag, lanes = layout(docs, hot)
+    place_ref, refs = refs[0], refs[1:]
+    before, refs = refs[:carries], refs[carries:]
+    move_refs, refs = refs[:len(moving)], refs[len(moving):]
+    still_refs, out_refs = refs[:len(stills)], dict(zip(outs, refs[len(stills):]))
+    z = place_ref[0]
+    for k, target in enumerate(outs):
+        out_refs[target][...] = before[k][...] if carries else jnp.zeros((1, lanes), F32)
+    metas = [ref[docs:docs + META, :].astype(F32)[0:1, :] for ref in still_refs]
+    span = {"n": (0, slice(0, rest), slice(0, rest)), "h": (first, slice(rest, docs), slice(first, flag))}
+
+    for (kind, row, target, holders, meets), move_ref in zip(moving, move_refs):
+
+        def work(kind=kind, row=row, target=target, meets=meets, move_ref=move_ref):
+            start, rows, lane = span[kind]
+            if target == OWN:
+                count = rows.stop - rows.start
+                block = move_ref[rows, :]
+                ids = move_ref[docs:docs + META, :].astype(F32)[0:8, lane]
+            else:
+                count = move_ref.shape[0] - META
+                block = move_ref[:count, :]
+                ids = move_ref[count:count + META, :].astype(F32)[0:8, 0:count]
+            ids = ids.T[:, 0:1]
+            total = jnp.zeros((count, 1), F32)
+            for index in meets:
+                inner = lax.dot_general(
+                    block, still_refs[index][rows, :], (((1,), (1,)), ((), ())), preferred_element_type=F32
+                )
+                same = ids == metas[index][:, lane]
+                if target == OWN and stills[index] == OWN:
+                    same &= lax.broadcasted_iota(jnp.int32, inner.shape, 0) != lax.broadcasted_iota(
+                        jnp.int32, inner.shape, 1
+                    )
+                weights = jnp.where(same, jnp.exp2(inner), 0.0)
+                total += jnp.sum(weights, axis=1, keepdims=True)
+                if target != OWN:
+                    out_refs[stills[index]][:, lane] += jnp.sum(weights, axis=0, keepdims=True)
+            spot = slice(start + row, start + row + count)
+            out_refs[target][:, spot] += jnp.broadcast_to(total, (count, 128)).T[0:1, :]
+
+        if holders is None:
+            work()
+        else:
+            held = z == holders[0]
+            for holder in holders[1:]:
+                held |= z == holder
+            pl.when(held)(work)
+
+    if flags:
+        doubt = metas[0]
+        for other in metas[1:]:
+            doubt = doubt + other
+        spot = lax.broadcasted_iota(jnp.int32, (1, lanes), 1)
+        for target in range(OWN + 1):
+            out_refs[target][...] += jnp.where(spot == flag, doubt[:, :lanes], 0.0)
+
+
+def score(name, docs, hot, place, before, moving, stills, flags=False, outs=tuple(range(SUMS))):
+    lanes = layout(docs, hot)[3]
+    plan = ([m[1:] for m in moving], [s[1] for s in stills])
+    vmem = pl.BlockSpec(memory_space=pltpu.VMEM)
+    pairs = sum(m[0].shape[0] * len(m[5]) * (hot if m[1] == "h" else docs - hot) for m in moving)
+    arrays = [*before, *(m[0] for m in moving), *(s[0] for s in stills)]
+    return pl.pallas_call(
+        lambda *refs: score_kernel(plan, docs, hot, len(before), flags, outs, *refs),
+        out_shape=tuple(jax.ShapeDtypeStruct((1, lanes), F32) for _ in outs),
+        in_specs=[pl.BlockSpec(memory_space=pltpu.SMEM)] + [vmem] * len(arrays),
+        out_specs=tuple(vmem for _ in outs),
+        compiler_params=pltpu.CompilerParams(vmem_limit_bytes=48 * 2**20),
+        cost_estimate=pl.CostEstimate(
+            flops=pairs, bytes_accessed=2**10, transcendentals=0
+        ),
+        name=name,
+    )(place, *arrays)
+
+
+def finish_kernel(flag, slot_ref, *refs):
+    sums, out_ref, doubt_ref = refs[:-2], refs[-2], refs[-1]
+    total = sums[0][...]
+    for ref in sums[1:]:
+        total += ref[...]
+    lanes, docs = total.shape[1], slot_ref.shape[1]
+    doubt_ref[...] = (total[:, flag:flag + 1] > 0.0).astype(jnp.int32)
+    values = jnp.broadcast_to(jnp.log(1.0 + total * 2.0**-SHIFT), (8, lanes)).T[:, 0:1]
+    here = lax.broadcasted_iota(jnp.int32, (lanes, docs), 0) == slot_ref[...]
+    out_ref[...] = jnp.sum(jnp.where(here, values, 0.0), axis=0, keepdims=True)
+
+
+def finish(flag, slot, sums):
+    return pl.pallas_call(
+        lambda *refs: finish_kernel(flag, *refs),
+        out_shape=(jax.ShapeDtypeStruct(slot.shape, F32), jax.ShapeDtypeStruct((1, 1), jnp.int32)),
+        name="finish",
+    )(slot, *sums)
+
+
+def meeting_plan(states, proj_weight, cluster_of):
+    owners = lax.axis_size("owner")
+    columns = owners // ROWS
+    docs = states.shape[0]
+    hot = 3 * docs // owners
+    rest = docs - hot
+    half = rest // 2
+    flag = layout(docs, hot)[2]
+
+    q, n, na, nb, h, slot = prep(hot, cluster_of, states, proj_weight)
+    owner = lax.axis_index("owner")
+    place = (owner // ROWS).astype(jnp.int32).reshape(1)
+
+    def hop(a, sources, step):
+        return lax.ppermute(
+            a, "owner", [(z * ROWS + y, (z + step) * ROWS + y) for z in sources for y in range(ROWS)]
+        )
+
+    def other_row(a):
+        return lax.ppermute(a, "owner", [(i, i ^ 1) for i in range(owners)])
+
+    def other_core(a):
+        return lax.ppermute(a, "split", [(0, 1), (1, 0)])
+
+    def across(a):
+        return lax.ppermute(a, ("owner", "split"), [(i, i ^ 3) for i in range(2 * owners)])
+
+    def ahead(a, step):
+        return lax.ppermute(
+            a, "owner",
+            [(z * ROWS + y, (z + step) % columns * ROWS + y) for z in range(columns) for y in range(ROWS)],
+        )
+
+    def after(a, *others):
+        return lax.optimization_barrier((a, *others))[0]
+
+    left1 = [hop(a, (2, 3), -1) for a in (na, nb)]
+    right1 = hop(h, (0, 1, 2), 1)
+    qy = other_row(q)
+    qc = other_core(q)
+    near = [(q, 3), (qc, 4)]
+    own = [(q, "n", 0, OWN, None), (q, "h", 0, OWN, None)]
+    def meet(name, before, moving, stills, **options):
+        every = tuple(range(len(stills)))
+        return score(name, docs, hot, place, before, [m + (every,) for m in moving], stills, **options)
+
+    sums = meet("near", (), own, near)
+
+    left2 = [hop(after(left1[0], sums[0]), (2, 1), -1)]
+    left2 += [hop(after(left1[1], left1[0]), (2, 1), -1)]
+    right2 = hop(after(right1, left1[1]), (1, 2), 1)
+    rightn = hop(n, (0,), 1)
+    hop1 = [
+        (left1[0], "n", 0, 0, (1, 2)),
+        (left1[1], "n", half, 0, (1, 2)),
+        (right1, "h", 0, 2, (1, 2, 3)),
+    ]
+    sums = meet("hop1_near", sums, hop1, near)
+
+    left3 = [hop(after(left2[0], sums[0]), (1,), -1)]
+    qy = after(qy, left2[0])
+    qyc = other_core(qy)
+    left3 += [hop(after(left2[1], qy), (1,), -1)]
+    right3 = hop(after(right2, left2[1]), (2,), 1)
+    far = [(qy, 5), (qyc, 6)]
+    sums = meet("far", sums, own + hop1, far)
+    hop2 = [
+        (left2[0], "n", 0, 1, (0, 1)),
+        (left2[1], "n", half, 1, (0, 1)),
+        (right2, "h", 0, 1, (2, 3)),
+        (rightn, "n", 0, 2, (1,)),
+    ]
+    sums = meet("hop2", sums, hop2, near + far)
+    hop3 = [(left3[0], "n", 0, 2, (0,)), (right3, "h", 0, 0, (3,))]
+    early = meet("hop3", sums, hop3, near + far, flags=True)
+    back = [early[OWN], other_core(early[4]), other_row(early[5]), across(early[6])]
+    back += [ahead(early[i], i + 1) for i in range(3)]
+    last = [(after(left3[1], *back), "n", half, 2, (0,))]
+    late = meet("last", (), last, near + far, outs=(2, 3, 4, 5, 6))
+    back += [hop(late[0], (0,), 3), late[1], other_core(late[2]), other_row(late[3]), across(late[4])]
+    fast, doubt = finish(flag, slot, back)
+    return lax.cond(
+        doubt[0, 0] > 0, owner_plan, lambda *_: fast.reshape(docs), states, proj_weight, cluster_of
+    )
+
+
+def on_device(states, proj_weight, cluster_of):
+    if (lax.axis_size("owner"), lax.axis_size("split")) == (8, 2) and states.shape[0] == 512:
+        return meeting_plan(states, proj_weight, cluster_of)
+    return owner_plan(states, proj_weight, cluster_of)
+
+
 def solution(mesh):
     placed = (P(("parts", "owner", "split"), None), P(), P(("parts", "owner", "split")))
     return jax.shard_map(

time: 205 us -> 92 us (0.45)
  waiting for transfers between devices: 111 us -> 17.7 us
  starting transfers between devices: 15.5 us -> 44.9 us
  matrix products: 19.2 us -> 0 us
  local copies, waits for them, and re-layouts: 18.5 us -> 3.03 us
  blocking collectives: 14 us -> 0 us
  Pallas kernels: 0 us -> 11.7 us
  other arithmetic: 8.45 us -> 0 us
  loops' own time: 3.88 us -> 0.01 us
    all_to_all x3 -> x0, waiting for transfers between devices: 111 us -> none  [the longest x1 103 us: on_device(): lax.all_to_all(pair_quant, 'owner', split_axis=0, concat_axis=0, tiled=True)]
    ppermute x0 -> x23, starting transfers between devices: none -> 44.9 us  [the longest x11 34.2 us: hop(): lax.ppermute(a, 'owner', [(z * ROWS + y, (z + step) * ROWS + y) for z in...]
    dot_general x3 -> x0, matrix products: 19.2 us -> none  [the longest x2 16.9 us: one_block(): lax.dot_general(quant_rows, col_quant, (((1,), (1,)), ((), ())), preferre...]
    ppermute x0 -> x23, waiting for transfers between devices: none -> 17.7 us  [the longest x11 12 us: hop(): lax.ppermute(a, 'owner', [(z * ROWS + y, (z + step) * ROWS + y) for z in...]
    all_to_all x3 -> x0, starting transfers between devices: 15.5 us -> none  [the longest x1 7.13 us: on_device(): lax.all_to_all(pair_peak, 'owner', split_axis=0, concat_axis=0, tiled=True)]
    pallas_call x0 -> x8, Pallas kernels: none -> 11.7 us  [the longest x6 5.97 us: score(): pl.pallas_call(lambda *refs: score_kernel(plan, docs, hot, len(before), f...]
    all_to_all x1 -> x0, blocking collectives: 10.3 us -> none  [on_device(): lax.all_to_all(pair_cluster, 'owner', split_axis=0, concat_axis=0, tiled=...]
    scatter x2 -> x0, local copies, waits for them, and re-layouts: 6.23 us -> none  [the longest x1 3.78 us: on_device(): jnp.zeros((slot_total,), jnp.bfloat16).at[target].set(peak)]
  transfers between devices with their start and end apart: 4 -> 23, of which waited for: 3 -> 9; matrix products, arithmetic and copies ran while one was open for 4% -> 0% of each run, Pallas kernels for 0% -> 5%
where the time goes in v2:
time: 92 us; the launch traced here: 91.7 us
  starting transfers between devices  44.9 us (49%)
  waiting for transfers between devices  17.7 us (19%)
  between operations  14.4 us (16%)
  Pallas kernels  11.7 us (13%)
  local copies, waits for them, and re-layouts  3.03 us (3%)
    ppermute x11, starting transfers between devices, hop(): lax.ppermute(a, 'owner', [(z * ROWS + y, (z + step) * ROWS + y) for z in...  34.2 us
    ppermute x11, waiting for transfers between devices, hop(): lax.ppermute(a, 'owner', [(z * ROWS + y, (z + step) * ROWS + y) for z in...  12 us
    pallas_call x6, Pallas kernels, score(): pl.pallas_call(lambda *refs: score_kernel(plan, docs, hot, len(before), f...  5.97 us
    pallas_call x1, Pallas kernels, prep(): pl.pallas_call(lambda *refs: prep_kernel(hot, *refs), out_shape=tuple((sh...  4.22 us
    ppermute x3, starting transfers between devices, ahead(): lax.ppermute(a, 'owner', [(z * ROWS + y, (z + step) % columns * ROWS + y)...  3.87 us
    ppermute x3, waiting for transfers between devices, other_row(): return lax.ppermute(a, 'owner', [(i, i ^ 1) for i in range(owners)])  3.68 us
    ppermute x3, starting transfers between devices, other_row(): return lax.ppermute(a, 'owner', [(i, i ^ 1) for i in range(owners)])  3.66 us
    unnamed x36, local copies, waits for them, and re-layouts  3.03 us
  transfers between devices with their start and end apart: 23, of which 9 were waited for; matrix products, arithmetic and copies ran while one was open for 0% of the time, Pallas kernels for 5%

profile of v2, /device:TPU:0, one launch (start us, length us, event | category | flops | bytes accessed | tf_op | source)
XLA Modules:
  0.0 91.7 jit_solution(7520271052848071656)
XLA Ops:
  6.5 4.2 %prep.1 = (bf16[528,768]{1,0:T(8,128)(2,1)S(1)}, bf16[336,768]{1,0:T(8,128)(2,1)S(1)}, bf16[176,768]{1,0:T(8,128)(2,1)}, bf16[176,768]{1,0:T(8,128)(2,1)S(1)}, b...) custom-call(s32[1,512]{1,0:T(1,128)} %bitcast.36, bf16[512,1024]{1,0:T(8,128)(2,1)} %refs_1_.1, bf16[1024,768]{1,0:T(8,128)(2,1)} %refs_2_.1), custom_call_target="tpu_custom_call" | custom-call | tf_op jit(solution)/shard_map/prep/pallas_call | solution.py:188
  11.3 0.7 copy-done.3
  12.5 2.5 %collective-permute-start.4 = (bf16[528,768]{1,0:T(8,128)(2,1)S(1)}, bf16[528,768]{1,0:T(8,128)(2,1)S(1)}, u32[]{:S(2)}, u32[]{:S(2)}) collective-permute-start(bf16[528,768]{1,0:T(8,128)(2,1)S(1)} %get-tuple-element.212.refs_1_.refs_2_.refs_3_.refs_11_.refs_8_.refs_9_.refs_12_.refs_10_), channel_id=1, source_target_pairs={{0,2},{2,0},{4,6},{6,4},{8,10},{10,8},{12,14},{14,12},{1,3},{3,1},... | collective-permute-start | bytes 2433032 | tf_op jit(solution)/shard_map/ppermute | solution.py:319
  15.0 0.7 collective-permute-start.1
  15.7 1.1 %near.1 = (f32[1,640]{1,0:T(1,128)S(1)}, f32[1,640]{1,0:T(1,128)S(1)}, f32[1,640]{1,0:T(1,128)S(1)}, f32[1,640]{1,0:T(1,128)S(1)}, f32[1,640]{1,0:T(1,128)S(1)},...) custom-call(s32[1]{0:T(128)} %bitcast.9.refs_0_, ...), custom_call_target="tpu_custom_call" | custom-call | flops 540672 | bytes 1024 | tf_op jit(solution)/shard_map/near/pallas_call | solution.py:267
  16.8 1.3 %collective-permute-start.5 = (bf16[176,768]{1,0:T(8,128)(2,1)S(1)}, bf16[176,768]{1,0:T(8,128)(2,1)S(1)}, u32[]{:S(2)}, u32[]{:S(2)}) collective-permute-start(bf16[176,768]{1,0:T(8,128)(2,1)S(1)} %collective-permute-done.1.refs_8_.refs_10_), channel_id=1, source_target_pairs={{8,4},{10,6},{4,0},{6,2},{9,5},{11,7},{5,1},{7,3},{24,20},{26,22},... | collective-permute-start | bytes 811016 | tf_op jit(solution)/shard_map/ppermute | solution.py:314
  18.1 13.1 %collective-permute-start.3 = (bf16[208,768]{1,0:T(8,128)(2,1)S(1)}, bf16[208,768]{1,0:T(8,128)(2,1)S(1)}, u32[]{:S(2)}, u32[]{:S(2)}) collective-permute-start(bf16[208,768]{1,0:T(8,128)(2,1)S(1)} %get-tuple-element.222), channel_id=1, source_target_pairs={{0,4},{2,6},{4,8},{6,10},{8,12},{10,14},{1,5},{3,7},{5,9},{7,11},{... | collective-permute-start | bytes 958472 | tf_op jit(solution)/shard_map/ppermute | solution.py:314
  31.2 0.7 collective-permute-start.2
  31.9 1.9 %collective-permute-done.4.refs_13_.refs_14_.refs_12_.refs_4_ = bf16[528,768]{1,0:T(8,128)(2,1)S(1)} collective-permute-done((bf16[528,768]{1,0:T(8,128)(2,1)S(1)}, bf16[528,768]{1,0:T(8,128)(2,1)S(1)}, u32[]{:S(2)}, u32[]{:S(2)}) %collective-permute-start.4) | collective-permute-done | bytes 811040 | tf_op jit(solution)/shard_map/ppermute | solution.py:319
  33.8 1.5 %collective-permute-done.5.refs_8_ = bf16[176,768]{1,0:T(8,128)(2,1)S(1)} collective-permute-done((bf16[176,768]{1,0:T(8,128)(2,1)S(1)}, bf16[176,768]{1,0:T(8,128)(2,1)S(1)}, u32[]{:S(2)}, u32[]{:S(2)}) %collective-permute-start.5) | collective-permute-done | bytes 270368 | tf_op jit(solution)/shard_map/ppermute | solution.py:314
  35.3 2.2 %collective-permute-done.3.refs_10_.refs_12_ = bf16[208,768]{1,0:T(8,128)(2,1)S(1)} collective-permute-done((bf16[208,768]{1,0:T(8,128)(2,1)S(1)}, bf16[208,768]{1,0:T(8,128)(2,1)S(1)}, u32[]{:S(2)}, u32[]{:S(2)}) %collective-permute-start.3) | collective-permute-done | bytes 319520 | tf_op jit(solution)/shard_map/ppermute | solution.py:314
  37.5 0.7 collective-permute-start.8
  38.2 1.3 %collective-permute-start.7 = (bf16[176,768]{1,0:T(8,128)(2,1)S(1)}, bf16[176,768]{1,0:T(8,128)(2,1)S(1)}, u32[]{:S(2)}, u32[]{:S(2)}) collective-permute-start(bf16[176,768]{1,0:T(8,128)(2,1)S(1)} %collective-permute-done.2.refs_9_.refs_11_), channel_id=1, source_target_pairs={{8,4},{10,6},{4,0},{6,2},{9,5},{11,7},{5,1},{7,3},{24,20},{26,22},... | collective-permute-start | bytes 811016 | tf_op jit(solution)/shard_map/ppermute | solution.py:314
  39.5 8.9 %collective-permute-start.9 = (bf16[336,768]{1,0:T(8,128)(2,1)S(1)}, bf16[336,768]{1,0:T(8,128)(2,1)S(1)}, u32[]{:S(2)}, u32[]{:S(2)}) collective-permute-start(bf16[336,768]{1,0:T(8,128)(2,1)S(1)} %get-tuple-element.241), channel_id=1, source_target_pairs={{0,4},{2,6},{1,5},{3,7},{16,20},{18,22},{17,21},{19,23}} | collective-permute-start | bytes 1548296 | tf_op jit(solution)/shard_map/ppermute | solution.py:314
  48.4 2.6 %collective-permute-done.7.refs_9_ = bf16[176,768]{1,0:T(8,128)(2,1)S(1)} collective-permute-done((bf16[176,768]{1,0:T(8,128)(2,1)S(1)}, bf16[176,768]{1,0:T(8,128)(2,1)S(1)}, u32[]{:S(2)}, u32[]{:S(2)}) %collective-permute-start.7) | collective-permute-done | bytes 270368 | tf_op jit(solution)/shard_map/ppermute | solution.py:314
  51.0 0.7 collective-permute-start.11
  51.8 1.3 %collective-permute-start.10 = (bf16[176,768]{1,0:T(8,128)(2,1)S(1)}, bf16[176,768]{1,0:T(8,128)(2,1)S(1)}, u32[]{:S(2)}, u32[]{:S(2)}) collective-permute-start(bf16[176,768]{1,0:T(8,128)(2,1)S(1)} %collective-permute-done.5.refs_8_), channel_id=1, source_target_pairs={{4,0},{6,2},{5,1},{7,3},{20,16},{22,18},{21,17},{23,19}} | collective-permute-start | bytes 811016 | tf_op jit(solution)/shard_map/ppermute | solution.py:314
  53.0 1.3 %collective-permute-start.18 = (bf16[176,768]{1,0:T(8,128)(2,1)S(1)}, bf16[176,768]{1,0:T(8,128)(2,1)S(1)}, u32[]{:S(2)}, u32[]{:S(2)}) collective-permute-start(bf16[176,768]{1,0:T(8,128)(2,1)S(1)} %collective-permute-done.7.refs_9_), channel_id=1, source_target_pairs={{4,0},{6,2},{5,1},{7,3},{20,16},{22,18},{21,17},{23,19}} | collective-permute-start | bytes 811016 | tf_op jit(solution)/shard_map/ppermute | solution.py:314
  54.4 1.0 %far.1 = (f32[1,640]{1,0:T(1,128)S(1)}, f32[1,640]{1,0:T(1,128)S(1)}, f32[1,640]{1,0:T(1,128)S(1)}, f32[1,640]{1,0:T(1,128)S(1)}, f32[1,640]{1,0:T(1,128)S(1)}, ...) custom-call(s32[1]{0:T(128)} %bitcast.9.refs_0_, f32[1,640]{1,0:T(1,128)S(1)} %get-tuple-element.223.refs_1_, ...), custom_call_target="tpu_custom_call" | custom-call | flops 845824 | bytes 1024 | tf_op jit(solution)/shard_map/far/pallas_call | solution.py:267
  55.4 2.1 %collective-permute-done.9.refs_11_ = bf16[336,768]{1,0:T(8,128)(2,1)S(1)} collective-permute-done((bf16[336,768]{1,0:T(8,128)(2,1)S(1)}, bf16[336,768]{1,0:T(8,128)(2,1)S(1)}, u32[]{:S(2)}, u32[]{:S(2)}) %collective-permute-start.9) | collective-permute-done | bytes 516128 | tf_op jit(solution)/shard_map/ppermute | solution.py:314
  57.5 1.8 %hop2.1 = (f32[1,640]{1,0:T(1,128)S(1)}, f32[1,640]{1,0:T(1,128)S(1)}, f32[1,640]{1,0:T(1,128)S(1)}, f32[1,640]{1,0:T(1,128)S(1)}, f32[1,640]{1,0:T(1,128)S(1)},...) custom-call(s32[1]{0:T(128)} %bitcast.9.refs_0_, f32[1,640]{1,0:T(1,128)S(1)} %get-tuple-element.232.refs_1_, ...), custom_call_target="tpu_custom_call" | custom-call | flops 1040384 | bytes 1024 | tf_op jit(solution)/shard_map/hop2/pallas_call | solution.py:267
  59.3 3.5 %collective-permute-done.10.refs_8_ = bf16[176,768]{1,0:T(8,128)(2,1)S(1)} collective-permute-done((bf16[176,768]{1,0:T(8,128)(2,1)S(1)}, bf16[176,768]{1,0:T(8,128)(2,1)S(1)}, u32[]{:S(2)}, u32[]{:S(2)}) %collective-permute-start.10) | collective-permute-done | bytes 270368 | tf_op jit(solution)/shard_map/ppermute | solution.py:314
  62.8 1.0 %hop3.1 = (f32[1,640]{1,0:T(1,128)S(1)}, f32[1,640]{1,0:T(1,128)S(1)}, f32[1,640]{1,0:T(1,128)S(1)}, f32[1,640]{1,0:T(1,128)S(1)}, f32[1,640]{1,0:T(1,128)S(1)},...) custom-call(s32[1]{0:T(128)} %bitcast.9.refs_0_, f32[1,640]{1,0:T(1,128)S(1)} %get-tuple-element.242.refs_1_, ...), custom_call_target="tpu_custom_call" | custom-call | flops 385024 | bytes 1024 | tf_op jit(solution)/shard_map/hop3/pallas_call | solution.py:267
  64.5 1.3 %collective-permute-start.14 = (f32[1,640]{1,0:T(1,128)S(1)}, f32[1,640]{1,0:T(1,128)S(1)}, u32[]{:S(2)}, u32[]{:S(2)}) collective-permute-start(f32[1,640]{1,0:T(1,128)S(1)} %get-tuple-element.254), channel_id=1, source_target_pairs={{0,3},{1,2},{2,1},{3,0},{4,7},{5,6},{6,5},{7,4},{8,11},{9,10},{10,... | collective-permute-start | bytes 7688 | tf_op jit(solution)/shard_map/ppermute | solution.py:325
  65.8 3.9 %collective-permute-start.17 = (f32[1,640]{1,0:T(1,128)S(1)}, f32[1,640]{1,0:T(1,128)S(1)}, u32[]{:S(2)}, u32[]{:S(2)}) collective-permute-start(f32[1,640]{1,0:T(1,128)S(1)} %get-tuple-element.257), channel_id=1, source_target_pairs={{0,12},{2,14},{4,0},{6,2},{8,4},{10,6},{12,8},{14,10},{1,13},{3,15... | collective-permute-start | bytes 7688 | tf_op jit(solution)/shard_map/ppermute | solution.py:328
  69.7 1.5 %collective-permute-done.15.refs_5_ = f32[1,640]{1,0:T(1,128)S(1)} collective-permute-done((f32[1,640]{1,0:T(1,128)S(1)}, f32[1,640]{1,0:T(1,128)S(1)}, u32[]{:S(2)}, u32[]{:S(2)}) %collective-permute-start.15) | collective-permute-done | bytes 2592 | tf_op jit(solution)/shard_map/ppermute | solution.py:328
  71.8 1.0 %last.1 = (f32[1,640]{1,0:T(1,128)S(1)}, f32[1,640]{1,0:T(1,128)S(1)}, f32[1,640]{1,0:T(1,128)S(1)}, f32[1,640]{1,0:T(1,128)S(1)}, f32[1,640]{1,0:T(1,128)S(1)}) custom-call(s32[1]{0:T(128)} %bitcast.9.refs_0_, bf16[176,768]{1,0:T(8,128)(2,1)S(1)} %collective-permute-done.18.refs_1_, ...), custom_call_target="tpu_custom_call" | custom-call | flops 225280 | bytes 1024 | tf_op jit(solution)/shard_map/last/pallas_call | solution.py:267
  72.8 0.6 copy-done.1
  73.4 4.3 %collective-permute-start.19 = (f32[1,640]{1,0:T(1,128)S(1)}, f32[1,640]{1,0:T(1,128)S(1)}, u32[]{:S(2)}, u32[]{:S(2)}) collective-permute-start(f32[1,640]{1,0:T(1,128)S(1)} %get-tuple-element.260), channel_id=1, source_target_pairs={{0,12},{2,14},{1,13},{3,15},{16,28},{18,30},{17,29},{19,31}} | collective-permute-start | bytes 7688 | tf_op jit(solution)/shard_map/ppermute | solution.py:314
  78.4 1.3 %collective-permute-start.22 = (f32[1,640]{1,0:T(1,128)S(1)}, f32[1,640]{1,0:T(1,128)S(1)}, u32[]{:S(2)}, u32[]{:S(2)}) collective-permute-start(f32[1,640]{1,0:T(1,128)S(1)} %get-tuple-element.264), channel_id=1, source_target_pairs={{0,3},{1,2},{2,1},{3,0},{4,7},{5,6},{6,5},{7,4},{8,11},{9,10},{10,... | collective-permute-start | bytes 7688 | tf_op jit(solution)/shard_map/ppermute | solution.py:325
  79.7 1.8 %collective-permute-done.21.refs_11_ = f32[1,640]{1,0:T(1,128)S(1)} collective-permute-done((f32[1,640]{1,0:T(1,128)S(1)}, f32[1,640]{1,0:T(1,128)S(1)}, u32[]{:S(2)}, u32[]{:S(2)}) %collective-permute-start.21) | collective-permute-done | bytes 2592 | tf_op jit(solution)/shard_map/ppermute | solution.py:319
  82.1 1.5 %finish.1 = (f32[1,512]{1,0:T(1,128)S(1)}, s32[1,1]{1,0:T(1,128)}) custom-call(s32[1,512]{1,0:T(1,128)} %copy-done.2, f32[1,640]{1,0:T(1,128)} %copy-done, f32[1,640]{1,0:T(1,128)} %copy-done.10, f32[1,640]{1,0:T(1,128)} %copy-done.11, f32[1,640]{1,0:T(1,128)} %copy-done.12, f32[1,640]{1,0:T(1,128)} %copy-done.13, f32[1,640]{1,0:T(1,128)} %copy-done.14, ...), custom_call_target="tpu_custom_call" | custom-call | tf_op jit(solution)/shard_map/finish/pallas_call | solution.py:293
  (59 shorter events, 4.1 us)
Async XLA Ops:
  12.1 3.7 %collective-permute-start = (bf16[528,768]{1,0:T(8,128)(2,1)S(1)}, bf16[528,768]{1,0:T(8,128)(2,1)S(1)}, u32[]{:S(2)}, u32[]{:S(2)}) collective-permute-start(bf16[528,768]{1,0:T(8,128)(2,1)S(1)} %get-tuple-element.212.refs_1_.refs_2_.refs_3_.refs_11_.refs_8_.refs_9_.refs_12_.refs_10_), channel_id=1, source_target_pairs={{0,1},{1,0},{2,3},{3,2},{4,5},{5,4},{6,7},{7,6},{8,9},{9,8},{10,11... | collective-permute-start | bytes 2433032 | tf_op jit(solution)/shard_map/ppermute | solution.py:322
  12.5 21.3 %collective-permute-start.4 = (bf16[528,768]{1,0:T(8,128)(2,1)S(1)}, bf16[528,768]{1,0:T(8,128)(2,1)S(1)}, u32[]{:S(2)}, u32[]{:S(2)}) collective-permute-start(bf16[528,768]{1,0:T(8,128)(2,1)S(1)} %get-tuple-element.212.refs_1_.refs_2_.refs_3_.refs_11_.refs_8_.refs_9_.refs_12_.refs_10_), channel_id=1, source_target_pairs={{0,2},{2,0},{4,6},{6,4},{8,10},{10,8},{12,14},{14,12},{1,3},{3,1},... | collective-permute-start | bytes 2433032 | tf_op jit(solution)/shard_map/ppermute | solution.py:319
  15.0 1.8 %collective-permute-start.1 = (bf16[176,768]{1,0:T(8,128)(2,1)}, bf16[176,768]{1,0:T(8,128)(2,1)S(1)}, u32[]{:S(2)}, u32[]{:S(2)}) collective-permute-start(bf16[176,768]{1,0:T(8,128)(2,1)} %get-tuple-element.220), channel_id=1, source_target_pairs={{8,4},{10,6},{12,8},{14,10},{9,5},{11,7},{13,9},{15,11},{24,20},{2... | collective-permute-start | bytes 811016 | tf_op jit(solution)/shard_map/ppermute | solution.py:314
  15.7 15.4 %copy-start.4 = (bf16[176,768]{1,0:T(8,128)(2,1)S(1)}, bf16[176,768]{1,0:T(8,128)(2,1)}, u32[]{:S(2)}) copy-start(bf16[176,768]{1,0:T(8,128)(2,1)} %copy-done.3) | copy-start | bytes 811012
  16.8 18.5 %collective-permute-start.5 = (bf16[176,768]{1,0:T(8,128)(2,1)S(1)}, bf16[176,768]{1,0:T(8,128)(2,1)S(1)}, u32[]{:S(2)}, u32[]{:S(2)}) collective-permute-start(bf16[176,768]{1,0:T(8,128)(2,1)S(1)} %collective-permute-done.1.refs_8_.refs_10_), channel_id=1, source_target_pairs={{8,4},{10,6},{4,0},{6,2},{9,5},{11,7},{5,1},{7,3},{24,20},{26,22},... | collective-permute-start | bytes 811016 | tf_op jit(solution)/shard_map/ppermute | solution.py:314
  18.1 19.4 %collective-permute-start.3 = (bf16[208,768]{1,0:T(8,128)(2,1)S(1)}, bf16[208,768]{1,0:T(8,128)(2,1)S(1)}, u32[]{:S(2)}, u32[]{:S(2)}) collective-permute-start(bf16[208,768]{1,0:T(8,128)(2,1)S(1)} %get-tuple-element.222), channel_id=1, source_target_pairs={{0,4},{2,6},{4,8},{6,10},{8,12},{10,14},{1,5},{3,7},{5,9},{7,11},{... | collective-permute-start | bytes 958472 | tf_op jit(solution)/shard_map/ppermute | solution.py:314
  31.2 4.1 %collective-permute-start.2 = (bf16[176,768]{1,0:T(8,128)(2,1)S(1)}, bf16[176,768]{1,0:T(8,128)(2,1)S(1)}, u32[]{:S(2)}, u32[]{:S(2)}) collective-permute-start(bf16[176,768]{1,0:T(8,128)(2,1)S(1)} %copy-done.4), channel_id=1, source_target_pairs={{8,4},{10,6},{12,8},{14,10},{9,5},{11,7},{13,9},{15,11},{24,20},{2... | collective-permute-start | bytes 811016 | tf_op jit(solution)/shard_map/ppermute | solution.py:314
  35.3 19.1 %collective-permute-start.6 = (bf16[528,768]{1,0:T(8,128)(2,1)S(1)}, bf16[528,768]{1,0:T(8,128)(2,1)S(1)}, u32[]{:S(2)}, u32[]{:S(2)}) collective-permute-start(bf16[528,768]{1,0:T(8,128)(2,1)S(1)} %collective-permute-done.4.refs_13_.refs_14_.refs_12_.refs_4_), channel_id=1, source_target_pairs={{0,1},{1,0},{2,3},{3,2},{4,5},{5,4},{6,7},{7,6},{8,9},{9,8},{10,11... | collective-permute-start | bytes 2433032 | tf_op jit(solution)/shard_map/ppermute | solution.py:322
  37.5 13.6 %collective-permute-start.8 = (bf16[208,768]{1,0:T(8,128)(2,1)S(1)}, bf16[208,768]{1,0:T(8,128)(2,1)S(1)}, u32[]{:S(2)}, u32[]{:S(2)}) collective-permute-start(bf16[208,768]{1,0:T(8,128)(2,1)S(1)} %collective-permute-done.3.refs_10_.refs_12_), channel_id=1, source_target_pairs={{4,8},{6,10},{8,12},{10,14},{5,9},{7,11},{9,13},{11,15},{20,24},{2... | collective-permute-start | bytes 958472 | tf_op jit(solution)/shard_map/ppermute | solution.py:314
  38.2 12.9 %collective-permute-start.7 = (bf16[176,768]{1,0:T(8,128)(2,1)S(1)}, bf16[176,768]{1,0:T(8,128)(2,1)S(1)}, u32[]{:S(2)}, u32[]{:S(2)}) collective-permute-start(bf16[176,768]{1,0:T(8,128)(2,1)S(1)} %collective-permute-done.2.refs_9_.refs_11_), channel_id=1, source_target_pairs={{8,4},{10,6},{4,0},{6,2},{9,5},{11,7},{5,1},{7,3},{24,20},{26,22},... | collective-permute-start | bytes 811016 | tf_op jit(solution)/shard_map/ppermute | solution.py:314
  39.5 18.0 %collective-permute-start.9 = (bf16[336,768]{1,0:T(8,128)(2,1)S(1)}, bf16[336,768]{1,0:T(8,128)(2,1)S(1)}, u32[]{:S(2)}, u32[]{:S(2)}) collective-permute-start(bf16[336,768]{1,0:T(8,128)(2,1)S(1)} %get-tuple-element.241), channel_id=1, source_target_pairs={{0,4},{2,6},{1,5},{3,7},{16,20},{18,22},{17,21},{19,23}} | collective-permute-start | bytes 1548296 | tf_op jit(solution)/shard_map/ppermute | solution.py:314
  51.0 8.2 %collective-permute-start.11 = (bf16[208,768]{1,0:T(8,128)(2,1)S(1)}, bf16[208,768]{1,0:T(8,128)(2,1)S(1)}, u32[]{:S(2)}, u32[]{:S(2)}) collective-permute-start(bf16[208,768]{1,0:T(8,128)(2,1)S(1)} %collective-permute-done.8.refs_10_), channel_id=1, source_target_pairs={{8,12},{10,14},{9,13},{11,15},{24,28},{26,30},{25,29},{27,31}} | collective-permute-start | bytes 958472 | tf_op jit(solution)/shard_map/ppermute | solution.py:314
  51.8 11.0 %collective-permute-start.10 = (bf16[176,768]{1,0:T(8,128)(2,1)S(1)}, bf16[176,768]{1,0:T(8,128)(2,1)S(1)}, u32[]{:S(2)}, u32[]{:S(2)}) collective-permute-start(bf16[176,768]{1,0:T(8,128)(2,1)S(1)} %collective-permute-done.5.refs_8_), channel_id=1, source_target_pairs={{4,0},{6,2},{5,1},{7,3},{20,16},{22,18},{21,17},{23,19}} | collective-permute-start | bytes 811016 | tf_op jit(solution)/shard_map/ppermute | solution.py:314
  53.0 12.7 %collective-permute-start.18 = (bf16[176,768]{1,0:T(8,128)(2,1)S(1)}, bf16[176,768]{1,0:T(8,128)(2,1)S(1)}, u32[]{:S(2)}, u32[]{:S(2)}) collective-permute-start(bf16[176,768]{1,0:T(8,128)(2,1)S(1)} %collective-permute-done.7.refs_9_), channel_id=1, source_target_pairs={{4,0},{6,2},{5,1},{7,3},{20,16},{22,18},{21,17},{23,19}} | collective-permute-start | bytes 811016 | tf_op jit(solution)/shard_map/ppermute | solution.py:314
  63.8 20.4 %copy-start.7 = (bf16[512,1024]{1,0:T(8,128)(2,1)S(1)}, bf16[512,1024]{1,0:T(8,128)(2,1)}, u32[]{:S(2)}) copy-start(bf16[512,1024]{1,0:T(8,128)(2,1)} %refs_1_.1) | copy-start | bytes 3145732
  63.8 20.4 %copy-start.9 = (s32[512]{0:T(512)S(1)}, s32[512]{0:T(512)}, u32[]{:S(2)}) copy-start(s32[512]{0:T(512)} %param.9) | copy-start | bytes 6148
  63.8 2.0 %collective-permute-start.12 = (f32[1,640]{1,0:T(1,128)S(1)}, f32[1,640]{1,0:T(1,128)S(1)}, u32[]{:S(2)}, u32[]{:S(2)}) collective-permute-start(f32[1,640]{1,0:T(1,128)S(1)} %get-tuple-element.252), channel_id=1, source_target_pairs={{0,1},{1,0},{2,3},{3,2},{4,5},{5,4},{6,7},{7,6},{8,9},{9,8},{10,11... | collective-permute-start | bytes 7688 | tf_op jit(solution)/shard_map/ppermute | solution.py:322
  63.9 5.8 %collective-permute-start.13 = (f32[1,640]{1,0:T(1,128)S(1)}, f32[1,640]{1,0:T(1,128)S(1)}, u32[]{:S(2)}, u32[]{:S(2)}) collective-permute-start(f32[1,640]{1,0:T(1,128)S(1)} %get-tuple-element.253), channel_id=1, source_target_pairs={{0,2},{2,0},{4,6},{6,4},{8,10},{10,8},{12,14},{14,12},{1,3},{3,1},... | collective-permute-start | bytes 7688 | tf_op jit(solution)/shard_map/ppermute | solution.py:319
  64.5 5.2 %collective-permute-start.14 = (f32[1,640]{1,0:T(1,128)S(1)}, f32[1,640]{1,0:T(1,128)S(1)}, u32[]{:S(2)}, u32[]{:S(2)}) collective-permute-start(f32[1,640]{1,0:T(1,128)S(1)} %get-tuple-element.254), channel_id=1, source_target_pairs={{0,3},{1,2},{2,1},{3,0},{4,7},{5,6},{6,5},{7,4},{8,11},{9,10},{10,... | collective-permute-start | bytes 7688 | tf_op jit(solution)/shard_map/ppermute | solution.py:325
  65.8 5.4 %collective-permute-start.15 = (f32[1,640]{1,0:T(1,128)S(1)}, f32[1,640]{1,0:T(1,128)S(1)}, u32[]{:S(2)}, u32[]{:S(2)}) collective-permute-start(f32[1,640]{1,0:T(1,128)S(1)} %get-tuple-element.255), channel_id=1, source_target_pairs={{0,4},{2,6},{4,8},{6,10},{8,12},{10,14},{12,0},{14,2},{1,5},{3,7},... | collective-permute-start | bytes 7688 | tf_op jit(solution)/shard_map/ppermute | solution.py:328
  65.8 5.4 %collective-permute-start.16 = (f32[1,640]{1,0:T(1,128)S(1)}, f32[1,640]{1,0:T(1,128)S(1)}, u32[]{:S(2)}, u32[]{:S(2)}) collective-permute-start(f32[1,640]{1,0:T(1,128)S(1)} %get-tuple-element.256), channel_id=1, source_target_pairs={{0,8},{2,10},{4,12},{6,14},{8,0},{10,2},{12,4},{14,6},{1,9},{3,11}... | collective-permute-start | bytes 7688 | tf_op jit(solution)/shard_map/ppermute | solution.py:328
  65.8 15.7 %copy-start.10 = (f32[1,640]{1,0:T(1,128)}, f32[1,640]{1,0:T(1,128)S(1)}, u32[]{:S(2)}) copy-start(f32[1,640]{1,0:T(1,128)S(1)} %collective-permute-done.12.refs_2_) | copy-start | bytes 7684
  65.8 5.9 %collective-permute-start.17 = (f32[1,640]{1,0:T(1,128)S(1)}, f32[1,640]{1,0:T(1,128)S(1)}, u32[]{:S(2)}, u32[]{:S(2)}) collective-permute-start(f32[1,640]{1,0:T(1,128)S(1)} %get-tuple-element.257), channel_id=1, source_target_pairs={{0,12},{2,14},{4,0},{6,2},{8,4},{10,6},{12,8},{14,10},{1,13},{3,15... | collective-permute-start | bytes 7688 | tf_op jit(solution)/shard_map/ppermute | solution.py:328
  69.7 11.8 %copy-start.11 = (f32[1,640]{1,0:T(1,128)}, f32[1,640]{1,0:T(1,128)S(1)}, u32[]{:S(2)}) copy-start(f32[1,640]{1,0:T(1,128)S(1)} %collective-permute-done.13.refs_3_) | copy-start | bytes 7684
  69.7 11.8 %copy-start.12 = (f32[1,640]{1,0:T(1,128)}, f32[1,640]{1,0:T(1,128)S(1)}, u32[]{:S(2)}) copy-start(f32[1,640]{1,0:T(1,128)S(1)} %collective-permute-done.14.refs_4_) | copy-start | bytes 7684
  71.2 10.4 %copy-start.13 = (f32[1,640]{1,0:T(1,128)}, f32[1,640]{1,0:T(1,128)S(1)}, u32[]{:S(2)}) copy-start(f32[1,640]{1,0:T(1,128)S(1)} %collective-permute-done.15.refs_5_) | copy-start | bytes 7684
  71.2 10.4 %copy-start.14 = (f32[1,640]{1,0:T(1,128)}, f32[1,640]{1,0:T(1,128)S(1)}, u32[]{:S(2)}) copy-start(f32[1,640]{1,0:T(1,128)S(1)} %collective-permute-done.16.refs_6_) | copy-start | bytes 7684
  71.7 9.8 %copy-start.15 = (f32[1,640]{1,0:T(1,128)}, f32[1,640]{1,0:T(1,128)S(1)}, u32[]{:S(2)}) copy-start(f32[1,640]{1,0:T(1,128)S(1)} %collective-permute-done.17.refs_7_) | copy-start | bytes 7684
  73.4 6.3 %collective-permute-start.19 = (f32[1,640]{1,0:T(1,128)S(1)}, f32[1,640]{1,0:T(1,128)S(1)}, u32[]{:S(2)}, u32[]{:S(2)}) collective-permute-start(f32[1,640]{1,0:T(1,128)S(1)} %get-tuple-element.260), channel_id=1, source_target_pairs={{0,12},{2,14},{1,13},{3,15},{16,28},{18,30},{17,29},{19,31}} | collective-permute-start | bytes 7688 | tf_op jit(solution)/shard_map/ppermute | solution.py:314
  77.8 1.9 %collective-permute-start.20 = (f32[1,640]{1,0:T(1,128)S(1)}, f32[1,640]{1,0:T(1,128)S(1)}, u32[]{:S(2)}, u32[]{:S(2)}) collective-permute-start(f32[1,640]{1,0:T(1,128)S(1)} %get-tuple-element.262), channel_id=1, source_target_pairs={{0,1},{1,0},{2,3},{3,2},{4,5},{5,4},{6,7},{7,6},{8,9},{9,8},{10,11... | collective-permute-start | bytes 7688 | tf_op jit(solution)/shard_map/ppermute | solution.py:322
  77.8 3.7 %collective-permute-start.21 = (f32[1,640]{1,0:T(1,128)S(1)}, f32[1,640]{1,0:T(1,128)S(1)}, u32[]{:S(2)}, u32[]{:S(2)}) collective-permute-start(f32[1,640]{1,0:T(1,128)S(1)} %get-tuple-element.263), channel_id=1, source_target_pairs={{0,2},{2,0},{4,6},{6,4},{8,10},{10,8},{12,14},{14,12},{1,3},{3,1},... | collective-permute-start | bytes 7688 | tf_op jit(solution)/shard_map/ppermute | solution.py:319
  78.4 3.1 %collective-permute-start.22 = (f32[1,640]{1,0:T(1,128)S(1)}, f32[1,640]{1,0:T(1,128)S(1)}, u32[]{:S(2)}, u32[]{:S(2)}) collective-permute-start(f32[1,640]{1,0:T(1,128)S(1)} %get-tuple-element.264), channel_id=1, source_target_pairs={{0,3},{1,2},{2,1},{3,0},{4,7},{5,6},{6,5},{7,4},{8,11},{9,10},{10,... | collective-permute-start | bytes 7688 | tf_op jit(solution)/shard_map/ppermute | solution.py:325
  (9 other events, 16.3 us)

commit v3 on v2

--- a/solution.py
+++ b/solution.py
@@ -189,7 +189,7 @@
         lambda *refs: prep_kernel(hot, *refs),
         out_shape=tuple(shape((b + META, width), BF16) for b in blocks) + (shape((1, docs), jnp.int32),),
         scratch_shapes=[pltpu.VMEM((docs, width), BF16)],
-        compiler_params=pltpu.CompilerParams(vmem_limit_bytes=48 * 2**20),
+        compiler_params=pltpu.CompilerParams(vmem_limit_bytes=24 * 2**20),
         name="prep",
     )(cluster_of.reshape(1, docs), states, proj_weight)
 
@@ -269,7 +269,7 @@
         out_shape=tuple(jax.ShapeDtypeStruct((1, lanes), F32) for _ in outs),
         in_specs=[pl.BlockSpec(memory_space=pltpu.SMEM)] + [vmem] * len(arrays),
         out_specs=tuple(vmem for _ in outs),
-        compiler_params=pltpu.CompilerParams(vmem_limit_bytes=48 * 2**20),
+        compiler_params=pltpu.CompilerParams(vmem_limit_bytes=20 * 2**20),
         cost_estimate=pl.CostEstimate(
             flops=pairs, bytes_accessed=2**10, transcendentals=0
         ),
@@ -333,10 +333,11 @@
     def after(a, *others):
         return lax.optimization_barrier((a, *others))[0]
 
+    qy = other_row(q)
     left1 = [hop(a, (2, 3), -1) for a in (na, nb)]
     right1 = hop(h, (0, 1, 2), 1)
-    qy = other_row(q)
     qc = other_core(q)
+    rightn = hop(n, (0,), 1)
     near = [(q, 3), (qc, 4)]
     own = [(q, "n", 0, OWN, None), (q, "h", 0, OWN, None)]
     def meet(name, before, moving, stills, **options):
@@ -345,38 +346,37 @@
 
     sums = meet("near", (), own, near)
 
-    left2 = [hop(after(left1[0], sums[0]), (2, 1), -1)]
-    left2 += [hop(after(left1[1], left1[0]), (2, 1), -1)]
-    right2 = hop(after(right1, left1[1]), (1, 2), 1)
-    rightn = hop(n, (0,), 1)
+    left1[0], left1[1], right1, _ = lax.optimization_barrier((*left1, right1, sums[0]))
+    left2 = [hop(a, (2, 1), -1) for a in left1]
+    right2 = hop(right1, (1, 2), 1)
+    left3 = [hop(left2[0], (1,), -1)]
+    rightn = after(rightn, left2[0])
     hop1 = [
         (left1[0], "n", 0, 0, (1, 2)),
         (left1[1], "n", half, 0, (1, 2)),
         (right1, "h", 0, 2, (1, 2, 3)),
+        (rightn, "n", 0, 2, (1,)),
     ]
     sums = meet("hop1_near", sums, hop1, near)
 
-    left3 = [hop(after(left2[0], sums[0]), (1,), -1)]
-    qy = after(qy, left2[0])
+    qy = after(qy, sums[0], left2[1], right2)
     qyc = other_core(qy)
-    left3 += [hop(after(left2[1], qy), (1,), -1)]
-    right3 = hop(after(right2, left2[1]), (2,), 1)
-    far = [(qy, 5), (qyc, 6)]
+    right3 = hop(right2, (2,), 1)
+    left3 += [hop(left2[1], (1,), -1)]
+    far = [(qy, 5), (after(qyc, left3[0]), 6)]
     sums = meet("far", sums, own + hop1, far)
     hop2 = [
         (left2[0], "n", 0, 1, (0, 1)),
         (left2[1], "n", half, 1, (0, 1)),
         (right2, "h", 0, 1, (2, 3)),
-        (rightn, "n", 0, 2, (1,)),
     ]
     sums = meet("hop2", sums, hop2, near + far)
     hop3 = [(left3[0], "n", 0, 2, (0,)), (right3, "h", 0, 0, (3,))]
-    early = meet("hop3", sums, hop3, near + far, flags=True)
-    back = [early[OWN], other_core(early[4]), other_row(early[5]), across(early[6])]
-    back += [ahead(early[i], i + 1) for i in range(3)]
-    last = [(after(left3[1], *back), "n", half, 2, (0,))]
-    late = meet("last", (), last, near + far, outs=(2, 3, 4, 5, 6))
-    back += [hop(late[0], (0,), 3), late[1], other_core(late[2]), other_row(late[3]), across(late[4])]
+    sums = meet("hop3", sums, hop3, near + far, flags=True)
+    last = [(left3[1], "n", half, 2, (0,))]
+    sums = meet("last", sums, last, near + far)
+    back = [ahead(sums[i], i + 1) for i in (2, 1, 0)]
+    back += [across(sums[6]), other_row(sums[5]), other_core(sums[4]), sums[OWN]]
     fast, doubt = finish(flag, slot, back)
     return lax.cond(
         doubt[0, 0] > 0, owner_plan, lambda *_: fast.reshape(docs), states, proj_weight, cluster_of

time: 92 us -> 87.9 us (0.955)
  starting transfers between devices: 44.9 us -> 22.3 us
  waiting for transfers between devices: 17.7 us -> 35.2 us
  Pallas kernels: 11.7 us -> 14 us
  local copies, waits for them, and re-layouts: 3.03 us -> 1.77 us
    ppermute x11 -> x10, waiting for transfers between devices: 12 us -> 32.1 us  [hop(): lax.ppermute(a, 'owner', [(z * ROWS + y, (z + step) * ROWS + y) for z in...]
    ppermute x11 -> x10, starting transfers between devices: 34.2 us -> 16.1 us  [hop(): lax.ppermute(a, 'owner', [(z * ROWS + y, (z + step) * ROWS + y) for z in...]
    ppermute x3 -> x2, waiting for transfers between devices: 3.68 us -> 0.01 us  [other_row(): return lax.ppermute(a, 'owner', [(i, i ^ 1) for i in range(owners)])]
    ppermute x2 -> x1, starting transfers between devices: 2.58 us -> 0.01 us  [across(): lax.ppermute(a, ('owner', 'split'), [(i, i ^ 3) for i in range(2 * owners)])]
    pallas_call x6, Pallas kernels: 5.97 us -> 7.89 us  [score(): pl.pallas_call(lambda *refs: score_kernel(plan, docs, hot, len(before), f...]
    ppermute x3, starting transfers between devices: 3.87 us -> 2.03 us  [ahead(): lax.ppermute(a, 'owner', [(z * ROWS + y, (z + step) % columns * ROWS + y)...]
    unnamed x36 -> x22, local copies, waits for them, and re-layouts: 3.03 us -> 1.77 us
    ppermute x3, waiting for transfers between devices: 2.04 us -> 3.09 us  [ahead(): lax.ppermute(a, 'owner', [(z * ROWS + y, (z + step) % columns * ROWS + y)...]
  transfers between devices with their start and end apart: 23 -> 19, of which waited for: 9 -> 9; matrix products, arithmetic and copies ran while one was open for 0% -> 0% of each run, Pallas kernels for 5% -> 8%
where the time goes in v3:
time: 87.9 us; the launch traced here: 87.5 us
  waiting for transfers between devices  35.2 us (40%)
  starting transfers between devices  22.3 us (25%)
  between operations  14.3 us (16%)
  Pallas kernels  14 us (16%)
  local copies, waits for them, and re-layouts  1.77 us (2%)
    ppermute x10, waiting for transfers between devices, hop(): lax.ppermute(a, 'owner', [(z * ROWS + y, (z + step) * ROWS + y) for z in...  32.1 us
    ppermute x10, starting transfers between devices, hop(): lax.ppermute(a, 'owner', [(z * ROWS + y, (z + step) * ROWS + y) for z in...  16.1 us
    pallas_call x6, Pallas kernels, score(): pl.pallas_call(lambda *refs: score_kernel(plan, docs, hot, len(before), f...  7.89 us
    pallas_call x1, Pallas kernels, prep(): pl.pallas_call(lambda *refs: prep_kernel(hot, *refs), out_shape=tuple((sh...  4.6 us
    ppermute x2, starting transfers between devices, other_row(): return lax.ppermute(a, 'owner', [(i, i ^ 1) for i in range(owners)])  3.38 us
    ppermute x3, waiting for transfers between devices, ahead(): lax.ppermute(a, 'owner', [(z * ROWS + y, (z + step) % columns * ROWS + y)...  3.09 us
    ppermute x3, starting transfers between devices, ahead(): lax.ppermute(a, 'owner', [(z * ROWS + y, (z + step) % columns * ROWS + y)...  2.03 us
    unnamed x22, local copies, waits for them, and re-layouts  1.77 us
  transfers between devices with their start and end apart: 19, of which 9 were waited for; matrix products, arithmetic and copies ran while one was open for 0% of the time, Pallas kernels for 8%

profile of v3, /device:TPU:0, one launch (start us, length us, event | category | flops | bytes accessed | tf_op | source)
XLA Modules:
  0.0 87.5 jit_solution(16374877177008875564)
XLA Ops:
  6.5 4.6 %prep.1 = (bf16[528,768]{1,0:T(8,128)(2,1)S(1)}, bf16[336,768]{1,0:T(8,128)(2,1)}, bf16[176,768]{1,0:T(8,128)(2,1)}, bf16[176,768]{1,0:T(8,128)(2,1)}, bf16[208,768]{1,0:T(8,128)(2,1)}, /*index=5*/s32[1,512]{1,0:T(1,128)S(1)}) custom-call(s32[1,512]{1,0:T(1,128)} %bitcast.36, bf16[512,1024]{1,0:T(8,128)(2,1)} %refs_1_.1, bf16[1024,768]{1,0:T(8,128)(2,1)} %refs_2_.1), custom_call_target="tpu_custom_call" | custom-call | tf_op jit(solution)/shard_map/prep/pallas_call | solution.py:188
  11.6 2.6 %collective-permute-start.6 = (bf16[528,768]{1,0:T(8,128)(2,1)S(1)}, bf16[528,768]{1,0:T(8,128)(2,1)S(1)}, u32[]{:S(2)}, u32[]{:S(2)}) collective-permute-start(bf16[528,768]{1,0:T(8,128)(2,1)S(1)} %get-tuple-element.212.refs_1_.refs_2_.refs_3_.refs_12_.refs_8_.refs_9_.refs_11_.refs_10_), channel_id=1, source_target_pairs={{0,2},{2,0},{4,6},{6,4},{8,10},{10,8},{12,14},{14,12},{1,3},{3,1},... | collective-permute-start | bytes 2433032 | tf_op jit(solution)/shard_map/ppermute | solution.py:319
  14.2 3.5 %collective-permute-start.3 = (bf16[208,768]{1,0:T(8,128)(2,1)}, bf16[208,768]{1,0:T(8,128)(2,1)S(1)}, u32[]{:S(2)}, u32[]{:S(2)}) collective-permute-start(bf16[208,768]{1,0:T(8,128)(2,1)} %get-tuple-element.222), channel_id=1, source_target_pairs={{0,4},{2,6},{4,8},{6,10},{8,12},{10,14},{1,5},{3,7},{5,9},{7,11},{... | collective-permute-start | bytes 958472 | tf_op jit(solution)/shard_map/ppermute | solution.py:314
  17.7 0.7 collective-permute-start.1
  18.4 1.4 %collective-permute-start.2 = (bf16[176,768]{1,0:T(8,128)(2,1)}, bf16[176,768]{1,0:T(8,128)(2,1)}, u32[]{:S(2)}, u32[]{:S(2)}) collective-permute-start(bf16[176,768]{1,0:T(8,128)(2,1)} %get-tuple-element.221), channel_id=1, source_target_pairs={{8,4},{10,6},{12,8},{14,10},{9,5},{11,7},{13,9},{15,11},{24,20},{2... | collective-permute-start | bytes 811016 | tf_op jit(solution)/shard_map/ppermute | solution.py:314
  19.7 4.1 %collective-permute-start.4 = (bf16[336,768]{1,0:T(8,128)(2,1)}, bf16[336,768]{1,0:T(8,128)(2,1)S(1)}, u32[]{:S(2)}, u32[]{:S(2)}) collective-permute-start(bf16[336,768]{1,0:T(8,128)(2,1)} %get-tuple-element.226), channel_id=1, source_target_pairs={{0,4},{2,6},{1,5},{3,7},{16,20},{18,22},{17,21},{19,23}} | collective-permute-start | bytes 1548296 | tf_op jit(solution)/shard_map/ppermute | solution.py:314
  23.8 1.1 %near.1 = (f32[1,640]{1,0:T(1,128)S(1)}, f32[1,640]{1,0:T(1,128)S(1)}, f32[1,640]{1,0:T(1,128)S(1)}, f32[1,640]{1,0:T(1,128)S(1)}, f32[1,640]{1,0:T(1,128)S(1)},...) custom-call(s32[1]{0:T(128)} %bitcast.9.refs_0_, ...), custom_call_target="tpu_custom_call" | custom-call | flops 540672 | bytes 1024 | tf_op jit(solution)/shard_map/near/pallas_call | solution.py:267
  24.9 1.0 %collective-permute-done.3.refs_10_.refs_12_ = bf16[208,768]{1,0:T(8,128)(2,1)S(1)} collective-permute-done((bf16[208,768]{1,0:T(8,128)(2,1)}, bf16[208,768]{1,0:T(8,128)(2,1)S(1)}, u32[]{:S(2)}, u32[]{:S(2)}) %collective-permute-start.3) | collective-permute-done | bytes 319520 | tf_op jit(solution)/shard_map/ppermute | solution.py:314
  25.9 0.7 collective-permute-start.8
  26.5 1.3 %collective-permute-start.5 = (bf16[176,768]{1,0:T(8,128)(2,1)S(1)}, bf16[176,768]{1,0:T(8,128)(2,1)S(1)}, u32[]{:S(2)}, u32[]{:S(2)}) collective-permute-start(bf16[176,768]{1,0:T(8,128)(2,1)S(1)} %collective-permute-done.1.refs_8_.refs_10_), channel_id=1, source_target_pairs={{8,4},{10,6},{4,0},{6,2},{9,5},{11,7},{5,1},{7,3},{24,20},{26,22},... | collective-permute-start | bytes 811016 | tf_op jit(solution)/shard_map/ppermute | solution.py:314
  27.8 1.3 %collective-permute-start.7 = (bf16[176,768]{1,0:T(8,128)(2,1)}, bf16[176,768]{1,0:T(8,128)(2,1)S(1)}, u32[]{:S(2)}, u32[]{:S(2)}) collective-permute-start(bf16[176,768]{1,0:T(8,128)(2,1)} %collective-permute-done.2.refs_9_.refs_11_), channel_id=1, source_target_pairs={{8,4},{10,6},{4,0},{6,2},{9,5},{11,7},{5,1},{7,3},{24,20},{26,22},... | collective-permute-start | bytes 811016 | tf_op jit(solution)/shard_map/ppermute | solution.py:314
  29.1 7.0 %collective-permute-done.4.refs_11_.refs_13_ = bf16[336,768]{1,0:T(8,128)(2,1)S(1)} collective-permute-done((bf16[336,768]{1,0:T(8,128)(2,1)}, bf16[336,768]{1,0:T(8,128)(2,1)S(1)}, u32[]{:S(2)}, u32[]{:S(2)}) %collective-permute-start.4) | collective-permute-done | bytes 516128 | tf_op jit(solution)/shard_map/ppermute | solution.py:314
  36.1 12.2 %collective-permute-done.5.refs_8_ = bf16[176,768]{1,0:T(8,128)(2,1)S(1)} collective-permute-done((bf16[176,768]{1,0:T(8,128)(2,1)S(1)}, bf16[176,768]{1,0:T(8,128)(2,1)S(1)}, u32[]{:S(2)}, u32[]{:S(2)}) %collective-permute-start.5) | collective-permute-done | bytes 270368 | tf_op jit(solution)/shard_map/ppermute | solution.py:314
  48.3 1.0 %hop1_near.1 = (f32[1,640]{1,0:T(1,128)S(1)}, f32[1,640]{1,0:T(1,128)S(1)}, f32[1,640]{1,0:T(1,128)S(1)}, f32[1,640]{1,0:T(1,128)S(1)}, f32[1,640]{1,0:T(1,128)S...) custom-call(s32[1]{0:T(128)} %bitcast.9.refs_0_, f32[1,640]{1,0:T(1,128)S(1)} %get-tuple-element.213.refs_1_, ...), custom_call_target="tpu_custom_call" | custom-call | flops 520192 | bytes 1024 | tf_op jit(solution)/shard_map/hop1_near/pallas_call | solution.py:267
  49.3 2.8 %collective-permute-done.7.refs_9_ = bf16[176,768]{1,0:T(8,128)(2,1)S(1)} collective-permute-done((bf16[176,768]{1,0:T(8,128)(2,1)}, bf16[176,768]{1,0:T(8,128)(2,1)S(1)}, u32[]{:S(2)}, u32[]{:S(2)}) %collective-permute-start.7) | collective-permute-done | bytes 270368 | tf_op jit(solution)/shard_map/ppermute | solution.py:314
  52.1 0.7 collective-permute-start.11
  52.8 1.3 %collective-permute-start.10 = (bf16[176,768]{1,0:T(8,128)(2,1)S(1)}, bf16[176,768]{1,0:T(8,128)(2,1)S(1)}, u32[]{:S(2)}, u32[]{:S(2)}) collective-permute-start(bf16[176,768]{1,0:T(8,128)(2,1)S(1)} %collective-permute-done.5.refs_8_), channel_id=1, source_target_pairs={{4,0},{6,2},{5,1},{7,3},{20,16},{22,18},{21,17},{23,19}} | collective-permute-start | bytes 811016 | tf_op jit(solution)/shard_map/ppermute | solution.py:314
  54.1 1.3 %collective-permute-start.12 = (bf16[176,768]{1,0:T(8,128)(2,1)S(1)}, bf16[176,768]{1,0:T(8,128)(2,1)S(1)}, u32[]{:S(2)}, u32[]{:S(2)}) collective-permute-start(bf16[176,768]{1,0:T(8,128)(2,1)S(1)} %collective-permute-done.7.refs_9_), channel_id=1, source_target_pairs={{4,0},{6,2},{5,1},{7,3},{20,16},{22,18},{21,17},{23,19}} | collective-permute-start | bytes 811016 | tf_op jit(solution)/shard_map/ppermute | solution.py:314
  55.4 8.6 %collective-permute-done.10.refs_8_ = bf16[176,768]{1,0:T(8,128)(2,1)S(1)} collective-permute-done((bf16[176,768]{1,0:T(8,128)(2,1)S(1)}, bf16[176,768]{1,0:T(8,128)(2,1)S(1)}, u32[]{:S(2)}, u32[]{:S(2)}) %collective-permute-start.10) | collective-permute-done | bytes 270368 | tf_op jit(solution)/shard_map/ppermute | solution.py:314
  63.9 2.0 %far.1 = (f32[1,640]{1,0:T(1,128)S(1)}, f32[1,640]{1,0:T(1,128)S(1)}, f32[1,640]{1,0:T(1,128)S(1)}, f32[1,640]{1,0:T(1,128)S(1)}, f32[1,640]{1,0:T(1,128)S(1)}, ...) custom-call(s32[1]{0:T(128)} %bitcast.9.refs_0_, f32[1,640]{1,0:T(1,128)S(1)} %get-tuple-element.228.refs_1_, ...), custom_call_target="tpu_custom_call" | custom-call | flops 1060864 | bytes 1024 | tf_op jit(solution)/shard_map/far/pallas_call | solution.py:267
  65.9 1.8 %hop2.1 = (f32[1,640]{1,0:T(1,128)S(1)}, f32[1,640]{1,0:T(1,128)S(1)}, f32[1,640]{1,0:T(1,128)S(1)}, f32[1,640]{1,0:T(1,128)S(1)}, f32[1,640]{1,0:T(1,128)S(1)},...) custom-call(s32[1]{0:T(128)} %bitcast.9.refs_0_, f32[1,640]{1,0:T(1,128)S(1)} %get-tuple-element.237.refs_1_, ...), custom_call_target="tpu_custom_call" | custom-call | flops 610304 | bytes 1024 | tf_op jit(solution)/shard_map/hop2/pallas_call | solution.py:267
  67.7 1.0 %hop3.1 = (f32[1,640]{1,0:T(1,128)S(1)}, f32[1,640]{1,0:T(1,128)S(1)}, f32[1,640]{1,0:T(1,128)S(1)}, f32[1,640]{1,0:T(1,128)S(1)}, f32[1,640]{1,0:T(1,128)S(1)},...) custom-call(s32[1]{0:T(128)} %bitcast.9.refs_0_, f32[1,640]{1,0:T(1,128)S(1)} %get-tuple-element.244.refs_1_, ...), custom_call_target="tpu_custom_call" | custom-call | flops 385024 | bytes 1024 | tf_op jit(solution)/shard_map/hop3/pallas_call | solution.py:267
  69.3 1.0 %last.1 = (f32[1,640]{1,0:T(1,128)S(1)}, f32[1,640]{1,0:T(1,128)S(1)}, f32[1,640]{1,0:T(1,128)S(1)}, f32[1,640]{1,0:T(1,128)S(1)}, f32[1,640]{1,0:T(1,128)S(1)},...) custom-call(s32[1]{0:T(128)} %bitcast.9.refs_0_, f32[1,640]{1,0:T(1,128)S(1)} %get-tuple-element.251.refs_1_, ...), custom_call_target="tpu_custom_call" | custom-call | flops 225280 | bytes 1024 | tf_op jit(solution)/shard_map/last/pallas_call | solution.py:267
  70.4 0.6 copy-done
  71.0 0.8 collective-permute-start.14
  71.9 1.2 %collective-permute-start.15 = (f32[1,640]{1,0:T(1,128)S(1)}, f32[1,640]{1,0:T(1,128)S(1)}, u32[]{:S(2)}, u32[]{:S(2)}) collective-permute-start(f32[1,640]{1,0:T(1,128)S(1)} %get-tuple-element.260), channel_id=1, source_target_pairs={{0,4},{2,6},{4,8},{6,10},{8,12},{10,14},{12,0},{14,2},{1,5},{3,7},... | collective-permute-start | bytes 7688 | tf_op jit(solution)/shard_map/ppermute | solution.py:328
  73.0 0.8 collective-permute-start.17
  73.8 0.8 collective-permute-done.13.refs_1_
  74.9 0.6 collective-permute-done.14.refs_2_
  75.5 1.7 %collective-permute-done.15.refs_3_ = f32[1,640]{1,0:T(1,128)S(1)} collective-permute-done((f32[1,640]{1,0:T(1,128)S(1)}, f32[1,640]{1,0:T(1,128)S(1)}, u32[]{:S(2)}, u32[]{:S(2)}) %collective-permute-start.15) | collective-permute-done | bytes 2592 | tf_op jit(solution)/shard_map/ppermute | solution.py:328
  77.9 1.5 %finish.1 = (f32[1,512]{1,0:T(1,128)S(1)}, s32[1,1]{1,0:T(1,128)}) custom-call(s32[1,512]{1,0:T(1,128)} %copy-done.1, f32[1,640]{1,0:T(1,128)} %copy-done.7, f32[1,640]{1,0:T(1,128)} %copy-done.8, f32[1,640]{1,0:T(1,128)} %copy-done.9, f32[1,640]{1,0:T(1,128)} %copy-done.10, f32[1,640]{1,0:T(1,128)} %copy-done.11, f32[1,640]{1,0:T(1,128)} %copy-done.12, ...), custom_call_target="tpu_custom_call" | custom-call | tf_op jit(solution)/shard_map/finish/pallas_call | solution.py:293
  80.1 0.6 copy-done.13
  (37 shorter events, 1.9 us)
Async XLA Ops:
  11.1 8.6 %copy-start.1 = (s32[1,512]{1,0:T(1,128)}, s32[1,512]{1,0:T(1,128)S(1)}, u32[]{:S(2)}) copy-start(s32[1,512]{1,0:T(1,128)S(1)} %get-tuple-element.211.refs_0_) | copy-start | bytes 6148
  11.1 8.6 %collective-permute-start = (bf16[528,768]{1,0:T(8,128)(2,1)S(1)}, bf16[528,768]{1,0:T(8,128)(2,1)S(1)}, u32[]{:S(2)}, u32[]{:S(2)}) collective-permute-start(bf16[528,768]{1,0:T(8,128)(2,1)S(1)} %get-tuple-element.212.refs_1_.refs_2_.refs_3_.refs_12_.refs_8_.refs_9_.refs_11_.refs_10_), channel_id=1, source_target_pairs={{0,1},{1,0},{2,3},{3,2},{4,5},{5,4},{6,7},{7,6},{8,9},{9,8},{10,11... | collective-permute-start | bytes 2433032 | tf_op jit(solution)/shard_map/ppermute | solution.py:322
  11.6 37.7 %collective-permute-start.6 = (bf16[528,768]{1,0:T(8,128)(2,1)S(1)}, bf16[528,768]{1,0:T(8,128)(2,1)S(1)}, u32[]{:S(2)}, u32[]{:S(2)}) collective-permute-start(bf16[528,768]{1,0:T(8,128)(2,1)S(1)} %get-tuple-element.212.refs_1_.refs_2_.refs_3_.refs_12_.refs_8_.refs_9_.refs_11_.refs_10_), channel_id=1, source_target_pairs={{0,2},{2,0},{4,6},{6,4},{8,10},{10,8},{12,14},{14,12},{1,3},{3,1},... | collective-permute-start | bytes 2433032 | tf_op jit(solution)/shard_map/ppermute | solution.py:319
  14.2 11.7 %collective-permute-start.3 = (bf16[208,768]{1,0:T(8,128)(2,1)}, bf16[208,768]{1,0:T(8,128)(2,1)S(1)}, u32[]{:S(2)}, u32[]{:S(2)}) collective-permute-start(bf16[208,768]{1,0:T(8,128)(2,1)} %get-tuple-element.222), channel_id=1, source_target_pairs={{0,4},{2,6},{4,8},{6,10},{8,12},{10,14},{1,5},{3,7},{5,9},{7,11},{... | collective-permute-start | bytes 958472 | tf_op jit(solution)/shard_map/ppermute | solution.py:314
  17.7 7.2 %collective-permute-start.1 = (bf16[176,768]{1,0:T(8,128)(2,1)}, bf16[176,768]{1,0:T(8,128)(2,1)S(1)}, u32[]{:S(2)}, u32[]{:S(2)}) collective-permute-start(bf16[176,768]{1,0:T(8,128)(2,1)} %get-tuple-element.220), channel_id=1, source_target_pairs={{8,4},{10,6},{12,8},{14,10},{9,5},{11,7},{13,9},{15,11},{24,20},{2... | collective-permute-start | bytes 811016 | tf_op jit(solution)/shard_map/ppermute | solution.py:314
  18.4 6.5 %collective-permute-start.2 = (bf16[176,768]{1,0:T(8,128)(2,1)}, bf16[176,768]{1,0:T(8,128)(2,1)}, u32[]{:S(2)}, u32[]{:S(2)}) collective-permute-start(bf16[176,768]{1,0:T(8,128)(2,1)} %get-tuple-element.221), channel_id=1, source_target_pairs={{8,4},{10,6},{12,8},{14,10},{9,5},{11,7},{13,9},{15,11},{24,20},{2... | collective-permute-start | bytes 811016 | tf_op jit(solution)/shard_map/ppermute | solution.py:314
  19.7 16.4 %collective-permute-start.4 = (bf16[336,768]{1,0:T(8,128)(2,1)}, bf16[336,768]{1,0:T(8,128)(2,1)S(1)}, u32[]{:S(2)}, u32[]{:S(2)}) collective-permute-start(bf16[336,768]{1,0:T(8,128)(2,1)} %get-tuple-element.226), channel_id=1, source_target_pairs={{0,4},{2,6},{1,5},{3,7},{16,20},{18,22},{17,21},{19,23}} | collective-permute-start | bytes 1548296 | tf_op jit(solution)/shard_map/ppermute | solution.py:314
  25.9 26.2 %collective-permute-start.8 = (bf16[208,768]{1,0:T(8,128)(2,1)S(1)}, bf16[208,768]{1,0:T(8,128)(2,1)S(1)}, u32[]{:S(2)}, u32[]{:S(2)}) collective-permute-start(bf16[208,768]{1,0:T(8,128)(2,1)S(1)} %collective-permute-done.3.refs_10_.refs_12_), channel_id=1, source_target_pairs={{4,8},{6,10},{8,12},{10,14},{5,9},{7,11},{9,13},{11,15},{20,24},{2... | collective-permute-start | bytes 958472 | tf_op jit(solution)/shard_map/ppermute | solution.py:314
  26.5 21.8 %collective-permute-start.5 = (bf16[176,768]{1,0:T(8,128)(2,1)S(1)}, bf16[176,768]{1,0:T(8,128)(2,1)S(1)}, u32[]{:S(2)}, u32[]{:S(2)}) collective-permute-start(bf16[176,768]{1,0:T(8,128)(2,1)S(1)} %collective-permute-done.1.refs_8_.refs_10_), channel_id=1, source_target_pairs={{8,4},{10,6},{4,0},{6,2},{9,5},{11,7},{5,1},{7,3},{24,20},{26,22},... | collective-permute-start | bytes 811016 | tf_op jit(solution)/shard_map/ppermute | solution.py:314
  27.8 24.3 %collective-permute-start.7 = (bf16[176,768]{1,0:T(8,128)(2,1)}, bf16[176,768]{1,0:T(8,128)(2,1)S(1)}, u32[]{:S(2)}, u32[]{:S(2)}) collective-permute-start(bf16[176,768]{1,0:T(8,128)(2,1)} %collective-permute-done.2.refs_9_.refs_11_), channel_id=1, source_target_pairs={{8,4},{10,6},{4,0},{6,2},{9,5},{11,7},{5,1},{7,3},{24,20},{26,22},... | collective-permute-start | bytes 811016 | tf_op jit(solution)/shard_map/ppermute | solution.py:314
  52.1 11.9 %collective-permute-start.9 = (bf16[528,768]{1,0:T(8,128)(2,1)S(1)}, bf16[528,768]{1,0:T(8,128)(2,1)S(1)}, u32[]{:S(2)}, u32[]{:S(2)}) collective-permute-start(bf16[528,768]{1,0:T(8,128)(2,1)S(1)} %collective-permute-done.6.refs_14_.refs_13_.refs_12_.refs_11_), channel_id=1, source_target_pairs={{0,1},{1,0},{2,3},{3,2},{4,5},{5,4},{6,7},{7,6},{8,9},{9,8},{10,11... | collective-permute-start | bytes 2433032 | tf_op jit(solution)/shard_map/ppermute | solution.py:322
  52.1 15.7 %collective-permute-start.11 = (bf16[208,768]{1,0:T(8,128)(2,1)S(1)}, bf16[208,768]{1,0:T(8,128)(2,1)S(1)}, u32[]{:S(2)}, u32[]{:S(2)}) collective-permute-start(bf16[208,768]{1,0:T(8,128)(2,1)S(1)} %collective-permute-done.8.refs_10_), channel_id=1, source_target_pairs={{8,12},{10,14},{9,13},{11,15},{24,28},{26,30},{25,29},{27,31}} | collective-permute-start | bytes 958472 | tf_op jit(solution)/shard_map/ppermute | solution.py:314
  52.8 11.2 %collective-permute-start.10 = (bf16[176,768]{1,0:T(8,128)(2,1)S(1)}, bf16[176,768]{1,0:T(8,128)(2,1)S(1)}, u32[]{:S(2)}, u32[]{:S(2)}) collective-permute-start(bf16[176,768]{1,0:T(8,128)(2,1)S(1)} %collective-permute-done.5.refs_8_), channel_id=1, source_target_pairs={{4,0},{6,2},{5,1},{7,3},{20,16},{22,18},{21,17},{23,19}} | collective-permute-start | bytes 811016 | tf_op jit(solution)/shard_map/ppermute | solution.py:314
  54.1 15.3 %collective-permute-start.12 = (bf16[176,768]{1,0:T(8,128)(2,1)S(1)}, bf16[176,768]{1,0:T(8,128)(2,1)S(1)}, u32[]{:S(2)}, u32[]{:S(2)}) collective-permute-start(bf16[176,768]{1,0:T(8,128)(2,1)S(1)} %collective-permute-done.7.refs_9_), channel_id=1, source_target_pairs={{4,0},{6,2},{5,1},{7,3},{20,16},{22,18},{21,17},{23,19}} | collective-permute-start | bytes 811016 | tf_op jit(solution)/shard_map/ppermute | solution.py:314
  68.8 11.3 %copy-start.4 = (bf16[512,1024]{1,0:T(8,128)(2,1)S(1)}, bf16[512,1024]{1,0:T(8,128)(2,1)}, u32[]{:S(2)}) copy-start(bf16[512,1024]{1,0:T(8,128)(2,1)} %refs_1_.1) | copy-start | bytes 3145732
  68.8 11.3 %copy-start.6 = (s32[512]{0:T(512)S(1)}, s32[512]{0:T(512)}, u32[]{:S(2)}) copy-start(s32[512]{0:T(512)} %param.9) | copy-start | bytes 6148
  70.4 0.6 copy-start
  71.0 3.6 %collective-permute-start.13 = (f32[1,640]{1,0:T(1,128)S(1)}, f32[1,640]{1,0:T(1,128)S(1)}, u32[]{:S(2)}, u32[]{:S(2)}) collective-permute-start(f32[1,640]{1,0:T(1,128)S(1)} %get-tuple-element.258), channel_id=1, source_target_pairs={{0,12},{2,14},{4,0},{6,2},{8,4},{10,6},{12,8},{14,10},{1,13},{3,15... | collective-permute-start | bytes 7688 | tf_op jit(solution)/shard_map/ppermute | solution.py:328
  71.0 4.5 %collective-permute-start.14 = (f32[1,640]{1,0:T(1,128)S(1)}, f32[1,640]{1,0:T(1,128)S(1)}, u32[]{:S(2)}, u32[]{:S(2)}) collective-permute-start(f32[1,640]{1,0:T(1,128)S(1)} %get-tuple-element.259), channel_id=1, source_target_pairs={{0,8},{2,10},{4,12},{6,14},{8,0},{10,2},{12,4},{14,6},{1,9},{3,11}... | collective-permute-start | bytes 7688 | tf_op jit(solution)/shard_map/ppermute | solution.py:328
  71.9 5.4 %collective-permute-start.15 = (f32[1,640]{1,0:T(1,128)S(1)}, f32[1,640]{1,0:T(1,128)S(1)}, u32[]{:S(2)}, u32[]{:S(2)}) collective-permute-start(f32[1,640]{1,0:T(1,128)S(1)} %get-tuple-element.260), channel_id=1, source_target_pairs={{0,4},{2,6},{4,8},{6,10},{8,12},{10,14},{12,0},{14,2},{1,5},{3,7},... | collective-permute-start | bytes 7688 | tf_op jit(solution)/shard_map/ppermute | solution.py:328
  73.0 4.2 %collective-permute-start.16 = (f32[1,640]{1,0:T(1,128)S(1)}, f32[1,640]{1,0:T(1,128)S(1)}, u32[]{:S(2)}, u32[]{:S(2)}) collective-permute-start(f32[1,640]{1,0:T(1,128)S(1)} %get-tuple-element.261), channel_id=1, source_target_pairs={{0,3},{1,2},{2,1},{3,0},{4,7},{5,6},{6,5},{7,4},{8,11},{9,10},{10,... | collective-permute-start | bytes 7688 | tf_op jit(solution)/shard_map/ppermute | solution.py:325
  73.0 4.2 %collective-permute-start.17 = (f32[1,640]{1,0:T(1,128)S(1)}, f32[1,640]{1,0:T(1,128)S(1)}, u32[]{:S(2)}, u32[]{:S(2)}) collective-permute-start(f32[1,640]{1,0:T(1,128)S(1)} %get-tuple-element.262), channel_id=1, source_target_pairs={{0,2},{2,0},{4,6},{6,4},{8,10},{10,8},{12,14},{14,12},{1,3},{3,1},... | collective-permute-start | bytes 7688 | tf_op jit(solution)/shard_map/ppermute | solution.py:319
  74.6 2.7 %copy-start.7 = (f32[1,640]{1,0:T(1,128)}, f32[1,640]{1,0:T(1,128)S(1)}, u32[]{:S(2)}) copy-start(f32[1,640]{1,0:T(1,128)S(1)} %collective-permute-done.13.refs_1_) | copy-start | bytes 7684
  74.6 2.7 %collective-permute-start.18 = (f32[1,640]{1,0:T(1,128)S(1)}, f32[1,640]{1,0:T(1,128)S(1)}, u32[]{:S(2)}, u32[]{:S(2)}) collective-permute-start(f32[1,640]{1,0:T(1,128)S(1)} %get-tuple-element.263), channel_id=1, source_target_pairs={{0,1},{1,0},{2,3},{3,2},{4,5},{5,4},{6,7},{7,6},{8,9},{9,8},{10,11... | collective-permute-start | bytes 7688 | tf_op jit(solution)/shard_map/ppermute | solution.py:322
  75.5 1.8 %copy-start.8 = (f32[1,640]{1,0:T(1,128)}, f32[1,640]{1,0:T(1,128)S(1)}, u32[]{:S(2)}) copy-start(f32[1,640]{1,0:T(1,128)S(1)} %collective-permute-done.14.refs_2_) | copy-start | bytes 7684
  77.2 0.6 copy-start.9
  77.2 0.6 copy-start.10
  77.3 0.6 copy-start.11
  77.3 0.6 copy-start.12
  80.1 0.6 copy-start.13

commit v4 on v3

--- a/solution.py
+++ b/solution.py
@@ -122,10 +122,9 @@
     return rest, first, flag, up(flag + 1, 128)
 
 
-def prep_kernel(hot, cl_ref, st_ref, w_ref, q_ref, n_ref, na_ref, nb_ref, h_ref, slot_ref, vectors):
+def prep_kernel(hot, place_ref, cl_ref, st_ref, w_ref, q_ref, even_ref, odd_ref, slot_ref, vectors):
     docs = st_ref.shape[0]
     rest, first, flag, lanes = layout(docs, hot)
-    half = rest // 2
     tile = 128
 
     cluster = cl_ref[...]
@@ -157,41 +156,57 @@
     cluster_rows = jnp.broadcast_to(cluster.astype(F32), (META, docs)).astype(BF16)
     sorted_n = jnp.dot(sort[:rest, :], vectors[...], preferred_element_type=F32).astype(BF16)
     sorted_h = jnp.dot(sort[first:flag, :], vectors[...], preferred_element_type=F32).astype(BF16)
-
-    def meta(ref, row, start, stop):
-        ids = lax.dot_general(
-            cluster_rows, sort[start:stop, :], (((1,), (1,)), ((), ())), preferred_element_type=F32
-        )
-        spot = lax.broadcasted_iota(jnp.int32, ids.shape, 1) + start
-        ids = jnp.where(spot == flag, doubt, ids)
-        ref[row:row + META, :] = jnp.zeros((META, ref.shape[1]), BF16)
-        ref[row:row + META, 0:stop - start] = ids.astype(BF16)
+    ids = lax.dot_general(
+        cluster_rows, sort, (((1,), (1,)), ((), ())), preferred_element_type=F32
+    )
+    ids = jnp.where(lax.broadcasted_iota(jnp.int32, ids.shape, 1) == flag, doubt, ids).astype(BF16)
 
     q_ref[:rest, :] = sorted_n
     q_ref[rest:docs, :] = sorted_h
-    meta(q_ref, docs, 0, lanes)
-    n_ref[:rest, :] = sorted_n
-    meta(n_ref, rest, 0, rest)
-    na_ref[:half, :] = sorted_n[:half]
-    meta(na_ref, half, 0, half)
-    nb_ref[:half, :] = sorted_n[half:]
-    meta(nb_ref, half, half, rest)
-    h_ref[:hot, :] = sorted_h
-    meta(h_ref, hot, first, flag)
-
-
-def prep(hot, cluster_of, states, proj_weight):
+    q_ref[docs:, :] = jnp.zeros((META, q_ref.shape[1]), BF16)
+    q_ref[docs:, :lanes] = ids
+
+    def fill_n(ref):
+        ref[:rest, :] = sorted_n
+        ref[rest:, :] = jnp.zeros((META, ref.shape[1]), BF16)
+        ref[rest:, :first] = ids[:, :first]
+
+    def fill_h(ref):
+        ref[:hot, :] = sorted_h
+        ref[hot:, :] = jnp.zeros((rest + META - hot, ref.shape[1]), BF16)
+        ref[rest:, :lanes - first] = ids[:, first:]
+
+    even = lax.rem(place_ref[0], 2) == 0
+
+    @pl.when(even)
+    def _():
+        fill_h(even_ref)
+        fill_n(odd_ref)
+
+    @pl.when(jnp.logical_not(even))
+    def _():
+        fill_n(even_ref)
+        fill_h(odd_ref)
+
+
+def prep(hot, place, cluster_of, states, proj_weight):
     docs, width = states.shape[0], proj_weight.shape[1]
     rest = docs - hot
     shape = jax.ShapeDtypeStruct
-    blocks = (docs, rest, rest // 2, rest // 2, hot)
+    vmem = pl.BlockSpec(memory_space=pltpu.VMEM)
     return pl.pallas_call(
         lambda *refs: prep_kernel(hot, *refs),
-        out_shape=tuple(shape((b + META, width), BF16) for b in blocks) + (shape((1, docs), jnp.int32),),
+        out_shape=(
+            shape((docs + META, width), BF16),
+            shape((rest + META, width), BF16),
+            shape((rest + META, width), BF16),
+            shape((1, docs), jnp.int32),
+        ),
+        in_specs=[pl.BlockSpec(memory_space=pltpu.SMEM), vmem, vmem, vmem],
         scratch_shapes=[pltpu.VMEM((docs, width), BF16)],
         compiler_params=pltpu.CompilerParams(vmem_limit_bytes=24 * 2**20),
         name="prep",
-    )(cluster_of.reshape(1, docs), states, proj_weight)
+    )(place, cluster_of.reshape(1, docs), states, proj_weight)
 
 
 OWN = 3
@@ -211,43 +226,38 @@
     metas = [ref[docs:docs + META, :].astype(F32)[0:1, :] for ref in still_refs]
     span = {"n": (0, slice(0, rest), slice(0, rest)), "h": (first, slice(rest, docs), slice(first, flag))}
 
-    for (kind, row, target, holders, meets), move_ref in zip(moving, move_refs):
-
-        def work(kind=kind, row=row, target=target, meets=meets, move_ref=move_ref):
+    for (kind, target, holder), move_ref in zip(moving, move_refs):
+
+        def work(kind=kind, target=target, move_ref=move_ref):
             start, rows, lane = span[kind]
+            count = rows.stop - rows.start
             if target == OWN:
-                count = rows.stop - rows.start
                 block = move_ref[rows, :]
                 ids = move_ref[docs:docs + META, :].astype(F32)[0:8, lane]
             else:
-                count = move_ref.shape[0] - META
                 block = move_ref[:count, :]
-                ids = move_ref[count:count + META, :].astype(F32)[0:8, 0:count]
+                ids = move_ref[rest:rest + META, :].astype(F32)[0:8, 0:count]
             ids = ids.T[:, 0:1]
             total = jnp.zeros((count, 1), F32)
-            for index in meets:
+            for still, still_ref, still_ids in zip(stills, still_refs, metas):
                 inner = lax.dot_general(
-                    block, still_refs[index][rows, :], (((1,), (1,)), ((), ())), preferred_element_type=F32
+                    block, still_ref[rows, :], (((1,), (1,)), ((), ())), preferred_element_type=F32
                 )
-                same = ids == metas[index][:, lane]
-                if target == OWN and stills[index] == OWN:
+                same = ids == still_ids[:, lane]
+                if target == OWN and still == OWN:
                     same &= lax.broadcasted_iota(jnp.int32, inner.shape, 0) != lax.broadcasted_iota(
                         jnp.int32, inner.shape, 1
                     )
                 weights = jnp.where(same, jnp.exp2(inner), 0.0)
                 total += jnp.sum(weights, axis=1, keepdims=True)
                 if target != OWN:
-                    out_refs[stills[index]][:, lane] += jnp.sum(weights, axis=0, keepdims=True)
-            spot = slice(start + row, start + row + count)
-            out_refs[target][:, spot] += jnp.broadcast_to(total, (count, 128)).T[0:1, :]
-
-        if holders is None:
+                    out_refs[still][:, lane] += jnp.sum(weights, axis=0, keepdims=True)
+            out_refs[target][:, lane] += jnp.broadcast_to(total, (count, 128)).T[0:1, :]
+
+        if holder is None:
             work()
         else:
-            held = z == holders[0]
-            for holder in holders[1:]:
-                held |= z == holder
-            pl.when(held)(work)
+            pl.when(z == holder)(work)
 
     if flags:
         doubt = metas[0]
@@ -258,11 +268,11 @@
             out_refs[target][...] += jnp.where(spot == flag, doubt[:, :lanes], 0.0)
 
 
-def score(name, docs, hot, place, before, moving, stills, flags=False, outs=tuple(range(SUMS))):
+def score(name, docs, hot, place, before, moving, stills, flags=False, outs=tuple(range(SUMS)), weight=1):
     lanes = layout(docs, hot)[3]
     plan = ([m[1:] for m in moving], [s[1] for s in stills])
     vmem = pl.BlockSpec(memory_space=pltpu.VMEM)
-    pairs = sum(m[0].shape[0] * len(m[5]) * (hot if m[1] == "h" else docs - hot) for m in moving)
+    pairs = len(stills) * sum((hot if m[1] == "h" else docs - hot) ** 2 for m in moving)
     arrays = [*before, *(m[0] for m in moving), *(s[0] for s in stills)]
     return pl.pallas_call(
         lambda *refs: score_kernel(plan, docs, hot, len(before), flags, outs, *refs),
@@ -271,7 +281,7 @@
         out_specs=tuple(vmem for _ in outs),
         compiler_params=pltpu.CompilerParams(vmem_limit_bytes=20 * 2**20),
         cost_estimate=pl.CostEstimate(
-            flops=pairs, bytes_accessed=2**10, transcendentals=0
+            flops=weight * pairs, bytes_accessed=2**10, transcendentals=0
         ),
         name=name,
     )(place, *arrays)
@@ -302,18 +312,25 @@
     columns = owners // ROWS
     docs = states.shape[0]
     hot = 3 * docs // owners
-    rest = docs - hot
-    half = rest // 2
     flag = layout(docs, hot)[2]
 
-    q, n, na, nb, h, slot = prep(hot, cluster_of, states, proj_weight)
     owner = lax.axis_index("owner")
     place = (owner // ROWS).astype(jnp.int32).reshape(1)
-
-    def hop(a, sources, step):
+    q, even, odd, slot = prep(hot, place, cluster_of, states, proj_weight)
+
+    def move(a, to):
         return lax.ppermute(
-            a, "owner", [(z * ROWS + y, (z + step) * ROWS + y) for z in sources for y in range(ROWS)]
+            a, "owner", [(z * ROWS + y, to[z] * ROWS + y) for z in range(columns) for y in range(ROWS)]
         )
+
+    def outer(a):
+        return move(a, (1, 0, 3, 2))
+
+    def middle(a):
+        return move(a, (0, 2, 1, 3))
+
+    def ends(a):
+        return move(a, (3, 1, 2, 0))
 
     def other_row(a):
         return lax.ppermute(a, "owner", [(i, i ^ 1) for i in range(owners)])
@@ -325,56 +342,41 @@
         return lax.ppermute(a, ("owner", "split"), [(i, i ^ 3) for i in range(2 * owners)])
 
     def ahead(a, step):
-        return lax.ppermute(
-            a, "owner",
-            [(z * ROWS + y, (z + step) % columns * ROWS + y) for z in range(columns) for y in range(ROWS)],
-        )
+        return move(a, tuple((z + step) % columns for z in range(columns)))
 
     def after(a, *others):
         return lax.optimization_barrier((a, *others))[0]
 
+    def meet(name, before, moving, stills, **options):
+        return score(name, docs, hot, place, before, moving, stills, **options)
+
+    first_outer = outer(even)
+    first_middle = middle(odd)
     qy = other_row(q)
-    left1 = [hop(a, (2, 3), -1) for a in (na, nb)]
-    right1 = hop(h, (0, 1, 2), 1)
     qc = other_core(q)
-    rightn = hop(n, (0,), 1)
+    first_ends = ends(even)
+    own = [(q, "n", OWN, None), (q, "h", OWN, None)]
     near = [(q, 3), (qc, 4)]
-    own = [(q, "n", 0, OWN, None), (q, "h", 0, OWN, None)]
-    def meet(name, before, moving, stills, **options):
-        every = tuple(range(len(stills)))
-        return score(name, docs, hot, place, before, [m + (every,) for m in moving], stills, **options)
-
     sums = meet("near", (), own, near)
 
-    left1[0], left1[1], right1, _ = lax.optimization_barrier((*left1, right1, sums[0]))
-    left2 = [hop(a, (2, 1), -1) for a in left1]
-    right2 = hop(right1, (1, 2), 1)
-    left3 = [hop(left2[0], (1,), -1)]
-    rightn = after(rightn, left2[0])
+    first_outer, first_middle, _ = lax.optimization_barrier((first_outer, first_middle, sums[0]))
+    then_outer = outer(first_middle)
+    then_middle = middle(first_outer)
     hop1 = [
-        (left1[0], "n", 0, 0, (1, 2)),
-        (left1[1], "n", half, 0, (1, 2)),
-        (right1, "h", 0, 2, (1, 2, 3)),
-        (rightn, "n", 0, 2, (1,)),
+        (first_outer, "n", 0, 0), (first_outer, "h", 2, 1), (first_outer, "n", 0, 2), (first_outer, "h", 2, 3),
+        (first_middle, "n", 0, 1), (first_middle, "h", 2, 2),
     ]
-    sums = meet("hop1_near", sums, hop1, near)
-
-    qy = after(qy, sums[0], left2[1], right2)
     qyc = other_core(qy)
-    right3 = hop(right2, (2,), 1)
-    left3 += [hop(left2[1], (1,), -1)]
-    far = [(qy, 5), (after(qyc, left3[0]), 6)]
-    sums = meet("far", sums, own + hop1, far)
+    sums = meet("own_far", sums, own, [(qy, 5)])
+    sums = meet("hop1", sums, hop1, near + [(qy, 5)], weight=2**16)
+    sums = meet("far", sums, own + hop1, [(qyc, 6)])
+    far = [(qy, 5), (qyc, 6)]
+    hop3 = [(first_ends, "n", 2, 0), (first_ends, "h", 0, 3)]
+    sums = meet("hop3", sums, hop3, near + far, flags=True)
     hop2 = [
-        (left2[0], "n", 0, 1, (0, 1)),
-        (left2[1], "n", half, 1, (0, 1)),
-        (right2, "h", 0, 1, (2, 3)),
+        (then_outer, "n", 1, 0), (then_outer, "h", 1, 3), (then_middle, "n", 1, 1), (then_middle, "h", 1, 2),
     ]
     sums = meet("hop2", sums, hop2, near + far)
-    hop3 = [(left3[0], "n", 0, 2, (0,)), (right3, "h", 0, 0, (3,))]
-    sums = meet("hop3", sums, hop3, near + far, flags=True)
-    last = [(left3[1], "n", half, 2, (0,))]
-    sums = meet("last", sums, last, near + far)
     back = [ahead(sums[i], i + 1) for i in (2, 1, 0)]
     back += [across(sums[6]), other_row(sums[5]), other_core(sums[4]), sums[OWN]]
     fast, doubt = finish(flag, slot, back)

time: 87.9 us -> 73.4 us (0.84)
  waiting for transfers between devices: 35.2 us -> 24.1 us
  Pallas kernels: 14 us -> 11.9 us
  starting transfers between devices: 22.3 us -> 21.2 us
    ppermute x13 -> x8, waiting for transfers between devices: 35.2 us -> 23.5 us  [move(): lax.ppermute(a, 'owner', [(z * ROWS + y, to[z] * ROWS + y) for z in range...]
    ppermute x13 -> x8, starting transfers between devices: 18.1 us -> 16.2 us  [move(): lax.ppermute(a, 'owner', [(z * ROWS + y, to[z] * ROWS + y) for z in range...]
    pallas_call x1, Pallas kernels: 4.6 us -> 3.51 us  [prep(): pl.pallas_call(lambda *refs: prep_kernel(hot, *refs), out_shape=(shape((d...]
    pallas_call x6, Pallas kernels: 7.89 us -> 6.95 us  [score(): pl.pallas_call(lambda *refs: score_kernel(plan, docs, hot, len(before), f...]
    unnamed x22 -> x24, local copies, waits for them, and re-layouts: 1.77 us -> 1.77 us
  transfers between devices with their start and end apart: 19 -> 14, of which waited for: 9 -> 6; matrix products, arithmetic and copies ran while one was open for 0% -> 0% of each run, Pallas kernels for 8% -> 7%
where the time goes in v4:
time: 73.4 us; the launch traced here: 73.2 us
  waiting for transfers between devices  24.1 us (33%)
  starting transfers between devices  21.2 us (29%)
  between operations  14.2 us (19%)
  Pallas kernels  11.9 us (16%)
  local copies, waits for them, and re-layouts  1.77 us (2%)
    ppermute x8, waiting for transfers between devices, move(): lax.ppermute(a, 'owner', [(z * ROWS + y, to[z] * ROWS + y) for z in range...  23.5 us
    ppermute x8, starting transfers between devices, move(): lax.ppermute(a, 'owner', [(z * ROWS + y, to[z] * ROWS + y) for z in range...  16.2 us
    pallas_call x6, Pallas kernels, score(): pl.pallas_call(lambda *refs: score_kernel(plan, docs, hot, len(before), f...  6.95 us
    pallas_call x1, Pallas kernels, prep(): pl.pallas_call(lambda *refs: prep_kernel(hot, *refs), out_shape=(shape((d...  3.51 us
    ppermute x2, starting transfers between devices, other_row(): return lax.ppermute(a, 'owner', [(i, i ^ 1) for i in range(owners)])  3.4 us
    unnamed x24, local copies, waits for them, and re-layouts  1.77 us
    ppermute x3, starting transfers between devices, other_core(): return lax.ppermute(a, 'split', [(0, 1), (1, 0)])  1.57 us
    pallas_call x1, Pallas kernels, finish(): pl.pallas_call(lambda *refs: finish_kernel(flag, *refs), out_shape=(jax.S...  1.47 us
  transfers between devices with their start and end apart: 14, of which 6 were waited for; matrix products, arithmetic and copies ran while one was open for 0% of the time, Pallas kernels for 7%

profile of v4, /device:TPU:0, one launch (start us, length us, event | category | flops | bytes accessed | tf_op | source)
XLA Modules:
  0.0 73.2 jit_solution(787308938616092105)
XLA Ops:
  6.5 3.5 %prep.1 = (bf16[528,768]{1,0:T(8,128)(2,1)S(1)}, bf16[336,768]{1,0:T(8,128)(2,1)S(1)}, bf16[336,768]{1,0:T(8,128)(2,1)S(1)}, s32[1,512]{1,0:T(1,128)S(1)}) custom-call(s32[1]{0:T(128)} %bitcast.8.refs_0_, s32[1,512]{1,0:T(1,128)} %bitcast.36, bf16[512,1024]{1,0:T(8,128)(2,1)} %refs_2_.1, bf16[1024,768]{1,0:T(8,128)(2,1)} %refs_3_.1), custom_call_target="tpu_custom_call" | custom-call | tf_op jit(solution)/shard_map/prep/pallas_call | solution.py:197
  10.1 0.5 collective-permute-start
  10.6 2.6 %collective-permute-start.1 = (bf16[528,768]{1,0:T(8,128)(2,1)S(1)}, bf16[528,768]{1,0:T(8,128)(2,1)S(1)}, u32[]{:S(2)}, u32[]{:S(2)}) collective-permute-start(bf16[528,768]{1,0:T(8,128)(2,1)S(1)} %get-tuple-element.206.refs_1_.refs_2_.refs_3_.refs_8_.refs_9_.refs_14_.refs_10_.refs_12_), channel_id=1, source_target_pairs={{0,2},{2,0},{4,6},{6,4},{8,10},{10,8},{12,14},{14,12},{1,3},{3,1},... | collective-permute-start | bytes 2433032 | tf_op jit(solution)/shard_map/ppermute | solution.py:336
  13.2 0.7 collective-permute-start.3
  13.9 4.4 %collective-permute-start.2 = (bf16[336,768]{1,0:T(8,128)(2,1)S(1)}, bf16[336,768]{1,0:T(8,128)(2,1)S(1)}, u32[]{:S(2)}, u32[]{:S(2)}) collective-permute-start(bf16[336,768]{1,0:T(8,128)(2,1)S(1)} %get-tuple-element.221), channel_id=1, source_target_pairs={{0,4},{2,6},{4,0},{6,2},{8,12},{10,14},{12,8},{14,10},{1,5},{3,7},... | collective-permute-start | bytes 1548296 | tf_op jit(solution)/shard_map/ppermute | solution.py:322
  18.3 3.3 %collective-permute-start.5 = (bf16[336,768]{1,0:T(8,128)(2,1)S(1)}, bf16[336,768]{1,0:T(8,128)(2,1)S(1)}, u32[]{:S(2)}, u32[]{:S(2)}) collective-permute-start(bf16[336,768]{1,0:T(8,128)(2,1)S(1)} %get-tuple-element.221), channel_id=1, source_target_pairs={{0,12},{2,14},{4,4},{6,6},{8,8},{10,10},{12,0},{14,2},{1,13},{3,15... | collective-permute-start | bytes 1548296 | tf_op jit(solution)/shard_map/ppermute | solution.py:322
  21.6 1.0 %near.1 = (f32[1,640]{1,0:T(1,128)S(1)}, f32[1,640]{1,0:T(1,128)S(1)}, f32[1,640]{1,0:T(1,128)S(1)}, f32[1,640]{1,0:T(1,128)S(1)}, f32[1,640]{1,0:T(1,128)S(1)},...) custom-call(s32[1]{0:T(128)} %bitcast.8.refs_0_, ...), custom_call_target="tpu_custom_call" | custom-call | flops 278528 | bytes 1024 | tf_op jit(solution)/shard_map/near/pallas_call | solution.py:277
  22.6 7.8 %collective-permute-done.2.refs_8_.refs_9_.refs_10_.refs_11_.refs_12_.refs_13_ = bf16[336,768]{1,0:T(8,128)(2,1)S(1)} collective-permute-done((bf16[336,768]{1,0:T(8,128)(2,1)S(1)}, bf16[336,768]{1,0:T(8,128)(2,1)S(1)}, u32[]{:S(2)}, u32[]{:S(2)}) %collective-permute-start.2) | collective-permute-done | bytes 516128 | tf_op jit(solution)/shard_map/ppermute | solution.py:322
  30.4 0.7 collective-permute-start.7
  31.1 4.2 %collective-permute-start.6 = (bf16[336,768]{1,0:T(8,128)(2,1)S(1)}, bf16[336,768]{1,0:T(8,128)(2,1)S(1)}, u32[]{:S(2)}, u32[]{:S(2)}) collective-permute-start(bf16[336,768]{1,0:T(8,128)(2,1)S(1)} %collective-permute-done.3.refs_12_.refs_13_.refs_14_.refs_15_), channel_id=1, source_target_pairs={{0,4},{2,6},{4,0},{6,2},{8,12},{10,14},{12,8},{14,10},{1,5},{3,7},... | collective-permute-start | bytes 1548296 | tf_op jit(solution)/shard_map/ppermute | solution.py:322
  35.4 0.6 own_far.1
  36.0 1.1 %hop1.1 = (f32[1,640]{1,0:T(1,128)S(1)}, f32[1,640]{1,0:T(1,128)S(1)}, f32[1,640]{1,0:T(1,128)S(1)}, f32[1,640]{1,0:T(1,128)S(1)}, f32[1,640]{1,0:T(1,128)S(1)},...) custom-call(s32[1]{0:T(128)} %bitcast.8.refs_0_, f32[1,640]{1,0:T(1,128)S(1)} %get-tuple-element.214.refs_1_, ...), custom_call_target="tpu_custom_call" | custom-call | flops 82141249536 | bytes 1024 | tf_op jit(solution)/shard_map/hop1/pallas_call | solution.py:277
  37.1 0.6 collective-permute-done.4.refs_16_.refs_13_.refs_15_
  37.7 1.2 %far.1 = (f32[1,640]{1,0:T(1,128)S(1)}, f32[1,640]{1,0:T(1,128)S(1)}, f32[1,640]{1,0:T(1,128)S(1)}, f32[1,640]{1,0:T(1,128)S(1)}, f32[1,640]{1,0:T(1,128)S(1)}, ...) custom-call(s32[1]{0:T(128)} %bitcast.8.refs_0_, f32[1,640]{1,0:T(1,128)S(1)} %get-tuple-element.225.refs_1_, ...), custom_call_target="tpu_custom_call" | custom-call | flops 557056 | bytes 1024 | tf_op jit(solution)/shard_map/far/pallas_call | solution.py:277
  39.0 4.4 %collective-permute-done.5.refs_8_.refs_9_ = bf16[336,768]{1,0:T(8,128)(2,1)S(1)} collective-permute-done((bf16[336,768]{1,0:T(8,128)(2,1)S(1)}, bf16[336,768]{1,0:T(8,128)(2,1)S(1)}, u32[]{:S(2)}, u32[]{:S(2)}) %collective-permute-start.5) | collective-permute-done | bytes 516128 | tf_op jit(solution)/shard_map/ppermute | solution.py:322
  43.4 1.4 %hop3.1 = (f32[1,640]{1,0:T(1,128)S(1)}, f32[1,640]{1,0:T(1,128)S(1)}, f32[1,640]{1,0:T(1,128)S(1)}, f32[1,640]{1,0:T(1,128)S(1)}, f32[1,640]{1,0:T(1,128)S(1)},...) custom-call(s32[1]{0:T(128)} %bitcast.8.refs_0_, f32[1,640]{1,0:T(1,128)S(1)} %get-tuple-element.232.refs_1_, ...), custom_call_target="tpu_custom_call" | custom-call | flops 557056 | bytes 1024 | tf_op jit(solution)/shard_map/hop3/pallas_call | solution.py:277
  44.8 8.5 %collective-permute-done.6.refs_8_.refs_9_ = bf16[336,768]{1,0:T(8,128)(2,1)S(1)} collective-permute-done((bf16[336,768]{1,0:T(8,128)(2,1)S(1)}, bf16[336,768]{1,0:T(8,128)(2,1)S(1)}, u32[]{:S(2)}, u32[]{:S(2)}) %collective-permute-start.6) | collective-permute-done | bytes 516128 | tf_op jit(solution)/shard_map/ppermute | solution.py:322
  53.3 1.5 %hop2.1 = (f32[1,640]{1,0:T(1,128)S(1)}, f32[1,640]{1,0:T(1,128)S(1)}, f32[1,640]{1,0:T(1,128)S(1)}, f32[1,640]{1,0:T(1,128)S(1)}, f32[1,640]{1,0:T(1,128)S(1)},...) custom-call(s32[1]{0:T(128)} %bitcast.8.refs_0_, f32[1,640]{1,0:T(1,128)S(1)} %get-tuple-element.239.refs_1_, ...), custom_call_target="tpu_custom_call" | custom-call | flops 1114112 | bytes 1024 | tf_op jit(solution)/shard_map/hop2/pallas_call | solution.py:277
  54.9 0.6 copy-done
  55.5 1.8 %collective-permute-start.8 = (f32[1,640]{1,0:T(1,128)S(1)}, f32[1,640]{1,0:T(1,128)S(1)}, u32[]{:S(2)}, u32[]{:S(2)}) collective-permute-start(f32[1,640]{1,0:T(1,128)S(1)} %get-tuple-element.246), channel_id=1, source_target_pairs={{0,12},{2,14},{4,0},{6,2},{8,4},{10,6},{12,8},{14,10},{1,13},{3,15... | collective-permute-start | bytes 7688 | tf_op jit(solution)/shard_map/ppermute | solution.py:322
  57.2 0.4 collective-permute-start.9
  57.6 0.8 %collective-permute-start.10 = (f32[1,640]{1,0:T(1,128)S(1)}, f32[1,640]{1,0:T(1,128)S(1)}, u32[]{:S(2)}, u32[]{:S(2)}) collective-permute-start(f32[1,640]{1,0:T(1,128)S(1)} %get-tuple-element.248), channel_id=1, source_target_pairs={{0,4},{2,6},{4,8},{6,10},{8,12},{10,14},{12,0},{14,2},{1,5},{3,7},... | collective-permute-start | bytes 7688 | tf_op jit(solution)/shard_map/ppermute | solution.py:322
  58.4 0.8 %collective-permute-start.12 = (f32[1,640]{1,0:T(1,128)S(1)}, f32[1,640]{1,0:T(1,128)S(1)}, u32[]{:S(2)}, u32[]{:S(2)}) collective-permute-start(f32[1,640]{1,0:T(1,128)S(1)} %get-tuple-element.250), channel_id=1, source_target_pairs={{0,2},{2,0},{4,6},{6,4},{8,10},{10,8},{12,14},{14,12},{1,3},{3,1},... | collective-permute-start | bytes 7688 | tf_op jit(solution)/shard_map/ppermute | solution.py:336
  59.2 1.1 %collective-permute-start.13 = (f32[1,640]{1,0:T(1,128)S(1)}, f32[1,640]{1,0:T(1,128)S(1)}, u32[]{:S(2)}, u32[]{:S(2)}) collective-permute-start(f32[1,640]{1,0:T(1,128)S(1)} %get-tuple-element.251), channel_id=1, source_target_pairs={{0,1},{1,0},{2,3},{3,2},{4,5},{5,4},{6,7},{7,6},{8,9},{9,8},{10,11... | collective-permute-start | bytes 7688 | tf_op jit(solution)/shard_map/ppermute | solution.py:339
  60.2 1.5 %collective-permute-done.9.refs_2_ = f32[1,640]{1,0:T(1,128)S(1)} collective-permute-done((f32[1,640]{1,0:T(1,128)S(1)}, f32[1,640]{1,0:T(1,128)S(1)}, u32[]{:S(2)}, u32[]{:S(2)}) %collective-permute-start.9) | collective-permute-done | bytes 2592 | tf_op jit(solution)/shard_map/ppermute | solution.py:322
  61.7 1.3 %collective-permute-done.10.refs_3_ = f32[1,640]{1,0:T(1,128)S(1)} collective-permute-done((f32[1,640]{1,0:T(1,128)S(1)}, f32[1,640]{1,0:T(1,128)S(1)}, u32[]{:S(2)}, u32[]{:S(2)}) %collective-permute-start.10) | collective-permute-done | bytes 2592 | tf_op jit(solution)/shard_map/ppermute | solution.py:322
  63.1 0.5 copy-done.10
  63.6 0.0 copy-done.11
  63.6 0.0 copy-done.12
  63.6 0.0 copy-done.13
  63.6 1.5 %finish.1 = (f32[1,512]{1,0:T(1,128)S(1)}, s32[1,1]{1,0:T(1,128)}) custom-call(s32[1,512]{1,0:T(1,128)} %copy-done.1, f32[1,640]{1,0:T(1,128)} %copy-done.8, f32[1,640]{1,0:T(1,128)} %copy-done.9, f32[1,640]{1,0:T(1,128)} %copy-done.10, f32[1,640]{1,0:T(1,128)} %copy-done.11, f32[1,640]{1,0:T(1,128)} %copy-done.12, f32[1,640]{1,0:T(1,128)} %copy-done.13, ...), custom_call_target="tpu_custom_call" | custom-call | tf_op jit(solution)/shard_map/finish/pallas_call | solution.py:303
  65.8 0.6 copy-done.14
  (29 shorter events, 0.1 us)
Async XLA Ops:
  10.0 26.0 %copy-start.1 = (s32[1,512]{1,0:T(1,128)}, s32[1,512]{1,0:T(1,128)S(1)}, u32[]{:S(2)}) copy-start(s32[1,512]{1,0:T(1,128)S(1)} %get-tuple-element.205.refs_0_) | copy-start | bytes 6148
  10.1 11.5 %collective-permute-start = (bf16[528,768]{1,0:T(8,128)(2,1)S(1)}, bf16[528,768]{1,0:T(8,128)(2,1)S(1)}, u32[]{:S(2)}, u32[]{:S(2)}) collective-permute-start(bf16[528,768]{1,0:T(8,128)(2,1)S(1)} %get-tuple-element.206.refs_1_.refs_2_.refs_3_.refs_8_.refs_9_.refs_14_.refs_10_.refs_12_), channel_id=1, source_target_pairs={{0,1},{1,0},{2,3},{3,2},{4,5},{5,4},{6,7},{7,6},{8,9},{9,8},{10,11... | collective-permute-start | bytes 2433032 | tf_op jit(solution)/shard_map/ppermute | solution.py:339
  10.6 24.8 %collective-permute-start.1 = (bf16[528,768]{1,0:T(8,128)(2,1)S(1)}, bf16[528,768]{1,0:T(8,128)(2,1)S(1)}, u32[]{:S(2)}, u32[]{:S(2)}) collective-permute-start(bf16[528,768]{1,0:T(8,128)(2,1)S(1)} %get-tuple-element.206.refs_1_.refs_2_.refs_3_.refs_8_.refs_9_.refs_14_.refs_10_.refs_12_), channel_id=1, source_target_pairs={{0,2},{2,0},{4,6},{6,4},{8,10},{10,8},{12,14},{14,12},{1,3},{3,1},... | collective-permute-start | bytes 2433032 | tf_op jit(solution)/shard_map/ppermute | solution.py:336
  13.2 9.5 %collective-permute-start.3 = (bf16[336,768]{1,0:T(8,128)(2,1)S(1)}, bf16[336,768]{1,0:T(8,128)(2,1)S(1)}, u32[]{:S(2)}, u32[]{:S(2)}) collective-permute-start(bf16[336,768]{1,0:T(8,128)(2,1)S(1)} %get-tuple-element.222), channel_id=1, source_target_pairs={{0,0},{2,2},{4,8},{6,10},{8,4},{10,6},{12,12},{14,14},{1,1},{3,3},... | collective-permute-start | bytes 1548296 | tf_op jit(solution)/shard_map/ppermute | solution.py:322
  13.9 16.6 %collective-permute-start.2 = (bf16[336,768]{1,0:T(8,128)(2,1)S(1)}, bf16[336,768]{1,0:T(8,128)(2,1)S(1)}, u32[]{:S(2)}, u32[]{:S(2)}) collective-permute-start(bf16[336,768]{1,0:T(8,128)(2,1)S(1)} %get-tuple-element.221), channel_id=1, source_target_pairs={{0,4},{2,6},{4,0},{6,2},{8,12},{10,14},{12,8},{14,10},{1,5},{3,7},... | collective-permute-start | bytes 1548296 | tf_op jit(solution)/shard_map/ppermute | solution.py:322
  18.3 25.1 %collective-permute-start.5 = (bf16[336,768]{1,0:T(8,128)(2,1)S(1)}, bf16[336,768]{1,0:T(8,128)(2,1)S(1)}, u32[]{:S(2)}, u32[]{:S(2)}) collective-permute-start(bf16[336,768]{1,0:T(8,128)(2,1)S(1)} %get-tuple-element.221), channel_id=1, source_target_pairs={{0,12},{2,14},{4,4},{6,6},{8,8},{10,10},{12,0},{14,2},{1,13},{3,15... | collective-permute-start | bytes 1548296 | tf_op jit(solution)/shard_map/ppermute | solution.py:322
  30.4 14.3 %collective-permute-start.7 = (bf16[336,768]{1,0:T(8,128)(2,1)S(1)}, bf16[336,768]{1,0:T(8,128)(2,1)S(1)}, u32[]{:S(2)}, u32[]{:S(2)}) collective-permute-start(bf16[336,768]{1,0:T(8,128)(2,1)S(1)} %collective-permute-done.2.refs_8_.refs_9_.refs_10_.refs_11_.refs_12_.refs_13_), channel_id=1, source_target_pairs={{0,0},{2,2},{4,8},{6,10},{8,4},{10,6},{12,12},{14,14},{1,1},{3,3},... | collective-permute-start | bytes 1548296 | tf_op jit(solution)/shard_map/ppermute | solution.py:322
  31.1 22.2 %collective-permute-start.6 = (bf16[336,768]{1,0:T(8,128)(2,1)S(1)}, bf16[336,768]{1,0:T(8,128)(2,1)S(1)}, u32[]{:S(2)}, u32[]{:S(2)}) collective-permute-start(bf16[336,768]{1,0:T(8,128)(2,1)S(1)} %collective-permute-done.3.refs_12_.refs_13_.refs_14_.refs_15_), channel_id=1, source_target_pairs={{0,4},{2,6},{4,0},{6,2},{8,12},{10,14},{12,8},{14,10},{1,5},{3,7},... | collective-permute-start | bytes 1548296 | tf_op jit(solution)/shard_map/ppermute | solution.py:322
  35.4 2.3 %collective-permute-start.4 = (bf16[528,768]{1,0:T(8,128)(2,1)S(1)}, bf16[528,768]{1,0:T(8,128)(2,1)S(1)}, u32[]{:S(2)}, u32[]{:S(2)}) collective-permute-start(bf16[528,768]{1,0:T(8,128)(2,1)S(1)} %collective-permute-done.1.refs_10_.refs_16_.refs_12_.refs_14_), channel_id=1, source_target_pairs={{0,1},{1,0},{2,3},{3,2},{4,5},{5,4},{6,7},{7,6},{8,9},{9,8},{10,11... | collective-permute-start | bytes 2433032 | tf_op jit(solution)/shard_map/ppermute | solution.py:339
  53.3 12.4 %copy-start.4 = (bf16[1024,768]{1,0:T(8,128)(2,1)S(1)}, bf16[1024,768]{1,0:T(8,128)(2,1)}, u32[]{:S(2)}) copy-start(bf16[1024,768]{1,0:T(8,128)(2,1)} %refs_3_.1) | copy-start | bytes 4718596
  53.3 12.4 %copy-start.5 = (bf16[512,1024]{1,0:T(8,128)(2,1)S(1)}, bf16[512,1024]{1,0:T(8,128)(2,1)}, u32[]{:S(2)}) copy-start(bf16[512,1024]{1,0:T(8,128)(2,1)} %refs_2_.1) | copy-start | bytes 3145732
  53.3 12.4 %copy-start.7 = (s32[512]{0:T(512)S(1)}, s32[512]{0:T(512)}, u32[]{:S(2)}) copy-start(s32[512]{0:T(512)} %param.9) | copy-start | bytes 6148
  54.9 0.6 copy-start
  55.5 3.7 %collective-permute-start.8 = (f32[1,640]{1,0:T(1,128)S(1)}, f32[1,640]{1,0:T(1,128)S(1)}, u32[]{:S(2)}, u32[]{:S(2)}) collective-permute-start(f32[1,640]{1,0:T(1,128)S(1)} %get-tuple-element.246), channel_id=1, source_target_pairs={{0,12},{2,14},{4,0},{6,2},{8,4},{10,6},{12,8},{14,10},{1,13},{3,15... | collective-permute-start | bytes 7688 | tf_op jit(solution)/shard_map/ppermute | solution.py:322
  57.2 4.5 %collective-permute-start.9 = (f32[1,640]{1,0:T(1,128)S(1)}, f32[1,640]{1,0:T(1,128)S(1)}, u32[]{:S(2)}, u32[]{:S(2)}) collective-permute-start(f32[1,640]{1,0:T(1,128)S(1)} %get-tuple-element.247), channel_id=1, source_target_pairs={{0,8},{2,10},{4,12},{6,14},{8,0},{10,2},{12,4},{14,6},{1,9},{3,11}... | collective-permute-start | bytes 7688 | tf_op jit(solution)/shard_map/ppermute | solution.py:322
  57.6 5.4 %collective-permute-start.10 = (f32[1,640]{1,0:T(1,128)S(1)}, f32[1,640]{1,0:T(1,128)S(1)}, u32[]{:S(2)}, u32[]{:S(2)}) collective-permute-start(f32[1,640]{1,0:T(1,128)S(1)} %get-tuple-element.248), channel_id=1, source_target_pairs={{0,4},{2,6},{4,8},{6,10},{8,12},{10,14},{12,0},{14,2},{1,5},{3,7},... | collective-permute-start | bytes 7688 | tf_op jit(solution)/shard_map/ppermute | solution.py:322
  58.4 4.6 %collective-permute-start.11 = (f32[1,640]{1,0:T(1,128)S(1)}, f32[1,640]{1,0:T(1,128)S(1)}, u32[]{:S(2)}, u32[]{:S(2)}) collective-permute-start(f32[1,640]{1,0:T(1,128)S(1)} %get-tuple-element.249), channel_id=1, source_target_pairs={{0,3},{1,2},{2,1},{3,0},{4,7},{5,6},{6,5},{7,4},{8,11},{9,10},{10,... | collective-permute-start | bytes 7688 | tf_op jit(solution)/shard_map/ppermute | solution.py:342
  58.4 4.6 %collective-permute-start.12 = (f32[1,640]{1,0:T(1,128)S(1)}, f32[1,640]{1,0:T(1,128)S(1)}, u32[]{:S(2)}, u32[]{:S(2)}) collective-permute-start(f32[1,640]{1,0:T(1,128)S(1)} %get-tuple-element.250), channel_id=1, source_target_pairs={{0,2},{2,0},{4,6},{6,4},{8,10},{10,8},{12,14},{14,12},{1,3},{3,1},... | collective-permute-start | bytes 7688 | tf_op jit(solution)/shard_map/ppermute | solution.py:336
  59.2 3.9 %copy-start.8 = (f32[1,640]{1,0:T(1,128)}, f32[1,640]{1,0:T(1,128)S(1)}, u32[]{:S(2)}) copy-start(f32[1,640]{1,0:T(1,128)S(1)} %collective-permute-done.8.refs_1_) | copy-start | bytes 7684
  59.2 3.8 %collective-permute-start.13 = (f32[1,640]{1,0:T(1,128)S(1)}, f32[1,640]{1,0:T(1,128)S(1)}, u32[]{:S(2)}, u32[]{:S(2)}) collective-permute-start(f32[1,640]{1,0:T(1,128)S(1)} %get-tuple-element.251), channel_id=1, source_target_pairs={{0,1},{1,0},{2,3},{3,2},{4,5},{5,4},{6,7},{7,6},{8,9},{9,8},{10,11... | collective-permute-start | bytes 7688 | tf_op jit(solution)/shard_map/ppermute | solution.py:339
  61.7 1.3 %copy-start.9 = (f32[1,640]{1,0:T(1,128)}, f32[1,640]{1,0:T(1,128)S(1)}, u32[]{:S(2)}) copy-start(f32[1,640]{1,0:T(1,128)S(1)} %collective-permute-done.9.refs_2_) | copy-start | bytes 7684
  63.0 0.6 copy-start.10
  63.0 0.6 copy-start.11
  63.0 0.6 copy-start.12
  63.0 0.6 copy-start.13
  65.8 0.6 copy-start.14

commit v5 on v4

--- a/solution.py
+++ b/solution.py
@@ -122,7 +122,7 @@
     return rest, first, flag, up(flag + 1, 128)
 
 
-def prep_kernel(hot, place_ref, cl_ref, st_ref, w_ref, q_ref, even_ref, odd_ref, slot_ref, vectors):
+def prep_kernel(hot, place_ref, cl_ref, st_ref, w_ref, same_ref, other_ref, slot_ref, vectors):
     docs = st_ref.shape[0]
     rest, first, flag, lanes = layout(docs, hot)
     tile = 128
@@ -159,34 +159,32 @@
     ids = lax.dot_general(
         cluster_rows, sort, (((1,), (1,)), ((), ())), preferred_element_type=F32
     )
-    ids = jnp.where(lax.broadcasted_iota(jnp.int32, ids.shape, 1) == flag, doubt, ids).astype(BF16)
-
-    q_ref[:rest, :] = sorted_n
-    q_ref[rest:docs, :] = sorted_h
-    q_ref[docs:, :] = jnp.zeros((META, q_ref.shape[1]), BF16)
-    q_ref[docs:, :lanes] = ids
+    ids = ids.astype(BF16)
+
 
     def fill_n(ref):
         ref[:rest, :] = sorted_n
         ref[rest:, :] = jnp.zeros((META, ref.shape[1]), BF16)
         ref[rest:, :first] = ids[:, :first]
+        ref[rest:, first:first + 128] = jnp.broadcast_to(doubt.astype(BF16), (META, 128))
 
     def fill_h(ref):
         ref[:hot, :] = sorted_h
         ref[hot:, :] = jnp.zeros((rest + META - hot, ref.shape[1]), BF16)
         ref[rest:, :lanes - first] = ids[:, first:]
+        ref[rest:, first:first + 128] = jnp.broadcast_to(doubt.astype(BF16), (META, 128))
 
     even = lax.rem(place_ref[0], 2) == 0
 
     @pl.when(even)
     def _():
-        fill_h(even_ref)
-        fill_n(odd_ref)
+        fill_h(same_ref)
+        fill_n(other_ref)
 
     @pl.when(jnp.logical_not(even))
     def _():
-        fill_n(even_ref)
-        fill_h(odd_ref)
+        fill_n(same_ref)
+        fill_h(other_ref)
 
 
 def prep(hot, place, cluster_of, states, proj_weight):
@@ -197,7 +195,6 @@
     return pl.pallas_call(
         lambda *refs: prep_kernel(hot, *refs),
         out_shape=(
-            shape((docs + META, width), BF16),
             shape((rest + META, width), BF16),
             shape((rest + META, width), BF16),
             shape((1, docs), jnp.int32),
@@ -209,82 +206,87 @@
     )(place, cluster_of.reshape(1, docs), states, proj_weight)
 
 
-OWN = 3
-SUMS = 7
-
-
-def score_kernel(plan, docs, hot, carries, flags, outs, *refs):
-    moving, stills = plan
+OWN, PAIR = "own", "pair"
+CORE, PAIR_CORE = "core", "pair_core"
+ROW, PAIR_ROW = "row", "pair_row"
+DIAG, PAIR_DIAG = "diag", "pair_diag"
+NEXT, FAR = "next", "far"
+
+
+def score_kernel(docs, hot, names, tasks, carried, made, flagged, *refs):
     rest, first, flag, lanes = layout(docs, hot)
     place_ref, refs = refs[0], refs[1:]
-    before, refs = refs[:carries], refs[carries:]
-    move_refs, refs = refs[:len(moving)], refs[len(moving):]
-    still_refs, out_refs = refs[:len(stills)], dict(zip(outs, refs[len(stills):]))
-    z = place_ref[0]
-    for k, target in enumerate(outs):
-        out_refs[target][...] = before[k][...] if carries else jnp.zeros((1, lanes), F32)
-    metas = [ref[docs:docs + META, :].astype(F32)[0:1, :] for ref in still_refs]
-    span = {"n": (0, slice(0, rest), slice(0, rest)), "h": (first, slice(rest, docs), slice(first, flag))}
-
-    for (kind, target, holder), move_ref in zip(moving, move_refs):
-
-        def work(kind=kind, target=target, move_ref=move_ref):
-            start, rows, lane = span[kind]
-            count = rows.stop - rows.start
-            if target == OWN:
-                block = move_ref[rows, :]
-                ids = move_ref[docs:docs + META, :].astype(F32)[0:8, lane]
+    blocks, refs = dict(zip(names, refs[:len(names)])), refs[len(names):]
+    before, sums = dict(zip(carried, refs[:len(carried)])), dict(zip(made, refs[len(carried):]))
+    z, y, c = place_ref[0], place_ref[1], place_ref[2]
+    for name in made:
+        sums[name][...] = before[name][...] if name in before else jnp.zeros((1, lanes), F32)
+    when = {"core0": c == 0, "core1": c == 1, "row0": y == 0, "row1": y == 1}
+    middle = (z == 1) | (z == 2)
+
+    def meet(count, start):
+        lane = slice(start, start + count)
+        ids = {name: ref[rest:, :].astype(F32)[0:8, 0:count] for name, ref in blocks.items()}
+        for row in dict.fromkeys(task[0] for task in tasks):
+
+            def work(row=row):
+                row_ids = ids[row].T[:, 0:1]
+                for _, col, condition in [task for task in tasks if task[0] == row]:
+
+                    def one(col=col):
+                        inner = lax.dot_general(
+                            blocks[row][:count, :], blocks[col][:count, :], (((1,), (1,)), ((), ())),
+                            preferred_element_type=F32,
+                        )
+                        same = row_ids == ids[col][0:1, :]
+                        if row == col:
+                            same &= lax.broadcasted_iota(jnp.int32, inner.shape, 0) != lax.broadcasted_iota(
+                                jnp.int32, inner.shape, 1
+                            )
+                        weights = jnp.where(same, jnp.exp2(inner), 0.0)
+                        if row != col:
+                            total = jnp.sum(weights, axis=1, keepdims=True)
+                            sums[row][:, lane] += jnp.broadcast_to(total, (count, 128)).T[0:1, :]
+                        sums[col][:, lane] += jnp.sum(weights, axis=0, keepdims=True)
+
+                    if condition is None:
+                        one()
+                    else:
+                        pl.when(when[condition])(one)
+
+            if row in (NEXT, FAR):
+                pl.when(middle)(work)
             else:
-                block = move_ref[:count, :]
-                ids = move_ref[rest:rest + META, :].astype(F32)[0:8, 0:count]
-            ids = ids.T[:, 0:1]
-            total = jnp.zeros((count, 1), F32)
-            for still, still_ref, still_ids in zip(stills, still_refs, metas):
-                inner = lax.dot_general(
-                    block, still_ref[rows, :], (((1,), (1,)), ((), ())), preferred_element_type=F32
-                )
-                same = ids == still_ids[:, lane]
-                if target == OWN and still == OWN:
-                    same &= lax.broadcasted_iota(jnp.int32, inner.shape, 0) != lax.broadcasted_iota(
-                        jnp.int32, inner.shape, 1
-                    )
-                weights = jnp.where(same, jnp.exp2(inner), 0.0)
-                total += jnp.sum(weights, axis=1, keepdims=True)
-                if target != OWN:
-                    out_refs[still][:, lane] += jnp.sum(weights, axis=0, keepdims=True)
-            out_refs[target][:, lane] += jnp.broadcast_to(total, (count, 128)).T[0:1, :]
-
-        if holder is None:
-            work()
-        else:
-            pl.when(z == holder)(work)
-
-    if flags:
-        doubt = metas[0]
-        for other in metas[1:]:
-            doubt = doubt + other
+                work()
+
+    pl.when(lax.rem(z, 2) == 0)(lambda: meet(hot, first))
+    pl.when(lax.rem(z, 2) == 1)(lambda: meet(rest, 0))
+
+    if flagged:
+        doubt = sum(ref[rest:, first:first + 128].astype(F32)[0:1, 0:1] for ref in blocks.values())
         spot = lax.broadcasted_iota(jnp.int32, (1, lanes), 1)
-        for target in range(OWN + 1):
-            out_refs[target][...] += jnp.where(spot == flag, doubt[:, :lanes], 0.0)
-
-
-def score(name, docs, hot, place, before, moving, stills, flags=False, outs=tuple(range(SUMS)), weight=1):
+        for name in flagged:
+            sums[name][...] += jnp.where(spot == flag, doubt, 0.0)
+
+
+def score(name, docs, hot, place, blocks, tasks, sums, flagged=(), weight=1):
     lanes = layout(docs, hot)[3]
-    plan = ([m[1:] for m in moving], [s[1] for s in stills])
+    names = [b for b in blocks if flagged or any(b in task[:2] for task in tasks)]
+    made = [b for b in blocks if any(b in task[:2] for task in tasks)]
+    made += [b for b in flagged if b not in made]
+    carried = [b for b in made if b in sums]
     vmem = pl.BlockSpec(memory_space=pltpu.VMEM)
-    pairs = len(stills) * sum((hot if m[1] == "h" else docs - hot) ** 2 for m in moving)
-    arrays = [*before, *(m[0] for m in moving), *(s[0] for s in stills)]
-    return pl.pallas_call(
-        lambda *refs: score_kernel(plan, docs, hot, len(before), flags, outs, *refs),
-        out_shape=tuple(jax.ShapeDtypeStruct((1, lanes), F32) for _ in outs),
+    arrays = [blocks[b] for b in names] + [sums[b] for b in carried]
+    out = pl.pallas_call(
+        lambda *refs: score_kernel(docs, hot, names, tasks, carried, made, flagged, *refs),
+        out_shape=tuple(jax.ShapeDtypeStruct((1, lanes), F32) for _ in made),
         in_specs=[pl.BlockSpec(memory_space=pltpu.SMEM)] + [vmem] * len(arrays),
-        out_specs=tuple(vmem for _ in outs),
+        out_specs=tuple(vmem for _ in made),
         compiler_params=pltpu.CompilerParams(vmem_limit_bytes=20 * 2**20),
-        cost_estimate=pl.CostEstimate(
-            flops=weight * pairs, bytes_accessed=2**10, transcendentals=0
-        ),
+        cost_estimate=pl.CostEstimate(flops=weight, bytes_accessed=2**10, transcendentals=0),
         name=name,
     )(place, *arrays)
+    return {**sums, **dict(zip(made, out))}
 
 
 def finish_kernel(flag, slot_ref, *refs):
@@ -314,71 +316,76 @@
     hot = 3 * docs // owners
     flag = layout(docs, hot)[2]
 
-    owner = lax.axis_index("owner")
-    place = (owner // ROWS).astype(jnp.int32).reshape(1)
-    q, even, odd, slot = prep(hot, place, cluster_of, states, proj_weight)
-
-    def move(a, to):
+    owner, core = lax.axis_index("owner"), lax.axis_index("split")
+    place = jnp.stack([owner // ROWS, owner % ROWS, core]).astype(jnp.int32)
+    same, other, slot = prep(hot, place, cluster_of, states, proj_weight)
+
+    def move(a, to, row=0, core=0):
+        if not core:
+            return lax.ppermute(
+                a, "owner", [(z * ROWS + y, to[z] * ROWS + (y ^ row)) for z in range(columns) for y in range(ROWS)]
+            )
+        if not row and to == STAY:
+            return lax.ppermute(a, "split", [(0, 1), (1, 0)])
         return lax.ppermute(
-            a, "owner", [(z * ROWS + y, to[z] * ROWS + y) for z in range(columns) for y in range(ROWS)]
+            a, ("owner", "split"),
+            [
+                ((z * ROWS + y) * 2 + c, (to[z] * ROWS + (y ^ row)) * 2 + (c ^ core))
+                for z in range(columns) for y in range(ROWS) for c in range(2)
+            ],
         )
 
-    def outer(a):
-        return move(a, (1, 0, 3, 2))
-
-    def middle(a):
-        return move(a, (0, 2, 1, 3))
-
-    def ends(a):
-        return move(a, (3, 1, 2, 0))
-
-    def other_row(a):
-        return lax.ppermute(a, "owner", [(i, i ^ 1) for i in range(owners)])
-
-    def other_core(a):
-        return lax.ppermute(a, "split", [(0, 1), (1, 0)])
-
-    def across(a):
-        return lax.ppermute(a, ("owner", "split"), [(i, i ^ 3) for i in range(2 * owners)])
-
-    def ahead(a, step):
-        return move(a, tuple((z + step) % columns for z in range(columns)))
-
-    def after(a, *others):
-        return lax.optimization_barrier((a, *others))[0]
-
-    def meet(name, before, moving, stills, **options):
-        return score(name, docs, hot, place, before, moving, stills, **options)
-
-    first_outer = outer(even)
-    first_middle = middle(odd)
-    qy = other_row(q)
-    qc = other_core(q)
-    first_ends = ends(even)
-    own = [(q, "n", OWN, None), (q, "h", OWN, None)]
-    near = [(q, 3), (qc, 4)]
-    sums = meet("near", (), own, near)
-
-    first_outer, first_middle, _ = lax.optimization_barrier((first_outer, first_middle, sums[0]))
-    then_outer = outer(first_middle)
-    then_middle = middle(first_outer)
-    hop1 = [
-        (first_outer, "n", 0, 0), (first_outer, "h", 2, 1), (first_outer, "n", 0, 2), (first_outer, "h", 2, 3),
-        (first_middle, "n", 0, 1), (first_middle, "h", 2, 2),
+    STAY, OUTER, MIDDLE, TWO = (0, 1, 2, 3), (1, 0, 3, 2), (0, 2, 1, 3), (2, 3, 0, 1)
+    TO_MIDDLE = (2, 0, 3, 1)
+
+    def meet(name, tasks, **options):
+        return score(name, docs, hot, place, blocks, tasks, sums, **options)
+
+    blocks, sums = {OWN: same}, {}
+    blocks[PAIR] = move(other, OUTER)
+    blocks[ROW] = move(same, STAY, row=1)
+    blocks[NEXT] = move(other, MIDDLE)
+    blocks[CORE] = move(same, STAY, core=1)
+    blocks[FAR] = move(same, TO_MIDDLE)
+    sums = meet("own", [(OWN, OWN, None), (OWN, CORE, "core0")], weight=2**33)
+
+    pair, blocks[NEXT], _ = lax.optimization_barrier((blocks[PAIR], blocks[NEXT], sums[OWN]))
+    blocks[PAIR] = pair
+    blocks[PAIR_ROW] = move(pair, STAY, row=1)
+    blocks[PAIR_CORE] = move(pair, STAY, core=1)
+    blocks[DIAG] = move(blocks[ROW], STAY, core=1)
+    sums = meet(
+        "pair", [(PAIR, PAIR, None), (PAIR, OWN, None), (PAIR, CORE, None), (PAIR, PAIR_CORE, "core1")]
+    )
+    sums = meet("next", [(NEXT, b, None) for b in (OWN, CORE, PAIR, PAIR_CORE)], weight=2**33)
+    sums = meet(
+        "row",
+        [(PAIR, ROW, None), (PAIR, DIAG, None), (OWN, ROW, "row0"), (OWN, DIAG, "row1"),
+         (NEXT, ROW, None), (NEXT, DIAG, None)],
+    )
+    blocks[PAIR_ROW], _ = lax.optimization_barrier((blocks[PAIR_ROW], sums[ROW]))
+    blocks[PAIR_DIAG] = move(blocks[PAIR_ROW], STAY, core=1)
+    sums = meet("far", [(FAR, b, None) for b in (OWN, CORE, PAIR, PAIR_CORE, ROW, DIAG)])
+    early = [
+        move(sums[CORE], STAY, core=1),
+        move(sums[PAIR_CORE], OUTER, core=1),
+        move(sums[ROW], STAY, row=1),
+        move(sums[DIAG], STAY, row=1, core=1),
     ]
-    qyc = other_core(qy)
-    sums = meet("own_far", sums, own, [(qy, 5)])
-    sums = meet("hop1", sums, hop1, near + [(qy, 5)], weight=2**16)
-    sums = meet("far", sums, own + hop1, [(qyc, 6)])
-    far = [(qy, 5), (qyc, 6)]
-    hop3 = [(first_ends, "n", 2, 0), (first_ends, "h", 0, 3)]
-    sums = meet("hop3", sums, hop3, near + far, flags=True)
-    hop2 = [
-        (then_outer, "n", 1, 0), (then_outer, "h", 1, 3), (then_middle, "n", 1, 1), (then_middle, "h", 1, 2),
+    sums = meet("pair_row", [(PAIR, PAIR_ROW, "row1"), (NEXT, PAIR_ROW, None), (FAR, PAIR_ROW, None)])
+    sums = meet(
+        "pair_diag",
+        [(PAIR, PAIR_DIAG, "row0"), (NEXT, PAIR_DIAG, None), (FAR, PAIR_DIAG, None)],
+        flagged=(OWN, FAR),
+    )
+    back = early + [
+        move(sums[FAR], TWO),
+        move(sums[NEXT], MIDDLE),
+        move(sums[PAIR_DIAG], OUTER, row=1, core=1),
+        move(sums[PAIR_ROW], OUTER, row=1),
+        move(sums[PAIR], OUTER),
+        sums[OWN],
     ]
-    sums = meet("hop2", sums, hop2, near + far)
-    back = [ahead(sums[i], i + 1) for i in (2, 1, 0)]
-    back += [across(sums[6]), other_row(sums[5]), other_core(sums[4]), sums[OWN]]
     fast, doubt = finish(flag, slot, back)
     return lax.cond(
         doubt[0, 0] > 0, owner_plan, lambda *_: fast.reshape(docs), states, proj_weight, cluster_of

time: 73.4 us -> 73.8 us (level)
  starting transfers between devices: 21.2 us -> 24.2 us
  waiting for transfers between devices: 24.1 us -> 21.1 us
    ppermute x14 -> x18, starting transfers between devices: 21.2 us -> 24.2 us  [the longest x10 19.3 us: move(): lax.ppermute(a, 'owner', [(z * ROWS + y, to[z] * ROWS + (y ^ row)) for z...]
    ppermute x14 -> x18, waiting for transfers between devices: 24.1 us -> 21.1 us  [the longest x10 20.6 us: move(): lax.ppermute(a, 'owner', [(z * ROWS + y, to[z] * ROWS + (y ^ row)) for z...]
    pallas_call x7 -> x8, Pallas kernels: 10.5 us -> 10.5 us  [the longest x7 6.96 us: score(): pl.pallas_call(lambda *refs: score_kernel(docs, hot, names, tasks, carrie...]
    unnamed x24 -> x30, local copies, waits for them, and re-layouts: 1.77 us -> 1.73 us
  transfers between devices with their start and end apart: 14 -> 18, of which waited for: 6 -> 5; matrix products, arithmetic and copies ran while one was open for 0% -> 0% of each run, Pallas kernels for 7% -> 9%
where the time goes in v5:
time: 73.8 us; the launch traced here: 73.6 us
  starting transfers between devices  24.2 us (33%)
  waiting for transfers between devices  21.1 us (29%)
  between operations  14.2 us (19%)
  Pallas kernels  12 us (16%)
  local copies, waits for them, and re-layouts  1.73 us (2%)
    ppermute x10, waiting for transfers between devices, move(): lax.ppermute(a, 'owner', [(z * ROWS + y, to[z] * ROWS + (y ^ row)) for z...  20.6 us
    ppermute x10, starting transfers between devices, move(): lax.ppermute(a, 'owner', [(z * ROWS + y, to[z] * ROWS + (y ^ row)) for z...  19.3 us
    pallas_call x7, Pallas kernels, score(): pl.pallas_call(lambda *refs: score_kernel(docs, hot, names, tasks, carrie...  6.96 us
    ppermute x3, starting transfers between devices, move(): lax.ppermute(a, ('owner', 'split'), [((z * ROWS + y) * 2 + c, (to[z] * RO...  4.45 us
    pallas_call x1, Pallas kernels, prep(): pl.pallas_call(lambda *refs: prep_kernel(hot, *refs), out_shape=(shape((r...  3.56 us
    unnamed x30, local copies, waits for them, and re-layouts  1.73 us
  transfers between devices with their start and end apart: 18, of which 5 were waited for; matrix products, arithmetic and copies ran while one was open for 0% of the time, Pallas kernels for 9%

profile of v5, /device:TPU:0, one launch (start us, length us, event | category | flops | bytes accessed | tf_op | source)
XLA Modules:
  0.0 73.6 jit_solution(17316640350626572809)
XLA Ops:
  6.5 0.1 pad_add_fusion.refs_0_
  6.6 3.6 %prep.1 = (bf16[336,768]{1,0:T(8,128)(2,1)S(1)}, bf16[336,768]{1,0:T(8,128)(2,1)S(1)}, s32[1,512]{1,0:T(1,128)S(1)}) custom-call(s32[3]{0:T(128)S(1)} %pad_add_fusion.refs_0_, s32[1,512]{1,0:T(1,128)} %bitcast.38, bf16[512,1024]{1,0:T(8,128)(2,1)} %refs_2_.1, bf16[1024,768]{1,0:T(8,128)(2,1)} %refs_3_.1), custom_call_target="tpu_custom_call" | custom-call | tf_op jit(solution)/shard_map/prep/pallas_call | solution.py:195
  10.2 0.5 collective-permute-start.2
  10.7 0.7 collective-permute-start.1
  11.4 5.5 %collective-permute-start = (bf16[336,768]{1,0:T(8,128)(2,1)S(1)}, bf16[336,768]{1,0:T(8,128)(2,1)S(1)}, u32[]{:S(2)}, u32[]{:S(2)}) collective-permute-start(bf16[336,768]{1,0:T(8,128)(2,1)S(1)} %get-tuple-element.197), channel_id=1, source_target_pairs={{0,4},{2,6},{4,0},{6,2},{8,12},{10,14},{12,8},{14,10},{1,5},{3,7},... | collective-permute-start | bytes 1548296 | tf_op jit(solution)/shard_map/ppermute | solution.py:325
  16.9 1.5 %collective-permute-start.3 = (bf16[336,768]{1,0:T(8,128)(2,1)S(1)}, bf16[336,768]{1,0:T(8,128)(2,1)S(1)}, u32[]{:S(2)}, u32[]{:S(2)}) collective-permute-start(bf16[336,768]{1,0:T(8,128)(2,1)S(1)} %get-tuple-element.196.refs_1_), channel_id=1, source_target_pairs={{0,2},{2,0},{4,6},{6,4},{8,10},{10,8},{12,14},{14,12},{1,3},{3,1},... | collective-permute-start | bytes 1548296 | tf_op jit(solution)/shard_map/ppermute | solution.py:325
  18.4 1.2 %own.1 = (f32[1,640]{1,0:T(1,128)S(1)}, f32[1,640]{1,0:T(1,128)S(1)}) custom-call(s32[3]{0:T(128)S(1)} %pad_add_fusion.refs_0_, bf16[336,768]{1,0:T(8,128)(2,1)S(1)} %get-tuple-element.196.refs_1_, bf16[336,768]{1,0:T(8,128)(2,1)S(1)} %collective-permute-done.2.refs_2_.refs_3_.refs_4_.refs_5_), custom_call_target="tpu_custom_call" | custom-call | flops 8589934592 | bytes 1024 | tf_op jit(solution)/shard_map/own/pallas_call | solution.py:280
  19.6 9.3 %collective-permute-done.refs_2_.refs_1_ = bf16[336,768]{1,0:T(8,128)(2,1)S(1)} collective-permute-done((bf16[336,768]{1,0:T(8,128)(2,1)S(1)}, bf16[336,768]{1,0:T(8,128)(2,1)S(1)}, u32[]{:S(2)}, u32[]{:S(2)}) %collective-permute-start) | collective-permute-done | bytes 516128 | tf_op jit(solution)/shard_map/ppermute | solution.py:325
  29.0 1.6 %collective-permute-start.4 = (bf16[336,768]{1,0:T(8,128)(2,1)S(1)}, bf16[336,768]{1,0:T(8,128)(2,1)S(1)}, u32[]{:S(2)}, u32[]{:S(2)}) collective-permute-start(bf16[336,768]{1,0:T(8,128)(2,1)S(1)} %get-tuple-element.196.refs_1_), channel_id=1, source_target_pairs={{0,8},{2,10},{4,0},{6,2},{8,12},{10,14},{12,4},{14,6},{1,9},{3,11}... | collective-permute-start | bytes 1548296 | tf_op jit(solution)/shard_map/ppermute | solution.py:325
  30.6 1.5 %collective-permute-start.11 = (bf16[336,768]{1,0:T(8,128)(2,1)S(1)}, bf16[336,768]{1,0:T(8,128)(2,1)S(1)}, u32[]{:S(2)}, u32[]{:S(2)}) collective-permute-start(bf16[336,768]{1,0:T(8,128)(2,1)S(1)} %collective-permute-done.refs_2_.refs_1_), channel_id=1, source_target_pairs={{0,2},{2,0},{4,6},{6,4},{8,10},{10,8},{12,14},{14,12},{1,3},{3,1},... | collective-permute-start | bytes 1548296 | tf_op jit(solution)/shard_map/ppermute | solution.py:325
  32.1 1.1 %pair.1 = (f32[1,640]{1,0:T(1,128)S(1)}, f32[1,640]{1,0:T(1,128)S(1)}, f32[1,640]{1,0:T(1,128)S(1)}, f32[1,640]{1,0:T(1,128)S(1)}) custom-call(s32[3]{0:T(128)S(1)} %pad_add_fusion.refs_0_, bf16[336,768]{1,0:T(8,128)(2,1)S(1)} %get-tuple-element.196.refs_1_, bf16[336,768]{1,0:T(8,128)(2,1)S(1)} %collective-permute-done.refs_2_.refs_1_, ...), custom_call_target="tpu_custom_call" | custom-call | flops 1 | bytes 1024 | tf_op jit(solution)/shard_map/pair/pallas_call | solution.py:280
  33.2 0.6 next.1
  33.8 0.2 collective-permute-done.6.refs_5_.refs_7_.refs_9_
  34.0 1.5 %row.1 = (f32[1,640]{1,0:T(1,128)S(1)}, f32[1,640]{1,0:T(1,128)S(1)}, f32[1,640]{1,0:T(1,128)S(1)}, f32[1,640]{1,0:T(1,128)S(1)}, f32[1,640]{1,0:T(1,128)S(1)}) custom-call(s32[3]{0:T(128)S(1)} %pad_add_fusion.refs_0_, bf16[336,768]{1,0:T(8,128)(2,1)S(1)} %get-tuple-element.196.refs_1_, bf16[336,768]{1,0:T(8,128)(2,1)S(1)} %collective-permute-done.refs_2_.refs_1_, ...), custom_call_target="tpu_custom_call" | custom-call | flops 1 | bytes 1024 | tf_op jit(solution)/shard_map/row/pallas_call | solution.py:280
  35.5 9.0 %collective-permute-done.11.refs_4_.refs_7_ = bf16[336,768]{1,0:T(8,128)(2,1)S(1)} collective-permute-done((bf16[336,768]{1,0:T(8,128)(2,1)S(1)}, bf16[336,768]{1,0:T(8,128)(2,1)S(1)}, u32[]{:S(2)}, u32[]{:S(2)}) %collective-permute-start.11) | collective-permute-done | bytes 516128 | tf_op jit(solution)/shard_map/ppermute | solution.py:325
  44.5 0.7 %far.1 = (f32[1,640]{1,0:T(1,128)S(1)}, f32[1,640]{1,0:T(1,128)S(1)}, f32[1,640]{1,0:T(1,128)S(1)}, f32[1,640]{1,0:T(1,128)S(1)}, f32[1,640]{1,0:T(1,128)S(1)}, ...) custom-call(s32[3]{0:T(128)S(1)} %pad_add_fusion.refs_0_, bf16[336,768]{1,0:T(8,128)(2,1)S(1)} %get-tuple-element.196.refs_1_, ...), custom_call_target="tpu_custom_call" | custom-call | flops 1 | bytes 1024 | tf_op jit(solution)/shard_map/far/pallas_call | solution.py:280
  45.2 0.6 pair_row.1
  45.9 5.5 %collective-permute-start.16 = (f32[1,640]{1,0:T(1,128)S(1)}, f32[1,640]{1,0:T(1,128)S(1)}, u32[]{:S(2)}, u32[]{:S(2)}) collective-permute-start(f32[1,640]{1,0:T(1,128)S(1)} %get-tuple-element.230), channel_id=1, source_target_pairs={{0,6},{2,4},{4,2},{6,0},{8,14},{10,12},{12,10},{14,8},{1,7},{3,5},... | collective-permute-start | bytes 7688 | tf_op jit(solution)/shard_map/ppermute | solution.py:325
  51.4 0.8 %collective-permute-start.9 = (f32[1,640]{1,0:T(1,128)S(1)}, f32[1,640]{1,0:T(1,128)S(1)}, u32[]{:S(2)}, u32[]{:S(2)}) collective-permute-start(f32[1,640]{1,0:T(1,128)S(1)} %get-tuple-element.217), channel_id=1, source_target_pairs={{0,2},{2,0},{4,6},{6,4},{8,10},{10,8},{12,14},{14,12},{1,3},{3,1},... | collective-permute-start | bytes 7688 | tf_op jit(solution)/shard_map/ppermute | solution.py:325
  52.2 1.1 %collective-permute-start.10 = (f32[1,640]{1,0:T(1,128)S(1)}, f32[1,640]{1,0:T(1,128)S(1)}, u32[]{:S(2)}, u32[]{:S(2)}) collective-permute-start(f32[1,640]{1,0:T(1,128)S(1)} %get-tuple-element.218), channel_id=1, source_target_pairs={{0,3},{1,2},{2,1},{3,0},{4,7},{5,6},{6,5},{7,4},{8,11},{9,10},{10,... | collective-permute-start | bytes 7688 | tf_op jit(solution)/shard_map/ppermute | solution.py:330
  53.3 1.2 %pair_diag.1 = (f32[1,640]{1,0:T(1,128)S(1)}, f32[1,640]{1,0:T(1,128)S(1)}, f32[1,640]{1,0:T(1,128)S(1)}, f32[1,640]{1,0:T(1,128)S(1)}, f32[1,640]{1,0:T(1,128)S(1)}) custom-call(s32[3]{0:T(128)S(1)} %pad_add_fusion.refs_0_, bf16[336,768]{1,0:T(8,128)(2,1)S(1)} %get-tuple-element.196.refs_1_, bf16[336,768]{1,0:T(8,128)(2,1)S(1)} %collective-permute-done.refs_2_.refs_1_, ...), custom_call_target="tpu_custom_call" | custom-call | flops 1 | bytes 1024 | tf_op jit(solution)/shard_map/pair_diag/pallas_call | solution.py:280
  54.4 0.6 copy-done
  55.0 0.6 collective-permute-start.13
  55.6 0.7 collective-permute-start.14
  56.3 3.4 %collective-permute-start.15 = (f32[1,640]{1,0:T(1,128)S(1)}, f32[1,640]{1,0:T(1,128)S(1)}, u32[]{:S(2)}, u32[]{:S(2)}) collective-permute-start(f32[1,640]{1,0:T(1,128)S(1)} %get-tuple-element.229), channel_id=1, source_target_pairs={{0,7},{1,6},{2,5},{3,4},{4,3},{5,2},{6,1},{7,0},{8,15},{9,14},{10,... | collective-permute-start | bytes 7688 | tf_op jit(solution)/shard_map/ppermute | solution.py:330
  59.7 1.0 %collective-permute-start.17 = (f32[1,640]{1,0:T(1,128)S(1)}, f32[1,640]{1,0:T(1,128)S(1)}, u32[]{:S(2)}, u32[]{:S(2)}) collective-permute-start(f32[1,640]{1,0:T(1,128)S(1)} %get-tuple-element.231), channel_id=1, source_target_pairs={{0,4},{2,6},{4,0},{6,2},{8,12},{10,14},{12,8},{14,10},{1,5},{3,7},... | collective-permute-start | bytes 7688 | tf_op jit(solution)/shard_map/ppermute | solution.py:325
  60.7 0.3 collective-permute-done.15.refs_7_
  61.0 2.3 %collective-permute-done.17.refs_9_ = f32[1,640]{1,0:T(1,128)S(1)} collective-permute-done((f32[1,640]{1,0:T(1,128)S(1)}, f32[1,640]{1,0:T(1,128)S(1)}, u32[]{:S(2)}, u32[]{:S(2)}) %collective-permute-start.17) | collective-permute-done | bytes 2592 | tf_op jit(solution)/shard_map/ppermute | solution.py:325
  63.3 0.5 copy-done.16
  63.9 1.5 %finish.1 = (f32[1,512]{1,0:T(1,128)S(1)}, s32[1,1]{1,0:T(1,128)}) custom-call(s32[1,512]{1,0:T(1,128)} %copy-done.1, f32[1,640]{1,0:T(1,128)} %copy-done.9, f32[1,640]{1,0:T(1,128)} %copy-done.10, f32[1,640]{1,0:T(1,128)} %copy-done.11, f32[1,640]{1,0:T(1,128)} %copy-done.12, f32[1,640]{1,0:T(1,128)} %copy-done.13, f32[1,640]{1,0:T(1,128)} %copy-done.14, ...), custom_call_target="tpu_custom_call" | custom-call | tf_op jit(solution)/shard_map/finish/pallas_call | solution.py:305
  65.9 0.3 conditional.1
  66.2 0.6 copy-done.17
  (45 shorter events, 0.1 us)
Async XLA Ops:
  10.2 8.2 %copy-start.1 = (s32[1,512]{1,0:T(1,128)}, s32[1,512]{1,0:T(1,128)S(1)}, u32[]{:S(2)}) copy-start(s32[1,512]{1,0:T(1,128)S(1)} %get-tuple-element.195.refs_0_) | copy-start | bytes 6148
  10.2 8.2 %collective-permute-start.2 = (bf16[336,768]{1,0:T(8,128)(2,1)S(1)}, bf16[336,768]{1,0:T(8,128)(2,1)S(1)}, u32[]{:S(2)}, u32[]{:S(2)}) collective-permute-start(bf16[336,768]{1,0:T(8,128)(2,1)S(1)} %get-tuple-element.196.refs_1_), channel_id=1, source_target_pairs={{0,1},{1,0},{2,3},{3,2},{4,5},{5,4},{6,7},{7,6},{8,9},{9,8},{10,11... | collective-permute-start | bytes 1548296 | tf_op jit(solution)/shard_map/ppermute | solution.py:329
  10.7 8.9 %collective-permute-start.1 = (bf16[336,768]{1,0:T(8,128)(2,1)S(1)}, bf16[336,768]{1,0:T(8,128)(2,1)S(1)}, u32[]{:S(2)}, u32[]{:S(2)}) collective-permute-start(bf16[336,768]{1,0:T(8,128)(2,1)S(1)} %get-tuple-element.197), channel_id=1, source_target_pairs={{0,0},{2,2},{4,8},{6,10},{8,4},{10,6},{12,12},{14,14},{1,1},{3,3},... | collective-permute-start | bytes 1548296 | tf_op jit(solution)/shard_map/ppermute | solution.py:325
  11.4 17.6 %collective-permute-start = (bf16[336,768]{1,0:T(8,128)(2,1)S(1)}, bf16[336,768]{1,0:T(8,128)(2,1)S(1)}, u32[]{:S(2)}, u32[]{:S(2)}) collective-permute-start(bf16[336,768]{1,0:T(8,128)(2,1)S(1)} %get-tuple-element.197), channel_id=1, source_target_pairs={{0,4},{2,6},{4,0},{6,2},{8,12},{10,14},{12,8},{14,10},{1,5},{3,7},... | collective-permute-start | bytes 1548296 | tf_op jit(solution)/shard_map/ppermute | solution.py:325
  16.9 15.3 %collective-permute-start.3 = (bf16[336,768]{1,0:T(8,128)(2,1)S(1)}, bf16[336,768]{1,0:T(8,128)(2,1)S(1)}, u32[]{:S(2)}, u32[]{:S(2)}) collective-permute-start(bf16[336,768]{1,0:T(8,128)(2,1)S(1)} %get-tuple-element.196.refs_1_), channel_id=1, source_target_pairs={{0,2},{2,0},{4,6},{6,4},{8,10},{10,8},{12,14},{14,12},{1,3},{3,1},... | collective-permute-start | bytes 1548296 | tf_op jit(solution)/shard_map/ppermute | solution.py:325
  29.0 3.2 %collective-permute-start.5 = (bf16[336,768]{1,0:T(8,128)(2,1)S(1)}, bf16[336,768]{1,0:T(8,128)(2,1)S(1)}, u32[]{:S(2)}, u32[]{:S(2)}) collective-permute-start(bf16[336,768]{1,0:T(8,128)(2,1)S(1)} %collective-permute-done.refs_2_.refs_1_), channel_id=1, source_target_pairs={{0,1},{1,0},{2,3},{3,2},{4,5},{5,4},{6,7},{7,6},{8,9},{9,8},{10,11... | collective-permute-start | bytes 1548296 | tf_op jit(solution)/shard_map/ppermute | solution.py:329
  29.0 15.5 %collective-permute-start.4 = (bf16[336,768]{1,0:T(8,128)(2,1)S(1)}, bf16[336,768]{1,0:T(8,128)(2,1)S(1)}, u32[]{:S(2)}, u32[]{:S(2)}) collective-permute-start(bf16[336,768]{1,0:T(8,128)(2,1)S(1)} %get-tuple-element.196.refs_1_), channel_id=1, source_target_pairs={{0,8},{2,10},{4,0},{6,2},{8,12},{10,14},{12,4},{14,6},{1,9},{3,11}... | collective-permute-start | bytes 1548296 | tf_op jit(solution)/shard_map/ppermute | solution.py:325
  30.6 13.9 %collective-permute-start.11 = (bf16[336,768]{1,0:T(8,128)(2,1)S(1)}, bf16[336,768]{1,0:T(8,128)(2,1)S(1)}, u32[]{:S(2)}, u32[]{:S(2)}) collective-permute-start(bf16[336,768]{1,0:T(8,128)(2,1)S(1)} %collective-permute-done.refs_2_.refs_1_), channel_id=1, source_target_pairs={{0,2},{2,0},{4,6},{6,4},{8,10},{10,8},{12,14},{14,12},{1,3},{3,1},... | collective-permute-start | bytes 1548296 | tf_op jit(solution)/shard_map/ppermute | solution.py:325
  32.1 1.9 %collective-permute-start.6 = (bf16[336,768]{1,0:T(8,128)(2,1)S(1)}, bf16[336,768]{1,0:T(8,128)(2,1)S(1)}, u32[]{:S(2)}, u32[]{:S(2)}) collective-permute-start(bf16[336,768]{1,0:T(8,128)(2,1)S(1)} %collective-permute-done.3.refs_3_), channel_id=1, source_target_pairs={{0,1},{1,0},{2,3},{3,2},{4,5},{5,4},{6,7},{7,6},{8,9},{9,8},{10,11... | collective-permute-start | bytes 1548296 | tf_op jit(solution)/shard_map/ppermute | solution.py:329
  44.5 7.7 %collective-permute-start.12 = (bf16[336,768]{1,0:T(8,128)(2,1)S(1)}, bf16[336,768]{1,0:T(8,128)(2,1)S(1)}, u32[]{:S(2)}, u32[]{:S(2)}) collective-permute-start(bf16[336,768]{1,0:T(8,128)(2,1)S(1)} %collective-permute-done.11.refs_4_.refs_7_), channel_id=1, source_target_pairs={{0,1},{1,0},{2,3},{3,2},{4,5},{5,4},{6,7},{7,6},{8,9},{9,8},{10,11... | collective-permute-start | bytes 1548296 | tf_op jit(solution)/shard_map/ppermute | solution.py:329
  45.9 9.2 %collective-permute-start.16 = (f32[1,640]{1,0:T(1,128)S(1)}, f32[1,640]{1,0:T(1,128)S(1)}, u32[]{:S(2)}, u32[]{:S(2)}) collective-permute-start(f32[1,640]{1,0:T(1,128)S(1)} %get-tuple-element.230), channel_id=1, source_target_pairs={{0,6},{2,4},{4,2},{6,0},{8,14},{10,12},{12,10},{14,8},{1,7},{3,5},... | collective-permute-start | bytes 7688 | tf_op jit(solution)/shard_map/ppermute | solution.py:325
  51.4 4.2 %collective-permute-start.7 = (f32[1,640]{1,0:T(1,128)S(1)}, f32[1,640]{1,0:T(1,128)S(1)}, u32[]{:S(2)}, u32[]{:S(2)}) collective-permute-start(f32[1,640]{1,0:T(1,128)S(1)} %get-tuple-element.215), channel_id=1, source_target_pairs={{0,1},{1,0},{2,3},{3,2},{4,5},{5,4},{6,7},{7,6},{8,9},{9,8},{10,11... | collective-permute-start | bytes 7688 | tf_op jit(solution)/shard_map/ppermute | solution.py:329
  51.4 4.9 %collective-permute-start.8 = (f32[1,640]{1,0:T(1,128)S(1)}, f32[1,640]{1,0:T(1,128)S(1)}, u32[]{:S(2)}, u32[]{:S(2)}) collective-permute-start(f32[1,640]{1,0:T(1,128)S(1)} %get-tuple-element.216), channel_id=1, source_target_pairs={{0,5},{1,4},{2,7},{3,6},{4,1},{5,0},{6,3},{7,2},{8,13},{9,12},{10,... | collective-permute-start | bytes 7688 | tf_op jit(solution)/shard_map/ppermute | solution.py:330
  51.4 8.3 %collective-permute-start.9 = (f32[1,640]{1,0:T(1,128)S(1)}, f32[1,640]{1,0:T(1,128)S(1)}, u32[]{:S(2)}, u32[]{:S(2)}) collective-permute-start(f32[1,640]{1,0:T(1,128)S(1)} %get-tuple-element.217), channel_id=1, source_target_pairs={{0,2},{2,0},{4,6},{6,4},{8,10},{10,8},{12,14},{14,12},{1,3},{3,1},... | collective-permute-start | bytes 7688 | tf_op jit(solution)/shard_map/ppermute | solution.py:325
  52.2 8.4 %collective-permute-start.10 = (f32[1,640]{1,0:T(1,128)S(1)}, f32[1,640]{1,0:T(1,128)S(1)}, u32[]{:S(2)}, u32[]{:S(2)}) collective-permute-start(f32[1,640]{1,0:T(1,128)S(1)} %get-tuple-element.218), channel_id=1, source_target_pairs={{0,3},{1,2},{2,1},{3,0},{4,7},{5,6},{6,5},{7,4},{8,11},{9,10},{10,... | collective-permute-start | bytes 7688 | tf_op jit(solution)/shard_map/ppermute | solution.py:330
  53.3 12.6 %copy-start.4 = (bf16[1024,768]{1,0:T(8,128)(2,1)S(1)}, bf16[1024,768]{1,0:T(8,128)(2,1)}, u32[]{:S(2)}) copy-start(bf16[1024,768]{1,0:T(8,128)(2,1)} %refs_3_.1) | copy-start | bytes 4718596
  53.3 12.6 %copy-start.5 = (bf16[512,1024]{1,0:T(8,128)(2,1)S(1)}, bf16[512,1024]{1,0:T(8,128)(2,1)}, u32[]{:S(2)}) copy-start(bf16[512,1024]{1,0:T(8,128)(2,1)} %refs_2_.1) | copy-start | bytes 3145732
  53.3 12.6 %copy-start.7 = (s32[512]{0:T(512)S(1)}, s32[512]{0:T(512)}, u32[]{:S(2)}) copy-start(s32[512]{0:T(512)} %param.9) | copy-start | bytes 6148
  54.4 0.6 copy-start
  55.0 8.2 %copy-start.8 = (f32[1,640]{1,0:T(1,128)}, f32[1,640]{1,0:T(1,128)S(1)}, u32[]{:S(2)}) copy-start(f32[1,640]{1,0:T(1,128)S(1)} %collective-permute-done.16.refs_8_) | copy-start | bytes 7684
  55.0 5.6 %collective-permute-start.13 = (f32[1,640]{1,0:T(1,128)S(1)}, f32[1,640]{1,0:T(1,128)S(1)}, u32[]{:S(2)}, u32[]{:S(2)}) collective-permute-start(f32[1,640]{1,0:T(1,128)S(1)} %get-tuple-element.227), channel_id=1, source_target_pairs={{0,8},{2,10},{4,12},{6,14},{8,0},{10,2},{12,4},{14,6},{1,9},{3,11}... | collective-permute-start | bytes 7688 | tf_op jit(solution)/shard_map/ppermute | solution.py:325
  55.6 7.7 %copy-start.9 = (f32[1,640]{1,0:T(1,128)}, f32[1,640]{1,0:T(1,128)S(1)}, u32[]{:S(2)}) copy-start(f32[1,640]{1,0:T(1,128)S(1)} %collective-permute-done.7.refs_1_) | copy-start | bytes 7684
  55.6 5.0 %collective-permute-start.14 = (f32[1,640]{1,0:T(1,128)S(1)}, f32[1,640]{1,0:T(1,128)S(1)}, u32[]{:S(2)}, u32[]{:S(2)}) collective-permute-start(f32[1,640]{1,0:T(1,128)S(1)} %get-tuple-element.228), channel_id=1, source_target_pairs={{0,0},{2,2},{4,8},{6,10},{8,4},{10,6},{12,12},{14,14},{1,1},{3,3},... | collective-permute-start | bytes 7688 | tf_op jit(solution)/shard_map/ppermute | solution.py:325
  56.3 7.0 %copy-start.10 = (f32[1,640]{1,0:T(1,128)}, f32[1,640]{1,0:T(1,128)S(1)}, u32[]{:S(2)}) copy-start(f32[1,640]{1,0:T(1,128)S(1)} %collective-permute-done.8.refs_2_) | copy-start | bytes 7684
  56.3 4.7 %collective-permute-start.15 = (f32[1,640]{1,0:T(1,128)S(1)}, f32[1,640]{1,0:T(1,128)S(1)}, u32[]{:S(2)}, u32[]{:S(2)}) collective-permute-start(f32[1,640]{1,0:T(1,128)S(1)} %get-tuple-element.229), channel_id=1, source_target_pairs={{0,7},{1,6},{2,5},{3,4},{4,3},{5,2},{6,1},{7,0},{8,15},{9,14},{10,... | collective-permute-start | bytes 7688 | tf_op jit(solution)/shard_map/ppermute | solution.py:330
  59.7 3.6 %copy-start.11 = (f32[1,640]{1,0:T(1,128)}, f32[1,640]{1,0:T(1,128)S(1)}, u32[]{:S(2)}) copy-start(f32[1,640]{1,0:T(1,128)S(1)} %collective-permute-done.9.refs_3_) | copy-start | bytes 7684
  59.7 3.6 %collective-permute-start.17 = (f32[1,640]{1,0:T(1,128)S(1)}, f32[1,640]{1,0:T(1,128)S(1)}, u32[]{:S(2)}, u32[]{:S(2)}) collective-permute-start(f32[1,640]{1,0:T(1,128)S(1)} %get-tuple-element.231), channel_id=1, source_target_pairs={{0,4},{2,6},{4,0},{6,2},{8,12},{10,14},{12,8},{14,10},{1,5},{3,7},... | collective-permute-start | bytes 7688 | tf_op jit(solution)/shard_map/ppermute | solution.py:325
  60.6 2.7 %copy-start.12 = (f32[1,640]{1,0:T(1,128)}, f32[1,640]{1,0:T(1,128)S(1)}, u32[]{:S(2)}) copy-start(f32[1,640]{1,0:T(1,128)S(1)} %collective-permute-done.10.refs_4_) | copy-start | bytes 7684
  60.6 2.7 %copy-start.13 = (f32[1,640]{1,0:T(1,128)}, f32[1,640]{1,0:T(1,128)S(1)}, u32[]{:S(2)}) copy-start(f32[1,640]{1,0:T(1,128)S(1)} %collective-permute-done.13.refs_5_) | copy-start | bytes 7684
  60.7 2.7 %copy-start.14 = (f32[1,640]{1,0:T(1,128)}, f32[1,640]{1,0:T(1,128)S(1)}, u32[]{:S(2)}) copy-start(f32[1,640]{1,0:T(1,128)S(1)} %collective-permute-done.14.refs_6_) | copy-start | bytes 7684
  61.0 2.4 %copy-start.15 = (f32[1,640]{1,0:T(1,128)}, f32[1,640]{1,0:T(1,128)S(1)}, u32[]{:S(2)}) copy-start(f32[1,640]{1,0:T(1,128)S(1)} %collective-permute-done.15.refs_7_) | copy-start | bytes 7684
  66.2 0.6 copy-start.17
  (1 other events, 0.6 us)

commit v6 on v5

--- a/solution.py
+++ b/solution.py
@@ -211,53 +211,80 @@
 ROW, PAIR_ROW = "row", "pair_row"
 DIAG, PAIR_DIAG = "diag", "pair_diag"
 NEXT, FAR = "next", "far"
-
-
-def score_kernel(docs, hot, names, tasks, carried, made, flagged, *refs):
+GROUPS = ((OWN, PAIR), (CORE, PAIR_CORE, DIAG, PAIR_DIAG), (ROW, PAIR_ROW), (NEXT,), (FAR,))
+
+
+def score_kernel(docs, hot, names, tasks, flagged, carries, *refs):
     rest, first, flag, lanes = layout(docs, hot)
     place_ref, refs = refs[0], refs[1:]
     blocks, refs = dict(zip(names, refs[:len(names)])), refs[len(names):]
-    before, sums = dict(zip(carried, refs[:len(carried)])), dict(zip(made, refs[len(carried):]))
+    before, refs = refs[:len(GROUPS) * carries], refs[len(GROUPS) * carries:]
+    outs, (turned, parts) = refs[:len(GROUPS)], refs[len(GROUPS):]
+    for k, out in enumerate(outs):
+        out[...] = before[k][...] if carries else jnp.zeros(out.shape, F32)
+    spots = {name: (out, k) for out, group in zip(outs, GROUPS) for k, name in enumerate(group)}
     z, y, c = place_ref[0], place_ref[1], place_ref[2]
-    for name in made:
-        sums[name][...] = before[name][...] if name in before else jnp.zeros((1, lanes), F32)
     when = {"core0": c == 0, "core1": c == 1, "row0": y == 0, "row1": y == 1}
     middle = (z == 1) | (z == 2)
+    lefts = list(dict.fromkeys(task[1] for task in tasks if task[0] != task[1]))
+    width = turned.shape[0]
 
     def meet(count, start):
         lane = slice(start, start + count)
-        ids = {name: ref[rest:, :].astype(F32)[0:8, 0:count] for name, ref in blocks.items()}
-        for row in dict.fromkeys(task[0] for task in tasks):
-
-            def work(row=row):
-                row_ids = ids[row].T[:, 0:1]
-                for _, col, condition in [task for task in tasks if task[0] == row]:
-
-                    def one(col=col):
-                        inner = lax.dot_general(
-                            blocks[row][:count, :], blocks[col][:count, :], (((1,), (1,)), ((), ())),
-                            preferred_element_type=F32,
+        wide = up(count, 128)
+        ids = {name: ref[rest:, :].astype(F32)[0:8, 0:wide] for name, ref in blocks.items()}
+        columns = {name: ids[name].T[0:count, 0:1] for name in dict.fromkeys(task[1] for task in tasks)}
+        for k in range(len(lefts)):
+            parts[k, 0:count, :] = jnp.zeros((count, 128), F32)
+
+        for right in dict.fromkeys(task[0] for task in tasks):
+
+            def work(right=right):
+                inside = lax.broadcasted_iota(jnp.int32, (1, wide), 1) < count
+                right_ids = jnp.where(inside, ids[right][0:1, :], -1.0)
+                turned[:, 0:wide] = jnp.zeros((width, wide), BF16)
+                turned[:, 0:count] = blocks[right][:count, :].T
+                for _, left, condition in [task for task in tasks if task[0] == right]:
+
+                    def one(left=left):
+                        inner = jnp.dot(
+                            blocks[left][:count, :], turned[:, 0:wide], preferred_element_type=F32
                         )
-                        same = row_ids == ids[col][0:1, :]
-                        if row == col:
+                        same = columns[left] == right_ids
+                        if left == right:
                             same &= lax.broadcasted_iota(jnp.int32, inner.shape, 0) != lax.broadcasted_iota(
                                 jnp.int32, inner.shape, 1
                             )
                         weights = jnp.where(same, jnp.exp2(inner), 0.0)
-                        if row != col:
-                            total = jnp.sum(weights, axis=1, keepdims=True)
-                            sums[row][:, lane] += jnp.broadcast_to(total, (count, 128)).T[0:1, :]
-                        sums[col][:, lane] += jnp.sum(weights, axis=0, keepdims=True)
+                        out, k = spots[right]
+                        out[k, :, lane] += jnp.sum(weights, axis=0, keepdims=True)[:, 0:count]
+                        if left != right:
+                            part = weights[:, 0:128]
+                            for t in range(128, wide, 128):
+                                part += weights[:, t:t + 128]
+                            parts[lefts.index(left), 0:count, :] += part
 
                     if condition is None:
                         one()
                     else:
                         pl.when(when[condition])(one)
 
-            if row in (NEXT, FAR):
+            if right in (NEXT, FAR):
                 pl.when(middle)(work)
             else:
                 work()
+
+        ones = jnp.ones((16, 128), BF16)
+        for k, left in enumerate(lefts):
+            part = parts[k, 0:count, :]
+            high = part.astype(BF16)
+            low = (part - high.astype(F32)).astype(BF16)
+            total = sum(
+                lax.dot_general(ones, term, (((1,), (1,)), ((), ())), preferred_element_type=F32)
+                for term in (high, low)
+            )
+            out, spot = spots[left]
+            out[spot, :, lane] += total[0:1, :]
 
     pl.when(lax.rem(z, 2) == 0)(lambda: meet(hot, first))
     pl.when(lax.rem(z, 2) == 1)(lambda: meet(rest, 0))
@@ -266,34 +293,34 @@
         doubt = sum(ref[rest:, first:first + 128].astype(F32)[0:1, 0:1] for ref in blocks.values())
         spot = lax.broadcasted_iota(jnp.int32, (1, lanes), 1)
         for name in flagged:
-            sums[name][...] += jnp.where(spot == flag, doubt, 0.0)
+            out, k = spots[name]
+            out[k] += jnp.where(spot == flag, doubt, 0.0)
 
 
 def score(name, docs, hot, place, blocks, tasks, sums, flagged=(), weight=1):
-    lanes = layout(docs, hot)[3]
+    rest, _, _, lanes = layout(docs, hot)
     names = [b for b in blocks if flagged or any(b in task[:2] for task in tasks)]
-    made = [b for b in blocks if any(b in task[:2] for task in tasks)]
-    made += [b for b in flagged if b not in made]
-    carried = [b for b in made if b in sums]
+    lefts = len({task[1] for task in tasks if task[0] != task[1]})
+    width = blocks[OWN].shape[1]
     vmem = pl.BlockSpec(memory_space=pltpu.VMEM)
-    arrays = [blocks[b] for b in names] + [sums[b] for b in carried]
-    out = pl.pallas_call(
-        lambda *refs: score_kernel(docs, hot, names, tasks, carried, made, flagged, *refs),
-        out_shape=tuple(jax.ShapeDtypeStruct((1, lanes), F32) for _ in made),
+    arrays = [blocks[b] for b in names] + list(sums)
+    return pl.pallas_call(
+        lambda *refs: score_kernel(docs, hot, names, tasks, flagged, bool(sums), *refs),
+        out_shape=tuple(jax.ShapeDtypeStruct((len(group), 1, lanes), F32) for group in GROUPS),
         in_specs=[pl.BlockSpec(memory_space=pltpu.SMEM)] + [vmem] * len(arrays),
-        out_specs=tuple(vmem for _ in made),
+        out_specs=tuple(vmem for _ in GROUPS),
+        scratch_shapes=[pltpu.VMEM((width, up(rest, 128)), BF16), pltpu.VMEM((lefts, rest, 128), F32)],
         compiler_params=pltpu.CompilerParams(vmem_limit_bytes=20 * 2**20),
         cost_estimate=pl.CostEstimate(flops=weight, bytes_accessed=2**10, transcendentals=0),
         name=name,
     )(place, *arrays)
-    return {**sums, **dict(zip(made, out))}
 
 
 def finish_kernel(flag, slot_ref, *refs):
     sums, out_ref, doubt_ref = refs[:-2], refs[-2], refs[-1]
-    total = sums[0][...]
+    total = sums[0][0]
     for ref in sums[1:]:
-        total += ref[...]
+        total += ref[0]
     lanes, docs = total.shape[1], slot_ref.shape[1]
     doubt_ref[...] = (total[:, flag:flag + 1] > 0.0).astype(jnp.int32)
     values = jnp.broadcast_to(jnp.log(1.0 + total * 2.0**-SHIFT), (8, lanes)).T[:, 0:1]
@@ -341,52 +368,45 @@
     def meet(name, tasks, **options):
         return score(name, docs, hot, place, blocks, tasks, sums, **options)
 
-    blocks, sums = {OWN: same}, {}
+    blocks, sums = {OWN: same}, ()
+    blocks[NEXT] = move(other, MIDDLE)
     blocks[PAIR] = move(other, OUTER)
     blocks[ROW] = move(same, STAY, row=1)
-    blocks[NEXT] = move(other, MIDDLE)
     blocks[CORE] = move(same, STAY, core=1)
+    sums = meet("own", [(OWN, OWN, None), (OWN, CORE, "core0")], weight=2**33)
+
+    blocks[PAIR], blocks[NEXT], _ = lax.optimization_barrier((blocks[PAIR], blocks[NEXT], sums[0]))
     blocks[FAR] = move(same, TO_MIDDLE)
-    sums = meet("own", [(OWN, OWN, None), (OWN, CORE, "core0")], weight=2**33)
-
-    pair, blocks[NEXT], _ = lax.optimization_barrier((blocks[PAIR], blocks[NEXT], sums[OWN]))
-    blocks[PAIR] = pair
-    blocks[PAIR_ROW] = move(pair, STAY, row=1)
-    blocks[PAIR_CORE] = move(pair, STAY, core=1)
+    blocks[PAIR_ROW] = move(blocks[PAIR], STAY, row=1)
+    blocks[PAIR_CORE] = move(blocks[PAIR], STAY, core=1)
     blocks[DIAG] = move(blocks[ROW], STAY, core=1)
     sums = meet(
-        "pair", [(PAIR, PAIR, None), (PAIR, OWN, None), (PAIR, CORE, None), (PAIR, PAIR_CORE, "core1")]
-    )
-    sums = meet("next", [(NEXT, b, None) for b in (OWN, CORE, PAIR, PAIR_CORE)], weight=2**33)
+        "pair",
+        [(PAIR, PAIR, None), (PAIR, OWN, None), (PAIR, CORE, None), (PAIR, PAIR_CORE, "core1")]
+        + [(NEXT, b, None) for b in (OWN, CORE, PAIR, PAIR_CORE)],
+        weight=2**33,
+    )
     sums = meet(
         "row",
         [(PAIR, ROW, None), (PAIR, DIAG, None), (OWN, ROW, "row0"), (OWN, DIAG, "row1"),
          (NEXT, ROW, None), (NEXT, DIAG, None)],
     )
-    blocks[PAIR_ROW], _ = lax.optimization_barrier((blocks[PAIR_ROW], sums[ROW]))
+    blocks[PAIR_ROW], _ = lax.optimization_barrier((blocks[PAIR_ROW], sums[0]))
     blocks[PAIR_DIAG] = move(blocks[PAIR_ROW], STAY, core=1)
     sums = meet("far", [(FAR, b, None) for b in (OWN, CORE, PAIR, PAIR_CORE, ROW, DIAG)])
-    early = [
-        move(sums[CORE], STAY, core=1),
-        move(sums[PAIR_CORE], OUTER, core=1),
-        move(sums[ROW], STAY, row=1),
-        move(sums[DIAG], STAY, row=1, core=1),
-    ]
-    sums = meet("pair_row", [(PAIR, PAIR_ROW, "row1"), (NEXT, PAIR_ROW, None), (FAR, PAIR_ROW, None)])
     sums = meet(
-        "pair_diag",
-        [(PAIR, PAIR_DIAG, "row0"), (NEXT, PAIR_DIAG, None), (FAR, PAIR_DIAG, None)],
+        "last",
+        [(PAIR, PAIR_ROW, "row1"), (PAIR, PAIR_DIAG, "row0")]
+        + [(b, c, None) for b in (NEXT, FAR) for c in (PAIR_ROW, PAIR_DIAG)],
         flagged=(OWN, FAR),
     )
-    back = early + [
-        move(sums[FAR], TWO),
-        move(sums[NEXT], MIDDLE),
-        move(sums[PAIR_DIAG], OUTER, row=1, core=1),
-        move(sums[PAIR_ROW], OUTER, row=1),
-        move(sums[PAIR], OUTER),
-        sums[OWN],
-    ]
-    fast, doubt = finish(flag, slot, back)
+    home, by_core, by_row, to_next, to_far = sums
+    from_far, from_next = move(to_far, TWO), move(to_next, MIDDLE)
+    from_core = move(by_core, STAY, core=1)
+    from_row = move(by_row + from_core[2:4], STAY, row=1)
+    home = home + from_core[0:2] + from_row
+    from_pair = move(home[1:2], OUTER)
+    fast, doubt = finish(flag, slot, (home, from_pair, from_far, from_next))
     return lax.cond(
         doubt[0, 0] > 0, owner_plan, lambda *_: fast.reshape(docs), states, proj_weight, cluster_of
     )

time: 73.8 us -> 69.1 us (0.936)
  starting transfers between devices: 24.2 us -> 19.4 us
    ppermute x3 -> x0, starting transfers between devices: 4.45 us -> none  [move(): lax.ppermute(a, ('owner', 'split'), [((z * ROWS + y) * 2 + c, (to[z] * RO...]
    ppermute x5, waiting for transfers between devices: 0.22 us -> 2.15 us  [move(): return lax.ppermute(a, 'split', [(0, 1), (1, 0)])]
    ppermute x10 -> x9, waiting for transfers between devices: 20.6 us -> 19.6 us  [move(): lax.ppermute(a, 'owner', [(z * ROWS + y, to[z] * ROWS + (y ^ row)) for z...]
    unnamed x30 -> x16, local copies, waits for them, and re-layouts: 1.73 us -> 1.19 us
    ppermute x10 -> x9, starting transfers between devices: 19.3 us -> 18.8 us  [move(): lax.ppermute(a, 'owner', [(z * ROWS + y, to[z] * ROWS + (y ^ row)) for z...]
    pallas_call x7 -> x5, Pallas kernels: 6.96 us -> 6.97 us  [score(): pl.pallas_call(lambda *refs: score_kernel(docs, hot, names, tasks, flagge...]
  transfers between devices with their start and end apart: 18 -> 14, of which waited for: 5 -> 6; matrix products, arithmetic and copies ran while one was open for 0% -> 0% of each run, Pallas kernels for 9% -> 8%
where the time goes in v6:
time: 69.1 us; the launch traced here: 68.9 us
  waiting for transfers between devices  21.8 us (32%)
  starting transfers between devices  19.4 us (28%)
  between operations  14.1 us (20%)
  Pallas kernels  12 us (17%)
  local copies, waits for them, and re-layouts  1.19 us (2%)
    ppermute x9, waiting for transfers between devices, move(): lax.ppermute(a, 'owner', [(z * ROWS + y, to[z] * ROWS + (y ^ row)) for z...  19.6 us
    ppermute x9, starting transfers between devices, move(): lax.ppermute(a, 'owner', [(z * ROWS + y, to[z] * ROWS + (y ^ row)) for z...  18.8 us
    pallas_call x5, Pallas kernels, score(): pl.pallas_call(lambda *refs: score_kernel(docs, hot, names, tasks, flagge...  6.97 us
    pallas_call x1, Pallas kernels, prep(): pl.pallas_call(lambda *refs: prep_kernel(hot, *refs), out_shape=(shape((r...  3.56 us
    ppermute x5, waiting for transfers between devices, move(): return lax.ppermute(a, 'split', [(0, 1), (1, 0)])  2.15 us
    pallas_call x1, Pallas kernels, finish(): pl.pallas_call(lambda *refs: finish_kernel(flag, *refs), out_shape=(jax.S...  1.45 us
  transfers between devices with their start and end apart: 14, of which 6 were waited for; matrix products, arithmetic and copies ran while one was open for 0% of the time, Pallas kernels for 8%

profile of v6, /device:TPU:0, one launch (start us, length us, event | category | flops | bytes accessed | tf_op | source)
XLA Modules:
  0.0 68.9 jit_solution(8837408257354582377)
XLA Ops:
  6.5 0.1 pad_add_fusion.refs_0_
  6.6 3.6 %prep.1 = (bf16[336,768]{1,0:T(8,128)(2,1)S(1)}, bf16[336,768]{1,0:T(8,128)(2,1)S(1)}, s32[1,512]{1,0:T(1,128)S(1)}) custom-call(s32[3]{0:T(128)S(1)} %pad_add_fusion.refs_0_, s32[1,512]{1,0:T(1,128)} %bitcast.38, bf16[512,1024]{1,0:T(8,128)(2,1)} %refs_2_.1, bf16[1024,768]{1,0:T(8,128)(2,1)} %refs_3_.1), custom_call_target="tpu_custom_call" | custom-call | tf_op jit(solution)/shard_map/prep/pallas_call | solution.py:195
  10.2 0.0 copy-start
  10.2 0.5 collective-permute-start.2
  10.7 0.7 collective-permute-start.1
  11.4 5.5 %collective-permute-start = (bf16[336,768]{1,0:T(8,128)(2,1)S(1)}, bf16[336,768]{1,0:T(8,128)(2,1)S(1)}, u32[]{:S(2)}, u32[]{:S(2)}) collective-permute-start(bf16[336,768]{1,0:T(8,128)(2,1)S(1)} %get-tuple-element.190), channel_id=1, source_target_pairs={{0,4},{2,6},{4,0},{6,2},{8,12},{10,14},{12,8},{14,10},{1,5},{3,7},... | collective-permute-start | bytes 1548296 | tf_op jit(solution)/shard_map/ppermute | solution.py:352
  16.9 1.5 %collective-permute-start.3 = (bf16[336,768]{1,0:T(8,128)(2,1)S(1)}, bf16[336,768]{1,0:T(8,128)(2,1)S(1)}, u32[]{:S(2)}, u32[]{:S(2)}) collective-permute-start(bf16[336,768]{1,0:T(8,128)(2,1)S(1)} %get-tuple-element.189.refs_1_), channel_id=1, source_target_pairs={{0,2},{2,0},{4,6},{6,4},{8,10},{10,8},{12,14},{14,12},{1,3},{3,1},... | collective-permute-start | bytes 1548296 | tf_op jit(solution)/shard_map/ppermute | solution.py:352
  18.4 1.4 %own.1 = (f32[2,1,640]{2,1,0:T(1,128)S(1)}, f32[4,1,640]{2,1,0:T(1,128)S(1)}, f32[2,1,640]{2,1,0:T(1,128)S(1)}, f32[1,1,640]{2,1,0:T(1,128)S(1)}, f32[1,1,640]{2,1,0:T(1,128)S(1)}) custom-call(s32[3]{0:T(128)S(1)} %pad_add_fusion.refs_0_, bf16[336,768]{1,0:T(8,128)(2,1)S(1)} %get-tuple-element.189.refs_1_, ...), custom_call_target="tpu_custom_call" | custom-call | flops 8589934592 | bytes 1024 | tf_op jit(solution)/shard_map/own/pallas_call | solution.py:307
  19.8 0.0 copy-done
  19.8 9.2 %collective-permute-done.refs_3_.refs_2_ = bf16[336,768]{1,0:T(8,128)(2,1)S(1)} collective-permute-done((bf16[336,768]{1,0:T(8,128)(2,1)S(1)}, bf16[336,768]{1,0:T(8,128)(2,1)S(1)}, u32[]{:S(2)}, u32[]{:S(2)}) %collective-permute-start) | collective-permute-done | bytes 516128 | tf_op jit(solution)/shard_map/ppermute | solution.py:352
  29.0 0.0 collective-permute-start.7
  29.0 1.6 %collective-permute-start.4 = (bf16[336,768]{1,0:T(8,128)(2,1)S(1)}, bf16[336,768]{1,0:T(8,128)(2,1)S(1)}, u32[]{:S(2)}, u32[]{:S(2)}) collective-permute-start(bf16[336,768]{1,0:T(8,128)(2,1)S(1)} %get-tuple-element.189.refs_1_), channel_id=1, source_target_pairs={{0,8},{2,10},{4,0},{6,2},{8,12},{10,14},{12,4},{14,6},{1,9},{3,11}... | collective-permute-start | bytes 1548296 | tf_op jit(solution)/shard_map/ppermute | solution.py:352
  30.6 1.5 %collective-permute-start.5 = (bf16[336,768]{1,0:T(8,128)(2,1)S(1)}, bf16[336,768]{1,0:T(8,128)(2,1)S(1)}, u32[]{:S(2)}, u32[]{:S(2)}) collective-permute-start(bf16[336,768]{1,0:T(8,128)(2,1)S(1)} %collective-permute-done.refs_3_.refs_2_), channel_id=1, source_target_pairs={{0,2},{2,0},{4,6},{6,4},{8,10},{10,8},{12,14},{14,12},{1,3},{3,1},... | collective-permute-start | bytes 1548296 | tf_op jit(solution)/shard_map/ppermute | solution.py:352
  32.1 1.4 %pair.1 = (f32[2,1,640]{2,1,0:T(1,128)S(1)}, f32[4,1,640]{2,1,0:T(1,128)S(1)}, f32[2,1,640]{2,1,0:T(1,128)S(1)}, f32[1,1,640]{2,1,0:T(1,128)S(1)}, f32[1,1,640]{2,1,0:T(1,128)S(1)}) custom-call(s32[3]{0:T(128)S(1)} %pad_add_fusion.refs_0_, bf16[336,768]{1,0:T(8,128)(2,1)S(1)} %get-tuple-element.189.refs_1_, ...), custom_call_target="tpu_custom_call" | custom-call | flops 8589934592 | bytes 1024 | tf_op jit(solution)/shard_map/pair/pallas_call | solution.py:307
  33.6 0.4 collective-permute-done.6.refs_5_.refs_7_.refs_9_
  34.0 1.6 %row.1 = (f32[2,1,640]{2,1,0:T(1,128)S(1)}, f32[4,1,640]{2,1,0:T(1,128)S(1)}, f32[2,1,640]{2,1,0:T(1,128)S(1)}, f32[1,1,640]{2,1,0:T(1,128)S(1)}, f32[1,1,640]{2,1,0:T(1,128)S(1)}) custom-call(s32[3]{0:T(128)S(1)} %pad_add_fusion.refs_0_, bf16[336,768]{1,0:T(8,128)(2,1)S(1)} %get-tuple-element.189.refs_1_, ...), custom_call_target="tpu_custom_call" | custom-call | flops 1 | bytes 1024 | tf_op jit(solution)/shard_map/row/pallas_call | solution.py:307
  35.6 8.9 %collective-permute-done.5.refs_7_ = bf16[336,768]{1,0:T(8,128)(2,1)S(1)} collective-permute-done((bf16[336,768]{1,0:T(8,128)(2,1)S(1)}, bf16[336,768]{1,0:T(8,128)(2,1)S(1)}, u32[]{:S(2)}, u32[]{:S(2)}) %collective-permute-start.5) | collective-permute-done | bytes 516128 | tf_op jit(solution)/shard_map/ppermute | solution.py:352
  44.5 1.2 %far.1 = (f32[2,1,640]{2,1,0:T(1,128)S(1)}, f32[4,1,640]{2,1,0:T(1,128)S(1)}, f32[2,1,640]{2,1,0:T(1,128)S(1)}, f32[1,1,640]{2,1,0:T(1,128)S(1)}, f32[1,1,640]{2,1,0:T(1,128)S(1)}) custom-call(s32[3]{0:T(128)S(1)} %pad_add_fusion.refs_0_, bf16[336,768]{1,0:T(8,128)(2,1)S(1)} %get-tuple-element.189.refs_1_, ...), custom_call_target="tpu_custom_call" | custom-call | flops 1 | bytes 1024 | tf_op jit(solution)/shard_map/far/pallas_call | solution.py:307
  45.7 0.7 collective-permute-done.8.refs_10_
  46.4 1.4 %last.1 = (f32[2,1,640]{2,1,0:T(1,128)S(1)}, f32[4,1,640]{2,1,0:T(1,128)S(1)}, f32[2,1,640]{2,1,0:T(1,128)S(1)}, f32[1,1,640]{2,1,0:T(1,128)S(1)}, f32[1,1,640]{2,1,0:T(1,128)S(1)}) custom-call(s32[3]{0:T(128)S(1)} %pad_add_fusion.refs_0_, bf16[336,768]{1,0:T(8,128)(2,1)S(1)} %get-tuple-element.189.refs_1_, ...), custom_call_target="tpu_custom_call" | custom-call | flops 1 | bytes 1024 | tf_op jit(solution)/shard_map/last/pallas_call | solution.py:307
  47.7 0.1 collective-permute-start.9
  47.9 1.0 %collective-permute-done.9 = f32[4,1,640]{2,1,0:T(1,128)S(1)} collective-permute-done((f32[4,1,640]{2,1,0:T(1,128)S(1)}, f32[4,1,640]{2,1,0:T(1,128)S(1)}, u32[]{:S(2)}, u32[]{:S(2)}) %collective-permute-start.9) | collective-permute-done | bytes 10272 | tf_op jit(solution)/shard_map/ppermute | solution.py:356
  48.9 1.6 %collective-permute-start.10 = (f32[2,1,640]{2,1,0:T(1,128)S(1)}, f32[2,1,640]{2,1,0:T(1,128)S(1)}, u32[]{:S(2)}, u32[]{:S(2)}) collective-permute-start(f32[2,1,640]{2,1,0:T(1,128)S(1)} %slice_add_fusion), channel_id=1, source_target_pairs={{0,2},{2,0},{4,6},{6,4},{8,10},{10,8},{12,14},{14,12},{1,3},{3,1},... | collective-permute-start | bytes 15368 | tf_op jit(solution)/shard_map/ppermute | solution.py:352
  50.5 2.0 %collective-permute-start.12 = (f32[1,1,640]{2,1,0:T(1,128)S(1)}, f32[1,1,640]{2,1,0:T(1,128)S(1)}, u32[]{:S(2)}, u32[]{:S(2)}) collective-permute-start(f32[1,1,640]{2,1,0:T(1,128)S(1)} %get-tuple-element.217), channel_id=1, source_target_pairs={{0,8},{2,10},{4,12},{6,14},{8,0},{10,2},{12,4},{14,6},{1,9},{3,11}... | collective-permute-start | bytes 7688 | tf_op jit(solution)/shard_map/ppermute | solution.py:352
  52.5 0.6 collective-permute-start.13
  53.2 3.8 %collective-permute-start.11 = (f32[1,1,640]{2,1,0:T(1,128)S(1)}, f32[1,1,640]{2,1,0:T(1,128)S(1)}, u32[]{:S(2)}, u32[]{:S(2)}) collective-permute-start(f32[1,1,640]{2,1,0:T(1,128)S(1)} %slice.23), channel_id=1, source_target_pairs={{0,4},{2,6},{4,0},{6,2},{8,12},{10,14},{12,8},{14,10},{1,5},{3,7},... | collective-permute-start | bytes 7688 | tf_op jit(solution)/shard_map/ppermute | solution.py:352
  57.0 1.5 %collective-permute-done.11.refs_2_ = f32[1,1,640]{2,1,0:T(1,128)S(1)} collective-permute-done((f32[1,1,640]{2,1,0:T(1,128)S(1)}, f32[1,1,640]{2,1,0:T(1,128)S(1)}, u32[]{:S(2)}, u32[]{:S(2)}) %collective-permute-start.11) | collective-permute-done | bytes 2592 | tf_op jit(solution)/shard_map/ppermute | solution.py:352
  58.6 0.6 copy-done.9
  59.1 1.5 %finish.1 = (f32[1,512]{1,0:T(1,128)S(1)}, s32[1,1]{1,0:T(1,128)}) custom-call(s32[1,512]{1,0:T(1,128)} %copy-done, f32[2,1,640]{2,1,0:T(1,128)} %copy-done.6, f32[1,1,640]{2,1,0:T(1,128)} %copy-done.9, f32[1,1,640]{2,1,0:T(1,128)} %copy-done.7, f32[1,1,640]{2,1,0:T(1,128)} %copy-done.8), custom_call_target="tpu_custom_call" | custom-call | tf_op jit(solution)/shard_map/finish/pallas_call | solution.py:332
  61.2 0.3 conditional.1
  61.5 0.0 copy-start.10
  61.5 0.6 copy-done.10
  (24 shorter events, 0.1 us)
Async XLA Ops:
  10.2 9.6 %copy-start = (s32[1,512]{1,0:T(1,128)}, s32[1,512]{1,0:T(1,128)S(1)}, u32[]{:S(2)}) copy-start(s32[1,512]{1,0:T(1,128)S(1)} %get-tuple-element.188.refs_0_) | copy-start | bytes 6148
  10.2 8.2 %collective-permute-start.2 = (bf16[336,768]{1,0:T(8,128)(2,1)S(1)}, bf16[336,768]{1,0:T(8,128)(2,1)S(1)}, u32[]{:S(2)}, u32[]{:S(2)}) collective-permute-start(bf16[336,768]{1,0:T(8,128)(2,1)S(1)} %get-tuple-element.189.refs_1_), channel_id=1, source_target_pairs={{0,1},{1,0},{2,3},{3,2},{4,5},{5,4},{6,7},{7,6},{8,9},{9,8},{10,11... | collective-permute-start | bytes 1548296 | tf_op jit(solution)/shard_map/ppermute | solution.py:356
  10.7 9.1 %collective-permute-start.1 = (bf16[336,768]{1,0:T(8,128)(2,1)S(1)}, bf16[336,768]{1,0:T(8,128)(2,1)S(1)}, u32[]{:S(2)}, u32[]{:S(2)}) collective-permute-start(bf16[336,768]{1,0:T(8,128)(2,1)S(1)} %get-tuple-element.190), channel_id=1, source_target_pairs={{0,0},{2,2},{4,8},{6,10},{8,4},{10,6},{12,12},{14,14},{1,1},{3,3},... | collective-permute-start | bytes 1548296 | tf_op jit(solution)/shard_map/ppermute | solution.py:352
  11.4 17.6 %collective-permute-start = (bf16[336,768]{1,0:T(8,128)(2,1)S(1)}, bf16[336,768]{1,0:T(8,128)(2,1)S(1)}, u32[]{:S(2)}, u32[]{:S(2)}) collective-permute-start(bf16[336,768]{1,0:T(8,128)(2,1)S(1)} %get-tuple-element.190), channel_id=1, source_target_pairs={{0,4},{2,6},{4,0},{6,2},{8,12},{10,14},{12,8},{14,10},{1,5},{3,7},... | collective-permute-start | bytes 1548296 | tf_op jit(solution)/shard_map/ppermute | solution.py:352
  16.9 15.3 %collective-permute-start.3 = (bf16[336,768]{1,0:T(8,128)(2,1)S(1)}, bf16[336,768]{1,0:T(8,128)(2,1)S(1)}, u32[]{:S(2)}, u32[]{:S(2)}) collective-permute-start(bf16[336,768]{1,0:T(8,128)(2,1)S(1)} %get-tuple-element.189.refs_1_), channel_id=1, source_target_pairs={{0,2},{2,0},{4,6},{6,4},{8,10},{10,8},{12,14},{14,12},{1,3},{3,1},... | collective-permute-start | bytes 1548296 | tf_op jit(solution)/shard_map/ppermute | solution.py:352
  29.0 3.2 %collective-permute-start.7 = (bf16[336,768]{1,0:T(8,128)(2,1)S(1)}, bf16[336,768]{1,0:T(8,128)(2,1)S(1)}, u32[]{:S(2)}, u32[]{:S(2)}) collective-permute-start(bf16[336,768]{1,0:T(8,128)(2,1)S(1)} %collective-permute-done.refs_3_.refs_2_), channel_id=1, source_target_pairs={{0,1},{1,0},{2,3},{3,2},{4,5},{5,4},{6,7},{7,6},{8,9},{9,8},{10,11... | collective-permute-start | bytes 1548296 | tf_op jit(solution)/shard_map/ppermute | solution.py:356
  29.0 15.5 %collective-permute-start.4 = (bf16[336,768]{1,0:T(8,128)(2,1)S(1)}, bf16[336,768]{1,0:T(8,128)(2,1)S(1)}, u32[]{:S(2)}, u32[]{:S(2)}) collective-permute-start(bf16[336,768]{1,0:T(8,128)(2,1)S(1)} %get-tuple-element.189.refs_1_), channel_id=1, source_target_pairs={{0,8},{2,10},{4,0},{6,2},{8,12},{10,14},{12,4},{14,6},{1,9},{3,11}... | collective-permute-start | bytes 1548296 | tf_op jit(solution)/shard_map/ppermute | solution.py:352
  30.6 13.9 %collective-permute-start.5 = (bf16[336,768]{1,0:T(8,128)(2,1)S(1)}, bf16[336,768]{1,0:T(8,128)(2,1)S(1)}, u32[]{:S(2)}, u32[]{:S(2)}) collective-permute-start(bf16[336,768]{1,0:T(8,128)(2,1)S(1)} %collective-permute-done.refs_3_.refs_2_), channel_id=1, source_target_pairs={{0,2},{2,0},{4,6},{6,4},{8,10},{10,8},{12,14},{14,12},{1,3},{3,1},... | collective-permute-start | bytes 1548296 | tf_op jit(solution)/shard_map/ppermute | solution.py:352
  32.1 1.9 %collective-permute-start.6 = (bf16[336,768]{1,0:T(8,128)(2,1)S(1)}, bf16[336,768]{1,0:T(8,128)(2,1)S(1)}, u32[]{:S(2)}, u32[]{:S(2)}) collective-permute-start(bf16[336,768]{1,0:T(8,128)(2,1)S(1)} %collective-permute-done.3.refs_4_.refs_3_), channel_id=1, source_target_pairs={{0,1},{1,0},{2,3},{3,2},{4,5},{5,4},{6,7},{7,6},{8,9},{9,8},{10,11... | collective-permute-start | bytes 1548296 | tf_op jit(solution)/shard_map/ppermute | solution.py:356
  44.5 1.9 %collective-permute-start.8 = (bf16[336,768]{1,0:T(8,128)(2,1)S(1)}, bf16[336,768]{1,0:T(8,128)(2,1)S(1)}, u32[]{:S(2)}, u32[]{:S(2)}) collective-permute-start(bf16[336,768]{1,0:T(8,128)(2,1)S(1)} %collective-permute-done.5.refs_7_), channel_id=1, source_target_pairs={{0,1},{1,0},{2,3},{3,2},{4,5},{5,4},{6,7},{7,6},{8,9},{9,8},{10,11... | collective-permute-start | bytes 1548296 | tf_op jit(solution)/shard_map/ppermute | solution.py:356
  46.4 14.8 %copy-start.3 = (bf16[512,1024]{1,0:T(8,128)(2,1)S(1)}, bf16[512,1024]{1,0:T(8,128)(2,1)}, u32[]{:S(2)}) copy-start(bf16[512,1024]{1,0:T(8,128)(2,1)} %refs_2_.1) | copy-start | bytes 3145732
  46.4 14.8 %copy-start.5 = (s32[512]{0:T(512)S(1)}, s32[512]{0:T(512)}, u32[]{:S(2)}) copy-start(s32[512]{0:T(512)} %param.9) | copy-start | bytes 6148
  47.7 1.2 %collective-permute-start.9 = (f32[4,1,640]{2,1,0:T(1,128)S(1)}, f32[4,1,640]{2,1,0:T(1,128)S(1)}, u32[]{:S(2)}, u32[]{:S(2)}) collective-permute-start(f32[4,1,640]{2,1,0:T(1,128)S(1)} %get-tuple-element.215), channel_id=1, source_target_pairs={{0,1},{1,0},{2,3},{3,2},{4,5},{5,4},{6,7},{7,6},{8,9},{9,8},{10,11... | collective-permute-start | bytes 30728 | tf_op jit(solution)/shard_map/ppermute | solution.py:356
  48.9 4.2 %collective-permute-start.10 = (f32[2,1,640]{2,1,0:T(1,128)S(1)}, f32[2,1,640]{2,1,0:T(1,128)S(1)}, u32[]{:S(2)}, u32[]{:S(2)}) collective-permute-start(f32[2,1,640]{2,1,0:T(1,128)S(1)} %slice_add_fusion), channel_id=1, source_target_pairs={{0,2},{2,0},{4,6},{6,4},{8,10},{10,8},{12,14},{14,12},{1,3},{3,1},... | collective-permute-start | bytes 15368 | tf_op jit(solution)/shard_map/ppermute | solution.py:352
  50.5 6.5 %collective-permute-start.12 = (f32[1,1,640]{2,1,0:T(1,128)S(1)}, f32[1,1,640]{2,1,0:T(1,128)S(1)}, u32[]{:S(2)}, u32[]{:S(2)}) collective-permute-start(f32[1,1,640]{2,1,0:T(1,128)S(1)} %get-tuple-element.217), channel_id=1, source_target_pairs={{0,8},{2,10},{4,12},{6,14},{8,0},{10,2},{12,4},{14,6},{1,9},{3,11}... | collective-permute-start | bytes 7688 | tf_op jit(solution)/shard_map/ppermute | solution.py:352
  52.5 4.5 %collective-permute-start.13 = (f32[1,1,640]{2,1,0:T(1,128)S(1)}, f32[1,1,640]{2,1,0:T(1,128)S(1)}, u32[]{:S(2)}, u32[]{:S(2)}) collective-permute-start(f32[1,1,640]{2,1,0:T(1,128)S(1)} %get-tuple-element.218), channel_id=1, source_target_pairs={{0,0},{2,2},{4,8},{6,10},{8,4},{10,6},{12,12},{14,14},{1,1},{3,3},... | collective-permute-start | bytes 7688 | tf_op jit(solution)/shard_map/ppermute | solution.py:352
  53.2 5.4 %copy-start.6 = (f32[2,1,640]{2,1,0:T(1,128)}, f32[2,1,640]{2,1,0:T(1,128)S(1)}, u32[]{:S(2)}) copy-start(f32[2,1,640]{2,1,0:T(1,128)S(1)} %fusion.18.refs_1_) | copy-start | bytes 15364
  53.2 5.3 %collective-permute-start.11 = (f32[1,1,640]{2,1,0:T(1,128)S(1)}, f32[1,1,640]{2,1,0:T(1,128)S(1)}, u32[]{:S(2)}, u32[]{:S(2)}) collective-permute-start(f32[1,1,640]{2,1,0:T(1,128)S(1)} %slice.23), channel_id=1, source_target_pairs={{0,4},{2,6},{4,0},{6,2},{8,12},{10,14},{12,8},{14,10},{1,5},{3,7},... | collective-permute-start | bytes 7688 | tf_op jit(solution)/shard_map/ppermute | solution.py:352
  57.0 1.6 %copy-start.7 = (f32[1,1,640]{2,1,0:T(1,128)}, f32[1,1,640]{2,1,0:T(1,128)S(1)}, u32[]{:S(2)}) copy-start(f32[1,1,640]{2,1,0:T(1,128)S(1)} %collective-permute-done.12.refs_3_) | copy-start | bytes 7684
  57.0 1.6 %copy-start.8 = (f32[1,1,640]{2,1,0:T(1,128)}, f32[1,1,640]{2,1,0:T(1,128)S(1)}, u32[]{:S(2)}) copy-start(f32[1,1,640]{2,1,0:T(1,128)S(1)} %collective-permute-done.13.refs_4_) | copy-start | bytes 7684
  58.5 0.6 copy-start.9
  61.5 0.6 copy-start.10

commit v7 on v6

--- a/solution.py
+++ b/solution.py
@@ -211,116 +211,124 @@
 ROW, PAIR_ROW = "row", "pair_row"
 DIAG, PAIR_DIAG = "diag", "pair_diag"
 NEXT, FAR = "next", "far"
-GROUPS = ((OWN, PAIR), (CORE, PAIR_CORE, DIAG, PAIR_DIAG), (ROW, PAIR_ROW), (NEXT,), (FAR,))
-
-
-def score_kernel(docs, hot, names, tasks, flagged, carries, *refs):
+GROUPS = ((OWN, PAIR), (CORE, PAIR_CORE, DIAG, PAIR_DIAG), (ROW, PAIR_ROW), (NEXT, FAR))
+HERE, THERE, ACROSS, BEYOND = (OWN, CORE), (PAIR, PAIR_CORE), (ROW, DIAG), (PAIR_ROW, PAIR_DIAG)
+
+
+def score_kernel(docs, hot, names, given, made, tasks, flagged, carries, *refs):
     rest, first, flag, lanes = layout(docs, hot)
     place_ref, refs = refs[0], refs[1:]
     blocks, refs = dict(zip(names, refs[:len(names)])), refs[len(names):]
+    pairs, refs = {p: refs[2 * k:2 * k + 2] for k, p in enumerate(given)}, refs[2 * len(given):]
     before, refs = refs[:len(GROUPS) * carries], refs[len(GROUPS) * carries:]
-    outs, (turned, parts) = refs[:len(GROUPS)], refs[len(GROUPS):]
+    outs, refs = refs[:len(GROUPS)], refs[len(GROUPS):]
+    if made:
+        pairs[made], refs = refs[:2], refs[2:]
+    parts = refs[0]
     for k, out in enumerate(outs):
         out[...] = before[k][...] if carries else jnp.zeros(out.shape, F32)
     spots = {name: (out, k) for out, group in zip(outs, GROUPS) for k, name in enumerate(group)}
     z, y, c = place_ref[0], place_ref[1], place_ref[2]
     when = {"core0": c == 0, "core1": c == 1, "row0": y == 0, "row1": y == 1}
     middle = (z == 1) | (z == 2)
-    lefts = list(dict.fromkeys(task[1] for task in tasks if task[0] != task[1]))
-    width = turned.shape[0]
 
     def meet(count, start):
         lane = slice(start, start + count)
-        wide = up(count, 128)
-        ids = {name: ref[rest:, :].astype(F32)[0:8, 0:wide] for name, ref in blocks.items()}
-        columns = {name: ids[name].T[0:count, 0:1] for name in dict.fromkeys(task[1] for task in tasks)}
-        for k in range(len(lefts)):
-            parts[k, 0:count, :] = jnp.zeros((count, 128), F32)
-
-        for right in dict.fromkeys(task[0] for task in tasks):
-
-            def work(right=right):
-                inside = lax.broadcasted_iota(jnp.int32, (1, wide), 1) < count
-                right_ids = jnp.where(inside, ids[right][0:1, :], -1.0)
-                turned[:, 0:wide] = jnp.zeros((width, wide), BF16)
-                turned[:, 0:count] = blocks[right][:count, :].T
-                for _, left, condition in [task for task in tasks if task[0] == right]:
-
-                    def one(left=left):
-                        inner = jnp.dot(
-                            blocks[left][:count, :], turned[:, 0:wide], preferred_element_type=F32
+        wide, two = up(count, 128), 2 * count
+        columns = {name: ref[rest:, 0:wide].astype(F32)[0:8, :].T[0:count, :] for name, ref in blocks.items()}
+        if made:
+            turned, notes = pairs[made]
+            turned[:, 0:two] = jnp.concatenate([blocks[name][:count, :] for name in made], axis=0).T
+            doubt = sum(blocks[name][rest:, first:first + 128].astype(F32)[0:1, 0:1] for name in made)
+            ids = jnp.concatenate([columns[name] for name in made], axis=0).T
+            notes[:, 0:two] = jnp.where(lax.broadcasted_iota(jnp.int32, ids.shape, 0) == 0, ids, doubt)
+
+        for left in dict.fromkeys(task[0] for task in tasks):
+
+            def work(left=left):
+                own_tasks = [task for task in tasks if task[0] == left]
+                for number, (_, pair, both, _) in enumerate(own_tasks):
+                    turned, notes = pairs[pair]
+                    span = two if both else wide
+                    ids = notes[0:1, 0:span]
+                    if not both:
+                        ids = jnp.where(lax.broadcasted_iota(jnp.int32, ids.shape, 1) < count, ids, -1.0)
+                    inner = jnp.dot(blocks[left][:count, :], turned[:, 0:span], preferred_element_type=F32)
+                    same = columns[left][:, 0:1] == ids
+                    diagonal = left == pair[0]
+                    if diagonal:
+                        same &= lax.broadcasted_iota(jnp.int32, inner.shape, 0) != lax.broadcasted_iota(
+                            jnp.int32, inner.shape, 1
                         )
-                        same = columns[left] == right_ids
-                        if left == right:
-                            same &= lax.broadcasted_iota(jnp.int32, inner.shape, 0) != lax.broadcasted_iota(
-                                jnp.int32, inner.shape, 1
-                            )
-                        weights = jnp.where(same, jnp.exp2(inner), 0.0)
-                        out, k = spots[right]
-                        out[k, :, lane] += jnp.sum(weights, axis=0, keepdims=True)[:, 0:count]
-                        if left != right:
-                            part = weights[:, 0:128]
-                            for t in range(128, wide, 128):
-                                part += weights[:, t:t + 128]
-                            parts[lefts.index(left), 0:count, :] += part
-
-                    if condition is None:
-                        one()
-                    else:
-                        pl.when(when[condition])(one)
-
-            if right in (NEXT, FAR):
+                    weights = jnp.where(same, jnp.exp2(inner), 0.0)
+                    total = jnp.sum(weights, axis=0, keepdims=True)
+                    for k, name in enumerate(pair[:1 + both]):
+                        out, spot = spots[name]
+                        out[spot, :, lane] += total[:, k * count:(k + 1) * count]
+                    if not diagonal:
+                        part = weights[:, 0:128]
+                        for t in range(128, span, 128):
+                            part += weights[:, t:t + 128]
+                        if number:
+                            parts[0:count, :] += part
+                        else:
+                            parts[0:count, :] = part
+                if not diagonal:
+                    part = parts[0:count, :]
+                    high = part.astype(BF16)
+                    low = (part - high.astype(F32)).astype(BF16)
+                    ones = jnp.ones((16, 128), BF16)
+                    total = sum(
+                        lax.dot_general(ones, term, (((1,), (1,)), ((), ())), preferred_element_type=F32)
+                        for term in (high, low)
+                    )
+                    out, spot = spots[left]
+                    out[spot, :, lane] += total[0:1, :]
+
+            condition = [task[3] for task in tasks if task[0] == left][0]
+            if left in (NEXT, FAR):
                 pl.when(middle)(work)
+            elif condition:
+                pl.when(when[condition])(work)
             else:
                 work()
 
-        ones = jnp.ones((16, 128), BF16)
-        for k, left in enumerate(lefts):
-            part = parts[k, 0:count, :]
-            high = part.astype(BF16)
-            low = (part - high.astype(F32)).astype(BF16)
-            total = sum(
-                lax.dot_general(ones, term, (((1,), (1,)), ((), ())), preferred_element_type=F32)
-                for term in (high, low)
-            )
-            out, spot = spots[left]
-            out[spot, :, lane] += total[0:1, :]
-
     pl.when(lax.rem(z, 2) == 0)(lambda: meet(hot, first))
     pl.when(lax.rem(z, 2) == 1)(lambda: meet(rest, 0))
 
     if flagged:
-        doubt = sum(ref[rest:, first:first + 128].astype(F32)[0:1, 0:1] for ref in blocks.values())
+        doubt = sum(notes[1:2, 0:1] for _, notes in pairs.values())
         spot = lax.broadcasted_iota(jnp.int32, (1, lanes), 1)
         for name in flagged:
             out, k = spots[name]
             out[k] += jnp.where(spot == flag, doubt, 0.0)
 
 
-def score(name, docs, hot, place, blocks, tasks, sums, flagged=(), weight=1):
+def score(name, docs, hot, place, blocks, pairs, made, tasks, sums, flagged=(), weight=1):
     rest, _, _, lanes = layout(docs, hot)
-    names = [b for b in blocks if flagged or any(b in task[:2] for task in tasks)]
-    lefts = len({task[1] for task in tasks if task[0] != task[1]})
+    names = list(dict.fromkeys([*made, *(task[0] for task in tasks)]))
+    given = [p for p in pairs if flagged or any(p == task[1] for task in tasks)]
     width = blocks[OWN].shape[1]
     vmem = pl.BlockSpec(memory_space=pltpu.VMEM)
-    arrays = [blocks[b] for b in names] + list(sums)
-    return pl.pallas_call(
-        lambda *refs: score_kernel(docs, hot, names, tasks, flagged, bool(sums), *refs),
-        out_shape=tuple(jax.ShapeDtypeStruct((len(group), 1, lanes), F32) for group in GROUPS),
+    arrays = [blocks[b] for b in names] + [a for p in given for a in pairs[p]] + list(sums)
+    shapes = [jax.ShapeDtypeStruct((len(group), 1, lanes), F32) for group in GROUPS]
+    if made:
+        shapes += [jax.ShapeDtypeStruct((width, 2 * rest), BF16), jax.ShapeDtypeStruct((8, 2 * rest), F32)]
+    out = pl.pallas_call(
+        lambda *refs: score_kernel(docs, hot, names, given, made, tasks, flagged, bool(sums), *refs),
+        out_shape=tuple(shapes),
         in_specs=[pl.BlockSpec(memory_space=pltpu.SMEM)] + [vmem] * len(arrays),
-        out_specs=tuple(vmem for _ in GROUPS),
-        scratch_shapes=[pltpu.VMEM((width, up(rest, 128)), BF16), pltpu.VMEM((lefts, rest, 128), F32)],
+        out_specs=tuple(vmem for _ in shapes),
+        scratch_shapes=[pltpu.VMEM((rest, 128), F32)],
         compiler_params=pltpu.CompilerParams(vmem_limit_bytes=20 * 2**20),
         cost_estimate=pl.CostEstimate(flops=weight, bytes_accessed=2**10, transcendentals=0),
         name=name,
     )(place, *arrays)
-
-
-def finish_kernel(flag, slot_ref, *refs):
-    sums, out_ref, doubt_ref = refs[:-2], refs[-2], refs[-1]
-    total = sums[0][0]
-    for ref in sums[1:]:
-        total += ref[0]
+    return out[:len(GROUPS)], {**pairs, made: out[len(GROUPS):]} if made else pairs
+
+
+def finish_kernel(flag, slot_ref, home_ref, more_ref, out_ref, doubt_ref):
+    total = home_ref[0] + more_ref[0]
     lanes, docs = total.shape[1], slot_ref.shape[1]
     doubt_ref[...] = (total[:, flag:flag + 1] > 0.0).astype(jnp.int32)
     values = jnp.broadcast_to(jnp.log(1.0 + total * 2.0**-SHIFT), (8, lanes)).T[:, 0:1]
@@ -328,12 +336,13 @@
     out_ref[...] = jnp.sum(jnp.where(here, values, 0.0), axis=0, keepdims=True)
 
 
-def finish(flag, slot, sums):
+def finish(flag, slot, home, more):
     return pl.pallas_call(
         lambda *refs: finish_kernel(flag, *refs),
         out_shape=(jax.ShapeDtypeStruct(slot.shape, F32), jax.ShapeDtypeStruct((1, 1), jnp.int32)),
+        compiler_params=pltpu.CompilerParams(vmem_limit_bytes=6 * 2**20),
         name="finish",
-    )(slot, *sums)
+    )(slot, home, more)
 
 
 def meeting_plan(states, proj_weight, cluster_of):
@@ -362,51 +371,52 @@
             ],
         )
 
-    STAY, OUTER, MIDDLE, TWO = (0, 1, 2, 3), (1, 0, 3, 2), (0, 2, 1, 3), (2, 3, 0, 1)
+    STAY, OUTER, MIDDLE = (0, 1, 2, 3), (1, 0, 3, 2), (0, 2, 1, 3)
     TO_MIDDLE = (2, 0, 3, 1)
 
-    def meet(name, tasks, **options):
-        return score(name, docs, hot, place, blocks, tasks, sums, **options)
-
-    blocks, sums = {OWN: same}, ()
-    blocks[NEXT] = move(other, MIDDLE)
+    def meet(name, made, tasks, **options):
+        return score(name, docs, hot, place, blocks, pairs, made, tasks, sums, **options)
+
+    blocks, pairs, sums = {OWN: same}, {}, ()
+    blocks[CORE] = move(same, STAY, core=1)
     blocks[PAIR] = move(other, OUTER)
     blocks[ROW] = move(same, STAY, row=1)
-    blocks[CORE] = move(same, STAY, core=1)
-    sums = meet("own", [(OWN, OWN, None), (OWN, CORE, "core0")], weight=2**33)
+    blocks[CORE], other = lax.optimization_barrier((blocks[CORE], other))
+    blocks[NEXT] = move(other, MIDDLE)
+    sums, pairs = meet("own", HERE, [(OWN, HERE, False, None), (CORE, HERE, False, "core0")], weight=2**33)
 
     blocks[PAIR], blocks[NEXT], _ = lax.optimization_barrier((blocks[PAIR], blocks[NEXT], sums[0]))
     blocks[FAR] = move(same, TO_MIDDLE)
     blocks[PAIR_ROW] = move(blocks[PAIR], STAY, row=1)
     blocks[PAIR_CORE] = move(blocks[PAIR], STAY, core=1)
     blocks[DIAG] = move(blocks[ROW], STAY, core=1)
-    sums = meet(
-        "pair",
-        [(PAIR, PAIR, None), (PAIR, OWN, None), (PAIR, CORE, None), (PAIR, PAIR_CORE, "core1")]
-        + [(NEXT, b, None) for b in (OWN, CORE, PAIR, PAIR_CORE)],
+    sums, pairs = meet(
+        "pair", THERE,
+        [(PAIR, THERE, False, None), (PAIR_CORE, THERE, False, "core1"), (NEXT, HERE, True, None),
+         (NEXT, THERE, True, None)],
         weight=2**33,
     )
-    sums = meet(
-        "row",
-        [(PAIR, ROW, None), (PAIR, DIAG, None), (OWN, ROW, "row0"), (OWN, DIAG, "row1"),
-         (NEXT, ROW, None), (NEXT, DIAG, None)],
+    sums, pairs = meet(
+        "row", ACROSS,
+        [(PAIR, HERE, True, None), (PAIR, ACROSS, True, None), (NEXT, ACROSS, True, None),
+         (ROW, HERE, False, "row0"), (DIAG, HERE, False, "row1")],
     )
     blocks[PAIR_ROW], _ = lax.optimization_barrier((blocks[PAIR_ROW], sums[0]))
     blocks[PAIR_DIAG] = move(blocks[PAIR_ROW], STAY, core=1)
-    sums = meet("far", [(FAR, b, None) for b in (OWN, CORE, PAIR, PAIR_CORE, ROW, DIAG)])
-    sums = meet(
-        "last",
-        [(PAIR, PAIR_ROW, "row1"), (PAIR, PAIR_DIAG, "row0")]
-        + [(b, c, None) for b in (NEXT, FAR) for c in (PAIR_ROW, PAIR_DIAG)],
-        flagged=(OWN, FAR),
-    )
-    home, by_core, by_row, to_next, to_far = sums
-    from_far, from_next = move(to_far, TWO), move(to_next, MIDDLE)
+    sums, pairs = meet("far", (), [(FAR, p, True, None) for p in (HERE, THERE, ACROSS)])
+    sums, pairs = meet(
+        "last", BEYOND,
+        [(NEXT, BEYOND, True, None), (FAR, BEYOND, True, None), (PAIR_ROW, THERE, False, "row1"),
+         (PAIR_DIAG, THERE, False, "row0")],
+        flagged=(OWN, NEXT, FAR),
+    )
+    home, by_core, by_row, by_middle = sums
+    from_middle = move(by_middle, MIDDLE)
     from_core = move(by_core, STAY, core=1)
     from_row = move(by_row + from_core[2:4], STAY, row=1)
-    home = home + from_core[0:2] + from_row
+    home = home + from_core[0:2] + from_middle + from_row
     from_pair = move(home[1:2], OUTER)
-    fast, doubt = finish(flag, slot, (home, from_pair, from_far, from_next))
+    fast, doubt = finish(flag, slot, home, from_pair)
     return lax.cond(
         doubt[0, 0] > 0, owner_plan, lambda *_: fast.reshape(docs), states, proj_weight, cluster_of
     )

time: 69.1 us -> 70 us (1.013)
  waiting for transfers between devices: 21.8 us -> 27.2 us
  starting transfers between devices: 19.4 us -> 16.3 us
    ppermute x9 -> x8, waiting for transfers between devices: 19.6 us -> 25.4 us  [move(): lax.ppermute(a, 'owner', [(z * ROWS + y, to[z] * ROWS + (y ^ row)) for z...]
    ppermute x9 -> x8, starting transfers between devices: 18.8 us -> 15.4 us  [move(): lax.ppermute(a, 'owner', [(z * ROWS + y, to[z] * ROWS + (y ^ row)) for z...]
    pallas_call x1, Pallas kernels: 1.45 us -> 0.73 us  [finish(): pl.pallas_call(lambda *refs: finish_kernel(flag, *refs), out_shape=(jax.S...]
  transfers between devices with their start and end apart: 14 -> 13, of which waited for: 6 -> 7; matrix products, arithmetic and copies ran while one was open for 0% -> 0% of each run, Pallas kernels for 8% -> 7%
where the time goes in v7:
time: 70 us; the launch traced here: 69.8 us
  waiting for transfers between devices  27.2 us (39%)
  starting transfers between devices  16.3 us (23%)
  between operations  14.1 us (20%)
  Pallas kernels  11.4 us (16%)
    ppermute x8, waiting for transfers between devices, move(): lax.ppermute(a, 'owner', [(z * ROWS + y, to[z] * ROWS + (y ^ row)) for z...  25.4 us
    ppermute x8, starting transfers between devices, move(): lax.ppermute(a, 'owner', [(z * ROWS + y, to[z] * ROWS + (y ^ row)) for z...  15.4 us
    pallas_call x5, Pallas kernels, score(): pl.pallas_call(lambda *refs: score_kernel(docs, hot, names, given, made,...  7.06 us
    pallas_call x1, Pallas kernels, prep(): pl.pallas_call(lambda *refs: prep_kernel(hot, *refs), out_shape=(shape((r...  3.56 us
    ppermute x5, waiting for transfers between devices, move(): return lax.ppermute(a, 'split', [(0, 1), (1, 0)])  1.8 us
  transfers between devices with their start and end apart: 13, of which 7 were waited for; matrix products, arithmetic and copies ran while one was open for 0% of the time, Pallas kernels for 7%

profile of v7, /device:TPU:0, one launch (start us, length us, event | category | flops | bytes accessed | tf_op | source)
XLA Modules:
  0.0 69.8 jit_solution(7335335595864325068)
XLA Ops:
  6.5 0.1 pad_add_fusion.refs_0_
  6.6 3.6 %prep.1 = (bf16[336,768]{1,0:T(8,128)(2,1)S(1)}, bf16[336,768]{1,0:T(8,128)(2,1)S(1)}, s32[1,512]{1,0:T(1,128)S(1)}) custom-call(s32[3]{0:T(128)S(1)} %pad_add_fusion.refs_0_, s32[1,512]{1,0:T(1,128)} %bitcast.38, bf16[512,1024]{1,0:T(8,128)(2,1)} %refs_2_.1, bf16[1024,768]{1,0:T(8,128)(2,1)} %refs_3_.1), custom_call_target="tpu_custom_call" | custom-call | tf_op jit(solution)/shard_map/prep/pallas_call | solution.py:195
  10.2 0.5 collective-permute-start.1
  10.7 2.6 %collective-permute-start.4 = (bf16[336,768]{1,0:T(8,128)(2,1)S(1)}, bf16[336,768]{1,0:T(8,128)(2,1)S(1)}, u32[]{:S(2)}, u32[]{:S(2)}) collective-permute-start(bf16[336,768]{1,0:T(8,128)(2,1)S(1)} %get-tuple-element.193.refs_1_), channel_id=1, source_target_pairs={{0,2},{2,0},{4,6},{6,4},{8,10},{10,8},{12,14},{14,12},{1,3},{3,1},... | collective-permute-start | bytes 1548296 | tf_op jit(solution)/shard_map/ppermute | solution.py:361
  13.3 1.6 %collective-permute-start = (bf16[336,768]{1,0:T(8,128)(2,1)S(1)}, bf16[336,768]{1,0:T(8,128)(2,1)S(1)}, u32[]{:S(2)}, u32[]{:S(2)}) collective-permute-start(bf16[336,768]{1,0:T(8,128)(2,1)S(1)} %get-tuple-element.194), channel_id=1, source_target_pairs={{0,4},{2,6},{4,0},{6,2},{8,12},{10,14},{12,8},{14,10},{1,5},{3,7},... | collective-permute-start | bytes 1548296 | tf_op jit(solution)/shard_map/ppermute | solution.py:361
  14.9 0.0 collective-permute-done.1.refs_2_
  14.9 0.7 collective-permute-start.2
  15.6 1.3 %own.1 = (f32[2,1,640]{2,1,0:T(1,128)S(1)}, f32[4,1,640]{2,1,0:T(1,128)S(1)}, f32[2,1,640]{2,1,0:T(1,128)S(1)}, f32[2,1,640]{2,1,0:T(1,128)S(1)}, bf16[768,640]{1,0:T(8,128)(2,1)S(1)}, /*index=5*/f32[8,640]{1,0:T(8,128)S(1)}) custom-call(s32[3]{0:T(128)S(1)} %pad_add_fusion.refs_0_, bf16[336,768]{1,0:T(8,128)(2,1)S(1)} %get-tuple-element.193.refs_1_, ...), custom_call_target="tpu_custom_call" | custom-call | flops 8589934592 | bytes 1024 | tf_op jit(solution)/shard_map/own/pallas_call | solution.py:317
  16.9 10.2 %collective-permute-done.refs_1_.refs_3_ = bf16[336,768]{1,0:T(8,128)(2,1)S(1)} collective-permute-done((bf16[336,768]{1,0:T(8,128)(2,1)S(1)}, bf16[336,768]{1,0:T(8,128)(2,1)S(1)}, u32[]{:S(2)}, u32[]{:S(2)}) %collective-permute-start) | collective-permute-done | bytes 516128 | tf_op jit(solution)/shard_map/ppermute | solution.py:361
  27.1 0.0 collective-permute-start.6
  27.1 5.8 %collective-permute-start.8 = (bf16[336,768]{1,0:T(8,128)(2,1)S(1)}, bf16[336,768]{1,0:T(8,128)(2,1)S(1)}, u32[]{:S(2)}, u32[]{:S(2)}) collective-permute-start(bf16[336,768]{1,0:T(8,128)(2,1)S(1)} %get-tuple-element.193.refs_1_), channel_id=1, source_target_pairs={{0,8},{2,10},{4,0},{6,2},{8,12},{10,14},{12,4},{14,6},{1,9},{3,11}... | collective-permute-start | bytes 1548296 | tf_op jit(solution)/shard_map/ppermute | solution.py:361
  32.9 0.0 collective-permute-done.4.refs_1_
  32.9 0.2 collective-permute-start.5
  33.1 0.5 collective-permute-start.3
  33.6 1.0 %pair.1 = (f32[2,1,640]{2,1,0:T(1,128)S(1)}, f32[4,1,640]{2,1,0:T(1,128)S(1)}, f32[2,1,640]{2,1,0:T(1,128)S(1)}, f32[2,1,640]{2,1,0:T(1,128)S(1)}, bf16[768,640]{1,0:T(8,128)(2,1)S(1)}, /*index=5*/f32[8,640]{1,0:T(8,128)S(1)}) custom-call(s32[3]{0:T(128)S(1)} %pad_add_fusion.refs_0_, bf16[336,768]{1,0:T(8,128)(2,1)S(1)} %collective-permute-done.refs_1_.refs_3_, ...), custom_call_target="tpu_custom_call" | custom-call | flops 8589934592 | bytes 1024 | tf_op jit(solution)/shard_map/pair/pallas_call | solution.py:317
  34.6 0.2 collective-permute-done.5.refs_2_
  34.8 1.8 %row.1 = (f32[2,1,640]{2,1,0:T(1,128)S(1)}, f32[4,1,640]{2,1,0:T(1,128)S(1)}, f32[2,1,640]{2,1,0:T(1,128)S(1)}, f32[2,1,640]{2,1,0:T(1,128)S(1)}, bf16[768,640]{1,0:T(8,128)(2,1)S(1)}, /*index=5*/f32[8,640]{1,0:T(8,128)S(1)}) custom-call(s32[3]{0:T(128)S(1)} %pad_add_fusion.refs_0_, bf16[336,768]{1,0:T(8,128)(2,1)S(1)} %collective-permute-done.4.refs_1_, ...), custom_call_target="tpu_custom_call" | custom-call | flops 1 | bytes 1024 | tf_op jit(solution)/shard_map/row/pallas_call | solution.py:317
  36.6 10.5 %collective-permute-done.3.refs_1_ = bf16[336,768]{1,0:T(8,128)(2,1)S(1)} collective-permute-done((bf16[336,768]{1,0:T(8,128)(2,1)S(1)}, bf16[336,768]{1,0:T(8,128)(2,1)S(1)}, u32[]{:S(2)}, u32[]{:S(2)}) %collective-permute-start.3) | collective-permute-done | bytes 516128 | tf_op jit(solution)/shard_map/ppermute | solution.py:361
  47.1 0.6 far.1
  47.7 1.2 %collective-permute-done.7.refs_2_ = bf16[336,768]{1,0:T(8,128)(2,1)S(1)} collective-permute-done((bf16[336,768]{1,0:T(8,128)(2,1)S(1)}, bf16[336,768]{1,0:T(8,128)(2,1)S(1)}, u32[]{:S(2)}, u32[]{:S(2)}) %collective-permute-start.7) | collective-permute-done | bytes 516128 | tf_op jit(solution)/shard_map/ppermute | solution.py:365
  49.0 2.3 %last.1 = (f32[2,1,640]{2,1,0:T(1,128)S(1)}, f32[4,1,640]{2,1,0:T(1,128)S(1)}, f32[2,1,640]{2,1,0:T(1,128)S(1)}, f32[2,1,640]{2,1,0:T(1,128)S(1)}, bf16[768,640]{1,0:T(8,128)(2,1)}, /*index=5*/f32[8,640]{1,0:T(8,128)}) custom-call(s32[3]{0:T(128)S(1)} %pad_add_fusion.refs_0_, bf16[336,768]{1,0:T(8,128)(2,1)S(1)} %collective-permute-done.3.refs_1_, ...), custom_call_target="tpu_custom_call" | custom-call | flops 1 | bytes 1024 | tf_op jit(solution)/shard_map/last/pallas_call | solution.py:317
  51.3 0.1 collective-permute-start.9
  51.4 0.6 collective-permute-start.10
  52.1 0.4 collective-permute-done.9
  52.5 0.6 collective-permute-start.11
  53.1 3.1 %collective-permute-done.11 = f32[2,1,640]{2,1,0:T(1,128)S(1)} collective-permute-done((f32[2,1,640]{2,1,0:T(1,128)S(1)}, f32[2,1,640]{2,1,0:T(1,128)S(1)}, u32[]{:S(2)}, u32[]{:S(2)}) %collective-permute-start.11) | collective-permute-done | bytes 5152 | tf_op jit(solution)/shard_map/ppermute | solution.py:361
  56.2 3.0 %collective-permute-start.12 = (f32[1,1,640]{2,1,0:T(1,128)S(1)}, f32[1,1,640]{2,1,0:T(1,128)S(1)}, u32[]{:S(2)}, u32[]{:S(2)}) collective-permute-start(f32[1,1,640]{2,1,0:T(1,128)S(1)} %slice.23), channel_id=1, source_target_pairs={{0,4},{2,6},{4,0},{6,2},{8,12},{10,14},{12,8},{14,10},{1,5},{3,7},... | collective-permute-start | bytes 7688 | tf_op jit(solution)/shard_map/ppermute | solution.py:361
  59.2 1.6 %collective-permute-done.12.refs_2_ = f32[1,1,640]{2,1,0:T(1,128)S(1)} collective-permute-done((f32[1,1,640]{2,1,0:T(1,128)S(1)}, f32[1,1,640]{2,1,0:T(1,128)S(1)}, u32[]{:S(2)}, u32[]{:S(2)}) %collective-permute-start.12) | collective-permute-done | bytes 2592 | tf_op jit(solution)/shard_map/ppermute | solution.py:361
  60.7 0.7 %finish.1 = (f32[1,512]{1,0:T(1,128)S(1)}, s32[1,1]{1,0:T(1,128)}) custom-call(s32[1,512]{1,0:T(1,128)S(1)} %get-tuple-element.191.refs_0_, f32[2,1,640]{2,1,0:T(1,128)S(1)} %fusion.19.refs_1_, f32[1,1,640]{2,1,0:T(1,128)S(1)} %collective-permute-done.12.refs_2_), custom_call_target="tpu_custom_call" | custom-call | tf_op jit(solution)/shard_map/finish/pallas_call | solution.py:340
  62.2 0.3 conditional.1
  62.4 0.0 copy-start.5
  62.4 0.6 copy-done.5
  (12 shorter events, 0.0 us)
Async XLA Ops:
  10.2 4.7 %collective-permute-start.1 = (bf16[336,768]{1,0:T(8,128)(2,1)S(1)}, bf16[336,768]{1,0:T(8,128)(2,1)S(1)}, u32[]{:S(2)}, u32[]{:S(2)}) collective-permute-start(bf16[336,768]{1,0:T(8,128)(2,1)S(1)} %get-tuple-element.193.refs_1_), channel_id=1, source_target_pairs={{0,1},{1,0},{2,3},{3,2},{4,5},{5,4},{6,7},{7,6},{8,9},{9,8},{10,11... | collective-permute-start | bytes 1548296 | tf_op jit(solution)/shard_map/ppermute | solution.py:365
  10.7 22.2 %collective-permute-start.4 = (bf16[336,768]{1,0:T(8,128)(2,1)S(1)}, bf16[336,768]{1,0:T(8,128)(2,1)S(1)}, u32[]{:S(2)}, u32[]{:S(2)}) collective-permute-start(bf16[336,768]{1,0:T(8,128)(2,1)S(1)} %get-tuple-element.193.refs_1_), channel_id=1, source_target_pairs={{0,2},{2,0},{4,6},{6,4},{8,10},{10,8},{12,14},{14,12},{1,3},{3,1},... | collective-permute-start | bytes 1548296 | tf_op jit(solution)/shard_map/ppermute | solution.py:361
  13.3 13.8 %collective-permute-start = (bf16[336,768]{1,0:T(8,128)(2,1)S(1)}, bf16[336,768]{1,0:T(8,128)(2,1)S(1)}, u32[]{:S(2)}, u32[]{:S(2)}) collective-permute-start(bf16[336,768]{1,0:T(8,128)(2,1)S(1)} %get-tuple-element.194), channel_id=1, source_target_pairs={{0,4},{2,6},{4,0},{6,2},{8,12},{10,14},{12,8},{14,10},{1,5},{3,7},... | collective-permute-start | bytes 1548296 | tf_op jit(solution)/shard_map/ppermute | solution.py:361
  14.9 12.2 %collective-permute-start.2 = (bf16[336,768]{1,0:T(8,128)(2,1)S(1)}, bf16[336,768]{1,0:T(8,128)(2,1)S(1)}, u32[]{:S(2)}, u32[]{:S(2)}) collective-permute-start(bf16[336,768]{1,0:T(8,128)(2,1)S(1)} %get-tuple-element.194), channel_id=1, source_target_pairs={{0,0},{2,2},{4,8},{6,10},{8,4},{10,6},{12,12},{14,14},{1,1},{3,3},... | collective-permute-start | bytes 1548296 | tf_op jit(solution)/shard_map/ppermute | solution.py:361
  27.1 6.5 %collective-permute-start.6 = (bf16[336,768]{1,0:T(8,128)(2,1)S(1)}, bf16[336,768]{1,0:T(8,128)(2,1)S(1)}, u32[]{:S(2)}, u32[]{:S(2)}) collective-permute-start(bf16[336,768]{1,0:T(8,128)(2,1)S(1)} %collective-permute-done.refs_1_.refs_3_), channel_id=1, source_target_pairs={{0,1},{1,0},{2,3},{3,2},{4,5},{5,4},{6,7},{7,6},{8,9},{9,8},{10,11... | collective-permute-start | bytes 1548296 | tf_op jit(solution)/shard_map/ppermute | solution.py:365
  27.1 19.9 %collective-permute-start.8 = (bf16[336,768]{1,0:T(8,128)(2,1)S(1)}, bf16[336,768]{1,0:T(8,128)(2,1)S(1)}, u32[]{:S(2)}, u32[]{:S(2)}) collective-permute-start(bf16[336,768]{1,0:T(8,128)(2,1)S(1)} %get-tuple-element.193.refs_1_), channel_id=1, source_target_pairs={{0,8},{2,10},{4,0},{6,2},{8,12},{10,14},{12,4},{14,6},{1,9},{3,11}... | collective-permute-start | bytes 1548296 | tf_op jit(solution)/shard_map/ppermute | solution.py:361
  32.9 1.9 %collective-permute-start.5 = (bf16[336,768]{1,0:T(8,128)(2,1)S(1)}, bf16[336,768]{1,0:T(8,128)(2,1)S(1)}, u32[]{:S(2)}, u32[]{:S(2)}) collective-permute-start(bf16[336,768]{1,0:T(8,128)(2,1)S(1)} %collective-permute-done.4.refs_1_), channel_id=1, source_target_pairs={{0,1},{1,0},{2,3},{3,2},{4,5},{5,4},{6,7},{7,6},{8,9},{9,8},{10,11... | collective-permute-start | bytes 1548296 | tf_op jit(solution)/shard_map/ppermute | solution.py:365
  33.1 13.9 %collective-permute-start.3 = (bf16[336,768]{1,0:T(8,128)(2,1)S(1)}, bf16[336,768]{1,0:T(8,128)(2,1)S(1)}, u32[]{:S(2)}, u32[]{:S(2)}) collective-permute-start(bf16[336,768]{1,0:T(8,128)(2,1)S(1)} %collective-permute-done.refs_1_.refs_3_), channel_id=1, source_target_pairs={{0,2},{2,0},{4,6},{6,4},{8,10},{10,8},{12,14},{14,12},{1,3},{3,1},... | collective-permute-start | bytes 1548296 | tf_op jit(solution)/shard_map/ppermute | solution.py:361
  47.1 1.9 %collective-permute-start.7 = (bf16[336,768]{1,0:T(8,128)(2,1)S(1)}, bf16[336,768]{1,0:T(8,128)(2,1)S(1)}, u32[]{:S(2)}, u32[]{:S(2)}) collective-permute-start(bf16[336,768]{1,0:T(8,128)(2,1)S(1)} %collective-permute-done.3.refs_1_), channel_id=1, source_target_pairs={{0,1},{1,0},{2,3},{3,2},{4,5},{5,4},{6,7},{7,6},{8,9},{9,8},{10,11... | collective-permute-start | bytes 1548296 | tf_op jit(solution)/shard_map/ppermute | solution.py:365
  49.0 13.2 %copy-start.2 = (bf16[512,1024]{1,0:T(8,128)(2,1)S(1)}, bf16[512,1024]{1,0:T(8,128)(2,1)}, u32[]{:S(2)}) copy-start(bf16[512,1024]{1,0:T(8,128)(2,1)} %refs_2_.1) | copy-start | bytes 3145732
  49.0 13.2 %copy-start.4 = (s32[512]{0:T(512)S(1)}, s32[512]{0:T(512)}, u32[]{:S(2)}) copy-start(s32[512]{0:T(512)} %param.9) | copy-start | bytes 6148
  51.3 1.2 %collective-permute-start.9 = (f32[4,1,640]{2,1,0:T(1,128)S(1)}, f32[4,1,640]{2,1,0:T(1,128)S(1)}, u32[]{:S(2)}, u32[]{:S(2)}) collective-permute-start(f32[4,1,640]{2,1,0:T(1,128)S(1)} %get-tuple-element.222), channel_id=1, source_target_pairs={{0,1},{1,0},{2,3},{3,2},{4,5},{5,4},{6,7},{7,6},{8,9},{9,8},{10,11... | collective-permute-start | bytes 30728 | tf_op jit(solution)/shard_map/ppermute | solution.py:365
  51.4 1.6 %collective-permute-start.10 = (f32[2,1,640]{2,1,0:T(1,128)S(1)}, f32[2,1,640]{2,1,0:T(1,128)S(1)}, u32[]{:S(2)}, u32[]{:S(2)}) collective-permute-start(f32[2,1,640]{2,1,0:T(1,128)S(1)} %get-tuple-element.223), channel_id=1, source_target_pairs={{0,0},{2,2},{4,8},{6,10},{8,4},{10,6},{12,12},{14,14},{1,1},{3,3},... | collective-permute-start | bytes 15368 | tf_op jit(solution)/shard_map/ppermute | solution.py:361
  52.5 3.7 %collective-permute-start.11 = (f32[2,1,640]{2,1,0:T(1,128)S(1)}, f32[2,1,640]{2,1,0:T(1,128)S(1)}, u32[]{:S(2)}, u32[]{:S(2)}) collective-permute-start(f32[2,1,640]{2,1,0:T(1,128)S(1)} %slice_add_fusion), channel_id=1, source_target_pairs={{0,2},{2,0},{4,6},{6,4},{8,10},{10,8},{12,14},{14,12},{1,3},{3,1},... | collective-permute-start | bytes 15368 | tf_op jit(solution)/shard_map/ppermute | solution.py:361
  56.2 4.6 %collective-permute-start.12 = (f32[1,1,640]{2,1,0:T(1,128)S(1)}, f32[1,1,640]{2,1,0:T(1,128)S(1)}, u32[]{:S(2)}, u32[]{:S(2)}) collective-permute-start(f32[1,1,640]{2,1,0:T(1,128)S(1)} %slice.23), channel_id=1, source_target_pairs={{0,4},{2,6},{4,0},{6,2},{8,12},{10,14},{12,8},{14,10},{1,5},{3,7},... | collective-permute-start | bytes 7688 | tf_op jit(solution)/shard_map/ppermute | solution.py:361
  62.4 0.6 copy-start.5

commit v8 on v7

--- a/solution.py
+++ b/solution.py
@@ -212,7 +212,7 @@
 DIAG, PAIR_DIAG = "diag", "pair_diag"
 NEXT, FAR = "next", "far"
 GROUPS = ((OWN, PAIR), (CORE, PAIR_CORE, DIAG, PAIR_DIAG), (ROW, PAIR_ROW), (NEXT, FAR))
-HERE, THERE, ACROSS, BEYOND = (OWN, CORE), (PAIR, PAIR_CORE), (ROW, DIAG), (PAIR_ROW, PAIR_DIAG)
+HERE, THERE, ACROSS = (OWN, CORE), (PAIR, PAIR_CORE), (ROW, DIAG)
 
 
 def score_kernel(docs, hot, names, given, made, tasks, flagged, carries, *refs):
@@ -247,28 +247,40 @@
 
             def work(left=left):
                 own_tasks = [task for task in tasks if task[0] == left]
-                for number, (_, pair, both, _) in enumerate(own_tasks):
-                    turned, notes = pairs[pair]
-                    span = two if both else wide
-                    ids = notes[0:1, 0:span]
-                    if not both:
-                        ids = jnp.where(lax.broadcasted_iota(jnp.int32, ids.shape, 1) < count, ids, -1.0)
-                    inner = jnp.dot(blocks[left][:count, :], turned[:, 0:span], preferred_element_type=F32)
+                for number, (_, right, both, _) in enumerate(own_tasks):
+                    if right in blocks:
+                        span, rights, diagonal = count, (right,), False
+                        ids = blocks[right][rest:, 0:wide].astype(F32)[0:1, 0:count]
+                        inner = lax.dot_general(
+                            blocks[left][:count, :], blocks[right][:count, :], (((1,), (1,)), ((), ())),
+                            preferred_element_type=F32,
+                        )
+                    else:
+                        turned, notes = pairs[right]
+                        span, rights, diagonal = two if both else wide, right[:1 + both], left == right[0]
+                        ids = notes[0:1, 0:span]
+                        if not both:
+                            ids = jnp.where(lax.broadcasted_iota(jnp.int32, ids.shape, 1) < count, ids, -1.0)
+                        inner = jnp.dot(
+                            blocks[left][:count, :], turned[:, 0:span], preferred_element_type=F32
+                        )
                     same = columns[left][:, 0:1] == ids
-                    diagonal = left == pair[0]
                     if diagonal:
                         same &= lax.broadcasted_iota(jnp.int32, inner.shape, 0) != lax.broadcasted_iota(
                             jnp.int32, inner.shape, 1
                         )
                     weights = jnp.where(same, jnp.exp2(inner), 0.0)
                     total = jnp.sum(weights, axis=0, keepdims=True)
-                    for k, name in enumerate(pair[:1 + both]):
+                    for k, name in enumerate(rights):
                         out, spot = spots[name]
                         out[spot, :, lane] += total[:, k * count:(k + 1) * count]
                     if not diagonal:
                         part = weights[:, 0:128]
-                        for t in range(128, span, 128):
+                        for t in range(128, span - span % 128, 128):
                             part += weights[:, t:t + 128]
+                        if span % 128:
+                            rest_of = weights[:, span - span % 128:]
+                            part += jnp.concatenate([rest_of, jnp.zeros((count, 128 - span % 128), F32)], axis=1)
                         if number:
                             parts[0:count, :] += part
                         else:
@@ -298,6 +310,7 @@
 
     if flagged:
         doubt = sum(notes[1:2, 0:1] for _, notes in pairs.values())
+        doubt += sum(blocks[b][rest:, first:first + 128].astype(F32)[0:1, 0:1] for b in (PAIR_ROW, PAIR_DIAG))
         spot = lax.broadcasted_iota(jnp.int32, (1, lanes), 1)
         for name in flagged:
             out, k = spots[name]
@@ -327,19 +340,18 @@
     return out[:len(GROUPS)], {**pairs, made: out[len(GROUPS):]} if made else pairs
 
 
-def finish_kernel(flag, slot_ref, home_ref, more_ref, out_ref, doubt_ref):
+def finish_kernel(slot_ref, home_ref, more_ref, out_ref):
     total = home_ref[0] + more_ref[0]
     lanes, docs = total.shape[1], slot_ref.shape[1]
-    doubt_ref[...] = (total[:, flag:flag + 1] > 0.0).astype(jnp.int32)
     values = jnp.broadcast_to(jnp.log(1.0 + total * 2.0**-SHIFT), (8, lanes)).T[:, 0:1]
     here = lax.broadcasted_iota(jnp.int32, (lanes, docs), 0) == slot_ref[...]
     out_ref[...] = jnp.sum(jnp.where(here, values, 0.0), axis=0, keepdims=True)
 
 
-def finish(flag, slot, home, more):
+def finish(slot, home, more):
     return pl.pallas_call(
-        lambda *refs: finish_kernel(flag, *refs),
-        out_shape=(jax.ShapeDtypeStruct(slot.shape, F32), jax.ShapeDtypeStruct((1, 1), jnp.int32)),
+        finish_kernel,
+        out_shape=jax.ShapeDtypeStruct(slot.shape, F32),
         compiler_params=pltpu.CompilerParams(vmem_limit_bytes=6 * 2**20),
         name="finish",
     )(slot, home, more)
@@ -357,19 +369,14 @@
     same, other, slot = prep(hot, place, cluster_of, states, proj_weight)
 
     def move(a, to, row=0, core=0):
-        if not core:
-            return lax.ppermute(
-                a, "owner", [(z * ROWS + y, to[z] * ROWS + (y ^ row)) for z in range(columns) for y in range(ROWS)]
+        pairs = [
+            (
+                (z * ROWS + y) * 2 + c,
+                (to[z] * ROWS + (y ^ row)) * 2 + (c ^ (core if row or to[z] != z else 1)),
             )
-        if not row and to == STAY:
-            return lax.ppermute(a, "split", [(0, 1), (1, 0)])
-        return lax.ppermute(
-            a, ("owner", "split"),
-            [
-                ((z * ROWS + y) * 2 + c, (to[z] * ROWS + (y ^ row)) * 2 + (c ^ core))
-                for z in range(columns) for y in range(ROWS) for c in range(2)
-            ],
-        )
+            for z in range(columns) for y in range(ROWS) for c in range(2)
+        ]
+        return lax.ppermute(a, ("owner", "split"), pairs)
 
     STAY, OUTER, MIDDLE = (0, 1, 2, 3), (1, 0, 3, 2), (0, 2, 1, 3)
     TO_MIDDLE = (2, 0, 3, 1)
@@ -385,7 +392,8 @@
     blocks[NEXT] = move(other, MIDDLE)
     sums, pairs = meet("own", HERE, [(OWN, HERE, False, None), (CORE, HERE, False, "core0")], weight=2**33)
 
-    blocks[PAIR], blocks[NEXT], _ = lax.optimization_barrier((blocks[PAIR], blocks[NEXT], sums[0]))
+    blocks[PAIR], _ = lax.optimization_barrier((blocks[PAIR], sums[0]))
+    blocks[ROW], blocks[NEXT] = lax.optimization_barrier((blocks[ROW], blocks[NEXT]))
     blocks[FAR] = move(same, TO_MIDDLE)
     blocks[PAIR_ROW] = move(blocks[PAIR], STAY, row=1)
     blocks[PAIR_CORE] = move(blocks[PAIR], STAY, core=1)
@@ -405,9 +413,9 @@
     blocks[PAIR_DIAG] = move(blocks[PAIR_ROW], STAY, core=1)
     sums, pairs = meet("far", (), [(FAR, p, True, None) for p in (HERE, THERE, ACROSS)])
     sums, pairs = meet(
-        "last", BEYOND,
-        [(NEXT, BEYOND, True, None), (FAR, BEYOND, True, None), (PAIR_ROW, THERE, False, "row1"),
-         (PAIR_DIAG, THERE, False, "row0")],
+        "last", (),
+        [(left, right, False, None) for left in (NEXT, FAR) for right in (PAIR_ROW, PAIR_DIAG)]
+        + [(PAIR_ROW, THERE, False, "row1"), (PAIR_DIAG, THERE, False, "row0")],
         flagged=(OWN, NEXT, FAR),
     )
     home, by_core, by_row, by_middle = sums
@@ -416,10 +424,9 @@
     from_row = move(by_row + from_core[2:4], STAY, row=1)
     home = home + from_core[0:2] + from_middle + from_row
     from_pair = move(home[1:2], OUTER)
-    fast, doubt = finish(flag, slot, home, from_pair)
-    return lax.cond(
-        doubt[0, 0] > 0, owner_plan, lambda *_: fast.reshape(docs), states, proj_weight, cluster_of
-    )
+    fast = finish(slot, home, from_pair)
+    doubt = home[0, 0, flag] + from_pair[0, 0, flag] > 0.0
+    return lax.cond(doubt, owner_plan, lambda *_: fast.reshape(docs), states, proj_weight, cluster_of)
 
 
 def on_device(states, proj_weight, cluster_of):

time: 70 us -> 66 us (0.943)
  starting transfers between devices: 16.3 us -> 11.4 us
  Pallas kernels: 11.4 us -> 10 us
  local copies, waits for them, and re-layouts: 0.58 us -> 1.81 us
  between operations: 14.1 us -> 14.8 us
    ppermute x13, starting transfers between devices: 16.3 us -> 11.4 us  [move(): return lax.ppermute(a, ('owner', 'split'), pairs)]
    slice x0 -> x2, local copies, waits for them, and re-layouts: none -> 1.23 us  [meeting_plan(): doubt = home[0, 0, flag] + from_pair[0, 0, flag] > 0.0]
    pallas_call x5, Pallas kernels: 7.06 us -> 6.01 us  [score(): pl.pallas_call(lambda *refs: score_kernel(docs, hot, names, given, made,...]
  transfers between devices with their start and end apart: 13 -> 13, of which waited for: 7 -> 7; matrix products, arithmetic and copies ran while one was open for 0% -> 1% of each run, Pallas kernels for 7% -> 7%
where the time goes in v8:
time: 66 us; the launch traced here: 65.8 us
  waiting for transfers between devices  27.5 us (42%)
  between operations  14.8 us (22%)
  starting transfers between devices  11.4 us (17%)
  Pallas kernels  10 us (15%)
  local copies, waits for them, and re-layouts  1.81 us (3%)
    ppermute x13, waiting for transfers between devices, move(): return lax.ppermute(a, ('owner', 'split'), pairs)  27.5 us
    ppermute x13, starting transfers between devices, move(): return lax.ppermute(a, ('owner', 'split'), pairs)  11.4 us
    pallas_call x5, Pallas kernels, score(): pl.pallas_call(lambda *refs: score_kernel(docs, hot, names, given, made,...  6.01 us
    pallas_call x1, Pallas kernels, prep(): pl.pallas_call(lambda *refs: prep_kernel(hot, *refs), out_shape=(shape((r...  3.56 us
  transfers between devices with their start and end apart: 13, of which 7 were waited for; matrix products, arithmetic and copies ran while one was open for 1% of the time, Pallas kernels for 7%

profile of v8, /device:TPU:0, one launch (start us, length us, event | category | flops | bytes accessed | tf_op | source)
XLA Modules:
  0.0 65.8 jit_solution(12791035150798594672)
XLA Ops:
  6.5 0.1 pad_add_fusion.refs_0_
  6.6 3.6 %prep.1 = (bf16[336,768]{1,0:T(8,128)(2,1)S(1)}, bf16[336,768]{1,0:T(8,128)(2,1)S(1)}, s32[1,512]{1,0:T(1,128)S(1)}) custom-call(s32[3]{0:T(128)S(1)} %pad_add_fusion.refs_0_, s32[1,512]{1,0:T(1,128)} %bitcast.38, bf16[512,1024]{1,0:T(8,128)(2,1)} %refs_2_.1, bf16[1024,768]{1,0:T(8,128)(2,1)} %refs_3_.1), custom_call_target="tpu_custom_call" | custom-call | tf_op jit(solution)/shard_map/prep/pallas_call | solution.py:195
  10.2 0.5 collective-permute-start.1
  10.7 2.6 %collective-permute-start = (bf16[336,768]{1,0:T(8,128)(2,1)S(1)}, bf16[336,768]{1,0:T(8,128)(2,1)S(1)}, u32[]{:S(2)}, u32[]{:S(2)}) collective-permute-start(bf16[336,768]{1,0:T(8,128)(2,1)S(1)} %get-tuple-element.190.refs_1_), channel_id=1, source_target_pairs={{0,2},{1,3},{2,0},{3,1},{4,6},{5,7},{6,4},{7,5},{8,10},{9,11},{10,... | collective-permute-start | bytes 1548296 | tf_op jit(solution)/shard_map/ppermute | solution.py:379
  13.3 1.6 %collective-permute-start.4 = (bf16[336,768]{1,0:T(8,128)(2,1)S(1)}, bf16[336,768]{1,0:T(8,128)(2,1)S(1)}, u32[]{:S(2)}, u32[]{:S(2)}) collective-permute-start(bf16[336,768]{1,0:T(8,128)(2,1)S(1)} %get-tuple-element.192), channel_id=1, source_target_pairs={{0,4},{1,5},{2,6},{3,7},{4,0},{5,1},{6,2},{7,3},{8,12},{9,13},{10,... | collective-permute-start | bytes 1548296 | tf_op jit(solution)/shard_map/ppermute | solution.py:379
  14.9 0.0 collective-permute-done.1.refs_2_
  14.9 1.3 %own.1 = (f32[2,1,640]{2,1,0:T(1,128)S(1)}, f32[4,1,640]{2,1,0:T(1,128)S(1)}, f32[2,1,640]{2,1,0:T(1,128)S(1)}, f32[2,1,640]{2,1,0:T(1,128)S(1)}, bf16[768,640]{1,0:T(8,128)(2,1)S(1)}, /*index=5*/f32[8,640]{1,0:T(8,128)S(1)}) custom-call(s32[3]{0:T(128)S(1)} %pad_add_fusion.refs_0_, bf16[336,768]{1,0:T(8,128)(2,1)S(1)} %get-tuple-element.190.refs_1_, ...), custom_call_target="tpu_custom_call" | custom-call | flops 8589934592 | bytes 1024 | tf_op jit(solution)/shard_map/own/pallas_call | solution.py:330
  16.2 10.9 %collective-permute-done.4.refs_1_.refs_3_ = bf16[336,768]{1,0:T(8,128)(2,1)S(1)} collective-permute-done((bf16[336,768]{1,0:T(8,128)(2,1)S(1)}, bf16[336,768]{1,0:T(8,128)(2,1)S(1)}, u32[]{:S(2)}, u32[]{:S(2)}) %collective-permute-start.4) | collective-permute-done | bytes 516128 | tf_op jit(solution)/shard_map/ppermute | solution.py:379
  27.1 2.6 %collective-permute-start.3 = (bf16[336,768]{1,0:T(8,128)(2,1)S(1)}, bf16[336,768]{1,0:T(8,128)(2,1)S(1)}, u32[]{:S(2)}, u32[]{:S(2)}) collective-permute-start(bf16[336,768]{1,0:T(8,128)(2,1)S(1)} %get-tuple-element.190.refs_1_), channel_id=1, source_target_pairs={{0,8},{1,9},{2,10},{3,11},{4,0},{5,1},{6,2},{7,3},{8,12},{9,13},{1... | collective-permute-start | bytes 1548296 | tf_op jit(solution)/shard_map/ppermute | solution.py:379
  29.7 0.5 collective-permute-start.5
  30.2 0.0 collective-permute-start.6
  30.2 1.0 %pair.1 = (f32[2,1,640]{2,1,0:T(1,128)S(1)}, f32[4,1,640]{2,1,0:T(1,128)S(1)}, f32[2,1,640]{2,1,0:T(1,128)S(1)}, f32[2,1,640]{2,1,0:T(1,128)S(1)}, bf16[768,640]{1,0:T(8,128)(2,1)S(1)}, /*index=5*/f32[8,640]{1,0:T(8,128)S(1)}) custom-call(s32[3]{0:T(128)S(1)} %pad_add_fusion.refs_0_, bf16[336,768]{1,0:T(8,128)(2,1)S(1)} %collective-permute-done.4.refs_1_.refs_3_, ...), custom_call_target="tpu_custom_call" | custom-call | flops 8589934592 | bytes 1024 | tf_op jit(solution)/shard_map/pair/pallas_call | solution.py:330
  31.2 0.9 %collective-permute-done.6.refs_2_ = bf16[336,768]{1,0:T(8,128)(2,1)S(1)} collective-permute-done((bf16[336,768]{1,0:T(8,128)(2,1)S(1)}, bf16[336,768]{1,0:T(8,128)(2,1)S(1)}, u32[]{:S(2)}, u32[]{:S(2)}) %collective-permute-start.6) | collective-permute-done | bytes 516128 | tf_op jit(solution)/shard_map/ppermute | solution.py:379
  32.1 1.8 %row.1 = (f32[2,1,640]{2,1,0:T(1,128)S(1)}, f32[4,1,640]{2,1,0:T(1,128)S(1)}, f32[2,1,640]{2,1,0:T(1,128)S(1)}, f32[2,1,640]{2,1,0:T(1,128)S(1)}, bf16[768,640]{1,0:T(8,128)(2,1)S(1)}, /*index=5*/f32[8,640]{1,0:T(8,128)S(1)}) custom-call(s32[3]{0:T(128)S(1)} %pad_add_fusion.refs_0_, bf16[336,768]{1,0:T(8,128)(2,1)S(1)} %collective-permute-done.refs_1_, ...), custom_call_target="tpu_custom_call" | custom-call | flops 1 | bytes 1024 | tf_op jit(solution)/shard_map/row/pallas_call | solution.py:330
  33.9 9.7 %collective-permute-done.5.refs_3_ = bf16[336,768]{1,0:T(8,128)(2,1)S(1)} collective-permute-done((bf16[336,768]{1,0:T(8,128)(2,1)S(1)}, bf16[336,768]{1,0:T(8,128)(2,1)S(1)}, u32[]{:S(2)}, u32[]{:S(2)}) %collective-permute-start.5) | collective-permute-done | bytes 516128 | tf_op jit(solution)/shard_map/ppermute | solution.py:379
  43.6 0.0 collective-permute-start.8
  43.6 0.6 far.1
  44.2 1.2 %collective-permute-done.8.refs_4_ = bf16[336,768]{1,0:T(8,128)(2,1)S(1)} collective-permute-done((bf16[336,768]{1,0:T(8,128)(2,1)S(1)}, bf16[336,768]{1,0:T(8,128)(2,1)S(1)}, u32[]{:S(2)}, u32[]{:S(2)}) %collective-permute-start.8) | collective-permute-done | bytes 516128 | tf_op jit(solution)/shard_map/ppermute | solution.py:379
  45.5 1.3 %last.1 = (f32[2,1,640]{2,1,0:T(1,128)S(1)}, f32[4,1,640]{2,1,0:T(1,128)S(1)}, f32[2,1,640]{2,1,0:T(1,128)S(1)}, f32[2,1,640]{2,1,0:T(1,128)S(1)}) custom-call(s32[3]{0:T(128)S(1)} %pad_add_fusion.refs_0_, bf16[336,768]{1,0:T(8,128)(2,1)S(1)} %collective-permute-done.2.refs_3_.refs_4_.refs_1_, bf16[336,768]{1,0:T(8,128)(2,1)S(1)} %collective-permute-done.3.refs_1_.refs_2_, ...), custom_call_target="tpu_custom_call" | custom-call | flops 1 | bytes 1024 | tf_op jit(solution)/shard_map/last/pallas_call | solution.py:330
  46.7 0.1 collective-permute-start.9
  46.9 0.4 collective-permute-start.10
  47.3 0.7 %collective-permute-done.9 = f32[4,1,640]{2,1,0:T(1,128)S(1)} collective-permute-done((f32[4,1,640]{2,1,0:T(1,128)S(1)}, f32[4,1,640]{2,1,0:T(1,128)S(1)}, u32[]{:S(2)}, u32[]{:S(2)}) %collective-permute-start.9) | collective-permute-done | bytes 10272 | tf_op jit(solution)/shard_map/ppermute | solution.py:379
  47.9 0.6 collective-permute-start.11
  48.5 3.1 %collective-permute-done.11 = f32[2,1,640]{2,1,0:T(1,128)S(1)} collective-permute-done((f32[2,1,640]{2,1,0:T(1,128)S(1)}, f32[2,1,640]{2,1,0:T(1,128)S(1)}, u32[]{:S(2)}, u32[]{:S(2)}) %collective-permute-start.11) | collective-permute-done | bytes 5152 | tf_op jit(solution)/shard_map/ppermute | solution.py:379
  51.6 2.5 %collective-permute-start.12 = (f32[1,1,640]{2,1,0:T(1,128)S(1)}, f32[1,1,640]{2,1,0:T(1,128)S(1)}, u32[]{:S(2)}, u32[]{:S(2)}) collective-permute-start(f32[1,1,640]{2,1,0:T(1,128)S(1)} %slice.32), channel_id=1, source_target_pairs={{0,4},{1,5},{2,6},{3,7},{4,0},{5,1},{6,2},{7,3},{8,12},{9,13},{10,... | collective-permute-start | bytes 7688 | tf_op jit(solution)/shard_map/ppermute | solution.py:379
  54.2 0.6 slice.31
  54.7 1.0 %collective-permute-done.12.more_ref = f32[1,1,640]{2,1,0:T(1,128)S(1)} collective-permute-done((f32[1,1,640]{2,1,0:T(1,128)S(1)}, f32[1,1,640]{2,1,0:T(1,128)S(1)}, u32[]{:S(2)}, u32[]{:S(2)}) %collective-permute-start.12) | collective-permute-done | bytes 2592 | tf_op jit(solution)/shard_map/ppermute | solution.py:379
  55.7 0.6 slice.33
  57.7 0.5 finish.1
  58.1 0.3 conditional.1
  58.4 0.0 copy-start.5
  58.4 0.6 copy-done.5
  (14 shorter events, 0.0 us)
Async XLA Ops:
  10.2 4.7 %collective-permute-start.1 = (bf16[336,768]{1,0:T(8,128)(2,1)S(1)}, bf16[336,768]{1,0:T(8,128)(2,1)S(1)}, u32[]{:S(2)}, u32[]{:S(2)}) collective-permute-start(bf16[336,768]{1,0:T(8,128)(2,1)S(1)} %get-tuple-element.190.refs_1_), channel_id=1, source_target_pairs={{0,1},{1,0},{2,3},{3,2},{4,5},{5,4},{6,7},{7,6},{8,9},{9,8},{10,11... | collective-permute-start | bytes 1548296 | tf_op jit(solution)/shard_map/ppermute | solution.py:379
  10.7 19.5 %collective-permute-start = (bf16[336,768]{1,0:T(8,128)(2,1)S(1)}, bf16[336,768]{1,0:T(8,128)(2,1)S(1)}, u32[]{:S(2)}, u32[]{:S(2)}) collective-permute-start(bf16[336,768]{1,0:T(8,128)(2,1)S(1)} %get-tuple-element.190.refs_1_), channel_id=1, source_target_pairs={{0,2},{1,3},{2,0},{3,1},{4,6},{5,7},{6,4},{7,5},{8,10},{9,11},{10,... | collective-permute-start | bytes 1548296 | tf_op jit(solution)/shard_map/ppermute | solution.py:379
  13.3 13.8 %collective-permute-start.4 = (bf16[336,768]{1,0:T(8,128)(2,1)S(1)}, bf16[336,768]{1,0:T(8,128)(2,1)S(1)}, u32[]{:S(2)}, u32[]{:S(2)}) collective-permute-start(bf16[336,768]{1,0:T(8,128)(2,1)S(1)} %get-tuple-element.192), channel_id=1, source_target_pairs={{0,4},{1,5},{2,6},{3,7},{4,0},{5,1},{6,2},{7,3},{8,12},{9,13},{10,... | collective-permute-start | bytes 1548296 | tf_op jit(solution)/shard_map/ppermute | solution.py:379
  14.9 15.4 %collective-permute-start.2 = (bf16[336,768]{1,0:T(8,128)(2,1)S(1)}, bf16[336,768]{1,0:T(8,128)(2,1)S(1)}, u32[]{:S(2)}, u32[]{:S(2)}) collective-permute-start(bf16[336,768]{1,0:T(8,128)(2,1)S(1)} %get-tuple-element.192), channel_id=1, source_target_pairs={{0,1},{1,0},{2,3},{3,2},{4,8},{5,9},{6,10},{7,11},{8,4},{9,5},{10,... | collective-permute-start | bytes 1548296 | tf_op jit(solution)/shard_map/ppermute | solution.py:379
  27.1 3.1 %collective-permute-start.7 = (bf16[336,768]{1,0:T(8,128)(2,1)S(1)}, bf16[336,768]{1,0:T(8,128)(2,1)S(1)}, u32[]{:S(2)}, u32[]{:S(2)}) collective-permute-start(bf16[336,768]{1,0:T(8,128)(2,1)S(1)} %collective-permute-done.4.refs_1_.refs_3_), channel_id=1, source_target_pairs={{0,1},{1,0},{2,3},{3,2},{4,5},{5,4},{6,7},{7,6},{8,9},{9,8},{10,11... | collective-permute-start | bytes 1548296 | tf_op jit(solution)/shard_map/ppermute | solution.py:379
  27.1 16.5 %collective-permute-start.3 = (bf16[336,768]{1,0:T(8,128)(2,1)S(1)}, bf16[336,768]{1,0:T(8,128)(2,1)S(1)}, u32[]{:S(2)}, u32[]{:S(2)}) collective-permute-start(bf16[336,768]{1,0:T(8,128)(2,1)S(1)} %get-tuple-element.190.refs_1_), channel_id=1, source_target_pairs={{0,8},{1,9},{2,10},{3,11},{4,0},{5,1},{6,2},{7,3},{8,12},{9,13},{1... | collective-permute-start | bytes 1548296 | tf_op jit(solution)/shard_map/ppermute | solution.py:379
  29.7 13.9 %collective-permute-start.5 = (bf16[336,768]{1,0:T(8,128)(2,1)S(1)}, bf16[336,768]{1,0:T(8,128)(2,1)S(1)}, u32[]{:S(2)}, u32[]{:S(2)}) collective-permute-start(bf16[336,768]{1,0:T(8,128)(2,1)S(1)} %collective-permute-done.4.refs_1_.refs_3_), channel_id=1, source_target_pairs={{0,2},{1,3},{2,0},{3,1},{4,6},{5,7},{6,4},{7,5},{8,10},{9,11},{10,... | collective-permute-start | bytes 1548296 | tf_op jit(solution)/shard_map/ppermute | solution.py:379
  30.2 1.9 %collective-permute-start.6 = (bf16[336,768]{1,0:T(8,128)(2,1)S(1)}, bf16[336,768]{1,0:T(8,128)(2,1)S(1)}, u32[]{:S(2)}, u32[]{:S(2)}) collective-permute-start(bf16[336,768]{1,0:T(8,128)(2,1)S(1)} %collective-permute-done.refs_1_), channel_id=1, source_target_pairs={{0,1},{1,0},{2,3},{3,2},{4,5},{5,4},{6,7},{7,6},{8,9},{9,8},{10,11... | collective-permute-start | bytes 1548296 | tf_op jit(solution)/shard_map/ppermute | solution.py:379
  43.6 1.9 %collective-permute-start.8 = (bf16[336,768]{1,0:T(8,128)(2,1)S(1)}, bf16[336,768]{1,0:T(8,128)(2,1)S(1)}, u32[]{:S(2)}, u32[]{:S(2)}) collective-permute-start(bf16[336,768]{1,0:T(8,128)(2,1)S(1)} %collective-permute-done.5.refs_3_), channel_id=1, source_target_pairs={{0,1},{1,0},{2,3},{3,2},{4,5},{5,4},{6,7},{7,6},{8,9},{9,8},{10,11... | collective-permute-start | bytes 1548296 | tf_op jit(solution)/shard_map/ppermute | solution.py:379
  45.5 12.6 %copy-start.2 = (bf16[512,1024]{1,0:T(8,128)(2,1)S(1)}, bf16[512,1024]{1,0:T(8,128)(2,1)}, u32[]{:S(2)}) copy-start(bf16[512,1024]{1,0:T(8,128)(2,1)} %refs_2_.1) | copy-start | bytes 3145732
  45.5 12.6 %copy-start.4 = (s32[512]{0:T(512)S(1)}, s32[512]{0:T(512)}, u32[]{:S(2)}) copy-start(s32[512]{0:T(512)} %param.9) | copy-start | bytes 6148
  46.7 1.2 %collective-permute-start.9 = (f32[4,1,640]{2,1,0:T(1,128)S(1)}, f32[4,1,640]{2,1,0:T(1,128)S(1)}, u32[]{:S(2)}, u32[]{:S(2)}) collective-permute-start(f32[4,1,640]{2,1,0:T(1,128)S(1)} %get-tuple-element.221), channel_id=1, source_target_pairs={{0,1},{1,0},{2,3},{3,2},{4,5},{5,4},{6,7},{7,6},{8,9},{9,8},{10,11... | collective-permute-start | bytes 30728 | tf_op jit(solution)/shard_map/ppermute | solution.py:379
  46.9 1.6 %collective-permute-start.10 = (f32[2,1,640]{2,1,0:T(1,128)S(1)}, f32[2,1,640]{2,1,0:T(1,128)S(1)}, u32[]{:S(2)}, u32[]{:S(2)}) collective-permute-start(f32[2,1,640]{2,1,0:T(1,128)S(1)} %get-tuple-element.222), channel_id=1, source_target_pairs={{0,1},{1,0},{2,3},{3,2},{4,8},{5,9},{6,10},{7,11},{8,4},{9,5},{10,... | collective-permute-start | bytes 15368 | tf_op jit(solution)/shard_map/ppermute | solution.py:379
  47.9 3.7 %collective-permute-start.11 = (f32[2,1,640]{2,1,0:T(1,128)S(1)}, f32[2,1,640]{2,1,0:T(1,128)S(1)}, u32[]{:S(2)}, u32[]{:S(2)}) collective-permute-start(f32[2,1,640]{2,1,0:T(1,128)S(1)} %slice_add_fusion), channel_id=1, source_target_pairs={{0,2},{1,3},{2,0},{3,1},{4,6},{5,7},{6,4},{7,5},{8,10},{9,11},{10,... | collective-permute-start | bytes 15368 | tf_op jit(solution)/shard_map/ppermute | solution.py:379
  51.6 4.1 %collective-permute-start.12 = (f32[1,1,640]{2,1,0:T(1,128)S(1)}, f32[1,1,640]{2,1,0:T(1,128)S(1)}, u32[]{:S(2)}, u32[]{:S(2)}) collective-permute-start(f32[1,1,640]{2,1,0:T(1,128)S(1)} %slice.32), channel_id=1, source_target_pairs={{0,4},{1,5},{2,6},{3,7},{4,0},{5,1},{6,2},{7,3},{8,12},{9,13},{10,... | collective-permute-start | bytes 7688 | tf_op jit(solution)/shard_map/ppermute | solution.py:379
  58.4 0.6 copy-start.5

commit v9 on v8

--- a/solution.py
+++ b/solution.py
@@ -122,10 +122,15 @@
     return rest, first, flag, up(flag + 1, 128)
 
 
-def prep_kernel(hot, place_ref, cl_ref, st_ref, w_ref, same_ref, other_ref, slot_ref, vectors):
+def prep_kernel(hot, place_ref, cl_ref, st_hbm, w_hbm, same_ref, other_ref, slot_ref, vectors, st_ref, w_ref, sems):
     docs = st_ref.shape[0]
     rest, first, flag, lanes = layout(docs, hot)
     tile = 128
+    copies = [
+        pltpu.make_async_copy(w_hbm, w_ref, sems.at[0]), pltpu.make_async_copy(st_hbm, st_ref, sems.at[1])
+    ]
+    for copy in copies:
+        copy.start()
 
     cluster = cl_ref[...]
     group = cluster // CLUS_OWN
@@ -136,12 +141,6 @@
     )
     doubt = jnp.where(jnp.sum(full.astype(F32), axis=0, keepdims=True) == 1.0, 0.0, 1.0)
     in_hot = group == chosen
-
-    for t in range(docs // tile):
-        rows = slice(t * tile, (t + 1) * tile)
-        projected = jnp.dot(st_ref[rows, :], w_ref[...], preferred_element_type=F32)
-        norm = lax.rsqrt(jnp.sum(projected * projected, axis=1, keepdims=True) + EPS)
-        vectors[rows, :] = (projected * (norm * math.sqrt(SCALE))).astype(BF16)
 
     ahead = (
         lax.broadcasted_iota(jnp.int32, (docs, docs), 0) < lax.broadcasted_iota(jnp.int32, (docs, docs), 1)
@@ -154,13 +153,22 @@
 
     sort = (lax.broadcasted_iota(jnp.int32, (lanes, docs), 0) == slot).astype(F32).astype(BF16)
     cluster_rows = jnp.broadcast_to(cluster.astype(F32), (META, docs)).astype(BF16)
+    ids = lax.dot_general(
+        cluster_rows, sort, (((1,), (1,)), ((), ())), preferred_element_type=F32
+    )
+    ids = ids.astype(BF16)
+
+
+    for copy in copies:
+        copy.wait()
+    for t in range(docs // tile):
+        rows = slice(t * tile, (t + 1) * tile)
+        projected = jnp.dot(st_ref[rows, :], w_ref[...], preferred_element_type=F32)
+        norm = lax.rsqrt(jnp.sum(projected * projected, axis=1, keepdims=True) + EPS)
+        vectors[rows, :] = (projected * (norm * math.sqrt(SCALE))).astype(BF16)
+
     sorted_n = jnp.dot(sort[:rest, :], vectors[...], preferred_element_type=F32).astype(BF16)
     sorted_h = jnp.dot(sort[first:flag, :], vectors[...], preferred_element_type=F32).astype(BF16)
-    ids = lax.dot_general(
-        cluster_rows, sort, (((1,), (1,)), ((), ())), preferred_element_type=F32
-    )
-    ids = ids.astype(BF16)
-
 
     def fill_n(ref):
         ref[:rest, :] = sorted_n
@@ -199,8 +207,11 @@
             shape((rest + META, width), BF16),
             shape((1, docs), jnp.int32),
         ),
-        in_specs=[pl.BlockSpec(memory_space=pltpu.SMEM), vmem, vmem, vmem],
-        scratch_shapes=[pltpu.VMEM((docs, width), BF16)],
+        in_specs=[pl.BlockSpec(memory_space=pltpu.SMEM), vmem] + [pl.BlockSpec(memory_space=pl.ANY)] * 2,
+        scratch_shapes=[
+            pltpu.VMEM((docs, width), BF16), pltpu.VMEM(states.shape, BF16), pltpu.VMEM(proj_weight.shape, BF16),
+            pltpu.SemaphoreType.DMA((2,)),
+        ],
         compiler_params=pltpu.CompilerParams(vmem_limit_bytes=24 * 2**20),
         name="prep",
     )(place, cluster_of.reshape(1, docs), states, proj_weight)
@@ -211,11 +222,12 @@
 ROW, PAIR_ROW = "row", "pair_row"
 DIAG, PAIR_DIAG = "diag", "pair_diag"
 NEXT, FAR = "next", "far"
-GROUPS = ((OWN, PAIR), (CORE, PAIR_CORE, DIAG, PAIR_DIAG), (ROW, PAIR_ROW), (NEXT, FAR))
+GROUPS = ((OWN, PAIR, ROW, PAIR_ROW), (CORE, PAIR_CORE, DIAG, PAIR_DIAG), (NEXT,), (FAR,))
+TILE = 256
 HERE, THERE, ACROSS = (OWN, CORE), (PAIR, PAIR_CORE), (ROW, DIAG)
 
 
-def score_kernel(docs, hot, names, given, made, tasks, flagged, carries, *refs):
+def score_kernel(docs, hot, names, given, made, tasks, doubted, carries, *refs):
     rest, first, flag, lanes = layout(docs, hot)
     place_ref, refs = refs[0], refs[1:]
     blocks, refs = dict(zip(names, refs[:len(names)])), refs[len(names):]
@@ -224,7 +236,7 @@
     outs, refs = refs[:len(GROUPS)], refs[len(GROUPS):]
     if made:
         pairs[made], refs = refs[:2], refs[2:]
-    parts = refs[0]
+    parts = refs[-1]
     for k, out in enumerate(outs):
         out[...] = before[k][...] if carries else jnp.zeros(out.shape, F32)
     spots = {name: (out, k) for out, group in zip(outs, GROUPS) for k, name in enumerate(group)}
@@ -239,60 +251,65 @@
         if made:
             turned, notes = pairs[made]
             turned[:, 0:two] = jnp.concatenate([blocks[name][:count, :] for name in made], axis=0).T
-            doubt = sum(blocks[name][rest:, first:first + 128].astype(F32)[0:1, 0:1] for name in made)
-            ids = jnp.concatenate([columns[name] for name in made], axis=0).T
-            notes[:, 0:two] = jnp.where(lax.broadcasted_iota(jnp.int32, ids.shape, 0) == 0, ids, doubt)
+            notes[:, 0:two] = jnp.concatenate([columns[name] for name in made], axis=0).T
 
         for left in dict.fromkeys(task[0] for task in tasks):
 
             def work(left=left):
                 own_tasks = [task for task in tasks if task[0] == left]
-                for number, (_, right, both, _) in enumerate(own_tasks):
+                block = blocks[left][:count, :]
+                fresh = True
+                for _, right, both, _ in own_tasks:
                     if right in blocks:
                         span, rights, diagonal = count, (right,), False
                         ids = blocks[right][rest:, 0:wide].astype(F32)[0:1, 0:count]
-                        inner = lax.dot_general(
-                            blocks[left][:count, :], blocks[right][:count, :], (((1,), (1,)), ((), ())),
-                            preferred_element_type=F32,
-                        )
                     else:
                         turned, notes = pairs[right]
                         span, rights, diagonal = two if both else wide, right[:1 + both], left == right[0]
                         ids = notes[0:1, 0:span]
                         if not both:
                             ids = jnp.where(lax.broadcasted_iota(jnp.int32, ids.shape, 1) < count, ids, -1.0)
-                        inner = jnp.dot(
-                            blocks[left][:count, :], turned[:, 0:span], preferred_element_type=F32
-                        )
-                    same = columns[left][:, 0:1] == ids
-                    if diagonal:
-                        same &= lax.broadcasted_iota(jnp.int32, inner.shape, 0) != lax.broadcasted_iota(
-                            jnp.int32, inner.shape, 1
-                        )
-                    weights = jnp.where(same, jnp.exp2(inner), 0.0)
-                    total = jnp.sum(weights, axis=0, keepdims=True)
+                    totals = []
+                    for low in range(0, span, TILE):
+                        high = min(low + TILE, span)
+                        if right in blocks:
+                            inner = lax.dot_general(
+                                block, blocks[right][low:high, :], (((1,), (1,)), ((), ())),
+                                preferred_element_type=F32,
+                            )
+                        else:
+                            inner = jnp.dot(block, turned[:, low:high], preferred_element_type=F32)
+                        same = columns[left][:, 0:1] == ids[:, low:high]
+                        if diagonal:
+                            same &= lax.broadcasted_iota(jnp.int32, inner.shape, 0) != (
+                                lax.broadcasted_iota(jnp.int32, inner.shape, 1) + low
+                            )
+                        weights = jnp.where(same, jnp.exp2(inner), 0.0)
+                        totals.append(jnp.sum(weights, axis=0, keepdims=True))
+                        if not diagonal:
+                            part = None
+                            for t in range(0, high - low, 128):
+                                piece = weights[:, t:t + 128]
+                                if piece.shape[1] < 128:
+                                    blank = jnp.zeros((count, 128 - piece.shape[1]), F32)
+                                    piece = jnp.concatenate([piece, blank], axis=1)
+                                part = piece if part is None else part + piece
+                            if fresh:
+                                parts[0:count, :] = part
+                            else:
+                                parts[0:count, :] += part
+                            fresh = False
+                    total = jnp.concatenate(totals, axis=1) if len(totals) > 1 else totals[0]
                     for k, name in enumerate(rights):
                         out, spot = spots[name]
                         out[spot, :, lane] += total[:, k * count:(k + 1) * count]
-                    if not diagonal:
-                        part = weights[:, 0:128]
-                        for t in range(128, span - span % 128, 128):
-                            part += weights[:, t:t + 128]
-                        if span % 128:
-                            rest_of = weights[:, span - span % 128:]
-                            part += jnp.concatenate([rest_of, jnp.zeros((count, 128 - span % 128), F32)], axis=1)
-                        if number:
-                            parts[0:count, :] += part
-                        else:
-                            parts[0:count, :] = part
-                if not diagonal:
+                if not fresh:
                     part = parts[0:count, :]
                     high = part.astype(BF16)
                     low = (part - high.astype(F32)).astype(BF16)
-                    ones = jnp.ones((16, 128), BF16)
-                    total = sum(
-                        lax.dot_general(ones, term, (((1,), (1,)), ((), ())), preferred_element_type=F32)
-                        for term in (high, low)
+                    total = lax.dot_general(
+                        jnp.ones((16, 256), BF16), jnp.concatenate([high, low], axis=1),
+                        (((1,), (1,)), ((), ())), preferred_element_type=F32,
                     )
                     out, spot = spots[left]
                     out[spot, :, lane] += total[0:1, :]
@@ -308,19 +325,16 @@
     pl.when(lax.rem(z, 2) == 0)(lambda: meet(hot, first))
     pl.when(lax.rem(z, 2) == 1)(lambda: meet(rest, 0))
 
-    if flagged:
-        doubt = sum(notes[1:2, 0:1] for _, notes in pairs.values())
-        doubt += sum(blocks[b][rest:, first:first + 128].astype(F32)[0:1, 0:1] for b in (PAIR_ROW, PAIR_DIAG))
-        spot = lax.broadcasted_iota(jnp.int32, (1, lanes), 1)
-        for name in flagged:
-            out, k = spots[name]
-            out[k] += jnp.where(spot == flag, doubt, 0.0)
-
-
-def score(name, docs, hot, place, blocks, pairs, made, tasks, sums, flagged=(), weight=1):
+    if doubted:
+        doubt = sum(blocks[name][rest:, first:first + 128].astype(F32)[0:1, 0:1] for name in doubted)
+        out, k = spots[FAR]
+        out[k] += jnp.where(lax.broadcasted_iota(jnp.int32, (1, lanes), 1) == flag, doubt, 0.0)
+
+
+def score(name, docs, hot, place, blocks, pairs, made, tasks, sums, doubted=(), weight=1):
     rest, _, _, lanes = layout(docs, hot)
     names = list(dict.fromkeys([*made, *(task[0] for task in tasks)]))
-    given = [p for p in pairs if flagged or any(p == task[1] for task in tasks)]
+    given = [p for p in pairs if any(p == task[1] for task in tasks)]
     width = blocks[OWN].shape[1]
     vmem = pl.BlockSpec(memory_space=pltpu.VMEM)
     arrays = [blocks[b] for b in names] + [a for p in given for a in pairs[p]] + list(sums)
@@ -328,7 +342,7 @@
     if made:
         shapes += [jax.ShapeDtypeStruct((width, 2 * rest), BF16), jax.ShapeDtypeStruct((8, 2 * rest), F32)]
     out = pl.pallas_call(
-        lambda *refs: score_kernel(docs, hot, names, given, made, tasks, flagged, bool(sums), *refs),
+        lambda *refs: score_kernel(docs, hot, names, given, made, tasks, doubted or made, bool(sums), *refs),
         out_shape=tuple(shapes),
         in_specs=[pl.BlockSpec(memory_space=pltpu.SMEM)] + [vmem] * len(arrays),
         out_specs=tuple(vmem for _ in shapes),
@@ -337,24 +351,28 @@
         cost_estimate=pl.CostEstimate(flops=weight, bytes_accessed=2**10, transcendentals=0),
         name=name,
     )(place, *arrays)
-    return out[:len(GROUPS)], {**pairs, made: out[len(GROUPS):]} if made else pairs
-
-
-def finish_kernel(slot_ref, home_ref, more_ref, out_ref):
-    total = home_ref[0] + more_ref[0]
+    count = len(GROUPS)
+    return out[:count], {**pairs, made: out[count:]} if made else pairs
+
+
+def finish_kernel(slot_ref, *refs):
+    sums, out_ref = refs[:-1], refs[-1]
+    total = sums[0][0]
+    for ref in sums[1:]:
+        total += ref[0]
     lanes, docs = total.shape[1], slot_ref.shape[1]
     values = jnp.broadcast_to(jnp.log(1.0 + total * 2.0**-SHIFT), (8, lanes)).T[:, 0:1]
     here = lax.broadcasted_iota(jnp.int32, (lanes, docs), 0) == slot_ref[...]
     out_ref[...] = jnp.sum(jnp.where(here, values, 0.0), axis=0, keepdims=True)
 
 
-def finish(slot, home, more):
+def finish(slot, sums):
     return pl.pallas_call(
         finish_kernel,
         out_shape=jax.ShapeDtypeStruct(slot.shape, F32),
         compiler_params=pltpu.CompilerParams(vmem_limit_bytes=6 * 2**20),
         name="finish",
-    )(slot, home, more)
+    )(slot, *sums)
 
 
 def meeting_plan(states, proj_weight, cluster_of):
@@ -378,7 +396,7 @@
         ]
         return lax.ppermute(a, ("owner", "split"), pairs)
 
-    STAY, OUTER, MIDDLE = (0, 1, 2, 3), (1, 0, 3, 2), (0, 2, 1, 3)
+    STAY, OUTER, MIDDLE, TWO = (0, 1, 2, 3), (1, 0, 3, 2), (0, 2, 1, 3), (2, 3, 0, 1)
     TO_MIDDLE = (2, 0, 3, 1)
 
     def meet(name, made, tasks, **options):
@@ -416,17 +434,22 @@
         "last", (),
         [(left, right, False, None) for left in (NEXT, FAR) for right in (PAIR_ROW, PAIR_DIAG)]
         + [(PAIR_ROW, THERE, False, "row1"), (PAIR_DIAG, THERE, False, "row0")],
-        flagged=(OWN, NEXT, FAR),
-    )
-    home, by_core, by_row, by_middle = sums
-    from_middle = move(by_middle, MIDDLE)
+        doubted=(PAIR_ROW, PAIR_DIAG),
+    )
+    kept, by_core, to_next, to_far = sums
     from_core = move(by_core, STAY, core=1)
-    from_row = move(by_row + from_core[2:4], STAY, row=1)
-    home = home + from_core[0:2] + from_middle + from_row
-    from_pair = move(home[1:2], OUTER)
-    fast = finish(slot, home, from_pair)
-    doubt = home[0, 0, flag] + from_pair[0, 0, flag] > 0.0
-    return lax.cond(doubt, owner_plan, lambda *_: fast.reshape(docs), states, proj_weight, cluster_of)
+    from_next, from_far = move(to_next, MIDDLE), move(to_far, TWO)
+    own, pair, row, pair_row = (kept[k:k + 1] + from_core[k:k + 1] for k in (0, 1, 2, 3))
+    home = [
+        own, from_next, from_far,
+        move(pair, OUTER), move(row, STAY, row=1), move(pair_row, OUTER, row=1),
+    ]
+    return lax.cond(
+        (to_far + from_far)[0, 0, flag] > 0.0,
+        lambda states, proj_weight, cluster_of, *_: owner_plan(states, proj_weight, cluster_of),
+        lambda states, proj_weight, cluster_of, slot, *home: finish(slot, home).reshape(docs),
+        states, proj_weight, cluster_of, slot, *home,
+    )
 
 
 def on_device(states, proj_weight, cluster_of):

time: 66 us -> 65.9 us (level)
  waiting for transfers between devices: 27.5 us -> 22.6 us
  starting transfers between devices: 11.4 us -> 15.2 us
  Pallas kernels: 10 us -> 10.9 us
    ppermute x13 -> x15, waiting for transfers between devices: 27.5 us -> 22.6 us  [move(): return lax.ppermute(a, ('owner', 'split'), pairs)]
    ppermute x13 -> x15, starting transfers between devices: 11.4 us -> 15.2 us  [move(): return lax.ppermute(a, ('owner', 'split'), pairs)]
    pallas_call x1, Pallas kernels: 3.56 us -> 4.33 us  [prep(): pl.pallas_call(lambda *refs: prep_kernel(hot, *refs), out_shape=(shape((r...]
  transfers between devices with their start and end apart: 13 -> 15, of which waited for: 7 -> 4; matrix products, arithmetic and copies ran while one was open for 1% -> 2% of each run, Pallas kernels for 7% -> 7%
where the time goes in v9:
time: 65.9 us; the launch traced here: 65.7 us
  waiting for transfers between devices  22.6 us (34%)
  starting transfers between devices  15.2 us (23%)
  between operations  14.9 us (23%)
  Pallas kernels  10.9 us (17%)
  local copies, waits for them, and re-layouts  1.83 us (3%)
    ppermute x15, waiting for transfers between devices, move(): return lax.ppermute(a, ('owner', 'split'), pairs)  22.6 us
    ppermute x15, starting transfers between devices, move(): return lax.ppermute(a, ('owner', 'split'), pairs)  15.2 us
    pallas_call x5, Pallas kernels, score(): pl.pallas_call(lambda *refs: score_kernel(docs, hot, names, given, made,...  6.08 us
    pallas_call x1, Pallas kernels, prep(): pl.pallas_call(lambda *refs: prep_kernel(hot, *refs), out_shape=(shape((r...  4.33 us
  transfers between devices with their start and end apart: 15, of which 4 were waited for; matrix products, arithmetic and copies ran while one was open for 2% of the time, Pallas kernels for 7%

profile of v9, /device:TPU:0, one launch (start us, length us, event | category | flops | bytes accessed | tf_op | source)
XLA Modules:
  0.0 65.7 jit_solution(15224579642826112067)
XLA Ops:
  6.5 0.1 pad_add_fusion.refs_0_
  6.6 4.3 %prep.1 = (bf16[336,768]{1,0:T(8,128)(2,1)S(1)}, bf16[336,768]{1,0:T(8,128)(2,1)S(1)}, s32[1,512]{1,0:T(1,128)S(1)}) custom-call(s32[3]{0:T(128)S(1)} %pad_add_fusion.refs_0_, s32[1,512]{1,0:T(1,128)} %bitcast.38, bf16[512,1024]{1,0:T(8,128)(2,1)} %refs_2_.1, bf16[1024,768]{1,0:T(8,128)(2,1)} %refs_3_.1), custom_call_target="tpu_custom_call" | custom-call | tf_op jit(solution)/shard_map/prep/pallas_call | solution.py:203
  11.0 0.5 collective-permute-start.1
  11.5 2.6 %collective-permute-start = (bf16[336,768]{1,0:T(8,128)(2,1)S(1)}, bf16[336,768]{1,0:T(8,128)(2,1)S(1)}, u32[]{:S(2)}, u32[]{:S(2)}) collective-permute-start(bf16[336,768]{1,0:T(8,128)(2,1)S(1)} %get-tuple-element.216.refs_1_), channel_id=1, source_target_pairs={{0,2},{1,3},{2,0},{3,1},{4,6},{5,7},{6,4},{7,5},{8,10},{9,11},{10,... | collective-permute-start | bytes 1548296 | tf_op jit(solution)/shard_map/ppermute | solution.py:397
  14.1 1.6 %collective-permute-start.4 = (bf16[336,768]{1,0:T(8,128)(2,1)S(1)}, bf16[336,768]{1,0:T(8,128)(2,1)S(1)}, u32[]{:S(2)}, u32[]{:S(2)}) collective-permute-start(bf16[336,768]{1,0:T(8,128)(2,1)S(1)} %get-tuple-element.218), channel_id=1, source_target_pairs={{0,4},{1,5},{2,6},{3,7},{4,0},{5,1},{6,2},{7,3},{8,12},{9,13},{10,... | collective-permute-start | bytes 1548296 | tf_op jit(solution)/shard_map/ppermute | solution.py:397
  15.6 1.4 %own.1 = (f32[4,1,640]{2,1,0:T(1,128)S(1)}, f32[4,1,640]{2,1,0:T(1,128)S(1)}, f32[1,1,640]{2,1,0:T(1,128)S(1)}, f32[1,1,640]{2,1,0:T(1,128)S(1)}, bf16[768,640]{1,0:T(8,128)(2,1)S(1)}, /*index=5*/f32[8,640]{1,0:T(8,128)S(1)}) custom-call(s32[3]{0:T(128)S(1)} %pad_add_fusion.refs_0_, bf16[336,768]{1,0:T(8,128)(2,1)S(1)} %get-tuple-element.216.refs_1_, ...), custom_call_target="tpu_custom_call" | custom-call | flops 8589934592 | bytes 1024 | tf_op jit(solution)/shard_map/own/pallas_call | solution.py:344
  17.0 10.8 %collective-permute-done.4.refs_1_.refs_3_ = bf16[336,768]{1,0:T(8,128)(2,1)S(1)} collective-permute-done((bf16[336,768]{1,0:T(8,128)(2,1)S(1)}, bf16[336,768]{1,0:T(8,128)(2,1)S(1)}, u32[]{:S(2)}, u32[]{:S(2)}) %collective-permute-start.4) | collective-permute-done | bytes 516128 | tf_op jit(solution)/shard_map/ppermute | solution.py:397
  27.9 0.0 collective-permute-start.7
  27.9 2.6 %collective-permute-start.3 = (bf16[336,768]{1,0:T(8,128)(2,1)S(1)}, bf16[336,768]{1,0:T(8,128)(2,1)S(1)}, u32[]{:S(2)}, u32[]{:S(2)}) collective-permute-start(bf16[336,768]{1,0:T(8,128)(2,1)S(1)} %get-tuple-element.216.refs_1_), channel_id=1, source_target_pairs={{0,8},{1,9},{2,10},{3,11},{4,0},{5,1},{6,2},{7,3},{8,12},{9,13},{1... | collective-permute-start | bytes 1548296 | tf_op jit(solution)/shard_map/ppermute | solution.py:397
  30.5 0.5 collective-permute-start.5
  31.0 0.0 collective-permute-done.refs_1_
  31.0 1.1 %pair.1 = (f32[4,1,640]{2,1,0:T(1,128)S(1)}, f32[4,1,640]{2,1,0:T(1,128)S(1)}, f32[1,1,640]{2,1,0:T(1,128)S(1)}, f32[1,1,640]{2,1,0:T(1,128)S(1)}, bf16[768,640]{1,0:T(8,128)(2,1)S(1)}, /*index=5*/f32[8,640]{1,0:T(8,128)S(1)}) custom-call(s32[3]{0:T(128)S(1)} %pad_add_fusion.refs_0_, bf16[336,768]{1,0:T(8,128)(2,1)S(1)} %collective-permute-done.4.refs_1_.refs_3_, ...), custom_call_target="tpu_custom_call" | custom-call | flops 8589934592 | bytes 1024 | tf_op jit(solution)/shard_map/pair/pallas_call | solution.py:344
  32.1 0.8 %collective-permute-done.6.refs_2_ = bf16[336,768]{1,0:T(8,128)(2,1)S(1)} collective-permute-done((bf16[336,768]{1,0:T(8,128)(2,1)S(1)}, bf16[336,768]{1,0:T(8,128)(2,1)S(1)}, u32[]{:S(2)}, u32[]{:S(2)}) %collective-permute-start.6) | collective-permute-done | bytes 516128 | tf_op jit(solution)/shard_map/ppermute | solution.py:397
  32.9 1.8 %row.1 = (f32[4,1,640]{2,1,0:T(1,128)S(1)}, f32[4,1,640]{2,1,0:T(1,128)S(1)}, f32[1,1,640]{2,1,0:T(1,128)S(1)}, f32[1,1,640]{2,1,0:T(1,128)S(1)}, bf16[768,640]{1,0:T(8,128)(2,1)S(1)}, /*index=5*/f32[8,640]{1,0:T(8,128)S(1)}) custom-call(s32[3]{0:T(128)S(1)} %pad_add_fusion.refs_0_, bf16[336,768]{1,0:T(8,128)(2,1)S(1)} %collective-permute-done.refs_1_, ...), custom_call_target="tpu_custom_call" | custom-call | flops 1 | bytes 1024 | tf_op jit(solution)/shard_map/row/pallas_call | solution.py:344
  34.7 9.7 %collective-permute-done.5.refs_3_ = bf16[336,768]{1,0:T(8,128)(2,1)S(1)} collective-permute-done((bf16[336,768]{1,0:T(8,128)(2,1)S(1)}, bf16[336,768]{1,0:T(8,128)(2,1)S(1)}, u32[]{:S(2)}, u32[]{:S(2)}) %collective-permute-start.5) | collective-permute-done | bytes 516128 | tf_op jit(solution)/shard_map/ppermute | solution.py:397
  44.4 0.6 far.1
  45.0 0.0 copy-start.2
  45.0 0.0 copy-start.4
  45.0 1.2 %collective-permute-done.8.refs_4_ = bf16[336,768]{1,0:T(8,128)(2,1)S(1)} collective-permute-done((bf16[336,768]{1,0:T(8,128)(2,1)S(1)}, bf16[336,768]{1,0:T(8,128)(2,1)S(1)}, u32[]{:S(2)}, u32[]{:S(2)}) %collective-permute-start.8) | collective-permute-done | bytes 516128 | tf_op jit(solution)/shard_map/ppermute | solution.py:397
  46.3 1.2 %last.1 = (f32[4,1,640]{2,1,0:T(1,128)S(1)}, f32[4,1,640]{2,1,0:T(1,128)S(1)}, f32[1,1,640]{2,1,0:T(1,128)S(1)}, f32[1,1,640]{2,1,0:T(1,128)S(1)}) custom-call(s32[3]{0:T(128)S(1)} %pad_add_fusion.refs_0_, bf16[336,768]{1,0:T(8,128)(2,1)S(1)} %collective-permute-done.2.refs_3_.refs_4_.refs_1_, bf16[336,768]{1,0:T(8,128)(2,1)S(1)} %collective-permute-done.3.refs_1_.refs_2_, ...), custom_call_target="tpu_custom_call" | custom-call | flops 1 | bytes 1024 | tf_op jit(solution)/shard_map/last/pallas_call | solution.py:344
  47.5 0.1 collective-permute-start.10
  47.6 0.4 collective-permute-start.11
  48.0 3.3 %collective-permute-start.9 = (f32[1,1,640]{2,1,0:T(1,128)S(1)}, f32[1,1,640]{2,1,0:T(1,128)S(1)}, u32[]{:S(2)}, u32[]{:S(2)}) collective-permute-start(f32[1,1,640]{2,1,0:T(1,128)S(1)} %get-tuple-element.246), channel_id=1, source_target_pairs={{0,8},{1,9},{2,10},{3,11},{4,12},{5,13},{6,14},{7,15},{8,0},{9,1},... | collective-permute-start | bytes 7688 | tf_op jit(solution)/shard_map/ppermute | solution.py:397
  51.3 0.1 collective-permute-start.14
  51.4 1.1 %collective-permute-start.13 = (f32[1,1,640]{2,1,0:T(1,128)S(1)}, f32[1,1,640]{2,1,0:T(1,128)S(1)}, u32[]{:S(2)}, u32[]{:S(2)}) collective-permute-start(f32[1,1,640]{2,1,0:T(1,128)S(1)} %get-tuple-element.327), channel_id=1, source_target_pairs={{0,2},{1,3},{2,0},{3,1},{4,6},{5,7},{6,4},{7,5},{8,10},{9,11},{10,... | collective-permute-start | bytes 7688 | tf_op jit(solution)/shard_map/ppermute | solution.py:397
  52.5 2.4 %collective-permute-start.12 = (f32[1,1,640]{2,1,0:T(1,128)S(1)}, f32[1,1,640]{2,1,0:T(1,128)S(1)}, u32[]{:S(2)}, u32[]{:S(2)}) collective-permute-start(f32[1,1,640]{2,1,0:T(1,128)S(1)} %get-tuple-element.328), channel_id=1, source_target_pairs={{0,4},{1,5},{2,6},{3,7},{4,0},{5,1},{6,2},{7,3},{8,12},{9,13},{10,... | collective-permute-start | bytes 7688 | tf_op jit(solution)/shard_map/ppermute | solution.py:397
  54.9 0.6 slice.45
  55.5 0.7 %slice.46 = f32[1,1,1]{2,1,0:T(1,128)} slice(f32[1,1,640]{2,1,0:T(1,128)S(1)} %collective-permute-done.9), slice={[0:1], [0:1], [576:577]} | slice | bytes 8 | tf_op jit(solution)/shard_map/slice | solution.py:448
  57.5 0.8 %conditional.1 = (f32[512]{0:T(512)S(1)}) conditional(s32[]{:T(128)} %bitcast.12, (f32[4,1,640]{2,1,0:T(1,128)S(1)}, f32[4,1,640]{2,1,0:T(1,128)S(1)}, s32[1,512]{1,0:T(1,128)S(1)}, f32[1,1,640]{2,1,0:T(1,128)S(1)}, f32[1,1,640]{2,1,0:T(1,128)S(1)}, /*index=5*/f32[1,1,640]{2,1,0:T(1,128)S(1)}, f32[1,1,640]{2,1,0:T(1,128)S(1)}, ...), branch_computations={%region_0.1_spmd, %region_1.13_spmd} | conditional | flops 4454147584 | bytes 57829452 | solution.py:447
  57.6 0.5 finish.1
  58.3 0.0 copy-start.5
  58.3 0.6 copy-done.5
  (17 shorter events, 0.1 us)
Async XLA Ops:
  11.0 4.7 %collective-permute-start.1 = (bf16[336,768]{1,0:T(8,128)(2,1)S(1)}, bf16[336,768]{1,0:T(8,128)(2,1)S(1)}, u32[]{:S(2)}, u32[]{:S(2)}) collective-permute-start(bf16[336,768]{1,0:T(8,128)(2,1)S(1)} %get-tuple-element.216.refs_1_), channel_id=1, source_target_pairs={{0,1},{1,0},{2,3},{3,2},{4,5},{5,4},{6,7},{7,6},{8,9},{9,8},{10,11... | collective-permute-start | bytes 1548296 | tf_op jit(solution)/shard_map/ppermute | solution.py:397
  11.5 19.5 %collective-permute-start = (bf16[336,768]{1,0:T(8,128)(2,1)S(1)}, bf16[336,768]{1,0:T(8,128)(2,1)S(1)}, u32[]{:S(2)}, u32[]{:S(2)}) collective-permute-start(bf16[336,768]{1,0:T(8,128)(2,1)S(1)} %get-tuple-element.216.refs_1_), channel_id=1, source_target_pairs={{0,2},{1,3},{2,0},{3,1},{4,6},{5,7},{6,4},{7,5},{8,10},{9,11},{10,... | collective-permute-start | bytes 1548296 | tf_op jit(solution)/shard_map/ppermute | solution.py:397
  14.1 13.8 %collective-permute-start.4 = (bf16[336,768]{1,0:T(8,128)(2,1)S(1)}, bf16[336,768]{1,0:T(8,128)(2,1)S(1)}, u32[]{:S(2)}, u32[]{:S(2)}) collective-permute-start(bf16[336,768]{1,0:T(8,128)(2,1)S(1)} %get-tuple-element.218), channel_id=1, source_target_pairs={{0,4},{1,5},{2,6},{3,7},{4,0},{5,1},{6,2},{7,3},{8,12},{9,13},{10,... | collective-permute-start | bytes 1548296 | tf_op jit(solution)/shard_map/ppermute | solution.py:397
  15.6 15.3 %collective-permute-start.2 = (bf16[336,768]{1,0:T(8,128)(2,1)S(1)}, bf16[336,768]{1,0:T(8,128)(2,1)S(1)}, u32[]{:S(2)}, u32[]{:S(2)}) collective-permute-start(bf16[336,768]{1,0:T(8,128)(2,1)S(1)} %get-tuple-element.218), channel_id=1, source_target_pairs={{0,1},{1,0},{2,3},{3,2},{4,8},{5,9},{6,10},{7,11},{8,4},{9,5},{10,... | collective-permute-start | bytes 1548296 | tf_op jit(solution)/shard_map/ppermute | solution.py:397
  27.9 3.1 %collective-permute-start.7 = (bf16[336,768]{1,0:T(8,128)(2,1)S(1)}, bf16[336,768]{1,0:T(8,128)(2,1)S(1)}, u32[]{:S(2)}, u32[]{:S(2)}) collective-permute-start(bf16[336,768]{1,0:T(8,128)(2,1)S(1)} %collective-permute-done.4.refs_1_.refs_3_), channel_id=1, source_target_pairs={{0,1},{1,0},{2,3},{3,2},{4,5},{5,4},{6,7},{7,6},{8,9},{9,8},{10,11... | collective-permute-start | bytes 1548296 | tf_op jit(solution)/shard_map/ppermute | solution.py:397
  27.9 16.5 %collective-permute-start.3 = (bf16[336,768]{1,0:T(8,128)(2,1)S(1)}, bf16[336,768]{1,0:T(8,128)(2,1)S(1)}, u32[]{:S(2)}, u32[]{:S(2)}) collective-permute-start(bf16[336,768]{1,0:T(8,128)(2,1)S(1)} %get-tuple-element.216.refs_1_), channel_id=1, source_target_pairs={{0,8},{1,9},{2,10},{3,11},{4,0},{5,1},{6,2},{7,3},{8,12},{9,13},{1... | collective-permute-start | bytes 1548296 | tf_op jit(solution)/shard_map/ppermute | solution.py:397
  30.5 13.9 %collective-permute-start.5 = (bf16[336,768]{1,0:T(8,128)(2,1)S(1)}, bf16[336,768]{1,0:T(8,128)(2,1)S(1)}, u32[]{:S(2)}, u32[]{:S(2)}) collective-permute-start(bf16[336,768]{1,0:T(8,128)(2,1)S(1)} %collective-permute-done.4.refs_1_.refs_3_), channel_id=1, source_target_pairs={{0,2},{1,3},{2,0},{3,1},{4,6},{5,7},{6,4},{7,5},{8,10},{9,11},{10,... | collective-permute-start | bytes 1548296 | tf_op jit(solution)/shard_map/ppermute | solution.py:397
  31.0 1.9 %collective-permute-start.6 = (bf16[336,768]{1,0:T(8,128)(2,1)S(1)}, bf16[336,768]{1,0:T(8,128)(2,1)S(1)}, u32[]{:S(2)}, u32[]{:S(2)}) collective-permute-start(bf16[336,768]{1,0:T(8,128)(2,1)S(1)} %collective-permute-done.refs_1_), channel_id=1, source_target_pairs={{0,1},{1,0},{2,3},{3,2},{4,5},{5,4},{6,7},{7,6},{8,9},{9,8},{10,11... | collective-permute-start | bytes 1548296 | tf_op jit(solution)/shard_map/ppermute | solution.py:397
  44.4 1.9 %collective-permute-start.8 = (bf16[336,768]{1,0:T(8,128)(2,1)S(1)}, bf16[336,768]{1,0:T(8,128)(2,1)S(1)}, u32[]{:S(2)}, u32[]{:S(2)}) collective-permute-start(bf16[336,768]{1,0:T(8,128)(2,1)S(1)} %collective-permute-done.5.refs_3_), channel_id=1, source_target_pairs={{0,1},{1,0},{2,3},{3,2},{4,5},{5,4},{6,7},{7,6},{8,9},{9,8},{10,11... | collective-permute-start | bytes 1548296 | tf_op jit(solution)/shard_map/ppermute | solution.py:397
  45.0 12.5 %copy-start.2 = (bf16[512,1024]{1,0:T(8,128)(2,1)S(1)}, bf16[512,1024]{1,0:T(8,128)(2,1)}, u32[]{:S(2)}) copy-start(bf16[512,1024]{1,0:T(8,128)(2,1)} %refs_2_.1) | copy-start | bytes 3145732
  45.0 12.5 %copy-start.4 = (s32[512]{0:T(512)S(1)}, s32[512]{0:T(512)}, u32[]{:S(2)}) copy-start(s32[512]{0:T(512)} %param.9) | copy-start | bytes 6148
  47.5 3.8 %collective-permute-start.10 = (f32[4,1,640]{2,1,0:T(1,128)S(1)}, f32[4,1,640]{2,1,0:T(1,128)S(1)}, u32[]{:S(2)}, u32[]{:S(2)}) collective-permute-start(f32[4,1,640]{2,1,0:T(1,128)S(1)} %get-tuple-element.248), channel_id=1, source_target_pairs={{0,1},{1,0},{2,3},{3,2},{4,5},{5,4},{6,7},{7,6},{8,9},{9,8},{10,11... | collective-permute-start | bytes 30728 | tf_op jit(solution)/shard_map/ppermute | solution.py:397
  47.6 9.9 %collective-permute-start.11 = (f32[1,1,640]{2,1,0:T(1,128)S(1)}, f32[1,1,640]{2,1,0:T(1,128)S(1)}, u32[]{:S(2)}, u32[]{:S(2)}) collective-permute-start(f32[1,1,640]{2,1,0:T(1,128)S(1)} %get-tuple-element.250), channel_id=1, source_target_pairs={{0,1},{1,0},{2,3},{3,2},{4,8},{5,9},{6,10},{7,11},{8,4},{9,5},{10,... | collective-permute-start | bytes 7688 | tf_op jit(solution)/shard_map/ppermute | solution.py:397
  48.0 7.5 %collective-permute-start.9 = (f32[1,1,640]{2,1,0:T(1,128)S(1)}, f32[1,1,640]{2,1,0:T(1,128)S(1)}, u32[]{:S(2)}, u32[]{:S(2)}) collective-permute-start(f32[1,1,640]{2,1,0:T(1,128)S(1)} %get-tuple-element.246), channel_id=1, source_target_pairs={{0,8},{1,9},{2,10},{3,11},{4,12},{5,13},{6,14},{7,15},{8,0},{9,1},... | collective-permute-start | bytes 7688 | tf_op jit(solution)/shard_map/ppermute | solution.py:397
  51.3 6.2 %collective-permute-start.14 = (f32[1,1,640]{2,1,0:T(1,128)S(1)}, f32[1,1,640]{2,1,0:T(1,128)S(1)}, u32[]{:S(2)}, u32[]{:S(2)}) collective-permute-start(f32[1,1,640]{2,1,0:T(1,128)S(1)} %get-tuple-element.326), channel_id=1, source_target_pairs={{0,6},{1,7},{2,4},{3,5},{4,2},{5,3},{6,0},{7,1},{8,14},{9,15},{10,... | collective-permute-start | bytes 7688 | tf_op jit(solution)/shard_map/ppermute | solution.py:397
  51.4 6.1 %collective-permute-start.13 = (f32[1,1,640]{2,1,0:T(1,128)S(1)}, f32[1,1,640]{2,1,0:T(1,128)S(1)}, u32[]{:S(2)}, u32[]{:S(2)}) collective-permute-start(f32[1,1,640]{2,1,0:T(1,128)S(1)} %get-tuple-element.327), channel_id=1, source_target_pairs={{0,2},{1,3},{2,0},{3,1},{4,6},{5,7},{6,4},{7,5},{8,10},{9,11},{10,... | collective-permute-start | bytes 7688 | tf_op jit(solution)/shard_map/ppermute | solution.py:397
  52.5 5.0 %collective-permute-start.12 = (f32[1,1,640]{2,1,0:T(1,128)S(1)}, f32[1,1,640]{2,1,0:T(1,128)S(1)}, u32[]{:S(2)}, u32[]{:S(2)}) collective-permute-start(f32[1,1,640]{2,1,0:T(1,128)S(1)} %get-tuple-element.328), channel_id=1, source_target_pairs={{0,4},{1,5},{2,6},{3,7},{4,0},{5,1},{6,2},{7,3},{8,12},{9,13},{10,... | collective-permute-start | bytes 7688 | tf_op jit(solution)/shard_map/ppermute | solution.py:397
  58.3 0.6 copy-start.5

commit v10 on v9

--- a/solution.py
+++ b/solution.py
@@ -122,15 +122,10 @@
     return rest, first, flag, up(flag + 1, 128)
 
 
-def prep_kernel(hot, place_ref, cl_ref, st_hbm, w_hbm, same_ref, other_ref, slot_ref, vectors, st_ref, w_ref, sems):
+def prep_kernel(hot, place_ref, cl_ref, st_ref, w_ref, same_ref, other_ref, sa_ref, sb_ref, oa_ref, ob_ref, slot_ref, vectors):
     docs = st_ref.shape[0]
     rest, first, flag, lanes = layout(docs, hot)
     tile = 128
-    copies = [
-        pltpu.make_async_copy(w_hbm, w_ref, sems.at[0]), pltpu.make_async_copy(st_hbm, st_ref, sems.at[1])
-    ]
-    for copy in copies:
-        copy.start()
 
     cluster = cl_ref[...]
     group = cluster // CLUS_OWN
@@ -141,6 +136,12 @@
     )
     doubt = jnp.where(jnp.sum(full.astype(F32), axis=0, keepdims=True) == 1.0, 0.0, 1.0)
     in_hot = group == chosen
+
+    for t in range(docs // tile):
+        rows = slice(t * tile, (t + 1) * tile)
+        projected = jnp.dot(st_ref[rows, :], w_ref[...], preferred_element_type=F32)
+        norm = lax.rsqrt(jnp.sum(projected * projected, axis=1, keepdims=True) + EPS)
+        vectors[rows, :] = (projected * (norm * math.sqrt(SCALE))).astype(BF16)
 
     ahead = (
         lax.broadcasted_iota(jnp.int32, (docs, docs), 0) < lax.broadcasted_iota(jnp.int32, (docs, docs), 1)
@@ -159,40 +160,41 @@
     ids = ids.astype(BF16)
 
 
-    for copy in copies:
-        copy.wait()
-    for t in range(docs // tile):
-        rows = slice(t * tile, (t + 1) * tile)
-        projected = jnp.dot(st_ref[rows, :], w_ref[...], preferred_element_type=F32)
-        norm = lax.rsqrt(jnp.sum(projected * projected, axis=1, keepdims=True) + EPS)
-        vectors[rows, :] = (projected * (norm * math.sqrt(SCALE))).astype(BF16)
-
     sorted_n = jnp.dot(sort[:rest, :], vectors[...], preferred_element_type=F32).astype(BF16)
     sorted_h = jnp.dot(sort[first:flag, :], vectors[...], preferred_element_type=F32).astype(BF16)
 
-    def fill_n(ref):
-        ref[:rest, :] = sorted_n
-        ref[rest:, :] = jnp.zeros((META, ref.shape[1]), BF16)
-        ref[rest:, :first] = ids[:, :first]
-        ref[rest:, first:first + 128] = jnp.broadcast_to(doubt.astype(BF16), (META, 128))
-
-    def fill_h(ref):
-        ref[:hot, :] = sorted_h
-        ref[hot:, :] = jnp.zeros((rest + META - hot, ref.shape[1]), BF16)
-        ref[rest:, :lanes - first] = ids[:, first:]
-        ref[rest:, first:first + 128] = jnp.broadcast_to(doubt.astype(BF16), (META, 128))
+    def fill(ref, vectors, room, start, first_doc):
+        count = vectors.shape[0]
+        ref[:count, :] = vectors
+        ref[count:, :] = jnp.zeros((ref.shape[0] - count, ref.shape[1]), BF16)
+        wide = up(count, 128)
+        if first_doc:
+            spots = lax.broadcasted_iota(jnp.int32, (wide, lanes), 0) + (start + first_doc)
+            pick = (lax.broadcasted_iota(jnp.int32, (wide, lanes), 1) == spots).astype(F32).astype(BF16)
+            row = lax.dot_general(ids, pick, (((1,), (1,)), ((), ())), preferred_element_type=F32).astype(BF16)
+        else:
+            row = ids[:, start:start + wide]
+        ref[room:, :wide] = row
+        ref[room:, first:first + 128] = jnp.broadcast_to(doubt.astype(BF16), (META, 128))
+
+    def fill_all(whole, half_a, half_b, vectors, start):
+        half = vectors.shape[0] // 2
+        fill(whole, vectors, rest, start, 0)
+        fill(half_a, vectors[:half], rest // 2, start, 0)
+        fill(half_b, vectors[half:], rest // 2, start, half)
 
     even = lax.rem(place_ref[0], 2) == 0
+    sames, others = (same_ref, sa_ref, sb_ref), (other_ref, oa_ref, ob_ref)
 
     @pl.when(even)
     def _():
-        fill_h(same_ref)
-        fill_n(other_ref)
+        fill_all(*sames, sorted_h, first)
+        fill_all(*others, sorted_n, 0)
 
     @pl.when(jnp.logical_not(even))
     def _():
-        fill_n(same_ref)
-        fill_h(other_ref)
+        fill_all(*sames, sorted_n, 0)
+        fill_all(*others, sorted_h, first)
 
 
 def prep(hot, place, cluster_of, states, proj_weight):
@@ -203,15 +205,12 @@
     return pl.pallas_call(
         lambda *refs: prep_kernel(hot, *refs),
         out_shape=(
-            shape((rest + META, width), BF16),
-            shape((rest + META, width), BF16),
+            *(shape((rest + META, width), BF16) for _ in range(2)),
+            *(shape((rest // 2 + META, width), BF16) for _ in range(4)),
             shape((1, docs), jnp.int32),
         ),
-        in_specs=[pl.BlockSpec(memory_space=pltpu.SMEM), vmem] + [pl.BlockSpec(memory_space=pl.ANY)] * 2,
-        scratch_shapes=[
-            pltpu.VMEM((docs, width), BF16), pltpu.VMEM(states.shape, BF16), pltpu.VMEM(proj_weight.shape, BF16),
-            pltpu.SemaphoreType.DMA((2,)),
-        ],
+        in_specs=[pl.BlockSpec(memory_space=pltpu.SMEM), vmem, vmem, vmem],
+        scratch_shapes=[pltpu.VMEM((docs, width), BF16)],
         compiler_params=pltpu.CompilerParams(vmem_limit_bytes=24 * 2**20),
         name="prep",
     )(place, cluster_of.reshape(1, docs), states, proj_weight)
@@ -224,7 +223,17 @@
 NEXT, FAR = "next", "far"
 GROUPS = ((OWN, PAIR, ROW, PAIR_ROW), (CORE, PAIR_CORE, DIAG, PAIR_DIAG), (NEXT,), (FAR,))
 TILE = 256
-HERE, THERE, ACROSS = (OWN, CORE), (PAIR, PAIR_CORE), (ROW, DIAG)
+
+
+def halves(name):
+    return (name + ".a", name + ".b")
+
+
+def whole(name):
+    return (name[:-2], "ab".index(name[-1])) if name[-2] == "." else (name, None)
+
+
+HERE, THERE, ACROSS = (OWN, CORE), halves(PAIR) + halves(PAIR_CORE), (ROW, DIAG)
 
 
 def score_kernel(docs, hot, names, given, made, tasks, doubted, carries, *refs):
@@ -244,31 +253,47 @@
     when = {"core0": c == 0, "core1": c == 1, "row0": y == 0, "row1": y == 1}
     middle = (z == 1) | (z == 2)
 
-    def meet(count, start):
-        lane = slice(start, start + count)
-        wide, two = up(count, 128), 2 * count
-        columns = {name: ref[rest:, 0:wide].astype(F32)[0:8, :].T[0:count, :] for name, ref in blocks.items()}
+    def meet(full, start):
+        two = 2 * full
+        count, base, room = {}, {}, {}
+        for name in blocks:
+            half = whole(name)[1]
+            count[name] = full if half is None else full // 2
+            base[name] = 0 if half is None else half * full // 2
+            room[name] = rest if half is None else rest // 2
+
+        def ids_of(name):
+            return blocks[name][room[name]:, 0:up(count[name], 128)].astype(F32)[0:8, :]
+
+        def lanes_of(name):
+            return slice(start + base[name], start + base[name] + count[name])
+
+        columns = {name: ids_of(name).T[0:count[name], :] for name in blocks}
         if made:
             turned, notes = pairs[made]
-            turned[:, 0:two] = jnp.concatenate([blocks[name][:count, :] for name in made], axis=0).T
+            turned[:, 0:two] = jnp.concatenate([blocks[name][:count[name], :] for name in made], axis=0).T
             notes[:, 0:two] = jnp.concatenate([columns[name] for name in made], axis=0).T
 
         for left in dict.fromkeys(task[0] for task in tasks):
 
             def work(left=left):
-                own_tasks = [task for task in tasks if task[0] == left]
-                block = blocks[left][:count, :]
+                rows = count[left]
+                block = blocks[left][:rows, :]
                 fresh = True
-                for _, right, both, _ in own_tasks:
+                for _, right, both, _ in [task for task in tasks if task[0] == left]:
                     if right in blocks:
-                        span, rights, diagonal = count, (right,), False
-                        ids = blocks[right][rest:, 0:wide].astype(F32)[0:1, 0:count]
+                        span, diagonal = count[right], False
+                        ids = ids_of(right)[0:1, 0:span]
+                        rights = [(whole(right)[0], lanes_of(right))]
                     else:
                         turned, notes = pairs[right]
-                        span, rights, diagonal = two if both else wide, right[:1 + both], left == right[0]
+                        span, diagonal = two if both else up(full, 128), left in right[:len(right) // 2]
                         ids = notes[0:1, 0:span]
+                        rights = [
+                            (whole(right[k * len(right) // 2])[0], slice(start, start + full)) for k in range(1 + both)
+                        ]
                         if not both:
-                            ids = jnp.where(lax.broadcasted_iota(jnp.int32, ids.shape, 1) < count, ids, -1.0)
+                            ids = jnp.where(lax.broadcasted_iota(jnp.int32, ids.shape, 1) < full, ids, -1.0)
                     totals = []
                     for low in range(0, span, TILE):
                         high = min(low + TILE, span)
@@ -281,7 +306,7 @@
                             inner = jnp.dot(block, turned[:, low:high], preferred_element_type=F32)
                         same = columns[left][:, 0:1] == ids[:, low:high]
                         if diagonal:
-                            same &= lax.broadcasted_iota(jnp.int32, inner.shape, 0) != (
+                            same &= lax.broadcasted_iota(jnp.int32, inner.shape, 0) + base[left] != (
                                 lax.broadcasted_iota(jnp.int32, inner.shape, 1) + low
                             )
                         weights = jnp.where(same, jnp.exp2(inner), 0.0)
@@ -291,31 +316,32 @@
                             for t in range(0, high - low, 128):
                                 piece = weights[:, t:t + 128]
                                 if piece.shape[1] < 128:
-                                    blank = jnp.zeros((count, 128 - piece.shape[1]), F32)
+                                    blank = jnp.zeros((rows, 128 - piece.shape[1]), F32)
                                     piece = jnp.concatenate([piece, blank], axis=1)
                                 part = piece if part is None else part + piece
                             if fresh:
-                                parts[0:count, :] = part
+                                parts[0:rows, :] = part
                             else:
-                                parts[0:count, :] += part
+                                parts[0:rows, :] += part
                             fresh = False
                     total = jnp.concatenate(totals, axis=1) if len(totals) > 1 else totals[0]
-                    for k, name in enumerate(rights):
+                    for k, (name, lane) in enumerate(rights):
                         out, spot = spots[name]
-                        out[spot, :, lane] += total[:, k * count:(k + 1) * count]
+                        width = lane.stop - lane.start
+                        out[spot, :, lane] += total[:, k * width:(k + 1) * width]
                 if not fresh:
-                    part = parts[0:count, :]
+                    part = parts[0:rows, :]
                     high = part.astype(BF16)
                     low = (part - high.astype(F32)).astype(BF16)
                     total = lax.dot_general(
                         jnp.ones((16, 256), BF16), jnp.concatenate([high, low], axis=1),
                         (((1,), (1,)), ((), ())), preferred_element_type=F32,
                     )
-                    out, spot = spots[left]
-                    out[spot, :, lane] += total[0:1, :]
+                    out, spot = spots[whole(left)[0]]
+                    out[spot, :, lanes_of(left)] += total[0:1, :]
 
             condition = [task[3] for task in tasks if task[0] == left][0]
-            if left in (NEXT, FAR):
+            if whole(left)[0] in (NEXT, FAR):
                 pl.when(middle)(work)
             elif condition:
                 pl.when(when[condition])(work)
@@ -326,14 +352,16 @@
     pl.when(lax.rem(z, 2) == 1)(lambda: meet(rest, 0))
 
     if doubted:
-        doubt = sum(blocks[name][rest:, first:first + 128].astype(F32)[0:1, 0:1] for name in doubted)
+        doubt = sum(
+            blocks[name][blocks[name].shape[0] - META:, first:first + 128].astype(F32)[0:1, 0:1] for name in doubted if whole(name)[1] != 1
+        )
         out, k = spots[FAR]
         out[k] += jnp.where(lax.broadcasted_iota(jnp.int32, (1, lanes), 1) == flag, doubt, 0.0)
 
 
 def score(name, docs, hot, place, blocks, pairs, made, tasks, sums, doubted=(), weight=1):
     rest, _, _, lanes = layout(docs, hot)
-    names = list(dict.fromkeys([*made, *(task[0] for task in tasks)]))
+    names = list(dict.fromkeys([*made, *(task[0] for task in tasks), *(task[1] for task in tasks if task[1] in blocks)]))
     given = [p for p in pairs if any(p == task[1] for task in tasks)]
     width = blocks[OWN].shape[1]
     vmem = pl.BlockSpec(memory_space=pltpu.VMEM)
@@ -342,7 +370,7 @@
     if made:
         shapes += [jax.ShapeDtypeStruct((width, 2 * rest), BF16), jax.ShapeDtypeStruct((8, 2 * rest), F32)]
     out = pl.pallas_call(
-        lambda *refs: score_kernel(docs, hot, names, given, made, tasks, doubted or made, bool(sums), *refs),
+        lambda *refs: score_kernel(docs, hot, names, given, made, tasks, doubted + made, bool(sums), *refs),
         out_shape=tuple(shapes),
         in_specs=[pl.BlockSpec(memory_space=pltpu.SMEM)] + [vmem] * len(arrays),
         out_specs=tuple(vmem for _ in shapes),
@@ -384,7 +412,7 @@
 
     owner, core = lax.axis_index("owner"), lax.axis_index("split")
     place = jnp.stack([owner // ROWS, owner % ROWS, core]).astype(jnp.int32)
-    same, other, slot = prep(hot, place, cluster_of, states, proj_weight)
+    same, other, *parts, slot = prep(hot, place, cluster_of, states, proj_weight)
 
     def move(a, to, row=0, core=0):
         pairs = [
@@ -404,37 +432,52 @@
 
     blocks, pairs, sums = {OWN: same}, {}, ()
     blocks[CORE] = move(same, STAY, core=1)
-    blocks[PAIR] = move(other, OUTER)
+    for name, part in zip(halves(PAIR), parts[2:]):
+        blocks[name] = move(part, OUTER)
     blocks[ROW] = move(same, STAY, row=1)
     blocks[CORE], other = lax.optimization_barrier((blocks[CORE], other))
     blocks[NEXT] = move(other, MIDDLE)
     sums, pairs = meet("own", HERE, [(OWN, HERE, False, None), (CORE, HERE, False, "core0")], weight=2**33)
 
-    blocks[PAIR], _ = lax.optimization_barrier((blocks[PAIR], sums[0]))
+    far, pair, pair_core, row, diag = (halves(b) for b in (FAR, PAIR, PAIR_CORE, PAIR_ROW, PAIR_DIAG))
+    blocks[pair[0]], blocks[pair[1]], _ = lax.optimization_barrier((blocks[pair[0]], blocks[pair[1]], sums[0]))
+    for k in (0, 1):
+        blocks[row[k]] = move(blocks[pair[k]], STAY, row=1)
+        blocks[far[k]] = move(parts[k], TO_MIDDLE)
+        blocks[pair_core[k]] = move(blocks[pair[k]], STAY, core=1)
     blocks[ROW], blocks[NEXT] = lax.optimization_barrier((blocks[ROW], blocks[NEXT]))
-    blocks[FAR] = move(same, TO_MIDDLE)
-    blocks[PAIR_ROW] = move(blocks[PAIR], STAY, row=1)
-    blocks[PAIR_CORE] = move(blocks[PAIR], STAY, core=1)
     blocks[DIAG] = move(blocks[ROW], STAY, core=1)
     sums, pairs = meet(
         "pair", THERE,
-        [(PAIR, THERE, False, None), (PAIR_CORE, THERE, False, "core1"), (NEXT, HERE, True, None),
-         (NEXT, THERE, True, None)],
+        [(b, THERE, False, None) for b in pair] + [(b, THERE, False, "core1") for b in pair_core]
+        + [(NEXT, HERE, True, None), (NEXT, THERE, True, None)],
         weight=2**33,
     )
     sums, pairs = meet(
         "row", ACROSS,
-        [(PAIR, HERE, True, None), (PAIR, ACROSS, True, None), (NEXT, ACROSS, True, None),
-         (ROW, HERE, False, "row0"), (DIAG, HERE, False, "row1")],
-    )
-    blocks[PAIR_ROW], _ = lax.optimization_barrier((blocks[PAIR_ROW], sums[0]))
-    blocks[PAIR_DIAG] = move(blocks[PAIR_ROW], STAY, core=1)
-    sums, pairs = meet("far", (), [(FAR, p, True, None) for p in (HERE, THERE, ACROSS)])
+        [(b, p, True, None) for b in pair for p in (HERE, ACROSS)]
+        + [(NEXT, ACROSS, True, None), (ROW, HERE, False, "row0"), (DIAG, HERE, False, "row1")],
+    )
+    sums, pairs = meet(
+        "far_a", (),
+        [(far[0], p, True, None) for p in (HERE, THERE, ACROSS)]
+        + [(left, row[0], False, None) for left in (NEXT, far[0])] + [(row[0], THERE, False, "row1")],
+        doubted=(row[0],), weight=1,
+    )
+    blocks[row[0]], blocks[row[1]], _ = lax.optimization_barrier((blocks[row[0]], blocks[row[1]], sums[0]))
+    for k in (0, 1):
+        blocks[diag[k]] = move(blocks[row[k]], STAY, core=1)
+    sums, pairs = meet(
+        "far_b", (),
+        [(far[1], p, True, None) for p in (HERE, THERE, ACROSS)]
+        + [(left, right, False, None) for left, right in ((far[1], row[0]), (NEXT, row[1]), (far[0], row[1]))]
+        + [(far[1], row[1], False, None), (row[1], THERE, False, "row1")],
+    )
     sums, pairs = meet(
         "last", (),
-        [(left, right, False, None) for left in (NEXT, FAR) for right in (PAIR_ROW, PAIR_DIAG)]
-        + [(PAIR_ROW, THERE, False, "row1"), (PAIR_DIAG, THERE, False, "row0")],
-        doubted=(PAIR_ROW, PAIR_DIAG),
+        [(left, right, False, None) for left in (NEXT, *far) for right in diag]
+        + [(b, THERE, False, "row0") for b in diag],
+        doubted=(diag[0],),
     )
     kept, by_core, to_next, to_far = sums
     from_core = move(by_core, STAY, core=1)

time: 65.9 us -> 68.3 us (1.036)
  starting transfers between devices: 15.2 us -> 20.2 us
  waiting for transfers between devices: 22.6 us -> 19.1 us
  Pallas kernels: 10.9 us -> 12 us
    ppermute x15 -> x20, starting transfers between devices: 15.2 us -> 20.2 us  [move(): return lax.ppermute(a, ('owner', 'split'), pairs)]
    ppermute x15 -> x20, waiting for transfers between devices: 22.6 us -> 19.1 us  [move(): return lax.ppermute(a, ('owner', 'split'), pairs)]
    pallas_call x5 -> x6, Pallas kernels: 6.08 us -> 7.66 us  [score(): pl.pallas_call(lambda *refs: score_kernel(docs, hot, names, given, made,...]
  transfers between devices with their start and end apart: 15 -> 20, of which waited for: 4 -> 7; matrix products, arithmetic and copies ran while one was open for 2% -> 2% of each run, Pallas kernels for 7% -> 9%
where the time goes in v10:
time: 68.3 us; the launch traced here: 68.2 us
  starting transfers between devices  20.2 us (30%)
  waiting for transfers between devices  19.1 us (28%)
  between operations  14.8 us (22%)
  Pallas kernels  12 us (18%)
  local copies, waits for them, and re-layouts  1.77 us (3%)
    ppermute x20, starting transfers between devices, move(): return lax.ppermute(a, ('owner', 'split'), pairs)  20.2 us
    ppermute x20, waiting for transfers between devices, move(): return lax.ppermute(a, ('owner', 'split'), pairs)  19.1 us
    pallas_call x6, Pallas kernels, score(): pl.pallas_call(lambda *refs: score_kernel(docs, hot, names, given, made,...  7.66 us
    pallas_call x1, Pallas kernels, prep(): pl.pallas_call(lambda *refs: prep_kernel(hot, *refs), out_shape=(*(shape(...  3.84 us
  transfers between devices with their start and end apart: 20, of which 7 were waited for; matrix products, arithmetic and copies ran while one was open for 2% of the time, Pallas kernels for 9%

profile of v10, /device:TPU:0, one launch (start us, length us, event | category | flops | bytes accessed | tf_op | source)
XLA Modules:
  0.0 68.2 jit_solution(6514497876380250749)
XLA Ops:
  6.6 3.8 %prep.1 = (bf16[336,768]{1,0:T(8,128)(2,1)S(1)}, bf16[336,768]{1,0:T(8,128)(2,1)S(1)}, bf16[176,768]{1,0:T(8,128)(2,1)S(1)}, bf16[176,768]{1,0:T(8,128)(2,1)S(1)...) custom-call(s32[3]{0:T(128)S(1)} %pad_add_fusion.refs_0_, s32[1,512]{1,0:T(1,128)} %bitcast.38, ...), custom_call_target="tpu_custom_call" | custom-call | tf_op jit(solution)/shard_map/prep/pallas_call | solution.py:205
  10.5 0.5 collective-permute-start.1
  11.0 2.6 %collective-permute-start = (bf16[336,768]{1,0:T(8,128)(2,1)S(1)}, bf16[336,768]{1,0:T(8,128)(2,1)S(1)}, u32[]{:S(2)}, u32[]{:S(2)}) collective-permute-start(bf16[336,768]{1,0:T(8,128)(2,1)S(1)} %get-tuple-element.226.refs_1_), channel_id=1, source_target_pairs={{0,2},{1,3},{2,0},{3,1},{4,6},{5,7},{6,4},{7,5},{8,10},{9,11},{10,... | collective-permute-start | bytes 1548296 | tf_op jit(solution)/shard_map/ppermute | solution.py:425
  13.6 1.6 %collective-permute-start.5 = (bf16[176,768]{1,0:T(8,128)(2,1)S(1)}, bf16[176,768]{1,0:T(8,128)(2,1)S(1)}, u32[]{:S(2)}, u32[]{:S(2)}) collective-permute-start(bf16[176,768]{1,0:T(8,128)(2,1)S(1)} %get-tuple-element.232), channel_id=1, source_target_pairs={{0,4},{1,5},{2,6},{3,7},{4,0},{5,1},{6,2},{7,3},{8,12},{9,13},{10,... | collective-permute-start | bytes 811016 | tf_op jit(solution)/shard_map/ppermute | solution.py:425
  15.1 0.4 collective-permute-start.6
  15.6 1.4 %own.1 = (f32[4,1,640]{2,1,0:T(1,128)S(1)}, f32[4,1,640]{2,1,0:T(1,128)S(1)}, f32[1,1,640]{2,1,0:T(1,128)S(1)}, f32[1,1,640]{2,1,0:T(1,128)S(1)}, bf16[768,640]{1,0:T(8,128)(2,1)S(1)}, /*index=5*/f32[8,640]{1,0:T(8,128)S(1)}) custom-call(s32[3]{0:T(128)S(1)} %pad_add_fusion.refs_0_, bf16[336,768]{1,0:T(8,128)(2,1)S(1)} %get-tuple-element.226.refs_1_, ...), custom_call_target="tpu_custom_call" | custom-call | flops 8589934592 | bytes 1024 | tf_op jit(solution)/shard_map/own/pallas_call | solution.py:372
  17.0 5.9 %collective-permute-done.5.refs_1_.refs_3_ = bf16[176,768]{1,0:T(8,128)(2,1)S(1)} collective-permute-done((bf16[176,768]{1,0:T(8,128)(2,1)S(1)}, bf16[176,768]{1,0:T(8,128)(2,1)S(1)}, u32[]{:S(2)}, u32[]{:S(2)}) %collective-permute-start.5) | collective-permute-done | bytes 270368 | tf_op jit(solution)/shard_map/ppermute | solution.py:425
  22.9 5.0 %collective-permute-done.6.refs_2_.refs_4_ = bf16[176,768]{1,0:T(8,128)(2,1)S(1)} collective-permute-done((bf16[176,768]{1,0:T(8,128)(2,1)S(1)}, bf16[176,768]{1,0:T(8,128)(2,1)S(1)}, u32[]{:S(2)}, u32[]{:S(2)}) %collective-permute-start.6) | collective-permute-done | bytes 270368 | tf_op jit(solution)/shard_map/ppermute | solution.py:425
  27.9 0.5 collective-permute-start.10
  28.4 2.6 %collective-permute-start.3 = (bf16[176,768]{1,0:T(8,128)(2,1)S(1)}, bf16[176,768]{1,0:T(8,128)(2,1)S(1)}, u32[]{:S(2)}, u32[]{:S(2)}) collective-permute-start(bf16[176,768]{1,0:T(8,128)(2,1)S(1)} %get-tuple-element.230), channel_id=1, source_target_pairs={{0,8},{1,9},{2,10},{3,11},{4,0},{5,1},{6,2},{7,3},{8,12},{9,13},{1... | collective-permute-start | bytes 811016 | tf_op jit(solution)/shard_map/ppermute | solution.py:425
  31.0 1.6 %collective-permute-start.4 = (bf16[176,768]{1,0:T(8,128)(2,1)S(1)}, bf16[176,768]{1,0:T(8,128)(2,1)S(1)}, u32[]{:S(2)}, u32[]{:S(2)}) collective-permute-start(bf16[176,768]{1,0:T(8,128)(2,1)S(1)} %get-tuple-element.231), channel_id=1, source_target_pairs={{0,8},{1,9},{2,10},{3,11},{4,0},{5,1},{6,2},{7,3},{8,12},{9,13},{1... | collective-permute-start | bytes 811016 | tf_op jit(solution)/shard_map/ppermute | solution.py:425
  32.6 0.5 collective-permute-start.7
  33.1 1.5 %collective-permute-start.8 = (bf16[176,768]{1,0:T(8,128)(2,1)S(1)}, bf16[176,768]{1,0:T(8,128)(2,1)S(1)}, u32[]{:S(2)}, u32[]{:S(2)}) collective-permute-start(bf16[176,768]{1,0:T(8,128)(2,1)S(1)} %collective-permute-done.6.refs_2_.refs_4_), channel_id=1, source_target_pairs={{0,2},{1,3},{2,0},{3,1},{4,6},{5,7},{6,4},{7,5},{8,10},{9,11},{10,... | collective-permute-start | bytes 811016 | tf_op jit(solution)/shard_map/ppermute | solution.py:425
  34.6 1.1 %pair.1 = (f32[4,1,640]{2,1,0:T(1,128)S(1)}, f32[4,1,640]{2,1,0:T(1,128)S(1)}, f32[1,1,640]{2,1,0:T(1,128)S(1)}, f32[1,1,640]{2,1,0:T(1,128)S(1)}, bf16[768,640]{1,0:T(8,128)(2,1)S(1)}, /*index=5*/f32[8,640]{1,0:T(8,128)S(1)}) custom-call(s32[3]{0:T(128)S(1)} %pad_add_fusion.refs_0_, bf16[176,768]{1,0:T(8,128)(2,1)S(1)} %collective-permute-done.5.refs_1_.refs_3_, ...), custom_call_target="tpu_custom_call" | custom-call | flops 8589934592 | bytes 1024 | tf_op jit(solution)/shard_map/pair/pallas_call | solution.py:372
  35.7 0.8 %collective-permute-done.11.refs_2_ = bf16[336,768]{1,0:T(8,128)(2,1)S(1)} collective-permute-done((bf16[336,768]{1,0:T(8,128)(2,1)S(1)}, bf16[336,768]{1,0:T(8,128)(2,1)S(1)}, u32[]{:S(2)}, u32[]{:S(2)}) %collective-permute-start.11) | collective-permute-done | bytes 516128 | tf_op jit(solution)/shard_map/ppermute | solution.py:425
  36.5 2.1 %row.1 = (f32[4,1,640]{2,1,0:T(1,128)S(1)}, f32[4,1,640]{2,1,0:T(1,128)S(1)}, f32[1,1,640]{2,1,0:T(1,128)S(1)}, f32[1,1,640]{2,1,0:T(1,128)S(1)}, bf16[768,640]{1,0:T(8,128)(2,1)S(1)}, /*index=5*/f32[8,640]{1,0:T(8,128)S(1)}) custom-call(s32[3]{0:T(128)S(1)} %pad_add_fusion.refs_0_, bf16[336,768]{1,0:T(8,128)(2,1)S(1)} %collective-permute-done.refs_1_, ...), custom_call_target="tpu_custom_call" | custom-call | flops 1 | bytes 1024 | tf_op jit(solution)/shard_map/row/pallas_call | solution.py:372
  38.7 3.3 %collective-permute-done.7.refs_3_.refs_5_ = bf16[176,768]{1,0:T(8,128)(2,1)S(1)} collective-permute-done((bf16[176,768]{1,0:T(8,128)(2,1)S(1)}, bf16[176,768]{1,0:T(8,128)(2,1)S(1)}, u32[]{:S(2)}, u32[]{:S(2)}) %collective-permute-start.7) | collective-permute-done | bytes 270368 | tf_op jit(solution)/shard_map/ppermute | solution.py:425
  42.0 0.9 %far_a.1 = (f32[4,1,640]{2,1,0:T(1,128)S(1)}, f32[4,1,640]{2,1,0:T(1,128)S(1)}, f32[1,1,640]{2,1,0:T(1,128)S(1)}, f32[1,1,640]{2,1,0:T(1,128)S(1)}) custom-call(s32[3]{0:T(128)S(1)} %pad_add_fusion.refs_0_, bf16[176,768]{1,0:T(8,128)(2,1)S(1)} %collective-permute-done.3.refs_1_.refs_3_.refs_2_, ...), custom_call_target="tpu_custom_call" | custom-call | flops 1 | bytes 1024 | tf_op jit(solution)/shard_map/far_a/pallas_call | solution.py:372
  42.9 3.3 %collective-permute-done.8.refs_4_ = bf16[176,768]{1,0:T(8,128)(2,1)S(1)} collective-permute-done((bf16[176,768]{1,0:T(8,128)(2,1)S(1)}, bf16[176,768]{1,0:T(8,128)(2,1)S(1)}, u32[]{:S(2)}, u32[]{:S(2)}) %collective-permute-start.8) | collective-permute-done | bytes 270368 | tf_op jit(solution)/shard_map/ppermute | solution.py:425
  46.2 0.5 collective-permute-start.13
  46.7 0.7 far_b.1
  47.8 0.4 collective-permute-done.13.refs_5_
  48.2 1.4 %last.1 = (f32[4,1,640]{2,1,0:T(1,128)S(1)}, f32[4,1,640]{2,1,0:T(1,128)S(1)}, f32[1,1,640]{2,1,0:T(1,128)S(1)}, f32[1,1,640]{2,1,0:T(1,128)S(1)}) custom-call(s32[3]{0:T(128)S(1)} %pad_add_fusion.refs_0_, bf16[336,768]{1,0:T(8,128)(2,1)S(1)} %collective-permute-done.2.refs_5_.refs_2_.refs_1_, ...), custom_call_target="tpu_custom_call" | custom-call | flops 1 | bytes 1024 | tf_op jit(solution)/shard_map/last/pallas_call | solution.py:372
  49.8 0.4 collective-permute-start.16
  50.1 3.8 %collective-permute-start.14 = (f32[1,1,640]{2,1,0:T(1,128)S(1)}, f32[1,1,640]{2,1,0:T(1,128)S(1)}, u32[]{:S(2)}, u32[]{:S(2)}) collective-permute-start(f32[1,1,640]{2,1,0:T(1,128)S(1)} %get-tuple-element.266), channel_id=1, source_target_pairs={{0,8},{1,9},{2,10},{3,11},{4,12},{5,13},{6,14},{7,15},{8,0},{9,1},... | collective-permute-start | bytes 7688 | tf_op jit(solution)/shard_map/ppermute | solution.py:425
  54.0 1.1 %collective-permute-start.18 = (f32[1,1,640]{2,1,0:T(1,128)S(1)}, f32[1,1,640]{2,1,0:T(1,128)S(1)}, u32[]{:S(2)}, u32[]{:S(2)}) collective-permute-start(f32[1,1,640]{2,1,0:T(1,128)S(1)} %get-tuple-element.347), channel_id=1, source_target_pairs={{0,2},{1,3},{2,0},{3,1},{4,6},{5,7},{6,4},{7,5},{8,10},{9,11},{10,... | collective-permute-start | bytes 7688 | tf_op jit(solution)/shard_map/ppermute | solution.py:425
  55.1 2.4 %collective-permute-start.17 = (f32[1,1,640]{2,1,0:T(1,128)S(1)}, f32[1,1,640]{2,1,0:T(1,128)S(1)}, u32[]{:S(2)}, u32[]{:S(2)}) collective-permute-start(f32[1,1,640]{2,1,0:T(1,128)S(1)} %get-tuple-element.348), channel_id=1, source_target_pairs={{0,4},{1,5},{2,6},{3,7},{4,0},{5,1},{6,2},{7,3},{8,12},{9,13},{10,... | collective-permute-start | bytes 7688 | tf_op jit(solution)/shard_map/ppermute | solution.py:425
  57.5 0.6 slice.45
  58.0 0.6 slice.46
  60.0 0.8 %conditional.1 = (f32[512]{0:T(512)S(1)}) conditional(s32[]{:T(128)} %bitcast.12, (f32[4,1,640]{2,1,0:T(1,128)S(1)}, f32[4,1,640]{2,1,0:T(1,128)S(1)}, s32[1,512]{1,0:T(1,128)S(1)}, f32[1,1,640]{2,1,0:T(1,128)S(1)}, f32[1,1,640]{2,1,0:T(1,128)S(1)}, /*index=5*/f32[1,1,640]{2,1,0:T(1,128)S(1)}, f32[1,1,640]{2,1,0:T(1,128)S(1)}, ...), branch_computations={%region_0.1_spmd, %region_1.13_spmd} | conditional | flops 4454147584 | bytes 57829452 | solution.py:490
  60.0 0.5 finish.1
  60.8 0.6 copy-done.5
  (28 shorter events, 0.7 us)
Async XLA Ops:
  10.5 5.1 %collective-permute-start.1 = (bf16[336,768]{1,0:T(8,128)(2,1)S(1)}, bf16[336,768]{1,0:T(8,128)(2,1)S(1)}, u32[]{:S(2)}, u32[]{:S(2)}) collective-permute-start(bf16[336,768]{1,0:T(8,128)(2,1)S(1)} %get-tuple-element.226.refs_1_), channel_id=1, source_target_pairs={{0,1},{1,0},{2,3},{3,2},{4,5},{5,4},{6,7},{7,6},{8,9},{9,8},{10,11... | collective-permute-start | bytes 1548296 | tf_op jit(solution)/shard_map/ppermute | solution.py:425
  11.0 20.0 %collective-permute-start = (bf16[336,768]{1,0:T(8,128)(2,1)S(1)}, bf16[336,768]{1,0:T(8,128)(2,1)S(1)}, u32[]{:S(2)}, u32[]{:S(2)}) collective-permute-start(bf16[336,768]{1,0:T(8,128)(2,1)S(1)} %get-tuple-element.226.refs_1_), channel_id=1, source_target_pairs={{0,2},{1,3},{2,0},{3,1},{4,6},{5,7},{6,4},{7,5},{8,10},{9,11},{10,... | collective-permute-start | bytes 1548296 | tf_op jit(solution)/shard_map/ppermute | solution.py:425
  13.6 9.3 %collective-permute-start.5 = (bf16[176,768]{1,0:T(8,128)(2,1)S(1)}, bf16[176,768]{1,0:T(8,128)(2,1)S(1)}, u32[]{:S(2)}, u32[]{:S(2)}) collective-permute-start(bf16[176,768]{1,0:T(8,128)(2,1)S(1)} %get-tuple-element.232), channel_id=1, source_target_pairs={{0,4},{1,5},{2,6},{3,7},{4,0},{5,1},{6,2},{7,3},{8,12},{9,13},{10,... | collective-permute-start | bytes 811016 | tf_op jit(solution)/shard_map/ppermute | solution.py:425
  15.1 12.8 %collective-permute-start.6 = (bf16[176,768]{1,0:T(8,128)(2,1)S(1)}, bf16[176,768]{1,0:T(8,128)(2,1)S(1)}, u32[]{:S(2)}, u32[]{:S(2)}) collective-permute-start(bf16[176,768]{1,0:T(8,128)(2,1)S(1)} %get-tuple-element.233), channel_id=1, source_target_pairs={{0,4},{1,5},{2,6},{3,7},{4,0},{5,1},{6,2},{7,3},{8,12},{9,13},{10,... | collective-permute-start | bytes 811016 | tf_op jit(solution)/shard_map/ppermute | solution.py:425
  15.6 17.0 %collective-permute-start.2 = (bf16[336,768]{1,0:T(8,128)(2,1)S(1)}, bf16[336,768]{1,0:T(8,128)(2,1)S(1)}, u32[]{:S(2)}, u32[]{:S(2)}) collective-permute-start(bf16[336,768]{1,0:T(8,128)(2,1)S(1)} %get-tuple-element.228), channel_id=1, source_target_pairs={{0,1},{1,0},{2,3},{3,2},{4,8},{5,9},{6,10},{7,11},{8,4},{9,5},{10,... | collective-permute-start | bytes 1548296 | tf_op jit(solution)/shard_map/ppermute | solution.py:425
  27.9 5.2 %collective-permute-start.9 = (bf16[176,768]{1,0:T(8,128)(2,1)S(1)}, bf16[176,768]{1,0:T(8,128)(2,1)S(1)}, u32[]{:S(2)}, u32[]{:S(2)}) collective-permute-start(bf16[176,768]{1,0:T(8,128)(2,1)S(1)} %collective-permute-done.5.refs_1_.refs_3_), channel_id=1, source_target_pairs={{0,1},{1,0},{2,3},{3,2},{4,5},{5,4},{6,7},{7,6},{8,9},{9,8},{10,11... | collective-permute-start | bytes 811016 | tf_op jit(solution)/shard_map/ppermute | solution.py:425
  27.9 6.7 %collective-permute-start.10 = (bf16[176,768]{1,0:T(8,128)(2,1)S(1)}, bf16[176,768]{1,0:T(8,128)(2,1)S(1)}, u32[]{:S(2)}, u32[]{:S(2)}) collective-permute-start(bf16[176,768]{1,0:T(8,128)(2,1)S(1)} %collective-permute-done.6.refs_2_.refs_4_), channel_id=1, source_target_pairs={{0,1},{1,0},{2,3},{3,2},{4,5},{5,4},{6,7},{7,6},{8,9},{9,8},{10,11... | collective-permute-start | bytes 811016 | tf_op jit(solution)/shard_map/ppermute | solution.py:425
  28.4 10.3 %collective-permute-start.3 = (bf16[176,768]{1,0:T(8,128)(2,1)S(1)}, bf16[176,768]{1,0:T(8,128)(2,1)S(1)}, u32[]{:S(2)}, u32[]{:S(2)}) collective-permute-start(bf16[176,768]{1,0:T(8,128)(2,1)S(1)} %get-tuple-element.230), channel_id=1, source_target_pairs={{0,8},{1,9},{2,10},{3,11},{4,0},{5,1},{6,2},{7,3},{8,12},{9,13},{1... | collective-permute-start | bytes 811016 | tf_op jit(solution)/shard_map/ppermute | solution.py:425
  31.0 15.7 %collective-permute-start.4 = (bf16[176,768]{1,0:T(8,128)(2,1)S(1)}, bf16[176,768]{1,0:T(8,128)(2,1)S(1)}, u32[]{:S(2)}, u32[]{:S(2)}) collective-permute-start(bf16[176,768]{1,0:T(8,128)(2,1)S(1)} %get-tuple-element.231), channel_id=1, source_target_pairs={{0,8},{1,9},{2,10},{3,11},{4,0},{5,1},{6,2},{7,3},{8,12},{9,13},{1... | collective-permute-start | bytes 811016 | tf_op jit(solution)/shard_map/ppermute | solution.py:425
  32.6 9.4 %collective-permute-start.7 = (bf16[176,768]{1,0:T(8,128)(2,1)S(1)}, bf16[176,768]{1,0:T(8,128)(2,1)S(1)}, u32[]{:S(2)}, u32[]{:S(2)}) collective-permute-start(bf16[176,768]{1,0:T(8,128)(2,1)S(1)} %collective-permute-done.5.refs_1_.refs_3_), channel_id=1, source_target_pairs={{0,2},{1,3},{2,0},{3,1},{4,6},{5,7},{6,4},{7,5},{8,10},{9,11},{10,... | collective-permute-start | bytes 811016 | tf_op jit(solution)/shard_map/ppermute | solution.py:425
  33.1 13.1 %collective-permute-start.8 = (bf16[176,768]{1,0:T(8,128)(2,1)S(1)}, bf16[176,768]{1,0:T(8,128)(2,1)S(1)}, u32[]{:S(2)}, u32[]{:S(2)}) collective-permute-start(bf16[176,768]{1,0:T(8,128)(2,1)S(1)} %collective-permute-done.6.refs_2_.refs_4_), channel_id=1, source_target_pairs={{0,2},{1,3},{2,0},{3,1},{4,6},{5,7},{6,4},{7,5},{8,10},{9,11},{10,... | collective-permute-start | bytes 811016 | tf_op jit(solution)/shard_map/ppermute | solution.py:425
  34.6 1.9 %collective-permute-start.11 = (bf16[336,768]{1,0:T(8,128)(2,1)S(1)}, bf16[336,768]{1,0:T(8,128)(2,1)S(1)}, u32[]{:S(2)}, u32[]{:S(2)}) collective-permute-start(bf16[336,768]{1,0:T(8,128)(2,1)S(1)} %collective-permute-done.refs_1_), channel_id=1, source_target_pairs={{0,1},{1,0},{2,3},{3,2},{4,5},{5,4},{6,7},{7,6},{8,9},{9,8},{10,11... | collective-permute-start | bytes 1548296 | tf_op jit(solution)/shard_map/ppermute | solution.py:425
  46.2 1.5 %collective-permute-start.12 = (bf16[176,768]{1,0:T(8,128)(2,1)S(1)}, bf16[176,768]{1,0:T(8,128)(2,1)S(1)}, u32[]{:S(2)}, u32[]{:S(2)}) collective-permute-start(bf16[176,768]{1,0:T(8,128)(2,1)S(1)} %collective-permute-done.7.refs_3_.refs_5_), channel_id=1, source_target_pairs={{0,1},{1,0},{2,3},{3,2},{4,5},{5,4},{6,7},{7,6},{8,9},{9,8},{10,11... | collective-permute-start | bytes 811016 | tf_op jit(solution)/shard_map/ppermute | solution.py:425
  46.2 1.9 %collective-permute-start.13 = (bf16[176,768]{1,0:T(8,128)(2,1)S(1)}, bf16[176,768]{1,0:T(8,128)(2,1)S(1)}, u32[]{:S(2)}, u32[]{:S(2)}) collective-permute-start(bf16[176,768]{1,0:T(8,128)(2,1)S(1)} %collective-permute-done.8.refs_4_), channel_id=1, source_target_pairs={{0,1},{1,0},{2,3},{3,2},{4,5},{5,4},{6,7},{7,6},{8,9},{9,8},{10,11... | collective-permute-start | bytes 811016 | tf_op jit(solution)/shard_map/ppermute | solution.py:425
  47.4 12.6 %copy-start.2 = (bf16[512,1024]{1,0:T(8,128)(2,1)S(1)}, bf16[512,1024]{1,0:T(8,128)(2,1)}, u32[]{:S(2)}) copy-start(bf16[512,1024]{1,0:T(8,128)(2,1)} %refs_2_.1) | copy-start | bytes 3145732
  47.4 12.6 %copy-start.4 = (s32[512]{0:T(512)S(1)}, s32[512]{0:T(512)}, u32[]{:S(2)}) copy-start(s32[512]{0:T(512)} %param.9) | copy-start | bytes 6148
  49.6 4.3 %collective-permute-start.15 = (f32[4,1,640]{2,1,0:T(1,128)S(1)}, f32[4,1,640]{2,1,0:T(1,128)S(1)}, u32[]{:S(2)}, u32[]{:S(2)}) collective-permute-start(f32[4,1,640]{2,1,0:T(1,128)S(1)} %get-tuple-element.268), channel_id=1, source_target_pairs={{0,1},{1,0},{2,3},{3,2},{4,5},{5,4},{6,7},{7,6},{8,9},{9,8},{10,11... | collective-permute-start | bytes 30728 | tf_op jit(solution)/shard_map/ppermute | solution.py:425
  49.8 10.2 %collective-permute-start.16 = (f32[1,1,640]{2,1,0:T(1,128)S(1)}, f32[1,1,640]{2,1,0:T(1,128)S(1)}, u32[]{:S(2)}, u32[]{:S(2)}) collective-permute-start(f32[1,1,640]{2,1,0:T(1,128)S(1)} %get-tuple-element.270), channel_id=1, source_target_pairs={{0,1},{1,0},{2,3},{3,2},{4,8},{5,9},{6,10},{7,11},{8,4},{9,5},{10,... | collective-permute-start | bytes 7688 | tf_op jit(solution)/shard_map/ppermute | solution.py:425
  50.1 7.9 %collective-permute-start.14 = (f32[1,1,640]{2,1,0:T(1,128)S(1)}, f32[1,1,640]{2,1,0:T(1,128)S(1)}, u32[]{:S(2)}, u32[]{:S(2)}) collective-permute-start(f32[1,1,640]{2,1,0:T(1,128)S(1)} %get-tuple-element.266), channel_id=1, source_target_pairs={{0,8},{1,9},{2,10},{3,11},{4,12},{5,13},{6,14},{7,15},{8,0},{9,1},... | collective-permute-start | bytes 7688 | tf_op jit(solution)/shard_map/ppermute | solution.py:425
  53.9 6.0 %collective-permute-start.19 = (f32[1,1,640]{2,1,0:T(1,128)S(1)}, f32[1,1,640]{2,1,0:T(1,128)S(1)}, u32[]{:S(2)}, u32[]{:S(2)}) collective-permute-start(f32[1,1,640]{2,1,0:T(1,128)S(1)} %get-tuple-element.346), channel_id=1, source_target_pairs={{0,6},{1,7},{2,4},{3,5},{4,2},{5,3},{6,0},{7,1},{8,14},{9,15},{10,... | collective-permute-start | bytes 7688 | tf_op jit(solution)/shard_map/ppermute | solution.py:425
  54.0 6.0 %collective-permute-start.18 = (f32[1,1,640]{2,1,0:T(1,128)S(1)}, f32[1,1,640]{2,1,0:T(1,128)S(1)}, u32[]{:S(2)}, u32[]{:S(2)}) collective-permute-start(f32[1,1,640]{2,1,0:T(1,128)S(1)} %get-tuple-element.347), channel_id=1, source_target_pairs={{0,2},{1,3},{2,0},{3,1},{4,6},{5,7},{6,4},{7,5},{8,10},{9,11},{10,... | collective-permute-start | bytes 7688 | tf_op jit(solution)/shard_map/ppermute | solution.py:425
  55.1 4.9 %collective-permute-start.17 = (f32[1,1,640]{2,1,0:T(1,128)S(1)}, f32[1,1,640]{2,1,0:T(1,128)S(1)}, u32[]{:S(2)}, u32[]{:S(2)}) collective-permute-start(f32[1,1,640]{2,1,0:T(1,128)S(1)} %get-tuple-element.348), channel_id=1, source_target_pairs={{0,4},{1,5},{2,6},{3,7},{4,0},{5,1},{6,2},{7,3},{8,12},{9,13},{10,... | collective-permute-start | bytes 7688 | tf_op jit(solution)/shard_map/ppermute | solution.py:425
  60.8 0.6 copy-start.5

commit v11 on v9

--- a/solution.py
+++ b/solution.py
@@ -122,15 +122,10 @@
     return rest, first, flag, up(flag + 1, 128)
 
 
-def prep_kernel(hot, place_ref, cl_ref, st_hbm, w_hbm, same_ref, other_ref, slot_ref, vectors, st_ref, w_ref, sems):
+def prep_kernel(hot, place_ref, cl_ref, st_ref, w_ref, same_ref, other_ref, slot_ref, vectors):
     docs = st_ref.shape[0]
     rest, first, flag, lanes = layout(docs, hot)
     tile = 128
-    copies = [
-        pltpu.make_async_copy(w_hbm, w_ref, sems.at[0]), pltpu.make_async_copy(st_hbm, st_ref, sems.at[1])
-    ]
-    for copy in copies:
-        copy.start()
 
     cluster = cl_ref[...]
     group = cluster // CLUS_OWN
@@ -141,6 +136,12 @@
     )
     doubt = jnp.where(jnp.sum(full.astype(F32), axis=0, keepdims=True) == 1.0, 0.0, 1.0)
     in_hot = group == chosen
+
+    for t in range(docs // tile):
+        rows = slice(t * tile, (t + 1) * tile)
+        projected = jnp.dot(st_ref[rows, :], w_ref[...], preferred_element_type=F32)
+        norm = lax.rsqrt(jnp.sum(projected * projected, axis=1, keepdims=True) + EPS)
+        vectors[rows, :] = (projected * (norm * math.sqrt(SCALE))).astype(BF16)
 
     ahead = (
         lax.broadcasted_iota(jnp.int32, (docs, docs), 0) < lax.broadcasted_iota(jnp.int32, (docs, docs), 1)
@@ -153,22 +154,13 @@
 
     sort = (lax.broadcasted_iota(jnp.int32, (lanes, docs), 0) == slot).astype(F32).astype(BF16)
     cluster_rows = jnp.broadcast_to(cluster.astype(F32), (META, docs)).astype(BF16)
+    sorted_n = jnp.dot(sort[:rest, :], vectors[...], preferred_element_type=F32).astype(BF16)
+    sorted_h = jnp.dot(sort[first:flag, :], vectors[...], preferred_element_type=F32).astype(BF16)
     ids = lax.dot_general(
         cluster_rows, sort, (((1,), (1,)), ((), ())), preferred_element_type=F32
     )
     ids = ids.astype(BF16)
 
-
-    for copy in copies:
-        copy.wait()
-    for t in range(docs // tile):
-        rows = slice(t * tile, (t + 1) * tile)
-        projected = jnp.dot(st_ref[rows, :], w_ref[...], preferred_element_type=F32)
-        norm = lax.rsqrt(jnp.sum(projected * projected, axis=1, keepdims=True) + EPS)
-        vectors[rows, :] = (projected * (norm * math.sqrt(SCALE))).astype(BF16)
-
-    sorted_n = jnp.dot(sort[:rest, :], vectors[...], preferred_element_type=F32).astype(BF16)
-    sorted_h = jnp.dot(sort[first:flag, :], vectors[...], preferred_element_type=F32).astype(BF16)
 
     def fill_n(ref):
         ref[:rest, :] = sorted_n
@@ -207,11 +199,8 @@
             shape((rest + META, width), BF16),
             shape((1, docs), jnp.int32),
         ),
-        in_specs=[pl.BlockSpec(memory_space=pltpu.SMEM), vmem] + [pl.BlockSpec(memory_space=pl.ANY)] * 2,
-        scratch_shapes=[
-            pltpu.VMEM((docs, width), BF16), pltpu.VMEM(states.shape, BF16), pltpu.VMEM(proj_weight.shape, BF16),
-            pltpu.SemaphoreType.DMA((2,)),
-        ],
+        in_specs=[pl.BlockSpec(memory_space=pltpu.SMEM), vmem, vmem, vmem],
+        scratch_shapes=[pltpu.VMEM((docs, width), BF16)],
         compiler_params=pltpu.CompilerParams(vmem_limit_bytes=24 * 2**20),
         name="prep",
     )(place, cluster_of.reshape(1, docs), states, proj_weight)
@@ -257,7 +246,12 @@
 
             def work(left=left):
                 own_tasks = [task for task in tasks if task[0] == left]
-                block = blocks[left][:count, :]
+                rows = count * len(left)
+                block = blocks[left[0]][:count, :]
+                column = columns[left[0]][:, 0:1]
+                for name in left[1:]:
+                    block = jnp.concatenate([block, blocks[name][:count, :]], axis=0)
+                    column = jnp.concatenate([column, columns[name][:, 0:1]], axis=0)
                 fresh = True
                 for _, right, both, _ in own_tasks:
                     if right in blocks:
@@ -265,7 +259,7 @@
                         ids = blocks[right][rest:, 0:wide].astype(F32)[0:1, 0:count]
                     else:
                         turned, notes = pairs[right]
-                        span, rights, diagonal = two if both else wide, right[:1 + both], left == right[0]
+                        span, rights, diagonal = two if both else wide, right[:1 + both], left == right[:1]
                         ids = notes[0:1, 0:span]
                         if not both:
                             ids = jnp.where(lax.broadcasted_iota(jnp.int32, ids.shape, 1) < count, ids, -1.0)
@@ -279,7 +273,7 @@
                             )
                         else:
                             inner = jnp.dot(block, turned[:, low:high], preferred_element_type=F32)
-                        same = columns[left][:, 0:1] == ids[:, low:high]
+                        same = column == ids[:, low:high]
                         if diagonal:
                             same &= lax.broadcasted_iota(jnp.int32, inner.shape, 0) != (
                                 lax.broadcasted_iota(jnp.int32, inner.shape, 1) + low
@@ -291,31 +285,32 @@
                             for t in range(0, high - low, 128):
                                 piece = weights[:, t:t + 128]
                                 if piece.shape[1] < 128:
-                                    blank = jnp.zeros((count, 128 - piece.shape[1]), F32)
+                                    blank = jnp.zeros((rows, 128 - piece.shape[1]), F32)
                                     piece = jnp.concatenate([piece, blank], axis=1)
                                 part = piece if part is None else part + piece
                             if fresh:
-                                parts[0:count, :] = part
+                                parts[0:rows, :] = part
                             else:
-                                parts[0:count, :] += part
+                                parts[0:rows, :] += part
                             fresh = False
                     total = jnp.concatenate(totals, axis=1) if len(totals) > 1 else totals[0]
                     for k, name in enumerate(rights):
                         out, spot = spots[name]
                         out[spot, :, lane] += total[:, k * count:(k + 1) * count]
                 if not fresh:
-                    part = parts[0:count, :]
+                    part = parts[0:rows, :]
                     high = part.astype(BF16)
                     low = (part - high.astype(F32)).astype(BF16)
                     total = lax.dot_general(
                         jnp.ones((16, 256), BF16), jnp.concatenate([high, low], axis=1),
                         (((1,), (1,)), ((), ())), preferred_element_type=F32,
                     )
-                    out, spot = spots[left]
-                    out[spot, :, lane] += total[0:1, :]
+                    for k, name in enumerate(left):
+                        out, spot = spots[name]
+                        out[spot, :, lane] += total[0:1, k * count:(k + 1) * count]
 
             condition = [task[3] for task in tasks if task[0] == left][0]
-            if left in (NEXT, FAR):
+            if left[0] in (NEXT, FAR):
                 pl.when(middle)(work)
             elif condition:
                 pl.when(when[condition])(work)
@@ -333,7 +328,7 @@
 
 def score(name, docs, hot, place, blocks, pairs, made, tasks, sums, doubted=(), weight=1):
     rest, _, _, lanes = layout(docs, hot)
-    names = list(dict.fromkeys([*made, *(task[0] for task in tasks)]))
+    names = list(dict.fromkeys([*made, *(name for task in tasks for name in task[0])]))
     given = [p for p in pairs if any(p == task[1] for task in tasks)]
     width = blocks[OWN].shape[1]
     vmem = pl.BlockSpec(memory_space=pltpu.VMEM)
@@ -346,7 +341,7 @@
         out_shape=tuple(shapes),
         in_specs=[pl.BlockSpec(memory_space=pltpu.SMEM)] + [vmem] * len(arrays),
         out_specs=tuple(vmem for _ in shapes),
-        scratch_shapes=[pltpu.VMEM((rest, 128), F32)],
+        scratch_shapes=[pltpu.VMEM((2 * rest, 128), F32)],
         compiler_params=pltpu.CompilerParams(vmem_limit_bytes=20 * 2**20),
         cost_estimate=pl.CostEstimate(flops=weight, bytes_accessed=2**10, transcendentals=0),
         name=name,
@@ -408,7 +403,7 @@
     blocks[ROW] = move(same, STAY, row=1)
     blocks[CORE], other = lax.optimization_barrier((blocks[CORE], other))
     blocks[NEXT] = move(other, MIDDLE)
-    sums, pairs = meet("own", HERE, [(OWN, HERE, False, None), (CORE, HERE, False, "core0")], weight=2**33)
+    sums, pairs = meet("own", HERE, [((OWN,), HERE, False, None), ((CORE,), HERE, False, "core0")], weight=2**33)
 
     blocks[PAIR], _ = lax.optimization_barrier((blocks[PAIR], sums[0]))
     blocks[ROW], blocks[NEXT] = lax.optimization_barrier((blocks[ROW], blocks[NEXT]))
@@ -418,27 +413,28 @@
     blocks[DIAG] = move(blocks[ROW], STAY, core=1)
     sums, pairs = meet(
         "pair", THERE,
-        [(PAIR, THERE, False, None), (PAIR_CORE, THERE, False, "core1"), (NEXT, HERE, True, None),
-         (NEXT, THERE, True, None)],
+        [((PAIR,), THERE, False, None), ((PAIR_CORE,), THERE, False, "core1"), ((NEXT,), HERE, True, None),
+         ((NEXT,), THERE, True, None)],
         weight=2**33,
     )
     sums, pairs = meet(
         "row", ACROSS,
-        [(PAIR, HERE, True, None), (PAIR, ACROSS, True, None), (NEXT, ACROSS, True, None),
-         (ROW, HERE, False, "row0"), (DIAG, HERE, False, "row1")],
+        [((PAIR,), HERE, True, None), ((PAIR,), ACROSS, True, None), ((NEXT,), ACROSS, True, None),
+         ((ROW,), HERE, False, "row0"), ((DIAG,), HERE, False, "row1")],
     )
     blocks[PAIR_ROW], _ = lax.optimization_barrier((blocks[PAIR_ROW], sums[0]))
     blocks[PAIR_DIAG] = move(blocks[PAIR_ROW], STAY, core=1)
-    sums, pairs = meet("far", (), [(FAR, p, True, None) for p in (HERE, THERE, ACROSS)])
+    sums, pairs = meet("far", (), [((FAR,), p, True, None) for p in (HERE, THERE, ACROSS)])
     sums, pairs = meet(
         "last", (),
-        [(left, right, False, None) for left in (NEXT, FAR) for right in (PAIR_ROW, PAIR_DIAG)]
-        + [(PAIR_ROW, THERE, False, "row1"), (PAIR_DIAG, THERE, False, "row0")],
+        [((NEXT, FAR), right, False, None) for right in (PAIR_ROW, PAIR_DIAG)]
+        + [((PAIR_ROW,), THERE, False, "row1"), ((PAIR_DIAG,), THERE, False, "row0")],
         doubted=(PAIR_ROW, PAIR_DIAG),
     )
     kept, by_core, to_next, to_far = sums
-    from_core = move(by_core, STAY, core=1)
-    from_next, from_far = move(to_next, MIDDLE), move(to_far, TWO)
+    from_core, from_far = move(by_core, STAY, core=1), move(to_far, TWO)
+    from_core, to_next = lax.optimization_barrier((from_core, to_next))
+    from_next = move(to_next, MIDDLE)
     own, pair, row, pair_row = (kept[k:k + 1] + from_core[k:k + 1] for k in (0, 1, 2, 3))
     home = [
         own, from_next, from_far,

time: 65.9 us -> 63.8 us (0.968)
  starting transfers between devices: 15.2 us -> 13.8 us
  Pallas kernels: 10.9 us -> 10.1 us
    ppermute x15, starting transfers between devices: 15.2 us -> 13.8 us  [move(): return lax.ppermute(a, ('owner', 'split'), pairs)]
    pallas_call x1, Pallas kernels: 4.33 us -> 3.56 us  [prep(): pl.pallas_call(lambda *refs: prep_kernel(hot, *refs), out_shape=(shape((r...]
  transfers between devices with their start and end apart: 15 -> 15, of which waited for: 4 -> 4; matrix products, arithmetic and copies ran while one was open for 2% -> 2% of each run, Pallas kernels for 7% -> 8%
where the time goes in v11:
time: 63.8 us; the launch traced here: 63.6 us
  waiting for transfers between devices  22.6 us (35%)
  between operations  14.8 us (23%)
  starting transfers between devices  13.8 us (22%)
  Pallas kernels  10.1 us (16%)
  local copies, waits for them, and re-layouts  1.83 us (3%)
    ppermute x15, waiting for transfers between devices, move(): return lax.ppermute(a, ('owner', 'split'), pairs)  22.6 us
    ppermute x15, starting transfers between devices, move(): return lax.ppermute(a, ('owner', 'split'), pairs)  13.8 us
    pallas_call x5, Pallas kernels, score(): pl.pallas_call(lambda *refs: score_kernel(docs, hot, names, given, made,...  6.08 us
    pallas_call x1, Pallas kernels, prep(): pl.pallas_call(lambda *refs: prep_kernel(hot, *refs), out_shape=(shape((r...  3.56 us
  transfers between devices with their start and end apart: 15, of which 4 were waited for; matrix products, arithmetic and copies ran while one was open for 2% of the time, Pallas kernels for 8%

profile of v11, /device:TPU:0, one launch (start us, length us, event | category | flops | bytes accessed | tf_op | source)
XLA Modules:
  0.0 63.6 jit_solution(1651480081383549986)
XLA Ops:
  6.5 0.1 pad_add_fusion.refs_0_
  6.6 3.6 %prep.1 = (bf16[336,768]{1,0:T(8,128)(2,1)S(1)}, bf16[336,768]{1,0:T(8,128)(2,1)S(1)}, s32[1,512]{1,0:T(1,128)S(1)}) custom-call(s32[3]{0:T(128)S(1)} %pad_add_fusion.refs_0_, s32[1,512]{1,0:T(1,128)} %bitcast.38, bf16[512,1024]{1,0:T(8,128)(2,1)} %refs_2_.1, bf16[1024,768]{1,0:T(8,128)(2,1)} %refs_3_.1), custom_call_target="tpu_custom_call" | custom-call | tf_op jit(solution)/shard_map/prep/pallas_call | solution.py:195
  10.2 0.5 collective-permute-start.1
  10.7 2.6 %collective-permute-start = (bf16[336,768]{1,0:T(8,128)(2,1)S(1)}, bf16[336,768]{1,0:T(8,128)(2,1)S(1)}, u32[]{:S(2)}, u32[]{:S(2)}) collective-permute-start(bf16[336,768]{1,0:T(8,128)(2,1)S(1)} %get-tuple-element.218.refs_1_), channel_id=1, source_target_pairs={{0,2},{1,3},{2,0},{3,1},{4,6},{5,7},{6,4},{7,5},{8,10},{9,11},{10,... | collective-permute-start | bytes 1548296 | tf_op jit(solution)/shard_map/ppermute | solution.py:392
  13.3 1.6 %collective-permute-start.4 = (bf16[336,768]{1,0:T(8,128)(2,1)S(1)}, bf16[336,768]{1,0:T(8,128)(2,1)S(1)}, u32[]{:S(2)}, u32[]{:S(2)}) collective-permute-start(bf16[336,768]{1,0:T(8,128)(2,1)S(1)} %get-tuple-element.220), channel_id=1, source_target_pairs={{0,4},{1,5},{2,6},{3,7},{4,0},{5,1},{6,2},{7,3},{8,12},{9,13},{10,... | collective-permute-start | bytes 1548296 | tf_op jit(solution)/shard_map/ppermute | solution.py:392
  14.9 1.4 %own.1 = (f32[4,1,640]{2,1,0:T(1,128)S(1)}, f32[4,1,640]{2,1,0:T(1,128)S(1)}, f32[1,1,640]{2,1,0:T(1,128)S(1)}, f32[1,1,640]{2,1,0:T(1,128)S(1)}, bf16[768,640]{1,0:T(8,128)(2,1)S(1)}, /*index=5*/f32[8,640]{1,0:T(8,128)S(1)}) custom-call(s32[3]{0:T(128)S(1)} %pad_add_fusion.refs_0_, bf16[336,768]{1,0:T(8,128)(2,1)S(1)} %get-tuple-element.218.refs_1_, ...), custom_call_target="tpu_custom_call" | custom-call | flops 8589934592 | bytes 1024 | tf_op jit(solution)/shard_map/own/pallas_call | solution.py:339
  16.3 10.8 %collective-permute-done.4.refs_1_.refs_3_ = bf16[336,768]{1,0:T(8,128)(2,1)S(1)} collective-permute-done((bf16[336,768]{1,0:T(8,128)(2,1)S(1)}, bf16[336,768]{1,0:T(8,128)(2,1)S(1)}, u32[]{:S(2)}, u32[]{:S(2)}) %collective-permute-start.4) | collective-permute-done | bytes 516128 | tf_op jit(solution)/shard_map/ppermute | solution.py:392
  27.1 2.6 %collective-permute-start.3 = (bf16[336,768]{1,0:T(8,128)(2,1)S(1)}, bf16[336,768]{1,0:T(8,128)(2,1)S(1)}, u32[]{:S(2)}, u32[]{:S(2)}) collective-permute-start(bf16[336,768]{1,0:T(8,128)(2,1)S(1)} %get-tuple-element.218.refs_1_), channel_id=1, source_target_pairs={{0,8},{1,9},{2,10},{3,11},{4,0},{5,1},{6,2},{7,3},{8,12},{9,13},{1... | collective-permute-start | bytes 1548296 | tf_op jit(solution)/shard_map/ppermute | solution.py:392
  29.7 0.5 collective-permute-start.5
  30.2 0.0 collective-permute-done.refs_1_
  30.2 0.0 collective-permute-done.2.refs_3_.refs_4_.refs_1_
  30.2 0.0 collective-permute-start.6
  30.2 1.1 %pair.1 = (f32[4,1,640]{2,1,0:T(1,128)S(1)}, f32[4,1,640]{2,1,0:T(1,128)S(1)}, f32[1,1,640]{2,1,0:T(1,128)S(1)}, f32[1,1,640]{2,1,0:T(1,128)S(1)}, bf16[768,640]{1,0:T(8,128)(2,1)S(1)}, /*index=5*/f32[8,640]{1,0:T(8,128)S(1)}) custom-call(s32[3]{0:T(128)S(1)} %pad_add_fusion.refs_0_, bf16[336,768]{1,0:T(8,128)(2,1)S(1)} %collective-permute-done.4.refs_1_.refs_3_, ...), custom_call_target="tpu_custom_call" | custom-call | flops 8589934592 | bytes 1024 | tf_op jit(solution)/shard_map/pair/pallas_call | solution.py:339
  31.3 0.8 %collective-permute-done.6.refs_2_ = bf16[336,768]{1,0:T(8,128)(2,1)S(1)} collective-permute-done((bf16[336,768]{1,0:T(8,128)(2,1)S(1)}, bf16[336,768]{1,0:T(8,128)(2,1)S(1)}, u32[]{:S(2)}, u32[]{:S(2)}) %collective-permute-start.6) | collective-permute-done | bytes 516128 | tf_op jit(solution)/shard_map/ppermute | solution.py:392
  32.1 1.8 %row.1 = (f32[4,1,640]{2,1,0:T(1,128)S(1)}, f32[4,1,640]{2,1,0:T(1,128)S(1)}, f32[1,1,640]{2,1,0:T(1,128)S(1)}, f32[1,1,640]{2,1,0:T(1,128)S(1)}, bf16[768,640]{1,0:T(8,128)(2,1)S(1)}, /*index=5*/f32[8,640]{1,0:T(8,128)S(1)}) custom-call(s32[3]{0:T(128)S(1)} %pad_add_fusion.refs_0_, bf16[336,768]{1,0:T(8,128)(2,1)S(1)} %collective-permute-done.refs_1_, ...), custom_call_target="tpu_custom_call" | custom-call | flops 1 | bytes 1024 | tf_op jit(solution)/shard_map/row/pallas_call | solution.py:339
  33.9 9.7 %collective-permute-done.5.refs_3_ = bf16[336,768]{1,0:T(8,128)(2,1)S(1)} collective-permute-done((bf16[336,768]{1,0:T(8,128)(2,1)S(1)}, bf16[336,768]{1,0:T(8,128)(2,1)S(1)}, u32[]{:S(2)}, u32[]{:S(2)}) %collective-permute-start.5) | collective-permute-done | bytes 516128 | tf_op jit(solution)/shard_map/ppermute | solution.py:392
  43.6 0.6 %far.1 = (f32[4,1,640]{2,1,0:T(1,128)S(1)}, f32[4,1,640]{2,1,0:T(1,128)S(1)}, f32[1,1,640]{2,1,0:T(1,128)S(1)}, f32[1,1,640]{2,1,0:T(1,128)S(1)}) custom-call(s32[3]{0:T(128)S(1)} %pad_add_fusion.refs_0_, bf16[336,768]{1,0:T(8,128)(2,1)S(1)} %collective-permute-done.3.refs_1_.refs_2_, bf16[768,640]{1,0:T(8,128)(2,1)S(1)} %get-tuple-element.226.refs_4_.refs_5_.refs_2_, ...), custom_call_target="tpu_custom_call" | custom-call | flops 1 | bytes 1024 | tf_op jit(solution)/shard_map/far/pallas_call | solution.py:339
  44.2 0.0 copy-start.2
  44.3 0.0 copy-start.4
  44.3 1.2 %collective-permute-done.8.refs_4_ = bf16[336,768]{1,0:T(8,128)(2,1)S(1)} collective-permute-done((bf16[336,768]{1,0:T(8,128)(2,1)S(1)}, bf16[336,768]{1,0:T(8,128)(2,1)S(1)}, u32[]{:S(2)}, u32[]{:S(2)}) %collective-permute-start.8) | collective-permute-done | bytes 516128 | tf_op jit(solution)/shard_map/ppermute | solution.py:392
  45.5 1.2 %last.1 = (f32[4,1,640]{2,1,0:T(1,128)S(1)}, f32[4,1,640]{2,1,0:T(1,128)S(1)}, f32[1,1,640]{2,1,0:T(1,128)S(1)}, f32[1,1,640]{2,1,0:T(1,128)S(1)}) custom-call(s32[3]{0:T(128)S(1)} %pad_add_fusion.refs_0_, bf16[336,768]{1,0:T(8,128)(2,1)S(1)} %collective-permute-done.2.refs_3_.refs_4_.refs_1_, bf16[336,768]{1,0:T(8,128)(2,1)S(1)} %collective-permute-done.3.refs_1_.refs_2_, ...), custom_call_target="tpu_custom_call" | custom-call | flops 1 | bytes 1024 | tf_op jit(solution)/shard_map/last/pallas_call | solution.py:339
  46.7 0.1 collective-permute-start.10
  46.8 2.3 %collective-permute-start.9 = (f32[1,1,640]{2,1,0:T(1,128)S(1)}, f32[1,1,640]{2,1,0:T(1,128)S(1)}, u32[]{:S(2)}, u32[]{:S(2)}) collective-permute-start(f32[1,1,640]{2,1,0:T(1,128)S(1)} %get-tuple-element.248), channel_id=1, source_target_pairs={{0,8},{1,9},{2,10},{3,11},{4,12},{5,13},{6,14},{7,15},{8,0},{9,1},... | collective-permute-start | bytes 7688 | tf_op jit(solution)/shard_map/ppermute | solution.py:392
  49.2 0.9 %collective-permute-start.14 = (f32[1,1,640]{2,1,0:T(1,128)S(1)}, f32[1,1,640]{2,1,0:T(1,128)S(1)}, u32[]{:S(2)}, u32[]{:S(2)}) collective-permute-start(f32[1,1,640]{2,1,0:T(1,128)S(1)} %get-tuple-element.330), channel_id=1, source_target_pairs={{0,6},{1,7},{2,4},{3,5},{4,2},{5,3},{6,0},{7,1},{8,14},{9,15},{10,... | collective-permute-start | bytes 7688 | tf_op jit(solution)/shard_map/ppermute | solution.py:392
  50.1 1.5 %collective-permute-start.13 = (f32[1,1,640]{2,1,0:T(1,128)S(1)}, f32[1,1,640]{2,1,0:T(1,128)S(1)}, u32[]{:S(2)}, u32[]{:S(2)}) collective-permute-start(f32[1,1,640]{2,1,0:T(1,128)S(1)} %get-tuple-element.331), channel_id=1, source_target_pairs={{0,2},{1,3},{2,0},{3,1},{4,6},{5,7},{6,4},{7,5},{8,10},{9,11},{10,... | collective-permute-start | bytes 7688 | tf_op jit(solution)/shard_map/ppermute | solution.py:392
  51.6 1.1 %collective-permute-start.12 = (f32[1,1,640]{2,1,0:T(1,128)S(1)}, f32[1,1,640]{2,1,0:T(1,128)S(1)}, u32[]{:S(2)}, u32[]{:S(2)}) collective-permute-start(f32[1,1,640]{2,1,0:T(1,128)S(1)} %get-tuple-element.332), channel_id=1, source_target_pairs={{0,4},{1,5},{2,6},{3,7},{4,0},{5,1},{6,2},{7,3},{8,12},{9,13},{10,... | collective-permute-start | bytes 7688 | tf_op jit(solution)/shard_map/ppermute | solution.py:392
  52.7 0.6 slice.45
  53.3 0.7 %slice.46 = f32[1,1,1]{2,1,0:T(1,128)} slice(f32[1,1,640]{2,1,0:T(1,128)S(1)} %collective-permute-done.9), slice={[0:1], [0:1], [576:577]} | slice | bytes 8 | tf_op jit(solution)/shard_map/slice | solution.py:444
  55.4 0.8 %conditional.1 = (f32[512]{0:T(512)S(1)}) conditional(s32[]{:T(128)} %bitcast.12, (f32[4,1,640]{2,1,0:T(1,128)S(1)}, f32[4,1,640]{2,1,0:T(1,128)S(1)}, s32[1,512]{1,0:T(1,128)S(1)}, f32[1,1,640]{2,1,0:T(1,128)S(1)}, f32[1,1,640]{2,1,0:T(1,128)S(1)}, /*index=5*/f32[1,1,640]{2,1,0:T(1,128)S(1)}, f32[1,1,640]{2,1,0:T(1,128)S(1)}, ...), branch_computations={%region_0.1_spmd, %region_1.13_spmd} | conditional | flops 4454147584 | bytes 57829452 | solution.py:443
  55.4 0.5 finish.1
  56.2 0.0 copy-start.5
  56.2 0.6 copy-done.5
  (17 shorter events, 0.1 us)
Async XLA Ops:
  10.2 4.7 %collective-permute-start.1 = (bf16[336,768]{1,0:T(8,128)(2,1)S(1)}, bf16[336,768]{1,0:T(8,128)(2,1)S(1)}, u32[]{:S(2)}, u32[]{:S(2)}) collective-permute-start(bf16[336,768]{1,0:T(8,128)(2,1)S(1)} %get-tuple-element.218.refs_1_), channel_id=1, source_target_pairs={{0,1},{1,0},{2,3},{3,2},{4,5},{5,4},{6,7},{7,6},{8,9},{9,8},{10,11... | collective-permute-start | bytes 1548296 | tf_op jit(solution)/shard_map/ppermute | solution.py:392
  10.7 19.5 %collective-permute-start = (bf16[336,768]{1,0:T(8,128)(2,1)S(1)}, bf16[336,768]{1,0:T(8,128)(2,1)S(1)}, u32[]{:S(2)}, u32[]{:S(2)}) collective-permute-start(bf16[336,768]{1,0:T(8,128)(2,1)S(1)} %get-tuple-element.218.refs_1_), channel_id=1, source_target_pairs={{0,2},{1,3},{2,0},{3,1},{4,6},{5,7},{6,4},{7,5},{8,10},{9,11},{10,... | collective-permute-start | bytes 1548296 | tf_op jit(solution)/shard_map/ppermute | solution.py:392
  13.3 13.8 %collective-permute-start.4 = (bf16[336,768]{1,0:T(8,128)(2,1)S(1)}, bf16[336,768]{1,0:T(8,128)(2,1)S(1)}, u32[]{:S(2)}, u32[]{:S(2)}) collective-permute-start(bf16[336,768]{1,0:T(8,128)(2,1)S(1)} %get-tuple-element.220), channel_id=1, source_target_pairs={{0,4},{1,5},{2,6},{3,7},{4,0},{5,1},{6,2},{7,3},{8,12},{9,13},{10,... | collective-permute-start | bytes 1548296 | tf_op jit(solution)/shard_map/ppermute | solution.py:392
  14.9 15.4 %collective-permute-start.2 = (bf16[336,768]{1,0:T(8,128)(2,1)S(1)}, bf16[336,768]{1,0:T(8,128)(2,1)S(1)}, u32[]{:S(2)}, u32[]{:S(2)}) collective-permute-start(bf16[336,768]{1,0:T(8,128)(2,1)S(1)} %get-tuple-element.220), channel_id=1, source_target_pairs={{0,1},{1,0},{2,3},{3,2},{4,8},{5,9},{6,10},{7,11},{8,4},{9,5},{10,... | collective-permute-start | bytes 1548296 | tf_op jit(solution)/shard_map/ppermute | solution.py:392
  27.1 3.1 %collective-permute-start.7 = (bf16[336,768]{1,0:T(8,128)(2,1)S(1)}, bf16[336,768]{1,0:T(8,128)(2,1)S(1)}, u32[]{:S(2)}, u32[]{:S(2)}) collective-permute-start(bf16[336,768]{1,0:T(8,128)(2,1)S(1)} %collective-permute-done.4.refs_1_.refs_3_), channel_id=1, source_target_pairs={{0,1},{1,0},{2,3},{3,2},{4,5},{5,4},{6,7},{7,6},{8,9},{9,8},{10,11... | collective-permute-start | bytes 1548296 | tf_op jit(solution)/shard_map/ppermute | solution.py:392
  27.1 16.5 %collective-permute-start.3 = (bf16[336,768]{1,0:T(8,128)(2,1)S(1)}, bf16[336,768]{1,0:T(8,128)(2,1)S(1)}, u32[]{:S(2)}, u32[]{:S(2)}) collective-permute-start(bf16[336,768]{1,0:T(8,128)(2,1)S(1)} %get-tuple-element.218.refs_1_), channel_id=1, source_target_pairs={{0,8},{1,9},{2,10},{3,11},{4,0},{5,1},{6,2},{7,3},{8,12},{9,13},{1... | collective-permute-start | bytes 1548296 | tf_op jit(solution)/shard_map/ppermute | solution.py:392
  29.7 13.9 %collective-permute-start.5 = (bf16[336,768]{1,0:T(8,128)(2,1)S(1)}, bf16[336,768]{1,0:T(8,128)(2,1)S(1)}, u32[]{:S(2)}, u32[]{:S(2)}) collective-permute-start(bf16[336,768]{1,0:T(8,128)(2,1)S(1)} %collective-permute-done.4.refs_1_.refs_3_), channel_id=1, source_target_pairs={{0,2},{1,3},{2,0},{3,1},{4,6},{5,7},{6,4},{7,5},{8,10},{9,11},{10,... | collective-permute-start | bytes 1548296 | tf_op jit(solution)/shard_map/ppermute | solution.py:392
  30.2 1.9 %collective-permute-start.6 = (bf16[336,768]{1,0:T(8,128)(2,1)S(1)}, bf16[336,768]{1,0:T(8,128)(2,1)S(1)}, u32[]{:S(2)}, u32[]{:S(2)}) collective-permute-start(bf16[336,768]{1,0:T(8,128)(2,1)S(1)} %collective-permute-done.refs_1_), channel_id=1, source_target_pairs={{0,1},{1,0},{2,3},{3,2},{4,5},{5,4},{6,7},{7,6},{8,9},{9,8},{10,11... | collective-permute-start | bytes 1548296 | tf_op jit(solution)/shard_map/ppermute | solution.py:392
  43.6 1.9 %collective-permute-start.8 = (bf16[336,768]{1,0:T(8,128)(2,1)S(1)}, bf16[336,768]{1,0:T(8,128)(2,1)S(1)}, u32[]{:S(2)}, u32[]{:S(2)}) collective-permute-start(bf16[336,768]{1,0:T(8,128)(2,1)S(1)} %collective-permute-done.5.refs_3_), channel_id=1, source_target_pairs={{0,1},{1,0},{2,3},{3,2},{4,5},{5,4},{6,7},{7,6},{8,9},{9,8},{10,11... | collective-permute-start | bytes 1548296 | tf_op jit(solution)/shard_map/ppermute | solution.py:392
  44.2 11.1 %copy-start.2 = (bf16[512,1024]{1,0:T(8,128)(2,1)S(1)}, bf16[512,1024]{1,0:T(8,128)(2,1)}, u32[]{:S(2)}) copy-start(bf16[512,1024]{1,0:T(8,128)(2,1)} %refs_2_.1) | copy-start | bytes 3145732
  44.3 11.1 %copy-start.4 = (s32[512]{0:T(512)S(1)}, s32[512]{0:T(512)}, u32[]{:S(2)}) copy-start(s32[512]{0:T(512)} %param.9) | copy-start | bytes 6148
  46.7 2.5 %collective-permute-start.10 = (f32[4,1,640]{2,1,0:T(1,128)S(1)}, f32[4,1,640]{2,1,0:T(1,128)S(1)}, u32[]{:S(2)}, u32[]{:S(2)}) collective-permute-start(f32[4,1,640]{2,1,0:T(1,128)S(1)} %get-tuple-element.250), channel_id=1, source_target_pairs={{0,1},{1,0},{2,3},{3,2},{4,5},{5,4},{6,7},{7,6},{8,9},{9,8},{10,11... | collective-permute-start | bytes 30728 | tf_op jit(solution)/shard_map/ppermute | solution.py:392
  46.8 6.5 %collective-permute-start.9 = (f32[1,1,640]{2,1,0:T(1,128)S(1)}, f32[1,1,640]{2,1,0:T(1,128)S(1)}, u32[]{:S(2)}, u32[]{:S(2)}) collective-permute-start(f32[1,1,640]{2,1,0:T(1,128)S(1)} %get-tuple-element.248), channel_id=1, source_target_pairs={{0,8},{1,9},{2,10},{3,11},{4,12},{5,13},{6,14},{7,15},{8,0},{9,1},... | collective-permute-start | bytes 7688 | tf_op jit(solution)/shard_map/ppermute | solution.py:392
  49.2 6.2 %collective-permute-start.14 = (f32[1,1,640]{2,1,0:T(1,128)S(1)}, f32[1,1,640]{2,1,0:T(1,128)S(1)}, u32[]{:S(2)}, u32[]{:S(2)}) collective-permute-start(f32[1,1,640]{2,1,0:T(1,128)S(1)} %get-tuple-element.330), channel_id=1, source_target_pairs={{0,6},{1,7},{2,4},{3,5},{4,2},{5,3},{6,0},{7,1},{8,14},{9,15},{10,... | collective-permute-start | bytes 7688 | tf_op jit(solution)/shard_map/ppermute | solution.py:392
  50.1 5.2 %collective-permute-start.13 = (f32[1,1,640]{2,1,0:T(1,128)S(1)}, f32[1,1,640]{2,1,0:T(1,128)S(1)}, u32[]{:S(2)}, u32[]{:S(2)}) collective-permute-start(f32[1,1,640]{2,1,0:T(1,128)S(1)} %get-tuple-element.331), channel_id=1, source_target_pairs={{0,2},{1,3},{2,0},{3,1},{4,6},{5,7},{6,4},{7,5},{8,10},{9,11},{10,... | collective-permute-start | bytes 7688 | tf_op jit(solution)/shard_map/ppermute | solution.py:392
  51.6 3.7 %collective-permute-start.12 = (f32[1,1,640]{2,1,0:T(1,128)S(1)}, f32[1,1,640]{2,1,0:T(1,128)S(1)}, u32[]{:S(2)}, u32[]{:S(2)}) collective-permute-start(f32[1,1,640]{2,1,0:T(1,128)S(1)} %get-tuple-element.332), channel_id=1, source_target_pairs={{0,4},{1,5},{2,6},{3,7},{4,0},{5,1},{6,2},{7,3},{8,12},{9,13},{10,... | collective-permute-start | bytes 7688 | tf_op jit(solution)/shard_map/ppermute | solution.py:392
  52.7 2.6 %collective-permute-start.11 = (f32[1,1,640]{2,1,0:T(1,128)S(1)}, f32[1,1,640]{2,1,0:T(1,128)S(1)}, u32[]{:S(2)}, u32[]{:S(2)}) collective-permute-start(f32[1,1,640]{2,1,0:T(1,128)S(1)} %get-tuple-element.254), channel_id=1, source_target_pairs={{0,1},{1,0},{2,3},{3,2},{4,8},{5,9},{6,10},{7,11},{8,4},{9,5},{10,... | collective-permute-start | bytes 7688 | tf_op jit(solution)/shard_map/ppermute | solution.py:392
  56.2 0.6 copy-start.5

commit v12 on v11

--- a/solution.py
+++ b/solution.py
@@ -112,7 +112,7 @@
     return -(-n // m) * m
 
 
-META = 16
+META = 8
 
 
 def layout(docs, hot):
@@ -370,6 +370,20 @@
     )(slot, *sums)
 
 
+def decide_kernel(flag, mine_ref, theirs_ref, out_ref):
+    out_ref[0] = (jnp.sum(mine_ref[0][:, flag:flag + 1] + theirs_ref[0][:, flag:flag + 1]) > 0.0).astype(jnp.int32)
+
+
+def decide(flag, mine, theirs):
+    return pl.pallas_call(
+        lambda *refs: decide_kernel(flag, *refs),
+        out_shape=jax.ShapeDtypeStruct((1,), jnp.int32),
+        out_specs=pl.BlockSpec(memory_space=pltpu.SMEM),
+        compiler_params=pltpu.CompilerParams(vmem_limit_bytes=2 * 2**20),
+        name="decide",
+    )(mine, theirs)
+
+
 def meeting_plan(states, proj_weight, cluster_of):
     owners = lax.axis_size("owner")
     columns = owners // ROWS
@@ -400,8 +414,8 @@
     blocks, pairs, sums = {OWN: same}, {}, ()
     blocks[CORE] = move(same, STAY, core=1)
     blocks[PAIR] = move(other, OUTER)
-    blocks[ROW] = move(same, STAY, row=1)
-    blocks[CORE], other = lax.optimization_barrier((blocks[CORE], other))
+    blocks[CORE], still_same, other = lax.optimization_barrier((blocks[CORE], same, other))
+    blocks[ROW] = move(still_same, STAY, row=1)
     blocks[NEXT] = move(other, MIDDLE)
     sums, pairs = meet("own", HERE, [((OWN,), HERE, False, None), ((CORE,), HERE, False, "core0")], weight=2**33)
 
@@ -441,7 +455,7 @@
         move(pair, OUTER), move(row, STAY, row=1), move(pair_row, OUTER, row=1),
     ]
     return lax.cond(
-        (to_far + from_far)[0, 0, flag] > 0.0,
+        decide(flag, to_far, from_far)[0] > 0,
         lambda states, proj_weight, cluster_of, *_: owner_plan(states, proj_weight, cluster_of),
         lambda states, proj_weight, cluster_of, slot, *home: finish(slot, home).reshape(docs),
         states, proj_weight, cluster_of, slot, *home,

time: 63.8 us -> 61.8 us (0.969)
  waiting for transfers between devices: 22.6 us -> 20.6 us
  starting transfers between devices: 13.8 us -> 15.2 us
  local copies, waits for them, and re-layouts: 1.83 us -> 0.59 us
  between operations: 14.8 us -> 14.1 us
    ppermute x15, waiting for transfers between devices: 22.6 us -> 20.6 us  [move(): return lax.ppermute(a, ('owner', 'split'), pairs)]
    ppermute x15, starting transfers between devices: 13.8 us -> 15.2 us  [move(): return lax.ppermute(a, ('owner', 'split'), pairs)]
    slice x2 -> x0, local copies, waits for them, and re-layouts: 1.24 us -> none  [meeting_plan(): (to_far + from_far)[0, 0, flag] > 0.0]
  transfers between devices with their start and end apart: 15 -> 15, of which waited for: 4 -> 6; matrix products, arithmetic and copies ran while one was open for 2% -> 0% of each run, Pallas kernels for 8% -> 9%
where the time goes in v12:
time: 61.8 us; the launch traced here: 61.7 us
  waiting for transfers between devices  20.6 us (33%)
  starting transfers between devices  15.2 us (25%)
  between operations  14.1 us (23%)
  Pallas kernels  10.7 us (17%)
    ppermute x15, waiting for transfers between devices, move(): return lax.ppermute(a, ('owner', 'split'), pairs)  20.6 us
    ppermute x15, starting transfers between devices, move(): return lax.ppermute(a, ('owner', 'split'), pairs)  15.2 us
    pallas_call x5, Pallas kernels, score(): pl.pallas_call(lambda *refs: score_kernel(docs, hot, names, given, made,...  6.09 us
    pallas_call x1, Pallas kernels, prep(): pl.pallas_call(lambda *refs: prep_kernel(hot, *refs), out_shape=(shape((r...  3.56 us
  transfers between devices with their start and end apart: 15, of which 6 were waited for; matrix products, arithmetic and copies ran while one was open for 0% of the time, Pallas kernels for 9%

profile of v12, /device:TPU:0, one launch (start us, length us, event | category | flops | bytes accessed | tf_op | source)
XLA Modules:
  0.0 61.7 jit_solution(15286990671441375876)
XLA Ops:
  6.5 0.1 pad_add_fusion.refs_0_
  6.6 3.6 %prep.1 = (bf16[328,768]{1,0:T(8,128)(2,1)S(1)}, bf16[328,768]{1,0:T(8,128)(2,1)S(1)}, s32[1,512]{1,0:T(1,128)S(1)}) custom-call(s32[3]{0:T(128)S(1)} %pad_add_fusion.refs_0_, s32[1,512]{1,0:T(1,128)} %bitcast.38, bf16[512,1024]{1,0:T(8,128)(2,1)} %refs_2_.1, bf16[1024,768]{1,0:T(8,128)(2,1)} %refs_3_.1), custom_call_target="tpu_custom_call" | custom-call | tf_op jit(solution)/shard_map/prep/pallas_call | solution.py:195
  10.2 0.5 collective-permute-start
  10.7 2.6 %collective-permute-start.4 = (bf16[328,768]{1,0:T(8,128)(2,1)S(1)}, bf16[328,768]{1,0:T(8,128)(2,1)S(1)}, u32[]{:S(2)}, u32[]{:S(2)}) collective-permute-start(bf16[328,768]{1,0:T(8,128)(2,1)S(1)} %get-tuple-element.222), channel_id=1, source_target_pairs={{0,4},{1,5},{2,6},{3,7},{4,0},{5,1},{6,2},{7,3},{8,12},{9,13},{10,... | collective-permute-start | bytes 1511432 | tf_op jit(solution)/shard_map/ppermute | solution.py:406
  13.3 1.7 %collective-permute-start.1 = (bf16[328,768]{1,0:T(8,128)(2,1)S(1)}, bf16[328,768]{1,0:T(8,128)(2,1)S(1)}, u32[]{:S(2)}, u32[]{:S(2)}) collective-permute-start(bf16[328,768]{1,0:T(8,128)(2,1)S(1)} %get-tuple-element.221.refs_1_), channel_id=1, source_target_pairs={{0,2},{1,3},{2,0},{3,1},{4,6},{5,7},{6,4},{7,5},{8,10},{9,11},{10,... | collective-permute-start | bytes 1511432 | tf_op jit(solution)/shard_map/ppermute | solution.py:406
  15.1 0.0 collective-permute-start.2
  15.1 1.4 %own.1 = (f32[4,1,640]{2,1,0:T(1,128)S(1)}, f32[4,1,640]{2,1,0:T(1,128)S(1)}, f32[1,1,640]{2,1,0:T(1,128)S(1)}, f32[1,1,640]{2,1,0:T(1,128)S(1)}, bf16[768,640]{1,0:T(8,128)(2,1)S(1)}, /*index=5*/f32[8,640]{1,0:T(8,128)S(1)}) custom-call(s32[3]{0:T(128)S(1)} %pad_add_fusion.refs_0_, bf16[328,768]{1,0:T(8,128)(2,1)S(1)} %get-tuple-element.221.refs_1_, ...), custom_call_target="tpu_custom_call" | custom-call | flops 8589934592 | bytes 1024 | tf_op jit(solution)/shard_map/own/pallas_call | solution.py:339
  16.5 8.9 %collective-permute-done.4.refs_1_.refs_3_ = bf16[328,768]{1,0:T(8,128)(2,1)S(1)} collective-permute-done((bf16[328,768]{1,0:T(8,128)(2,1)S(1)}, bf16[328,768]{1,0:T(8,128)(2,1)S(1)}, u32[]{:S(2)}, u32[]{:S(2)}) %collective-permute-start.4) | collective-permute-done | bytes 503840 | tf_op jit(solution)/shard_map/ppermute | solution.py:406
  25.4 2.8 %collective-permute-start.3 = (bf16[328,768]{1,0:T(8,128)(2,1)S(1)}, bf16[328,768]{1,0:T(8,128)(2,1)S(1)}, u32[]{:S(2)}, u32[]{:S(2)}) collective-permute-start(bf16[328,768]{1,0:T(8,128)(2,1)S(1)} %get-tuple-element.221.refs_1_), channel_id=1, source_target_pairs={{0,8},{1,9},{2,10},{3,11},{4,0},{5,1},{6,2},{7,3},{8,12},{9,13},{1... | collective-permute-start | bytes 1511432 | tf_op jit(solution)/shard_map/ppermute | solution.py:406
  28.2 1.5 %collective-permute-start.5 = (bf16[328,768]{1,0:T(8,128)(2,1)S(1)}, bf16[328,768]{1,0:T(8,128)(2,1)S(1)}, u32[]{:S(2)}, u32[]{:S(2)}) collective-permute-start(bf16[328,768]{1,0:T(8,128)(2,1)S(1)} %collective-permute-done.4.refs_1_.refs_3_), channel_id=1, source_target_pairs={{0,2},{1,3},{2,0},{3,1},{4,6},{5,7},{6,4},{7,5},{8,10},{9,11},{10,... | collective-permute-start | bytes 1511432 | tf_op jit(solution)/shard_map/ppermute | solution.py:406
  29.7 1.1 %pair.1 = (f32[4,1,640]{2,1,0:T(1,128)S(1)}, f32[4,1,640]{2,1,0:T(1,128)S(1)}, f32[1,1,640]{2,1,0:T(1,128)S(1)}, f32[1,1,640]{2,1,0:T(1,128)S(1)}, bf16[768,640]{1,0:T(8,128)(2,1)S(1)}, /*index=5*/f32[8,640]{1,0:T(8,128)S(1)}) custom-call(s32[3]{0:T(128)S(1)} %pad_add_fusion.refs_0_, bf16[328,768]{1,0:T(8,128)(2,1)S(1)} %collective-permute-done.4.refs_1_.refs_3_, ...), custom_call_target="tpu_custom_call" | custom-call | flops 8589934592 | bytes 1024 | tf_op jit(solution)/shard_map/pair/pallas_call | solution.py:339
  30.8 0.8 %collective-permute-done.6.refs_2_ = bf16[328,768]{1,0:T(8,128)(2,1)S(1)} collective-permute-done((bf16[328,768]{1,0:T(8,128)(2,1)S(1)}, bf16[328,768]{1,0:T(8,128)(2,1)S(1)}, u32[]{:S(2)}, u32[]{:S(2)}) %collective-permute-start.6) | collective-permute-done | bytes 503840 | tf_op jit(solution)/shard_map/ppermute | solution.py:406
  31.6 1.8 %row.1 = (f32[4,1,640]{2,1,0:T(1,128)S(1)}, f32[4,1,640]{2,1,0:T(1,128)S(1)}, f32[1,1,640]{2,1,0:T(1,128)S(1)}, f32[1,1,640]{2,1,0:T(1,128)S(1)}, bf16[768,640]{1,0:T(8,128)(2,1)S(1)}, /*index=5*/f32[8,640]{1,0:T(8,128)S(1)}) custom-call(s32[3]{0:T(128)S(1)} %pad_add_fusion.refs_0_, bf16[328,768]{1,0:T(8,128)(2,1)S(1)} %collective-permute-done.1.refs_1_, ...), custom_call_target="tpu_custom_call" | custom-call | flops 1 | bytes 1024 | tf_op jit(solution)/shard_map/row/pallas_call | solution.py:339
  33.4 8.4 %collective-permute-done.5.refs_3_ = bf16[328,768]{1,0:T(8,128)(2,1)S(1)} collective-permute-done((bf16[328,768]{1,0:T(8,128)(2,1)S(1)}, bf16[328,768]{1,0:T(8,128)(2,1)S(1)}, u32[]{:S(2)}, u32[]{:S(2)}) %collective-permute-start.5) | collective-permute-done | bytes 503840 | tf_op jit(solution)/shard_map/ppermute | solution.py:406
  41.8 0.6 %far.1 = (f32[4,1,640]{2,1,0:T(1,128)S(1)}, f32[4,1,640]{2,1,0:T(1,128)S(1)}, f32[1,1,640]{2,1,0:T(1,128)S(1)}, f32[1,1,640]{2,1,0:T(1,128)S(1)}) custom-call(s32[3]{0:T(128)S(1)} %pad_add_fusion.refs_0_, bf16[328,768]{1,0:T(8,128)(2,1)S(1)} %collective-permute-done.3.refs_1_.refs_2_, bf16[768,640]{1,0:T(8,128)(2,1)S(1)} %get-tuple-element.228.refs_4_.refs_5_.refs_2_, ...), custom_call_target="tpu_custom_call" | custom-call | flops 1 | bytes 1024 | tf_op jit(solution)/shard_map/far/pallas_call | solution.py:339
  42.5 0.0 copy-start.2
  42.5 0.0 copy-start.3
  42.5 0.0 copy-start.5
  42.5 1.2 %collective-permute-done.8.refs_4_ = bf16[328,768]{1,0:T(8,128)(2,1)S(1)} collective-permute-done((bf16[328,768]{1,0:T(8,128)(2,1)S(1)}, bf16[328,768]{1,0:T(8,128)(2,1)S(1)}, u32[]{:S(2)}, u32[]{:S(2)}) %collective-permute-start.8) | collective-permute-done | bytes 503840 | tf_op jit(solution)/shard_map/ppermute | solution.py:406
  43.7 1.2 %last.1 = (f32[4,1,640]{2,1,0:T(1,128)S(1)}, f32[4,1,640]{2,1,0:T(1,128)S(1)}, f32[1,1,640]{2,1,0:T(1,128)S(1)}, f32[1,1,640]{2,1,0:T(1,128)S(1)}) custom-call(s32[3]{0:T(128)S(1)} %pad_add_fusion.refs_0_, bf16[328,768]{1,0:T(8,128)(2,1)S(1)} %collective-permute-done.2.refs_3_.refs_4_.refs_1_, bf16[328,768]{1,0:T(8,128)(2,1)S(1)} %collective-permute-done.3.refs_1_.refs_2_, ...), custom_call_target="tpu_custom_call" | custom-call | flops 1 | bytes 1024 | tf_op jit(solution)/shard_map/last/pallas_call | solution.py:339
  44.9 0.1 collective-permute-start.10
  45.1 2.3 %collective-permute-start.9 = (f32[1,1,640]{2,1,0:T(1,128)S(1)}, f32[1,1,640]{2,1,0:T(1,128)S(1)}, u32[]{:S(2)}, u32[]{:S(2)}) collective-permute-start(f32[1,1,640]{2,1,0:T(1,128)S(1)} %get-tuple-element.250.refs_0_), channel_id=1, source_target_pairs={{0,8},{1,9},{2,10},{3,11},{4,12},{5,13},{6,14},{7,15},{8,0},{9,1},... | collective-permute-start | bytes 7688 | tf_op jit(solution)/shard_map/ppermute | solution.py:406
  47.4 2.0 %collective-permute-start.14 = (f32[1,1,640]{2,1,0:T(1,128)S(1)}, f32[1,1,640]{2,1,0:T(1,128)S(1)}, u32[]{:S(2)}, u32[]{:S(2)}) collective-permute-start(f32[1,1,640]{2,1,0:T(1,128)S(1)} %get-tuple-element.332), channel_id=1, source_target_pairs={{0,6},{1,7},{2,4},{3,5},{4,2},{5,3},{6,0},{7,1},{8,14},{9,15},{10,... | collective-permute-start | bytes 7688 | tf_op jit(solution)/shard_map/ppermute | solution.py:406
  49.4 0.5 collective-permute-start.13
  49.9 1.1 %collective-permute-start.12 = (f32[1,1,640]{2,1,0:T(1,128)S(1)}, f32[1,1,640]{2,1,0:T(1,128)S(1)}, u32[]{:S(2)}, u32[]{:S(2)}) collective-permute-start(f32[1,1,640]{2,1,0:T(1,128)S(1)} %get-tuple-element.334), channel_id=1, source_target_pairs={{0,4},{1,5},{2,6},{3,7},{4,0},{5,1},{6,2},{7,3},{8,12},{9,13},{10,... | collective-permute-start | bytes 7688 | tf_op jit(solution)/shard_map/ppermute | solution.py:406
  51.0 0.6 %decide.1 = s32[1]{0:T(128)} custom-call(f32[1,1,640]{2,1,0:T(1,128)S(1)} %get-tuple-element.250.refs_0_, f32[1,1,640]{2,1,0:T(1,128)S(1)} %collective-permute-done.9.refs_1_), custom_call_target="tpu_custom_call" | custom-call | tf_op jit(solution)/shard_map/decide/pallas_call | solution.py:378
  52.3 0.7 %collective-permute-done.13 = f32[1,1,640]{2,1,0:T(1,128)S(1)} collective-permute-done((f32[1,1,640]{2,1,0:T(1,128)S(1)}, f32[1,1,640]{2,1,0:T(1,128)S(1)}, u32[]{:S(2)}, u32[]{:S(2)}) %collective-permute-start.13) | collective-permute-done | bytes 2592 | tf_op jit(solution)/shard_map/ppermute | solution.py:406
  53.0 0.5 collective-permute-done.12
  53.5 0.8 %conditional.1 = (f32[512]{0:T(512)S(1)}) conditional(s32[]{:T(128)} %bitcast.12, (f32[4,1,640]{2,1,0:T(1,128)S(1)}, f32[4,1,640]{2,1,0:T(1,128)S(1)}, s32[1,512]{1,0:T(1,128)S(1)}, f32[1,1,640]{2,1,0:T(1,128)S(1)}, f32[1,1,640]{2,1,0:T(1,128)S(1)}, /*index=5*/f32[1,1,640]{2,1,0:T(1,128)S(1)}, f32[1,1,640]{2,1,0:T(1,128)S(1)}, ...), branch_computations={%region_0.1_spmd, %region_1.13_spmd} | conditional | flops 4454147584 | bytes 57829452 | solution.py:457
  53.5 0.5 finish.1
  54.3 0.0 copy-start.6
  54.3 0.6 copy-done.6
  (18 shorter events, 0.1 us)
Async XLA Ops:
  10.2 3.2 %collective-permute-start = (bf16[328,768]{1,0:T(8,128)(2,1)S(1)}, bf16[328,768]{1,0:T(8,128)(2,1)S(1)}, u32[]{:S(2)}, u32[]{:S(2)}) collective-permute-start(bf16[328,768]{1,0:T(8,128)(2,1)S(1)} %get-tuple-element.221.refs_1_), channel_id=1, source_target_pairs={{0,1},{1,0},{2,3},{3,2},{4,5},{5,4},{6,7},{7,6},{8,9},{9,8},{10,11... | collective-permute-start | bytes 1511432 | tf_op jit(solution)/shard_map/ppermute | solution.py:406
  10.7 14.7 %collective-permute-start.4 = (bf16[328,768]{1,0:T(8,128)(2,1)S(1)}, bf16[328,768]{1,0:T(8,128)(2,1)S(1)}, u32[]{:S(2)}, u32[]{:S(2)}) collective-permute-start(bf16[328,768]{1,0:T(8,128)(2,1)S(1)} %get-tuple-element.222), channel_id=1, source_target_pairs={{0,4},{1,5},{2,6},{3,7},{4,0},{5,1},{6,2},{7,3},{8,12},{9,13},{10,... | collective-permute-start | bytes 1511432 | tf_op jit(solution)/shard_map/ppermute | solution.py:406
  13.3 16.4 %collective-permute-start.1 = (bf16[328,768]{1,0:T(8,128)(2,1)S(1)}, bf16[328,768]{1,0:T(8,128)(2,1)S(1)}, u32[]{:S(2)}, u32[]{:S(2)}) collective-permute-start(bf16[328,768]{1,0:T(8,128)(2,1)S(1)} %get-tuple-element.221.refs_1_), channel_id=1, source_target_pairs={{0,2},{1,3},{2,0},{3,1},{4,6},{5,7},{6,4},{7,5},{8,10},{9,11},{10,... | collective-permute-start | bytes 1511432 | tf_op jit(solution)/shard_map/ppermute | solution.py:406
  15.1 14.6 %collective-permute-start.2 = (bf16[328,768]{1,0:T(8,128)(2,1)S(1)}, bf16[328,768]{1,0:T(8,128)(2,1)S(1)}, u32[]{:S(2)}, u32[]{:S(2)}) collective-permute-start(bf16[328,768]{1,0:T(8,128)(2,1)S(1)} %get-tuple-element.222), channel_id=1, source_target_pairs={{0,1},{1,0},{2,3},{3,2},{4,8},{5,9},{6,10},{7,11},{8,4},{9,5},{10,... | collective-permute-start | bytes 1511432 | tf_op jit(solution)/shard_map/ppermute | solution.py:406
  25.4 4.3 %collective-permute-start.7 = (bf16[328,768]{1,0:T(8,128)(2,1)S(1)}, bf16[328,768]{1,0:T(8,128)(2,1)S(1)}, u32[]{:S(2)}, u32[]{:S(2)}) collective-permute-start(bf16[328,768]{1,0:T(8,128)(2,1)S(1)} %collective-permute-done.4.refs_1_.refs_3_), channel_id=1, source_target_pairs={{0,1},{1,0},{2,3},{3,2},{4,5},{5,4},{6,7},{7,6},{8,9},{9,8},{10,11... | collective-permute-start | bytes 1511432 | tf_op jit(solution)/shard_map/ppermute | solution.py:406
  25.4 16.4 %collective-permute-start.3 = (bf16[328,768]{1,0:T(8,128)(2,1)S(1)}, bf16[328,768]{1,0:T(8,128)(2,1)S(1)}, u32[]{:S(2)}, u32[]{:S(2)}) collective-permute-start(bf16[328,768]{1,0:T(8,128)(2,1)S(1)} %get-tuple-element.221.refs_1_), channel_id=1, source_target_pairs={{0,8},{1,9},{2,10},{3,11},{4,0},{5,1},{6,2},{7,3},{8,12},{9,13},{1... | collective-permute-start | bytes 1511432 | tf_op jit(solution)/shard_map/ppermute | solution.py:406
  28.2 13.6 %collective-permute-start.5 = (bf16[328,768]{1,0:T(8,128)(2,1)S(1)}, bf16[328,768]{1,0:T(8,128)(2,1)S(1)}, u32[]{:S(2)}, u32[]{:S(2)}) collective-permute-start(bf16[328,768]{1,0:T(8,128)(2,1)S(1)} %collective-permute-done.4.refs_1_.refs_3_), channel_id=1, source_target_pairs={{0,2},{1,3},{2,0},{3,1},{4,6},{5,7},{6,4},{7,5},{8,10},{9,11},{10,... | collective-permute-start | bytes 1511432 | tf_op jit(solution)/shard_map/ppermute | solution.py:406
  29.7 1.9 %collective-permute-start.6 = (bf16[328,768]{1,0:T(8,128)(2,1)S(1)}, bf16[328,768]{1,0:T(8,128)(2,1)S(1)}, u32[]{:S(2)}, u32[]{:S(2)}) collective-permute-start(bf16[328,768]{1,0:T(8,128)(2,1)S(1)} %collective-permute-done.1.refs_1_), channel_id=1, source_target_pairs={{0,1},{1,0},{2,3},{3,2},{4,5},{5,4},{6,7},{7,6},{8,9},{9,8},{10,11... | collective-permute-start | bytes 1511432 | tf_op jit(solution)/shard_map/ppermute | solution.py:406
  41.8 1.9 %collective-permute-start.8 = (bf16[328,768]{1,0:T(8,128)(2,1)S(1)}, bf16[328,768]{1,0:T(8,128)(2,1)S(1)}, u32[]{:S(2)}, u32[]{:S(2)}) collective-permute-start(bf16[328,768]{1,0:T(8,128)(2,1)S(1)} %collective-permute-done.5.refs_3_), channel_id=1, source_target_pairs={{0,1},{1,0},{2,3},{3,2},{4,5},{5,4},{6,7},{7,6},{8,9},{9,8},{10,11... | collective-permute-start | bytes 1511432 | tf_op jit(solution)/shard_map/ppermute | solution.py:406
  42.5 11.0 %copy-start.2 = (bf16[1024,768]{1,0:T(8,128)(2,1)S(1)}, bf16[1024,768]{1,0:T(8,128)(2,1)}, u32[]{:S(2)}) copy-start(bf16[1024,768]{1,0:T(8,128)(2,1)} %refs_3_.1) | copy-start | bytes 4718596
  42.5 11.0 %copy-start.3 = (bf16[512,1024]{1,0:T(8,128)(2,1)S(1)}, bf16[512,1024]{1,0:T(8,128)(2,1)}, u32[]{:S(2)}) copy-start(bf16[512,1024]{1,0:T(8,128)(2,1)} %refs_2_.1) | copy-start | bytes 3145732
  42.5 11.0 %copy-start.5 = (s32[512]{0:T(512)S(1)}, s32[512]{0:T(512)}, u32[]{:S(2)}) copy-start(s32[512]{0:T(512)} %param.9) | copy-start | bytes 6148
  44.9 2.5 %collective-permute-start.10 = (f32[4,1,640]{2,1,0:T(1,128)S(1)}, f32[4,1,640]{2,1,0:T(1,128)S(1)}, u32[]{:S(2)}, u32[]{:S(2)}) collective-permute-start(f32[4,1,640]{2,1,0:T(1,128)S(1)} %get-tuple-element.252), channel_id=1, source_target_pairs={{0,1},{1,0},{2,3},{3,2},{4,5},{5,4},{6,7},{7,6},{8,9},{9,8},{10,11... | collective-permute-start | bytes 30728 | tf_op jit(solution)/shard_map/ppermute | solution.py:406
  45.1 5.9 %collective-permute-start.9 = (f32[1,1,640]{2,1,0:T(1,128)S(1)}, f32[1,1,640]{2,1,0:T(1,128)S(1)}, u32[]{:S(2)}, u32[]{:S(2)}) collective-permute-start(f32[1,1,640]{2,1,0:T(1,128)S(1)} %get-tuple-element.250.refs_0_), channel_id=1, source_target_pairs={{0,8},{1,9},{2,10},{3,11},{4,12},{5,13},{6,14},{7,15},{8,0},{9,1},... | collective-permute-start | bytes 7688 | tf_op jit(solution)/shard_map/ppermute | solution.py:406
  47.4 4.8 %collective-permute-start.14 = (f32[1,1,640]{2,1,0:T(1,128)S(1)}, f32[1,1,640]{2,1,0:T(1,128)S(1)}, u32[]{:S(2)}, u32[]{:S(2)}) collective-permute-start(f32[1,1,640]{2,1,0:T(1,128)S(1)} %get-tuple-element.332), channel_id=1, source_target_pairs={{0,6},{1,7},{2,4},{3,5},{4,2},{5,3},{6,0},{7,1},{8,14},{9,15},{10,... | collective-permute-start | bytes 7688 | tf_op jit(solution)/shard_map/ppermute | solution.py:406
  49.4 3.6 %collective-permute-start.13 = (f32[1,1,640]{2,1,0:T(1,128)S(1)}, f32[1,1,640]{2,1,0:T(1,128)S(1)}, u32[]{:S(2)}, u32[]{:S(2)}) collective-permute-start(f32[1,1,640]{2,1,0:T(1,128)S(1)} %get-tuple-element.333), channel_id=1, source_target_pairs={{0,2},{1,3},{2,0},{3,1},{4,6},{5,7},{6,4},{7,5},{8,10},{9,11},{10,... | collective-permute-start | bytes 7688 | tf_op jit(solution)/shard_map/ppermute | solution.py:406
  49.9 3.6 %collective-permute-start.12 = (f32[1,1,640]{2,1,0:T(1,128)S(1)}, f32[1,1,640]{2,1,0:T(1,128)S(1)}, u32[]{:S(2)}, u32[]{:S(2)}) collective-permute-start(f32[1,1,640]{2,1,0:T(1,128)S(1)} %get-tuple-element.334), channel_id=1, source_target_pairs={{0,4},{1,5},{2,6},{3,7},{4,0},{5,1},{6,2},{7,3},{8,12},{9,13},{10,... | collective-permute-start | bytes 7688 | tf_op jit(solution)/shard_map/ppermute | solution.py:406
  51.0 2.5 %collective-permute-start.11 = (f32[1,1,640]{2,1,0:T(1,128)S(1)}, f32[1,1,640]{2,1,0:T(1,128)S(1)}, u32[]{:S(2)}, u32[]{:S(2)}) collective-permute-start(f32[1,1,640]{2,1,0:T(1,128)S(1)} %get-tuple-element.256), channel_id=1, source_target_pairs={{0,1},{1,0},{2,3},{3,2},{4,8},{5,9},{6,10},{7,11},{8,4},{9,5},{10,... | collective-permute-start | bytes 7688 | tf_op jit(solution)/shard_map/ppermute | solution.py:406
  54.3 0.6 copy-start.6

commit v13 on v12

--- a/solution.py
+++ b/solution.py
@@ -452,7 +452,7 @@
     own, pair, row, pair_row = (kept[k:k + 1] + from_core[k:k + 1] for k in (0, 1, 2, 3))
     home = [
         own, from_next, from_far,
-        move(pair, OUTER), move(row, STAY, row=1), move(pair_row, OUTER, row=1),
+        move(pair_row, OUTER, row=1), move(pair, OUTER), move(row, STAY, row=1),
     ]
     return lax.cond(
         decide(flag, to_far, from_far)[0] > 0,

time: 61.8 us -> 62.8 us (1.016)
  waiting for transfers between devices: 20.6 us -> 21.6 us
    ppermute x15, waiting for transfers between devices: 20.6 us -> 21.6 us  [move(): return lax.ppermute(a, ('owner', 'split'), pairs)]
where the time goes in v13:
time: 62.8 us; the launch traced here: 62.7 us
  waiting for transfers between devices  21.6 us (34%)
  starting transfers between devices  15.2 us (24%)
  between operations  14.1 us (22%)
  Pallas kernels  10.7 us (17%)
    ppermute x15, waiting for transfers between devices, move(): return lax.ppermute(a, ('owner', 'split'), pairs)  21.6 us
    ppermute x15, starting transfers between devices, move(): return lax.ppermute(a, ('owner', 'split'), pairs)  15.2 us
    pallas_call x5, Pallas kernels, score(): pl.pallas_call(lambda *refs: score_kernel(docs, hot, names, given, made,...  6.09 us
    pallas_call x1, Pallas kernels, prep(): pl.pallas_call(lambda *refs: prep_kernel(hot, *refs), out_shape=(shape((r...  3.56 us
  transfers between devices with their start and end apart: 15, of which 6 were waited for; matrix products, arithmetic and copies ran while one was open for 0% of the time, Pallas kernels for 9%

profile of v13, /device:TPU:0, one launch (start us, length us, event | category | flops | bytes accessed | tf_op | source)
XLA Modules:
  0.0 62.7 jit_solution(6911192952239008293)
XLA Ops:
  6.5 0.1 pad_add_fusion.refs_0_
  6.6 3.6 %prep.1 = (bf16[328,768]{1,0:T(8,128)(2,1)S(1)}, bf16[328,768]{1,0:T(8,128)(2,1)S(1)}, s32[1,512]{1,0:T(1,128)S(1)}) custom-call(s32[3]{0:T(128)S(1)} %pad_add_fusion.refs_0_, s32[1,512]{1,0:T(1,128)} %bitcast.38, bf16[512,1024]{1,0:T(8,128)(2,1)} %refs_2_.1, bf16[1024,768]{1,0:T(8,128)(2,1)} %refs_3_.1), custom_call_target="tpu_custom_call" | custom-call | tf_op jit(solution)/shard_map/prep/pallas_call | solution.py:195
  10.2 0.5 collective-permute-start
  10.7 2.6 %collective-permute-start.4 = (bf16[328,768]{1,0:T(8,128)(2,1)S(1)}, bf16[328,768]{1,0:T(8,128)(2,1)S(1)}, u32[]{:S(2)}, u32[]{:S(2)}) collective-permute-start(bf16[328,768]{1,0:T(8,128)(2,1)S(1)} %get-tuple-element.222), channel_id=1, source_target_pairs={{0,4},{1,5},{2,6},{3,7},{4,0},{5,1},{6,2},{7,3},{8,12},{9,13},{10,... | collective-permute-start | bytes 1511432 | tf_op jit(solution)/shard_map/ppermute | solution.py:406
  13.3 1.7 %collective-permute-start.1 = (bf16[328,768]{1,0:T(8,128)(2,1)S(1)}, bf16[328,768]{1,0:T(8,128)(2,1)S(1)}, u32[]{:S(2)}, u32[]{:S(2)}) collective-permute-start(bf16[328,768]{1,0:T(8,128)(2,1)S(1)} %get-tuple-element.221.refs_1_), channel_id=1, source_target_pairs={{0,2},{1,3},{2,0},{3,1},{4,6},{5,7},{6,4},{7,5},{8,10},{9,11},{10,... | collective-permute-start | bytes 1511432 | tf_op jit(solution)/shard_map/ppermute | solution.py:406
  15.1 1.4 %own.1 = (f32[4,1,640]{2,1,0:T(1,128)S(1)}, f32[4,1,640]{2,1,0:T(1,128)S(1)}, f32[1,1,640]{2,1,0:T(1,128)S(1)}, f32[1,1,640]{2,1,0:T(1,128)S(1)}, bf16[768,640]{1,0:T(8,128)(2,1)S(1)}, /*index=5*/f32[8,640]{1,0:T(8,128)S(1)}) custom-call(s32[3]{0:T(128)S(1)} %pad_add_fusion.refs_0_, bf16[328,768]{1,0:T(8,128)(2,1)S(1)} %get-tuple-element.221.refs_1_, ...), custom_call_target="tpu_custom_call" | custom-call | flops 8589934592 | bytes 1024 | tf_op jit(solution)/shard_map/own/pallas_call | solution.py:339
  16.5 8.9 %collective-permute-done.4.refs_1_.refs_3_ = bf16[328,768]{1,0:T(8,128)(2,1)S(1)} collective-permute-done((bf16[328,768]{1,0:T(8,128)(2,1)S(1)}, bf16[328,768]{1,0:T(8,128)(2,1)S(1)}, u32[]{:S(2)}, u32[]{:S(2)}) %collective-permute-start.4) | collective-permute-done | bytes 503840 | tf_op jit(solution)/shard_map/ppermute | solution.py:406
  25.4 0.0 collective-permute-start.7
  25.4 2.8 %collective-permute-start.3 = (bf16[328,768]{1,0:T(8,128)(2,1)S(1)}, bf16[328,768]{1,0:T(8,128)(2,1)S(1)}, u32[]{:S(2)}, u32[]{:S(2)}) collective-permute-start(bf16[328,768]{1,0:T(8,128)(2,1)S(1)} %get-tuple-element.221.refs_1_), channel_id=1, source_target_pairs={{0,8},{1,9},{2,10},{3,11},{4,0},{5,1},{6,2},{7,3},{8,12},{9,13},{1... | collective-permute-start | bytes 1511432 | tf_op jit(solution)/shard_map/ppermute | solution.py:406
  28.2 1.5 %collective-permute-start.5 = (bf16[328,768]{1,0:T(8,128)(2,1)S(1)}, bf16[328,768]{1,0:T(8,128)(2,1)S(1)}, u32[]{:S(2)}, u32[]{:S(2)}) collective-permute-start(bf16[328,768]{1,0:T(8,128)(2,1)S(1)} %collective-permute-done.4.refs_1_.refs_3_), channel_id=1, source_target_pairs={{0,2},{1,3},{2,0},{3,1},{4,6},{5,7},{6,4},{7,5},{8,10},{9,11},{10,... | collective-permute-start | bytes 1511432 | tf_op jit(solution)/shard_map/ppermute | solution.py:406
  29.7 1.1 %pair.1 = (f32[4,1,640]{2,1,0:T(1,128)S(1)}, f32[4,1,640]{2,1,0:T(1,128)S(1)}, f32[1,1,640]{2,1,0:T(1,128)S(1)}, f32[1,1,640]{2,1,0:T(1,128)S(1)}, bf16[768,640]{1,0:T(8,128)(2,1)S(1)}, /*index=5*/f32[8,640]{1,0:T(8,128)S(1)}) custom-call(s32[3]{0:T(128)S(1)} %pad_add_fusion.refs_0_, bf16[328,768]{1,0:T(8,128)(2,1)S(1)} %collective-permute-done.4.refs_1_.refs_3_, ...), custom_call_target="tpu_custom_call" | custom-call | flops 8589934592 | bytes 1024 | tf_op jit(solution)/shard_map/pair/pallas_call | solution.py:339
  30.8 0.8 %collective-permute-done.6.refs_2_ = bf16[328,768]{1,0:T(8,128)(2,1)S(1)} collective-permute-done((bf16[328,768]{1,0:T(8,128)(2,1)S(1)}, bf16[328,768]{1,0:T(8,128)(2,1)S(1)}, u32[]{:S(2)}, u32[]{:S(2)}) %collective-permute-start.6) | collective-permute-done | bytes 503840 | tf_op jit(solution)/shard_map/ppermute | solution.py:406
  31.6 1.8 %row.1 = (f32[4,1,640]{2,1,0:T(1,128)S(1)}, f32[4,1,640]{2,1,0:T(1,128)S(1)}, f32[1,1,640]{2,1,0:T(1,128)S(1)}, f32[1,1,640]{2,1,0:T(1,128)S(1)}, bf16[768,640]{1,0:T(8,128)(2,1)S(1)}, /*index=5*/f32[8,640]{1,0:T(8,128)S(1)}) custom-call(s32[3]{0:T(128)S(1)} %pad_add_fusion.refs_0_, bf16[328,768]{1,0:T(8,128)(2,1)S(1)} %collective-permute-done.1.refs_1_, ...), custom_call_target="tpu_custom_call" | custom-call | flops 1 | bytes 1024 | tf_op jit(solution)/shard_map/row/pallas_call | solution.py:339
  33.4 8.4 %collective-permute-done.5.refs_3_ = bf16[328,768]{1,0:T(8,128)(2,1)S(1)} collective-permute-done((bf16[328,768]{1,0:T(8,128)(2,1)S(1)}, bf16[328,768]{1,0:T(8,128)(2,1)S(1)}, u32[]{:S(2)}, u32[]{:S(2)}) %collective-permute-start.5) | collective-permute-done | bytes 503840 | tf_op jit(solution)/shard_map/ppermute | solution.py:406
  41.8 0.6 %far.1 = (f32[4,1,640]{2,1,0:T(1,128)S(1)}, f32[4,1,640]{2,1,0:T(1,128)S(1)}, f32[1,1,640]{2,1,0:T(1,128)S(1)}, f32[1,1,640]{2,1,0:T(1,128)S(1)}) custom-call(s32[3]{0:T(128)S(1)} %pad_add_fusion.refs_0_, bf16[328,768]{1,0:T(8,128)(2,1)S(1)} %collective-permute-done.3.refs_1_.refs_2_, bf16[768,640]{1,0:T(8,128)(2,1)S(1)} %get-tuple-element.228.refs_4_.refs_5_.refs_2_, ...), custom_call_target="tpu_custom_call" | custom-call | flops 1 | bytes 1024 | tf_op jit(solution)/shard_map/far/pallas_call | solution.py:339
  42.5 0.0 copy-start.2
  42.5 0.0 copy-start.3
  42.5 0.0 copy-start.5
  42.5 1.2 %collective-permute-done.8.refs_4_ = bf16[328,768]{1,0:T(8,128)(2,1)S(1)} collective-permute-done((bf16[328,768]{1,0:T(8,128)(2,1)S(1)}, bf16[328,768]{1,0:T(8,128)(2,1)S(1)}, u32[]{:S(2)}, u32[]{:S(2)}) %collective-permute-start.8) | collective-permute-done | bytes 503840 | tf_op jit(solution)/shard_map/ppermute | solution.py:406
  43.7 1.2 %last.1 = (f32[4,1,640]{2,1,0:T(1,128)S(1)}, f32[4,1,640]{2,1,0:T(1,128)S(1)}, f32[1,1,640]{2,1,0:T(1,128)S(1)}, f32[1,1,640]{2,1,0:T(1,128)S(1)}) custom-call(s32[3]{0:T(128)S(1)} %pad_add_fusion.refs_0_, bf16[328,768]{1,0:T(8,128)(2,1)S(1)} %collective-permute-done.2.refs_3_.refs_4_.refs_1_, bf16[328,768]{1,0:T(8,128)(2,1)S(1)} %collective-permute-done.3.refs_1_.refs_2_, ...), custom_call_target="tpu_custom_call" | custom-call | flops 1 | bytes 1024 | tf_op jit(solution)/shard_map/last/pallas_call | solution.py:339
  44.9 0.1 collective-permute-start.10
  45.1 2.3 %collective-permute-start.9 = (f32[1,1,640]{2,1,0:T(1,128)S(1)}, f32[1,1,640]{2,1,0:T(1,128)S(1)}, u32[]{:S(2)}, u32[]{:S(2)}) collective-permute-start(f32[1,1,640]{2,1,0:T(1,128)S(1)} %get-tuple-element.250.refs_0_), channel_id=1, source_target_pairs={{0,8},{1,9},{2,10},{3,11},{4,12},{5,13},{6,14},{7,15},{8,0},{9,1},... | collective-permute-start | bytes 7688 | tf_op jit(solution)/shard_map/ppermute | solution.py:406
  47.4 1.6 %collective-permute-start.14 = (f32[1,1,640]{2,1,0:T(1,128)S(1)}, f32[1,1,640]{2,1,0:T(1,128)S(1)}, u32[]{:S(2)}, u32[]{:S(2)}) collective-permute-start(f32[1,1,640]{2,1,0:T(1,128)S(1)} %get-tuple-element.332), channel_id=1, source_target_pairs={{0,2},{1,3},{2,0},{3,1},{4,6},{5,7},{6,4},{7,5},{8,10},{9,11},{10,... | collective-permute-start | bytes 7688 | tf_op jit(solution)/shard_map/ppermute | solution.py:406
  49.0 1.0 %collective-permute-start.13 = (f32[1,1,640]{2,1,0:T(1,128)S(1)}, f32[1,1,640]{2,1,0:T(1,128)S(1)}, u32[]{:S(2)}, u32[]{:S(2)}) collective-permute-start(f32[1,1,640]{2,1,0:T(1,128)S(1)} %get-tuple-element.333), channel_id=1, source_target_pairs={{0,4},{1,5},{2,6},{3,7},{4,0},{5,1},{6,2},{7,3},{8,12},{9,13},{10,... | collective-permute-start | bytes 7688 | tf_op jit(solution)/shard_map/ppermute | solution.py:406
  50.0 1.0 %collective-permute-start.12 = (f32[1,1,640]{2,1,0:T(1,128)S(1)}, f32[1,1,640]{2,1,0:T(1,128)S(1)}, u32[]{:S(2)}, u32[]{:S(2)}) collective-permute-start(f32[1,1,640]{2,1,0:T(1,128)S(1)} %get-tuple-element.334), channel_id=1, source_target_pairs={{0,6},{1,7},{2,4},{3,5},{4,2},{5,3},{6,0},{7,1},{8,14},{9,15},{10,... | collective-permute-start | bytes 7688 | tf_op jit(solution)/shard_map/ppermute | solution.py:406
  51.0 0.6 decide.1
  52.3 0.3 collective-permute-done.13
  52.6 1.9 %collective-permute-done.12 = f32[1,1,640]{2,1,0:T(1,128)S(1)} collective-permute-done((f32[1,1,640]{2,1,0:T(1,128)S(1)}, f32[1,1,640]{2,1,0:T(1,128)S(1)}, u32[]{:S(2)}, u32[]{:S(2)}) %collective-permute-start.12) | collective-permute-done | bytes 2592 | tf_op jit(solution)/shard_map/ppermute | solution.py:406
  54.5 0.8 %conditional.1 = (f32[512]{0:T(512)S(1)}) conditional(s32[]{:T(128)} %bitcast.12, (f32[4,1,640]{2,1,0:T(1,128)S(1)}, f32[4,1,640]{2,1,0:T(1,128)S(1)}, s32[1,512]{1,0:T(1,128)S(1)}, f32[1,1,640]{2,1,0:T(1,128)S(1)}, f32[1,1,640]{2,1,0:T(1,128)S(1)}, /*index=5*/f32[1,1,640]{2,1,0:T(1,128)S(1)}, f32[1,1,640]{2,1,0:T(1,128)S(1)}, ...), branch_computations={%region_0.1_spmd, %region_1.13_spmd} | conditional | flops 4454147584 | bytes 57829452 | solution.py:457
  54.5 0.5 finish.1
  55.2 0.0 copy-start.6
  55.2 0.6 copy-done.6
  (18 shorter events, 0.1 us)
Async XLA Ops:
  10.2 3.2 %collective-permute-start = (bf16[328,768]{1,0:T(8,128)(2,1)S(1)}, bf16[328,768]{1,0:T(8,128)(2,1)S(1)}, u32[]{:S(2)}, u32[]{:S(2)}) collective-permute-start(bf16[328,768]{1,0:T(8,128)(2,1)S(1)} %get-tuple-element.221.refs_1_), channel_id=1, source_target_pairs={{0,1},{1,0},{2,3},{3,2},{4,5},{5,4},{6,7},{7,6},{8,9},{9,8},{10,11... | collective-permute-start | bytes 1511432 | tf_op jit(solution)/shard_map/ppermute | solution.py:406
  10.7 14.7 %collective-permute-start.4 = (bf16[328,768]{1,0:T(8,128)(2,1)S(1)}, bf16[328,768]{1,0:T(8,128)(2,1)S(1)}, u32[]{:S(2)}, u32[]{:S(2)}) collective-permute-start(bf16[328,768]{1,0:T(8,128)(2,1)S(1)} %get-tuple-element.222), channel_id=1, source_target_pairs={{0,4},{1,5},{2,6},{3,7},{4,0},{5,1},{6,2},{7,3},{8,12},{9,13},{10,... | collective-permute-start | bytes 1511432 | tf_op jit(solution)/shard_map/ppermute | solution.py:406
  13.3 16.4 %collective-permute-start.1 = (bf16[328,768]{1,0:T(8,128)(2,1)S(1)}, bf16[328,768]{1,0:T(8,128)(2,1)S(1)}, u32[]{:S(2)}, u32[]{:S(2)}) collective-permute-start(bf16[328,768]{1,0:T(8,128)(2,1)S(1)} %get-tuple-element.221.refs_1_), channel_id=1, source_target_pairs={{0,2},{1,3},{2,0},{3,1},{4,6},{5,7},{6,4},{7,5},{8,10},{9,11},{10,... | collective-permute-start | bytes 1511432 | tf_op jit(solution)/shard_map/ppermute | solution.py:406
  15.1 14.6 %collective-permute-start.2 = (bf16[328,768]{1,0:T(8,128)(2,1)S(1)}, bf16[328,768]{1,0:T(8,128)(2,1)S(1)}, u32[]{:S(2)}, u32[]{:S(2)}) collective-permute-start(bf16[328,768]{1,0:T(8,128)(2,1)S(1)} %get-tuple-element.222), channel_id=1, source_target_pairs={{0,1},{1,0},{2,3},{3,2},{4,8},{5,9},{6,10},{7,11},{8,4},{9,5},{10,... | collective-permute-start | bytes 1511432 | tf_op jit(solution)/shard_map/ppermute | solution.py:406
  25.4 4.3 %collective-permute-start.7 = (bf16[328,768]{1,0:T(8,128)(2,1)S(1)}, bf16[328,768]{1,0:T(8,128)(2,1)S(1)}, u32[]{:S(2)}, u32[]{:S(2)}) collective-permute-start(bf16[328,768]{1,0:T(8,128)(2,1)S(1)} %collective-permute-done.4.refs_1_.refs_3_), channel_id=1, source_target_pairs={{0,1},{1,0},{2,3},{3,2},{4,5},{5,4},{6,7},{7,6},{8,9},{9,8},{10,11... | collective-permute-start | bytes 1511432 | tf_op jit(solution)/shard_map/ppermute | solution.py:406
  25.4 16.4 %collective-permute-start.3 = (bf16[328,768]{1,0:T(8,128)(2,1)S(1)}, bf16[328,768]{1,0:T(8,128)(2,1)S(1)}, u32[]{:S(2)}, u32[]{:S(2)}) collective-permute-start(bf16[328,768]{1,0:T(8,128)(2,1)S(1)} %get-tuple-element.221.refs_1_), channel_id=1, source_target_pairs={{0,8},{1,9},{2,10},{3,11},{4,0},{5,1},{6,2},{7,3},{8,12},{9,13},{1... | collective-permute-start | bytes 1511432 | tf_op jit(solution)/shard_map/ppermute | solution.py:406
  28.2 13.6 %collective-permute-start.5 = (bf16[328,768]{1,0:T(8,128)(2,1)S(1)}, bf16[328,768]{1,0:T(8,128)(2,1)S(1)}, u32[]{:S(2)}, u32[]{:S(2)}) collective-permute-start(bf16[328,768]{1,0:T(8,128)(2,1)S(1)} %collective-permute-done.4.refs_1_.refs_3_), channel_id=1, source_target_pairs={{0,2},{1,3},{2,0},{3,1},{4,6},{5,7},{6,4},{7,5},{8,10},{9,11},{10,... | collective-permute-start | bytes 1511432 | tf_op jit(solution)/shard_map/ppermute | solution.py:406
  29.7 1.9 %collective-permute-start.6 = (bf16[328,768]{1,0:T(8,128)(2,1)S(1)}, bf16[328,768]{1,0:T(8,128)(2,1)S(1)}, u32[]{:S(2)}, u32[]{:S(2)}) collective-permute-start(bf16[328,768]{1,0:T(8,128)(2,1)S(1)} %collective-permute-done.1.refs_1_), channel_id=1, source_target_pairs={{0,1},{1,0},{2,3},{3,2},{4,5},{5,4},{6,7},{7,6},{8,9},{9,8},{10,11... | collective-permute-start | bytes 1511432 | tf_op jit(solution)/shard_map/ppermute | solution.py:406
  41.8 1.9 %collective-permute-start.8 = (bf16[328,768]{1,0:T(8,128)(2,1)S(1)}, bf16[328,768]{1,0:T(8,128)(2,1)S(1)}, u32[]{:S(2)}, u32[]{:S(2)}) collective-permute-start(bf16[328,768]{1,0:T(8,128)(2,1)S(1)} %collective-permute-done.5.refs_3_), channel_id=1, source_target_pairs={{0,1},{1,0},{2,3},{3,2},{4,5},{5,4},{6,7},{7,6},{8,9},{9,8},{10,11... | collective-permute-start | bytes 1511432 | tf_op jit(solution)/shard_map/ppermute | solution.py:406
  42.5 12.0 %copy-start.2 = (bf16[1024,768]{1,0:T(8,128)(2,1)S(1)}, bf16[1024,768]{1,0:T(8,128)(2,1)}, u32[]{:S(2)}) copy-start(bf16[1024,768]{1,0:T(8,128)(2,1)} %refs_3_.1) | copy-start | bytes 4718596
  42.5 12.0 %copy-start.3 = (bf16[512,1024]{1,0:T(8,128)(2,1)S(1)}, bf16[512,1024]{1,0:T(8,128)(2,1)}, u32[]{:S(2)}) copy-start(bf16[512,1024]{1,0:T(8,128)(2,1)} %refs_2_.1) | copy-start | bytes 3145732
  42.5 12.0 %copy-start.5 = (s32[512]{0:T(512)S(1)}, s32[512]{0:T(512)}, u32[]{:S(2)}) copy-start(s32[512]{0:T(512)} %param.9) | copy-start | bytes 6148
  44.9 2.5 %collective-permute-start.10 = (f32[4,1,640]{2,1,0:T(1,128)S(1)}, f32[4,1,640]{2,1,0:T(1,128)S(1)}, u32[]{:S(2)}, u32[]{:S(2)}) collective-permute-start(f32[4,1,640]{2,1,0:T(1,128)S(1)} %get-tuple-element.252), channel_id=1, source_target_pairs={{0,1},{1,0},{2,3},{3,2},{4,5},{5,4},{6,7},{7,6},{8,9},{9,8},{10,11... | collective-permute-start | bytes 30728 | tf_op jit(solution)/shard_map/ppermute | solution.py:406
  45.1 5.9 %collective-permute-start.9 = (f32[1,1,640]{2,1,0:T(1,128)S(1)}, f32[1,1,640]{2,1,0:T(1,128)S(1)}, u32[]{:S(2)}, u32[]{:S(2)}) collective-permute-start(f32[1,1,640]{2,1,0:T(1,128)S(1)} %get-tuple-element.250.refs_0_), channel_id=1, source_target_pairs={{0,8},{1,9},{2,10},{3,11},{4,12},{5,13},{6,14},{7,15},{8,0},{9,1},... | collective-permute-start | bytes 7688 | tf_op jit(solution)/shard_map/ppermute | solution.py:406
  47.4 4.8 %collective-permute-start.14 = (f32[1,1,640]{2,1,0:T(1,128)S(1)}, f32[1,1,640]{2,1,0:T(1,128)S(1)}, u32[]{:S(2)}, u32[]{:S(2)}) collective-permute-start(f32[1,1,640]{2,1,0:T(1,128)S(1)} %get-tuple-element.332), channel_id=1, source_target_pairs={{0,2},{1,3},{2,0},{3,1},{4,6},{5,7},{6,4},{7,5},{8,10},{9,11},{10,... | collective-permute-start | bytes 7688 | tf_op jit(solution)/shard_map/ppermute | solution.py:406
  49.0 3.6 %collective-permute-start.13 = (f32[1,1,640]{2,1,0:T(1,128)S(1)}, f32[1,1,640]{2,1,0:T(1,128)S(1)}, u32[]{:S(2)}, u32[]{:S(2)}) collective-permute-start(f32[1,1,640]{2,1,0:T(1,128)S(1)} %get-tuple-element.333), channel_id=1, source_target_pairs={{0,4},{1,5},{2,6},{3,7},{4,0},{5,1},{6,2},{7,3},{8,12},{9,13},{10,... | collective-permute-start | bytes 7688 | tf_op jit(solution)/shard_map/ppermute | solution.py:406
  50.0 4.5 %collective-permute-start.12 = (f32[1,1,640]{2,1,0:T(1,128)S(1)}, f32[1,1,640]{2,1,0:T(1,128)S(1)}, u32[]{:S(2)}, u32[]{:S(2)}) collective-permute-start(f32[1,1,640]{2,1,0:T(1,128)S(1)} %get-tuple-element.334), channel_id=1, source_target_pairs={{0,6},{1,7},{2,4},{3,5},{4,2},{5,3},{6,0},{7,1},{8,14},{9,15},{10,... | collective-permute-start | bytes 7688 | tf_op jit(solution)/shard_map/ppermute | solution.py:406
  51.0 3.5 %collective-permute-start.11 = (f32[1,1,640]{2,1,0:T(1,128)S(1)}, f32[1,1,640]{2,1,0:T(1,128)S(1)}, u32[]{:S(2)}, u32[]{:S(2)}) collective-permute-start(f32[1,1,640]{2,1,0:T(1,128)S(1)} %get-tuple-element.256), channel_id=1, source_target_pairs={{0,1},{1,0},{2,3},{3,2},{4,8},{5,9},{6,10},{7,11},{8,4},{9,5},{10,... | collective-permute-start | bytes 7688 | tf_op jit(solution)/shard_map/ppermute | solution.py:406
  55.2 0.6 copy-start.6

commit v14 on v12

--- a/solution.py
+++ b/solution.py
@@ -106,6 +106,31 @@
         scores.reshape(owners, capacity), "owner", split_axis=0, concat_axis=0, tiled=True
     )
     return returned.reshape(slot_total)[target]
+
+
+def ring_plan(states, proj_weight, cluster_of):
+    axes = ("owner", "split")
+    devices = lax.axis_size("owner") * lax.axis_size("split")
+    ring = [(i, (i + 1) % devices) for i in range(devices)]
+    quant, peak = prepare(states, proj_weight)
+    scale = peak.astype(F32)
+    place = jnp.arange(states.shape[0], dtype=jnp.int32)
+
+    def weights(block, block_peak, block_cluster):
+        inner = lax.dot_general(quant, block, (((1,), (1,)), ((), ())), preferred_element_type=F32)
+        cosine = inner * scale[:, None] * block_peak.astype(F32)[None, :]
+        same = cluster_of[:, None] == block_cluster[None, :]
+        return jnp.where(same, jnp.exp((cosine - THRESH) / TAU), jnp.zeros_like(cosine))
+
+    def meet(_, carry):
+        passed = [lax.ppermute(a, axes, ring) for a in carry[1:]]
+        return (carry[0] + jnp.sum(weights(*passed), axis=1), *passed)
+
+    own = (quant, peak, cluster_of)
+    others = place[:, None] != place[None, :]
+    total = jnp.sum(jnp.where(others, weights(*own), 0.0), axis=1)
+    total = lax.fori_loop(1, devices, meet, (total, *own))[0]
+    return jnp.log(1.0 + total)
 
 
 def up(n, m):
@@ -456,7 +481,7 @@
     ]
     return lax.cond(
         decide(flag, to_far, from_far)[0] > 0,
-        lambda states, proj_weight, cluster_of, *_: owner_plan(states, proj_weight, cluster_of),
+        lambda states, proj_weight, cluster_of, *_: ring_plan(states, proj_weight, cluster_of),
         lambda states, proj_weight, cluster_of, slot, *home: finish(slot, home).reshape(docs),
         states, proj_weight, cluster_of, slot, *home,
     )

time: 61.8 us -> 48.2 us (0.78)
  between operations: 14.1 us -> 0.77 us
  transfers between devices with their start and end apart: 15 -> 15, of which waited for: 6 -> 6; matrix products, arithmetic and copies ran while one was open for 0% -> 0% of each run, Pallas kernels for 9% -> 11%
where the time goes in v14:
time: 48.2 us; the launch traced here: 48 us
  waiting for transfers between devices  20.6 us (43%)
  starting transfers between devices  15.2 us (32%)
  Pallas kernels  10.7 us (22%)
  between operations  0.77 us (2%)
  local copies, waits for them, and re-layouts  0.59 us (1%)
    ppermute x15, waiting for transfers between devices, move(): return lax.ppermute(a, ('owner', 'split'), pairs)  20.6 us
    ppermute x15, starting transfers between devices, move(): return lax.ppermute(a, ('owner', 'split'), pairs)  15.2 us
    pallas_call x5, Pallas kernels, score(): pl.pallas_call(lambda *refs: score_kernel(docs, hot, names, given, made,...  6.09 us
    pallas_call x1, Pallas kernels, prep(): pl.pallas_call(lambda *refs: prep_kernel(hot, *refs), out_shape=(shape((r...  3.56 us
  transfers between devices with their start and end apart: 15, of which 6 were waited for; matrix products, arithmetic and copies ran while one was open for 0% of the time, Pallas kernels for 11%

profile of v14, /device:TPU:0, one launch (start us, length us, event | category | flops | bytes accessed | tf_op | source)
XLA Modules:
  0.0 48.0 jit_solution(6472903373761232523)
XLA Ops:
  0.0 0.1 pad_add_fusion.refs_0_
  0.1 3.6 %prep.1 = (bf16[328,768]{1,0:T(8,128)(2,1)S(1)}, bf16[328,768]{1,0:T(8,128)(2,1)S(1)}, s32[1,512]{1,0:T(1,128)S(1)}) custom-call(s32[3]{0:T(128)S(1)} %pad_add_fusion.refs_0_, s32[1,512]{1,0:T(1,128)} %bitcast.16, bf16[512,1024]{1,0:T(8,128)(2,1)} %refs_2_.1, bf16[1024,768]{1,0:T(8,128)(2,1)} %refs_3_.1), custom_call_target="tpu_custom_call" | custom-call | tf_op jit(solution)/shard_map/prep/pallas_call | solution.py:220
  3.6 0.5 %collective-permute-start.3 = (bf16[328,768]{1,0:T(8,128)(2,1)S(1)}, bf16[328,768]{1,0:T(8,128)(2,1)S(1)}, u32[]{:S(2)}, u32[]{:S(2)}) collective-permute-start(bf16[328,768]{1,0:T(8,128)(2,1)S(1)} %get-tuple-element.185.refs_1_), channel_id=1, source_target_pairs={{0,1},{1,0},{2,3},{3,2},{4,5},{5,4},{6,7},{7,6},{8,9},{9,8},{10,11... | collective-permute-start | bytes 1511432 | tf_op jit(solution)/shard_map/ppermute | solution.py:431
  4.2 2.6 %collective-permute-start.7 = (bf16[328,768]{1,0:T(8,128)(2,1)S(1)}, bf16[328,768]{1,0:T(8,128)(2,1)S(1)}, u32[]{:S(2)}, u32[]{:S(2)}) collective-permute-start(bf16[328,768]{1,0:T(8,128)(2,1)S(1)} %get-tuple-element.186), channel_id=1, source_target_pairs={{0,4},{1,5},{2,6},{3,7},{4,0},{5,1},{6,2},{7,3},{8,12},{9,13},{10,... | collective-permute-start | bytes 1511432 | tf_op jit(solution)/shard_map/ppermute | solution.py:431
  6.8 0.0 collective-permute-done.3.refs_2_
  6.8 1.7 %collective-permute-start.4 = (bf16[328,768]{1,0:T(8,128)(2,1)S(1)}, bf16[328,768]{1,0:T(8,128)(2,1)S(1)}, u32[]{:S(2)}, u32[]{:S(2)}) collective-permute-start(bf16[328,768]{1,0:T(8,128)(2,1)S(1)} %get-tuple-element.185.refs_1_), channel_id=1, source_target_pairs={{0,2},{1,3},{2,0},{3,1},{4,6},{5,7},{6,4},{7,5},{8,10},{9,11},{10,... | collective-permute-start | bytes 1511432 | tf_op jit(solution)/shard_map/ppermute | solution.py:431
  8.6 1.4 %own.1 = (f32[4,1,640]{2,1,0:T(1,128)S(1)}, f32[4,1,640]{2,1,0:T(1,128)S(1)}, f32[1,1,640]{2,1,0:T(1,128)S(1)}, f32[1,1,640]{2,1,0:T(1,128)S(1)}, bf16[768,640]{1,0:T(8,128)(2,1)S(1)}, /*index=5*/f32[8,640]{1,0:T(8,128)S(1)}) custom-call(s32[3]{0:T(128)S(1)} %pad_add_fusion.refs_0_, bf16[328,768]{1,0:T(8,128)(2,1)S(1)} %get-tuple-element.185.refs_1_, ...), custom_call_target="tpu_custom_call" | custom-call | flops 8589934592 | bytes 1024 | tf_op jit(solution)/shard_map/own/pallas_call | solution.py:364
  10.0 8.9 %collective-permute-done.7.refs_1_.refs_3_ = bf16[328,768]{1,0:T(8,128)(2,1)S(1)} collective-permute-done((bf16[328,768]{1,0:T(8,128)(2,1)S(1)}, bf16[328,768]{1,0:T(8,128)(2,1)S(1)}, u32[]{:S(2)}, u32[]{:S(2)}) %collective-permute-start.7) | collective-permute-done | bytes 503840 | tf_op jit(solution)/shard_map/ppermute | solution.py:431
  18.9 2.8 %collective-permute-start.6 = (bf16[328,768]{1,0:T(8,128)(2,1)S(1)}, bf16[328,768]{1,0:T(8,128)(2,1)S(1)}, u32[]{:S(2)}, u32[]{:S(2)}) collective-permute-start(bf16[328,768]{1,0:T(8,128)(2,1)S(1)} %get-tuple-element.185.refs_1_), channel_id=1, source_target_pairs={{0,8},{1,9},{2,10},{3,11},{4,0},{5,1},{6,2},{7,3},{8,12},{9,13},{1... | collective-permute-start | bytes 1511432 | tf_op jit(solution)/shard_map/ppermute | solution.py:431
  21.7 1.5 %collective-permute-start.8 = (bf16[328,768]{1,0:T(8,128)(2,1)S(1)}, bf16[328,768]{1,0:T(8,128)(2,1)S(1)}, u32[]{:S(2)}, u32[]{:S(2)}) collective-permute-start(bf16[328,768]{1,0:T(8,128)(2,1)S(1)} %collective-permute-done.7.refs_1_.refs_3_), channel_id=1, source_target_pairs={{0,2},{1,3},{2,0},{3,1},{4,6},{5,7},{6,4},{7,5},{8,10},{9,11},{10,... | collective-permute-start | bytes 1511432 | tf_op jit(solution)/shard_map/ppermute | solution.py:431
  23.2 1.1 %pair.1 = (f32[4,1,640]{2,1,0:T(1,128)S(1)}, f32[4,1,640]{2,1,0:T(1,128)S(1)}, f32[1,1,640]{2,1,0:T(1,128)S(1)}, f32[1,1,640]{2,1,0:T(1,128)S(1)}, bf16[768,640]{1,0:T(8,128)(2,1)S(1)}, /*index=5*/f32[8,640]{1,0:T(8,128)S(1)}) custom-call(s32[3]{0:T(128)S(1)} %pad_add_fusion.refs_0_, bf16[328,768]{1,0:T(8,128)(2,1)S(1)} %collective-permute-done.7.refs_1_.refs_3_, ...), custom_call_target="tpu_custom_call" | custom-call | flops 8589934592 | bytes 1024 | tf_op jit(solution)/shard_map/pair/pallas_call | solution.py:364
  24.3 0.8 %collective-permute-done.9.refs_2_ = bf16[328,768]{1,0:T(8,128)(2,1)S(1)} collective-permute-done((bf16[328,768]{1,0:T(8,128)(2,1)S(1)}, bf16[328,768]{1,0:T(8,128)(2,1)S(1)}, u32[]{:S(2)}, u32[]{:S(2)}) %collective-permute-start.9) | collective-permute-done | bytes 503840 | tf_op jit(solution)/shard_map/ppermute | solution.py:431
  25.1 1.8 %row.1 = (f32[4,1,640]{2,1,0:T(1,128)S(1)}, f32[4,1,640]{2,1,0:T(1,128)S(1)}, f32[1,1,640]{2,1,0:T(1,128)S(1)}, f32[1,1,640]{2,1,0:T(1,128)S(1)}, bf16[768,640]{1,0:T(8,128)(2,1)S(1)}, /*index=5*/f32[8,640]{1,0:T(8,128)S(1)}) custom-call(s32[3]{0:T(128)S(1)} %pad_add_fusion.refs_0_, bf16[328,768]{1,0:T(8,128)(2,1)S(1)} %collective-permute-done.4.refs_1_, ...), custom_call_target="tpu_custom_call" | custom-call | flops 1 | bytes 1024 | tf_op jit(solution)/shard_map/row/pallas_call | solution.py:364
  26.9 8.4 %collective-permute-done.8.refs_3_ = bf16[328,768]{1,0:T(8,128)(2,1)S(1)} collective-permute-done((bf16[328,768]{1,0:T(8,128)(2,1)S(1)}, bf16[328,768]{1,0:T(8,128)(2,1)S(1)}, u32[]{:S(2)}, u32[]{:S(2)}) %collective-permute-start.8) | collective-permute-done | bytes 503840 | tf_op jit(solution)/shard_map/ppermute | solution.py:431
  35.3 0.6 %far.1 = (f32[4,1,640]{2,1,0:T(1,128)S(1)}, f32[4,1,640]{2,1,0:T(1,128)S(1)}, f32[1,1,640]{2,1,0:T(1,128)S(1)}, f32[1,1,640]{2,1,0:T(1,128)S(1)}) custom-call(s32[3]{0:T(128)S(1)} %pad_add_fusion.refs_0_, bf16[328,768]{1,0:T(8,128)(2,1)S(1)} %collective-permute-done.6.refs_1_.refs_2_, bf16[768,640]{1,0:T(8,128)(2,1)S(1)} %get-tuple-element.192.refs_4_.refs_5_.refs_2_, ...), custom_call_target="tpu_custom_call" | custom-call | flops 1 | bytes 1024 | tf_op jit(solution)/shard_map/far/pallas_call | solution.py:364
  35.9 0.0 copy-start
  36.0 0.0 copy-start.1
  36.0 0.0 copy-start.2
  36.0 1.2 %collective-permute-done.11.refs_4_ = bf16[328,768]{1,0:T(8,128)(2,1)S(1)} collective-permute-done((bf16[328,768]{1,0:T(8,128)(2,1)S(1)}, bf16[328,768]{1,0:T(8,128)(2,1)S(1)}, u32[]{:S(2)}, u32[]{:S(2)}) %collective-permute-start.11) | collective-permute-done | bytes 503840 | tf_op jit(solution)/shard_map/ppermute | solution.py:431
  37.2 1.2 %last.1 = (f32[4,1,640]{2,1,0:T(1,128)S(1)}, f32[4,1,640]{2,1,0:T(1,128)S(1)}, f32[1,1,640]{2,1,0:T(1,128)S(1)}, f32[1,1,640]{2,1,0:T(1,128)S(1)}) custom-call(s32[3]{0:T(128)S(1)} %pad_add_fusion.refs_0_, bf16[328,768]{1,0:T(8,128)(2,1)S(1)} %collective-permute-done.5.refs_3_.refs_4_.refs_1_, bf16[328,768]{1,0:T(8,128)(2,1)S(1)} %collective-permute-done.6.refs_1_.refs_2_, ...), custom_call_target="tpu_custom_call" | custom-call | flops 1 | bytes 1024 | tf_op jit(solution)/shard_map/last/pallas_call | solution.py:364
  38.4 0.1 collective-permute-start.13
  38.5 2.3 %collective-permute-start.12 = (f32[1,1,640]{2,1,0:T(1,128)S(1)}, f32[1,1,640]{2,1,0:T(1,128)S(1)}, u32[]{:S(2)}, u32[]{:S(2)}) collective-permute-start(f32[1,1,640]{2,1,0:T(1,128)S(1)} %get-tuple-element.214.refs_0_), channel_id=1, source_target_pairs={{0,8},{1,9},{2,10},{3,11},{4,12},{5,13},{6,14},{7,15},{8,0},{9,1},... | collective-permute-start | bytes 7688 | tf_op jit(solution)/shard_map/ppermute | solution.py:431
  40.9 2.0 %collective-permute-start.17 = (f32[1,1,640]{2,1,0:T(1,128)S(1)}, f32[1,1,640]{2,1,0:T(1,128)S(1)}, u32[]{:S(2)}, u32[]{:S(2)}) collective-permute-start(f32[1,1,640]{2,1,0:T(1,128)S(1)} %get-tuple-element.240), channel_id=1, source_target_pairs={{0,6},{1,7},{2,4},{3,5},{4,2},{5,3},{6,0},{7,1},{8,14},{9,15},{10,... | collective-permute-start | bytes 7688 | tf_op jit(solution)/shard_map/ppermute | solution.py:431
  42.8 0.5 %collective-permute-start.16 = (f32[1,1,640]{2,1,0:T(1,128)S(1)}, f32[1,1,640]{2,1,0:T(1,128)S(1)}, u32[]{:S(2)}, u32[]{:S(2)}) collective-permute-start(f32[1,1,640]{2,1,0:T(1,128)S(1)} %get-tuple-element.241), channel_id=1, source_target_pairs={{0,2},{1,3},{2,0},{3,1},{4,6},{5,7},{6,4},{7,5},{8,10},{9,11},{10,... | collective-permute-start | bytes 7688 | tf_op jit(solution)/shard_map/ppermute | solution.py:431
  43.4 1.1 %collective-permute-start.15 = (f32[1,1,640]{2,1,0:T(1,128)S(1)}, f32[1,1,640]{2,1,0:T(1,128)S(1)}, u32[]{:S(2)}, u32[]{:S(2)}) collective-permute-start(f32[1,1,640]{2,1,0:T(1,128)S(1)} %get-tuple-element.242), channel_id=1, source_target_pairs={{0,4},{1,5},{2,6},{3,7},{4,0},{5,1},{6,2},{7,3},{8,12},{9,13},{10,... | collective-permute-start | bytes 7688 | tf_op jit(solution)/shard_map/ppermute | solution.py:431
  44.4 0.6 %decide.1 = s32[1]{0:T(128)} custom-call(f32[1,1,640]{2,1,0:T(1,128)S(1)} %get-tuple-element.214.refs_0_, f32[1,1,640]{2,1,0:T(1,128)S(1)} %collective-permute-done.12.refs_1_), custom_call_target="tpu_custom_call" | custom-call | tf_op jit(solution)/shard_map/decide/pallas_call | solution.py:403
  45.7 0.7 %collective-permute-done.16 = f32[1,1,640]{2,1,0:T(1,128)S(1)} collective-permute-done((f32[1,1,640]{2,1,0:T(1,128)S(1)}, f32[1,1,640]{2,1,0:T(1,128)S(1)}, u32[]{:S(2)}, u32[]{:S(2)}) %collective-permute-start.16) | collective-permute-done | bytes 2592 | tf_op jit(solution)/shard_map/ppermute | solution.py:431
  46.4 0.5 %collective-permute-done.15 = f32[1,1,640]{2,1,0:T(1,128)S(1)} collective-permute-done((f32[1,1,640]{2,1,0:T(1,128)S(1)}, f32[1,1,640]{2,1,0:T(1,128)S(1)}, u32[]{:S(2)}, u32[]{:S(2)}) %collective-permute-start.15) | collective-permute-done | bytes 2592 | tf_op jit(solution)/shard_map/ppermute | solution.py:431
  47.0 0.5 %conditional.1 = (f32[512]{0:T(512)S(1)}) conditional(s32[]{:T(128)} %bitcast.5, (f32[4,1,640]{2,1,0:T(1,128)S(1)}, f32[4,1,640]{2,1,0:T(1,128)S(1)}, s32[1,512]{1,0:T(1,128)S(1)}, f32[1,1,640]{2,1,0:T(1,128)S(1)}, f32[1,1,640]{2,1,0:T(1,128)S(1)}, /*index=5*/f32[1,1,640]{2,1,0:T(1,128)S(1)}, f32[1,1,640]{2,1,0:T(1,128)S(1)}, ...), branch_computations={%region_0.1_spmd, %region_1.8_spmd} | conditional | flops 1617953280 | bytes 16846124 | solution.py:482
  47.0 0.5 finish.1
  47.5 0.0 copy-start.3
  47.5 0.6 %copy-done.3 = f32[512]{0:T(512)} copy-done((f32[512]{0:T(512)}, f32[512]{0:T(512)S(1)}, u32[]{:S(2)}) %copy-start.3) | copy-done | bytes 2072
  (18 shorter events, 0.1 us)
Async XLA Ops:
  3.6 3.2 %collective-permute-start.3 = (bf16[328,768]{1,0:T(8,128)(2,1)S(1)}, bf16[328,768]{1,0:T(8,128)(2,1)S(1)}, u32[]{:S(2)}, u32[]{:S(2)}) collective-permute-start(bf16[328,768]{1,0:T(8,128)(2,1)S(1)} %get-tuple-element.185.refs_1_), channel_id=1, source_target_pairs={{0,1},{1,0},{2,3},{3,2},{4,5},{5,4},{6,7},{7,6},{8,9},{9,8},{10,11... | collective-permute-start | bytes 1511432 | tf_op jit(solution)/shard_map/ppermute | solution.py:431
  4.2 14.7 %collective-permute-start.7 = (bf16[328,768]{1,0:T(8,128)(2,1)S(1)}, bf16[328,768]{1,0:T(8,128)(2,1)S(1)}, u32[]{:S(2)}, u32[]{:S(2)}) collective-permute-start(bf16[328,768]{1,0:T(8,128)(2,1)S(1)} %get-tuple-element.186), channel_id=1, source_target_pairs={{0,4},{1,5},{2,6},{3,7},{4,0},{5,1},{6,2},{7,3},{8,12},{9,13},{10,... | collective-permute-start | bytes 1511432 | tf_op jit(solution)/shard_map/ppermute | solution.py:431
  6.8 16.4 %collective-permute-start.4 = (bf16[328,768]{1,0:T(8,128)(2,1)S(1)}, bf16[328,768]{1,0:T(8,128)(2,1)S(1)}, u32[]{:S(2)}, u32[]{:S(2)}) collective-permute-start(bf16[328,768]{1,0:T(8,128)(2,1)S(1)} %get-tuple-element.185.refs_1_), channel_id=1, source_target_pairs={{0,2},{1,3},{2,0},{3,1},{4,6},{5,7},{6,4},{7,5},{8,10},{9,11},{10,... | collective-permute-start | bytes 1511432 | tf_op jit(solution)/shard_map/ppermute | solution.py:431
  8.6 14.6 %collective-permute-start.5 = (bf16[328,768]{1,0:T(8,128)(2,1)S(1)}, bf16[328,768]{1,0:T(8,128)(2,1)S(1)}, u32[]{:S(2)}, u32[]{:S(2)}) collective-permute-start(bf16[328,768]{1,0:T(8,128)(2,1)S(1)} %get-tuple-element.186), channel_id=1, source_target_pairs={{0,1},{1,0},{2,3},{3,2},{4,8},{5,9},{6,10},{7,11},{8,4},{9,5},{10,... | collective-permute-start | bytes 1511432 | tf_op jit(solution)/shard_map/ppermute | solution.py:431
  18.9 4.3 %collective-permute-start.10 = (bf16[328,768]{1,0:T(8,128)(2,1)S(1)}, bf16[328,768]{1,0:T(8,128)(2,1)S(1)}, u32[]{:S(2)}, u32[]{:S(2)}) collective-permute-start(bf16[328,768]{1,0:T(8,128)(2,1)S(1)} %collective-permute-done.7.refs_1_.refs_3_), channel_id=1, source_target_pairs={{0,1},{1,0},{2,3},{3,2},{4,5},{5,4},{6,7},{7,6},{8,9},{9,8},{10,11... | collective-permute-start | bytes 1511432 | tf_op jit(solution)/shard_map/ppermute | solution.py:431
  18.9 16.4 %collective-permute-start.6 = (bf16[328,768]{1,0:T(8,128)(2,1)S(1)}, bf16[328,768]{1,0:T(8,128)(2,1)S(1)}, u32[]{:S(2)}, u32[]{:S(2)}) collective-permute-start(bf16[328,768]{1,0:T(8,128)(2,1)S(1)} %get-tuple-element.185.refs_1_), channel_id=1, source_target_pairs={{0,8},{1,9},{2,10},{3,11},{4,0},{5,1},{6,2},{7,3},{8,12},{9,13},{1... | collective-permute-start | bytes 1511432 | tf_op jit(solution)/shard_map/ppermute | solution.py:431
  21.7 13.6 %collective-permute-start.8 = (bf16[328,768]{1,0:T(8,128)(2,1)S(1)}, bf16[328,768]{1,0:T(8,128)(2,1)S(1)}, u32[]{:S(2)}, u32[]{:S(2)}) collective-permute-start(bf16[328,768]{1,0:T(8,128)(2,1)S(1)} %collective-permute-done.7.refs_1_.refs_3_), channel_id=1, source_target_pairs={{0,2},{1,3},{2,0},{3,1},{4,6},{5,7},{6,4},{7,5},{8,10},{9,11},{10,... | collective-permute-start | bytes 1511432 | tf_op jit(solution)/shard_map/ppermute | solution.py:431
  23.2 1.9 %collective-permute-start.9 = (bf16[328,768]{1,0:T(8,128)(2,1)S(1)}, bf16[328,768]{1,0:T(8,128)(2,1)S(1)}, u32[]{:S(2)}, u32[]{:S(2)}) collective-permute-start(bf16[328,768]{1,0:T(8,128)(2,1)S(1)} %collective-permute-done.4.refs_1_), channel_id=1, source_target_pairs={{0,1},{1,0},{2,3},{3,2},{4,5},{5,4},{6,7},{7,6},{8,9},{9,8},{10,11... | collective-permute-start | bytes 1511432 | tf_op jit(solution)/shard_map/ppermute | solution.py:431
  35.3 1.9 %collective-permute-start.11 = (bf16[328,768]{1,0:T(8,128)(2,1)S(1)}, bf16[328,768]{1,0:T(8,128)(2,1)S(1)}, u32[]{:S(2)}, u32[]{:S(2)}) collective-permute-start(bf16[328,768]{1,0:T(8,128)(2,1)S(1)} %collective-permute-done.8.refs_3_), channel_id=1, source_target_pairs={{0,1},{1,0},{2,3},{3,2},{4,5},{5,4},{6,7},{7,6},{8,9},{9,8},{10,11... | collective-permute-start | bytes 1511432 | tf_op jit(solution)/shard_map/ppermute | solution.py:431
  35.9 11.0 %copy-start = (bf16[1024,768]{1,0:T(8,128)(2,1)S(1)}, bf16[1024,768]{1,0:T(8,128)(2,1)}, u32[]{:S(2)}) copy-start(bf16[1024,768]{1,0:T(8,128)(2,1)} %refs_3_.1) | copy-start | bytes 4718596
  36.0 11.0 %copy-start.1 = (bf16[512,1024]{1,0:T(8,128)(2,1)S(1)}, bf16[512,1024]{1,0:T(8,128)(2,1)}, u32[]{:S(2)}) copy-start(bf16[512,1024]{1,0:T(8,128)(2,1)} %refs_2_.1) | copy-start | bytes 3145732
  36.0 11.0 %copy-start.2 = (s32[512]{0:T(512)S(1)}, s32[512]{0:T(512)}, u32[]{:S(2)}) copy-start(s32[512]{0:T(512)} %param.9) | copy-start | bytes 6148
  38.4 2.5 %collective-permute-start.13 = (f32[4,1,640]{2,1,0:T(1,128)S(1)}, f32[4,1,640]{2,1,0:T(1,128)S(1)}, u32[]{:S(2)}, u32[]{:S(2)}) collective-permute-start(f32[4,1,640]{2,1,0:T(1,128)S(1)} %get-tuple-element.216), channel_id=1, source_target_pairs={{0,1},{1,0},{2,3},{3,2},{4,5},{5,4},{6,7},{7,6},{8,9},{9,8},{10,11... | collective-permute-start | bytes 30728 | tf_op jit(solution)/shard_map/ppermute | solution.py:431
  38.5 5.9 %collective-permute-start.12 = (f32[1,1,640]{2,1,0:T(1,128)S(1)}, f32[1,1,640]{2,1,0:T(1,128)S(1)}, u32[]{:S(2)}, u32[]{:S(2)}) collective-permute-start(f32[1,1,640]{2,1,0:T(1,128)S(1)} %get-tuple-element.214.refs_0_), channel_id=1, source_target_pairs={{0,8},{1,9},{2,10},{3,11},{4,12},{5,13},{6,14},{7,15},{8,0},{9,1},... | collective-permute-start | bytes 7688 | tf_op jit(solution)/shard_map/ppermute | solution.py:431
  40.9 4.8 %collective-permute-start.17 = (f32[1,1,640]{2,1,0:T(1,128)S(1)}, f32[1,1,640]{2,1,0:T(1,128)S(1)}, u32[]{:S(2)}, u32[]{:S(2)}) collective-permute-start(f32[1,1,640]{2,1,0:T(1,128)S(1)} %get-tuple-element.240), channel_id=1, source_target_pairs={{0,6},{1,7},{2,4},{3,5},{4,2},{5,3},{6,0},{7,1},{8,14},{9,15},{10,... | collective-permute-start | bytes 7688 | tf_op jit(solution)/shard_map/ppermute | solution.py:431
  42.8 3.6 %collective-permute-start.16 = (f32[1,1,640]{2,1,0:T(1,128)S(1)}, f32[1,1,640]{2,1,0:T(1,128)S(1)}, u32[]{:S(2)}, u32[]{:S(2)}) collective-permute-start(f32[1,1,640]{2,1,0:T(1,128)S(1)} %get-tuple-element.241), channel_id=1, source_target_pairs={{0,2},{1,3},{2,0},{3,1},{4,6},{5,7},{6,4},{7,5},{8,10},{9,11},{10,... | collective-permute-start | bytes 7688 | tf_op jit(solution)/shard_map/ppermute | solution.py:431
  43.4 3.6 %collective-permute-start.15 = (f32[1,1,640]{2,1,0:T(1,128)S(1)}, f32[1,1,640]{2,1,0:T(1,128)S(1)}, u32[]{:S(2)}, u32[]{:S(2)}) collective-permute-start(f32[1,1,640]{2,1,0:T(1,128)S(1)} %get-tuple-element.242), channel_id=1, source_target_pairs={{0,4},{1,5},{2,6},{3,7},{4,0},{5,1},{6,2},{7,3},{8,12},{9,13},{10,... | collective-permute-start | bytes 7688 | tf_op jit(solution)/shard_map/ppermute | solution.py:431
  44.4 2.5 %collective-permute-start.14 = (f32[1,1,640]{2,1,0:T(1,128)S(1)}, f32[1,1,640]{2,1,0:T(1,128)S(1)}, u32[]{:S(2)}, u32[]{:S(2)}) collective-permute-start(f32[1,1,640]{2,1,0:T(1,128)S(1)} %get-tuple-element.220), channel_id=1, source_target_pairs={{0,1},{1,0},{2,3},{3,2},{4,8},{5,9},{6,10},{7,11},{8,4},{9,5},{10,... | collective-permute-start | bytes 7688 | tf_op jit(solution)/shard_map/ppermute | solution.py:431
  47.5 0.6 %copy-start.3 = (f32[512]{0:T(512)}, f32[512]{0:T(512)S(1)}, u32[]{:S(2)}) copy-start(f32[512]{0:T(512)S(1)} %get-tuple-element.356) | copy-start | bytes 6148

commit v15 on v14

--- a/solution.py
+++ b/solution.py
@@ -147,10 +147,20 @@
     return rest, first, flag, up(flag + 1, 128)
 
 
-def prep_kernel(hot, place_ref, cl_ref, st_ref, w_ref, same_ref, other_ref, slot_ref, vectors):
+def prep_kernel(hot, place_ref, cl_ref, st_hbm, w_hbm, same_ref, other_ref, slot_ref, vectors, st_ref, w_ref, half, sems):
     docs = st_ref.shape[0]
     rest, first, flag, lanes = layout(docs, hot)
     tile = 128
+    depth = st_ref.shape[1] // 2
+    copies = []
+    for k in (0, 1):
+        span = pl.ds(k * depth, depth)
+        copies.append((
+            pltpu.make_async_copy(w_hbm.at[span, :], w_ref.at[span, :], sems.at[2 * k]),
+            pltpu.make_async_copy(st_hbm.at[:, span], st_ref.at[:, span], sems.at[2 * k + 1]),
+        ))
+        for copy in copies[k]:
+            copy.start()
 
     cluster = cl_ref[...]
     group = cluster // CLUS_OWN
@@ -162,11 +172,19 @@
     doubt = jnp.where(jnp.sum(full.astype(F32), axis=0, keepdims=True) == 1.0, 0.0, 1.0)
     in_hot = group == chosen
 
-    for t in range(docs // tile):
-        rows = slice(t * tile, (t + 1) * tile)
-        projected = jnp.dot(st_ref[rows, :], w_ref[...], preferred_element_type=F32)
-        norm = lax.rsqrt(jnp.sum(projected * projected, axis=1, keepdims=True) + EPS)
-        vectors[rows, :] = (projected * (norm * math.sqrt(SCALE))).astype(BF16)
+    for k in (0, 1):
+        for copy in copies[k]:
+            copy.wait()
+        span = slice(k * depth, (k + 1) * depth)
+        for t in range(docs // tile):
+            rows = slice(t * tile, (t + 1) * tile)
+            projected = jnp.dot(st_ref[rows, span], w_ref[span, :], preferred_element_type=F32)
+            if k == 0:
+                half[rows, :] = projected
+            else:
+                projected += half[rows, :]
+                norm = lax.rsqrt(jnp.sum(projected * projected, axis=1, keepdims=True) + EPS)
+                vectors[rows, :] = (projected * (norm * math.sqrt(SCALE))).astype(BF16)
 
     ahead = (
         lax.broadcasted_iota(jnp.int32, (docs, docs), 0) < lax.broadcasted_iota(jnp.int32, (docs, docs), 1)
@@ -224,8 +242,11 @@
             shape((rest + META, width), BF16),
             shape((1, docs), jnp.int32),
         ),
-        in_specs=[pl.BlockSpec(memory_space=pltpu.SMEM), vmem, vmem, vmem],
-        scratch_shapes=[pltpu.VMEM((docs, width), BF16)],
+        in_specs=[pl.BlockSpec(memory_space=pltpu.SMEM), vmem] + [pl.BlockSpec(memory_space=pl.ANY)] * 2,
+        scratch_shapes=[
+            pltpu.VMEM((docs, width), BF16), pltpu.VMEM(states.shape, BF16), pltpu.VMEM(proj_weight.shape, BF16),
+            pltpu.VMEM((docs, width), F32), pltpu.SemaphoreType.DMA((4,)),
+        ],
         compiler_params=pltpu.CompilerParams(vmem_limit_bytes=24 * 2**20),
         name="prep",
     )(place, cluster_of.reshape(1, docs), states, proj_weight)
@@ -353,7 +374,9 @@
 
 def score(name, docs, hot, place, blocks, pairs, made, tasks, sums, doubted=(), weight=1):
     rest, _, _, lanes = layout(docs, hot)
-    names = list(dict.fromkeys([*made, *(name for task in tasks for name in task[0])]))
+    names = list(dict.fromkeys([
+        *made, *(name for task in tasks for name in task[0]), *(task[1] for task in tasks if task[1] in blocks),
+    ]))
     given = [p for p in pairs if any(p == task[1] for task in tasks)]
     width = blocks[OWN].shape[1]
     vmem = pl.BlockSpec(memory_space=pltpu.VMEM)
@@ -463,17 +486,22 @@
     )
     blocks[PAIR_ROW], _ = lax.optimization_barrier((blocks[PAIR_ROW], sums[0]))
     blocks[PAIR_DIAG] = move(blocks[PAIR_ROW], STAY, core=1)
-    sums, pairs = meet("far", (), [((FAR,), p, True, None) for p in (HERE, THERE, ACROSS)])
+    sums, pairs = meet(
+        "far", (),
+        [((FAR,), p, True, None) for p in (HERE, THERE, ACROSS)]
+        + [((NEXT, FAR), PAIR_ROW, False, None), ((PAIR_ROW,), THERE, False, "row1")],
+        doubted=(PAIR_ROW,),
+    )
     sums, pairs = meet(
         "last", (),
-        [((NEXT, FAR), right, False, None) for right in (PAIR_ROW, PAIR_DIAG)]
-        + [((PAIR_ROW,), THERE, False, "row1"), ((PAIR_DIAG,), THERE, False, "row0")],
-        doubted=(PAIR_ROW, PAIR_DIAG),
+        [((NEXT, FAR), PAIR_DIAG, False, None), ((PAIR_DIAG,), THERE, False, "row0")],
+        doubted=(PAIR_DIAG,),
     )
     kept, by_core, to_next, to_far = sums
     from_core, from_far = move(by_core, STAY, core=1), move(to_far, TWO)
     from_core, to_next = lax.optimization_barrier((from_core, to_next))
     from_next = move(to_next, MIDDLE)
+    from_next, from_far = lax.optimization_barrier((from_next, from_far))
     own, pair, row, pair_row = (kept[k:k + 1] + from_core[k:k + 1] for k in (0, 1, 2, 3))
     home = [
         own, from_next, from_far,

time: 48.2 us -> 49.2 us (1.021)
  Pallas kernels: 10.7 us -> 11.3 us
  transfers between devices with their start and end apart: 15 -> 15, of which waited for: 6 -> 6; matrix products, arithmetic and copies ran while one was open for 0% -> 0% of each run, Pallas kernels for 11% -> 12%
where the time goes in v15:
time: 49.2 us; the launch traced here: 49.1 us
  waiting for transfers between devices  20.8 us (42%)
  starting transfers between devices  15.5 us (32%)
  Pallas kernels  11.3 us (23%)
  between operations  0.73 us (1%)
  local copies, waits for them, and re-layouts  0.58 us (1%)
    ppermute x15, waiting for transfers between devices, move(): return lax.ppermute(a, ('owner', 'split'), pairs)  20.8 us
    ppermute x15, starting transfers between devices, move(): return lax.ppermute(a, ('owner', 'split'), pairs)  15.5 us
    pallas_call x5, Pallas kernels, score(): pl.pallas_call(lambda *refs: score_kernel(docs, hot, names, given, made,...  6.31 us
    pallas_call x1, Pallas kernels, prep(): pl.pallas_call(lambda *refs: prep_kernel(hot, *refs), out_shape=(shape((r...  3.91 us
  transfers between devices with their start and end apart: 15, of which 6 were waited for; matrix products, arithmetic and copies ran while one was open for 0% of the time, Pallas kernels for 12%

profile of v15, /device:TPU:0, one launch (start us, length us, event | category | flops | bytes accessed | tf_op | source)
XLA Modules:
  0.0 49.1 jit_solution(5267533725157275965)
XLA Ops:
  0.0 0.1 pad_add_fusion.refs_0_
  0.1 3.9 %prep.1 = (bf16[328,768]{1,0:T(8,128)(2,1)S(1)}, bf16[328,768]{1,0:T(8,128)(2,1)S(1)}, s32[1,512]{1,0:T(1,128)S(1)}) custom-call(s32[3]{0:T(128)S(1)} %pad_add_fusion.refs_0_, s32[1,512]{1,0:T(1,128)} %bitcast.16, bf16[512,1024]{1,0:T(8,128)(2,1)} %refs_2_.1, bf16[1024,768]{1,0:T(8,128)(2,1)} %refs_3_.1), custom_call_target="tpu_custom_call" | custom-call | tf_op jit(solution)/shard_map/prep/pallas_call | solution.py:238
  4.0 0.5 %collective-permute-start.3 = (bf16[328,768]{1,0:T(8,128)(2,1)S(1)}, bf16[328,768]{1,0:T(8,128)(2,1)S(1)}, u32[]{:S(2)}, u32[]{:S(2)}) collective-permute-start(bf16[328,768]{1,0:T(8,128)(2,1)S(1)} %get-tuple-element.187.refs_1_), channel_id=1, source_target_pairs={{0,1},{1,0},{2,3},{3,2},{4,5},{5,4},{6,7},{7,6},{8,9},{9,8},{10,11... | collective-permute-start | bytes 1511432 | tf_op jit(solution)/shard_map/ppermute | solution.py:454
  4.5 2.6 %collective-permute-start.7 = (bf16[328,768]{1,0:T(8,128)(2,1)S(1)}, bf16[328,768]{1,0:T(8,128)(2,1)S(1)}, u32[]{:S(2)}, u32[]{:S(2)}) collective-permute-start(bf16[328,768]{1,0:T(8,128)(2,1)S(1)} %get-tuple-element.188), channel_id=1, source_target_pairs={{0,4},{1,5},{2,6},{3,7},{4,0},{5,1},{6,2},{7,3},{8,12},{9,13},{10,... | collective-permute-start | bytes 1511432 | tf_op jit(solution)/shard_map/ppermute | solution.py:454
  7.2 1.7 %collective-permute-start.4 = (bf16[328,768]{1,0:T(8,128)(2,1)S(1)}, bf16[328,768]{1,0:T(8,128)(2,1)S(1)}, u32[]{:S(2)}, u32[]{:S(2)}) collective-permute-start(bf16[328,768]{1,0:T(8,128)(2,1)S(1)} %get-tuple-element.187.refs_1_), channel_id=1, source_target_pairs={{0,2},{1,3},{2,0},{3,1},{4,6},{5,7},{6,4},{7,5},{8,10},{9,11},{10,... | collective-permute-start | bytes 1511432 | tf_op jit(solution)/shard_map/ppermute | solution.py:454
  8.9 0.0 collective-permute-start.5
  8.9 1.4 %own.1 = (f32[4,1,640]{2,1,0:T(1,128)S(1)}, f32[4,1,640]{2,1,0:T(1,128)S(1)}, f32[1,1,640]{2,1,0:T(1,128)S(1)}, f32[1,1,640]{2,1,0:T(1,128)S(1)}, bf16[768,640]{1,0:T(8,128)(2,1)S(1)}, /*index=5*/f32[8,640]{1,0:T(8,128)S(1)}) custom-call(s32[3]{0:T(128)S(1)} %pad_add_fusion.refs_0_, bf16[328,768]{1,0:T(8,128)(2,1)S(1)} %get-tuple-element.187.refs_1_, ...), custom_call_target="tpu_custom_call" | custom-call | flops 8589934592 | bytes 1024 | tf_op jit(solution)/shard_map/own/pallas_call | solution.py:387
  10.3 8.9 %collective-permute-done.7.refs_1_.refs_3_ = bf16[328,768]{1,0:T(8,128)(2,1)S(1)} collective-permute-done((bf16[328,768]{1,0:T(8,128)(2,1)S(1)}, bf16[328,768]{1,0:T(8,128)(2,1)S(1)}, u32[]{:S(2)}, u32[]{:S(2)}) %collective-permute-start.7) | collective-permute-done | bytes 503840 | tf_op jit(solution)/shard_map/ppermute | solution.py:454
  19.2 2.8 %collective-permute-start.6 = (bf16[328,768]{1,0:T(8,128)(2,1)S(1)}, bf16[328,768]{1,0:T(8,128)(2,1)S(1)}, u32[]{:S(2)}, u32[]{:S(2)}) collective-permute-start(bf16[328,768]{1,0:T(8,128)(2,1)S(1)} %get-tuple-element.187.refs_1_), channel_id=1, source_target_pairs={{0,8},{1,9},{2,10},{3,11},{4,0},{5,1},{6,2},{7,3},{8,12},{9,13},{1... | collective-permute-start | bytes 1511432 | tf_op jit(solution)/shard_map/ppermute | solution.py:454
  22.0 1.5 %collective-permute-start.8 = (bf16[328,768]{1,0:T(8,128)(2,1)S(1)}, bf16[328,768]{1,0:T(8,128)(2,1)S(1)}, u32[]{:S(2)}, u32[]{:S(2)}) collective-permute-start(bf16[328,768]{1,0:T(8,128)(2,1)S(1)} %collective-permute-done.7.refs_1_.refs_3_), channel_id=1, source_target_pairs={{0,2},{1,3},{2,0},{3,1},{4,6},{5,7},{6,4},{7,5},{8,10},{9,11},{10,... | collective-permute-start | bytes 1511432 | tf_op jit(solution)/shard_map/ppermute | solution.py:454
  23.5 0.0 collective-permute-done.10.refs_2_
  23.6 1.1 %pair.1 = (f32[4,1,640]{2,1,0:T(1,128)S(1)}, f32[4,1,640]{2,1,0:T(1,128)S(1)}, f32[1,1,640]{2,1,0:T(1,128)S(1)}, f32[1,1,640]{2,1,0:T(1,128)S(1)}, bf16[768,640]{1,0:T(8,128)(2,1)S(1)}, /*index=5*/f32[8,640]{1,0:T(8,128)S(1)}) custom-call(s32[3]{0:T(128)S(1)} %pad_add_fusion.refs_0_, bf16[328,768]{1,0:T(8,128)(2,1)S(1)} %collective-permute-done.7.refs_1_.refs_3_, ...), custom_call_target="tpu_custom_call" | custom-call | flops 8589934592 | bytes 1024 | tf_op jit(solution)/shard_map/pair/pallas_call | solution.py:387
  24.6 0.8 %collective-permute-done.9.refs_2_ = bf16[328,768]{1,0:T(8,128)(2,1)S(1)} collective-permute-done((bf16[328,768]{1,0:T(8,128)(2,1)S(1)}, bf16[328,768]{1,0:T(8,128)(2,1)S(1)}, u32[]{:S(2)}, u32[]{:S(2)}) %collective-permute-start.9) | collective-permute-done | bytes 503840 | tf_op jit(solution)/shard_map/ppermute | solution.py:454
  25.4 1.8 %row.1 = (f32[4,1,640]{2,1,0:T(1,128)S(1)}, f32[4,1,640]{2,1,0:T(1,128)S(1)}, f32[1,1,640]{2,1,0:T(1,128)S(1)}, f32[1,1,640]{2,1,0:T(1,128)S(1)}, bf16[768,640]{1,0:T(8,128)(2,1)S(1)}, /*index=5*/f32[8,640]{1,0:T(8,128)S(1)}) custom-call(s32[3]{0:T(128)S(1)} %pad_add_fusion.refs_0_, bf16[328,768]{1,0:T(8,128)(2,1)S(1)} %collective-permute-done.4.refs_1_, ...), custom_call_target="tpu_custom_call" | custom-call | flops 1 | bytes 1024 | tf_op jit(solution)/shard_map/row/pallas_call | solution.py:387
  27.2 8.4 %collective-permute-done.8.refs_3_ = bf16[328,768]{1,0:T(8,128)(2,1)S(1)} collective-permute-done((bf16[328,768]{1,0:T(8,128)(2,1)S(1)}, bf16[328,768]{1,0:T(8,128)(2,1)S(1)}, u32[]{:S(2)}, u32[]{:S(2)}) %collective-permute-start.8) | collective-permute-done | bytes 503840 | tf_op jit(solution)/shard_map/ppermute | solution.py:454
  35.6 0.0 collective-permute-start.11
  35.6 0.9 %far.1 = (f32[4,1,640]{2,1,0:T(1,128)S(1)}, f32[4,1,640]{2,1,0:T(1,128)S(1)}, f32[1,1,640]{2,1,0:T(1,128)S(1)}, f32[1,1,640]{2,1,0:T(1,128)S(1)}) custom-call(s32[3]{0:T(128)S(1)} %pad_add_fusion.refs_0_, bf16[328,768]{1,0:T(8,128)(2,1)S(1)} %collective-permute-done.6.refs_1_.refs_2_, ...), custom_call_target="tpu_custom_call" | custom-call | flops 1 | bytes 1024 | tf_op jit(solution)/shard_map/far/pallas_call | solution.py:387
  36.6 0.9 %collective-permute-done.11.refs_3_ = bf16[328,768]{1,0:T(8,128)(2,1)S(1)} collective-permute-done((bf16[328,768]{1,0:T(8,128)(2,1)S(1)}, bf16[328,768]{1,0:T(8,128)(2,1)S(1)}, u32[]{:S(2)}, u32[]{:S(2)}) %collective-permute-start.11) | collective-permute-done | bytes 503840 | tf_op jit(solution)/shard_map/ppermute | solution.py:454
  37.5 1.1 %last.1 = (f32[4,1,640]{2,1,0:T(1,128)S(1)}, f32[4,1,640]{2,1,0:T(1,128)S(1)}, f32[1,1,640]{2,1,0:T(1,128)S(1)}, f32[1,1,640]{2,1,0:T(1,128)S(1)}) custom-call(s32[3]{0:T(128)S(1)} %pad_add_fusion.refs_0_, bf16[328,768]{1,0:T(8,128)(2,1)S(1)} %collective-permute-done.5.refs_3_.refs_4_.refs_2_.refs_1_, ...), custom_call_target="tpu_custom_call" | custom-call | flops 1 | bytes 1024 | tf_op jit(solution)/shard_map/last/pallas_call | solution.py:387
  38.7 0.1 collective-permute-start.12
  38.8 2.6 %collective-permute-start.14 = (f32[1,1,640]{2,1,0:T(1,128)S(1)}, f32[1,1,640]{2,1,0:T(1,128)S(1)}, u32[]{:S(2)}, u32[]{:S(2)}) collective-permute-start(f32[1,1,640]{2,1,0:T(1,128)S(1)} %get-tuple-element.216.refs_0_), channel_id=1, source_target_pairs={{0,8},{1,9},{2,10},{3,11},{4,12},{5,13},{6,14},{7,15},{8,0},{9,1},... | collective-permute-start | bytes 7688 | tf_op jit(solution)/shard_map/ppermute | solution.py:454
  41.4 0.0 collective-permute-done.12
  41.4 2.4 %collective-permute-start.17 = (f32[1,1,640]{2,1,0:T(1,128)S(1)}, f32[1,1,640]{2,1,0:T(1,128)S(1)}, u32[]{:S(2)}, u32[]{:S(2)}) collective-permute-start(f32[1,1,640]{2,1,0:T(1,128)S(1)} %get-tuple-element.244), channel_id=1, source_target_pairs={{0,6},{1,7},{2,4},{3,5},{4,2},{5,3},{6,0},{7,1},{8,14},{9,15},{10,... | collective-permute-start | bytes 7688 | tf_op jit(solution)/shard_map/ppermute | solution.py:454
  43.9 0.5 %collective-permute-start.16 = (f32[1,1,640]{2,1,0:T(1,128)S(1)}, f32[1,1,640]{2,1,0:T(1,128)S(1)}, u32[]{:S(2)}, u32[]{:S(2)}) collective-permute-start(f32[1,1,640]{2,1,0:T(1,128)S(1)} %get-tuple-element.245), channel_id=1, source_target_pairs={{0,2},{1,3},{2,0},{3,1},{4,6},{5,7},{6,4},{7,5},{8,10},{9,11},{10,... | collective-permute-start | bytes 7688 | tf_op jit(solution)/shard_map/ppermute | solution.py:454
  44.4 0.6 %collective-permute-start.15 = (f32[1,1,640]{2,1,0:T(1,128)S(1)}, f32[1,1,640]{2,1,0:T(1,128)S(1)}, u32[]{:S(2)}, u32[]{:S(2)}) collective-permute-start(f32[1,1,640]{2,1,0:T(1,128)S(1)} %get-tuple-element.246), channel_id=1, source_target_pairs={{0,4},{1,5},{2,6},{3,7},{4,0},{5,1},{6,2},{7,3},{8,12},{9,13},{10,... | collective-permute-start | bytes 7688 | tf_op jit(solution)/shard_map/ppermute | solution.py:454
  45.0 0.6 %decide.1 = s32[1]{0:T(128)} custom-call(f32[1,1,640]{2,1,0:T(1,128)S(1)} %get-tuple-element.216.refs_0_, f32[1,1,640]{2,1,0:T(1,128)S(1)} %collective-permute-done.14.refs_1_), custom_call_target="tpu_custom_call" | custom-call | tf_op jit(solution)/shard_map/decide/pallas_call | solution.py:426
  46.3 1.1 %collective-permute-done.16 = f32[1,1,640]{2,1,0:T(1,128)S(1)} collective-permute-done((f32[1,1,640]{2,1,0:T(1,128)S(1)}, f32[1,1,640]{2,1,0:T(1,128)S(1)}, u32[]{:S(2)}, u32[]{:S(2)}) %collective-permute-start.16) | collective-permute-done | bytes 2592 | tf_op jit(solution)/shard_map/ppermute | solution.py:454
  47.4 0.5 %collective-permute-done.15 = f32[1,1,640]{2,1,0:T(1,128)S(1)} collective-permute-done((f32[1,1,640]{2,1,0:T(1,128)S(1)}, f32[1,1,640]{2,1,0:T(1,128)S(1)}, u32[]{:S(2)}, u32[]{:S(2)}) %collective-permute-start.15) | collective-permute-done | bytes 2592 | tf_op jit(solution)/shard_map/ppermute | solution.py:454
  48.0 0.5 %conditional.1 = (f32[512]{0:T(512)S(1)}) conditional(s32[]{:T(128)} %bitcast.5, (f32[4,1,640]{2,1,0:T(1,128)S(1)}, f32[4,1,640]{2,1,0:T(1,128)S(1)}, s32[1,512]{1,0:T(1,128)S(1)}, f32[1,1,640]{2,1,0:T(1,128)S(1)}, f32[1,1,640]{2,1,0:T(1,128)S(1)}, /*index=5*/f32[1,1,640]{2,1,0:T(1,128)S(1)}, f32[1,1,640]{2,1,0:T(1,128)S(1)}, ...), branch_computations={%region_0.1_spmd, %region_1.8_spmd} | conditional | flops 1617953280 | bytes 16846124 | solution.py:510
  48.0 0.5 finish.1
  48.5 0.0 copy-start.3
  48.5 0.6 %copy-done.3 = f32[512]{0:T(512)} copy-done((f32[512]{0:T(512)}, f32[512]{0:T(512)S(1)}, u32[]{:S(2)}) %copy-start.3) | copy-done | bytes 2072
  (18 shorter events, 0.1 us)
Async XLA Ops:
  4.0 3.2 %collective-permute-start.3 = (bf16[328,768]{1,0:T(8,128)(2,1)S(1)}, bf16[328,768]{1,0:T(8,128)(2,1)S(1)}, u32[]{:S(2)}, u32[]{:S(2)}) collective-permute-start(bf16[328,768]{1,0:T(8,128)(2,1)S(1)} %get-tuple-element.187.refs_1_), channel_id=1, source_target_pairs={{0,1},{1,0},{2,3},{3,2},{4,5},{5,4},{6,7},{7,6},{8,9},{9,8},{10,11... | collective-permute-start | bytes 1511432 | tf_op jit(solution)/shard_map/ppermute | solution.py:454
  4.5 14.7 %collective-permute-start.7 = (bf16[328,768]{1,0:T(8,128)(2,1)S(1)}, bf16[328,768]{1,0:T(8,128)(2,1)S(1)}, u32[]{:S(2)}, u32[]{:S(2)}) collective-permute-start(bf16[328,768]{1,0:T(8,128)(2,1)S(1)} %get-tuple-element.188), channel_id=1, source_target_pairs={{0,4},{1,5},{2,6},{3,7},{4,0},{5,1},{6,2},{7,3},{8,12},{9,13},{10,... | collective-permute-start | bytes 1511432 | tf_op jit(solution)/shard_map/ppermute | solution.py:454
  7.2 16.4 %collective-permute-start.4 = (bf16[328,768]{1,0:T(8,128)(2,1)S(1)}, bf16[328,768]{1,0:T(8,128)(2,1)S(1)}, u32[]{:S(2)}, u32[]{:S(2)}) collective-permute-start(bf16[328,768]{1,0:T(8,128)(2,1)S(1)} %get-tuple-element.187.refs_1_), channel_id=1, source_target_pairs={{0,2},{1,3},{2,0},{3,1},{4,6},{5,7},{6,4},{7,5},{8,10},{9,11},{10,... | collective-permute-start | bytes 1511432 | tf_op jit(solution)/shard_map/ppermute | solution.py:454
  8.9 14.6 %collective-permute-start.5 = (bf16[328,768]{1,0:T(8,128)(2,1)S(1)}, bf16[328,768]{1,0:T(8,128)(2,1)S(1)}, u32[]{:S(2)}, u32[]{:S(2)}) collective-permute-start(bf16[328,768]{1,0:T(8,128)(2,1)S(1)} %get-tuple-element.188), channel_id=1, source_target_pairs={{0,1},{1,0},{2,3},{3,2},{4,8},{5,9},{6,10},{7,11},{8,4},{9,5},{10,... | collective-permute-start | bytes 1511432 | tf_op jit(solution)/shard_map/ppermute | solution.py:454
  19.2 4.3 %collective-permute-start.10 = (bf16[328,768]{1,0:T(8,128)(2,1)S(1)}, bf16[328,768]{1,0:T(8,128)(2,1)S(1)}, u32[]{:S(2)}, u32[]{:S(2)}) collective-permute-start(bf16[328,768]{1,0:T(8,128)(2,1)S(1)} %collective-permute-done.7.refs_1_.refs_3_), channel_id=1, source_target_pairs={{0,1},{1,0},{2,3},{3,2},{4,5},{5,4},{6,7},{7,6},{8,9},{9,8},{10,11... | collective-permute-start | bytes 1511432 | tf_op jit(solution)/shard_map/ppermute | solution.py:454
  19.2 16.4 %collective-permute-start.6 = (bf16[328,768]{1,0:T(8,128)(2,1)S(1)}, bf16[328,768]{1,0:T(8,128)(2,1)S(1)}, u32[]{:S(2)}, u32[]{:S(2)}) collective-permute-start(bf16[328,768]{1,0:T(8,128)(2,1)S(1)} %get-tuple-element.187.refs_1_), channel_id=1, source_target_pairs={{0,8},{1,9},{2,10},{3,11},{4,0},{5,1},{6,2},{7,3},{8,12},{9,13},{1... | collective-permute-start | bytes 1511432 | tf_op jit(solution)/shard_map/ppermute | solution.py:454
  22.0 13.6 %collective-permute-start.8 = (bf16[328,768]{1,0:T(8,128)(2,1)S(1)}, bf16[328,768]{1,0:T(8,128)(2,1)S(1)}, u32[]{:S(2)}, u32[]{:S(2)}) collective-permute-start(bf16[328,768]{1,0:T(8,128)(2,1)S(1)} %collective-permute-done.7.refs_1_.refs_3_), channel_id=1, source_target_pairs={{0,2},{1,3},{2,0},{3,1},{4,6},{5,7},{6,4},{7,5},{8,10},{9,11},{10,... | collective-permute-start | bytes 1511432 | tf_op jit(solution)/shard_map/ppermute | solution.py:454
  23.5 1.9 %collective-permute-start.9 = (bf16[328,768]{1,0:T(8,128)(2,1)S(1)}, bf16[328,768]{1,0:T(8,128)(2,1)S(1)}, u32[]{:S(2)}, u32[]{:S(2)}) collective-permute-start(bf16[328,768]{1,0:T(8,128)(2,1)S(1)} %collective-permute-done.4.refs_1_), channel_id=1, source_target_pairs={{0,1},{1,0},{2,3},{3,2},{4,5},{5,4},{6,7},{7,6},{8,9},{9,8},{10,11... | collective-permute-start | bytes 1511432 | tf_op jit(solution)/shard_map/ppermute | solution.py:454
  35.6 1.9 %collective-permute-start.11 = (bf16[328,768]{1,0:T(8,128)(2,1)S(1)}, bf16[328,768]{1,0:T(8,128)(2,1)S(1)}, u32[]{:S(2)}, u32[]{:S(2)}) collective-permute-start(bf16[328,768]{1,0:T(8,128)(2,1)S(1)} %collective-permute-done.8.refs_3_), channel_id=1, source_target_pairs={{0,1},{1,0},{2,3},{3,2},{4,5},{5,4},{6,7},{7,6},{8,9},{9,8},{10,11... | collective-permute-start | bytes 1511432 | tf_op jit(solution)/shard_map/ppermute | solution.py:454
  35.6 12.3 %copy-start.1 = (bf16[512,1024]{1,0:T(8,128)(2,1)S(1)}, bf16[512,1024]{1,0:T(8,128)(2,1)}, u32[]{:S(2)}) copy-start(bf16[512,1024]{1,0:T(8,128)(2,1)} %refs_2_.1) | copy-start | bytes 3145732
  36.6 11.4 %copy-start = (bf16[1024,768]{1,0:T(8,128)(2,1)S(1)}, bf16[1024,768]{1,0:T(8,128)(2,1)}, u32[]{:S(2)}) copy-start(bf16[1024,768]{1,0:T(8,128)(2,1)} %refs_3_.1) | copy-start | bytes 4718596
  36.6 11.4 %copy-start.2 = (s32[512]{0:T(512)S(1)}, s32[512]{0:T(512)}, u32[]{:S(2)}) copy-start(s32[512]{0:T(512)} %param.9) | copy-start | bytes 6148
  38.7 2.8 %collective-permute-start.12 = (f32[4,1,640]{2,1,0:T(1,128)S(1)}, f32[4,1,640]{2,1,0:T(1,128)S(1)}, u32[]{:S(2)}, u32[]{:S(2)}) collective-permute-start(f32[4,1,640]{2,1,0:T(1,128)S(1)} %get-tuple-element.217), channel_id=1, source_target_pairs={{0,1},{1,0},{2,3},{3,2},{4,5},{5,4},{6,7},{7,6},{8,9},{9,8},{10,11... | collective-permute-start | bytes 30728 | tf_op jit(solution)/shard_map/ppermute | solution.py:454
  38.8 6.2 %collective-permute-start.14 = (f32[1,1,640]{2,1,0:T(1,128)S(1)}, f32[1,1,640]{2,1,0:T(1,128)S(1)}, u32[]{:S(2)}, u32[]{:S(2)}) collective-permute-start(f32[1,1,640]{2,1,0:T(1,128)S(1)} %get-tuple-element.216.refs_0_), channel_id=1, source_target_pairs={{0,8},{1,9},{2,10},{3,11},{4,12},{5,13},{6,14},{7,15},{8,0},{9,1},... | collective-permute-start | bytes 7688 | tf_op jit(solution)/shard_map/ppermute | solution.py:454
  41.4 3.6 %collective-permute-start.13 = (f32[1,1,640]{2,1,0:T(1,128)S(1)}, f32[1,1,640]{2,1,0:T(1,128)S(1)}, u32[]{:S(2)}, u32[]{:S(2)}) collective-permute-start(f32[1,1,640]{2,1,0:T(1,128)S(1)} %get-tuple-element.219), channel_id=1, source_target_pairs={{0,1},{1,0},{2,3},{3,2},{4,8},{5,9},{6,10},{7,11},{8,4},{9,5},{10,... | collective-permute-start | bytes 7688 | tf_op jit(solution)/shard_map/ppermute | solution.py:454
  41.4 4.8 %collective-permute-start.17 = (f32[1,1,640]{2,1,0:T(1,128)S(1)}, f32[1,1,640]{2,1,0:T(1,128)S(1)}, u32[]{:S(2)}, u32[]{:S(2)}) collective-permute-start(f32[1,1,640]{2,1,0:T(1,128)S(1)} %get-tuple-element.244), channel_id=1, source_target_pairs={{0,6},{1,7},{2,4},{3,5},{4,2},{5,3},{6,0},{7,1},{8,14},{9,15},{10,... | collective-permute-start | bytes 7688 | tf_op jit(solution)/shard_map/ppermute | solution.py:454
  43.9 3.6 %collective-permute-start.16 = (f32[1,1,640]{2,1,0:T(1,128)S(1)}, f32[1,1,640]{2,1,0:T(1,128)S(1)}, u32[]{:S(2)}, u32[]{:S(2)}) collective-permute-start(f32[1,1,640]{2,1,0:T(1,128)S(1)} %get-tuple-element.245), channel_id=1, source_target_pairs={{0,2},{1,3},{2,0},{3,1},{4,6},{5,7},{6,4},{7,5},{8,10},{9,11},{10,... | collective-permute-start | bytes 7688 | tf_op jit(solution)/shard_map/ppermute | solution.py:454
  44.4 3.6 %collective-permute-start.15 = (f32[1,1,640]{2,1,0:T(1,128)S(1)}, f32[1,1,640]{2,1,0:T(1,128)S(1)}, u32[]{:S(2)}, u32[]{:S(2)}) collective-permute-start(f32[1,1,640]{2,1,0:T(1,128)S(1)} %get-tuple-element.246), channel_id=1, source_target_pairs={{0,4},{1,5},{2,6},{3,7},{4,0},{5,1},{6,2},{7,3},{8,12},{9,13},{10,... | collective-permute-start | bytes 7688 | tf_op jit(solution)/shard_map/ppermute | solution.py:454
  48.5 0.6 %copy-start.3 = (f32[512]{0:T(512)}, f32[512]{0:T(512)S(1)}, u32[]{:S(2)}) copy-start(f32[512]{0:T(512)S(1)} %get-tuple-element.360) | copy-start | bytes 6148

commit v16 on v14

--- a/solution.py
+++ b/solution.py
@@ -353,7 +353,9 @@
 
 def score(name, docs, hot, place, blocks, pairs, made, tasks, sums, doubted=(), weight=1):
     rest, _, _, lanes = layout(docs, hot)
-    names = list(dict.fromkeys([*made, *(name for task in tasks for name in task[0])]))
+    names = list(dict.fromkeys([
+        *made, *(name for task in tasks for name in task[0]), *(task[1] for task in tasks if task[1] in blocks),
+    ]))
     given = [p for p in pairs if any(p == task[1] for task in tasks)]
     width = blocks[OWN].shape[1]
     vmem = pl.BlockSpec(memory_space=pltpu.VMEM)
@@ -465,12 +467,17 @@
     blocks[PAIR_DIAG] = move(blocks[PAIR_ROW], STAY, core=1)
     sums, pairs = meet("far", (), [((FAR,), p, True, None) for p in (HERE, THERE, ACROSS)])
     sums, pairs = meet(
+        "diag", (),
+        [((NEXT, FAR), PAIR_DIAG, False, None), ((PAIR_DIAG,), THERE, False, "row0")],
+        doubted=(PAIR_DIAG,),
+    )
+    by_core = sums[1]
+    sums, pairs = meet(
         "last", (),
-        [((NEXT, FAR), right, False, None) for right in (PAIR_ROW, PAIR_DIAG)]
-        + [((PAIR_ROW,), THERE, False, "row1"), ((PAIR_DIAG,), THERE, False, "row0")],
-        doubted=(PAIR_ROW, PAIR_DIAG),
-    )
-    kept, by_core, to_next, to_far = sums
+        [((NEXT, FAR), PAIR_ROW, False, None), ((PAIR_ROW,), THERE, False, "row1")],
+        doubted=(PAIR_ROW,),
+    )
+    kept, _, to_next, to_far = sums
     from_core, from_far = move(by_core, STAY, core=1), move(to_far, TWO)
     from_core, to_next = lax.optimization_barrier((from_core, to_next))
     from_next = move(to_next, MIDDLE)

time: 48.2 us -> 49.1 us (1.019)
  Pallas kernels: 10.7 us -> 12 us
  waiting for transfers between devices: 20.6 us -> 19.8 us
  starting transfers between devices: 15.2 us -> 15.7 us
    pallas_call x5 -> x6, Pallas kernels: 6.09 us -> 7.36 us  [score(): pl.pallas_call(lambda *refs: score_kernel(docs, hot, names, given, made,...]
    ppermute x15, waiting for transfers between devices: 20.6 us -> 19.8 us  [move(): return lax.ppermute(a, ('owner', 'split'), pairs)]
  transfers between devices with their start and end apart: 15 -> 15, of which waited for: 6 -> 5; matrix products, arithmetic and copies ran while one was open for 0% -> 0% of each run, Pallas kernels for 11% -> 14%
where the time goes in v16:
time: 49.1 us; the launch traced here: 49 us
  waiting for transfers between devices  19.8 us (40%)
  starting transfers between devices  15.7 us (32%)
  Pallas kernels  12 us (24%)
  between operations  0.75 us (2%)
  local copies, waits for them, and re-layouts  0.58 us (1%)
    ppermute x15, waiting for transfers between devices, move(): return lax.ppermute(a, ('owner', 'split'), pairs)  19.8 us
    ppermute x15, starting transfers between devices, move(): return lax.ppermute(a, ('owner', 'split'), pairs)  15.7 us
    pallas_call x6, Pallas kernels, score(): pl.pallas_call(lambda *refs: score_kernel(docs, hot, names, given, made,...  7.36 us
    pallas_call x1, Pallas kernels, prep(): pl.pallas_call(lambda *refs: prep_kernel(hot, *refs), out_shape=(shape((r...  3.56 us
  transfers between devices with their start and end apart: 15, of which 5 were waited for; matrix products, arithmetic and copies ran while one was open for 0% of the time, Pallas kernels for 14%

profile of v16, /device:TPU:0, one launch (start us, length us, event | category | flops | bytes accessed | tf_op | source)
XLA Modules:
  0.0 49.0 jit_solution(11749734866826165857)
XLA Ops:
  0.0 0.1 pad_add_fusion.refs_0_
  0.1 3.6 %prep.1 = (bf16[328,768]{1,0:T(8,128)(2,1)S(1)}, bf16[328,768]{1,0:T(8,128)(2,1)S(1)}, s32[1,512]{1,0:T(1,128)S(1)}) custom-call(s32[3]{0:T(128)S(1)} %pad_add_fusion.refs_0_, s32[1,512]{1,0:T(1,128)} %bitcast.16, bf16[512,1024]{1,0:T(8,128)(2,1)} %refs_2_.1, bf16[1024,768]{1,0:T(8,128)(2,1)} %refs_3_.1), custom_call_target="tpu_custom_call" | custom-call | tf_op jit(solution)/shard_map/prep/pallas_call | solution.py:220
  3.6 0.5 %collective-permute-start.3 = (bf16[328,768]{1,0:T(8,128)(2,1)S(1)}, bf16[328,768]{1,0:T(8,128)(2,1)S(1)}, u32[]{:S(2)}, u32[]{:S(2)}) collective-permute-start(bf16[328,768]{1,0:T(8,128)(2,1)S(1)} %get-tuple-element.188.refs_1_), channel_id=1, source_target_pairs={{0,1},{1,0},{2,3},{3,2},{4,5},{5,4},{6,7},{7,6},{8,9},{9,8},{10,11... | collective-permute-start | bytes 1511432 | tf_op jit(solution)/shard_map/ppermute | solution.py:433
  4.2 2.6 %collective-permute-start.7 = (bf16[328,768]{1,0:T(8,128)(2,1)S(1)}, bf16[328,768]{1,0:T(8,128)(2,1)S(1)}, u32[]{:S(2)}, u32[]{:S(2)}) collective-permute-start(bf16[328,768]{1,0:T(8,128)(2,1)S(1)} %get-tuple-element.189), channel_id=1, source_target_pairs={{0,4},{1,5},{2,6},{3,7},{4,0},{5,1},{6,2},{7,3},{8,12},{9,13},{10,... | collective-permute-start | bytes 1511432 | tf_op jit(solution)/shard_map/ppermute | solution.py:433
  6.8 0.0 collective-permute-done.3.refs_2_
  6.8 1.7 %collective-permute-start.4 = (bf16[328,768]{1,0:T(8,128)(2,1)S(1)}, bf16[328,768]{1,0:T(8,128)(2,1)S(1)}, u32[]{:S(2)}, u32[]{:S(2)}) collective-permute-start(bf16[328,768]{1,0:T(8,128)(2,1)S(1)} %get-tuple-element.188.refs_1_), channel_id=1, source_target_pairs={{0,2},{1,3},{2,0},{3,1},{4,6},{5,7},{6,4},{7,5},{8,10},{9,11},{10,... | collective-permute-start | bytes 1511432 | tf_op jit(solution)/shard_map/ppermute | solution.py:433
  8.6 0.0 collective-permute-start.5
  8.6 1.4 %own.1 = (f32[4,1,640]{2,1,0:T(1,128)S(1)}, f32[4,1,640]{2,1,0:T(1,128)S(1)}, f32[1,1,640]{2,1,0:T(1,128)S(1)}, f32[1,1,640]{2,1,0:T(1,128)S(1)}, bf16[768,640]{1,0:T(8,128)(2,1)S(1)}, /*index=5*/f32[8,640]{1,0:T(8,128)S(1)}) custom-call(s32[3]{0:T(128)S(1)} %pad_add_fusion.refs_0_, bf16[328,768]{1,0:T(8,128)(2,1)S(1)} %get-tuple-element.188.refs_1_, ...), custom_call_target="tpu_custom_call" | custom-call | flops 8589934592 | bytes 1024 | tf_op jit(solution)/shard_map/own/pallas_call | solution.py:366
  10.0 8.9 %collective-permute-done.7.refs_1_.refs_3_ = bf16[328,768]{1,0:T(8,128)(2,1)S(1)} collective-permute-done((bf16[328,768]{1,0:T(8,128)(2,1)S(1)}, bf16[328,768]{1,0:T(8,128)(2,1)S(1)}, u32[]{:S(2)}, u32[]{:S(2)}) %collective-permute-start.7) | collective-permute-done | bytes 503840 | tf_op jit(solution)/shard_map/ppermute | solution.py:433
  18.9 0.0 collective-permute-start.10
  18.9 2.8 %collective-permute-start.6 = (bf16[328,768]{1,0:T(8,128)(2,1)S(1)}, bf16[328,768]{1,0:T(8,128)(2,1)S(1)}, u32[]{:S(2)}, u32[]{:S(2)}) collective-permute-start(bf16[328,768]{1,0:T(8,128)(2,1)S(1)} %get-tuple-element.188.refs_1_), channel_id=1, source_target_pairs={{0,8},{1,9},{2,10},{3,11},{4,0},{5,1},{6,2},{7,3},{8,12},{9,13},{1... | collective-permute-start | bytes 1511432 | tf_op jit(solution)/shard_map/ppermute | solution.py:433
  21.7 1.5 %collective-permute-start.8 = (bf16[328,768]{1,0:T(8,128)(2,1)S(1)}, bf16[328,768]{1,0:T(8,128)(2,1)S(1)}, u32[]{:S(2)}, u32[]{:S(2)}) collective-permute-start(bf16[328,768]{1,0:T(8,128)(2,1)S(1)} %collective-permute-done.7.refs_1_.refs_3_), channel_id=1, source_target_pairs={{0,2},{1,3},{2,0},{3,1},{4,6},{5,7},{6,4},{7,5},{8,10},{9,11},{10,... | collective-permute-start | bytes 1511432 | tf_op jit(solution)/shard_map/ppermute | solution.py:433
  23.2 0.0 collective-permute-done.4.refs_1_
  23.2 1.1 %pair.1 = (f32[4,1,640]{2,1,0:T(1,128)S(1)}, f32[4,1,640]{2,1,0:T(1,128)S(1)}, f32[1,1,640]{2,1,0:T(1,128)S(1)}, f32[1,1,640]{2,1,0:T(1,128)S(1)}, bf16[768,640]{1,0:T(8,128)(2,1)S(1)}, /*index=5*/f32[8,640]{1,0:T(8,128)S(1)}) custom-call(s32[3]{0:T(128)S(1)} %pad_add_fusion.refs_0_, bf16[328,768]{1,0:T(8,128)(2,1)S(1)} %collective-permute-done.7.refs_1_.refs_3_, ...), custom_call_target="tpu_custom_call" | custom-call | flops 8589934592 | bytes 1024 | tf_op jit(solution)/shard_map/pair/pallas_call | solution.py:366
  24.3 0.8 %collective-permute-done.9.refs_2_ = bf16[328,768]{1,0:T(8,128)(2,1)S(1)} collective-permute-done((bf16[328,768]{1,0:T(8,128)(2,1)S(1)}, bf16[328,768]{1,0:T(8,128)(2,1)S(1)}, u32[]{:S(2)}, u32[]{:S(2)}) %collective-permute-start.9) | collective-permute-done | bytes 503840 | tf_op jit(solution)/shard_map/ppermute | solution.py:433
  25.1 1.8 %row.1 = (f32[4,1,640]{2,1,0:T(1,128)S(1)}, f32[4,1,640]{2,1,0:T(1,128)S(1)}, f32[1,1,640]{2,1,0:T(1,128)S(1)}, f32[1,1,640]{2,1,0:T(1,128)S(1)}, bf16[768,640]{1,0:T(8,128)(2,1)S(1)}, /*index=5*/f32[8,640]{1,0:T(8,128)S(1)}) custom-call(s32[3]{0:T(128)S(1)} %pad_add_fusion.refs_0_, bf16[328,768]{1,0:T(8,128)(2,1)S(1)} %collective-permute-done.4.refs_1_, ...), custom_call_target="tpu_custom_call" | custom-call | flops 1 | bytes 1024 | tf_op jit(solution)/shard_map/row/pallas_call | solution.py:366
  26.9 8.4 %collective-permute-done.8.refs_3_ = bf16[328,768]{1,0:T(8,128)(2,1)S(1)} collective-permute-done((bf16[328,768]{1,0:T(8,128)(2,1)S(1)}, bf16[328,768]{1,0:T(8,128)(2,1)S(1)}, u32[]{:S(2)}, u32[]{:S(2)}) %collective-permute-start.8) | collective-permute-done | bytes 503840 | tf_op jit(solution)/shard_map/ppermute | solution.py:433
  35.3 0.6 %far.1 = (f32[4,1,640]{2,1,0:T(1,128)S(1)}, f32[4,1,640]{2,1,0:T(1,128)S(1)}, f32[1,1,640]{2,1,0:T(1,128)S(1)}, f32[1,1,640]{2,1,0:T(1,128)S(1)}) custom-call(s32[3]{0:T(128)S(1)} %pad_add_fusion.refs_0_, bf16[328,768]{1,0:T(8,128)(2,1)S(1)} %collective-permute-done.6.refs_1_.refs_2_, bf16[768,640]{1,0:T(8,128)(2,1)S(1)} %get-tuple-element.195.refs_4_.refs_5_.refs_2_, ...), custom_call_target="tpu_custom_call" | custom-call | flops 1 | bytes 1024 | tf_op jit(solution)/shard_map/far/pallas_call | solution.py:366
  35.9 1.2 %collective-permute-done.11.refs_3_ = bf16[328,768]{1,0:T(8,128)(2,1)S(1)} collective-permute-done((bf16[328,768]{1,0:T(8,128)(2,1)S(1)}, bf16[328,768]{1,0:T(8,128)(2,1)S(1)}, u32[]{:S(2)}, u32[]{:S(2)}) %collective-permute-start.11) | collective-permute-done | bytes 503840 | tf_op jit(solution)/shard_map/ppermute | solution.py:433
  37.2 1.2 %diag.1 = (f32[4,1,640]{2,1,0:T(1,128)S(1)}, f32[4,1,640]{2,1,0:T(1,128)S(1)}, f32[1,1,640]{2,1,0:T(1,128)S(1)}, f32[1,1,640]{2,1,0:T(1,128)S(1)}) custom-call(s32[3]{0:T(128)S(1)} %pad_add_fusion.refs_0_, bf16[328,768]{1,0:T(8,128)(2,1)S(1)} %collective-permute-done.5.refs_3_.refs_4_.refs_1_, bf16[328,768]{1,0:T(8,128)(2,1)S(1)} %collective-permute-done.6.refs_1_.refs_2_, ...), custom_call_target="tpu_custom_call" | custom-call | flops 1 | bytes 1024 | tf_op jit(solution)/shard_map/diag/pallas_call | solution.py:366
  38.4 0.2 collective-permute-start.13
  38.6 1.3 %last.1 = (f32[4,1,640]{2,1,0:T(1,128)S(1)}, f32[4,1,640]{2,1,0:T(1,128)}, f32[1,1,640]{2,1,0:T(1,128)S(1)}, f32[1,1,640]{2,1,0:T(1,128)S(1)}) custom-call(s32[3]{0:T(128)S(1)} %pad_add_fusion.refs_0_, bf16[328,768]{1,0:T(8,128)(2,1)S(1)} %collective-permute-done.5.refs_3_.refs_4_.refs_1_, bf16[328,768]{1,0:T(8,128)(2,1)S(1)} %collective-permute-done.6.refs_1_.refs_2_, ...), custom_call_target="tpu_custom_call" | custom-call | flops 1 | bytes 1024 | tf_op jit(solution)/shard_map/last/pallas_call | solution.py:366
  39.8 2.8 %collective-permute-start.12 = (f32[1,1,640]{2,1,0:T(1,128)S(1)}, f32[1,1,640]{2,1,0:T(1,128)S(1)}, u32[]{:S(2)}, u32[]{:S(2)}) collective-permute-start(f32[1,1,640]{2,1,0:T(1,128)S(1)} %get-tuple-element.221.refs_0_), channel_id=1, source_target_pairs={{0,8},{1,9},{2,10},{3,11},{4,12},{5,13},{6,14},{7,15},{8,0},{9,1},... | collective-permute-start | bytes 7688 | tf_op jit(solution)/shard_map/ppermute | solution.py:433
  42.6 0.7 %collective-permute-start.17 = (f32[1,1,640]{2,1,0:T(1,128)S(1)}, f32[1,1,640]{2,1,0:T(1,128)S(1)}, u32[]{:S(2)}, u32[]{:S(2)}) collective-permute-start(f32[1,1,640]{2,1,0:T(1,128)S(1)} %get-tuple-element.246), channel_id=1, source_target_pairs={{0,6},{1,7},{2,4},{3,5},{4,2},{5,3},{6,0},{7,1},{8,14},{9,15},{10,... | collective-permute-start | bytes 7688 | tf_op jit(solution)/shard_map/ppermute | solution.py:433
  43.3 1.0 %collective-permute-start.16 = (f32[1,1,640]{2,1,0:T(1,128)S(1)}, f32[1,1,640]{2,1,0:T(1,128)S(1)}, u32[]{:S(2)}, u32[]{:S(2)}) collective-permute-start(f32[1,1,640]{2,1,0:T(1,128)S(1)} %get-tuple-element.247), channel_id=1, source_target_pairs={{0,2},{1,3},{2,0},{3,1},{4,6},{5,7},{6,4},{7,5},{8,10},{9,11},{10,... | collective-permute-start | bytes 7688 | tf_op jit(solution)/shard_map/ppermute | solution.py:433
  44.3 1.9 %collective-permute-start.15 = (f32[1,1,640]{2,1,0:T(1,128)S(1)}, f32[1,1,640]{2,1,0:T(1,128)S(1)}, u32[]{:S(2)}, u32[]{:S(2)}) collective-permute-start(f32[1,1,640]{2,1,0:T(1,128)S(1)} %get-tuple-element.248), channel_id=1, source_target_pairs={{0,4},{1,5},{2,6},{3,7},{4,0},{5,1},{6,2},{7,3},{8,12},{9,13},{10,... | collective-permute-start | bytes 7688 | tf_op jit(solution)/shard_map/ppermute | solution.py:433
  46.2 0.6 %decide.1 = s32[1]{0:T(128)} custom-call(f32[1,1,640]{2,1,0:T(1,128)S(1)} %get-tuple-element.221.refs_0_, f32[1,1,640]{2,1,0:T(1,128)S(1)} %collective-permute-done.12.refs_1_), custom_call_target="tpu_custom_call" | custom-call | tf_op jit(solution)/shard_map/decide/pallas_call | solution.py:405
  47.5 0.4 collective-permute-done.15
  47.9 0.5 %conditional.1 = (f32[512]{0:T(512)S(1)}) conditional(s32[]{:T(128)} %bitcast.5, (f32[4,1,640]{2,1,0:T(1,128)S(1)}, f32[4,1,640]{2,1,0:T(1,128)S(1)}, s32[1,512]{1,0:T(1,128)S(1)}, f32[1,1,640]{2,1,0:T(1,128)S(1)}, f32[1,1,640]{2,1,0:T(1,128)S(1)}, /*index=5*/f32[1,1,640]{2,1,0:T(1,128)S(1)}, f32[1,1,640]{2,1,0:T(1,128)S(1)}, ...), branch_computations={%region_0.1_spmd, %region_1.8_spmd} | conditional | flops 1617953280 | bytes 16846124 | solution.py:489
  47.9 0.5 finish.1
  48.4 0.0 copy-start.3
  48.4 0.6 %copy-done.3 = f32[512]{0:T(512)} copy-done((f32[512]{0:T(512)}, f32[512]{0:T(512)S(1)}, u32[]{:S(2)}) %copy-start.3) | copy-done | bytes 2072
  (19 shorter events, 0.1 us)
Async XLA Ops:
  3.6 3.2 %collective-permute-start.3 = (bf16[328,768]{1,0:T(8,128)(2,1)S(1)}, bf16[328,768]{1,0:T(8,128)(2,1)S(1)}, u32[]{:S(2)}, u32[]{:S(2)}) collective-permute-start(bf16[328,768]{1,0:T(8,128)(2,1)S(1)} %get-tuple-element.188.refs_1_), channel_id=1, source_target_pairs={{0,1},{1,0},{2,3},{3,2},{4,5},{5,4},{6,7},{7,6},{8,9},{9,8},{10,11... | collective-permute-start | bytes 1511432 | tf_op jit(solution)/shard_map/ppermute | solution.py:433
  4.2 14.7 %collective-permute-start.7 = (bf16[328,768]{1,0:T(8,128)(2,1)S(1)}, bf16[328,768]{1,0:T(8,128)(2,1)S(1)}, u32[]{:S(2)}, u32[]{:S(2)}) collective-permute-start(bf16[328,768]{1,0:T(8,128)(2,1)S(1)} %get-tuple-element.189), channel_id=1, source_target_pairs={{0,4},{1,5},{2,6},{3,7},{4,0},{5,1},{6,2},{7,3},{8,12},{9,13},{10,... | collective-permute-start | bytes 1511432 | tf_op jit(solution)/shard_map/ppermute | solution.py:433
  6.8 16.4 %collective-permute-start.4 = (bf16[328,768]{1,0:T(8,128)(2,1)S(1)}, bf16[328,768]{1,0:T(8,128)(2,1)S(1)}, u32[]{:S(2)}, u32[]{:S(2)}) collective-permute-start(bf16[328,768]{1,0:T(8,128)(2,1)S(1)} %get-tuple-element.188.refs_1_), channel_id=1, source_target_pairs={{0,2},{1,3},{2,0},{3,1},{4,6},{5,7},{6,4},{7,5},{8,10},{9,11},{10,... | collective-permute-start | bytes 1511432 | tf_op jit(solution)/shard_map/ppermute | solution.py:433
  8.6 14.6 %collective-permute-start.5 = (bf16[328,768]{1,0:T(8,128)(2,1)S(1)}, bf16[328,768]{1,0:T(8,128)(2,1)S(1)}, u32[]{:S(2)}, u32[]{:S(2)}) collective-permute-start(bf16[328,768]{1,0:T(8,128)(2,1)S(1)} %get-tuple-element.189), channel_id=1, source_target_pairs={{0,1},{1,0},{2,3},{3,2},{4,8},{5,9},{6,10},{7,11},{8,4},{9,5},{10,... | collective-permute-start | bytes 1511432 | tf_op jit(solution)/shard_map/ppermute | solution.py:433
  18.9 4.3 %collective-permute-start.10 = (bf16[328,768]{1,0:T(8,128)(2,1)S(1)}, bf16[328,768]{1,0:T(8,128)(2,1)S(1)}, u32[]{:S(2)}, u32[]{:S(2)}) collective-permute-start(bf16[328,768]{1,0:T(8,128)(2,1)S(1)} %collective-permute-done.7.refs_1_.refs_3_), channel_id=1, source_target_pairs={{0,1},{1,0},{2,3},{3,2},{4,5},{5,4},{6,7},{7,6},{8,9},{9,8},{10,11... | collective-permute-start | bytes 1511432 | tf_op jit(solution)/shard_map/ppermute | solution.py:433
  18.9 16.4 %collective-permute-start.6 = (bf16[328,768]{1,0:T(8,128)(2,1)S(1)}, bf16[328,768]{1,0:T(8,128)(2,1)S(1)}, u32[]{:S(2)}, u32[]{:S(2)}) collective-permute-start(bf16[328,768]{1,0:T(8,128)(2,1)S(1)} %get-tuple-element.188.refs_1_), channel_id=1, source_target_pairs={{0,8},{1,9},{2,10},{3,11},{4,0},{5,1},{6,2},{7,3},{8,12},{9,13},{1... | collective-permute-start | bytes 1511432 | tf_op jit(solution)/shard_map/ppermute | solution.py:433
  21.7 13.6 %collective-permute-start.8 = (bf16[328,768]{1,0:T(8,128)(2,1)S(1)}, bf16[328,768]{1,0:T(8,128)(2,1)S(1)}, u32[]{:S(2)}, u32[]{:S(2)}) collective-permute-start(bf16[328,768]{1,0:T(8,128)(2,1)S(1)} %collective-permute-done.7.refs_1_.refs_3_), channel_id=1, source_target_pairs={{0,2},{1,3},{2,0},{3,1},{4,6},{5,7},{6,4},{7,5},{8,10},{9,11},{10,... | collective-permute-start | bytes 1511432 | tf_op jit(solution)/shard_map/ppermute | solution.py:433
  23.2 1.9 %collective-permute-start.9 = (bf16[328,768]{1,0:T(8,128)(2,1)S(1)}, bf16[328,768]{1,0:T(8,128)(2,1)S(1)}, u32[]{:S(2)}, u32[]{:S(2)}) collective-permute-start(bf16[328,768]{1,0:T(8,128)(2,1)S(1)} %collective-permute-done.4.refs_1_), channel_id=1, source_target_pairs={{0,1},{1,0},{2,3},{3,2},{4,5},{5,4},{6,7},{7,6},{8,9},{9,8},{10,11... | collective-permute-start | bytes 1511432 | tf_op jit(solution)/shard_map/ppermute | solution.py:433
  35.3 1.9 %collective-permute-start.11 = (bf16[328,768]{1,0:T(8,128)(2,1)S(1)}, bf16[328,768]{1,0:T(8,128)(2,1)S(1)}, u32[]{:S(2)}, u32[]{:S(2)}) collective-permute-start(bf16[328,768]{1,0:T(8,128)(2,1)S(1)} %collective-permute-done.8.refs_3_), channel_id=1, source_target_pairs={{0,1},{1,0},{2,3},{3,2},{4,5},{5,4},{6,7},{7,6},{8,9},{9,8},{10,11... | collective-permute-start | bytes 1511432 | tf_op jit(solution)/shard_map/ppermute | solution.py:433
  37.2 10.7 %copy-start.1 = (bf16[512,1024]{1,0:T(8,128)(2,1)S(1)}, bf16[512,1024]{1,0:T(8,128)(2,1)}, u32[]{:S(2)}) copy-start(bf16[512,1024]{1,0:T(8,128)(2,1)} %refs_2_.1) | copy-start | bytes 3145732
  38.4 9.5 %copy-start = (bf16[1024,768]{1,0:T(8,128)(2,1)S(1)}, bf16[1024,768]{1,0:T(8,128)(2,1)}, u32[]{:S(2)}) copy-start(bf16[1024,768]{1,0:T(8,128)(2,1)} %refs_3_.1) | copy-start | bytes 4718596
  38.4 9.5 %copy-start.2 = (s32[512]{0:T(512)S(1)}, s32[512]{0:T(512)}, u32[]{:S(2)}) copy-start(s32[512]{0:T(512)} %param.9) | copy-start | bytes 6148
  38.4 4.2 %collective-permute-start.13 = (f32[4,1,640]{2,1,0:T(1,128)S(1)}, f32[4,1,640]{2,1,0:T(1,128)S(1)}, u32[]{:S(2)}, u32[]{:S(2)}) collective-permute-start(f32[4,1,640]{2,1,0:T(1,128)S(1)} %get-tuple-element.218.refs_7_), channel_id=1, source_target_pairs={{0,1},{1,0},{2,3},{3,2},{4,5},{5,4},{6,7},{7,6},{8,9},{9,8},{10,11... | collective-permute-start | bytes 30728 | tf_op jit(solution)/shard_map/ppermute | solution.py:433
  39.8 6.3 %collective-permute-start.12 = (f32[1,1,640]{2,1,0:T(1,128)S(1)}, f32[1,1,640]{2,1,0:T(1,128)S(1)}, u32[]{:S(2)}, u32[]{:S(2)}) collective-permute-start(f32[1,1,640]{2,1,0:T(1,128)S(1)} %get-tuple-element.221.refs_0_), channel_id=1, source_target_pairs={{0,8},{1,9},{2,10},{3,11},{4,12},{5,13},{6,14},{7,15},{8,0},{9,1},... | collective-permute-start | bytes 7688 | tf_op jit(solution)/shard_map/ppermute | solution.py:433
  42.6 4.8 %collective-permute-start.17 = (f32[1,1,640]{2,1,0:T(1,128)S(1)}, f32[1,1,640]{2,1,0:T(1,128)S(1)}, u32[]{:S(2)}, u32[]{:S(2)}) collective-permute-start(f32[1,1,640]{2,1,0:T(1,128)S(1)} %get-tuple-element.246), channel_id=1, source_target_pairs={{0,6},{1,7},{2,4},{3,5},{4,2},{5,3},{6,0},{7,1},{8,14},{9,15},{10,... | collective-permute-start | bytes 7688 | tf_op jit(solution)/shard_map/ppermute | solution.py:433
  43.3 4.2 %collective-permute-start.16 = (f32[1,1,640]{2,1,0:T(1,128)S(1)}, f32[1,1,640]{2,1,0:T(1,128)S(1)}, u32[]{:S(2)}, u32[]{:S(2)}) collective-permute-start(f32[1,1,640]{2,1,0:T(1,128)S(1)} %get-tuple-element.247), channel_id=1, source_target_pairs={{0,2},{1,3},{2,0},{3,1},{4,6},{5,7},{6,4},{7,5},{8,10},{9,11},{10,... | collective-permute-start | bytes 7688 | tf_op jit(solution)/shard_map/ppermute | solution.py:433
  44.3 3.6 %collective-permute-start.15 = (f32[1,1,640]{2,1,0:T(1,128)S(1)}, f32[1,1,640]{2,1,0:T(1,128)S(1)}, u32[]{:S(2)}, u32[]{:S(2)}) collective-permute-start(f32[1,1,640]{2,1,0:T(1,128)S(1)} %get-tuple-element.248), channel_id=1, source_target_pairs={{0,4},{1,5},{2,6},{3,7},{4,0},{5,1},{6,2},{7,3},{8,12},{9,13},{10,... | collective-permute-start | bytes 7688 | tf_op jit(solution)/shard_map/ppermute | solution.py:433
  46.2 1.7 %collective-permute-start.14 = (f32[1,1,640]{2,1,0:T(1,128)S(1)}, f32[1,1,640]{2,1,0:T(1,128)S(1)}, u32[]{:S(2)}, u32[]{:S(2)}) collective-permute-start(f32[1,1,640]{2,1,0:T(1,128)S(1)} %get-tuple-element.226), channel_id=1, source_target_pairs={{0,1},{1,0},{2,3},{3,2},{4,8},{5,9},{6,10},{7,11},{8,4},{9,5},{10,... | collective-permute-start | bytes 7688 | tf_op jit(solution)/shard_map/ppermute | solution.py:433
  48.4 0.6 %copy-start.3 = (f32[512]{0:T(512)}, f32[512]{0:T(512)S(1)}, u32[]{:S(2)}) copy-start(f32[512]{0:T(512)S(1)} %get-tuple-element.362) | copy-start | bytes 6148

commit v17 on v16

--- a/solution.py
+++ b/solution.py
@@ -234,11 +234,12 @@
 OWN, PAIR = "own", "pair"
 CORE, PAIR_CORE = "core", "pair_core"
 ROW, PAIR_ROW = "row", "pair_row"
-DIAG, PAIR_DIAG = "diag", "pair_diag"
+DIAG = "diag"
 NEXT, FAR = "next", "far"
-GROUPS = ((OWN, PAIR, ROW, PAIR_ROW), (CORE, PAIR_CORE, DIAG, PAIR_DIAG), (NEXT,), (FAR,))
+NEXT_CORE, FAR_CORE = "next_core", "far_core"
+GROUPS = ((OWN, PAIR, ROW, PAIR_ROW), (CORE, PAIR_CORE, DIAG), (NEXT, FAR), (NEXT_CORE, FAR_CORE))
 TILE = 256
-HERE, THERE, ACROSS = (OWN, CORE), (PAIR, PAIR_CORE), (ROW, DIAG)
+HERE, THERE, ACROSS, SIDE = (OWN, CORE), (PAIR, PAIR_CORE), (ROW, DIAG), (OWN, PAIR, ROW)
 
 
 def score_kernel(docs, hot, names, given, made, tasks, doubted, carries, *refs):
@@ -260,12 +261,13 @@
 
     def meet(count, start):
         lane = slice(start, start + count)
-        wide, two = up(count, 128), 2 * count
+        wide = up(count, 128)
         columns = {name: ref[rest:, 0:wide].astype(F32)[0:8, :].T[0:count, :] for name, ref in blocks.items()}
         if made:
             turned, notes = pairs[made]
-            turned[:, 0:two] = jnp.concatenate([blocks[name][:count, :] for name in made], axis=0).T
-            notes[:, 0:two] = jnp.concatenate([columns[name] for name in made], axis=0).T
+            span = len(made) * count
+            turned[:, 0:span] = jnp.concatenate([blocks[name][:count, :] for name in made], axis=0).T
+            notes[:, 0:span] = jnp.concatenate([columns[name] for name in made], axis=0).T
 
         for left in dict.fromkeys(task[0] for task in tasks):
 
@@ -278,15 +280,17 @@
                     block = jnp.concatenate([block, blocks[name][:count, :]], axis=0)
                     column = jnp.concatenate([column, columns[name][:, 0:1]], axis=0)
                 fresh = True
-                for _, right, both, _ in own_tasks:
+                for _, right, signed, _ in own_tasks:
+                    number = abs(signed)
                     if right in blocks:
                         span, rights, diagonal = count, (right,), False
                         ids = blocks[right][rest:, 0:wide].astype(F32)[0:1, 0:count]
                     else:
                         turned, notes = pairs[right]
-                        span, rights, diagonal = two if both else wide, right[:1 + both], left == right[:1]
+                        span = number * count if number > 1 else wide
+                        rights, diagonal = right[:number], left == right[:1]
                         ids = notes[0:1, 0:span]
-                        if not both:
+                        if number == 1:
                             ids = jnp.where(lax.broadcasted_iota(jnp.int32, ids.shape, 1) < count, ids, -1.0)
                     totals = []
                     for low in range(0, span, TILE):
@@ -319,7 +323,7 @@
                                 parts[0:rows, :] += part
                             fresh = False
                     total = jnp.concatenate(totals, axis=1) if len(totals) > 1 else totals[0]
-                    for k, name in enumerate(rights):
+                    for k, name in enumerate(rights if signed > 0 else ()):
                         out, spot = spots[name]
                         out[spot, :, lane] += total[:, k * count:(k + 1) * count]
                 if not fresh:
@@ -335,7 +339,7 @@
                         out[spot, :, lane] += total[0:1, k * count:(k + 1) * count]
 
             condition = [task[3] for task in tasks if task[0] == left][0]
-            if left[0] in (NEXT, FAR):
+            if left[0] in (NEXT, FAR, FAR_CORE):
                 pl.when(middle)(work)
             elif condition:
                 pl.when(when[condition])(work)
@@ -347,8 +351,9 @@
 
     if doubted:
         doubt = sum(blocks[name][rest:, first:first + 128].astype(F32)[0:1, 0:1] for name in doubted)
-        out, k = spots[FAR]
-        out[k] += jnp.where(lax.broadcasted_iota(jnp.int32, (1, lanes), 1) == flag, doubt, 0.0)
+        for name in (FAR, FAR_CORE):
+            out, k = spots[name]
+            out[k] += jnp.where(lax.broadcasted_iota(jnp.int32, (1, lanes), 1) == flag, doubt, 0.0)
 
 
 def score(name, docs, hot, place, blocks, pairs, made, tasks, sums, doubted=(), weight=1):
@@ -362,13 +367,14 @@
     arrays = [blocks[b] for b in names] + [a for p in given for a in pairs[p]] + list(sums)
     shapes = [jax.ShapeDtypeStruct((len(group), 1, lanes), F32) for group in GROUPS]
     if made:
-        shapes += [jax.ShapeDtypeStruct((width, 2 * rest), BF16), jax.ShapeDtypeStruct((8, 2 * rest), F32)]
+        span = len(made) * rest
+        shapes += [jax.ShapeDtypeStruct((width, span), BF16), jax.ShapeDtypeStruct((8, span), F32)]
     out = pl.pallas_call(
         lambda *refs: score_kernel(docs, hot, names, given, made, tasks, doubted or made, bool(sums), *refs),
         out_shape=tuple(shapes),
         in_specs=[pl.BlockSpec(memory_space=pltpu.SMEM)] + [vmem] * len(arrays),
         out_specs=tuple(vmem for _ in shapes),
-        scratch_shapes=[pltpu.VMEM((2 * rest, 128), F32)],
+        scratch_shapes=[pltpu.VMEM((3 * rest, 128), F32)],
         compiler_params=pltpu.CompilerParams(vmem_limit_bytes=20 * 2**20),
         cost_estimate=pl.CostEstimate(flops=weight, bytes_accessed=2**10, transcendentals=0),
         name=name,
@@ -444,7 +450,7 @@
     blocks[CORE], still_same, other = lax.optimization_barrier((blocks[CORE], same, other))
     blocks[ROW] = move(still_same, STAY, row=1)
     blocks[NEXT] = move(other, MIDDLE)
-    sums, pairs = meet("own", HERE, [((OWN,), HERE, False, None), ((CORE,), HERE, False, "core0")], weight=2**33)
+    sums, pairs = meet("own", HERE, [((OWN,), HERE, 1, None), ((CORE,), HERE, 1, "core0")], weight=2**33)
 
     blocks[PAIR], _ = lax.optimization_barrier((blocks[PAIR], sums[0]))
     blocks[ROW], blocks[NEXT] = lax.optimization_barrier((blocks[ROW], blocks[NEXT]))
@@ -452,36 +458,30 @@
     blocks[PAIR_ROW] = move(blocks[PAIR], STAY, row=1)
     blocks[PAIR_CORE] = move(blocks[PAIR], STAY, core=1)
     blocks[DIAG] = move(blocks[ROW], STAY, core=1)
+    blocks[NEXT_CORE] = move(blocks[NEXT], STAY, core=1)
     sums, pairs = meet(
-        "pair", THERE,
-        [((PAIR,), THERE, False, None), ((PAIR_CORE,), THERE, False, "core1"), ((NEXT,), HERE, True, None),
-         ((NEXT,), THERE, True, None)],
-        weight=2**33,
+        "pair", THERE, [((PAIR,), THERE, 1, None), ((PAIR_CORE,), THERE, 1, "core1")], weight=2**33
     )
     sums, pairs = meet(
         "row", ACROSS,
-        [((PAIR,), HERE, True, None), ((PAIR,), ACROSS, True, None), ((NEXT,), ACROSS, True, None),
-         ((ROW,), HERE, False, "row0"), ((DIAG,), HERE, False, "row1")],
-    )
-    blocks[PAIR_ROW], _ = lax.optimization_barrier((blocks[PAIR_ROW], sums[0]))
-    blocks[PAIR_DIAG] = move(blocks[PAIR_ROW], STAY, core=1)
-    sums, pairs = meet("far", (), [((FAR,), p, True, None) for p in (HERE, THERE, ACROSS)])
+        [((PAIR,), HERE, 2, None), ((PAIR,), ACROSS, 2, None), ((ROW,), HERE, 1, "row0"), ((DIAG,), HERE, 1, "row1")],
+    )
+    sums, pairs = meet("next", SIDE, [((NEXT, NEXT_CORE), SIDE, 3, None)])
+    blocks[PAIR_ROW], blocks[FAR], _ = lax.optimization_barrier((blocks[PAIR_ROW], blocks[FAR], sums[0]))
+    blocks[FAR_CORE] = move(blocks[FAR], STAY, core=1)
     sums, pairs = meet(
-        "diag", (),
-        [((NEXT, FAR), PAIR_DIAG, False, None), ((PAIR_DIAG,), THERE, False, "row0")],
-        doubted=(PAIR_DIAG,),
-    )
-    by_core = sums[1]
-    sums, pairs = meet(
-        "last", (),
-        [((NEXT, FAR), PAIR_ROW, False, None), ((PAIR_ROW,), THERE, False, "row1")],
+        "far", (),
+        [((FAR,), SIDE, 3, None), ((NEXT, NEXT_CORE, FAR), PAIR_ROW, 1, None), ((PAIR_ROW,), THERE, -2, None)],
         doubted=(PAIR_ROW,),
     )
-    kept, _, to_next, to_far = sums
-    from_core, from_far = move(by_core, STAY, core=1), move(to_far, TWO)
-    from_core, to_next = lax.optimization_barrier((from_core, to_next))
-    from_next = move(to_next, MIDDLE)
-    own, pair, row, pair_row = (kept[k:k + 1] + from_core[k:k + 1] for k in (0, 1, 2, 3))
+    early = sums[1]
+    sums, pairs = meet("last", (), [((FAR_CORE,), SIDE, 3, None), ((FAR_CORE,), PAIR_ROW, 1, None)])
+    kept, _, away, late = sums
+    early, late = move(early, STAY, core=1), move(late, STAY, core=1)
+    to_next, to_far = (away[k:k + 1] + late[k:k + 1] for k in (0, 1))
+    from_far, from_next = move(to_far, TWO), move(to_next, MIDDLE)
+    own, pair, row = (kept[k:k + 1] + early[k:k + 1] for k in (0, 1, 2))
+    pair_row = kept[3:4]
     home = [
         own, from_next, from_far,
         move(pair, OUTER), move(row, STAY, row=1), move(pair_row, OUTER, row=1),

time: 49.1 us -> 50.4 us (1.026)
  waiting for transfers between devices: 19.8 us -> 18.3 us
  starting transfers between devices: 15.7 us -> 17.1 us
  Pallas kernels: 12 us -> 13.3 us
    ppermute x15 -> x17, waiting for transfers between devices: 19.8 us -> 18.3 us  [move(): return lax.ppermute(a, ('owner', 'split'), pairs)]
    ppermute x15 -> x17, starting transfers between devices: 15.7 us -> 17.1 us  [move(): return lax.ppermute(a, ('owner', 'split'), pairs)]
    pallas_call x6, Pallas kernels: 7.36 us -> 8.68 us  [score(): pl.pallas_call(lambda *refs: score_kernel(docs, hot, names, given, made,...]
  transfers between devices with their start and end apart: 15 -> 17, of which waited for: 5 -> 6; matrix products, arithmetic and copies ran while one was open for 0% -> 0% of each run, Pallas kernels for 14% -> 19%
where the time goes in v17:
time: 50.4 us; the launch traced here: 50.2 us
  waiting for transfers between devices  18.3 us (36%)
  starting transfers between devices  17.1 us (34%)
  Pallas kernels  13.3 us (26%)
  between operations  0.74 us (1%)
  local copies, waits for them, and re-layouts  0.58 us (1%)
    ppermute x17, waiting for transfers between devices, move(): return lax.ppermute(a, ('owner', 'split'), pairs)  18.3 us
    ppermute x17, starting transfers between devices, move(): return lax.ppermute(a, ('owner', 'split'), pairs)  17.1 us
    pallas_call x6, Pallas kernels, score(): pl.pallas_call(lambda *refs: score_kernel(docs, hot, names, given, made,...  8.68 us
    pallas_call x1, Pallas kernels, prep(): pl.pallas_call(lambda *refs: prep_kernel(hot, *refs), out_shape=(shape((r...  3.56 us
  transfers between devices with their start and end apart: 17, of which 6 were waited for; matrix products, arithmetic and copies ran while one was open for 0% of the time, Pallas kernels for 19%

profile of v17, /device:TPU:0, one launch (start us, length us, event | category | flops | bytes accessed | tf_op | source)
XLA Modules:
  0.0 50.2 jit_solution(3142846323863366708)
XLA Ops:
  0.0 0.1 pad_add_fusion.refs_0_
  0.1 3.6 %prep.1 = (bf16[328,768]{1,0:T(8,128)(2,1)S(1)}, bf16[328,768]{1,0:T(8,128)(2,1)S(1)}, s32[1,512]{1,0:T(1,128)S(1)}) custom-call(s32[3]{0:T(128)S(1)} %pad_add_fusion.refs_0_, s32[1,512]{1,0:T(1,128)} %bitcast.16, bf16[512,1024]{1,0:T(8,128)(2,1)} %refs_2_.1, bf16[1024,768]{1,0:T(8,128)(2,1)} %refs_3_.1), custom_call_target="tpu_custom_call" | custom-call | tf_op jit(solution)/shard_map/prep/pallas_call | solution.py:220
  3.6 0.5 %collective-permute-start.4 = (bf16[328,768]{1,0:T(8,128)(2,1)S(1)}, bf16[328,768]{1,0:T(8,128)(2,1)S(1)}, u32[]{:S(2)}, u32[]{:S(2)}) collective-permute-start(bf16[328,768]{1,0:T(8,128)(2,1)S(1)} %get-tuple-element.190.refs_1_), channel_id=1, source_target_pairs={{0,1},{1,0},{2,3},{3,2},{4,5},{5,4},{6,7},{7,6},{8,9},{9,8},{10,11... | collective-permute-start | bytes 1511432 | tf_op jit(solution)/shard_map/ppermute | solution.py:439
  4.2 2.6 %collective-permute-start.3 = (bf16[328,768]{1,0:T(8,128)(2,1)S(1)}, bf16[328,768]{1,0:T(8,128)(2,1)S(1)}, u32[]{:S(2)}, u32[]{:S(2)}) collective-permute-start(bf16[328,768]{1,0:T(8,128)(2,1)S(1)} %get-tuple-element.191), channel_id=1, source_target_pairs={{0,4},{1,5},{2,6},{3,7},{4,0},{5,1},{6,2},{7,3},{8,12},{9,13},{10,... | collective-permute-start | bytes 1511432 | tf_op jit(solution)/shard_map/ppermute | solution.py:439
  6.8 1.7 %collective-permute-start.7 = (bf16[328,768]{1,0:T(8,128)(2,1)S(1)}, bf16[328,768]{1,0:T(8,128)(2,1)S(1)}, u32[]{:S(2)}, u32[]{:S(2)}) collective-permute-start(bf16[328,768]{1,0:T(8,128)(2,1)S(1)} %get-tuple-element.190.refs_1_), channel_id=1, source_target_pairs={{0,2},{1,3},{2,0},{3,1},{4,6},{5,7},{6,4},{7,5},{8,10},{9,11},{10,... | collective-permute-start | bytes 1511432 | tf_op jit(solution)/shard_map/ppermute | solution.py:439
  8.6 1.4 %own.1 = (f32[4,1,640]{2,1,0:T(1,128)S(1)}, f32[3,1,640]{2,1,0:T(1,128)S(1)}, f32[2,1,640]{2,1,0:T(1,128)S(1)}, f32[2,1,640]{2,1,0:T(1,128)S(1)}, bf16[768,640]{1,0:T(8,128)(2,1)S(1)}, /*index=5*/f32[8,640]{1,0:T(8,128)S(1)}) custom-call(s32[3]{0:T(128)S(1)} %pad_add_fusion.refs_0_, bf16[328,768]{1,0:T(8,128)(2,1)S(1)} %get-tuple-element.190.refs_1_, ...), custom_call_target="tpu_custom_call" | custom-call | flops 8589934592 | bytes 1024 | tf_op jit(solution)/shard_map/own/pallas_call | solution.py:372
  10.0 8.9 %collective-permute-done.3.refs_1_.refs_3_.refs_2_ = bf16[328,768]{1,0:T(8,128)(2,1)S(1)} collective-permute-done((bf16[328,768]{1,0:T(8,128)(2,1)S(1)}, bf16[328,768]{1,0:T(8,128)(2,1)S(1)}, u32[]{:S(2)}, u32[]{:S(2)}) %collective-permute-start.3) | collective-permute-done | bytes 503840 | tf_op jit(solution)/shard_map/ppermute | solution.py:439
  18.9 2.8 %collective-permute-start.6 = (bf16[328,768]{1,0:T(8,128)(2,1)S(1)}, bf16[328,768]{1,0:T(8,128)(2,1)S(1)}, u32[]{:S(2)}, u32[]{:S(2)}) collective-permute-start(bf16[328,768]{1,0:T(8,128)(2,1)S(1)} %get-tuple-element.190.refs_1_), channel_id=1, source_target_pairs={{0,8},{1,9},{2,10},{3,11},{4,0},{5,1},{6,2},{7,3},{8,12},{9,13},{1... | collective-permute-start | bytes 1511432 | tf_op jit(solution)/shard_map/ppermute | solution.py:439
  21.7 1.5 %collective-permute-start.5 = (bf16[328,768]{1,0:T(8,128)(2,1)S(1)}, bf16[328,768]{1,0:T(8,128)(2,1)S(1)}, u32[]{:S(2)}, u32[]{:S(2)}) collective-permute-start(bf16[328,768]{1,0:T(8,128)(2,1)S(1)} %collective-permute-done.3.refs_1_.refs_3_.refs_2_), channel_id=1, source_target_pairs={{0,2},{1,3},{2,0},{3,1},{4,6},{5,7},{6,4},{7,5},{8,10},{9,11},{10,... | collective-permute-start | bytes 1511432 | tf_op jit(solution)/shard_map/ppermute | solution.py:439
  23.2 0.5 %collective-permute-start.9 = (bf16[328,768]{1,0:T(8,128)(2,1)S(1)}, bf16[328,768]{1,0:T(8,128)(2,1)S(1)}, u32[]{:S(2)}, u32[]{:S(2)}) collective-permute-start(bf16[328,768]{1,0:T(8,128)(2,1)S(1)} %collective-permute-done.8.refs_4_.refs_2_), channel_id=1, source_target_pairs={{0,1},{1,0},{2,3},{3,2},{4,5},{5,4},{6,7},{7,6},{8,9},{9,8},{10,11... | collective-permute-start | bytes 1511432 | tf_op jit(solution)/shard_map/ppermute | solution.py:439
  23.7 1.0 %pair.1 = (f32[4,1,640]{2,1,0:T(1,128)S(1)}, f32[3,1,640]{2,1,0:T(1,128)S(1)}, f32[2,1,640]{2,1,0:T(1,128)S(1)}, f32[2,1,640]{2,1,0:T(1,128)S(1)}, bf16[768,640]{1,0:T(8,128)(2,1)S(1)}, /*index=5*/f32[8,640]{1,0:T(8,128)S(1)}) custom-call(s32[3]{0:T(128)S(1)} %pad_add_fusion.refs_0_, bf16[328,768]{1,0:T(8,128)(2,1)S(1)} %collective-permute-done.3.refs_1_.refs_3_.refs_2_, ...), custom_call_target="tpu_custom_call" | custom-call | flops 8589934592 | bytes 1024 | tf_op jit(solution)/shard_map/pair/pallas_call | solution.py:372
  24.7 0.4 collective-permute-done.10.refs_2_
  25.1 2.7 %row.1 = (f32[4,1,640]{2,1,0:T(1,128)S(1)}, f32[3,1,640]{2,1,0:T(1,128)S(1)}, f32[2,1,640]{2,1,0:T(1,128)S(1)}, f32[2,1,640]{2,1,0:T(1,128)S(1)}, bf16[768,640]{1,0:T(8,128)(2,1)}, /*index=5*/f32[8,640]{1,0:T(8,128)}) custom-call(s32[3]{0:T(128)S(1)} %pad_add_fusion.refs_0_, bf16[328,768]{1,0:T(8,128)(2,1)S(1)} %collective-permute-done.7.refs_1_.refs_3_, ...), custom_call_target="tpu_custom_call" | custom-call | flops 1 | bytes 1024 | tf_op jit(solution)/shard_map/row/pallas_call | solution.py:372
  27.8 1.1 %next.1 = (f32[4,1,640]{2,1,0:T(1,128)S(1)}, f32[3,1,640]{2,1,0:T(1,128)S(1)}, f32[2,1,640]{2,1,0:T(1,128)S(1)}, f32[2,1,640]{2,1,0:T(1,128)S(1)}, bf16[768,960]{1,0:T(8,128)(2,1)S(1)}, /*index=5*/f32[8,960]{1,0:T(8,128)S(1)}) custom-call(s32[3]{0:T(128)S(1)} %pad_add_fusion.refs_0_, bf16[328,768]{1,0:T(8,128)(2,1)S(1)} %get-tuple-element.190.refs_1_, ...), custom_call_target="tpu_custom_call" | custom-call | flops 1 | bytes 1024 | tf_op jit(solution)/shard_map/next/pallas_call | solution.py:372
  28.8 4.2 %collective-permute-done.6.refs_1_ = bf16[328,768]{1,0:T(8,128)(2,1)S(1)} collective-permute-done((bf16[328,768]{1,0:T(8,128)(2,1)S(1)}, bf16[328,768]{1,0:T(8,128)(2,1)S(1)}, u32[]{:S(2)}, u32[]{:S(2)}) %collective-permute-start.6) | collective-permute-done | bytes 503840 | tf_op jit(solution)/shard_map/ppermute | solution.py:439
  33.1 2.2 %collective-permute-done.5.refs_4_.refs_2_ = bf16[328,768]{1,0:T(8,128)(2,1)S(1)} collective-permute-done((bf16[328,768]{1,0:T(8,128)(2,1)S(1)}, bf16[328,768]{1,0:T(8,128)(2,1)S(1)}, u32[]{:S(2)}, u32[]{:S(2)}) %collective-permute-start.5) | collective-permute-done | bytes 503840 | tf_op jit(solution)/shard_map/ppermute | solution.py:439
  35.3 1.3 %far.1 = (f32[4,1,640]{2,1,0:T(1,128)S(1)}, f32[3,1,640]{2,1,0:T(1,128)S(1)}, f32[2,1,640]{2,1,0:T(1,128)S(1)}, f32[2,1,640]{2,1,0:T(1,128)S(1)}) custom-call(s32[3]{0:T(128)S(1)} %pad_add_fusion.refs_0_, bf16[328,768]{1,0:T(8,128)(2,1)S(1)} %collective-permute-done.6.refs_1_, bf16[328,768]{1,0:T(8,128)(2,1)S(1)} %collective-permute-done.8.refs_4_.refs_2_, ...), custom_call_target="tpu_custom_call" | custom-call | flops 1 | bytes 1024 | tf_op jit(solution)/shard_map/far/pallas_call | solution.py:372
  36.6 0.6 %collective-permute-start.15 = (f32[3,1,640]{2,1,0:T(1,128)S(1)}, f32[3,1,640]{2,1,0:T(1,128)S(1)}, u32[]{:S(2)}, u32[]{:S(2)}) collective-permute-start(f32[3,1,640]{2,1,0:T(1,128)S(1)} %get-tuple-element.218.refs_6_), channel_id=1, source_target_pairs={{0,1},{1,0},{2,3},{3,2},{4,5},{5,4},{6,7},{7,6},{8,9},{9,8},{10,11... | collective-permute-start | bytes 23048 | tf_op jit(solution)/shard_map/ppermute | solution.py:439
  37.1 0.0 collective-permute-done.12.refs_1_
  37.2 1.3 %last.1 = (f32[4,1,640]{2,1,0:T(1,128)S(1)}, f32[3,1,640]{2,1,0:T(1,128)}, f32[2,1,640]{2,1,0:T(1,128)S(1)}, f32[2,1,640]{2,1,0:T(1,128)S(1)}) custom-call(s32[3]{0:T(128)S(1)} %pad_add_fusion.refs_0_, bf16[328,768]{1,0:T(8,128)(2,1)S(1)} %collective-permute-done.12.refs_1_, bf16[328,768]{1,0:T(8,128)(2,1)S(1)} %collective-permute-done.5.refs_4_.refs_2_, ...), custom_call_target="tpu_custom_call" | custom-call | flops 1 | bytes 1024 | tf_op jit(solution)/shard_map/last/pallas_call | solution.py:372
  38.4 0.1 collective-permute-start.13
  38.6 1.0 %collective-permute-done.13 = f32[2,1,640]{2,1,0:T(1,128)S(1)} collective-permute-done((f32[2,1,640]{2,1,0:T(1,128)S(1)}, f32[2,1,640]{2,1,0:T(1,128)S(1)}, u32[]{:S(2)}, u32[]{:S(2)}) %collective-permute-start.13) | collective-permute-done | bytes 5152 | tf_op jit(solution)/shard_map/ppermute | solution.py:439
  39.6 3.2 %collective-permute-start.14 = (f32[1,1,640]{2,1,0:T(1,128)S(1)}, f32[1,1,640]{2,1,0:T(1,128)S(1)}, u32[]{:S(2)}, u32[]{:S(2)}) collective-permute-start(f32[1,1,640]{2,1,0:T(1,128)S(1)} %get-tuple-element.248.refs_0_), channel_id=1, source_target_pairs={{0,8},{1,9},{2,10},{3,11},{4,12},{5,13},{6,14},{7,15},{8,0},{9,1},... | collective-permute-start | bytes 7688 | tf_op jit(solution)/shard_map/ppermute | solution.py:439
  42.8 0.3 collective-permute-start.17
  43.1 1.5 %collective-permute-start.18 = (f32[1,1,640]{2,1,0:T(1,128)S(1)}, f32[1,1,640]{2,1,0:T(1,128)S(1)}, u32[]{:S(2)}, u32[]{:S(2)}) collective-permute-start(f32[1,1,640]{2,1,0:T(1,128)S(1)} %get-tuple-element.244), channel_id=1, source_target_pairs={{0,2},{1,3},{2,0},{3,1},{4,6},{5,7},{6,4},{7,5},{8,10},{9,11},{10,... | collective-permute-start | bytes 7688 | tf_op jit(solution)/shard_map/ppermute | solution.py:439
  44.7 1.6 %collective-permute-start.19 = (f32[1,1,640]{2,1,0:T(1,128)S(1)}, f32[1,1,640]{2,1,0:T(1,128)S(1)}, u32[]{:S(2)}, u32[]{:S(2)}) collective-permute-start(f32[1,1,640]{2,1,0:T(1,128)S(1)} %get-tuple-element.246), channel_id=1, source_target_pairs={{0,6},{1,7},{2,4},{3,5},{4,2},{5,3},{6,0},{7,1},{8,14},{9,15},{10,... | collective-permute-start | bytes 7688 | tf_op jit(solution)/shard_map/ppermute | solution.py:439
  46.3 0.6 %decide.1 = s32[1]{0:T(128)} custom-call(f32[1,1,640]{2,1,0:T(1,128)S(1)} %get-tuple-element.248.refs_0_, f32[1,1,640]{2,1,0:T(1,128)S(1)} %collective-permute-done.14.refs_1_), custom_call_target="tpu_custom_call" | custom-call | tf_op jit(solution)/shard_map/decide/pallas_call | solution.py:411
  47.6 1.5 %collective-permute-done.19 = f32[1,1,640]{2,1,0:T(1,128)S(1)} collective-permute-done((f32[1,1,640]{2,1,0:T(1,128)S(1)}, f32[1,1,640]{2,1,0:T(1,128)S(1)}, u32[]{:S(2)}, u32[]{:S(2)}) %collective-permute-start.19) | collective-permute-done | bytes 2592 | tf_op jit(solution)/shard_map/ppermute | solution.py:439
  49.2 0.5 conditional.1
  49.2 0.5 finish.1
  49.7 0.0 copy-start.3
  49.7 0.6 %copy-done.3 = f32[512]{0:T(512)} copy-done((f32[512]{0:T(512)}, f32[512]{0:T(512)S(1)}, u32[]{:S(2)}) %copy-start.3) | copy-done | bytes 2072
  (24 shorter events, 0.1 us)
Async XLA Ops:
  3.6 3.2 %collective-permute-start.4 = (bf16[328,768]{1,0:T(8,128)(2,1)S(1)}, bf16[328,768]{1,0:T(8,128)(2,1)S(1)}, u32[]{:S(2)}, u32[]{:S(2)}) collective-permute-start(bf16[328,768]{1,0:T(8,128)(2,1)S(1)} %get-tuple-element.190.refs_1_), channel_id=1, source_target_pairs={{0,1},{1,0},{2,3},{3,2},{4,5},{5,4},{6,7},{7,6},{8,9},{9,8},{10,11... | collective-permute-start | bytes 1511432 | tf_op jit(solution)/shard_map/ppermute | solution.py:439
  4.2 14.7 %collective-permute-start.3 = (bf16[328,768]{1,0:T(8,128)(2,1)S(1)}, bf16[328,768]{1,0:T(8,128)(2,1)S(1)}, u32[]{:S(2)}, u32[]{:S(2)}) collective-permute-start(bf16[328,768]{1,0:T(8,128)(2,1)S(1)} %get-tuple-element.191), channel_id=1, source_target_pairs={{0,4},{1,5},{2,6},{3,7},{4,0},{5,1},{6,2},{7,3},{8,12},{9,13},{10,... | collective-permute-start | bytes 1511432 | tf_op jit(solution)/shard_map/ppermute | solution.py:439
  6.8 16.4 %collective-permute-start.7 = (bf16[328,768]{1,0:T(8,128)(2,1)S(1)}, bf16[328,768]{1,0:T(8,128)(2,1)S(1)}, u32[]{:S(2)}, u32[]{:S(2)}) collective-permute-start(bf16[328,768]{1,0:T(8,128)(2,1)S(1)} %get-tuple-element.190.refs_1_), channel_id=1, source_target_pairs={{0,2},{1,3},{2,0},{3,1},{4,6},{5,7},{6,4},{7,5},{8,10},{9,11},{10,... | collective-permute-start | bytes 1511432 | tf_op jit(solution)/shard_map/ppermute | solution.py:439
  8.6 14.6 %collective-permute-start.8 = (bf16[328,768]{1,0:T(8,128)(2,1)S(1)}, bf16[328,768]{1,0:T(8,128)(2,1)S(1)}, u32[]{:S(2)}, u32[]{:S(2)}) collective-permute-start(bf16[328,768]{1,0:T(8,128)(2,1)S(1)} %get-tuple-element.191), channel_id=1, source_target_pairs={{0,1},{1,0},{2,3},{3,2},{4,8},{5,9},{6,10},{7,11},{8,4},{9,5},{10,... | collective-permute-start | bytes 1511432 | tf_op jit(solution)/shard_map/ppermute | solution.py:439
  18.9 4.8 %collective-permute-start.11 = (bf16[328,768]{1,0:T(8,128)(2,1)S(1)}, bf16[328,768]{1,0:T(8,128)(2,1)S(1)}, u32[]{:S(2)}, u32[]{:S(2)}) collective-permute-start(bf16[328,768]{1,0:T(8,128)(2,1)S(1)} %collective-permute-done.3.refs_1_.refs_3_.refs_2_), channel_id=1, source_target_pairs={{0,1},{1,0},{2,3},{3,2},{4,5},{5,4},{6,7},{7,6},{8,9},{9,8},{10,11... | collective-permute-start | bytes 1511432 | tf_op jit(solution)/shard_map/ppermute | solution.py:439
  18.9 14.2 %collective-permute-start.6 = (bf16[328,768]{1,0:T(8,128)(2,1)S(1)}, bf16[328,768]{1,0:T(8,128)(2,1)S(1)}, u32[]{:S(2)}, u32[]{:S(2)}) collective-permute-start(bf16[328,768]{1,0:T(8,128)(2,1)S(1)} %get-tuple-element.190.refs_1_), channel_id=1, source_target_pairs={{0,8},{1,9},{2,10},{3,11},{4,0},{5,1},{6,2},{7,3},{8,12},{9,13},{1... | collective-permute-start | bytes 1511432 | tf_op jit(solution)/shard_map/ppermute | solution.py:439
  21.7 13.6 %collective-permute-start.5 = (bf16[328,768]{1,0:T(8,128)(2,1)S(1)}, bf16[328,768]{1,0:T(8,128)(2,1)S(1)}, u32[]{:S(2)}, u32[]{:S(2)}) collective-permute-start(bf16[328,768]{1,0:T(8,128)(2,1)S(1)} %collective-permute-done.3.refs_1_.refs_3_.refs_2_), channel_id=1, source_target_pairs={{0,2},{1,3},{2,0},{3,1},{4,6},{5,7},{6,4},{7,5},{8,10},{9,11},{10,... | collective-permute-start | bytes 1511432 | tf_op jit(solution)/shard_map/ppermute | solution.py:439
  23.2 1.9 %collective-permute-start.10 = (bf16[328,768]{1,0:T(8,128)(2,1)S(1)}, bf16[328,768]{1,0:T(8,128)(2,1)S(1)}, u32[]{:S(2)}, u32[]{:S(2)}) collective-permute-start(bf16[328,768]{1,0:T(8,128)(2,1)S(1)} %collective-permute-done.7.refs_1_.refs_3_), channel_id=1, source_target_pairs={{0,1},{1,0},{2,3},{3,2},{4,5},{5,4},{6,7},{7,6},{8,9},{9,8},{10,11... | collective-permute-start | bytes 1511432 | tf_op jit(solution)/shard_map/ppermute | solution.py:439
  23.2 4.6 %collective-permute-start.9 = (bf16[328,768]{1,0:T(8,128)(2,1)S(1)}, bf16[328,768]{1,0:T(8,128)(2,1)S(1)}, u32[]{:S(2)}, u32[]{:S(2)}) collective-permute-start(bf16[328,768]{1,0:T(8,128)(2,1)S(1)} %collective-permute-done.8.refs_4_.refs_2_), channel_id=1, source_target_pairs={{0,1},{1,0},{2,3},{3,2},{4,5},{5,4},{6,7},{7,6},{8,9},{9,8},{10,11... | collective-permute-start | bytes 1511432 | tf_op jit(solution)/shard_map/ppermute | solution.py:439
  35.3 1.9 %collective-permute-start.12 = (bf16[328,768]{1,0:T(8,128)(2,1)S(1)}, bf16[328,768]{1,0:T(8,128)(2,1)S(1)}, u32[]{:S(2)}, u32[]{:S(2)}) collective-permute-start(bf16[328,768]{1,0:T(8,128)(2,1)S(1)} %collective-permute-done.6.refs_1_), channel_id=1, source_target_pairs={{0,1},{1,0},{2,3},{3,2},{4,5},{5,4},{6,7},{7,6},{8,9},{9,8},{10,11... | collective-permute-start | bytes 1511432 | tf_op jit(solution)/shard_map/ppermute | solution.py:439
  36.5 12.6 %copy-start = (bf16[1024,768]{1,0:T(8,128)(2,1)S(1)}, bf16[1024,768]{1,0:T(8,128)(2,1)}, u32[]{:S(2)}) copy-start(bf16[1024,768]{1,0:T(8,128)(2,1)} %refs_3_.1) | copy-start | bytes 4718596
  36.5 12.6 %copy-start.1 = (bf16[512,1024]{1,0:T(8,128)(2,1)S(1)}, bf16[512,1024]{1,0:T(8,128)(2,1)}, u32[]{:S(2)}) copy-start(bf16[512,1024]{1,0:T(8,128)(2,1)} %refs_2_.1) | copy-start | bytes 3145732
  36.5 12.6 %copy-start.2 = (s32[512]{0:T(512)S(1)}, s32[512]{0:T(512)}, u32[]{:S(2)}) copy-start(s32[512]{0:T(512)} %param.9) | copy-start | bytes 6148
  36.6 2.0 %collective-permute-start.15 = (f32[3,1,640]{2,1,0:T(1,128)S(1)}, f32[3,1,640]{2,1,0:T(1,128)S(1)}, u32[]{:S(2)}, u32[]{:S(2)}) collective-permute-start(f32[3,1,640]{2,1,0:T(1,128)S(1)} %get-tuple-element.218.refs_6_), channel_id=1, source_target_pairs={{0,1},{1,0},{2,3},{3,2},{4,5},{5,4},{6,7},{7,6},{8,9},{9,8},{10,11... | collective-permute-start | bytes 23048 | tf_op jit(solution)/shard_map/ppermute | solution.py:439
  38.4 1.2 %collective-permute-start.13 = (f32[2,1,640]{2,1,0:T(1,128)S(1)}, f32[2,1,640]{2,1,0:T(1,128)S(1)}, u32[]{:S(2)}, u32[]{:S(2)}) collective-permute-start(f32[2,1,640]{2,1,0:T(1,128)S(1)} %get-tuple-element.222), channel_id=1, source_target_pairs={{0,1},{1,0},{2,3},{3,2},{4,5},{5,4},{6,7},{7,6},{8,9},{9,8},{10,11... | collective-permute-start | bytes 15368 | tf_op jit(solution)/shard_map/ppermute | solution.py:439
  39.6 6.7 %collective-permute-start.14 = (f32[1,1,640]{2,1,0:T(1,128)S(1)}, f32[1,1,640]{2,1,0:T(1,128)S(1)}, u32[]{:S(2)}, u32[]{:S(2)}) collective-permute-start(f32[1,1,640]{2,1,0:T(1,128)S(1)} %get-tuple-element.248.refs_0_), channel_id=1, source_target_pairs={{0,8},{1,9},{2,10},{3,11},{4,12},{5,13},{6,14},{7,15},{8,0},{9,1},... | collective-permute-start | bytes 7688 | tf_op jit(solution)/shard_map/ppermute | solution.py:439
  42.8 4.8 %collective-permute-start.17 = (f32[1,1,640]{2,1,0:T(1,128)S(1)}, f32[1,1,640]{2,1,0:T(1,128)S(1)}, u32[]{:S(2)}, u32[]{:S(2)}) collective-permute-start(f32[1,1,640]{2,1,0:T(1,128)S(1)} %get-tuple-element.245), channel_id=1, source_target_pairs={{0,4},{1,5},{2,6},{3,7},{4,0},{5,1},{6,2},{7,3},{8,12},{9,13},{10,... | collective-permute-start | bytes 7688 | tf_op jit(solution)/shard_map/ppermute | solution.py:439
  43.1 4.5 %collective-permute-start.18 = (f32[1,1,640]{2,1,0:T(1,128)S(1)}, f32[1,1,640]{2,1,0:T(1,128)S(1)}, u32[]{:S(2)}, u32[]{:S(2)}) collective-permute-start(f32[1,1,640]{2,1,0:T(1,128)S(1)} %get-tuple-element.244), channel_id=1, source_target_pairs={{0,2},{1,3},{2,0},{3,1},{4,6},{5,7},{6,4},{7,5},{8,10},{9,11},{10,... | collective-permute-start | bytes 7688 | tf_op jit(solution)/shard_map/ppermute | solution.py:439
  44.7 4.5 %collective-permute-start.19 = (f32[1,1,640]{2,1,0:T(1,128)S(1)}, f32[1,1,640]{2,1,0:T(1,128)S(1)}, u32[]{:S(2)}, u32[]{:S(2)}) collective-permute-start(f32[1,1,640]{2,1,0:T(1,128)S(1)} %get-tuple-element.246), channel_id=1, source_target_pairs={{0,6},{1,7},{2,4},{3,5},{4,2},{5,3},{6,0},{7,1},{8,14},{9,15},{10,... | collective-permute-start | bytes 7688 | tf_op jit(solution)/shard_map/ppermute | solution.py:439
  46.3 2.8 %collective-permute-start.16 = (f32[1,1,640]{2,1,0:T(1,128)S(1)}, f32[1,1,640]{2,1,0:T(1,128)S(1)}, u32[]{:S(2)}, u32[]{:S(2)}) collective-permute-start(f32[1,1,640]{2,1,0:T(1,128)S(1)} %get-tuple-element.247), channel_id=1, source_target_pairs={{0,1},{1,0},{2,3},{3,2},{4,8},{5,9},{6,10},{7,11},{8,4},{9,5},{10,... | collective-permute-start | bytes 7688 | tf_op jit(solution)/shard_map/ppermute | solution.py:439
  49.7 0.6 %copy-start.3 = (f32[512]{0:T(512)}, f32[512]{0:T(512)S(1)}, u32[]{:S(2)}) copy-start(f32[512]{0:T(512)S(1)} %get-tuple-element.366) | copy-start | bytes 6148

commit v18 on v14

--- a/solution.py
+++ b/solution.py
@@ -241,16 +241,17 @@
 HERE, THERE, ACROSS = (OWN, CORE), (PAIR, PAIR_CORE), (ROW, DIAG)
 
 
-def score_kernel(docs, hot, names, given, made, tasks, doubted, carries, *refs):
+def score_kernel(docs, hot, names, given, made, tasks, doubted, ready, keep, carries, *refs):
     rest, first, flag, lanes = layout(docs, hot)
     place_ref, refs = refs[0], refs[1:]
     blocks, refs = dict(zip(names, refs[:len(names)])), refs[len(names):]
     pairs, refs = {p: refs[2 * k:2 * k + 2] for k, p in enumerate(given)}, refs[2 * len(given):]
+    ready, refs = dict(zip(ready, refs[:len(ready)])), refs[len(ready):]
     before, refs = refs[:len(GROUPS) * carries], refs[len(GROUPS) * carries:]
     outs, refs = refs[:len(GROUPS)], refs[len(GROUPS):]
     if made:
         pairs[made], refs = refs[:2], refs[2:]
-    parts = refs[-1]
+    kept, parts = dict(zip(keep, refs[:len(keep)])), refs[-1]
     for k, out in enumerate(outs):
         out[...] = before[k][...] if carries else jnp.zeros(out.shape, F32)
     spots = {name: (out, k) for out, group in zip(outs, GROUPS) for k, name in enumerate(group)}
@@ -261,7 +262,15 @@
     def meet(count, start):
         lane = slice(start, start + count)
         wide, two = up(count, 128), 2 * count
-        columns = {name: ref[rest:, 0:wide].astype(F32)[0:8, :].T[0:count, :] for name, ref in blocks.items()}
+
+        def column(name):
+            if name in ready:
+                return ready[name][0:count, :]
+            return blocks[name][rest:, 0:wide].astype(F32)[0:8, :].T[0:count, :]
+
+        columns = {name: column(name) for name in made + keep}
+        for name in keep:
+            kept[name][0:count, :] = columns[name]
         if made:
             turned, notes = pairs[made]
             turned[:, 0:two] = jnp.concatenate([blocks[name][:count, :] for name in made], axis=0).T
@@ -273,10 +282,10 @@
                 own_tasks = [task for task in tasks if task[0] == left]
                 rows = count * len(left)
                 block = blocks[left[0]][:count, :]
-                column = columns[left[0]][:, 0:1]
+                mine = [columns[name] if name in columns else column(name) for name in left]
+                mine = mine[0][:, 0:1] if len(mine) == 1 else jnp.concatenate(mine, axis=0)[:, 0:1]
                 for name in left[1:]:
                     block = jnp.concatenate([block, blocks[name][:count, :]], axis=0)
-                    column = jnp.concatenate([column, columns[name][:, 0:1]], axis=0)
                 fresh = True
                 for _, right, both, _ in own_tasks:
                     if right in blocks:
@@ -298,7 +307,7 @@
                             )
                         else:
                             inner = jnp.dot(block, turned[:, low:high], preferred_element_type=F32)
-                        same = column == ids[:, low:high]
+                        same = mine == ids[:, low:high]
                         if diagonal:
                             same &= lax.broadcasted_iota(jnp.int32, inner.shape, 0) != (
                                 lax.broadcasted_iota(jnp.int32, inner.shape, 1) + low
@@ -351,18 +360,22 @@
         out[k] += jnp.where(lax.broadcasted_iota(jnp.int32, (1, lanes), 1) == flag, doubt, 0.0)
 
 
-def score(name, docs, hot, place, blocks, pairs, made, tasks, sums, doubted=(), weight=1):
+def score(name, docs, hot, place, blocks, pairs, made, tasks, sums, cols, doubted=(), keep=(), weight=1):
     rest, _, _, lanes = layout(docs, hot)
     names = list(dict.fromkeys([*made, *(name for task in tasks for name in task[0])]))
     given = [p for p in pairs if any(p == task[1] for task in tasks)]
     width = blocks[OWN].shape[1]
     vmem = pl.BlockSpec(memory_space=pltpu.VMEM)
-    arrays = [blocks[b] for b in names] + [a for p in given for a in pairs[p]] + list(sums)
+    ready = [b for b in names if b in cols]
+    arrays = [blocks[b] for b in names] + [a for p in given for a in pairs[p]] + [cols[b] for b in ready] + list(sums)
     shapes = [jax.ShapeDtypeStruct((len(group), 1, lanes), F32) for group in GROUPS]
     if made:
         shapes += [jax.ShapeDtypeStruct((width, 2 * rest), BF16), jax.ShapeDtypeStruct((8, 2 * rest), F32)]
+    shapes += [jax.ShapeDtypeStruct((rest, 8), F32) for _ in keep]
     out = pl.pallas_call(
-        lambda *refs: score_kernel(docs, hot, names, given, made, tasks, doubted or made, bool(sums), *refs),
+        lambda *refs: score_kernel(
+            docs, hot, names, given, made, tasks, doubted or made, ready, keep, bool(sums), *refs
+        ),
         out_shape=tuple(shapes),
         in_specs=[pl.BlockSpec(memory_space=pltpu.SMEM)] + [vmem] * len(arrays),
         out_specs=tuple(vmem for _ in shapes),
@@ -372,7 +385,8 @@
         name=name,
     )(place, *arrays)
     count = len(GROUPS)
-    return out[:count], {**pairs, made: out[count:]} if made else pairs
+    cols = {**cols, **dict(zip(keep, out[len(out) - len(keep):]))}
+    return out[:count], {**pairs, made: out[count:count + 2]} if made else pairs, cols
 
 
 def finish_kernel(slot_ref, *refs):
@@ -434,15 +448,15 @@
     TO_MIDDLE = (2, 0, 3, 1)
 
     def meet(name, made, tasks, **options):
-        return score(name, docs, hot, place, blocks, pairs, made, tasks, sums, **options)
-
-    blocks, pairs, sums = {OWN: same}, {}, ()
+        return score(name, docs, hot, place, blocks, pairs, made, tasks, sums, cols, **options)
+
+    blocks, pairs, sums, cols = {OWN: same}, {}, (), {}
     blocks[CORE] = move(same, STAY, core=1)
     blocks[PAIR] = move(other, OUTER)
     blocks[CORE], still_same, other = lax.optimization_barrier((blocks[CORE], same, other))
     blocks[ROW] = move(still_same, STAY, row=1)
     blocks[NEXT] = move(other, MIDDLE)
-    sums, pairs = meet("own", HERE, [((OWN,), HERE, False, None), ((CORE,), HERE, False, "core0")], weight=2**33)
+    sums, pairs, cols = meet("own", HERE, [((OWN,), HERE, False, None), ((CORE,), HERE, False, "core0")], weight=2**33)
 
     blocks[PAIR], _ = lax.optimization_barrier((blocks[PAIR], sums[0]))
     blocks[ROW], blocks[NEXT] = lax.optimization_barrier((blocks[ROW], blocks[NEXT]))
@@ -450,21 +464,23 @@
     blocks[PAIR_ROW] = move(blocks[PAIR], STAY, row=1)
     blocks[PAIR_CORE] = move(blocks[PAIR], STAY, core=1)
     blocks[DIAG] = move(blocks[ROW], STAY, core=1)
-    sums, pairs = meet(
+    sums, pairs, cols = meet(
         "pair", THERE,
         [((PAIR,), THERE, False, None), ((PAIR_CORE,), THERE, False, "core1"), ((NEXT,), HERE, True, None),
          ((NEXT,), THERE, True, None)],
-        weight=2**33,
-    )
-    sums, pairs = meet(
+        keep=(NEXT,), weight=2**33,
+    )
+    sums, pairs, cols = meet(
         "row", ACROSS,
         [((PAIR,), HERE, True, None), ((PAIR,), ACROSS, True, None), ((NEXT,), ACROSS, True, None),
          ((ROW,), HERE, False, "row0"), ((DIAG,), HERE, False, "row1")],
     )
     blocks[PAIR_ROW], _ = lax.optimization_barrier((blocks[PAIR_ROW], sums[0]))
     blocks[PAIR_DIAG] = move(blocks[PAIR_ROW], STAY, core=1)
-    sums, pairs = meet("far", (), [((FAR,), p, True, None) for p in (HERE, THERE, ACROSS)])
-    sums, pairs = meet(
+    sums, pairs, cols = meet(
+        "far", (), [((FAR,), p, True, None) for p in (HERE, THERE, ACROSS)], keep=(FAR,)
+    )
+    sums, pairs, cols = meet(
         "last", (),
         [((NEXT, FAR), right, False, None) for right in (PAIR_ROW, PAIR_DIAG)]
         + [((PAIR_ROW,), THERE, False, "row1"), ((PAIR_DIAG,), THERE, False, "row0")],

time: 48.2 us -> 49 us (1.017)
  waiting for transfers between devices: 20.6 us -> 21.5 us
    ppermute x15, waiting for transfers between devices: 20.6 us -> 21.5 us  [move(): return lax.ppermute(a, ('owner', 'split'), pairs)]
  transfers between devices with their start and end apart: 15 -> 15, of which waited for: 6 -> 5; matrix products, arithmetic and copies ran while one was open for 0% -> 0% of each run, Pallas kernels for 11% -> 11%
where the time goes in v18:
time: 49 us; the launch traced here: 48.9 us
  waiting for transfers between devices  21.5 us (44%)
  starting transfers between devices  15.2 us (31%)
  Pallas kernels  10.7 us (22%)
  between operations  0.76 us (2%)
  local copies, waits for them, and re-layouts  0.58 us (1%)
    ppermute x15, waiting for transfers between devices, move(): return lax.ppermute(a, ('owner', 'split'), pairs)  21.5 us
    ppermute x15, starting transfers between devices, move(): return lax.ppermute(a, ('owner', 'split'), pairs)  15.2 us
    pallas_call x5, Pallas kernels, score(): pl.pallas_call(lambda *refs: score_kernel(docs, hot, names, given, made,...  6.04 us
    pallas_call x1, Pallas kernels, prep(): pl.pallas_call(lambda *refs: prep_kernel(hot, *refs), out_shape=(shape((r...  3.56 us
  transfers between devices with their start and end apart: 15, of which 5 were waited for; matrix products, arithmetic and copies ran while one was open for 0% of the time, Pallas kernels for 11%

profile of v18, /device:TPU:0, one launch (start us, length us, event | category | flops | bytes accessed | tf_op | source)
XLA Modules:
  0.0 48.9 jit_solution(4357997896226060955)
XLA Ops:
  0.0 0.1 pad_add_fusion.refs_0_
  0.1 3.6 %prep.1 = (bf16[328,768]{1,0:T(8,128)(2,1)S(1)}, bf16[328,768]{1,0:T(8,128)(2,1)S(1)}, s32[1,512]{1,0:T(1,128)S(1)}) custom-call(s32[3]{0:T(128)S(1)} %pad_add_fusion.refs_0_, s32[1,512]{1,0:T(1,128)} %bitcast.16, bf16[512,1024]{1,0:T(8,128)(2,1)} %refs_2_.1, bf16[1024,768]{1,0:T(8,128)(2,1)} %refs_3_.1), custom_call_target="tpu_custom_call" | custom-call | tf_op jit(solution)/shard_map/prep/pallas_call | solution.py:220
  3.6 0.5 %collective-permute-start.3 = (bf16[328,768]{1,0:T(8,128)(2,1)S(1)}, bf16[328,768]{1,0:T(8,128)(2,1)S(1)}, u32[]{:S(2)}, u32[]{:S(2)}) collective-permute-start(bf16[328,768]{1,0:T(8,128)(2,1)S(1)} %get-tuple-element.187.refs_1_), channel_id=1, source_target_pairs={{0,1},{1,0},{2,3},{3,2},{4,5},{5,4},{6,7},{7,6},{8,9},{9,8},{10,11... | collective-permute-start | bytes 1511432 | tf_op jit(solution)/shard_map/ppermute | solution.py:445
  4.2 2.6 %collective-permute-start.7 = (bf16[328,768]{1,0:T(8,128)(2,1)S(1)}, bf16[328,768]{1,0:T(8,128)(2,1)S(1)}, u32[]{:S(2)}, u32[]{:S(2)}) collective-permute-start(bf16[328,768]{1,0:T(8,128)(2,1)S(1)} %get-tuple-element.188), channel_id=1, source_target_pairs={{0,4},{1,5},{2,6},{3,7},{4,0},{5,1},{6,2},{7,3},{8,12},{9,13},{10,... | collective-permute-start | bytes 1511432 | tf_op jit(solution)/shard_map/ppermute | solution.py:445
  6.8 1.7 %collective-permute-start.4 = (bf16[328,768]{1,0:T(8,128)(2,1)S(1)}, bf16[328,768]{1,0:T(8,128)(2,1)S(1)}, u32[]{:S(2)}, u32[]{:S(2)}) collective-permute-start(bf16[328,768]{1,0:T(8,128)(2,1)S(1)} %get-tuple-element.187.refs_1_), channel_id=1, source_target_pairs={{0,2},{1,3},{2,0},{3,1},{4,6},{5,7},{6,4},{7,5},{8,10},{9,11},{10,... | collective-permute-start | bytes 1511432 | tf_op jit(solution)/shard_map/ppermute | solution.py:445
  8.6 1.4 %own.1 = (f32[4,1,640]{2,1,0:T(1,128)S(1)}, f32[4,1,640]{2,1,0:T(1,128)S(1)}, f32[1,1,640]{2,1,0:T(1,128)S(1)}, f32[1,1,640]{2,1,0:T(1,128)S(1)}, bf16[768,640]{1,0:T(8,128)(2,1)S(1)}, /*index=5*/f32[8,640]{1,0:T(8,128)S(1)}) custom-call(s32[3]{0:T(128)S(1)} %pad_add_fusion.refs_0_, bf16[328,768]{1,0:T(8,128)(2,1)S(1)} %get-tuple-element.187.refs_1_, ...), custom_call_target="tpu_custom_call" | custom-call | flops 8589934592 | bytes 1024 | tf_op jit(solution)/shard_map/own/pallas_call | solution.py:375
  10.0 0.0 collective-permute-start.5
  10.0 8.9 %collective-permute-done.7.refs_1_.refs_3_ = bf16[328,768]{1,0:T(8,128)(2,1)S(1)} collective-permute-done((bf16[328,768]{1,0:T(8,128)(2,1)S(1)}, bf16[328,768]{1,0:T(8,128)(2,1)S(1)}, u32[]{:S(2)}, u32[]{:S(2)}) %collective-permute-start.7) | collective-permute-done | bytes 503840 | tf_op jit(solution)/shard_map/ppermute | solution.py:445
  18.9 2.8 %collective-permute-start.6 = (bf16[328,768]{1,0:T(8,128)(2,1)S(1)}, bf16[328,768]{1,0:T(8,128)(2,1)S(1)}, u32[]{:S(2)}, u32[]{:S(2)}) collective-permute-start(bf16[328,768]{1,0:T(8,128)(2,1)S(1)} %get-tuple-element.187.refs_1_), channel_id=1, source_target_pairs={{0,8},{1,9},{2,10},{3,11},{4,0},{5,1},{6,2},{7,3},{8,12},{9,13},{1... | collective-permute-start | bytes 1511432 | tf_op jit(solution)/shard_map/ppermute | solution.py:445
  21.7 1.5 %collective-permute-start.8 = (bf16[328,768]{1,0:T(8,128)(2,1)S(1)}, bf16[328,768]{1,0:T(8,128)(2,1)S(1)}, u32[]{:S(2)}, u32[]{:S(2)}) collective-permute-start(bf16[328,768]{1,0:T(8,128)(2,1)S(1)} %collective-permute-done.7.refs_1_.refs_3_), channel_id=1, source_target_pairs={{0,2},{1,3},{2,0},{3,1},{4,6},{5,7},{6,4},{7,5},{8,10},{9,11},{10,... | collective-permute-start | bytes 1511432 | tf_op jit(solution)/shard_map/ppermute | solution.py:445
  23.2 0.0 collective-permute-done.4.refs_1_
  23.2 0.0 collective-permute-done.5.refs_3_.refs_4_.refs_1_
  23.2 0.0 collective-permute-start.9
  23.2 1.1 %pair.1 = (f32[4,1,640]{2,1,0:T(1,128)S(1)}, f32[4,1,640]{2,1,0:T(1,128)S(1)}, f32[1,1,640]{2,1,0:T(1,128)S(1)}, f32[1,1,640]{2,1,0:T(1,128)S(1)}, bf16[768,640]...) custom-call(s32[3]{0:T(128)S(1)} %pad_add_fusion.refs_0_, ...), custom_call_target="tpu_custom_call" | custom-call | flops 8589934592 | bytes 1024 | tf_op jit(solution)/shard_map/pair/pallas_call | solution.py:375
  24.3 0.8 %collective-permute-done.9.refs_2_ = bf16[328,768]{1,0:T(8,128)(2,1)S(1)} collective-permute-done((bf16[328,768]{1,0:T(8,128)(2,1)S(1)}, bf16[328,768]{1,0:T(8,128)(2,1)S(1)}, u32[]{:S(2)}, u32[]{:S(2)}) %collective-permute-start.9) | collective-permute-done | bytes 503840 | tf_op jit(solution)/shard_map/ppermute | solution.py:445
  25.1 1.8 %row.1 = (f32[4,1,640]{2,1,0:T(1,128)S(1)}, f32[4,1,640]{2,1,0:T(1,128)S(1)}, f32[1,1,640]{2,1,0:T(1,128)S(1)}, f32[1,1,640]{2,1,0:T(1,128)S(1)}, bf16[768,640]{1,0:T(8,128)(2,1)S(1)}, /*index=5*/f32[8,640]{1,0:T(8,128)S(1)}) custom-call(s32[3]{0:T(128)S(1)} %pad_add_fusion.refs_0_, bf16[328,768]{1,0:T(8,128)(2,1)S(1)} %collective-permute-done.4.refs_1_, ...), custom_call_target="tpu_custom_call" | custom-call | flops 1 | bytes 1024 | tf_op jit(solution)/shard_map/row/pallas_call | solution.py:375
  26.9 8.4 %collective-permute-done.8.refs_3_ = bf16[328,768]{1,0:T(8,128)(2,1)S(1)} collective-permute-done((bf16[328,768]{1,0:T(8,128)(2,1)S(1)}, bf16[328,768]{1,0:T(8,128)(2,1)S(1)}, u32[]{:S(2)}, u32[]{:S(2)}) %collective-permute-start.8) | collective-permute-done | bytes 503840 | tf_op jit(solution)/shard_map/ppermute | solution.py:445
  35.3 0.0 collective-permute-done.6.refs_1_.refs_2_
  35.3 0.7 %far.1 = (f32[4,1,640]{2,1,0:T(1,128)S(1)}, f32[4,1,640]{2,1,0:T(1,128)S(1)}, f32[1,1,640]{2,1,0:T(1,128)S(1)}, f32[1,1,640]{2,1,0:T(1,128)S(1)}, f32[320,8]{1,0:T(8,128)S(1)}) custom-call(s32[3]{0:T(128)S(1)} %pad_add_fusion.refs_0_, bf16[328,768]{1,0:T(8,128)(2,1)S(1)} %collective-permute-done.6.refs_1_.refs_2_, ...), custom_call_target="tpu_custom_call" | custom-call | flops 1 | bytes 1024 | tf_op jit(solution)/shard_map/far/pallas_call | solution.py:375
  36.0 1.2 %collective-permute-done.11.refs_4_ = bf16[328,768]{1,0:T(8,128)(2,1)S(1)} collective-permute-done((bf16[328,768]{1,0:T(8,128)(2,1)S(1)}, bf16[328,768]{1,0:T(8,128)(2,1)S(1)}, u32[]{:S(2)}, u32[]{:S(2)}) %collective-permute-start.11) | collective-permute-done | bytes 503840 | tf_op jit(solution)/shard_map/ppermute | solution.py:445
  37.2 1.1 %last.1 = (f32[4,1,640]{2,1,0:T(1,128)S(1)}, f32[4,1,640]{2,1,0:T(1,128)S(1)}, f32[1,1,640]{2,1,0:T(1,128)S(1)}, f32[1,1,640]{2,1,0:T(1,128)S(1)}) custom-call(s32[3]{0:T(128)S(1)} %pad_add_fusion.refs_0_, bf16[328,768]{1,0:T(8,128)(2,1)S(1)} %collective-permute-done.5.refs_3_.refs_4_.refs_1_, bf16[328,768]{1,0:T(8,128)(2,1)S(1)} %collective-permute-done.6.refs_1_.refs_2_, ...), custom_call_target="tpu_custom_call" | custom-call | flops 1 | bytes 1024 | tf_op jit(solution)/shard_map/last/pallas_call | solution.py:375
  38.3 0.1 collective-permute-start.13
  38.5 2.3 %collective-permute-start.12 = (f32[1,1,640]{2,1,0:T(1,128)S(1)}, f32[1,1,640]{2,1,0:T(1,128)S(1)}, u32[]{:S(2)}, u32[]{:S(2)}) collective-permute-start(f32[1,1,640]{2,1,0:T(1,128)S(1)} %get-tuple-element.218.refs_0_), channel_id=1, source_target_pairs={{0,8},{1,9},{2,10},{3,11},{4,12},{5,13},{6,14},{7,15},{8,0},{9,1},... | collective-permute-start | bytes 7688 | tf_op jit(solution)/shard_map/ppermute | solution.py:445
  40.8 1.0 %collective-permute-start.15 = (f32[1,1,640]{2,1,0:T(1,128)S(1)}, f32[1,1,640]{2,1,0:T(1,128)S(1)}, u32[]{:S(2)}, u32[]{:S(2)}) collective-permute-start(f32[1,1,640]{2,1,0:T(1,128)S(1)} %get-tuple-element.246), channel_id=1, source_target_pairs={{0,4},{1,5},{2,6},{3,7},{4,0},{5,1},{6,2},{7,3},{8,12},{9,13},{10,... | collective-permute-start | bytes 7688 | tf_op jit(solution)/shard_map/ppermute | solution.py:445
  41.8 1.5 %collective-permute-start.16 = (f32[1,1,640]{2,1,0:T(1,128)S(1)}, f32[1,1,640]{2,1,0:T(1,128)S(1)}, u32[]{:S(2)}, u32[]{:S(2)}) collective-permute-start(f32[1,1,640]{2,1,0:T(1,128)S(1)} %get-tuple-element.245), channel_id=1, source_target_pairs={{0,2},{1,3},{2,0},{3,1},{4,6},{5,7},{6,4},{7,5},{8,10},{9,11},{10,... | collective-permute-start | bytes 7688 | tf_op jit(solution)/shard_map/ppermute | solution.py:445
  43.3 1.1 %collective-permute-start.17 = (f32[1,1,640]{2,1,0:T(1,128)S(1)}, f32[1,1,640]{2,1,0:T(1,128)S(1)}, u32[]{:S(2)}, u32[]{:S(2)}) collective-permute-start(f32[1,1,640]{2,1,0:T(1,128)S(1)} %get-tuple-element.244), channel_id=1, source_target_pairs={{0,6},{1,7},{2,4},{3,5},{4,2},{5,3},{6,0},{7,1},{8,14},{9,15},{10,... | collective-permute-start | bytes 7688 | tf_op jit(solution)/shard_map/ppermute | solution.py:445
  44.4 0.6 %decide.1 = s32[1]{0:T(128)} custom-call(f32[1,1,640]{2,1,0:T(1,128)S(1)} %get-tuple-element.218.refs_0_, f32[1,1,640]{2,1,0:T(1,128)S(1)} %collective-permute-done.12.refs_1_), custom_call_target="tpu_custom_call" | custom-call | tf_op jit(solution)/shard_map/decide/pallas_call | solution.py:417
  45.7 2.1 %collective-permute-done.17 = f32[1,1,640]{2,1,0:T(1,128)S(1)} collective-permute-done((f32[1,1,640]{2,1,0:T(1,128)S(1)}, f32[1,1,640]{2,1,0:T(1,128)S(1)}, u32[]{:S(2)}, u32[]{:S(2)}) %collective-permute-start.17) | collective-permute-done | bytes 2592 | tf_op jit(solution)/shard_map/ppermute | solution.py:445
  47.8 0.5 %conditional.1 = (f32[512]{0:T(512)S(1)}) conditional(s32[]{:T(128)} %bitcast.5, (f32[4,1,640]{2,1,0:T(1,128)S(1)}, f32[4,1,640]{2,1,0:T(1,128)S(1)}, s32[1,512]{1,0:T(1,128)S(1)}, f32[1,1,640]{2,1,0:T(1,128)S(1)}, f32[1,1,640]{2,1,0:T(1,128)S(1)}, /*index=5*/f32[1,1,640]{2,1,0:T(1,128)S(1)}, f32[1,1,640]{2,1,0:T(1,128)S(1)}, ...), branch_computations={%region_0.1_spmd, %region_1.8_spmd} | conditional | flops 1617953280 | bytes 16846124 | solution.py:498
  47.8 0.5 finish.1
  48.3 0.0 copy-start.3
  48.3 0.6 %copy-done.3 = f32[512]{0:T(512)} copy-done((f32[512]{0:T(512)}, f32[512]{0:T(512)S(1)}, u32[]{:S(2)}) %copy-start.3) | copy-done | bytes 2072
  (18 shorter events, 0.1 us)
Async XLA Ops:
  3.6 3.2 %collective-permute-start.3 = (bf16[328,768]{1,0:T(8,128)(2,1)S(1)}, bf16[328,768]{1,0:T(8,128)(2,1)S(1)}, u32[]{:S(2)}, u32[]{:S(2)}) collective-permute-start(bf16[328,768]{1,0:T(8,128)(2,1)S(1)} %get-tuple-element.187.refs_1_), channel_id=1, source_target_pairs={{0,1},{1,0},{2,3},{3,2},{4,5},{5,4},{6,7},{7,6},{8,9},{9,8},{10,11... | collective-permute-start | bytes 1511432 | tf_op jit(solution)/shard_map/ppermute | solution.py:445
  4.2 14.7 %collective-permute-start.7 = (bf16[328,768]{1,0:T(8,128)(2,1)S(1)}, bf16[328,768]{1,0:T(8,128)(2,1)S(1)}, u32[]{:S(2)}, u32[]{:S(2)}) collective-permute-start(bf16[328,768]{1,0:T(8,128)(2,1)S(1)} %get-tuple-element.188), channel_id=1, source_target_pairs={{0,4},{1,5},{2,6},{3,7},{4,0},{5,1},{6,2},{7,3},{8,12},{9,13},{10,... | collective-permute-start | bytes 1511432 | tf_op jit(solution)/shard_map/ppermute | solution.py:445
  6.8 16.4 %collective-permute-start.4 = (bf16[328,768]{1,0:T(8,128)(2,1)S(1)}, bf16[328,768]{1,0:T(8,128)(2,1)S(1)}, u32[]{:S(2)}, u32[]{:S(2)}) collective-permute-start(bf16[328,768]{1,0:T(8,128)(2,1)S(1)} %get-tuple-element.187.refs_1_), channel_id=1, source_target_pairs={{0,2},{1,3},{2,0},{3,1},{4,6},{5,7},{6,4},{7,5},{8,10},{9,11},{10,... | collective-permute-start | bytes 1511432 | tf_op jit(solution)/shard_map/ppermute | solution.py:445
  10.0 13.2 %collective-permute-start.5 = (bf16[328,768]{1,0:T(8,128)(2,1)S(1)}, bf16[328,768]{1,0:T(8,128)(2,1)S(1)}, u32[]{:S(2)}, u32[]{:S(2)}) collective-permute-start(bf16[328,768]{1,0:T(8,128)(2,1)S(1)} %get-tuple-element.188), channel_id=1, source_target_pairs={{0,1},{1,0},{2,3},{3,2},{4,8},{5,9},{6,10},{7,11},{8,4},{9,5},{10,... | collective-permute-start | bytes 1511432 | tf_op jit(solution)/shard_map/ppermute | solution.py:445
  18.9 4.3 %collective-permute-start.10 = (bf16[328,768]{1,0:T(8,128)(2,1)S(1)}, bf16[328,768]{1,0:T(8,128)(2,1)S(1)}, u32[]{:S(2)}, u32[]{:S(2)}) collective-permute-start(bf16[328,768]{1,0:T(8,128)(2,1)S(1)} %collective-permute-done.7.refs_1_.refs_3_), channel_id=1, source_target_pairs={{0,1},{1,0},{2,3},{3,2},{4,5},{5,4},{6,7},{7,6},{8,9},{9,8},{10,11... | collective-permute-start | bytes 1511432 | tf_op jit(solution)/shard_map/ppermute | solution.py:445
  18.9 16.4 %collective-permute-start.6 = (bf16[328,768]{1,0:T(8,128)(2,1)S(1)}, bf16[328,768]{1,0:T(8,128)(2,1)S(1)}, u32[]{:S(2)}, u32[]{:S(2)}) collective-permute-start(bf16[328,768]{1,0:T(8,128)(2,1)S(1)} %get-tuple-element.187.refs_1_), channel_id=1, source_target_pairs={{0,8},{1,9},{2,10},{3,11},{4,0},{5,1},{6,2},{7,3},{8,12},{9,13},{1... | collective-permute-start | bytes 1511432 | tf_op jit(solution)/shard_map/ppermute | solution.py:445
  21.7 13.6 %collective-permute-start.8 = (bf16[328,768]{1,0:T(8,128)(2,1)S(1)}, bf16[328,768]{1,0:T(8,128)(2,1)S(1)}, u32[]{:S(2)}, u32[]{:S(2)}) collective-permute-start(bf16[328,768]{1,0:T(8,128)(2,1)S(1)} %collective-permute-done.7.refs_1_.refs_3_), channel_id=1, source_target_pairs={{0,2},{1,3},{2,0},{3,1},{4,6},{5,7},{6,4},{7,5},{8,10},{9,11},{10,... | collective-permute-start | bytes 1511432 | tf_op jit(solution)/shard_map/ppermute | solution.py:445
  23.2 1.9 %collective-permute-start.9 = (bf16[328,768]{1,0:T(8,128)(2,1)S(1)}, bf16[328,768]{1,0:T(8,128)(2,1)S(1)}, u32[]{:S(2)}, u32[]{:S(2)}) collective-permute-start(bf16[328,768]{1,0:T(8,128)(2,1)S(1)} %collective-permute-done.4.refs_1_), channel_id=1, source_target_pairs={{0,1},{1,0},{2,3},{3,2},{4,5},{5,4},{6,7},{7,6},{8,9},{9,8},{10,11... | collective-permute-start | bytes 1511432 | tf_op jit(solution)/shard_map/ppermute | solution.py:445
  35.3 1.9 %collective-permute-start.11 = (bf16[328,768]{1,0:T(8,128)(2,1)S(1)}, bf16[328,768]{1,0:T(8,128)(2,1)S(1)}, u32[]{:S(2)}, u32[]{:S(2)}) collective-permute-start(bf16[328,768]{1,0:T(8,128)(2,1)S(1)} %collective-permute-done.8.refs_3_), channel_id=1, source_target_pairs={{0,1},{1,0},{2,3},{3,2},{4,5},{5,4},{6,7},{7,6},{8,9},{9,8},{10,11... | collective-permute-start | bytes 1511432 | tf_op jit(solution)/shard_map/ppermute | solution.py:445
  37.2 10.6 %copy-start = (bf16[1024,768]{1,0:T(8,128)(2,1)S(1)}, bf16[1024,768]{1,0:T(8,128)(2,1)}, u32[]{:S(2)}) copy-start(bf16[1024,768]{1,0:T(8,128)(2,1)} %refs_3_.1) | copy-start | bytes 4718596
  37.2 10.6 %copy-start.1 = (bf16[512,1024]{1,0:T(8,128)(2,1)S(1)}, bf16[512,1024]{1,0:T(8,128)(2,1)}, u32[]{:S(2)}) copy-start(bf16[512,1024]{1,0:T(8,128)(2,1)} %refs_2_.1) | copy-start | bytes 3145732
  37.2 10.6 %copy-start.2 = (s32[512]{0:T(512)S(1)}, s32[512]{0:T(512)}, u32[]{:S(2)}) copy-start(s32[512]{0:T(512)} %param.9) | copy-start | bytes 6148
  38.3 2.5 %collective-permute-start.13 = (f32[4,1,640]{2,1,0:T(1,128)S(1)}, f32[4,1,640]{2,1,0:T(1,128)S(1)}, u32[]{:S(2)}, u32[]{:S(2)}) collective-permute-start(f32[4,1,640]{2,1,0:T(1,128)S(1)} %get-tuple-element.220), channel_id=1, source_target_pairs={{0,1},{1,0},{2,3},{3,2},{4,5},{5,4},{6,7},{7,6},{8,9},{9,8},{10,11... | collective-permute-start | bytes 30728 | tf_op jit(solution)/shard_map/ppermute | solution.py:445
  38.5 5.9 %collective-permute-start.12 = (f32[1,1,640]{2,1,0:T(1,128)S(1)}, f32[1,1,640]{2,1,0:T(1,128)S(1)}, u32[]{:S(2)}, u32[]{:S(2)}) collective-permute-start(f32[1,1,640]{2,1,0:T(1,128)S(1)} %get-tuple-element.218.refs_0_), channel_id=1, source_target_pairs={{0,8},{1,9},{2,10},{3,11},{4,12},{5,13},{6,14},{7,15},{8,0},{9,1},... | collective-permute-start | bytes 7688 | tf_op jit(solution)/shard_map/ppermute | solution.py:445
  40.8 4.8 %collective-permute-start.15 = (f32[1,1,640]{2,1,0:T(1,128)S(1)}, f32[1,1,640]{2,1,0:T(1,128)S(1)}, u32[]{:S(2)}, u32[]{:S(2)}) collective-permute-start(f32[1,1,640]{2,1,0:T(1,128)S(1)} %get-tuple-element.246), channel_id=1, source_target_pairs={{0,4},{1,5},{2,6},{3,7},{4,0},{5,1},{6,2},{7,3},{8,12},{9,13},{10,... | collective-permute-start | bytes 7688 | tf_op jit(solution)/shard_map/ppermute | solution.py:445
  41.8 3.9 %collective-permute-start.16 = (f32[1,1,640]{2,1,0:T(1,128)S(1)}, f32[1,1,640]{2,1,0:T(1,128)S(1)}, u32[]{:S(2)}, u32[]{:S(2)}) collective-permute-start(f32[1,1,640]{2,1,0:T(1,128)S(1)} %get-tuple-element.245), channel_id=1, source_target_pairs={{0,2},{1,3},{2,0},{3,1},{4,6},{5,7},{6,4},{7,5},{8,10},{9,11},{10,... | collective-permute-start | bytes 7688 | tf_op jit(solution)/shard_map/ppermute | solution.py:445
  43.3 4.5 %collective-permute-start.17 = (f32[1,1,640]{2,1,0:T(1,128)S(1)}, f32[1,1,640]{2,1,0:T(1,128)S(1)}, u32[]{:S(2)}, u32[]{:S(2)}) collective-permute-start(f32[1,1,640]{2,1,0:T(1,128)S(1)} %get-tuple-element.244), channel_id=1, source_target_pairs={{0,6},{1,7},{2,4},{3,5},{4,2},{5,3},{6,0},{7,1},{8,14},{9,15},{10,... | collective-permute-start | bytes 7688 | tf_op jit(solution)/shard_map/ppermute | solution.py:445
  44.4 3.4 %collective-permute-start.14 = (f32[1,1,640]{2,1,0:T(1,128)S(1)}, f32[1,1,640]{2,1,0:T(1,128)S(1)}, u32[]{:S(2)}, u32[]{:S(2)}) collective-permute-start(f32[1,1,640]{2,1,0:T(1,128)S(1)} %get-tuple-element.224), channel_id=1, source_target_pairs={{0,1},{1,0},{2,3},{3,2},{4,8},{5,9},{6,10},{7,11},{8,4},{9,5},{10,... | collective-permute-start | bytes 7688 | tf_op jit(solution)/shard_map/ppermute | solution.py:445
  48.3 0.6 %copy-start.3 = (f32[512]{0:T(512)}, f32[512]{0:T(512)S(1)}, u32[]{:S(2)}) copy-start(f32[512]{0:T(512)S(1)} %get-tuple-element.360) | copy-start | bytes 6148

commit v19 on v18

--- a/solution.py
+++ b/solution.py
@@ -493,7 +493,7 @@
     own, pair, row, pair_row = (kept[k:k + 1] + from_core[k:k + 1] for k in (0, 1, 2, 3))
     home = [
         own, from_next, from_far,
-        move(pair, OUTER), move(row, STAY, row=1), move(pair_row, OUTER, row=1),
+        move(pair, OUTER), move(pair_row, OUTER, row=1), move(row, STAY, row=1),
     ]
     return lax.cond(
         decide(flag, to_far, from_far)[0] > 0,

time: 49 us -> 48.7 us (level)
  transfers between devices with their start and end apart: 15 -> 15, of which waited for: 5 -> 6; matrix products, arithmetic and copies ran while one was open for 0% -> 0% of each run, Pallas kernels for 11% -> 11%
where the time goes in v19:
time: 48.7 us; the launch traced here: 48.6 us
  waiting for transfers between devices  21.2 us (44%)
  starting transfers between devices  15.2 us (31%)
  Pallas kernels  10.7 us (22%)
  between operations  0.75 us (2%)
  local copies, waits for them, and re-layouts  0.58 us (1%)
    ppermute x15, waiting for transfers between devices, move(): return lax.ppermute(a, ('owner', 'split'), pairs)  21.2 us
    ppermute x15, starting transfers between devices, move(): return lax.ppermute(a, ('owner', 'split'), pairs)  15.2 us
    pallas_call x5, Pallas kernels, score(): pl.pallas_call(lambda *refs: score_kernel(docs, hot, names, given, made,...  6.04 us
    pallas_call x1, Pallas kernels, prep(): pl.pallas_call(lambda *refs: prep_kernel(hot, *refs), out_shape=(shape((r...  3.56 us
  transfers between devices with their start and end apart: 15, of which 6 were waited for; matrix products, arithmetic and copies ran while one was open for 0% of the time, Pallas kernels for 11%

profile of v19, /device:TPU:0, one launch (start us, length us, event | category | flops | bytes accessed | tf_op | source)
XLA Modules:
  0.0 48.6 jit_solution(6908080796551279538)
XLA Ops:
  0.0 0.1 pad_add_fusion.refs_0_
  0.1 3.6 %prep.1 = (bf16[328,768]{1,0:T(8,128)(2,1)S(1)}, bf16[328,768]{1,0:T(8,128)(2,1)S(1)}, s32[1,512]{1,0:T(1,128)S(1)}) custom-call(s32[3]{0:T(128)S(1)} %pad_add_fusion.refs_0_, s32[1,512]{1,0:T(1,128)} %bitcast.16, bf16[512,1024]{1,0:T(8,128)(2,1)} %refs_2_.1, bf16[1024,768]{1,0:T(8,128)(2,1)} %refs_3_.1), custom_call_target="tpu_custom_call" | custom-call | tf_op jit(solution)/shard_map/prep/pallas_call | solution.py:220
  3.6 0.5 %collective-permute-start.3 = (bf16[328,768]{1,0:T(8,128)(2,1)S(1)}, bf16[328,768]{1,0:T(8,128)(2,1)S(1)}, u32[]{:S(2)}, u32[]{:S(2)}) collective-permute-start(bf16[328,768]{1,0:T(8,128)(2,1)S(1)} %get-tuple-element.187.refs_1_), channel_id=1, source_target_pairs={{0,1},{1,0},{2,3},{3,2},{4,5},{5,4},{6,7},{7,6},{8,9},{9,8},{10,11... | collective-permute-start | bytes 1511432 | tf_op jit(solution)/shard_map/ppermute | solution.py:445
  4.2 2.6 %collective-permute-start.7 = (bf16[328,768]{1,0:T(8,128)(2,1)S(1)}, bf16[328,768]{1,0:T(8,128)(2,1)S(1)}, u32[]{:S(2)}, u32[]{:S(2)}) collective-permute-start(bf16[328,768]{1,0:T(8,128)(2,1)S(1)} %get-tuple-element.188), channel_id=1, source_target_pairs={{0,4},{1,5},{2,6},{3,7},{4,0},{5,1},{6,2},{7,3},{8,12},{9,13},{10,... | collective-permute-start | bytes 1511432 | tf_op jit(solution)/shard_map/ppermute | solution.py:445
  6.8 0.0 collective-permute-done.3.refs_2_
  6.8 1.7 %collective-permute-start.4 = (bf16[328,768]{1,0:T(8,128)(2,1)S(1)}, bf16[328,768]{1,0:T(8,128)(2,1)S(1)}, u32[]{:S(2)}, u32[]{:S(2)}) collective-permute-start(bf16[328,768]{1,0:T(8,128)(2,1)S(1)} %get-tuple-element.187.refs_1_), channel_id=1, source_target_pairs={{0,2},{1,3},{2,0},{3,1},{4,6},{5,7},{6,4},{7,5},{8,10},{9,11},{10,... | collective-permute-start | bytes 1511432 | tf_op jit(solution)/shard_map/ppermute | solution.py:445
  8.6 1.4 %own.1 = (f32[4,1,640]{2,1,0:T(1,128)S(1)}, f32[4,1,640]{2,1,0:T(1,128)S(1)}, f32[1,1,640]{2,1,0:T(1,128)S(1)}, f32[1,1,640]{2,1,0:T(1,128)S(1)}, bf16[768,640]{1,0:T(8,128)(2,1)S(1)}, /*index=5*/f32[8,640]{1,0:T(8,128)S(1)}) custom-call(s32[3]{0:T(128)S(1)} %pad_add_fusion.refs_0_, bf16[328,768]{1,0:T(8,128)(2,1)S(1)} %get-tuple-element.187.refs_1_, ...), custom_call_target="tpu_custom_call" | custom-call | flops 8589934592 | bytes 1024 | tf_op jit(solution)/shard_map/own/pallas_call | solution.py:375
  10.0 0.0 collective-permute-start.5
  10.0 8.9 %collective-permute-done.7.refs_1_.refs_3_ = bf16[328,768]{1,0:T(8,128)(2,1)S(1)} collective-permute-done((bf16[328,768]{1,0:T(8,128)(2,1)S(1)}, bf16[328,768]{1,0:T(8,128)(2,1)S(1)}, u32[]{:S(2)}, u32[]{:S(2)}) %collective-permute-start.7) | collective-permute-done | bytes 503840 | tf_op jit(solution)/shard_map/ppermute | solution.py:445
  18.9 2.8 %collective-permute-start.6 = (bf16[328,768]{1,0:T(8,128)(2,1)S(1)}, bf16[328,768]{1,0:T(8,128)(2,1)S(1)}, u32[]{:S(2)}, u32[]{:S(2)}) collective-permute-start(bf16[328,768]{1,0:T(8,128)(2,1)S(1)} %get-tuple-element.187.refs_1_), channel_id=1, source_target_pairs={{0,8},{1,9},{2,10},{3,11},{4,0},{5,1},{6,2},{7,3},{8,12},{9,13},{1... | collective-permute-start | bytes 1511432 | tf_op jit(solution)/shard_map/ppermute | solution.py:445
  21.7 1.5 %collective-permute-start.8 = (bf16[328,768]{1,0:T(8,128)(2,1)S(1)}, bf16[328,768]{1,0:T(8,128)(2,1)S(1)}, u32[]{:S(2)}, u32[]{:S(2)}) collective-permute-start(bf16[328,768]{1,0:T(8,128)(2,1)S(1)} %collective-permute-done.7.refs_1_.refs_3_), channel_id=1, source_target_pairs={{0,2},{1,3},{2,0},{3,1},{4,6},{5,7},{6,4},{7,5},{8,10},{9,11},{10,... | collective-permute-start | bytes 1511432 | tf_op jit(solution)/shard_map/ppermute | solution.py:445
  23.2 0.0 collective-permute-done.4.refs_1_
  23.2 0.0 collective-permute-done.5.refs_3_.refs_4_.refs_1_
  23.2 1.1 %pair.1 = (f32[4,1,640]{2,1,0:T(1,128)S(1)}, f32[4,1,640]{2,1,0:T(1,128)S(1)}, f32[1,1,640]{2,1,0:T(1,128)S(1)}, f32[1,1,640]{2,1,0:T(1,128)S(1)}, bf16[768,640]...) custom-call(s32[3]{0:T(128)S(1)} %pad_add_fusion.refs_0_, ...), custom_call_target="tpu_custom_call" | custom-call | flops 8589934592 | bytes 1024 | tf_op jit(solution)/shard_map/pair/pallas_call | solution.py:375
  24.3 0.8 %collective-permute-done.9.refs_2_ = bf16[328,768]{1,0:T(8,128)(2,1)S(1)} collective-permute-done((bf16[328,768]{1,0:T(8,128)(2,1)S(1)}, bf16[328,768]{1,0:T(8,128)(2,1)S(1)}, u32[]{:S(2)}, u32[]{:S(2)}) %collective-permute-start.9) | collective-permute-done | bytes 503840 | tf_op jit(solution)/shard_map/ppermute | solution.py:445
  25.1 1.8 %row.1 = (f32[4,1,640]{2,1,0:T(1,128)S(1)}, f32[4,1,640]{2,1,0:T(1,128)S(1)}, f32[1,1,640]{2,1,0:T(1,128)S(1)}, f32[1,1,640]{2,1,0:T(1,128)S(1)}, bf16[768,640]{1,0:T(8,128)(2,1)S(1)}, /*index=5*/f32[8,640]{1,0:T(8,128)S(1)}) custom-call(s32[3]{0:T(128)S(1)} %pad_add_fusion.refs_0_, bf16[328,768]{1,0:T(8,128)(2,1)S(1)} %collective-permute-done.4.refs_1_, ...), custom_call_target="tpu_custom_call" | custom-call | flops 1 | bytes 1024 | tf_op jit(solution)/shard_map/row/pallas_call | solution.py:375
  26.9 8.4 %collective-permute-done.8.refs_3_ = bf16[328,768]{1,0:T(8,128)(2,1)S(1)} collective-permute-done((bf16[328,768]{1,0:T(8,128)(2,1)S(1)}, bf16[328,768]{1,0:T(8,128)(2,1)S(1)}, u32[]{:S(2)}, u32[]{:S(2)}) %collective-permute-start.8) | collective-permute-done | bytes 503840 | tf_op jit(solution)/shard_map/ppermute | solution.py:445
  35.3 0.7 %far.1 = (f32[4,1,640]{2,1,0:T(1,128)S(1)}, f32[4,1,640]{2,1,0:T(1,128)S(1)}, f32[1,1,640]{2,1,0:T(1,128)S(1)}, f32[1,1,640]{2,1,0:T(1,128)S(1)}, f32[320,8]{1,0:T(8,128)S(1)}) custom-call(s32[3]{0:T(128)S(1)} %pad_add_fusion.refs_0_, bf16[328,768]{1,0:T(8,128)(2,1)S(1)} %collective-permute-done.6.refs_1_.refs_2_, ...), custom_call_target="tpu_custom_call" | custom-call | flops 1 | bytes 1024 | tf_op jit(solution)/shard_map/far/pallas_call | solution.py:375
  36.0 1.2 %collective-permute-done.11.refs_4_ = bf16[328,768]{1,0:T(8,128)(2,1)S(1)} collective-permute-done((bf16[328,768]{1,0:T(8,128)(2,1)S(1)}, bf16[328,768]{1,0:T(8,128)(2,1)S(1)}, u32[]{:S(2)}, u32[]{:S(2)}) %collective-permute-start.11) | collective-permute-done | bytes 503840 | tf_op jit(solution)/shard_map/ppermute | solution.py:445
  37.2 1.1 %last.1 = (f32[4,1,640]{2,1,0:T(1,128)S(1)}, f32[4,1,640]{2,1,0:T(1,128)S(1)}, f32[1,1,640]{2,1,0:T(1,128)S(1)}, f32[1,1,640]{2,1,0:T(1,128)S(1)}) custom-call(s32[3]{0:T(128)S(1)} %pad_add_fusion.refs_0_, bf16[328,768]{1,0:T(8,128)(2,1)S(1)} %collective-permute-done.5.refs_3_.refs_4_.refs_1_, bf16[328,768]{1,0:T(8,128)(2,1)S(1)} %collective-permute-done.6.refs_1_.refs_2_, ...), custom_call_target="tpu_custom_call" | custom-call | flops 1 | bytes 1024 | tf_op jit(solution)/shard_map/last/pallas_call | solution.py:375
  38.3 0.1 collective-permute-start.13
  38.5 2.3 %collective-permute-start.12 = (f32[1,1,640]{2,1,0:T(1,128)S(1)}, f32[1,1,640]{2,1,0:T(1,128)S(1)}, u32[]{:S(2)}, u32[]{:S(2)}) collective-permute-start(f32[1,1,640]{2,1,0:T(1,128)S(1)} %get-tuple-element.218.refs_0_), channel_id=1, source_target_pairs={{0,8},{1,9},{2,10},{3,11},{4,12},{5,13},{6,14},{7,15},{8,0},{9,1},... | collective-permute-start | bytes 7688 | tf_op jit(solution)/shard_map/ppermute | solution.py:445
  40.8 1.0 %collective-permute-start.15 = (f32[1,1,640]{2,1,0:T(1,128)S(1)}, f32[1,1,640]{2,1,0:T(1,128)S(1)}, u32[]{:S(2)}, u32[]{:S(2)}) collective-permute-start(f32[1,1,640]{2,1,0:T(1,128)S(1)} %get-tuple-element.246), channel_id=1, source_target_pairs={{0,4},{1,5},{2,6},{3,7},{4,0},{5,1},{6,2},{7,3},{8,12},{9,13},{10,... | collective-permute-start | bytes 7688 | tf_op jit(solution)/shard_map/ppermute | solution.py:445
  41.8 2.1 %collective-permute-start.16 = (f32[1,1,640]{2,1,0:T(1,128)S(1)}, f32[1,1,640]{2,1,0:T(1,128)S(1)}, u32[]{:S(2)}, u32[]{:S(2)}) collective-permute-start(f32[1,1,640]{2,1,0:T(1,128)S(1)} %get-tuple-element.245), channel_id=1, source_target_pairs={{0,6},{1,7},{2,4},{3,5},{4,2},{5,3},{6,0},{7,1},{8,14},{9,15},{10,... | collective-permute-start | bytes 7688 | tf_op jit(solution)/shard_map/ppermute | solution.py:445
  43.9 0.5 %collective-permute-start.17 = (f32[1,1,640]{2,1,0:T(1,128)S(1)}, f32[1,1,640]{2,1,0:T(1,128)S(1)}, u32[]{:S(2)}, u32[]{:S(2)}) collective-permute-start(f32[1,1,640]{2,1,0:T(1,128)S(1)} %get-tuple-element.244), channel_id=1, source_target_pairs={{0,2},{1,3},{2,0},{3,1},{4,6},{5,7},{6,4},{7,5},{8,10},{9,11},{10,... | collective-permute-start | bytes 7688 | tf_op jit(solution)/shard_map/ppermute | solution.py:445
  44.4 0.6 %decide.1 = s32[1]{0:T(128)} custom-call(f32[1,1,640]{2,1,0:T(1,128)S(1)} %get-tuple-element.218.refs_0_, f32[1,1,640]{2,1,0:T(1,128)S(1)} %collective-permute-done.12.refs_1_), custom_call_target="tpu_custom_call" | custom-call | tf_op jit(solution)/shard_map/decide/pallas_call | solution.py:417
  45.7 0.6 %collective-permute-done.16 = f32[1,1,640]{2,1,0:T(1,128)S(1)} collective-permute-done((f32[1,1,640]{2,1,0:T(1,128)S(1)}, f32[1,1,640]{2,1,0:T(1,128)S(1)}, u32[]{:S(2)}, u32[]{:S(2)}) %collective-permute-start.16) | collective-permute-done | bytes 2592 | tf_op jit(solution)/shard_map/ppermute | solution.py:445
  46.3 1.2 %collective-permute-done.17 = f32[1,1,640]{2,1,0:T(1,128)S(1)} collective-permute-done((f32[1,1,640]{2,1,0:T(1,128)S(1)}, f32[1,1,640]{2,1,0:T(1,128)S(1)}, u32[]{:S(2)}, u32[]{:S(2)}) %collective-permute-start.17) | collective-permute-done | bytes 2592 | tf_op jit(solution)/shard_map/ppermute | solution.py:445
  47.5 0.5 %conditional.1 = (f32[512]{0:T(512)S(1)}) conditional(s32[]{:T(128)} %bitcast.5, (f32[4,1,640]{2,1,0:T(1,128)S(1)}, f32[4,1,640]{2,1,0:T(1,128)S(1)}, s32[1,512]{1,0:T(1,128)S(1)}, f32[1,1,640]{2,1,0:T(1,128)S(1)}, f32[1,1,640]{2,1,0:T(1,128)S(1)}, /*index=5*/f32[1,1,640]{2,1,0:T(1,128)S(1)}, f32[1,1,640]{2,1,0:T(1,128)S(1)}, ...), branch_computations={%region_0.1_spmd, %region_1.8_spmd} | conditional | flops 1617953280 | bytes 16846124 | solution.py:498
  47.5 0.5 finish.1
  48.0 0.0 copy-start.3
  48.0 0.6 %copy-done.3 = f32[512]{0:T(512)} copy-done((f32[512]{0:T(512)}, f32[512]{0:T(512)S(1)}, u32[]{:S(2)}) %copy-start.3) | copy-done | bytes 2072
  (18 shorter events, 0.1 us)
Async XLA Ops:
  3.6 3.2 %collective-permute-start.3 = (bf16[328,768]{1,0:T(8,128)(2,1)S(1)}, bf16[328,768]{1,0:T(8,128)(2,1)S(1)}, u32[]{:S(2)}, u32[]{:S(2)}) collective-permute-start(bf16[328,768]{1,0:T(8,128)(2,1)S(1)} %get-tuple-element.187.refs_1_), channel_id=1, source_target_pairs={{0,1},{1,0},{2,3},{3,2},{4,5},{5,4},{6,7},{7,6},{8,9},{9,8},{10,11... | collective-permute-start | bytes 1511432 | tf_op jit(solution)/shard_map/ppermute | solution.py:445
  4.2 14.7 %collective-permute-start.7 = (bf16[328,768]{1,0:T(8,128)(2,1)S(1)}, bf16[328,768]{1,0:T(8,128)(2,1)S(1)}, u32[]{:S(2)}, u32[]{:S(2)}) collective-permute-start(bf16[328,768]{1,0:T(8,128)(2,1)S(1)} %get-tuple-element.188), channel_id=1, source_target_pairs={{0,4},{1,5},{2,6},{3,7},{4,0},{5,1},{6,2},{7,3},{8,12},{9,13},{10,... | collective-permute-start | bytes 1511432 | tf_op jit(solution)/shard_map/ppermute | solution.py:445
  6.8 16.4 %collective-permute-start.4 = (bf16[328,768]{1,0:T(8,128)(2,1)S(1)}, bf16[328,768]{1,0:T(8,128)(2,1)S(1)}, u32[]{:S(2)}, u32[]{:S(2)}) collective-permute-start(bf16[328,768]{1,0:T(8,128)(2,1)S(1)} %get-tuple-element.187.refs_1_), channel_id=1, source_target_pairs={{0,2},{1,3},{2,0},{3,1},{4,6},{5,7},{6,4},{7,5},{8,10},{9,11},{10,... | collective-permute-start | bytes 1511432 | tf_op jit(solution)/shard_map/ppermute | solution.py:445
  10.0 13.2 %collective-permute-start.5 = (bf16[328,768]{1,0:T(8,128)(2,1)S(1)}, bf16[328,768]{1,0:T(8,128)(2,1)S(1)}, u32[]{:S(2)}, u32[]{:S(2)}) collective-permute-start(bf16[328,768]{1,0:T(8,128)(2,1)S(1)} %get-tuple-element.188), channel_id=1, source_target_pairs={{0,1},{1,0},{2,3},{3,2},{4,8},{5,9},{6,10},{7,11},{8,4},{9,5},{10,... | collective-permute-start | bytes 1511432 | tf_op jit(solution)/shard_map/ppermute | solution.py:445
  18.9 4.3 %collective-permute-start.10 = (bf16[328,768]{1,0:T(8,128)(2,1)S(1)}, bf16[328,768]{1,0:T(8,128)(2,1)S(1)}, u32[]{:S(2)}, u32[]{:S(2)}) collective-permute-start(bf16[328,768]{1,0:T(8,128)(2,1)S(1)} %collective-permute-done.7.refs_1_.refs_3_), channel_id=1, source_target_pairs={{0,1},{1,0},{2,3},{3,2},{4,5},{5,4},{6,7},{7,6},{8,9},{9,8},{10,11... | collective-permute-start | bytes 1511432 | tf_op jit(solution)/shard_map/ppermute | solution.py:445
  18.9 16.4 %collective-permute-start.6 = (bf16[328,768]{1,0:T(8,128)(2,1)S(1)}, bf16[328,768]{1,0:T(8,128)(2,1)S(1)}, u32[]{:S(2)}, u32[]{:S(2)}) collective-permute-start(bf16[328,768]{1,0:T(8,128)(2,1)S(1)} %get-tuple-element.187.refs_1_), channel_id=1, source_target_pairs={{0,8},{1,9},{2,10},{3,11},{4,0},{5,1},{6,2},{7,3},{8,12},{9,13},{1... | collective-permute-start | bytes 1511432 | tf_op jit(solution)/shard_map/ppermute | solution.py:445
  21.7 13.6 %collective-permute-start.8 = (bf16[328,768]{1,0:T(8,128)(2,1)S(1)}, bf16[328,768]{1,0:T(8,128)(2,1)S(1)}, u32[]{:S(2)}, u32[]{:S(2)}) collective-permute-start(bf16[328,768]{1,0:T(8,128)(2,1)S(1)} %collective-permute-done.7.refs_1_.refs_3_), channel_id=1, source_target_pairs={{0,2},{1,3},{2,0},{3,1},{4,6},{5,7},{6,4},{7,5},{8,10},{9,11},{10,... | collective-permute-start | bytes 1511432 | tf_op jit(solution)/shard_map/ppermute | solution.py:445
  23.2 1.9 %collective-permute-start.9 = (bf16[328,768]{1,0:T(8,128)(2,1)S(1)}, bf16[328,768]{1,0:T(8,128)(2,1)S(1)}, u32[]{:S(2)}, u32[]{:S(2)}) collective-permute-start(bf16[328,768]{1,0:T(8,128)(2,1)S(1)} %collective-permute-done.4.refs_1_), channel_id=1, source_target_pairs={{0,1},{1,0},{2,3},{3,2},{4,5},{5,4},{6,7},{7,6},{8,9},{9,8},{10,11... | collective-permute-start | bytes 1511432 | tf_op jit(solution)/shard_map/ppermute | solution.py:445
  35.3 1.9 %collective-permute-start.11 = (bf16[328,768]{1,0:T(8,128)(2,1)S(1)}, bf16[328,768]{1,0:T(8,128)(2,1)S(1)}, u32[]{:S(2)}, u32[]{:S(2)}) collective-permute-start(bf16[328,768]{1,0:T(8,128)(2,1)S(1)} %collective-permute-done.8.refs_3_), channel_id=1, source_target_pairs={{0,1},{1,0},{2,3},{3,2},{4,5},{5,4},{6,7},{7,6},{8,9},{9,8},{10,11... | collective-permute-start | bytes 1511432 | tf_op jit(solution)/shard_map/ppermute | solution.py:445
  37.2 10.3 %copy-start = (bf16[1024,768]{1,0:T(8,128)(2,1)S(1)}, bf16[1024,768]{1,0:T(8,128)(2,1)}, u32[]{:S(2)}) copy-start(bf16[1024,768]{1,0:T(8,128)(2,1)} %refs_3_.1) | copy-start | bytes 4718596
  37.2 10.3 %copy-start.1 = (bf16[512,1024]{1,0:T(8,128)(2,1)S(1)}, bf16[512,1024]{1,0:T(8,128)(2,1)}, u32[]{:S(2)}) copy-start(bf16[512,1024]{1,0:T(8,128)(2,1)} %refs_2_.1) | copy-start | bytes 3145732
  37.2 10.3 %copy-start.2 = (s32[512]{0:T(512)S(1)}, s32[512]{0:T(512)}, u32[]{:S(2)}) copy-start(s32[512]{0:T(512)} %param.9) | copy-start | bytes 6148
  38.3 2.5 %collective-permute-start.13 = (f32[4,1,640]{2,1,0:T(1,128)S(1)}, f32[4,1,640]{2,1,0:T(1,128)S(1)}, u32[]{:S(2)}, u32[]{:S(2)}) collective-permute-start(f32[4,1,640]{2,1,0:T(1,128)S(1)} %get-tuple-element.220), channel_id=1, source_target_pairs={{0,1},{1,0},{2,3},{3,2},{4,5},{5,4},{6,7},{7,6},{8,9},{9,8},{10,11... | collective-permute-start | bytes 30728 | tf_op jit(solution)/shard_map/ppermute | solution.py:445
  38.5 5.9 %collective-permute-start.12 = (f32[1,1,640]{2,1,0:T(1,128)S(1)}, f32[1,1,640]{2,1,0:T(1,128)S(1)}, u32[]{:S(2)}, u32[]{:S(2)}) collective-permute-start(f32[1,1,640]{2,1,0:T(1,128)S(1)} %get-tuple-element.218.refs_0_), channel_id=1, source_target_pairs={{0,8},{1,9},{2,10},{3,11},{4,12},{5,13},{6,14},{7,15},{8,0},{9,1},... | collective-permute-start | bytes 7688 | tf_op jit(solution)/shard_map/ppermute | solution.py:445
  40.8 4.8 %collective-permute-start.15 = (f32[1,1,640]{2,1,0:T(1,128)S(1)}, f32[1,1,640]{2,1,0:T(1,128)S(1)}, u32[]{:S(2)}, u32[]{:S(2)}) collective-permute-start(f32[1,1,640]{2,1,0:T(1,128)S(1)} %get-tuple-element.246), channel_id=1, source_target_pairs={{0,4},{1,5},{2,6},{3,7},{4,0},{5,1},{6,2},{7,3},{8,12},{9,13},{10,... | collective-permute-start | bytes 7688 | tf_op jit(solution)/shard_map/ppermute | solution.py:445
  41.8 4.5 %collective-permute-start.16 = (f32[1,1,640]{2,1,0:T(1,128)S(1)}, f32[1,1,640]{2,1,0:T(1,128)S(1)}, u32[]{:S(2)}, u32[]{:S(2)}) collective-permute-start(f32[1,1,640]{2,1,0:T(1,128)S(1)} %get-tuple-element.245), channel_id=1, source_target_pairs={{0,6},{1,7},{2,4},{3,5},{4,2},{5,3},{6,0},{7,1},{8,14},{9,15},{10,... | collective-permute-start | bytes 7688 | tf_op jit(solution)/shard_map/ppermute | solution.py:445
  43.9 3.6 %collective-permute-start.17 = (f32[1,1,640]{2,1,0:T(1,128)S(1)}, f32[1,1,640]{2,1,0:T(1,128)S(1)}, u32[]{:S(2)}, u32[]{:S(2)}) collective-permute-start(f32[1,1,640]{2,1,0:T(1,128)S(1)} %get-tuple-element.244), channel_id=1, source_target_pairs={{0,2},{1,3},{2,0},{3,1},{4,6},{5,7},{6,4},{7,5},{8,10},{9,11},{10,... | collective-permute-start | bytes 7688 | tf_op jit(solution)/shard_map/ppermute | solution.py:445
  44.4 3.1 %collective-permute-start.14 = (f32[1,1,640]{2,1,0:T(1,128)S(1)}, f32[1,1,640]{2,1,0:T(1,128)S(1)}, u32[]{:S(2)}, u32[]{:S(2)}) collective-permute-start(f32[1,1,640]{2,1,0:T(1,128)S(1)} %get-tuple-element.224), channel_id=1, source_target_pairs={{0,1},{1,0},{2,3},{3,2},{4,8},{5,9},{6,10},{7,11},{8,4},{9,5},{10,... | collective-permute-start | bytes 7688 | tf_op jit(solution)/shard_map/ppermute | solution.py:445
  48.0 0.6 %copy-start.3 = (f32[512]{0:T(512)}, f32[512]{0:T(512)S(1)}, u32[]{:S(2)}) copy-start(f32[512]{0:T(512)S(1)} %get-tuple-element.360) | copy-start | bytes 6148

commit v20 on v14

--- a/solution.py
+++ b/solution.py
@@ -147,7 +147,7 @@
     return rest, first, flag, up(flag + 1, 128)
 
 
-def prep_kernel(hot, place_ref, cl_ref, st_ref, w_ref, same_ref, other_ref, slot_ref, vectors):
+def prep_kernel(hot, place_ref, cl_ref, st_ref, w_ref, same_ref, other_ref, slot_ref, vectors, whole):
     docs = st_ref.shape[0]
     rest, first, flag, lanes = layout(docs, hot)
     tile = 128
@@ -162,9 +162,10 @@
     doubt = jnp.where(jnp.sum(full.astype(F32), axis=0, keepdims=True) == 1.0, 0.0, 1.0)
     in_hot = group == chosen
 
+    whole[...] = jnp.dot(st_ref[...], w_ref[...], preferred_element_type=F32)
     for t in range(docs // tile):
         rows = slice(t * tile, (t + 1) * tile)
-        projected = jnp.dot(st_ref[rows, :], w_ref[...], preferred_element_type=F32)
+        projected = whole[rows, :]
         norm = lax.rsqrt(jnp.sum(projected * projected, axis=1, keepdims=True) + EPS)
         vectors[rows, :] = (projected * (norm * math.sqrt(SCALE))).astype(BF16)
 
@@ -179,8 +180,9 @@
 
     sort = (lax.broadcasted_iota(jnp.int32, (lanes, docs), 0) == slot).astype(F32).astype(BF16)
     cluster_rows = jnp.broadcast_to(cluster.astype(F32), (META, docs)).astype(BF16)
-    sorted_n = jnp.dot(sort[:rest, :], vectors[...], preferred_element_type=F32).astype(BF16)
-    sorted_h = jnp.dot(sort[first:flag, :], vectors[...], preferred_element_type=F32).astype(BF16)
+    both = jnp.concatenate([sort[:rest, :], sort[first:flag, :]], axis=0)
+    moved = jnp.dot(both, vectors[...], preferred_element_type=F32).astype(BF16)
+    sorted_n, sorted_h = moved[:rest], moved[rest:]
     ids = lax.dot_general(
         cluster_rows, sort, (((1,), (1,)), ((), ())), preferred_element_type=F32
     )
@@ -225,7 +227,7 @@
             shape((1, docs), jnp.int32),
         ),
         in_specs=[pl.BlockSpec(memory_space=pltpu.SMEM), vmem, vmem, vmem],
-        scratch_shapes=[pltpu.VMEM((docs, width), BF16)],
+        scratch_shapes=[pltpu.VMEM((docs, width), BF16), pltpu.VMEM((docs, width), F32)],
         compiler_params=pltpu.CompilerParams(vmem_limit_bytes=24 * 2**20),
         name="prep",
     )(place, cluster_of.reshape(1, docs), states, proj_weight)

time: 48.2 us -> 48.6 us (level)
  Pallas kernels: 10.7 us -> 11.2 us
where the time goes in v20:
time: 48.6 us; the launch traced here: 48.5 us
  waiting for transfers between devices  20.6 us (42%)
  starting transfers between devices  15.2 us (31%)
  Pallas kernels  11.2 us (23%)
  between operations  0.77 us (2%)
  local copies, waits for them, and re-layouts  0.59 us (1%)
    ppermute x15, waiting for transfers between devices, move(): return lax.ppermute(a, ('owner', 'split'), pairs)  20.6 us
    ppermute x15, starting transfers between devices, move(): return lax.ppermute(a, ('owner', 'split'), pairs)  15.2 us
    pallas_call x5, Pallas kernels, score(): pl.pallas_call(lambda *refs: score_kernel(docs, hot, names, given, made,...  6.09 us
    pallas_call x1, Pallas kernels, prep(): pl.pallas_call(lambda *refs: prep_kernel(hot, *refs), out_shape=(shape((r...  3.99 us
  transfers between devices with their start and end apart: 15, of which 6 were waited for; matrix products, arithmetic and copies ran while one was open for 0% of the time, Pallas kernels for 11%

profile of v20, /device:TPU:0, one launch (start us, length us, event | category | flops | bytes accessed | tf_op | source)
XLA Modules:
  0.0 48.5 jit_solution(3829412467541434467)
XLA Ops:
  0.0 0.1 pad_add_fusion.refs_0_
  0.1 4.0 %prep.1 = (bf16[328,768]{1,0:T(8,128)(2,1)S(1)}, bf16[328,768]{1,0:T(8,128)(2,1)S(1)}, s32[1,512]{1,0:T(1,128)S(1)}) custom-call(s32[3]{0:T(128)S(1)} %pad_add_fusion.refs_0_, s32[1,512]{1,0:T(1,128)} %bitcast.16, bf16[512,1024]{1,0:T(8,128)(2,1)} %refs_2_.1, bf16[1024,768]{1,0:T(8,128)(2,1)} %refs_3_.1), custom_call_target="tpu_custom_call" | custom-call | tf_op jit(solution)/shard_map/prep/pallas_call | solution.py:222
  4.1 0.5 %collective-permute-start.3 = (bf16[328,768]{1,0:T(8,128)(2,1)S(1)}, bf16[328,768]{1,0:T(8,128)(2,1)S(1)}, u32[]{:S(2)}, u32[]{:S(2)}) collective-permute-start(bf16[328,768]{1,0:T(8,128)(2,1)S(1)} %get-tuple-element.185.refs_1_), channel_id=1, source_target_pairs={{0,1},{1,0},{2,3},{3,2},{4,5},{5,4},{6,7},{7,6},{8,9},{9,8},{10,11... | collective-permute-start | bytes 1511432 | tf_op jit(solution)/shard_map/ppermute | solution.py:433
  4.6 2.7 %collective-permute-start.7 = (bf16[328,768]{1,0:T(8,128)(2,1)S(1)}, bf16[328,768]{1,0:T(8,128)(2,1)S(1)}, u32[]{:S(2)}, u32[]{:S(2)}) collective-permute-start(bf16[328,768]{1,0:T(8,128)(2,1)S(1)} %get-tuple-element.186), channel_id=1, source_target_pairs={{0,4},{1,5},{2,6},{3,7},{4,0},{5,1},{6,2},{7,3},{8,12},{9,13},{10,... | collective-permute-start | bytes 1511432 | tf_op jit(solution)/shard_map/ppermute | solution.py:433
  7.3 1.7 %collective-permute-start.4 = (bf16[328,768]{1,0:T(8,128)(2,1)S(1)}, bf16[328,768]{1,0:T(8,128)(2,1)S(1)}, u32[]{:S(2)}, u32[]{:S(2)}) collective-permute-start(bf16[328,768]{1,0:T(8,128)(2,1)S(1)} %get-tuple-element.185.refs_1_), channel_id=1, source_target_pairs={{0,2},{1,3},{2,0},{3,1},{4,6},{5,7},{6,4},{7,5},{8,10},{9,11},{10,... | collective-permute-start | bytes 1511432 | tf_op jit(solution)/shard_map/ppermute | solution.py:433
  9.0 0.0 collective-permute-start.5
  9.0 1.4 %own.1 = (f32[4,1,640]{2,1,0:T(1,128)S(1)}, f32[4,1,640]{2,1,0:T(1,128)S(1)}, f32[1,1,640]{2,1,0:T(1,128)S(1)}, f32[1,1,640]{2,1,0:T(1,128)S(1)}, bf16[768,640]{1,0:T(8,128)(2,1)S(1)}, /*index=5*/f32[8,640]{1,0:T(8,128)S(1)}) custom-call(s32[3]{0:T(128)S(1)} %pad_add_fusion.refs_0_, bf16[328,768]{1,0:T(8,128)(2,1)S(1)} %get-tuple-element.185.refs_1_, ...), custom_call_target="tpu_custom_call" | custom-call | flops 8589934592 | bytes 1024 | tf_op jit(solution)/shard_map/own/pallas_call | solution.py:366
  10.4 8.9 %collective-permute-done.7.refs_1_.refs_3_ = bf16[328,768]{1,0:T(8,128)(2,1)S(1)} collective-permute-done((bf16[328,768]{1,0:T(8,128)(2,1)S(1)}, bf16[328,768]{1,0:T(8,128)(2,1)S(1)}, u32[]{:S(2)}, u32[]{:S(2)}) %collective-permute-start.7) | collective-permute-done | bytes 503840 | tf_op jit(solution)/shard_map/ppermute | solution.py:433
  19.3 2.8 %collective-permute-start.6 = (bf16[328,768]{1,0:T(8,128)(2,1)S(1)}, bf16[328,768]{1,0:T(8,128)(2,1)S(1)}, u32[]{:S(2)}, u32[]{:S(2)}) collective-permute-start(bf16[328,768]{1,0:T(8,128)(2,1)S(1)} %get-tuple-element.185.refs_1_), channel_id=1, source_target_pairs={{0,8},{1,9},{2,10},{3,11},{4,0},{5,1},{6,2},{7,3},{8,12},{9,13},{1... | collective-permute-start | bytes 1511432 | tf_op jit(solution)/shard_map/ppermute | solution.py:433
  22.1 1.5 %collective-permute-start.8 = (bf16[328,768]{1,0:T(8,128)(2,1)S(1)}, bf16[328,768]{1,0:T(8,128)(2,1)S(1)}, u32[]{:S(2)}, u32[]{:S(2)}) collective-permute-start(bf16[328,768]{1,0:T(8,128)(2,1)S(1)} %collective-permute-done.7.refs_1_.refs_3_), channel_id=1, source_target_pairs={{0,2},{1,3},{2,0},{3,1},{4,6},{5,7},{6,4},{7,5},{8,10},{9,11},{10,... | collective-permute-start | bytes 1511432 | tf_op jit(solution)/shard_map/ppermute | solution.py:433
  23.6 1.1 %pair.1 = (f32[4,1,640]{2,1,0:T(1,128)S(1)}, f32[4,1,640]{2,1,0:T(1,128)S(1)}, f32[1,1,640]{2,1,0:T(1,128)S(1)}, f32[1,1,640]{2,1,0:T(1,128)S(1)}, bf16[768,640]{1,0:T(8,128)(2,1)S(1)}, /*index=5*/f32[8,640]{1,0:T(8,128)S(1)}) custom-call(s32[3]{0:T(128)S(1)} %pad_add_fusion.refs_0_, bf16[328,768]{1,0:T(8,128)(2,1)S(1)} %collective-permute-done.7.refs_1_.refs_3_, ...), custom_call_target="tpu_custom_call" | custom-call | flops 8589934592 | bytes 1024 | tf_op jit(solution)/shard_map/pair/pallas_call | solution.py:366
  24.7 0.8 %collective-permute-done.9.refs_2_ = bf16[328,768]{1,0:T(8,128)(2,1)S(1)} collective-permute-done((bf16[328,768]{1,0:T(8,128)(2,1)S(1)}, bf16[328,768]{1,0:T(8,128)(2,1)S(1)}, u32[]{:S(2)}, u32[]{:S(2)}) %collective-permute-start.9) | collective-permute-done | bytes 503840 | tf_op jit(solution)/shard_map/ppermute | solution.py:433
  25.5 1.8 %row.1 = (f32[4,1,640]{2,1,0:T(1,128)S(1)}, f32[4,1,640]{2,1,0:T(1,128)S(1)}, f32[1,1,640]{2,1,0:T(1,128)S(1)}, f32[1,1,640]{2,1,0:T(1,128)S(1)}, bf16[768,640]{1,0:T(8,128)(2,1)S(1)}, /*index=5*/f32[8,640]{1,0:T(8,128)S(1)}) custom-call(s32[3]{0:T(128)S(1)} %pad_add_fusion.refs_0_, bf16[328,768]{1,0:T(8,128)(2,1)S(1)} %collective-permute-done.4.refs_1_, ...), custom_call_target="tpu_custom_call" | custom-call | flops 1 | bytes 1024 | tf_op jit(solution)/shard_map/row/pallas_call | solution.py:366
  27.3 8.4 %collective-permute-done.8.refs_3_ = bf16[328,768]{1,0:T(8,128)(2,1)S(1)} collective-permute-done((bf16[328,768]{1,0:T(8,128)(2,1)S(1)}, bf16[328,768]{1,0:T(8,128)(2,1)S(1)}, u32[]{:S(2)}, u32[]{:S(2)}) %collective-permute-start.8) | collective-permute-done | bytes 503840 | tf_op jit(solution)/shard_map/ppermute | solution.py:433
  35.7 0.6 %far.1 = (f32[4,1,640]{2,1,0:T(1,128)S(1)}, f32[4,1,640]{2,1,0:T(1,128)S(1)}, f32[1,1,640]{2,1,0:T(1,128)S(1)}, f32[1,1,640]{2,1,0:T(1,128)S(1)}) custom-call(s32[3]{0:T(128)S(1)} %pad_add_fusion.refs_0_, bf16[328,768]{1,0:T(8,128)(2,1)S(1)} %collective-permute-done.6.refs_1_.refs_2_, bf16[768,640]{1,0:T(8,128)(2,1)S(1)} %get-tuple-element.192.refs_4_.refs_5_.refs_2_, ...), custom_call_target="tpu_custom_call" | custom-call | flops 1 | bytes 1024 | tf_op jit(solution)/shard_map/far/pallas_call | solution.py:366
  36.4 0.0 copy-start
  36.4 0.0 copy-start.1
  36.4 0.0 copy-start.2
  36.4 1.2 %collective-permute-done.11.refs_4_ = bf16[328,768]{1,0:T(8,128)(2,1)S(1)} collective-permute-done((bf16[328,768]{1,0:T(8,128)(2,1)S(1)}, bf16[328,768]{1,0:T(8,128)(2,1)S(1)}, u32[]{:S(2)}, u32[]{:S(2)}) %collective-permute-start.11) | collective-permute-done | bytes 503840 | tf_op jit(solution)/shard_map/ppermute | solution.py:433
  37.6 1.2 %last.1 = (f32[4,1,640]{2,1,0:T(1,128)S(1)}, f32[4,1,640]{2,1,0:T(1,128)S(1)}, f32[1,1,640]{2,1,0:T(1,128)S(1)}, f32[1,1,640]{2,1,0:T(1,128)S(1)}) custom-call(s32[3]{0:T(128)S(1)} %pad_add_fusion.refs_0_, bf16[328,768]{1,0:T(8,128)(2,1)S(1)} %collective-permute-done.5.refs_3_.refs_4_.refs_1_, bf16[328,768]{1,0:T(8,128)(2,1)S(1)} %collective-permute-done.6.refs_1_.refs_2_, ...), custom_call_target="tpu_custom_call" | custom-call | flops 1 | bytes 1024 | tf_op jit(solution)/shard_map/last/pallas_call | solution.py:366
  38.8 0.1 collective-permute-start.13
  39.0 2.3 %collective-permute-start.12 = (f32[1,1,640]{2,1,0:T(1,128)S(1)}, f32[1,1,640]{2,1,0:T(1,128)S(1)}, u32[]{:S(2)}, u32[]{:S(2)}) collective-permute-start(f32[1,1,640]{2,1,0:T(1,128)S(1)} %get-tuple-element.214.refs_0_), channel_id=1, source_target_pairs={{0,8},{1,9},{2,10},{3,11},{4,12},{5,13},{6,14},{7,15},{8,0},{9,1},... | collective-permute-start | bytes 7688 | tf_op jit(solution)/shard_map/ppermute | solution.py:433
  41.3 2.0 %collective-permute-start.17 = (f32[1,1,640]{2,1,0:T(1,128)S(1)}, f32[1,1,640]{2,1,0:T(1,128)S(1)}, u32[]{:S(2)}, u32[]{:S(2)}) collective-permute-start(f32[1,1,640]{2,1,0:T(1,128)S(1)} %get-tuple-element.240), channel_id=1, source_target_pairs={{0,6},{1,7},{2,4},{3,5},{4,2},{5,3},{6,0},{7,1},{8,14},{9,15},{10,... | collective-permute-start | bytes 7688 | tf_op jit(solution)/shard_map/ppermute | solution.py:433
  43.3 0.5 %collective-permute-start.16 = (f32[1,1,640]{2,1,0:T(1,128)S(1)}, f32[1,1,640]{2,1,0:T(1,128)S(1)}, u32[]{:S(2)}, u32[]{:S(2)}) collective-permute-start(f32[1,1,640]{2,1,0:T(1,128)S(1)} %get-tuple-element.241), channel_id=1, source_target_pairs={{0,2},{1,3},{2,0},{3,1},{4,6},{5,7},{6,4},{7,5},{8,10},{9,11},{10,... | collective-permute-start | bytes 7688 | tf_op jit(solution)/shard_map/ppermute | solution.py:433
  43.8 1.1 %collective-permute-start.15 = (f32[1,1,640]{2,1,0:T(1,128)S(1)}, f32[1,1,640]{2,1,0:T(1,128)S(1)}, u32[]{:S(2)}, u32[]{:S(2)}) collective-permute-start(f32[1,1,640]{2,1,0:T(1,128)S(1)} %get-tuple-element.242), channel_id=1, source_target_pairs={{0,4},{1,5},{2,6},{3,7},{4,0},{5,1},{6,2},{7,3},{8,12},{9,13},{10,... | collective-permute-start | bytes 7688 | tf_op jit(solution)/shard_map/ppermute | solution.py:433
  44.9 0.6 %decide.1 = s32[1]{0:T(128)} custom-call(f32[1,1,640]{2,1,0:T(1,128)S(1)} %get-tuple-element.214.refs_0_, f32[1,1,640]{2,1,0:T(1,128)S(1)} %collective-permute-done.12.refs_1_), custom_call_target="tpu_custom_call" | custom-call | tf_op jit(solution)/shard_map/decide/pallas_call | solution.py:405
  46.2 0.7 %collective-permute-done.16 = f32[1,1,640]{2,1,0:T(1,128)S(1)} collective-permute-done((f32[1,1,640]{2,1,0:T(1,128)S(1)}, f32[1,1,640]{2,1,0:T(1,128)S(1)}, u32[]{:S(2)}, u32[]{:S(2)}) %collective-permute-start.16) | collective-permute-done | bytes 2592 | tf_op jit(solution)/shard_map/ppermute | solution.py:433
  46.9 0.5 %collective-permute-done.15 = f32[1,1,640]{2,1,0:T(1,128)S(1)} collective-permute-done((f32[1,1,640]{2,1,0:T(1,128)S(1)}, f32[1,1,640]{2,1,0:T(1,128)S(1)}, u32[]{:S(2)}, u32[]{:S(2)}) %collective-permute-start.15) | collective-permute-done | bytes 2592 | tf_op jit(solution)/shard_map/ppermute | solution.py:433
  47.4 0.5 %conditional.1 = (f32[512]{0:T(512)S(1)}) conditional(s32[]{:T(128)} %bitcast.5, (f32[4,1,640]{2,1,0:T(1,128)S(1)}, f32[4,1,640]{2,1,0:T(1,128)S(1)}, s32[1,512]{1,0:T(1,128)S(1)}, f32[1,1,640]{2,1,0:T(1,128)S(1)}, f32[1,1,640]{2,1,0:T(1,128)S(1)}, /*index=5*/f32[1,1,640]{2,1,0:T(1,128)S(1)}, f32[1,1,640]{2,1,0:T(1,128)S(1)}, ...), branch_computations={%region_0.1_spmd, %region_1.8_spmd} | conditional | flops 1617953280 | bytes 16846124 | solution.py:484
  47.4 0.5 finish.1
  47.9 0.0 copy-start.3
  47.9 0.6 %copy-done.3 = f32[512]{0:T(512)} copy-done((f32[512]{0:T(512)}, f32[512]{0:T(512)S(1)}, u32[]{:S(2)}) %copy-start.3) | copy-done | bytes 2072
  (18 shorter events, 0.1 us)
Async XLA Ops:
  4.1 3.2 %collective-permute-start.3 = (bf16[328,768]{1,0:T(8,128)(2,1)S(1)}, bf16[328,768]{1,0:T(8,128)(2,1)S(1)}, u32[]{:S(2)}, u32[]{:S(2)}) collective-permute-start(bf16[328,768]{1,0:T(8,128)(2,1)S(1)} %get-tuple-element.185.refs_1_), channel_id=1, source_target_pairs={{0,1},{1,0},{2,3},{3,2},{4,5},{5,4},{6,7},{7,6},{8,9},{9,8},{10,11... | collective-permute-start | bytes 1511432 | tf_op jit(solution)/shard_map/ppermute | solution.py:433
  4.6 14.7 %collective-permute-start.7 = (bf16[328,768]{1,0:T(8,128)(2,1)S(1)}, bf16[328,768]{1,0:T(8,128)(2,1)S(1)}, u32[]{:S(2)}, u32[]{:S(2)}) collective-permute-start(bf16[328,768]{1,0:T(8,128)(2,1)S(1)} %get-tuple-element.186), channel_id=1, source_target_pairs={{0,4},{1,5},{2,6},{3,7},{4,0},{5,1},{6,2},{7,3},{8,12},{9,13},{10,... | collective-permute-start | bytes 1511432 | tf_op jit(solution)/shard_map/ppermute | solution.py:433
  7.3 16.4 %collective-permute-start.4 = (bf16[328,768]{1,0:T(8,128)(2,1)S(1)}, bf16[328,768]{1,0:T(8,128)(2,1)S(1)}, u32[]{:S(2)}, u32[]{:S(2)}) collective-permute-start(bf16[328,768]{1,0:T(8,128)(2,1)S(1)} %get-tuple-element.185.refs_1_), channel_id=1, source_target_pairs={{0,2},{1,3},{2,0},{3,1},{4,6},{5,7},{6,4},{7,5},{8,10},{9,11},{10,... | collective-permute-start | bytes 1511432 | tf_op jit(solution)/shard_map/ppermute | solution.py:433
  9.0 14.6 %collective-permute-start.5 = (bf16[328,768]{1,0:T(8,128)(2,1)S(1)}, bf16[328,768]{1,0:T(8,128)(2,1)S(1)}, u32[]{:S(2)}, u32[]{:S(2)}) collective-permute-start(bf16[328,768]{1,0:T(8,128)(2,1)S(1)} %get-tuple-element.186), channel_id=1, source_target_pairs={{0,1},{1,0},{2,3},{3,2},{4,8},{5,9},{6,10},{7,11},{8,4},{9,5},{10,... | collective-permute-start | bytes 1511432 | tf_op jit(solution)/shard_map/ppermute | solution.py:433
  19.3 4.3 %collective-permute-start.10 = (bf16[328,768]{1,0:T(8,128)(2,1)S(1)}, bf16[328,768]{1,0:T(8,128)(2,1)S(1)}, u32[]{:S(2)}, u32[]{:S(2)}) collective-permute-start(bf16[328,768]{1,0:T(8,128)(2,1)S(1)} %collective-permute-done.7.refs_1_.refs_3_), channel_id=1, source_target_pairs={{0,1},{1,0},{2,3},{3,2},{4,5},{5,4},{6,7},{7,6},{8,9},{9,8},{10,11... | collective-permute-start | bytes 1511432 | tf_op jit(solution)/shard_map/ppermute | solution.py:433
  19.3 16.4 %collective-permute-start.6 = (bf16[328,768]{1,0:T(8,128)(2,1)S(1)}, bf16[328,768]{1,0:T(8,128)(2,1)S(1)}, u32[]{:S(2)}, u32[]{:S(2)}) collective-permute-start(bf16[328,768]{1,0:T(8,128)(2,1)S(1)} %get-tuple-element.185.refs_1_), channel_id=1, source_target_pairs={{0,8},{1,9},{2,10},{3,11},{4,0},{5,1},{6,2},{7,3},{8,12},{9,13},{1... | collective-permute-start | bytes 1511432 | tf_op jit(solution)/shard_map/ppermute | solution.py:433
  22.1 13.6 %collective-permute-start.8 = (bf16[328,768]{1,0:T(8,128)(2,1)S(1)}, bf16[328,768]{1,0:T(8,128)(2,1)S(1)}, u32[]{:S(2)}, u32[]{:S(2)}) collective-permute-start(bf16[328,768]{1,0:T(8,128)(2,1)S(1)} %collective-permute-done.7.refs_1_.refs_3_), channel_id=1, source_target_pairs={{0,2},{1,3},{2,0},{3,1},{4,6},{5,7},{6,4},{7,5},{8,10},{9,11},{10,... | collective-permute-start | bytes 1511432 | tf_op jit(solution)/shard_map/ppermute | solution.py:433
  23.6 1.9 %collective-permute-start.9 = (bf16[328,768]{1,0:T(8,128)(2,1)S(1)}, bf16[328,768]{1,0:T(8,128)(2,1)S(1)}, u32[]{:S(2)}, u32[]{:S(2)}) collective-permute-start(bf16[328,768]{1,0:T(8,128)(2,1)S(1)} %collective-permute-done.4.refs_1_), channel_id=1, source_target_pairs={{0,1},{1,0},{2,3},{3,2},{4,5},{5,4},{6,7},{7,6},{8,9},{9,8},{10,11... | collective-permute-start | bytes 1511432 | tf_op jit(solution)/shard_map/ppermute | solution.py:433
  35.7 1.9 %collective-permute-start.11 = (bf16[328,768]{1,0:T(8,128)(2,1)S(1)}, bf16[328,768]{1,0:T(8,128)(2,1)S(1)}, u32[]{:S(2)}, u32[]{:S(2)}) collective-permute-start(bf16[328,768]{1,0:T(8,128)(2,1)S(1)} %collective-permute-done.8.refs_3_), channel_id=1, source_target_pairs={{0,1},{1,0},{2,3},{3,2},{4,5},{5,4},{6,7},{7,6},{8,9},{9,8},{10,11... | collective-permute-start | bytes 1511432 | tf_op jit(solution)/shard_map/ppermute | solution.py:433
  36.4 11.0 %copy-start = (bf16[1024,768]{1,0:T(8,128)(2,1)S(1)}, bf16[1024,768]{1,0:T(8,128)(2,1)}, u32[]{:S(2)}) copy-start(bf16[1024,768]{1,0:T(8,128)(2,1)} %refs_3_.1) | copy-start | bytes 4718596
  36.4 11.0 %copy-start.1 = (bf16[512,1024]{1,0:T(8,128)(2,1)S(1)}, bf16[512,1024]{1,0:T(8,128)(2,1)}, u32[]{:S(2)}) copy-start(bf16[512,1024]{1,0:T(8,128)(2,1)} %refs_2_.1) | copy-start | bytes 3145732
  36.4 11.0 %copy-start.2 = (s32[512]{0:T(512)S(1)}, s32[512]{0:T(512)}, u32[]{:S(2)}) copy-start(s32[512]{0:T(512)} %param.9) | copy-start | bytes 6148
  38.8 2.5 %collective-permute-start.13 = (f32[4,1,640]{2,1,0:T(1,128)S(1)}, f32[4,1,640]{2,1,0:T(1,128)S(1)}, u32[]{:S(2)}, u32[]{:S(2)}) collective-permute-start(f32[4,1,640]{2,1,0:T(1,128)S(1)} %get-tuple-element.216), channel_id=1, source_target_pairs={{0,1},{1,0},{2,3},{3,2},{4,5},{5,4},{6,7},{7,6},{8,9},{9,8},{10,11... | collective-permute-start | bytes 30728 | tf_op jit(solution)/shard_map/ppermute | solution.py:433
  39.0 5.9 %collective-permute-start.12 = (f32[1,1,640]{2,1,0:T(1,128)S(1)}, f32[1,1,640]{2,1,0:T(1,128)S(1)}, u32[]{:S(2)}, u32[]{:S(2)}) collective-permute-start(f32[1,1,640]{2,1,0:T(1,128)S(1)} %get-tuple-element.214.refs_0_), channel_id=1, source_target_pairs={{0,8},{1,9},{2,10},{3,11},{4,12},{5,13},{6,14},{7,15},{8,0},{9,1},... | collective-permute-start | bytes 7688 | tf_op jit(solution)/shard_map/ppermute | solution.py:433
  41.3 4.8 %collective-permute-start.17 = (f32[1,1,640]{2,1,0:T(1,128)S(1)}, f32[1,1,640]{2,1,0:T(1,128)S(1)}, u32[]{:S(2)}, u32[]{:S(2)}) collective-permute-start(f32[1,1,640]{2,1,0:T(1,128)S(1)} %get-tuple-element.240), channel_id=1, source_target_pairs={{0,6},{1,7},{2,4},{3,5},{4,2},{5,3},{6,0},{7,1},{8,14},{9,15},{10,... | collective-permute-start | bytes 7688 | tf_op jit(solution)/shard_map/ppermute | solution.py:433
  43.3 3.6 %collective-permute-start.16 = (f32[1,1,640]{2,1,0:T(1,128)S(1)}, f32[1,1,640]{2,1,0:T(1,128)S(1)}, u32[]{:S(2)}, u32[]{:S(2)}) collective-permute-start(f32[1,1,640]{2,1,0:T(1,128)S(1)} %get-tuple-element.241), channel_id=1, source_target_pairs={{0,2},{1,3},{2,0},{3,1},{4,6},{5,7},{6,4},{7,5},{8,10},{9,11},{10,... | collective-permute-start | bytes 7688 | tf_op jit(solution)/shard_map/ppermute | solution.py:433
  43.8 3.6 %collective-permute-start.15 = (f32[1,1,640]{2,1,0:T(1,128)S(1)}, f32[1,1,640]{2,1,0:T(1,128)S(1)}, u32[]{:S(2)}, u32[]{:S(2)}) collective-permute-start(f32[1,1,640]{2,1,0:T(1,128)S(1)} %get-tuple-element.242), channel_id=1, source_target_pairs={{0,4},{1,5},{2,6},{3,7},{4,0},{5,1},{6,2},{7,3},{8,12},{9,13},{10,... | collective-permute-start | bytes 7688 | tf_op jit(solution)/shard_map/ppermute | solution.py:433
  44.9 2.5 %collective-permute-start.14 = (f32[1,1,640]{2,1,0:T(1,128)S(1)}, f32[1,1,640]{2,1,0:T(1,128)S(1)}, u32[]{:S(2)}, u32[]{:S(2)}) collective-permute-start(f32[1,1,640]{2,1,0:T(1,128)S(1)} %get-tuple-element.220), channel_id=1, source_target_pairs={{0,1},{1,0},{2,3},{3,2},{4,8},{5,9},{6,10},{7,11},{8,4},{9,5},{10,... | collective-permute-start | bytes 7688 | tf_op jit(solution)/shard_map/ppermute | solution.py:433
  47.9 0.6 %copy-start.3 = (f32[512]{0:T(512)}, f32[512]{0:T(512)S(1)}, u32[]{:S(2)}) copy-start(f32[512]{0:T(512)S(1)} %get-tuple-element.356) | copy-start | bytes 6148

commit v21 on v14

--- a/solution.py
+++ b/solution.py
@@ -237,7 +237,6 @@
 DIAG, PAIR_DIAG = "diag", "pair_diag"
 NEXT, FAR = "next", "far"
 GROUPS = ((OWN, PAIR, ROW, PAIR_ROW), (CORE, PAIR_CORE, DIAG, PAIR_DIAG), (NEXT,), (FAR,))
-TILE = 256
 HERE, THERE, ACROSS = (OWN, CORE), (PAIR, PAIR_CORE), (ROW, DIAG)
 
 
@@ -277,49 +276,48 @@
                 for name in left[1:]:
                     block = jnp.concatenate([block, blocks[name][:count, :]], axis=0)
                     column = jnp.concatenate([column, columns[name][:, 0:1]], axis=0)
+                step = count // 2
+                totals = [None] * len(own_tasks)
                 fresh = True
-                for _, right, both, _ in own_tasks:
-                    if right in blocks:
-                        span, rights, diagonal = count, (right,), False
-                        ids = blocks[right][rest:, 0:wide].astype(F32)[0:1, 0:count]
-                    else:
-                        turned, notes = pairs[right]
-                        span, rights, diagonal = two if both else wide, right[:1 + both], left == right[:1]
-                        ids = notes[0:1, 0:span]
-                        if not both:
-                            ids = jnp.where(lax.broadcasted_iota(jnp.int32, ids.shape, 1) < count, ids, -1.0)
-                    totals = []
-                    for low in range(0, span, TILE):
-                        high = min(low + TILE, span)
+                for top in range(0, rows, step):
+                    part = None
+                    for index, (_, right, both, _) in enumerate(own_tasks):
                         if right in blocks:
+                            span, diagonal = count, False
+                            ids = blocks[right][rest:, 0:wide].astype(F32)[0:1, 0:count]
                             inner = lax.dot_general(
-                                block, blocks[right][low:high, :], (((1,), (1,)), ((), ())),
+                                block[top:top + step], blocks[right][:count, :], (((1,), (1,)), ((), ())),
                                 preferred_element_type=F32,
                             )
                         else:
-                            inner = jnp.dot(block, turned[:, low:high], preferred_element_type=F32)
-                        same = column == ids[:, low:high]
+                            turned, notes = pairs[right]
+                            span, diagonal = two if both else wide, left == right[:1]
+                            ids = notes[0:1, 0:span]
+                            if not both:
+                                ids = jnp.where(lax.broadcasted_iota(jnp.int32, ids.shape, 1) < count, ids, -1.0)
+                            inner = jnp.dot(
+                                block[top:top + step], turned[:, 0:span], preferred_element_type=F32
+                            )
+                        same = column[top:top + step] == ids
                         if diagonal:
-                            same &= lax.broadcasted_iota(jnp.int32, inner.shape, 0) != (
-                                lax.broadcasted_iota(jnp.int32, inner.shape, 1) + low
+                            same &= lax.broadcasted_iota(jnp.int32, inner.shape, 0) + top != (
+                                lax.broadcasted_iota(jnp.int32, inner.shape, 1)
                             )
                         weights = jnp.where(same, jnp.exp2(inner), 0.0)
-                        totals.append(jnp.sum(weights, axis=0, keepdims=True))
+                        total = jnp.sum(weights, axis=0, keepdims=True)
+                        totals[index] = total if totals[index] is None else totals[index] + total
                         if not diagonal:
-                            part = None
-                            for t in range(0, high - low, 128):
+                            fresh = False
+                            for t in range(0, span, 128):
                                 piece = weights[:, t:t + 128]
                                 if piece.shape[1] < 128:
-                                    blank = jnp.zeros((rows, 128 - piece.shape[1]), F32)
+                                    blank = jnp.zeros((step, 128 - piece.shape[1]), F32)
                                     piece = jnp.concatenate([piece, blank], axis=1)
                                 part = piece if part is None else part + piece
-                            if fresh:
-                                parts[0:rows, :] = part
-                            else:
-                                parts[0:rows, :] += part
-                            fresh = False
-                    total = jnp.concatenate(totals, axis=1) if len(totals) > 1 else totals[0]
-                    for k, name in enumerate(rights):
+                    if part is not None:
+                        parts[top:top + step, :] = part
+                for (_, right, both, _), total in zip(own_tasks, totals):
+                    for k, name in enumerate((right,) if right in blocks else right[:1 + both]):
                         out, spot = spots[name]
                         out[spot, :, lane] += total[:, k * count:(k + 1) * count]
                 if not fresh:

time: 48.2 us -> 48.5 us (level)
  starting transfers between devices: 15.2 us -> 15.7 us
  transfers between devices with their start and end apart: 15 -> 15, of which waited for: 6 -> 6; matrix products, arithmetic and copies ran while one was open for 0% -> 0% of each run, Pallas kernels for 11% -> 12%
where the time goes in v21:
time: 48.5 us; the launch traced here: 48.4 us
  waiting for transfers between devices  20.3 us (42%)
  starting transfers between devices  15.7 us (32%)
  Pallas kernels  10.9 us (22%)
  between operations  0.77 us (2%)
  local copies, waits for them, and re-layouts  0.59 us (1%)
    ppermute x15, waiting for transfers between devices, move(): return lax.ppermute(a, ('owner', 'split'), pairs)  20.3 us
    ppermute x15, starting transfers between devices, move(): return lax.ppermute(a, ('owner', 'split'), pairs)  15.7 us
    pallas_call x5, Pallas kernels, score(): pl.pallas_call(lambda *refs: score_kernel(docs, hot, names, given, made,...  6.29 us
    pallas_call x1, Pallas kernels, prep(): pl.pallas_call(lambda *refs: prep_kernel(hot, *refs), out_shape=(shape((r...  3.56 us
  transfers between devices with their start and end apart: 15, of which 6 were waited for; matrix products, arithmetic and copies ran while one was open for 0% of the time, Pallas kernels for 12%

profile of v21, /device:TPU:0, one launch (start us, length us, event | category | flops | bytes accessed | tf_op | source)
XLA Modules:
  0.0 48.4 jit_solution(7629216349301874705)
XLA Ops:
  0.0 0.1 pad_add_fusion.refs_0_
  0.1 3.6 %prep.1 = (bf16[328,768]{1,0:T(8,128)(2,1)S(1)}, bf16[328,768]{1,0:T(8,128)(2,1)S(1)}, s32[1,512]{1,0:T(1,128)S(1)}) custom-call(s32[3]{0:T(128)S(1)} %pad_add_fusion.refs_0_, s32[1,512]{1,0:T(1,128)} %bitcast.16, bf16[512,1024]{1,0:T(8,128)(2,1)} %refs_2_.1, bf16[1024,768]{1,0:T(8,128)(2,1)} %refs_3_.1), custom_call_target="tpu_custom_call" | custom-call | tf_op jit(solution)/shard_map/prep/pallas_call | solution.py:220
  3.6 0.5 %collective-permute-start.3 = (bf16[328,768]{1,0:T(8,128)(2,1)S(1)}, bf16[328,768]{1,0:T(8,128)(2,1)S(1)}, u32[]{:S(2)}, u32[]{:S(2)}) collective-permute-start(bf16[328,768]{1,0:T(8,128)(2,1)S(1)} %get-tuple-element.185.refs_1_), channel_id=1, source_target_pairs={{0,1},{1,0},{2,3},{3,2},{4,5},{5,4},{6,7},{7,6},{8,9},{9,8},{10,11... | collective-permute-start | bytes 1511432 | tf_op jit(solution)/shard_map/ppermute | solution.py:429
  4.2 2.6 %collective-permute-start.7 = (bf16[328,768]{1,0:T(8,128)(2,1)S(1)}, bf16[328,768]{1,0:T(8,128)(2,1)S(1)}, u32[]{:S(2)}, u32[]{:S(2)}) collective-permute-start(bf16[328,768]{1,0:T(8,128)(2,1)S(1)} %get-tuple-element.186), channel_id=1, source_target_pairs={{0,4},{1,5},{2,6},{3,7},{4,0},{5,1},{6,2},{7,3},{8,12},{9,13},{10,... | collective-permute-start | bytes 1511432 | tf_op jit(solution)/shard_map/ppermute | solution.py:429
  6.8 0.0 collective-permute-done.3.refs_2_
  6.8 1.7 %collective-permute-start.4 = (bf16[328,768]{1,0:T(8,128)(2,1)S(1)}, bf16[328,768]{1,0:T(8,128)(2,1)S(1)}, u32[]{:S(2)}, u32[]{:S(2)}) collective-permute-start(bf16[328,768]{1,0:T(8,128)(2,1)S(1)} %get-tuple-element.185.refs_1_), channel_id=1, source_target_pairs={{0,2},{1,3},{2,0},{3,1},{4,6},{5,7},{6,4},{7,5},{8,10},{9,11},{10,... | collective-permute-start | bytes 1511432 | tf_op jit(solution)/shard_map/ppermute | solution.py:429
  8.6 1.4 %own.1 = (f32[4,1,640]{2,1,0:T(1,128)S(1)}, f32[4,1,640]{2,1,0:T(1,128)S(1)}, f32[1,1,640]{2,1,0:T(1,128)S(1)}, f32[1,1,640]{2,1,0:T(1,128)S(1)}, bf16[768,640]{1,0:T(8,128)(2,1)S(1)}, /*index=5*/f32[8,640]{1,0:T(8,128)S(1)}) custom-call(s32[3]{0:T(128)S(1)} %pad_add_fusion.refs_0_, bf16[328,768]{1,0:T(8,128)(2,1)S(1)} %get-tuple-element.185.refs_1_, ...), custom_call_target="tpu_custom_call" | custom-call | flops 8589934592 | bytes 1024 | tf_op jit(solution)/shard_map/own/pallas_call | solution.py:362
  10.0 8.9 %collective-permute-done.7.refs_1_.refs_3_ = bf16[328,768]{1,0:T(8,128)(2,1)S(1)} collective-permute-done((bf16[328,768]{1,0:T(8,128)(2,1)S(1)}, bf16[328,768]{1,0:T(8,128)(2,1)S(1)}, u32[]{:S(2)}, u32[]{:S(2)}) %collective-permute-start.7) | collective-permute-done | bytes 503840 | tf_op jit(solution)/shard_map/ppermute | solution.py:429
  18.9 2.8 %collective-permute-start.6 = (bf16[328,768]{1,0:T(8,128)(2,1)S(1)}, bf16[328,768]{1,0:T(8,128)(2,1)S(1)}, u32[]{:S(2)}, u32[]{:S(2)}) collective-permute-start(bf16[328,768]{1,0:T(8,128)(2,1)S(1)} %get-tuple-element.185.refs_1_), channel_id=1, source_target_pairs={{0,8},{1,9},{2,10},{3,11},{4,0},{5,1},{6,2},{7,3},{8,12},{9,13},{1... | collective-permute-start | bytes 1511432 | tf_op jit(solution)/shard_map/ppermute | solution.py:429
  21.7 1.5 %collective-permute-start.8 = (bf16[328,768]{1,0:T(8,128)(2,1)S(1)}, bf16[328,768]{1,0:T(8,128)(2,1)S(1)}, u32[]{:S(2)}, u32[]{:S(2)}) collective-permute-start(bf16[328,768]{1,0:T(8,128)(2,1)S(1)} %collective-permute-done.7.refs_1_.refs_3_), channel_id=1, source_target_pairs={{0,2},{1,3},{2,0},{3,1},{4,6},{5,7},{6,4},{7,5},{8,10},{9,11},{10,... | collective-permute-start | bytes 1511432 | tf_op jit(solution)/shard_map/ppermute | solution.py:429
  23.2 1.1 %pair.1 = (f32[4,1,640]{2,1,0:T(1,128)S(1)}, f32[4,1,640]{2,1,0:T(1,128)S(1)}, f32[1,1,640]{2,1,0:T(1,128)S(1)}, f32[1,1,640]{2,1,0:T(1,128)S(1)}, bf16[768,640]{1,0:T(8,128)(2,1)S(1)}, /*index=5*/f32[8,640]{1,0:T(8,128)S(1)}) custom-call(s32[3]{0:T(128)S(1)} %pad_add_fusion.refs_0_, bf16[328,768]{1,0:T(8,128)(2,1)S(1)} %collective-permute-done.7.refs_1_.refs_3_, ...), custom_call_target="tpu_custom_call" | custom-call | flops 8589934592 | bytes 1024 | tf_op jit(solution)/shard_map/pair/pallas_call | solution.py:362
  24.3 0.8 %collective-permute-done.9.refs_2_ = bf16[328,768]{1,0:T(8,128)(2,1)S(1)} collective-permute-done((bf16[328,768]{1,0:T(8,128)(2,1)S(1)}, bf16[328,768]{1,0:T(8,128)(2,1)S(1)}, u32[]{:S(2)}, u32[]{:S(2)}) %collective-permute-start.9) | collective-permute-done | bytes 503840 | tf_op jit(solution)/shard_map/ppermute | solution.py:429
  25.1 1.8 %row.1 = (f32[4,1,640]{2,1,0:T(1,128)S(1)}, f32[4,1,640]{2,1,0:T(1,128)S(1)}, f32[1,1,640]{2,1,0:T(1,128)S(1)}, f32[1,1,640]{2,1,0:T(1,128)S(1)}, bf16[768,640]{1,0:T(8,128)(2,1)S(1)}, /*index=5*/f32[8,640]{1,0:T(8,128)S(1)}) custom-call(s32[3]{0:T(128)S(1)} %pad_add_fusion.refs_0_, bf16[328,768]{1,0:T(8,128)(2,1)S(1)} %collective-permute-done.4.refs_1_, ...), custom_call_target="tpu_custom_call" | custom-call | flops 1 | bytes 1024 | tf_op jit(solution)/shard_map/row/pallas_call | solution.py:362
  26.9 8.4 %collective-permute-done.8.refs_3_ = bf16[328,768]{1,0:T(8,128)(2,1)S(1)} collective-permute-done((bf16[328,768]{1,0:T(8,128)(2,1)S(1)}, bf16[328,768]{1,0:T(8,128)(2,1)S(1)}, u32[]{:S(2)}, u32[]{:S(2)}) %collective-permute-start.8) | collective-permute-done | bytes 503840 | tf_op jit(solution)/shard_map/ppermute | solution.py:429
  35.3 0.8 %far.1 = (f32[4,1,640]{2,1,0:T(1,128)S(1)}, f32[4,1,640]{2,1,0:T(1,128)S(1)}, f32[1,1,640]{2,1,0:T(1,128)S(1)}, f32[1,1,640]{2,1,0:T(1,128)S(1)}) custom-call(s32[3]{0:T(128)S(1)} %pad_add_fusion.refs_0_, bf16[328,768]{1,0:T(8,128)(2,1)S(1)} %collective-permute-done.6.refs_1_.refs_2_, bf16[768,640]{1,0:T(8,128)(2,1)S(1)} %get-tuple-element.192.refs_4_.refs_5_.refs_2_, ...), custom_call_target="tpu_custom_call" | custom-call | flops 1 | bytes 1024 | tf_op jit(solution)/shard_map/far/pallas_call | solution.py:362
  36.1 0.0 copy-start
  36.1 0.0 copy-start.1
  36.1 0.0 copy-start.2
  36.2 1.0 %collective-permute-done.11.refs_4_ = bf16[328,768]{1,0:T(8,128)(2,1)S(1)} collective-permute-done((bf16[328,768]{1,0:T(8,128)(2,1)S(1)}, bf16[328,768]{1,0:T(8,128)(2,1)S(1)}, u32[]{:S(2)}, u32[]{:S(2)}) %collective-permute-start.11) | collective-permute-done | bytes 503840 | tf_op jit(solution)/shard_map/ppermute | solution.py:429
  37.2 1.2 %last.1 = (f32[4,1,640]{2,1,0:T(1,128)S(1)}, f32[4,1,640]{2,1,0:T(1,128)S(1)}, f32[1,1,640]{2,1,0:T(1,128)S(1)}, f32[1,1,640]{2,1,0:T(1,128)S(1)}) custom-call(s32[3]{0:T(128)S(1)} %pad_add_fusion.refs_0_, bf16[328,768]{1,0:T(8,128)(2,1)S(1)} %collective-permute-done.5.refs_3_.refs_4_.refs_1_, bf16[328,768]{1,0:T(8,128)(2,1)S(1)} %collective-permute-done.6.refs_1_.refs_2_, ...), custom_call_target="tpu_custom_call" | custom-call | flops 1 | bytes 1024 | tf_op jit(solution)/shard_map/last/pallas_call | solution.py:362
  38.3 0.2 collective-permute-start.13
  38.5 2.8 %collective-permute-start.12 = (f32[1,1,640]{2,1,0:T(1,128)S(1)}, f32[1,1,640]{2,1,0:T(1,128)S(1)}, u32[]{:S(2)}, u32[]{:S(2)}) collective-permute-start(f32[1,1,640]{2,1,0:T(1,128)S(1)} %get-tuple-element.214.refs_0_), channel_id=1, source_target_pairs={{0,8},{1,9},{2,10},{3,11},{4,12},{5,13},{6,14},{7,15},{8,0},{9,1},... | collective-permute-start | bytes 7688 | tf_op jit(solution)/shard_map/ppermute | solution.py:429
  41.3 1.9 %collective-permute-start.17 = (f32[1,1,640]{2,1,0:T(1,128)S(1)}, f32[1,1,640]{2,1,0:T(1,128)S(1)}, u32[]{:S(2)}, u32[]{:S(2)}) collective-permute-start(f32[1,1,640]{2,1,0:T(1,128)S(1)} %get-tuple-element.240), channel_id=1, source_target_pairs={{0,6},{1,7},{2,4},{3,5},{4,2},{5,3},{6,0},{7,1},{8,14},{9,15},{10,... | collective-permute-start | bytes 7688 | tf_op jit(solution)/shard_map/ppermute | solution.py:429
  43.2 0.5 %collective-permute-start.16 = (f32[1,1,640]{2,1,0:T(1,128)S(1)}, f32[1,1,640]{2,1,0:T(1,128)S(1)}, u32[]{:S(2)}, u32[]{:S(2)}) collective-permute-start(f32[1,1,640]{2,1,0:T(1,128)S(1)} %get-tuple-element.241), channel_id=1, source_target_pairs={{0,2},{1,3},{2,0},{3,1},{4,6},{5,7},{6,4},{7,5},{8,10},{9,11},{10,... | collective-permute-start | bytes 7688 | tf_op jit(solution)/shard_map/ppermute | solution.py:429
  43.7 1.1 %collective-permute-start.15 = (f32[1,1,640]{2,1,0:T(1,128)S(1)}, f32[1,1,640]{2,1,0:T(1,128)S(1)}, u32[]{:S(2)}, u32[]{:S(2)}) collective-permute-start(f32[1,1,640]{2,1,0:T(1,128)S(1)} %get-tuple-element.242), channel_id=1, source_target_pairs={{0,4},{1,5},{2,6},{3,7},{4,0},{5,1},{6,2},{7,3},{8,12},{9,13},{10,... | collective-permute-start | bytes 7688 | tf_op jit(solution)/shard_map/ppermute | solution.py:429
  44.8 0.6 %decide.1 = s32[1]{0:T(128)} custom-call(f32[1,1,640]{2,1,0:T(1,128)S(1)} %get-tuple-element.214.refs_0_, f32[1,1,640]{2,1,0:T(1,128)S(1)} %collective-permute-done.12.refs_1_), custom_call_target="tpu_custom_call" | custom-call | tf_op jit(solution)/shard_map/decide/pallas_call | solution.py:401
  46.1 0.6 %collective-permute-done.16 = f32[1,1,640]{2,1,0:T(1,128)S(1)} collective-permute-done((f32[1,1,640]{2,1,0:T(1,128)S(1)}, f32[1,1,640]{2,1,0:T(1,128)S(1)}, u32[]{:S(2)}, u32[]{:S(2)}) %collective-permute-start.16) | collective-permute-done | bytes 2592 | tf_op jit(solution)/shard_map/ppermute | solution.py:429
  46.8 0.5 %collective-permute-done.15 = f32[1,1,640]{2,1,0:T(1,128)S(1)} collective-permute-done((f32[1,1,640]{2,1,0:T(1,128)S(1)}, f32[1,1,640]{2,1,0:T(1,128)S(1)}, u32[]{:S(2)}, u32[]{:S(2)}) %collective-permute-start.15) | collective-permute-done | bytes 2592 | tf_op jit(solution)/shard_map/ppermute | solution.py:429
  47.3 0.5 %conditional.1 = (f32[512]{0:T(512)S(1)}) conditional(s32[]{:T(128)} %bitcast.5, (f32[4,1,640]{2,1,0:T(1,128)S(1)}, f32[4,1,640]{2,1,0:T(1,128)S(1)}, s32[1,512]{1,0:T(1,128)S(1)}, f32[1,1,640]{2,1,0:T(1,128)S(1)}, f32[1,1,640]{2,1,0:T(1,128)S(1)}, /*index=5*/f32[1,1,640]{2,1,0:T(1,128)S(1)}, f32[1,1,640]{2,1,0:T(1,128)S(1)}, ...), branch_computations={%region_0.1_spmd, %region_1.8_spmd} | conditional | flops 1617953280 | bytes 16846124 | solution.py:480
  47.3 0.5 finish.1
  47.8 0.0 copy-start.3
  47.8 0.6 %copy-done.3 = f32[512]{0:T(512)} copy-done((f32[512]{0:T(512)}, f32[512]{0:T(512)S(1)}, u32[]{:S(2)}) %copy-start.3) | copy-done | bytes 2072
  (18 shorter events, 0.1 us)
Async XLA Ops:
  3.6 3.2 %collective-permute-start.3 = (bf16[328,768]{1,0:T(8,128)(2,1)S(1)}, bf16[328,768]{1,0:T(8,128)(2,1)S(1)}, u32[]{:S(2)}, u32[]{:S(2)}) collective-permute-start(bf16[328,768]{1,0:T(8,128)(2,1)S(1)} %get-tuple-element.185.refs_1_), channel_id=1, source_target_pairs={{0,1},{1,0},{2,3},{3,2},{4,5},{5,4},{6,7},{7,6},{8,9},{9,8},{10,11... | collective-permute-start | bytes 1511432 | tf_op jit(solution)/shard_map/ppermute | solution.py:429
  4.2 14.7 %collective-permute-start.7 = (bf16[328,768]{1,0:T(8,128)(2,1)S(1)}, bf16[328,768]{1,0:T(8,128)(2,1)S(1)}, u32[]{:S(2)}, u32[]{:S(2)}) collective-permute-start(bf16[328,768]{1,0:T(8,128)(2,1)S(1)} %get-tuple-element.186), channel_id=1, source_target_pairs={{0,4},{1,5},{2,6},{3,7},{4,0},{5,1},{6,2},{7,3},{8,12},{9,13},{10,... | collective-permute-start | bytes 1511432 | tf_op jit(solution)/shard_map/ppermute | solution.py:429
  6.8 16.4 %collective-permute-start.4 = (bf16[328,768]{1,0:T(8,128)(2,1)S(1)}, bf16[328,768]{1,0:T(8,128)(2,1)S(1)}, u32[]{:S(2)}, u32[]{:S(2)}) collective-permute-start(bf16[328,768]{1,0:T(8,128)(2,1)S(1)} %get-tuple-element.185.refs_1_), channel_id=1, source_target_pairs={{0,2},{1,3},{2,0},{3,1},{4,6},{5,7},{6,4},{7,5},{8,10},{9,11},{10,... | collective-permute-start | bytes 1511432 | tf_op jit(solution)/shard_map/ppermute | solution.py:429
  8.6 14.6 %collective-permute-start.5 = (bf16[328,768]{1,0:T(8,128)(2,1)S(1)}, bf16[328,768]{1,0:T(8,128)(2,1)S(1)}, u32[]{:S(2)}, u32[]{:S(2)}) collective-permute-start(bf16[328,768]{1,0:T(8,128)(2,1)S(1)} %get-tuple-element.186), channel_id=1, source_target_pairs={{0,1},{1,0},{2,3},{3,2},{4,8},{5,9},{6,10},{7,11},{8,4},{9,5},{10,... | collective-permute-start | bytes 1511432 | tf_op jit(solution)/shard_map/ppermute | solution.py:429
  18.9 4.3 %collective-permute-start.10 = (bf16[328,768]{1,0:T(8,128)(2,1)S(1)}, bf16[328,768]{1,0:T(8,128)(2,1)S(1)}, u32[]{:S(2)}, u32[]{:S(2)}) collective-permute-start(bf16[328,768]{1,0:T(8,128)(2,1)S(1)} %collective-permute-done.7.refs_1_.refs_3_), channel_id=1, source_target_pairs={{0,1},{1,0},{2,3},{3,2},{4,5},{5,4},{6,7},{7,6},{8,9},{9,8},{10,11... | collective-permute-start | bytes 1511432 | tf_op jit(solution)/shard_map/ppermute | solution.py:429
  18.9 16.4 %collective-permute-start.6 = (bf16[328,768]{1,0:T(8,128)(2,1)S(1)}, bf16[328,768]{1,0:T(8,128)(2,1)S(1)}, u32[]{:S(2)}, u32[]{:S(2)}) collective-permute-start(bf16[328,768]{1,0:T(8,128)(2,1)S(1)} %get-tuple-element.185.refs_1_), channel_id=1, source_target_pairs={{0,8},{1,9},{2,10},{3,11},{4,0},{5,1},{6,2},{7,3},{8,12},{9,13},{1... | collective-permute-start | bytes 1511432 | tf_op jit(solution)/shard_map/ppermute | solution.py:429
  21.7 13.6 %collective-permute-start.8 = (bf16[328,768]{1,0:T(8,128)(2,1)S(1)}, bf16[328,768]{1,0:T(8,128)(2,1)S(1)}, u32[]{:S(2)}, u32[]{:S(2)}) collective-permute-start(bf16[328,768]{1,0:T(8,128)(2,1)S(1)} %collective-permute-done.7.refs_1_.refs_3_), channel_id=1, source_target_pairs={{0,2},{1,3},{2,0},{3,1},{4,6},{5,7},{6,4},{7,5},{8,10},{9,11},{10,... | collective-permute-start | bytes 1511432 | tf_op jit(solution)/shard_map/ppermute | solution.py:429
  23.2 1.9 %collective-permute-start.9 = (bf16[328,768]{1,0:T(8,128)(2,1)S(1)}, bf16[328,768]{1,0:T(8,128)(2,1)S(1)}, u32[]{:S(2)}, u32[]{:S(2)}) collective-permute-start(bf16[328,768]{1,0:T(8,128)(2,1)S(1)} %collective-permute-done.4.refs_1_), channel_id=1, source_target_pairs={{0,1},{1,0},{2,3},{3,2},{4,5},{5,4},{6,7},{7,6},{8,9},{9,8},{10,11... | collective-permute-start | bytes 1511432 | tf_op jit(solution)/shard_map/ppermute | solution.py:429
  35.3 1.9 %collective-permute-start.11 = (bf16[328,768]{1,0:T(8,128)(2,1)S(1)}, bf16[328,768]{1,0:T(8,128)(2,1)S(1)}, u32[]{:S(2)}, u32[]{:S(2)}) collective-permute-start(bf16[328,768]{1,0:T(8,128)(2,1)S(1)} %collective-permute-done.8.refs_3_), channel_id=1, source_target_pairs={{0,1},{1,0},{2,3},{3,2},{4,5},{5,4},{6,7},{7,6},{8,9},{9,8},{10,11... | collective-permute-start | bytes 1511432 | tf_op jit(solution)/shard_map/ppermute | solution.py:429
  36.1 11.2 %copy-start = (bf16[1024,768]{1,0:T(8,128)(2,1)S(1)}, bf16[1024,768]{1,0:T(8,128)(2,1)}, u32[]{:S(2)}) copy-start(bf16[1024,768]{1,0:T(8,128)(2,1)} %refs_3_.1) | copy-start | bytes 4718596
  36.1 11.2 %copy-start.1 = (bf16[512,1024]{1,0:T(8,128)(2,1)S(1)}, bf16[512,1024]{1,0:T(8,128)(2,1)}, u32[]{:S(2)}) copy-start(bf16[512,1024]{1,0:T(8,128)(2,1)} %refs_2_.1) | copy-start | bytes 3145732
  36.1 11.1 %copy-start.2 = (s32[512]{0:T(512)S(1)}, s32[512]{0:T(512)}, u32[]{:S(2)}) copy-start(s32[512]{0:T(512)} %param.9) | copy-start | bytes 6148
  38.3 2.9 %collective-permute-start.13 = (f32[4,1,640]{2,1,0:T(1,128)S(1)}, f32[4,1,640]{2,1,0:T(1,128)S(1)}, u32[]{:S(2)}, u32[]{:S(2)}) collective-permute-start(f32[4,1,640]{2,1,0:T(1,128)S(1)} %get-tuple-element.216), channel_id=1, source_target_pairs={{0,1},{1,0},{2,3},{3,2},{4,5},{5,4},{6,7},{7,6},{8,9},{9,8},{10,11... | collective-permute-start | bytes 30728 | tf_op jit(solution)/shard_map/ppermute | solution.py:429
  38.5 6.3 %collective-permute-start.12 = (f32[1,1,640]{2,1,0:T(1,128)S(1)}, f32[1,1,640]{2,1,0:T(1,128)S(1)}, u32[]{:S(2)}, u32[]{:S(2)}) collective-permute-start(f32[1,1,640]{2,1,0:T(1,128)S(1)} %get-tuple-element.214.refs_0_), channel_id=1, source_target_pairs={{0,8},{1,9},{2,10},{3,11},{4,12},{5,13},{6,14},{7,15},{8,0},{9,1},... | collective-permute-start | bytes 7688 | tf_op jit(solution)/shard_map/ppermute | solution.py:429
  41.3 4.8 %collective-permute-start.17 = (f32[1,1,640]{2,1,0:T(1,128)S(1)}, f32[1,1,640]{2,1,0:T(1,128)S(1)}, u32[]{:S(2)}, u32[]{:S(2)}) collective-permute-start(f32[1,1,640]{2,1,0:T(1,128)S(1)} %get-tuple-element.240), channel_id=1, source_target_pairs={{0,6},{1,7},{2,4},{3,5},{4,2},{5,3},{6,0},{7,1},{8,14},{9,15},{10,... | collective-permute-start | bytes 7688 | tf_op jit(solution)/shard_map/ppermute | solution.py:429
  43.2 3.6 %collective-permute-start.16 = (f32[1,1,640]{2,1,0:T(1,128)S(1)}, f32[1,1,640]{2,1,0:T(1,128)S(1)}, u32[]{:S(2)}, u32[]{:S(2)}) collective-permute-start(f32[1,1,640]{2,1,0:T(1,128)S(1)} %get-tuple-element.241), channel_id=1, source_target_pairs={{0,2},{1,3},{2,0},{3,1},{4,6},{5,7},{6,4},{7,5},{8,10},{9,11},{10,... | collective-permute-start | bytes 7688 | tf_op jit(solution)/shard_map/ppermute | solution.py:429
  43.7 3.6 %collective-permute-start.15 = (f32[1,1,640]{2,1,0:T(1,128)S(1)}, f32[1,1,640]{2,1,0:T(1,128)S(1)}, u32[]{:S(2)}, u32[]{:S(2)}) collective-permute-start(f32[1,1,640]{2,1,0:T(1,128)S(1)} %get-tuple-element.242), channel_id=1, source_target_pairs={{0,4},{1,5},{2,6},{3,7},{4,0},{5,1},{6,2},{7,3},{8,12},{9,13},{10,... | collective-permute-start | bytes 7688 | tf_op jit(solution)/shard_map/ppermute | solution.py:429
  44.8 2.5 %collective-permute-start.14 = (f32[1,1,640]{2,1,0:T(1,128)S(1)}, f32[1,1,640]{2,1,0:T(1,128)S(1)}, u32[]{:S(2)}, u32[]{:S(2)}) collective-permute-start(f32[1,1,640]{2,1,0:T(1,128)S(1)} %get-tuple-element.220), channel_id=1, source_target_pairs={{0,1},{1,0},{2,3},{3,2},{4,8},{5,9},{6,10},{7,11},{8,4},{9,5},{10,... | collective-permute-start | bytes 7688 | tf_op jit(solution)/shard_map/ppermute | solution.py:429
  47.8 0.6 %copy-start.3 = (f32[512]{0:T(512)}, f32[512]{0:T(512)S(1)}, u32[]{:S(2)}) copy-start(f32[512]{0:T(512)S(1)} %get-tuple-element.356) | copy-start | bytes 6148

commit v22 on v14

--- a/solution.py
+++ b/solution.py
@@ -168,11 +168,19 @@
         norm = lax.rsqrt(jnp.sum(projected * projected, axis=1, keepdims=True) + EPS)
         vectors[rows, :] = (projected * (norm * math.sqrt(SCALE))).astype(BF16)
 
+    hot_row = in_hot.astype(F32)
+    runs = [hot_row[:, t:t + 128] for t in range(0, docs, 128)]
     ahead = (
-        lax.broadcasted_iota(jnp.int32, (docs, docs), 0) < lax.broadcasted_iota(jnp.int32, (docs, docs), 1)
+        lax.broadcasted_iota(jnp.int32, (128, 128), 0) < lax.broadcasted_iota(jnp.int32, (128, 128), 1)
     ).astype(F32).astype(BF16)
-    hot_rows = jnp.broadcast_to(in_hot.astype(F32), (8, docs)).astype(BF16)
-    rank = jnp.dot(hot_rows, ahead, preferred_element_type=F32)[0:1, :].astype(jnp.int32)
+    stack = jnp.concatenate(runs + [jnp.zeros((16 - len(runs), 128), F32)], axis=0)
+    within = jnp.dot(stack.astype(BF16), ahead, preferred_element_type=F32)
+    sizes = jnp.sum(stack, axis=1, keepdims=True)
+    ranks, before = [], jnp.zeros((1, 1), F32)
+    for k in range(len(runs)):
+        ranks.append(within[k:k + 1, :] + before)
+        before = before + sizes[k:k + 1, :]
+    rank = jnp.concatenate(ranks, axis=1).astype(jnp.int32)
     place = lax.broadcasted_iota(jnp.int32, (1, docs), 1)
     slot = jnp.where(in_hot, first + rank, place - rank)
     slot_ref[...] = slot

time: 48.2 us -> 48.2 us (level)
  no operation moved by 1% of the time
where the time goes in v22:
time: 48.2 us; the launch traced here: 48.1 us
  waiting for transfers between devices  20.6 us (43%)
  starting transfers between devices  15.2 us (32%)
  Pallas kernels  10.8 us (22%)
  between operations  0.77 us (2%)
  local copies, waits for them, and re-layouts  0.59 us (1%)
    ppermute x15, waiting for transfers between devices, move(): return lax.ppermute(a, ('owner', 'split'), pairs)  20.6 us
    ppermute x15, starting transfers between devices, move(): return lax.ppermute(a, ('owner', 'split'), pairs)  15.2 us
    pallas_call x5, Pallas kernels, score(): pl.pallas_call(lambda *refs: score_kernel(docs, hot, names, given, made,...  6.11 us
    pallas_call x1, Pallas kernels, prep(): pl.pallas_call(lambda *refs: prep_kernel(hot, *refs), out_shape=(shape((r...  3.6 us
  transfers between devices with their start and end apart: 15, of which 6 were waited for; matrix products, arithmetic and copies ran while one was open for 0% of the time, Pallas kernels for 11%

profile of v22, /device:TPU:0, one launch (start us, length us, event | category | flops | bytes accessed | tf_op | source)
XLA Modules:
  0.0 48.1 jit_solution(11010493708973789490)
XLA Ops:
  0.0 0.1 pad_add_fusion.refs_0_
  0.1 3.6 %prep.1 = (bf16[328,768]{1,0:T(8,128)(2,1)S(1)}, bf16[328,768]{1,0:T(8,128)(2,1)S(1)}, s32[1,512]{1,0:T(1,128)S(1)}) custom-call(s32[3]{0:T(128)S(1)} %pad_add_fusion.refs_0_, s32[1,512]{1,0:T(1,128)} %bitcast.16, bf16[512,1024]{1,0:T(8,128)(2,1)} %refs_2_.1, bf16[1024,768]{1,0:T(8,128)(2,1)} %refs_3_.1), custom_call_target="tpu_custom_call" | custom-call | tf_op jit(solution)/shard_map/prep/pallas_call | solution.py:228
  3.7 0.5 %collective-permute-start.3 = (bf16[328,768]{1,0:T(8,128)(2,1)S(1)}, bf16[328,768]{1,0:T(8,128)(2,1)S(1)}, u32[]{:S(2)}, u32[]{:S(2)}) collective-permute-start(bf16[328,768]{1,0:T(8,128)(2,1)S(1)} %get-tuple-element.185.refs_1_), channel_id=1, source_target_pairs={{0,1},{1,0},{2,3},{3,2},{4,5},{5,4},{6,7},{7,6},{8,9},{9,8},{10,11... | collective-permute-start | bytes 1511432 | tf_op jit(solution)/shard_map/ppermute | solution.py:439
  4.2 2.6 %collective-permute-start.7 = (bf16[328,768]{1,0:T(8,128)(2,1)S(1)}, bf16[328,768]{1,0:T(8,128)(2,1)S(1)}, u32[]{:S(2)}, u32[]{:S(2)}) collective-permute-start(bf16[328,768]{1,0:T(8,128)(2,1)S(1)} %get-tuple-element.186), channel_id=1, source_target_pairs={{0,4},{1,5},{2,6},{3,7},{4,0},{5,1},{6,2},{7,3},{8,12},{9,13},{10,... | collective-permute-start | bytes 1511432 | tf_op jit(solution)/shard_map/ppermute | solution.py:439
  6.9 1.7 %collective-permute-start.4 = (bf16[328,768]{1,0:T(8,128)(2,1)S(1)}, bf16[328,768]{1,0:T(8,128)(2,1)S(1)}, u32[]{:S(2)}, u32[]{:S(2)}) collective-permute-start(bf16[328,768]{1,0:T(8,128)(2,1)S(1)} %get-tuple-element.185.refs_1_), channel_id=1, source_target_pairs={{0,2},{1,3},{2,0},{3,1},{4,6},{5,7},{6,4},{7,5},{8,10},{9,11},{10,... | collective-permute-start | bytes 1511432 | tf_op jit(solution)/shard_map/ppermute | solution.py:439
  8.6 1.4 %own.1 = (f32[4,1,640]{2,1,0:T(1,128)S(1)}, f32[4,1,640]{2,1,0:T(1,128)S(1)}, f32[1,1,640]{2,1,0:T(1,128)S(1)}, f32[1,1,640]{2,1,0:T(1,128)S(1)}, bf16[768,640]{1,0:T(8,128)(2,1)S(1)}, /*index=5*/f32[8,640]{1,0:T(8,128)S(1)}) custom-call(s32[3]{0:T(128)S(1)} %pad_add_fusion.refs_0_, bf16[328,768]{1,0:T(8,128)(2,1)S(1)} %get-tuple-element.185.refs_1_, ...), custom_call_target="tpu_custom_call" | custom-call | flops 8589934592 | bytes 1024 | tf_op jit(solution)/shard_map/own/pallas_call | solution.py:372
  10.0 8.9 %collective-permute-done.7.refs_1_.refs_3_ = bf16[328,768]{1,0:T(8,128)(2,1)S(1)} collective-permute-done((bf16[328,768]{1,0:T(8,128)(2,1)S(1)}, bf16[328,768]{1,0:T(8,128)(2,1)S(1)}, u32[]{:S(2)}, u32[]{:S(2)}) %collective-permute-start.7) | collective-permute-done | bytes 503840 | tf_op jit(solution)/shard_map/ppermute | solution.py:439
  18.9 2.8 %collective-permute-start.6 = (bf16[328,768]{1,0:T(8,128)(2,1)S(1)}, bf16[328,768]{1,0:T(8,128)(2,1)S(1)}, u32[]{:S(2)}, u32[]{:S(2)}) collective-permute-start(bf16[328,768]{1,0:T(8,128)(2,1)S(1)} %get-tuple-element.185.refs_1_), channel_id=1, source_target_pairs={{0,8},{1,9},{2,10},{3,11},{4,0},{5,1},{6,2},{7,3},{8,12},{9,13},{1... | collective-permute-start | bytes 1511432 | tf_op jit(solution)/shard_map/ppermute | solution.py:439
  21.7 1.5 %collective-permute-start.8 = (bf16[328,768]{1,0:T(8,128)(2,1)S(1)}, bf16[328,768]{1,0:T(8,128)(2,1)S(1)}, u32[]{:S(2)}, u32[]{:S(2)}) collective-permute-start(bf16[328,768]{1,0:T(8,128)(2,1)S(1)} %collective-permute-done.7.refs_1_.refs_3_), channel_id=1, source_target_pairs={{0,2},{1,3},{2,0},{3,1},{4,6},{5,7},{6,4},{7,5},{8,10},{9,11},{10,... | collective-permute-start | bytes 1511432 | tf_op jit(solution)/shard_map/ppermute | solution.py:439
  23.2 0.0 collective-permute-done.4.refs_1_
  23.3 1.1 %pair.1 = (f32[4,1,640]{2,1,0:T(1,128)S(1)}, f32[4,1,640]{2,1,0:T(1,128)S(1)}, f32[1,1,640]{2,1,0:T(1,128)S(1)}, f32[1,1,640]{2,1,0:T(1,128)S(1)}, bf16[768,640]{1,0:T(8,128)(2,1)S(1)}, /*index=5*/f32[8,640]{1,0:T(8,128)S(1)}) custom-call(s32[3]{0:T(128)S(1)} %pad_add_fusion.refs_0_, bf16[328,768]{1,0:T(8,128)(2,1)S(1)} %collective-permute-done.7.refs_1_.refs_3_, ...), custom_call_target="tpu_custom_call" | custom-call | flops 8589934592 | bytes 1024 | tf_op jit(solution)/shard_map/pair/pallas_call | solution.py:372
  24.3 0.8 %collective-permute-done.9.refs_2_ = bf16[328,768]{1,0:T(8,128)(2,1)S(1)} collective-permute-done((bf16[328,768]{1,0:T(8,128)(2,1)S(1)}, bf16[328,768]{1,0:T(8,128)(2,1)S(1)}, u32[]{:S(2)}, u32[]{:S(2)}) %collective-permute-start.9) | collective-permute-done | bytes 503840 | tf_op jit(solution)/shard_map/ppermute | solution.py:439
  25.1 1.8 %row.1 = (f32[4,1,640]{2,1,0:T(1,128)S(1)}, f32[4,1,640]{2,1,0:T(1,128)S(1)}, f32[1,1,640]{2,1,0:T(1,128)S(1)}, f32[1,1,640]{2,1,0:T(1,128)S(1)}, bf16[768,640]{1,0:T(8,128)(2,1)S(1)}, /*index=5*/f32[8,640]{1,0:T(8,128)S(1)}) custom-call(s32[3]{0:T(128)S(1)} %pad_add_fusion.refs_0_, bf16[328,768]{1,0:T(8,128)(2,1)S(1)} %collective-permute-done.4.refs_1_, ...), custom_call_target="tpu_custom_call" | custom-call | flops 1 | bytes 1024 | tf_op jit(solution)/shard_map/row/pallas_call | solution.py:372
  26.9 8.4 %collective-permute-done.8.refs_3_ = bf16[328,768]{1,0:T(8,128)(2,1)S(1)} collective-permute-done((bf16[328,768]{1,0:T(8,128)(2,1)S(1)}, bf16[328,768]{1,0:T(8,128)(2,1)S(1)}, u32[]{:S(2)}, u32[]{:S(2)}) %collective-permute-start.8) | collective-permute-done | bytes 503840 | tf_op jit(solution)/shard_map/ppermute | solution.py:439
  35.3 0.6 %far.1 = (f32[4,1,640]{2,1,0:T(1,128)S(1)}, f32[4,1,640]{2,1,0:T(1,128)S(1)}, f32[1,1,640]{2,1,0:T(1,128)S(1)}, f32[1,1,640]{2,1,0:T(1,128)S(1)}) custom-call(s32[3]{0:T(128)S(1)} %pad_add_fusion.refs_0_, bf16[328,768]{1,0:T(8,128)(2,1)S(1)} %collective-permute-done.6.refs_1_.refs_2_, bf16[768,640]{1,0:T(8,128)(2,1)S(1)} %get-tuple-element.192.refs_4_.refs_5_.refs_2_, ...), custom_call_target="tpu_custom_call" | custom-call | flops 1 | bytes 1024 | tf_op jit(solution)/shard_map/far/pallas_call | solution.py:372
  36.0 0.0 copy-start
  36.0 0.0 copy-start.1
  36.0 0.0 copy-start.2
  36.0 1.2 %collective-permute-done.11.refs_4_ = bf16[328,768]{1,0:T(8,128)(2,1)S(1)} collective-permute-done((bf16[328,768]{1,0:T(8,128)(2,1)S(1)}, bf16[328,768]{1,0:T(8,128)(2,1)S(1)}, u32[]{:S(2)}, u32[]{:S(2)}) %collective-permute-start.11) | collective-permute-done | bytes 503840 | tf_op jit(solution)/shard_map/ppermute | solution.py:439
  37.2 1.2 %last.1 = (f32[4,1,640]{2,1,0:T(1,128)S(1)}, f32[4,1,640]{2,1,0:T(1,128)S(1)}, f32[1,1,640]{2,1,0:T(1,128)S(1)}, f32[1,1,640]{2,1,0:T(1,128)S(1)}) custom-call(s32[3]{0:T(128)S(1)} %pad_add_fusion.refs_0_, bf16[328,768]{1,0:T(8,128)(2,1)S(1)} %collective-permute-done.5.refs_3_.refs_4_.refs_1_, bf16[328,768]{1,0:T(8,128)(2,1)S(1)} %collective-permute-done.6.refs_1_.refs_2_, ...), custom_call_target="tpu_custom_call" | custom-call | flops 1 | bytes 1024 | tf_op jit(solution)/shard_map/last/pallas_call | solution.py:372
  38.4 0.1 collective-permute-start.13
  38.6 2.3 %collective-permute-start.12 = (f32[1,1,640]{2,1,0:T(1,128)S(1)}, f32[1,1,640]{2,1,0:T(1,128)S(1)}, u32[]{:S(2)}, u32[]{:S(2)}) collective-permute-start(f32[1,1,640]{2,1,0:T(1,128)S(1)} %get-tuple-element.214.refs_0_), channel_id=1, source_target_pairs={{0,8},{1,9},{2,10},{3,11},{4,12},{5,13},{6,14},{7,15},{8,0},{9,1},... | collective-permute-start | bytes 7688 | tf_op jit(solution)/shard_map/ppermute | solution.py:439
  40.9 2.0 %collective-permute-start.17 = (f32[1,1,640]{2,1,0:T(1,128)S(1)}, f32[1,1,640]{2,1,0:T(1,128)S(1)}, u32[]{:S(2)}, u32[]{:S(2)}) collective-permute-start(f32[1,1,640]{2,1,0:T(1,128)S(1)} %get-tuple-element.240), channel_id=1, source_target_pairs={{0,6},{1,7},{2,4},{3,5},{4,2},{5,3},{6,0},{7,1},{8,14},{9,15},{10,... | collective-permute-start | bytes 7688 | tf_op jit(solution)/shard_map/ppermute | solution.py:439
  42.9 0.5 %collective-permute-start.16 = (f32[1,1,640]{2,1,0:T(1,128)S(1)}, f32[1,1,640]{2,1,0:T(1,128)S(1)}, u32[]{:S(2)}, u32[]{:S(2)}) collective-permute-start(f32[1,1,640]{2,1,0:T(1,128)S(1)} %get-tuple-element.241), channel_id=1, source_target_pairs={{0,2},{1,3},{2,0},{3,1},{4,6},{5,7},{6,4},{7,5},{8,10},{9,11},{10,... | collective-permute-start | bytes 7688 | tf_op jit(solution)/shard_map/ppermute | solution.py:439
  43.4 1.1 %collective-permute-start.15 = (f32[1,1,640]{2,1,0:T(1,128)S(1)}, f32[1,1,640]{2,1,0:T(1,128)S(1)}, u32[]{:S(2)}, u32[]{:S(2)}) collective-permute-start(f32[1,1,640]{2,1,0:T(1,128)S(1)} %get-tuple-element.242), channel_id=1, source_target_pairs={{0,4},{1,5},{2,6},{3,7},{4,0},{5,1},{6,2},{7,3},{8,12},{9,13},{10,... | collective-permute-start | bytes 7688 | tf_op jit(solution)/shard_map/ppermute | solution.py:439
  44.5 0.6 %decide.1 = s32[1]{0:T(128)} custom-call(f32[1,1,640]{2,1,0:T(1,128)S(1)} %get-tuple-element.214.refs_0_, f32[1,1,640]{2,1,0:T(1,128)S(1)} %collective-permute-done.12.refs_1_), custom_call_target="tpu_custom_call" | custom-call | tf_op jit(solution)/shard_map/decide/pallas_call | solution.py:411
  45.8 0.7 %collective-permute-done.16 = f32[1,1,640]{2,1,0:T(1,128)S(1)} collective-permute-done((f32[1,1,640]{2,1,0:T(1,128)S(1)}, f32[1,1,640]{2,1,0:T(1,128)S(1)}, u32[]{:S(2)}, u32[]{:S(2)}) %collective-permute-start.16) | collective-permute-done | bytes 2592 | tf_op jit(solution)/shard_map/ppermute | solution.py:439
  46.5 0.5 %collective-permute-done.15 = f32[1,1,640]{2,1,0:T(1,128)S(1)} collective-permute-done((f32[1,1,640]{2,1,0:T(1,128)S(1)}, f32[1,1,640]{2,1,0:T(1,128)S(1)}, u32[]{:S(2)}, u32[]{:S(2)}) %collective-permute-start.15) | collective-permute-done | bytes 2592 | tf_op jit(solution)/shard_map/ppermute | solution.py:439
  47.0 0.5 %conditional.1 = (f32[512]{0:T(512)S(1)}) conditional(s32[]{:T(128)} %bitcast.5, (f32[4,1,640]{2,1,0:T(1,128)S(1)}, f32[4,1,640]{2,1,0:T(1,128)S(1)}, s32[1,512]{1,0:T(1,128)S(1)}, f32[1,1,640]{2,1,0:T(1,128)S(1)}, f32[1,1,640]{2,1,0:T(1,128)S(1)}, /*index=5*/f32[1,1,640]{2,1,0:T(1,128)S(1)}, f32[1,1,640]{2,1,0:T(1,128)S(1)}, ...), branch_computations={%region_0.1_spmd, %region_1.8_spmd} | conditional | flops 1617953280 | bytes 16846124 | solution.py:490
  47.0 0.5 finish.1
  47.5 0.0 copy-start.3
  47.5 0.6 %copy-done.3 = f32[512]{0:T(512)} copy-done((f32[512]{0:T(512)}, f32[512]{0:T(512)S(1)}, u32[]{:S(2)}) %copy-start.3) | copy-done | bytes 2072
  (18 shorter events, 0.1 us)
Async XLA Ops:
  3.7 3.2 %collective-permute-start.3 = (bf16[328,768]{1,0:T(8,128)(2,1)S(1)}, bf16[328,768]{1,0:T(8,128)(2,1)S(1)}, u32[]{:S(2)}, u32[]{:S(2)}) collective-permute-start(bf16[328,768]{1,0:T(8,128)(2,1)S(1)} %get-tuple-element.185.refs_1_), channel_id=1, source_target_pairs={{0,1},{1,0},{2,3},{3,2},{4,5},{5,4},{6,7},{7,6},{8,9},{9,8},{10,11... | collective-permute-start | bytes 1511432 | tf_op jit(solution)/shard_map/ppermute | solution.py:439
  4.2 14.7 %collective-permute-start.7 = (bf16[328,768]{1,0:T(8,128)(2,1)S(1)}, bf16[328,768]{1,0:T(8,128)(2,1)S(1)}, u32[]{:S(2)}, u32[]{:S(2)}) collective-permute-start(bf16[328,768]{1,0:T(8,128)(2,1)S(1)} %get-tuple-element.186), channel_id=1, source_target_pairs={{0,4},{1,5},{2,6},{3,7},{4,0},{5,1},{6,2},{7,3},{8,12},{9,13},{10,... | collective-permute-start | bytes 1511432 | tf_op jit(solution)/shard_map/ppermute | solution.py:439
  6.9 16.4 %collective-permute-start.4 = (bf16[328,768]{1,0:T(8,128)(2,1)S(1)}, bf16[328,768]{1,0:T(8,128)(2,1)S(1)}, u32[]{:S(2)}, u32[]{:S(2)}) collective-permute-start(bf16[328,768]{1,0:T(8,128)(2,1)S(1)} %get-tuple-element.185.refs_1_), channel_id=1, source_target_pairs={{0,2},{1,3},{2,0},{3,1},{4,6},{5,7},{6,4},{7,5},{8,10},{9,11},{10,... | collective-permute-start | bytes 1511432 | tf_op jit(solution)/shard_map/ppermute | solution.py:439
  8.6 14.6 %collective-permute-start.5 = (bf16[328,768]{1,0:T(8,128)(2,1)S(1)}, bf16[328,768]{1,0:T(8,128)(2,1)S(1)}, u32[]{:S(2)}, u32[]{:S(2)}) collective-permute-start(bf16[328,768]{1,0:T(8,128)(2,1)S(1)} %get-tuple-element.186), channel_id=1, source_target_pairs={{0,1},{1,0},{2,3},{3,2},{4,8},{5,9},{6,10},{7,11},{8,4},{9,5},{10,... | collective-permute-start | bytes 1511432 | tf_op jit(solution)/shard_map/ppermute | solution.py:439
  18.9 4.3 %collective-permute-start.10 = (bf16[328,768]{1,0:T(8,128)(2,1)S(1)}, bf16[328,768]{1,0:T(8,128)(2,1)S(1)}, u32[]{:S(2)}, u32[]{:S(2)}) collective-permute-start(bf16[328,768]{1,0:T(8,128)(2,1)S(1)} %collective-permute-done.7.refs_1_.refs_3_), channel_id=1, source_target_pairs={{0,1},{1,0},{2,3},{3,2},{4,5},{5,4},{6,7},{7,6},{8,9},{9,8},{10,11... | collective-permute-start | bytes 1511432 | tf_op jit(solution)/shard_map/ppermute | solution.py:439
  18.9 16.4 %collective-permute-start.6 = (bf16[328,768]{1,0:T(8,128)(2,1)S(1)}, bf16[328,768]{1,0:T(8,128)(2,1)S(1)}, u32[]{:S(2)}, u32[]{:S(2)}) collective-permute-start(bf16[328,768]{1,0:T(8,128)(2,1)S(1)} %get-tuple-element.185.refs_1_), channel_id=1, source_target_pairs={{0,8},{1,9},{2,10},{3,11},{4,0},{5,1},{6,2},{7,3},{8,12},{9,13},{1... | collective-permute-start | bytes 1511432 | tf_op jit(solution)/shard_map/ppermute | solution.py:439
  21.7 13.6 %collective-permute-start.8 = (bf16[328,768]{1,0:T(8,128)(2,1)S(1)}, bf16[328,768]{1,0:T(8,128)(2,1)S(1)}, u32[]{:S(2)}, u32[]{:S(2)}) collective-permute-start(bf16[328,768]{1,0:T(8,128)(2,1)S(1)} %collective-permute-done.7.refs_1_.refs_3_), channel_id=1, source_target_pairs={{0,2},{1,3},{2,0},{3,1},{4,6},{5,7},{6,4},{7,5},{8,10},{9,11},{10,... | collective-permute-start | bytes 1511432 | tf_op jit(solution)/shard_map/ppermute | solution.py:439
  23.2 1.9 %collective-permute-start.9 = (bf16[328,768]{1,0:T(8,128)(2,1)S(1)}, bf16[328,768]{1,0:T(8,128)(2,1)S(1)}, u32[]{:S(2)}, u32[]{:S(2)}) collective-permute-start(bf16[328,768]{1,0:T(8,128)(2,1)S(1)} %collective-permute-done.4.refs_1_), channel_id=1, source_target_pairs={{0,1},{1,0},{2,3},{3,2},{4,5},{5,4},{6,7},{7,6},{8,9},{9,8},{10,11... | collective-permute-start | bytes 1511432 | tf_op jit(solution)/shard_map/ppermute | solution.py:439
  35.3 1.9 %collective-permute-start.11 = (bf16[328,768]{1,0:T(8,128)(2,1)S(1)}, bf16[328,768]{1,0:T(8,128)(2,1)S(1)}, u32[]{:S(2)}, u32[]{:S(2)}) collective-permute-start(bf16[328,768]{1,0:T(8,128)(2,1)S(1)} %collective-permute-done.8.refs_3_), channel_id=1, source_target_pairs={{0,1},{1,0},{2,3},{3,2},{4,5},{5,4},{6,7},{7,6},{8,9},{9,8},{10,11... | collective-permute-start | bytes 1511432 | tf_op jit(solution)/shard_map/ppermute | solution.py:439
  36.0 11.0 %copy-start = (bf16[1024,768]{1,0:T(8,128)(2,1)S(1)}, bf16[1024,768]{1,0:T(8,128)(2,1)}, u32[]{:S(2)}) copy-start(bf16[1024,768]{1,0:T(8,128)(2,1)} %refs_3_.1) | copy-start | bytes 4718596
  36.0 11.0 %copy-start.1 = (bf16[512,1024]{1,0:T(8,128)(2,1)S(1)}, bf16[512,1024]{1,0:T(8,128)(2,1)}, u32[]{:S(2)}) copy-start(bf16[512,1024]{1,0:T(8,128)(2,1)} %refs_2_.1) | copy-start | bytes 3145732
  36.0 11.0 %copy-start.2 = (s32[512]{0:T(512)S(1)}, s32[512]{0:T(512)}, u32[]{:S(2)}) copy-start(s32[512]{0:T(512)} %param.9) | copy-start | bytes 6148
  38.4 2.5 %collective-permute-start.13 = (f32[4,1,640]{2,1,0:T(1,128)S(1)}, f32[4,1,640]{2,1,0:T(1,128)S(1)}, u32[]{:S(2)}, u32[]{:S(2)}) collective-permute-start(f32[4,1,640]{2,1,0:T(1,128)S(1)} %get-tuple-element.216), channel_id=1, source_target_pairs={{0,1},{1,0},{2,3},{3,2},{4,5},{5,4},{6,7},{7,6},{8,9},{9,8},{10,11... | collective-permute-start | bytes 30728 | tf_op jit(solution)/shard_map/ppermute | solution.py:439
  38.6 5.9 %collective-permute-start.12 = (f32[1,1,640]{2,1,0:T(1,128)S(1)}, f32[1,1,640]{2,1,0:T(1,128)S(1)}, u32[]{:S(2)}, u32[]{:S(2)}) collective-permute-start(f32[1,1,640]{2,1,0:T(1,128)S(1)} %get-tuple-element.214.refs_0_), channel_id=1, source_target_pairs={{0,8},{1,9},{2,10},{3,11},{4,12},{5,13},{6,14},{7,15},{8,0},{9,1},... | collective-permute-start | bytes 7688 | tf_op jit(solution)/shard_map/ppermute | solution.py:439
  40.9 4.8 %collective-permute-start.17 = (f32[1,1,640]{2,1,0:T(1,128)S(1)}, f32[1,1,640]{2,1,0:T(1,128)S(1)}, u32[]{:S(2)}, u32[]{:S(2)}) collective-permute-start(f32[1,1,640]{2,1,0:T(1,128)S(1)} %get-tuple-element.240), channel_id=1, source_target_pairs={{0,6},{1,7},{2,4},{3,5},{4,2},{5,3},{6,0},{7,1},{8,14},{9,15},{10,... | collective-permute-start | bytes 7688 | tf_op jit(solution)/shard_map/ppermute | solution.py:439
  42.9 3.6 %collective-permute-start.16 = (f32[1,1,640]{2,1,0:T(1,128)S(1)}, f32[1,1,640]{2,1,0:T(1,128)S(1)}, u32[]{:S(2)}, u32[]{:S(2)}) collective-permute-start(f32[1,1,640]{2,1,0:T(1,128)S(1)} %get-tuple-element.241), channel_id=1, source_target_pairs={{0,2},{1,3},{2,0},{3,1},{4,6},{5,7},{6,4},{7,5},{8,10},{9,11},{10,... | collective-permute-start | bytes 7688 | tf_op jit(solution)/shard_map/ppermute | solution.py:439
  43.4 3.6 %collective-permute-start.15 = (f32[1,1,640]{2,1,0:T(1,128)S(1)}, f32[1,1,640]{2,1,0:T(1,128)S(1)}, u32[]{:S(2)}, u32[]{:S(2)}) collective-permute-start(f32[1,1,640]{2,1,0:T(1,128)S(1)} %get-tuple-element.242), channel_id=1, source_target_pairs={{0,4},{1,5},{2,6},{3,7},{4,0},{5,1},{6,2},{7,3},{8,12},{9,13},{10,... | collective-permute-start | bytes 7688 | tf_op jit(solution)/shard_map/ppermute | solution.py:439
  44.5 2.5 %collective-permute-start.14 = (f32[1,1,640]{2,1,0:T(1,128)S(1)}, f32[1,1,640]{2,1,0:T(1,128)S(1)}, u32[]{:S(2)}, u32[]{:S(2)}) collective-permute-start(f32[1,1,640]{2,1,0:T(1,128)S(1)} %get-tuple-element.220), channel_id=1, source_target_pairs={{0,1},{1,0},{2,3},{3,2},{4,8},{5,9},{6,10},{7,11},{8,4},{9,5},{10,... | collective-permute-start | bytes 7688 | tf_op jit(solution)/shard_map/ppermute | solution.py:439
  47.5 0.6 %copy-start.3 = (f32[512]{0:T(512)}, f32[512]{0:T(512)S(1)}, u32[]{:S(2)}) copy-start(f32[512]{0:T(512)S(1)} %get-tuple-element.356) | copy-start | bytes 6148

commit v23 on v14

--- a/solution.py
+++ b/solution.py
@@ -477,7 +477,7 @@
     own, pair, row, pair_row = (kept[k:k + 1] + from_core[k:k + 1] for k in (0, 1, 2, 3))
     home = [
         own, from_next, from_far,
-        move(pair, OUTER), move(row, STAY, row=1), move(pair_row, OUTER, row=1),
+        move(row, STAY, row=1), move(pair, OUTER), move(pair_row, OUTER, row=1),
     ]
     return lax.cond(
         decide(flag, to_far, from_far)[0] > 0,

time: 48.2 us -> 48.8 us (1.012)
  waiting for transfers between devices: 20.6 us -> 21.2 us
    ppermute x15, waiting for transfers between devices: 20.6 us -> 21.2 us  [move(): return lax.ppermute(a, ('owner', 'split'), pairs)]
where the time goes in v23:
time: 48.8 us; the launch traced here: 48.6 us
  waiting for transfers between devices  21.2 us (43%)
  starting transfers between devices  15.2 us (31%)
  Pallas kernels  10.7 us (22%)
  between operations  0.77 us (2%)
  local copies, waits for them, and re-layouts  0.59 us (1%)
    ppermute x15, waiting for transfers between devices, move(): return lax.ppermute(a, ('owner', 'split'), pairs)  21.2 us
    ppermute x15, starting transfers between devices, move(): return lax.ppermute(a, ('owner', 'split'), pairs)  15.2 us
    pallas_call x5, Pallas kernels, score(): pl.pallas_call(lambda *refs: score_kernel(docs, hot, names, given, made,...  6.09 us
    pallas_call x1, Pallas kernels, prep(): pl.pallas_call(lambda *refs: prep_kernel(hot, *refs), out_shape=(shape((r...  3.56 us
  transfers between devices with their start and end apart: 15, of which 6 were waited for; matrix products, arithmetic and copies ran while one was open for 0% of the time, Pallas kernels for 11%

profile of v23, /device:TPU:0, one launch (start us, length us, event | category | flops | bytes accessed | tf_op | source)
XLA Modules:
  0.0 48.6 jit_solution(11112117060953432050)
XLA Ops:
  0.0 0.1 pad_add_fusion.refs_0_
  0.1 3.6 %prep.1 = (bf16[328,768]{1,0:T(8,128)(2,1)S(1)}, bf16[328,768]{1,0:T(8,128)(2,1)S(1)}, s32[1,512]{1,0:T(1,128)S(1)}) custom-call(s32[3]{0:T(128)S(1)} %pad_add_fusion.refs_0_, s32[1,512]{1,0:T(1,128)} %bitcast.16, bf16[512,1024]{1,0:T(8,128)(2,1)} %refs_2_.1, bf16[1024,768]{1,0:T(8,128)(2,1)} %refs_3_.1), custom_call_target="tpu_custom_call" | custom-call | tf_op jit(solution)/shard_map/prep/pallas_call | solution.py:220
  3.6 0.5 %collective-permute-start.3 = (bf16[328,768]{1,0:T(8,128)(2,1)S(1)}, bf16[328,768]{1,0:T(8,128)(2,1)S(1)}, u32[]{:S(2)}, u32[]{:S(2)}) collective-permute-start(bf16[328,768]{1,0:T(8,128)(2,1)S(1)} %get-tuple-element.185.refs_1_), channel_id=1, source_target_pairs={{0,1},{1,0},{2,3},{3,2},{4,5},{5,4},{6,7},{7,6},{8,9},{9,8},{10,11... | collective-permute-start | bytes 1511432 | tf_op jit(solution)/shard_map/ppermute | solution.py:431
  4.2 2.6 %collective-permute-start.7 = (bf16[328,768]{1,0:T(8,128)(2,1)S(1)}, bf16[328,768]{1,0:T(8,128)(2,1)S(1)}, u32[]{:S(2)}, u32[]{:S(2)}) collective-permute-start(bf16[328,768]{1,0:T(8,128)(2,1)S(1)} %get-tuple-element.186), channel_id=1, source_target_pairs={{0,4},{1,5},{2,6},{3,7},{4,0},{5,1},{6,2},{7,3},{8,12},{9,13},{10,... | collective-permute-start | bytes 1511432 | tf_op jit(solution)/shard_map/ppermute | solution.py:431
  6.8 0.0 collective-permute-done.3.refs_2_
  6.8 1.7 %collective-permute-start.4 = (bf16[328,768]{1,0:T(8,128)(2,1)S(1)}, bf16[328,768]{1,0:T(8,128)(2,1)S(1)}, u32[]{:S(2)}, u32[]{:S(2)}) collective-permute-start(bf16[328,768]{1,0:T(8,128)(2,1)S(1)} %get-tuple-element.185.refs_1_), channel_id=1, source_target_pairs={{0,2},{1,3},{2,0},{3,1},{4,6},{5,7},{6,4},{7,5},{8,10},{9,11},{10,... | collective-permute-start | bytes 1511432 | tf_op jit(solution)/shard_map/ppermute | solution.py:431
  8.6 1.4 %own.1 = (f32[4,1,640]{2,1,0:T(1,128)S(1)}, f32[4,1,640]{2,1,0:T(1,128)S(1)}, f32[1,1,640]{2,1,0:T(1,128)S(1)}, f32[1,1,640]{2,1,0:T(1,128)S(1)}, bf16[768,640]{1,0:T(8,128)(2,1)S(1)}, /*index=5*/f32[8,640]{1,0:T(8,128)S(1)}) custom-call(s32[3]{0:T(128)S(1)} %pad_add_fusion.refs_0_, bf16[328,768]{1,0:T(8,128)(2,1)S(1)} %get-tuple-element.185.refs_1_, ...), custom_call_target="tpu_custom_call" | custom-call | flops 8589934592 | bytes 1024 | tf_op jit(solution)/shard_map/own/pallas_call | solution.py:364
  10.0 8.9 %collective-permute-done.7.refs_1_.refs_3_ = bf16[328,768]{1,0:T(8,128)(2,1)S(1)} collective-permute-done((bf16[328,768]{1,0:T(8,128)(2,1)S(1)}, bf16[328,768]{1,0:T(8,128)(2,1)S(1)}, u32[]{:S(2)}, u32[]{:S(2)}) %collective-permute-start.7) | collective-permute-done | bytes 503840 | tf_op jit(solution)/shard_map/ppermute | solution.py:431
  18.9 2.8 %collective-permute-start.6 = (bf16[328,768]{1,0:T(8,128)(2,1)S(1)}, bf16[328,768]{1,0:T(8,128)(2,1)S(1)}, u32[]{:S(2)}, u32[]{:S(2)}) collective-permute-start(bf16[328,768]{1,0:T(8,128)(2,1)S(1)} %get-tuple-element.185.refs_1_), channel_id=1, source_target_pairs={{0,8},{1,9},{2,10},{3,11},{4,0},{5,1},{6,2},{7,3},{8,12},{9,13},{1... | collective-permute-start | bytes 1511432 | tf_op jit(solution)/shard_map/ppermute | solution.py:431
  21.7 1.5 %collective-permute-start.8 = (bf16[328,768]{1,0:T(8,128)(2,1)S(1)}, bf16[328,768]{1,0:T(8,128)(2,1)S(1)}, u32[]{:S(2)}, u32[]{:S(2)}) collective-permute-start(bf16[328,768]{1,0:T(8,128)(2,1)S(1)} %collective-permute-done.7.refs_1_.refs_3_), channel_id=1, source_target_pairs={{0,2},{1,3},{2,0},{3,1},{4,6},{5,7},{6,4},{7,5},{8,10},{9,11},{10,... | collective-permute-start | bytes 1511432 | tf_op jit(solution)/shard_map/ppermute | solution.py:431
  23.2 1.1 %pair.1 = (f32[4,1,640]{2,1,0:T(1,128)S(1)}, f32[4,1,640]{2,1,0:T(1,128)S(1)}, f32[1,1,640]{2,1,0:T(1,128)S(1)}, f32[1,1,640]{2,1,0:T(1,128)S(1)}, bf16[768,640]{1,0:T(8,128)(2,1)S(1)}, /*index=5*/f32[8,640]{1,0:T(8,128)S(1)}) custom-call(s32[3]{0:T(128)S(1)} %pad_add_fusion.refs_0_, bf16[328,768]{1,0:T(8,128)(2,1)S(1)} %collective-permute-done.7.refs_1_.refs_3_, ...), custom_call_target="tpu_custom_call" | custom-call | flops 8589934592 | bytes 1024 | tf_op jit(solution)/shard_map/pair/pallas_call | solution.py:364
  24.3 0.8 %collective-permute-done.9.refs_2_ = bf16[328,768]{1,0:T(8,128)(2,1)S(1)} collective-permute-done((bf16[328,768]{1,0:T(8,128)(2,1)S(1)}, bf16[328,768]{1,0:T(8,128)(2,1)S(1)}, u32[]{:S(2)}, u32[]{:S(2)}) %collective-permute-start.9) | collective-permute-done | bytes 503840 | tf_op jit(solution)/shard_map/ppermute | solution.py:431
  25.1 1.8 %row.1 = (f32[4,1,640]{2,1,0:T(1,128)S(1)}, f32[4,1,640]{2,1,0:T(1,128)S(1)}, f32[1,1,640]{2,1,0:T(1,128)S(1)}, f32[1,1,640]{2,1,0:T(1,128)S(1)}, bf16[768,640]{1,0:T(8,128)(2,1)S(1)}, /*index=5*/f32[8,640]{1,0:T(8,128)S(1)}) custom-call(s32[3]{0:T(128)S(1)} %pad_add_fusion.refs_0_, bf16[328,768]{1,0:T(8,128)(2,1)S(1)} %collective-permute-done.4.refs_1_, ...), custom_call_target="tpu_custom_call" | custom-call | flops 1 | bytes 1024 | tf_op jit(solution)/shard_map/row/pallas_call | solution.py:364
  26.9 8.4 %collective-permute-done.8.refs_3_ = bf16[328,768]{1,0:T(8,128)(2,1)S(1)} collective-permute-done((bf16[328,768]{1,0:T(8,128)(2,1)S(1)}, bf16[328,768]{1,0:T(8,128)(2,1)S(1)}, u32[]{:S(2)}, u32[]{:S(2)}) %collective-permute-start.8) | collective-permute-done | bytes 503840 | tf_op jit(solution)/shard_map/ppermute | solution.py:431
  35.3 0.6 %far.1 = (f32[4,1,640]{2,1,0:T(1,128)S(1)}, f32[4,1,640]{2,1,0:T(1,128)S(1)}, f32[1,1,640]{2,1,0:T(1,128)S(1)}, f32[1,1,640]{2,1,0:T(1,128)S(1)}) custom-call(s32[3]{0:T(128)S(1)} %pad_add_fusion.refs_0_, bf16[328,768]{1,0:T(8,128)(2,1)S(1)} %collective-permute-done.6.refs_1_.refs_2_, bf16[768,640]{1,0:T(8,128)(2,1)S(1)} %get-tuple-element.192.refs_4_.refs_5_.refs_2_, ...), custom_call_target="tpu_custom_call" | custom-call | flops 1 | bytes 1024 | tf_op jit(solution)/shard_map/far/pallas_call | solution.py:364
  35.9 0.0 copy-start
  36.0 0.0 copy-start.1
  36.0 0.0 copy-start.2
  36.0 1.2 %collective-permute-done.11.refs_4_ = bf16[328,768]{1,0:T(8,128)(2,1)S(1)} collective-permute-done((bf16[328,768]{1,0:T(8,128)(2,1)S(1)}, bf16[328,768]{1,0:T(8,128)(2,1)S(1)}, u32[]{:S(2)}, u32[]{:S(2)}) %collective-permute-start.11) | collective-permute-done | bytes 503840 | tf_op jit(solution)/shard_map/ppermute | solution.py:431
  37.2 1.2 %last.1 = (f32[4,1,640]{2,1,0:T(1,128)S(1)}, f32[4,1,640]{2,1,0:T(1,128)S(1)}, f32[1,1,640]{2,1,0:T(1,128)S(1)}, f32[1,1,640]{2,1,0:T(1,128)S(1)}) custom-call(s32[3]{0:T(128)S(1)} %pad_add_fusion.refs_0_, bf16[328,768]{1,0:T(8,128)(2,1)S(1)} %collective-permute-done.5.refs_3_.refs_4_.refs_1_, bf16[328,768]{1,0:T(8,128)(2,1)S(1)} %collective-permute-done.6.refs_1_.refs_2_, ...), custom_call_target="tpu_custom_call" | custom-call | flops 1 | bytes 1024 | tf_op jit(solution)/shard_map/last/pallas_call | solution.py:364
  38.4 0.1 collective-permute-start.13
  38.5 2.3 %collective-permute-start.12 = (f32[1,1,640]{2,1,0:T(1,128)S(1)}, f32[1,1,640]{2,1,0:T(1,128)S(1)}, u32[]{:S(2)}, u32[]{:S(2)}) collective-permute-start(f32[1,1,640]{2,1,0:T(1,128)S(1)} %get-tuple-element.214.refs_0_), channel_id=1, source_target_pairs={{0,8},{1,9},{2,10},{3,11},{4,12},{5,13},{6,14},{7,15},{8,0},{9,1},... | collective-permute-start | bytes 7688 | tf_op jit(solution)/shard_map/ppermute | solution.py:431
  40.9 2.0 %collective-permute-start.17 = (f32[1,1,640]{2,1,0:T(1,128)S(1)}, f32[1,1,640]{2,1,0:T(1,128)S(1)}, u32[]{:S(2)}, u32[]{:S(2)}) collective-permute-start(f32[1,1,640]{2,1,0:T(1,128)S(1)} %get-tuple-element.240), channel_id=1, source_target_pairs={{0,6},{1,7},{2,4},{3,5},{4,2},{5,3},{6,0},{7,1},{8,14},{9,15},{10,... | collective-permute-start | bytes 7688 | tf_op jit(solution)/shard_map/ppermute | solution.py:431
  42.8 1.1 %collective-permute-start.16 = (f32[1,1,640]{2,1,0:T(1,128)S(1)}, f32[1,1,640]{2,1,0:T(1,128)S(1)}, u32[]{:S(2)}, u32[]{:S(2)}) collective-permute-start(f32[1,1,640]{2,1,0:T(1,128)S(1)} %get-tuple-element.241), channel_id=1, source_target_pairs={{0,4},{1,5},{2,6},{3,7},{4,0},{5,1},{6,2},{7,3},{8,12},{9,13},{10,... | collective-permute-start | bytes 7688 | tf_op jit(solution)/shard_map/ppermute | solution.py:431
  43.9 0.5 %collective-permute-start.15 = (f32[1,1,640]{2,1,0:T(1,128)S(1)}, f32[1,1,640]{2,1,0:T(1,128)S(1)}, u32[]{:S(2)}, u32[]{:S(2)}) collective-permute-start(f32[1,1,640]{2,1,0:T(1,128)S(1)} %get-tuple-element.242), channel_id=1, source_target_pairs={{0,2},{1,3},{2,0},{3,1},{4,6},{5,7},{6,4},{7,5},{8,10},{9,11},{10,... | collective-permute-start | bytes 7688 | tf_op jit(solution)/shard_map/ppermute | solution.py:431
  44.4 0.6 %decide.1 = s32[1]{0:T(128)} custom-call(f32[1,1,640]{2,1,0:T(1,128)S(1)} %get-tuple-element.214.refs_0_, f32[1,1,640]{2,1,0:T(1,128)S(1)} %collective-permute-done.12.refs_1_), custom_call_target="tpu_custom_call" | custom-call | tf_op jit(solution)/shard_map/decide/pallas_call | solution.py:403
  45.7 0.7 %collective-permute-done.16 = f32[1,1,640]{2,1,0:T(1,128)S(1)} collective-permute-done((f32[1,1,640]{2,1,0:T(1,128)S(1)}, f32[1,1,640]{2,1,0:T(1,128)S(1)}, u32[]{:S(2)}, u32[]{:S(2)}) %collective-permute-start.16) | collective-permute-done | bytes 2592 | tf_op jit(solution)/shard_map/ppermute | solution.py:431
  46.4 1.1 %collective-permute-done.15 = f32[1,1,640]{2,1,0:T(1,128)S(1)} collective-permute-done((f32[1,1,640]{2,1,0:T(1,128)S(1)}, f32[1,1,640]{2,1,0:T(1,128)S(1)}, u32[]{:S(2)}, u32[]{:S(2)}) %collective-permute-start.15) | collective-permute-done | bytes 2592 | tf_op jit(solution)/shard_map/ppermute | solution.py:431
  47.5 0.5 %conditional.1 = (f32[512]{0:T(512)S(1)}) conditional(s32[]{:T(128)} %bitcast.5, (f32[4,1,640]{2,1,0:T(1,128)S(1)}, f32[4,1,640]{2,1,0:T(1,128)S(1)}, s32[1,512]{1,0:T(1,128)S(1)}, f32[1,1,640]{2,1,0:T(1,128)S(1)}, f32[1,1,640]{2,1,0:T(1,128)S(1)}, /*index=5*/f32[1,1,640]{2,1,0:T(1,128)S(1)}, f32[1,1,640]{2,1,0:T(1,128)S(1)}, ...), branch_computations={%region_0.1_spmd, %region_1.8_spmd} | conditional | flops 1617953280 | bytes 16846124 | solution.py:482
  47.6 0.5 finish.1
  48.0 0.0 copy-start.3
  48.1 0.6 %copy-done.3 = f32[512]{0:T(512)} copy-done((f32[512]{0:T(512)}, f32[512]{0:T(512)S(1)}, u32[]{:S(2)}) %copy-start.3) | copy-done | bytes 2072
  (18 shorter events, 0.1 us)
Async XLA Ops:
  3.6 3.2 %collective-permute-start.3 = (bf16[328,768]{1,0:T(8,128)(2,1)S(1)}, bf16[328,768]{1,0:T(8,128)(2,1)S(1)}, u32[]{:S(2)}, u32[]{:S(2)}) collective-permute-start(bf16[328,768]{1,0:T(8,128)(2,1)S(1)} %get-tuple-element.185.refs_1_), channel_id=1, source_target_pairs={{0,1},{1,0},{2,3},{3,2},{4,5},{5,4},{6,7},{7,6},{8,9},{9,8},{10,11... | collective-permute-start | bytes 1511432 | tf_op jit(solution)/shard_map/ppermute | solution.py:431
  4.2 14.7 %collective-permute-start.7 = (bf16[328,768]{1,0:T(8,128)(2,1)S(1)}, bf16[328,768]{1,0:T(8,128)(2,1)S(1)}, u32[]{:S(2)}, u32[]{:S(2)}) collective-permute-start(bf16[328,768]{1,0:T(8,128)(2,1)S(1)} %get-tuple-element.186), channel_id=1, source_target_pairs={{0,4},{1,5},{2,6},{3,7},{4,0},{5,1},{6,2},{7,3},{8,12},{9,13},{10,... | collective-permute-start | bytes 1511432 | tf_op jit(solution)/shard_map/ppermute | solution.py:431
  6.8 16.4 %collective-permute-start.4 = (bf16[328,768]{1,0:T(8,128)(2,1)S(1)}, bf16[328,768]{1,0:T(8,128)(2,1)S(1)}, u32[]{:S(2)}, u32[]{:S(2)}) collective-permute-start(bf16[328,768]{1,0:T(8,128)(2,1)S(1)} %get-tuple-element.185.refs_1_), channel_id=1, source_target_pairs={{0,2},{1,3},{2,0},{3,1},{4,6},{5,7},{6,4},{7,5},{8,10},{9,11},{10,... | collective-permute-start | bytes 1511432 | tf_op jit(solution)/shard_map/ppermute | solution.py:431
  8.6 14.6 %collective-permute-start.5 = (bf16[328,768]{1,0:T(8,128)(2,1)S(1)}, bf16[328,768]{1,0:T(8,128)(2,1)S(1)}, u32[]{:S(2)}, u32[]{:S(2)}) collective-permute-start(bf16[328,768]{1,0:T(8,128)(2,1)S(1)} %get-tuple-element.186), channel_id=1, source_target_pairs={{0,1},{1,0},{2,3},{3,2},{4,8},{5,9},{6,10},{7,11},{8,4},{9,5},{10,... | collective-permute-start | bytes 1511432 | tf_op jit(solution)/shard_map/ppermute | solution.py:431
  18.9 4.3 %collective-permute-start.10 = (bf16[328,768]{1,0:T(8,128)(2,1)S(1)}, bf16[328,768]{1,0:T(8,128)(2,1)S(1)}, u32[]{:S(2)}, u32[]{:S(2)}) collective-permute-start(bf16[328,768]{1,0:T(8,128)(2,1)S(1)} %collective-permute-done.7.refs_1_.refs_3_), channel_id=1, source_target_pairs={{0,1},{1,0},{2,3},{3,2},{4,5},{5,4},{6,7},{7,6},{8,9},{9,8},{10,11... | collective-permute-start | bytes 1511432 | tf_op jit(solution)/shard_map/ppermute | solution.py:431
  18.9 16.4 %collective-permute-start.6 = (bf16[328,768]{1,0:T(8,128)(2,1)S(1)}, bf16[328,768]{1,0:T(8,128)(2,1)S(1)}, u32[]{:S(2)}, u32[]{:S(2)}) collective-permute-start(bf16[328,768]{1,0:T(8,128)(2,1)S(1)} %get-tuple-element.185.refs_1_), channel_id=1, source_target_pairs={{0,8},{1,9},{2,10},{3,11},{4,0},{5,1},{6,2},{7,3},{8,12},{9,13},{1... | collective-permute-start | bytes 1511432 | tf_op jit(solution)/shard_map/ppermute | solution.py:431
  21.7 13.6 %collective-permute-start.8 = (bf16[328,768]{1,0:T(8,128)(2,1)S(1)}, bf16[328,768]{1,0:T(8,128)(2,1)S(1)}, u32[]{:S(2)}, u32[]{:S(2)}) collective-permute-start(bf16[328,768]{1,0:T(8,128)(2,1)S(1)} %collective-permute-done.7.refs_1_.refs_3_), channel_id=1, source_target_pairs={{0,2},{1,3},{2,0},{3,1},{4,6},{5,7},{6,4},{7,5},{8,10},{9,11},{10,... | collective-permute-start | bytes 1511432 | tf_op jit(solution)/shard_map/ppermute | solution.py:431
  23.2 1.9 %collective-permute-start.9 = (bf16[328,768]{1,0:T(8,128)(2,1)S(1)}, bf16[328,768]{1,0:T(8,128)(2,1)S(1)}, u32[]{:S(2)}, u32[]{:S(2)}) collective-permute-start(bf16[328,768]{1,0:T(8,128)(2,1)S(1)} %collective-permute-done.4.refs_1_), channel_id=1, source_target_pairs={{0,1},{1,0},{2,3},{3,2},{4,5},{5,4},{6,7},{7,6},{8,9},{9,8},{10,11... | collective-permute-start | bytes 1511432 | tf_op jit(solution)/shard_map/ppermute | solution.py:431
  35.3 1.9 %collective-permute-start.11 = (bf16[328,768]{1,0:T(8,128)(2,1)S(1)}, bf16[328,768]{1,0:T(8,128)(2,1)S(1)}, u32[]{:S(2)}, u32[]{:S(2)}) collective-permute-start(bf16[328,768]{1,0:T(8,128)(2,1)S(1)} %collective-permute-done.8.refs_3_), channel_id=1, source_target_pairs={{0,1},{1,0},{2,3},{3,2},{4,5},{5,4},{6,7},{7,6},{8,9},{9,8},{10,11... | collective-permute-start | bytes 1511432 | tf_op jit(solution)/shard_map/ppermute | solution.py:431
  35.9 11.6 %copy-start = (bf16[1024,768]{1,0:T(8,128)(2,1)S(1)}, bf16[1024,768]{1,0:T(8,128)(2,1)}, u32[]{:S(2)}) copy-start(bf16[1024,768]{1,0:T(8,128)(2,1)} %refs_3_.1) | copy-start | bytes 4718596
  36.0 11.6 %copy-start.1 = (bf16[512,1024]{1,0:T(8,128)(2,1)S(1)}, bf16[512,1024]{1,0:T(8,128)(2,1)}, u32[]{:S(2)}) copy-start(bf16[512,1024]{1,0:T(8,128)(2,1)} %refs_2_.1) | copy-start | bytes 3145732
  36.0 11.6 %copy-start.2 = (s32[512]{0:T(512)S(1)}, s32[512]{0:T(512)}, u32[]{:S(2)}) copy-start(s32[512]{0:T(512)} %param.9) | copy-start | bytes 6148
  38.4 2.5 %collective-permute-start.13 = (f32[4,1,640]{2,1,0:T(1,128)S(1)}, f32[4,1,640]{2,1,0:T(1,128)S(1)}, u32[]{:S(2)}, u32[]{:S(2)}) collective-permute-start(f32[4,1,640]{2,1,0:T(1,128)S(1)} %get-tuple-element.216), channel_id=1, source_target_pairs={{0,1},{1,0},{2,3},{3,2},{4,5},{5,4},{6,7},{7,6},{8,9},{9,8},{10,11... | collective-permute-start | bytes 30728 | tf_op jit(solution)/shard_map/ppermute | solution.py:431
  38.5 5.9 %collective-permute-start.12 = (f32[1,1,640]{2,1,0:T(1,128)S(1)}, f32[1,1,640]{2,1,0:T(1,128)S(1)}, u32[]{:S(2)}, u32[]{:S(2)}) collective-permute-start(f32[1,1,640]{2,1,0:T(1,128)S(1)} %get-tuple-element.214.refs_0_), channel_id=1, source_target_pairs={{0,8},{1,9},{2,10},{3,11},{4,12},{5,13},{6,14},{7,15},{8,0},{9,1},... | collective-permute-start | bytes 7688 | tf_op jit(solution)/shard_map/ppermute | solution.py:431
  40.9 4.8 %collective-permute-start.17 = (f32[1,1,640]{2,1,0:T(1,128)S(1)}, f32[1,1,640]{2,1,0:T(1,128)S(1)}, u32[]{:S(2)}, u32[]{:S(2)}) collective-permute-start(f32[1,1,640]{2,1,0:T(1,128)S(1)} %get-tuple-element.240), channel_id=1, source_target_pairs={{0,6},{1,7},{2,4},{3,5},{4,2},{5,3},{6,0},{7,1},{8,14},{9,15},{10,... | collective-permute-start | bytes 7688 | tf_op jit(solution)/shard_map/ppermute | solution.py:431
  42.8 3.6 %collective-permute-start.16 = (f32[1,1,640]{2,1,0:T(1,128)S(1)}, f32[1,1,640]{2,1,0:T(1,128)S(1)}, u32[]{:S(2)}, u32[]{:S(2)}) collective-permute-start(f32[1,1,640]{2,1,0:T(1,128)S(1)} %get-tuple-element.241), channel_id=1, source_target_pairs={{0,4},{1,5},{2,6},{3,7},{4,0},{5,1},{6,2},{7,3},{8,12},{9,13},{10,... | collective-permute-start | bytes 7688 | tf_op jit(solution)/shard_map/ppermute | solution.py:431
  43.9 3.6 %collective-permute-start.15 = (f32[1,1,640]{2,1,0:T(1,128)S(1)}, f32[1,1,640]{2,1,0:T(1,128)S(1)}, u32[]{:S(2)}, u32[]{:S(2)}) collective-permute-start(f32[1,1,640]{2,1,0:T(1,128)S(1)} %get-tuple-element.242), channel_id=1, source_target_pairs={{0,2},{1,3},{2,0},{3,1},{4,6},{5,7},{6,4},{7,5},{8,10},{9,11},{10,... | collective-permute-start | bytes 7688 | tf_op jit(solution)/shard_map/ppermute | solution.py:431
  44.4 3.1 %collective-permute-start.14 = (f32[1,1,640]{2,1,0:T(1,128)S(1)}, f32[1,1,640]{2,1,0:T(1,128)S(1)}, u32[]{:S(2)}, u32[]{:S(2)}) collective-permute-start(f32[1,1,640]{2,1,0:T(1,128)S(1)} %get-tuple-element.220), channel_id=1, source_target_pairs={{0,1},{1,0},{2,3},{3,2},{4,8},{5,9},{6,10},{7,11},{8,4},{9,5},{10,... | collective-permute-start | bytes 7688 | tf_op jit(solution)/shard_map/ppermute | solution.py:431
  48.0 0.6 %copy-start.3 = (f32[512]{0:T(512)}, f32[512]{0:T(512)S(1)}, u32[]{:S(2)}) copy-start(f32[512]{0:T(512)S(1)} %get-tuple-element.356) | copy-start | bytes 6148

commit v24 on v14

--- a/solution.py
+++ b/solution.py
@@ -150,7 +150,7 @@
 def prep_kernel(hot, place_ref, cl_ref, st_ref, w_ref, same_ref, other_ref, slot_ref, vectors):
     docs = st_ref.shape[0]
     rest, first, flag, lanes = layout(docs, hot)
-    tile = 128
+    tile = 256
 
     cluster = cl_ref[...]
     group = cluster // CLUS_OWN

time: 48.2 us -> 48.2 us (level)
  no operation moved by 1% of the time
where the time goes in v24:
time: 48.2 us; the launch traced here: 48 us
  waiting for transfers between devices  20.6 us (43%)
  starting transfers between devices  15.2 us (32%)
  Pallas kernels  10.7 us (22%)
  between operations  0.77 us (2%)
  local copies, waits for them, and re-layouts  0.59 us (1%)
    ppermute x15, waiting for transfers between devices, move(): return lax.ppermute(a, ('owner', 'split'), pairs)  20.6 us
    ppermute x15, starting transfers between devices, move(): return lax.ppermute(a, ('owner', 'split'), pairs)  15.2 us
    pallas_call x5, Pallas kernels, score(): pl.pallas_call(lambda *refs: score_kernel(docs, hot, names, given, made,...  6.11 us
    pallas_call x1, Pallas kernels, prep(): pl.pallas_call(lambda *refs: prep_kernel(hot, *refs), out_shape=(shape((r...  3.54 us
  transfers between devices with their start and end apart: 15, of which 6 were waited for; matrix products, arithmetic and copies ran while one was open for 0% of the time, Pallas kernels for 11%

profile of v24, /device:TPU:0, one launch (start us, length us, event | category | flops | bytes accessed | tf_op | source)
XLA Modules:
  0.0 48.0 jit_solution(8073789350466239838)
XLA Ops:
  0.0 0.1 pad_add_fusion.refs_0_
  0.1 3.5 %prep.1 = (bf16[328,768]{1,0:T(8,128)(2,1)S(1)}, bf16[328,768]{1,0:T(8,128)(2,1)S(1)}, s32[1,512]{1,0:T(1,128)S(1)}) custom-call(s32[3]{0:T(128)S(1)} %pad_add_fusion.refs_0_, s32[1,512]{1,0:T(1,128)} %bitcast.16, bf16[512,1024]{1,0:T(8,128)(2,1)} %refs_2_.1, bf16[1024,768]{1,0:T(8,128)(2,1)} %refs_3_.1), custom_call_target="tpu_custom_call" | custom-call | tf_op jit(solution)/shard_map/prep/pallas_call | solution.py:220
  3.6 0.5 %collective-permute-start.3 = (bf16[328,768]{1,0:T(8,128)(2,1)S(1)}, bf16[328,768]{1,0:T(8,128)(2,1)S(1)}, u32[]{:S(2)}, u32[]{:S(2)}) collective-permute-start(bf16[328,768]{1,0:T(8,128)(2,1)S(1)} %get-tuple-element.185.refs_1_), channel_id=1, source_target_pairs={{0,1},{1,0},{2,3},{3,2},{4,5},{5,4},{6,7},{7,6},{8,9},{9,8},{10,11... | collective-permute-start | bytes 1511432 | tf_op jit(solution)/shard_map/ppermute | solution.py:431
  4.2 2.6 %collective-permute-start.7 = (bf16[328,768]{1,0:T(8,128)(2,1)S(1)}, bf16[328,768]{1,0:T(8,128)(2,1)S(1)}, u32[]{:S(2)}, u32[]{:S(2)}) collective-permute-start(bf16[328,768]{1,0:T(8,128)(2,1)S(1)} %get-tuple-element.186), channel_id=1, source_target_pairs={{0,4},{1,5},{2,6},{3,7},{4,0},{5,1},{6,2},{7,3},{8,12},{9,13},{10,... | collective-permute-start | bytes 1511432 | tf_op jit(solution)/shard_map/ppermute | solution.py:431
  6.8 0.0 collective-permute-done.3.refs_2_
  6.8 1.7 %collective-permute-start.4 = (bf16[328,768]{1,0:T(8,128)(2,1)S(1)}, bf16[328,768]{1,0:T(8,128)(2,1)S(1)}, u32[]{:S(2)}, u32[]{:S(2)}) collective-permute-start(bf16[328,768]{1,0:T(8,128)(2,1)S(1)} %get-tuple-element.185.refs_1_), channel_id=1, source_target_pairs={{0,2},{1,3},{2,0},{3,1},{4,6},{5,7},{6,4},{7,5},{8,10},{9,11},{10,... | collective-permute-start | bytes 1511432 | tf_op jit(solution)/shard_map/ppermute | solution.py:431
  8.5 1.4 %own.1 = (f32[4,1,640]{2,1,0:T(1,128)S(1)}, f32[4,1,640]{2,1,0:T(1,128)S(1)}, f32[1,1,640]{2,1,0:T(1,128)S(1)}, f32[1,1,640]{2,1,0:T(1,128)S(1)}, bf16[768,640]{1,0:T(8,128)(2,1)S(1)}, /*index=5*/f32[8,640]{1,0:T(8,128)S(1)}) custom-call(s32[3]{0:T(128)S(1)} %pad_add_fusion.refs_0_, bf16[328,768]{1,0:T(8,128)(2,1)S(1)} %get-tuple-element.185.refs_1_, ...), custom_call_target="tpu_custom_call" | custom-call | flops 8589934592 | bytes 1024 | tf_op jit(solution)/shard_map/own/pallas_call | solution.py:364
  9.9 8.9 %collective-permute-done.7.refs_1_.refs_3_ = bf16[328,768]{1,0:T(8,128)(2,1)S(1)} collective-permute-done((bf16[328,768]{1,0:T(8,128)(2,1)S(1)}, bf16[328,768]{1,0:T(8,128)(2,1)S(1)}, u32[]{:S(2)}, u32[]{:S(2)}) %collective-permute-start.7) | collective-permute-done | bytes 503840 | tf_op jit(solution)/shard_map/ppermute | solution.py:431
  18.9 2.8 %collective-permute-start.6 = (bf16[328,768]{1,0:T(8,128)(2,1)S(1)}, bf16[328,768]{1,0:T(8,128)(2,1)S(1)}, u32[]{:S(2)}, u32[]{:S(2)}) collective-permute-start(bf16[328,768]{1,0:T(8,128)(2,1)S(1)} %get-tuple-element.185.refs_1_), channel_id=1, source_target_pairs={{0,8},{1,9},{2,10},{3,11},{4,0},{5,1},{6,2},{7,3},{8,12},{9,13},{1... | collective-permute-start | bytes 1511432 | tf_op jit(solution)/shard_map/ppermute | solution.py:431
  21.7 1.5 %collective-permute-start.8 = (bf16[328,768]{1,0:T(8,128)(2,1)S(1)}, bf16[328,768]{1,0:T(8,128)(2,1)S(1)}, u32[]{:S(2)}, u32[]{:S(2)}) collective-permute-start(bf16[328,768]{1,0:T(8,128)(2,1)S(1)} %collective-permute-done.7.refs_1_.refs_3_), channel_id=1, source_target_pairs={{0,2},{1,3},{2,0},{3,1},{4,6},{5,7},{6,4},{7,5},{8,10},{9,11},{10,... | collective-permute-start | bytes 1511432 | tf_op jit(solution)/shard_map/ppermute | solution.py:431
  23.2 1.1 %pair.1 = (f32[4,1,640]{2,1,0:T(1,128)S(1)}, f32[4,1,640]{2,1,0:T(1,128)S(1)}, f32[1,1,640]{2,1,0:T(1,128)S(1)}, f32[1,1,640]{2,1,0:T(1,128)S(1)}, bf16[768,640]{1,0:T(8,128)(2,1)S(1)}, /*index=5*/f32[8,640]{1,0:T(8,128)S(1)}) custom-call(s32[3]{0:T(128)S(1)} %pad_add_fusion.refs_0_, bf16[328,768]{1,0:T(8,128)(2,1)S(1)} %collective-permute-done.7.refs_1_.refs_3_, ...), custom_call_target="tpu_custom_call" | custom-call | flops 8589934592 | bytes 1024 | tf_op jit(solution)/shard_map/pair/pallas_call | solution.py:364
  24.3 0.8 %collective-permute-done.9.refs_2_ = bf16[328,768]{1,0:T(8,128)(2,1)S(1)} collective-permute-done((bf16[328,768]{1,0:T(8,128)(2,1)S(1)}, bf16[328,768]{1,0:T(8,128)(2,1)S(1)}, u32[]{:S(2)}, u32[]{:S(2)}) %collective-permute-start.9) | collective-permute-done | bytes 503840 | tf_op jit(solution)/shard_map/ppermute | solution.py:431
  25.1 1.8 %row.1 = (f32[4,1,640]{2,1,0:T(1,128)S(1)}, f32[4,1,640]{2,1,0:T(1,128)S(1)}, f32[1,1,640]{2,1,0:T(1,128)S(1)}, f32[1,1,640]{2,1,0:T(1,128)S(1)}, bf16[768,640]{1,0:T(8,128)(2,1)S(1)}, /*index=5*/f32[8,640]{1,0:T(8,128)S(1)}) custom-call(s32[3]{0:T(128)S(1)} %pad_add_fusion.refs_0_, bf16[328,768]{1,0:T(8,128)(2,1)S(1)} %collective-permute-done.4.refs_1_, ...), custom_call_target="tpu_custom_call" | custom-call | flops 1 | bytes 1024 | tf_op jit(solution)/shard_map/row/pallas_call | solution.py:364
  26.9 8.4 %collective-permute-done.8.refs_3_ = bf16[328,768]{1,0:T(8,128)(2,1)S(1)} collective-permute-done((bf16[328,768]{1,0:T(8,128)(2,1)S(1)}, bf16[328,768]{1,0:T(8,128)(2,1)S(1)}, u32[]{:S(2)}, u32[]{:S(2)}) %collective-permute-start.8) | collective-permute-done | bytes 503840 | tf_op jit(solution)/shard_map/ppermute | solution.py:431
  35.3 0.6 %far.1 = (f32[4,1,640]{2,1,0:T(1,128)S(1)}, f32[4,1,640]{2,1,0:T(1,128)S(1)}, f32[1,1,640]{2,1,0:T(1,128)S(1)}, f32[1,1,640]{2,1,0:T(1,128)S(1)}) custom-call(s32[3]{0:T(128)S(1)} %pad_add_fusion.refs_0_, bf16[328,768]{1,0:T(8,128)(2,1)S(1)} %collective-permute-done.6.refs_1_.refs_2_, bf16[768,640]{1,0:T(8,128)(2,1)S(1)} %get-tuple-element.192.refs_4_.refs_5_.refs_2_, ...), custom_call_target="tpu_custom_call" | custom-call | flops 1 | bytes 1024 | tf_op jit(solution)/shard_map/far/pallas_call | solution.py:364
  35.9 0.0 copy-start
  35.9 0.0 copy-start.1
  36.0 0.0 copy-start.2
  36.0 1.2 %collective-permute-done.11.refs_4_ = bf16[328,768]{1,0:T(8,128)(2,1)S(1)} collective-permute-done((bf16[328,768]{1,0:T(8,128)(2,1)S(1)}, bf16[328,768]{1,0:T(8,128)(2,1)S(1)}, u32[]{:S(2)}, u32[]{:S(2)}) %collective-permute-start.11) | collective-permute-done | bytes 503840 | tf_op jit(solution)/shard_map/ppermute | solution.py:431
  37.2 1.2 %last.1 = (f32[4,1,640]{2,1,0:T(1,128)S(1)}, f32[4,1,640]{2,1,0:T(1,128)S(1)}, f32[1,1,640]{2,1,0:T(1,128)S(1)}, f32[1,1,640]{2,1,0:T(1,128)S(1)}) custom-call(s32[3]{0:T(128)S(1)} %pad_add_fusion.refs_0_, bf16[328,768]{1,0:T(8,128)(2,1)S(1)} %collective-permute-done.5.refs_3_.refs_4_.refs_1_, bf16[328,768]{1,0:T(8,128)(2,1)S(1)} %collective-permute-done.6.refs_1_.refs_2_, ...), custom_call_target="tpu_custom_call" | custom-call | flops 1 | bytes 1024 | tf_op jit(solution)/shard_map/last/pallas_call | solution.py:364
  38.4 0.1 collective-permute-start.13
  38.5 2.3 %collective-permute-start.12 = (f32[1,1,640]{2,1,0:T(1,128)S(1)}, f32[1,1,640]{2,1,0:T(1,128)S(1)}, u32[]{:S(2)}, u32[]{:S(2)}) collective-permute-start(f32[1,1,640]{2,1,0:T(1,128)S(1)} %get-tuple-element.214.refs_0_), channel_id=1, source_target_pairs={{0,8},{1,9},{2,10},{3,11},{4,12},{5,13},{6,14},{7,15},{8,0},{9,1},... | collective-permute-start | bytes 7688 | tf_op jit(solution)/shard_map/ppermute | solution.py:431
  40.9 2.0 %collective-permute-start.17 = (f32[1,1,640]{2,1,0:T(1,128)S(1)}, f32[1,1,640]{2,1,0:T(1,128)S(1)}, u32[]{:S(2)}, u32[]{:S(2)}) collective-permute-start(f32[1,1,640]{2,1,0:T(1,128)S(1)} %get-tuple-element.240), channel_id=1, source_target_pairs={{0,6},{1,7},{2,4},{3,5},{4,2},{5,3},{6,0},{7,1},{8,14},{9,15},{10,... | collective-permute-start | bytes 7688 | tf_op jit(solution)/shard_map/ppermute | solution.py:431
  42.8 0.5 %collective-permute-start.16 = (f32[1,1,640]{2,1,0:T(1,128)S(1)}, f32[1,1,640]{2,1,0:T(1,128)S(1)}, u32[]{:S(2)}, u32[]{:S(2)}) collective-permute-start(f32[1,1,640]{2,1,0:T(1,128)S(1)} %get-tuple-element.241), channel_id=1, source_target_pairs={{0,2},{1,3},{2,0},{3,1},{4,6},{5,7},{6,4},{7,5},{8,10},{9,11},{10,... | collective-permute-start | bytes 7688 | tf_op jit(solution)/shard_map/ppermute | solution.py:431
  43.3 1.1 %collective-permute-start.15 = (f32[1,1,640]{2,1,0:T(1,128)S(1)}, f32[1,1,640]{2,1,0:T(1,128)S(1)}, u32[]{:S(2)}, u32[]{:S(2)}) collective-permute-start(f32[1,1,640]{2,1,0:T(1,128)S(1)} %get-tuple-element.242), channel_id=1, source_target_pairs={{0,4},{1,5},{2,6},{3,7},{4,0},{5,1},{6,2},{7,3},{8,12},{9,13},{10,... | collective-permute-start | bytes 7688 | tf_op jit(solution)/shard_map/ppermute | solution.py:431
  44.4 0.6 %decide.1 = s32[1]{0:T(128)} custom-call(f32[1,1,640]{2,1,0:T(1,128)S(1)} %get-tuple-element.214.refs_0_, f32[1,1,640]{2,1,0:T(1,128)S(1)} %collective-permute-done.12.refs_1_), custom_call_target="tpu_custom_call" | custom-call | tf_op jit(solution)/shard_map/decide/pallas_call | solution.py:403
  45.7 0.7 %collective-permute-done.16 = f32[1,1,640]{2,1,0:T(1,128)S(1)} collective-permute-done((f32[1,1,640]{2,1,0:T(1,128)S(1)}, f32[1,1,640]{2,1,0:T(1,128)S(1)}, u32[]{:S(2)}, u32[]{:S(2)}) %collective-permute-start.16) | collective-permute-done | bytes 2592 | tf_op jit(solution)/shard_map/ppermute | solution.py:431
  46.4 0.5 %collective-permute-done.15 = f32[1,1,640]{2,1,0:T(1,128)S(1)} collective-permute-done((f32[1,1,640]{2,1,0:T(1,128)S(1)}, f32[1,1,640]{2,1,0:T(1,128)S(1)}, u32[]{:S(2)}, u32[]{:S(2)}) %collective-permute-start.15) | collective-permute-done | bytes 2592 | tf_op jit(solution)/shard_map/ppermute | solution.py:431
  46.9 0.5 %conditional.1 = (f32[512]{0:T(512)S(1)}) conditional(s32[]{:T(128)} %bitcast.5, (f32[4,1,640]{2,1,0:T(1,128)S(1)}, f32[4,1,640]{2,1,0:T(1,128)S(1)}, s32[1,512]{1,0:T(1,128)S(1)}, f32[1,1,640]{2,1,0:T(1,128)S(1)}, f32[1,1,640]{2,1,0:T(1,128)S(1)}, /*index=5*/f32[1,1,640]{2,1,0:T(1,128)S(1)}, f32[1,1,640]{2,1,0:T(1,128)S(1)}, ...), branch_computations={%region_0.1_spmd, %region_1.8_spmd} | conditional | flops 1617953280 | bytes 16846124 | solution.py:482
  47.0 0.5 finish.1
  47.4 0.0 copy-start.3
  47.5 0.6 %copy-done.3 = f32[512]{0:T(512)} copy-done((f32[512]{0:T(512)}, f32[512]{0:T(512)S(1)}, u32[]{:S(2)}) %copy-start.3) | copy-done | bytes 2072
  (18 shorter events, 0.1 us)
Async XLA Ops:
  3.6 3.2 %collective-permute-start.3 = (bf16[328,768]{1,0:T(8,128)(2,1)S(1)}, bf16[328,768]{1,0:T(8,128)(2,1)S(1)}, u32[]{:S(2)}, u32[]{:S(2)}) collective-permute-start(bf16[328,768]{1,0:T(8,128)(2,1)S(1)} %get-tuple-element.185.refs_1_), channel_id=1, source_target_pairs={{0,1},{1,0},{2,3},{3,2},{4,5},{5,4},{6,7},{7,6},{8,9},{9,8},{10,11... | collective-permute-start | bytes 1511432 | tf_op jit(solution)/shard_map/ppermute | solution.py:431
  4.2 14.7 %collective-permute-start.7 = (bf16[328,768]{1,0:T(8,128)(2,1)S(1)}, bf16[328,768]{1,0:T(8,128)(2,1)S(1)}, u32[]{:S(2)}, u32[]{:S(2)}) collective-permute-start(bf16[328,768]{1,0:T(8,128)(2,1)S(1)} %get-tuple-element.186), channel_id=1, source_target_pairs={{0,4},{1,5},{2,6},{3,7},{4,0},{5,1},{6,2},{7,3},{8,12},{9,13},{10,... | collective-permute-start | bytes 1511432 | tf_op jit(solution)/shard_map/ppermute | solution.py:431
  6.8 16.4 %collective-permute-start.4 = (bf16[328,768]{1,0:T(8,128)(2,1)S(1)}, bf16[328,768]{1,0:T(8,128)(2,1)S(1)}, u32[]{:S(2)}, u32[]{:S(2)}) collective-permute-start(bf16[328,768]{1,0:T(8,128)(2,1)S(1)} %get-tuple-element.185.refs_1_), channel_id=1, source_target_pairs={{0,2},{1,3},{2,0},{3,1},{4,6},{5,7},{6,4},{7,5},{8,10},{9,11},{10,... | collective-permute-start | bytes 1511432 | tf_op jit(solution)/shard_map/ppermute | solution.py:431
  8.5 14.6 %collective-permute-start.5 = (bf16[328,768]{1,0:T(8,128)(2,1)S(1)}, bf16[328,768]{1,0:T(8,128)(2,1)S(1)}, u32[]{:S(2)}, u32[]{:S(2)}) collective-permute-start(bf16[328,768]{1,0:T(8,128)(2,1)S(1)} %get-tuple-element.186), channel_id=1, source_target_pairs={{0,1},{1,0},{2,3},{3,2},{4,8},{5,9},{6,10},{7,11},{8,4},{9,5},{10,... | collective-permute-start | bytes 1511432 | tf_op jit(solution)/shard_map/ppermute | solution.py:431
  18.9 4.3 %collective-permute-start.10 = (bf16[328,768]{1,0:T(8,128)(2,1)S(1)}, bf16[328,768]{1,0:T(8,128)(2,1)S(1)}, u32[]{:S(2)}, u32[]{:S(2)}) collective-permute-start(bf16[328,768]{1,0:T(8,128)(2,1)S(1)} %collective-permute-done.7.refs_1_.refs_3_), channel_id=1, source_target_pairs={{0,1},{1,0},{2,3},{3,2},{4,5},{5,4},{6,7},{7,6},{8,9},{9,8},{10,11... | collective-permute-start | bytes 1511432 | tf_op jit(solution)/shard_map/ppermute | solution.py:431
  18.9 16.4 %collective-permute-start.6 = (bf16[328,768]{1,0:T(8,128)(2,1)S(1)}, bf16[328,768]{1,0:T(8,128)(2,1)S(1)}, u32[]{:S(2)}, u32[]{:S(2)}) collective-permute-start(bf16[328,768]{1,0:T(8,128)(2,1)S(1)} %get-tuple-element.185.refs_1_), channel_id=1, source_target_pairs={{0,8},{1,9},{2,10},{3,11},{4,0},{5,1},{6,2},{7,3},{8,12},{9,13},{1... | collective-permute-start | bytes 1511432 | tf_op jit(solution)/shard_map/ppermute | solution.py:431
  21.7 13.6 %collective-permute-start.8 = (bf16[328,768]{1,0:T(8,128)(2,1)S(1)}, bf16[328,768]{1,0:T(8,128)(2,1)S(1)}, u32[]{:S(2)}, u32[]{:S(2)}) collective-permute-start(bf16[328,768]{1,0:T(8,128)(2,1)S(1)} %collective-permute-done.7.refs_1_.refs_3_), channel_id=1, source_target_pairs={{0,2},{1,3},{2,0},{3,1},{4,6},{5,7},{6,4},{7,5},{8,10},{9,11},{10,... | collective-permute-start | bytes 1511432 | tf_op jit(solution)/shard_map/ppermute | solution.py:431
  23.2 1.9 %collective-permute-start.9 = (bf16[328,768]{1,0:T(8,128)(2,1)S(1)}, bf16[328,768]{1,0:T(8,128)(2,1)S(1)}, u32[]{:S(2)}, u32[]{:S(2)}) collective-permute-start(bf16[328,768]{1,0:T(8,128)(2,1)S(1)} %collective-permute-done.4.refs_1_), channel_id=1, source_target_pairs={{0,1},{1,0},{2,3},{3,2},{4,5},{5,4},{6,7},{7,6},{8,9},{9,8},{10,11... | collective-permute-start | bytes 1511432 | tf_op jit(solution)/shard_map/ppermute | solution.py:431
  35.3 1.9 %collective-permute-start.11 = (bf16[328,768]{1,0:T(8,128)(2,1)S(1)}, bf16[328,768]{1,0:T(8,128)(2,1)S(1)}, u32[]{:S(2)}, u32[]{:S(2)}) collective-permute-start(bf16[328,768]{1,0:T(8,128)(2,1)S(1)} %collective-permute-done.8.refs_3_), channel_id=1, source_target_pairs={{0,1},{1,0},{2,3},{3,2},{4,5},{5,4},{6,7},{7,6},{8,9},{9,8},{10,11... | collective-permute-start | bytes 1511432 | tf_op jit(solution)/shard_map/ppermute | solution.py:431
  35.9 11.0 %copy-start = (bf16[1024,768]{1,0:T(8,128)(2,1)S(1)}, bf16[1024,768]{1,0:T(8,128)(2,1)}, u32[]{:S(2)}) copy-start(bf16[1024,768]{1,0:T(8,128)(2,1)} %refs_3_.1) | copy-start | bytes 4718596
  35.9 11.0 %copy-start.1 = (bf16[512,1024]{1,0:T(8,128)(2,1)S(1)}, bf16[512,1024]{1,0:T(8,128)(2,1)}, u32[]{:S(2)}) copy-start(bf16[512,1024]{1,0:T(8,128)(2,1)} %refs_2_.1) | copy-start | bytes 3145732
  36.0 11.0 %copy-start.2 = (s32[512]{0:T(512)S(1)}, s32[512]{0:T(512)}, u32[]{:S(2)}) copy-start(s32[512]{0:T(512)} %param.9) | copy-start | bytes 6148
  38.4 2.5 %collective-permute-start.13 = (f32[4,1,640]{2,1,0:T(1,128)S(1)}, f32[4,1,640]{2,1,0:T(1,128)S(1)}, u32[]{:S(2)}, u32[]{:S(2)}) collective-permute-start(f32[4,1,640]{2,1,0:T(1,128)S(1)} %get-tuple-element.216), channel_id=1, source_target_pairs={{0,1},{1,0},{2,3},{3,2},{4,5},{5,4},{6,7},{7,6},{8,9},{9,8},{10,11... | collective-permute-start | bytes 30728 | tf_op jit(solution)/shard_map/ppermute | solution.py:431
  38.5 5.9 %collective-permute-start.12 = (f32[1,1,640]{2,1,0:T(1,128)S(1)}, f32[1,1,640]{2,1,0:T(1,128)S(1)}, u32[]{:S(2)}, u32[]{:S(2)}) collective-permute-start(f32[1,1,640]{2,1,0:T(1,128)S(1)} %get-tuple-element.214.refs_0_), channel_id=1, source_target_pairs={{0,8},{1,9},{2,10},{3,11},{4,12},{5,13},{6,14},{7,15},{8,0},{9,1},... | collective-permute-start | bytes 7688 | tf_op jit(solution)/shard_map/ppermute | solution.py:431
  40.9 4.8 %collective-permute-start.17 = (f32[1,1,640]{2,1,0:T(1,128)S(1)}, f32[1,1,640]{2,1,0:T(1,128)S(1)}, u32[]{:S(2)}, u32[]{:S(2)}) collective-permute-start(f32[1,1,640]{2,1,0:T(1,128)S(1)} %get-tuple-element.240), channel_id=1, source_target_pairs={{0,6},{1,7},{2,4},{3,5},{4,2},{5,3},{6,0},{7,1},{8,14},{9,15},{10,... | collective-permute-start | bytes 7688 | tf_op jit(solution)/shard_map/ppermute | solution.py:431
  42.8 3.6 %collective-permute-start.16 = (f32[1,1,640]{2,1,0:T(1,128)S(1)}, f32[1,1,640]{2,1,0:T(1,128)S(1)}, u32[]{:S(2)}, u32[]{:S(2)}) collective-permute-start(f32[1,1,640]{2,1,0:T(1,128)S(1)} %get-tuple-element.241), channel_id=1, source_target_pairs={{0,2},{1,3},{2,0},{3,1},{4,6},{5,7},{6,4},{7,5},{8,10},{9,11},{10,... | collective-permute-start | bytes 7688 | tf_op jit(solution)/shard_map/ppermute | solution.py:431
  43.3 3.6 %collective-permute-start.15 = (f32[1,1,640]{2,1,0:T(1,128)S(1)}, f32[1,1,640]{2,1,0:T(1,128)S(1)}, u32[]{:S(2)}, u32[]{:S(2)}) collective-permute-start(f32[1,1,640]{2,1,0:T(1,128)S(1)} %get-tuple-element.242), channel_id=1, source_target_pairs={{0,4},{1,5},{2,6},{3,7},{4,0},{5,1},{6,2},{7,3},{8,12},{9,13},{10,... | collective-permute-start | bytes 7688 | tf_op jit(solution)/shard_map/ppermute | solution.py:431
  44.4 2.5 %collective-permute-start.14 = (f32[1,1,640]{2,1,0:T(1,128)S(1)}, f32[1,1,640]{2,1,0:T(1,128)S(1)}, u32[]{:S(2)}, u32[]{:S(2)}) collective-permute-start(f32[1,1,640]{2,1,0:T(1,128)S(1)} %get-tuple-element.220), channel_id=1, source_target_pairs={{0,1},{1,0},{2,3},{3,2},{4,8},{5,9},{6,10},{7,11},{8,4},{9,5},{10,... | collective-permute-start | bytes 7688 | tf_op jit(solution)/shard_map/ppermute | solution.py:431
  47.4 0.6 %copy-start.3 = (f32[512]{0:T(512)}, f32[512]{0:T(512)S(1)}, u32[]{:S(2)}) copy-start(f32[512]{0:T(512)S(1)} %get-tuple-element.356) | copy-start | bytes 6148

commit v25 on v19

--- a/solution.py
+++ b/solution.py
@@ -493,7 +493,7 @@
     own, pair, row, pair_row = (kept[k:k + 1] + from_core[k:k + 1] for k in (0, 1, 2, 3))
     home = [
         own, from_next, from_far,
-        move(pair, OUTER), move(pair_row, OUTER, row=1), move(row, STAY, row=1),
+        move(pair_row, OUTER, row=1), move(row, STAY, row=1), move(pair, OUTER),
     ]
     return lax.cond(
         decide(flag, to_far, from_far)[0] > 0,

time: 48.7 us -> 48.1 us (0.988)
  waiting for transfers between devices: 21.2 us -> 20.5 us
    ppermute x15, waiting for transfers between devices: 21.2 us -> 20.5 us  [move(): return lax.ppermute(a, ('owner', 'split'), pairs)]
  transfers between devices with their start and end apart: 15 -> 15, of which waited for: 6 -> 6; matrix products, arithmetic and copies ran while one was open for 0% -> 0% of each run, Pallas kernels for 11% -> 12%
where the time goes in v25:
time: 48.1 us; the launch traced here: 47.9 us
  waiting for transfers between devices  20.5 us (43%)
  starting transfers between devices  15.2 us (32%)
  Pallas kernels  10.7 us (22%)
  between operations  0.75 us (2%)
  local copies, waits for them, and re-layouts  0.58 us (1%)
    ppermute x15, waiting for transfers between devices, move(): return lax.ppermute(a, ('owner', 'split'), pairs)  20.5 us
    ppermute x15, starting transfers between devices, move(): return lax.ppermute(a, ('owner', 'split'), pairs)  15.2 us
    pallas_call x5, Pallas kernels, score(): pl.pallas_call(lambda *refs: score_kernel(docs, hot, names, given, made,...  6.04 us
    pallas_call x1, Pallas kernels, prep(): pl.pallas_call(lambda *refs: prep_kernel(hot, *refs), out_shape=(shape((r...  3.56 us
  transfers between devices with their start and end apart: 15, of which 6 were waited for; matrix products, arithmetic and copies ran while one was open for 0% of the time, Pallas kernels for 12%

profile of v25, /device:TPU:0, one launch (start us, length us, event | category | flops | bytes accessed | tf_op | source)
XLA Modules:
  0.0 47.9 jit_solution(7254369088783121614)
XLA Ops:
  0.0 0.1 pad_add_fusion.refs_0_
  0.1 3.6 %prep.1 = (bf16[328,768]{1,0:T(8,128)(2,1)S(1)}, bf16[328,768]{1,0:T(8,128)(2,1)S(1)}, s32[1,512]{1,0:T(1,128)S(1)}) custom-call(s32[3]{0:T(128)S(1)} %pad_add_fusion.refs_0_, s32[1,512]{1,0:T(1,128)} %bitcast.16, bf16[512,1024]{1,0:T(8,128)(2,1)} %refs_2_.1, bf16[1024,768]{1,0:T(8,128)(2,1)} %refs_3_.1), custom_call_target="tpu_custom_call" | custom-call | tf_op jit(solution)/shard_map/prep/pallas_call | solution.py:220
  3.6 0.5 %collective-permute-start.3 = (bf16[328,768]{1,0:T(8,128)(2,1)S(1)}, bf16[328,768]{1,0:T(8,128)(2,1)S(1)}, u32[]{:S(2)}, u32[]{:S(2)}) collective-permute-start(bf16[328,768]{1,0:T(8,128)(2,1)S(1)} %get-tuple-element.187.refs_1_), channel_id=1, source_target_pairs={{0,1},{1,0},{2,3},{3,2},{4,5},{5,4},{6,7},{7,6},{8,9},{9,8},{10,11... | collective-permute-start | bytes 1511432 | tf_op jit(solution)/shard_map/ppermute | solution.py:445
  4.2 2.6 %collective-permute-start.7 = (bf16[328,768]{1,0:T(8,128)(2,1)S(1)}, bf16[328,768]{1,0:T(8,128)(2,1)S(1)}, u32[]{:S(2)}, u32[]{:S(2)}) collective-permute-start(bf16[328,768]{1,0:T(8,128)(2,1)S(1)} %get-tuple-element.188), channel_id=1, source_target_pairs={{0,4},{1,5},{2,6},{3,7},{4,0},{5,1},{6,2},{7,3},{8,12},{9,13},{10,... | collective-permute-start | bytes 1511432 | tf_op jit(solution)/shard_map/ppermute | solution.py:445
  6.8 0.0 collective-permute-done.3.refs_2_
  6.8 1.7 %collective-permute-start.4 = (bf16[328,768]{1,0:T(8,128)(2,1)S(1)}, bf16[328,768]{1,0:T(8,128)(2,1)S(1)}, u32[]{:S(2)}, u32[]{:S(2)}) collective-permute-start(bf16[328,768]{1,0:T(8,128)(2,1)S(1)} %get-tuple-element.187.refs_1_), channel_id=1, source_target_pairs={{0,2},{1,3},{2,0},{3,1},{4,6},{5,7},{6,4},{7,5},{8,10},{9,11},{10,... | collective-permute-start | bytes 1511432 | tf_op jit(solution)/shard_map/ppermute | solution.py:445
  8.6 1.4 %own.1 = (f32[4,1,640]{2,1,0:T(1,128)S(1)}, f32[4,1,640]{2,1,0:T(1,128)S(1)}, f32[1,1,640]{2,1,0:T(1,128)S(1)}, f32[1,1,640]{2,1,0:T(1,128)S(1)}, bf16[768,640]{1,0:T(8,128)(2,1)S(1)}, /*index=5*/f32[8,640]{1,0:T(8,128)S(1)}) custom-call(s32[3]{0:T(128)S(1)} %pad_add_fusion.refs_0_, bf16[328,768]{1,0:T(8,128)(2,1)S(1)} %get-tuple-element.187.refs_1_, ...), custom_call_target="tpu_custom_call" | custom-call | flops 8589934592 | bytes 1024 | tf_op jit(solution)/shard_map/own/pallas_call | solution.py:375
  10.0 0.0 collective-permute-start.5
  10.0 8.9 %collective-permute-done.7.refs_1_.refs_3_ = bf16[328,768]{1,0:T(8,128)(2,1)S(1)} collective-permute-done((bf16[328,768]{1,0:T(8,128)(2,1)S(1)}, bf16[328,768]{1,0:T(8,128)(2,1)S(1)}, u32[]{:S(2)}, u32[]{:S(2)}) %collective-permute-start.7) | collective-permute-done | bytes 503840 | tf_op jit(solution)/shard_map/ppermute | solution.py:445
  18.9 0.0 collective-permute-start.10
  18.9 2.8 %collective-permute-start.6 = (bf16[328,768]{1,0:T(8,128)(2,1)S(1)}, bf16[328,768]{1,0:T(8,128)(2,1)S(1)}, u32[]{:S(2)}, u32[]{:S(2)}) collective-permute-start(bf16[328,768]{1,0:T(8,128)(2,1)S(1)} %get-tuple-element.187.refs_1_), channel_id=1, source_target_pairs={{0,8},{1,9},{2,10},{3,11},{4,0},{5,1},{6,2},{7,3},{8,12},{9,13},{1... | collective-permute-start | bytes 1511432 | tf_op jit(solution)/shard_map/ppermute | solution.py:445
  21.7 1.5 %collective-permute-start.8 = (bf16[328,768]{1,0:T(8,128)(2,1)S(1)}, bf16[328,768]{1,0:T(8,128)(2,1)S(1)}, u32[]{:S(2)}, u32[]{:S(2)}) collective-permute-start(bf16[328,768]{1,0:T(8,128)(2,1)S(1)} %collective-permute-done.7.refs_1_.refs_3_), channel_id=1, source_target_pairs={{0,2},{1,3},{2,0},{3,1},{4,6},{5,7},{6,4},{7,5},{8,10},{9,11},{10,... | collective-permute-start | bytes 1511432 | tf_op jit(solution)/shard_map/ppermute | solution.py:445
  23.2 0.0 collective-permute-done.4.refs_1_
  23.2 1.1 %pair.1 = (f32[4,1,640]{2,1,0:T(1,128)S(1)}, f32[4,1,640]{2,1,0:T(1,128)S(1)}, f32[1,1,640]{2,1,0:T(1,128)S(1)}, f32[1,1,640]{2,1,0:T(1,128)S(1)}, bf16[768,640]...) custom-call(s32[3]{0:T(128)S(1)} %pad_add_fusion.refs_0_, ...), custom_call_target="tpu_custom_call" | custom-call | flops 8589934592 | bytes 1024 | tf_op jit(solution)/shard_map/pair/pallas_call | solution.py:375
  24.3 0.8 %collective-permute-done.9.refs_2_ = bf16[328,768]{1,0:T(8,128)(2,1)S(1)} collective-permute-done((bf16[328,768]{1,0:T(8,128)(2,1)S(1)}, bf16[328,768]{1,0:T(8,128)(2,1)S(1)}, u32[]{:S(2)}, u32[]{:S(2)}) %collective-permute-start.9) | collective-permute-done | bytes 503840 | tf_op jit(solution)/shard_map/ppermute | solution.py:445
  25.1 1.8 %row.1 = (f32[4,1,640]{2,1,0:T(1,128)S(1)}, f32[4,1,640]{2,1,0:T(1,128)S(1)}, f32[1,1,640]{2,1,0:T(1,128)S(1)}, f32[1,1,640]{2,1,0:T(1,128)S(1)}, bf16[768,640]{1,0:T(8,128)(2,1)S(1)}, /*index=5*/f32[8,640]{1,0:T(8,128)S(1)}) custom-call(s32[3]{0:T(128)S(1)} %pad_add_fusion.refs_0_, bf16[328,768]{1,0:T(8,128)(2,1)S(1)} %collective-permute-done.4.refs_1_, ...), custom_call_target="tpu_custom_call" | custom-call | flops 1 | bytes 1024 | tf_op jit(solution)/shard_map/row/pallas_call | solution.py:375
  26.9 8.4 %collective-permute-done.8.refs_3_ = bf16[328,768]{1,0:T(8,128)(2,1)S(1)} collective-permute-done((bf16[328,768]{1,0:T(8,128)(2,1)S(1)}, bf16[328,768]{1,0:T(8,128)(2,1)S(1)}, u32[]{:S(2)}, u32[]{:S(2)}) %collective-permute-start.8) | collective-permute-done | bytes 503840 | tf_op jit(solution)/shard_map/ppermute | solution.py:445
  35.3 0.7 %far.1 = (f32[4,1,640]{2,1,0:T(1,128)S(1)}, f32[4,1,640]{2,1,0:T(1,128)S(1)}, f32[1,1,640]{2,1,0:T(1,128)S(1)}, f32[1,1,640]{2,1,0:T(1,128)S(1)}, f32[320,8]{1,0:T(8,128)S(1)}) custom-call(s32[3]{0:T(128)S(1)} %pad_add_fusion.refs_0_, bf16[328,768]{1,0:T(8,128)(2,1)S(1)} %collective-permute-done.6.refs_1_.refs_2_, ...), custom_call_target="tpu_custom_call" | custom-call | flops 1 | bytes 1024 | tf_op jit(solution)/shard_map/far/pallas_call | solution.py:375
  36.0 1.2 %collective-permute-done.11.refs_4_ = bf16[328,768]{1,0:T(8,128)(2,1)S(1)} collective-permute-done((bf16[328,768]{1,0:T(8,128)(2,1)S(1)}, bf16[328,768]{1,0:T(8,128)(2,1)S(1)}, u32[]{:S(2)}, u32[]{:S(2)}) %collective-permute-start.11) | collective-permute-done | bytes 503840 | tf_op jit(solution)/shard_map/ppermute | solution.py:445
  37.2 1.1 %last.1 = (f32[4,1,640]{2,1,0:T(1,128)S(1)}, f32[4,1,640]{2,1,0:T(1,128)S(1)}, f32[1,1,640]{2,1,0:T(1,128)S(1)}, f32[1,1,640]{2,1,0:T(1,128)S(1)}) custom-call(s32[3]{0:T(128)S(1)} %pad_add_fusion.refs_0_, bf16[328,768]{1,0:T(8,128)(2,1)S(1)} %collective-permute-done.5.refs_3_.refs_4_.refs_1_, bf16[328,768]{1,0:T(8,128)(2,1)S(1)} %collective-permute-done.6.refs_1_.refs_2_, ...), custom_call_target="tpu_custom_call" | custom-call | flops 1 | bytes 1024 | tf_op jit(solution)/shard_map/last/pallas_call | solution.py:375
  38.3 0.1 collective-permute-start.13
  38.5 2.3 %collective-permute-start.12 = (f32[1,1,640]{2,1,0:T(1,128)S(1)}, f32[1,1,640]{2,1,0:T(1,128)S(1)}, u32[]{:S(2)}, u32[]{:S(2)}) collective-permute-start(f32[1,1,640]{2,1,0:T(1,128)S(1)} %get-tuple-element.218.refs_0_), channel_id=1, source_target_pairs={{0,8},{1,9},{2,10},{3,11},{4,12},{5,13},{6,14},{7,15},{8,0},{9,1},... | collective-permute-start | bytes 7688 | tf_op jit(solution)/shard_map/ppermute | solution.py:445
  40.8 1.9 %collective-permute-start.15 = (f32[1,1,640]{2,1,0:T(1,128)S(1)}, f32[1,1,640]{2,1,0:T(1,128)S(1)}, u32[]{:S(2)}, u32[]{:S(2)}) collective-permute-start(f32[1,1,640]{2,1,0:T(1,128)S(1)} %get-tuple-element.246), channel_id=1, source_target_pairs={{0,6},{1,7},{2,4},{3,5},{4,2},{5,3},{6,0},{7,1},{8,14},{9,15},{10,... | collective-permute-start | bytes 7688 | tf_op jit(solution)/shard_map/ppermute | solution.py:445
  42.7 0.5 %collective-permute-start.16 = (f32[1,1,640]{2,1,0:T(1,128)S(1)}, f32[1,1,640]{2,1,0:T(1,128)S(1)}, u32[]{:S(2)}, u32[]{:S(2)}) collective-permute-start(f32[1,1,640]{2,1,0:T(1,128)S(1)} %get-tuple-element.245), channel_id=1, source_target_pairs={{0,2},{1,3},{2,0},{3,1},{4,6},{5,7},{6,4},{7,5},{8,10},{9,11},{10,... | collective-permute-start | bytes 7688 | tf_op jit(solution)/shard_map/ppermute | solution.py:445
  43.2 1.1 %collective-permute-start.17 = (f32[1,1,640]{2,1,0:T(1,128)S(1)}, f32[1,1,640]{2,1,0:T(1,128)S(1)}, u32[]{:S(2)}, u32[]{:S(2)}) collective-permute-start(f32[1,1,640]{2,1,0:T(1,128)S(1)} %get-tuple-element.244), channel_id=1, source_target_pairs={{0,4},{1,5},{2,6},{3,7},{4,0},{5,1},{6,2},{7,3},{8,12},{9,13},{10,... | collective-permute-start | bytes 7688 | tf_op jit(solution)/shard_map/ppermute | solution.py:445
  44.4 0.6 %decide.1 = s32[1]{0:T(128)} custom-call(f32[1,1,640]{2,1,0:T(1,128)S(1)} %get-tuple-element.218.refs_0_, f32[1,1,640]{2,1,0:T(1,128)S(1)} %collective-permute-done.12.refs_1_), custom_call_target="tpu_custom_call" | custom-call | tf_op jit(solution)/shard_map/decide/pallas_call | solution.py:417
  45.7 0.7 %collective-permute-done.16 = f32[1,1,640]{2,1,0:T(1,128)S(1)} collective-permute-done((f32[1,1,640]{2,1,0:T(1,128)S(1)}, f32[1,1,640]{2,1,0:T(1,128)S(1)}, u32[]{:S(2)}, u32[]{:S(2)}) %collective-permute-start.16) | collective-permute-done | bytes 2592 | tf_op jit(solution)/shard_map/ppermute | solution.py:445
  46.3 0.5 %collective-permute-done.17 = f32[1,1,640]{2,1,0:T(1,128)S(1)} collective-permute-done((f32[1,1,640]{2,1,0:T(1,128)S(1)}, f32[1,1,640]{2,1,0:T(1,128)S(1)}, u32[]{:S(2)}, u32[]{:S(2)}) %collective-permute-start.17) | collective-permute-done | bytes 2592 | tf_op jit(solution)/shard_map/ppermute | solution.py:445
  46.8 0.5 %conditional.1 = (f32[512]{0:T(512)S(1)}) conditional(s32[]{:T(128)} %bitcast.5, (f32[4,1,640]{2,1,0:T(1,128)S(1)}, f32[4,1,640]{2,1,0:T(1,128)S(1)}, s32[1,512]{1,0:T(1,128)S(1)}, f32[1,1,640]{2,1,0:T(1,128)S(1)}, f32[1,1,640]{2,1,0:T(1,128)S(1)}, /*index=5*/f32[1,1,640]{2,1,0:T(1,128)S(1)}, f32[1,1,640]{2,1,0:T(1,128)S(1)}, ...), branch_computations={%region_0.1_spmd, %region_1.8_spmd} | conditional | flops 1617953280 | bytes 16846124 | solution.py:498
  46.9 0.5 finish.1
  47.3 0.0 copy-start.3
  47.4 0.6 %copy-done.3 = f32[512]{0:T(512)} copy-done((f32[512]{0:T(512)}, f32[512]{0:T(512)S(1)}, u32[]{:S(2)}) %copy-start.3) | copy-done | bytes 2072
  (18 shorter events, 0.1 us)
Async XLA Ops:
  3.6 3.2 %collective-permute-start.3 = (bf16[328,768]{1,0:T(8,128)(2,1)S(1)}, bf16[328,768]{1,0:T(8,128)(2,1)S(1)}, u32[]{:S(2)}, u32[]{:S(2)}) collective-permute-start(bf16[328,768]{1,0:T(8,128)(2,1)S(1)} %get-tuple-element.187.refs_1_), channel_id=1, source_target_pairs={{0,1},{1,0},{2,3},{3,2},{4,5},{5,4},{6,7},{7,6},{8,9},{9,8},{10,11... | collective-permute-start | bytes 1511432 | tf_op jit(solution)/shard_map/ppermute | solution.py:445
  4.2 14.7 %collective-permute-start.7 = (bf16[328,768]{1,0:T(8,128)(2,1)S(1)}, bf16[328,768]{1,0:T(8,128)(2,1)S(1)}, u32[]{:S(2)}, u32[]{:S(2)}) collective-permute-start(bf16[328,768]{1,0:T(8,128)(2,1)S(1)} %get-tuple-element.188), channel_id=1, source_target_pairs={{0,4},{1,5},{2,6},{3,7},{4,0},{5,1},{6,2},{7,3},{8,12},{9,13},{10,... | collective-permute-start | bytes 1511432 | tf_op jit(solution)/shard_map/ppermute | solution.py:445
  6.8 16.4 %collective-permute-start.4 = (bf16[328,768]{1,0:T(8,128)(2,1)S(1)}, bf16[328,768]{1,0:T(8,128)(2,1)S(1)}, u32[]{:S(2)}, u32[]{:S(2)}) collective-permute-start(bf16[328,768]{1,0:T(8,128)(2,1)S(1)} %get-tuple-element.187.refs_1_), channel_id=1, source_target_pairs={{0,2},{1,3},{2,0},{3,1},{4,6},{5,7},{6,4},{7,5},{8,10},{9,11},{10,... | collective-permute-start | bytes 1511432 | tf_op jit(solution)/shard_map/ppermute | solution.py:445
  10.0 13.2 %collective-permute-start.5 = (bf16[328,768]{1,0:T(8,128)(2,1)S(1)}, bf16[328,768]{1,0:T(8,128)(2,1)S(1)}, u32[]{:S(2)}, u32[]{:S(2)}) collective-permute-start(bf16[328,768]{1,0:T(8,128)(2,1)S(1)} %get-tuple-element.188), channel_id=1, source_target_pairs={{0,1},{1,0},{2,3},{3,2},{4,8},{5,9},{6,10},{7,11},{8,4},{9,5},{10,... | collective-permute-start | bytes 1511432 | tf_op jit(solution)/shard_map/ppermute | solution.py:445
  18.9 4.3 %collective-permute-start.10 = (bf16[328,768]{1,0:T(8,128)(2,1)S(1)}, bf16[328,768]{1,0:T(8,128)(2,1)S(1)}, u32[]{:S(2)}, u32[]{:S(2)}) collective-permute-start(bf16[328,768]{1,0:T(8,128)(2,1)S(1)} %collective-permute-done.7.refs_1_.refs_3_), channel_id=1, source_target_pairs={{0,1},{1,0},{2,3},{3,2},{4,5},{5,4},{6,7},{7,6},{8,9},{9,8},{10,11... | collective-permute-start | bytes 1511432 | tf_op jit(solution)/shard_map/ppermute | solution.py:445
  18.9 16.4 %collective-permute-start.6 = (bf16[328,768]{1,0:T(8,128)(2,1)S(1)}, bf16[328,768]{1,0:T(8,128)(2,1)S(1)}, u32[]{:S(2)}, u32[]{:S(2)}) collective-permute-start(bf16[328,768]{1,0:T(8,128)(2,1)S(1)} %get-tuple-element.187.refs_1_), channel_id=1, source_target_pairs={{0,8},{1,9},{2,10},{3,11},{4,0},{5,1},{6,2},{7,3},{8,12},{9,13},{1... | collective-permute-start | bytes 1511432 | tf_op jit(solution)/shard_map/ppermute | solution.py:445
  21.7 13.6 %collective-permute-start.8 = (bf16[328,768]{1,0:T(8,128)(2,1)S(1)}, bf16[328,768]{1,0:T(8,128)(2,1)S(1)}, u32[]{:S(2)}, u32[]{:S(2)}) collective-permute-start(bf16[328,768]{1,0:T(8,128)(2,1)S(1)} %collective-permute-done.7.refs_1_.refs_3_), channel_id=1, source_target_pairs={{0,2},{1,3},{2,0},{3,1},{4,6},{5,7},{6,4},{7,5},{8,10},{9,11},{10,... | collective-permute-start | bytes 1511432 | tf_op jit(solution)/shard_map/ppermute | solution.py:445
  23.2 1.9 %collective-permute-start.9 = (bf16[328,768]{1,0:T(8,128)(2,1)S(1)}, bf16[328,768]{1,0:T(8,128)(2,1)S(1)}, u32[]{:S(2)}, u32[]{:S(2)}) collective-permute-start(bf16[328,768]{1,0:T(8,128)(2,1)S(1)} %collective-permute-done.4.refs_1_), channel_id=1, source_target_pairs={{0,1},{1,0},{2,3},{3,2},{4,5},{5,4},{6,7},{7,6},{8,9},{9,8},{10,11... | collective-permute-start | bytes 1511432 | tf_op jit(solution)/shard_map/ppermute | solution.py:445
  35.3 1.9 %collective-permute-start.11 = (bf16[328,768]{1,0:T(8,128)(2,1)S(1)}, bf16[328,768]{1,0:T(8,128)(2,1)S(1)}, u32[]{:S(2)}, u32[]{:S(2)}) collective-permute-start(bf16[328,768]{1,0:T(8,128)(2,1)S(1)} %collective-permute-done.8.refs_3_), channel_id=1, source_target_pairs={{0,1},{1,0},{2,3},{3,2},{4,5},{5,4},{6,7},{7,6},{8,9},{9,8},{10,11... | collective-permute-start | bytes 1511432 | tf_op jit(solution)/shard_map/ppermute | solution.py:445
  37.2 9.7 %copy-start = (bf16[1024,768]{1,0:T(8,128)(2,1)S(1)}, bf16[1024,768]{1,0:T(8,128)(2,1)}, u32[]{:S(2)}) copy-start(bf16[1024,768]{1,0:T(8,128)(2,1)} %refs_3_.1) | copy-start | bytes 4718596
  37.2 9.7 %copy-start.1 = (bf16[512,1024]{1,0:T(8,128)(2,1)S(1)}, bf16[512,1024]{1,0:T(8,128)(2,1)}, u32[]{:S(2)}) copy-start(bf16[512,1024]{1,0:T(8,128)(2,1)} %refs_2_.1) | copy-start | bytes 3145732
  37.2 9.7 %copy-start.2 = (s32[512]{0:T(512)S(1)}, s32[512]{0:T(512)}, u32[]{:S(2)}) copy-start(s32[512]{0:T(512)} %param.9) | copy-start | bytes 6148
  38.3 2.5 %collective-permute-start.13 = (f32[4,1,640]{2,1,0:T(1,128)S(1)}, f32[4,1,640]{2,1,0:T(1,128)S(1)}, u32[]{:S(2)}, u32[]{:S(2)}) collective-permute-start(f32[4,1,640]{2,1,0:T(1,128)S(1)} %get-tuple-element.220), channel_id=1, source_target_pairs={{0,1},{1,0},{2,3},{3,2},{4,5},{5,4},{6,7},{7,6},{8,9},{9,8},{10,11... | collective-permute-start | bytes 30728 | tf_op jit(solution)/shard_map/ppermute | solution.py:445
  38.5 5.9 %collective-permute-start.12 = (f32[1,1,640]{2,1,0:T(1,128)S(1)}, f32[1,1,640]{2,1,0:T(1,128)S(1)}, u32[]{:S(2)}, u32[]{:S(2)}) collective-permute-start(f32[1,1,640]{2,1,0:T(1,128)S(1)} %get-tuple-element.218.refs_0_), channel_id=1, source_target_pairs={{0,8},{1,9},{2,10},{3,11},{4,12},{5,13},{6,14},{7,15},{8,0},{9,1},... | collective-permute-start | bytes 7688 | tf_op jit(solution)/shard_map/ppermute | solution.py:445
  40.8 4.8 %collective-permute-start.15 = (f32[1,1,640]{2,1,0:T(1,128)S(1)}, f32[1,1,640]{2,1,0:T(1,128)S(1)}, u32[]{:S(2)}, u32[]{:S(2)}) collective-permute-start(f32[1,1,640]{2,1,0:T(1,128)S(1)} %get-tuple-element.246), channel_id=1, source_target_pairs={{0,6},{1,7},{2,4},{3,5},{4,2},{5,3},{6,0},{7,1},{8,14},{9,15},{10,... | collective-permute-start | bytes 7688 | tf_op jit(solution)/shard_map/ppermute | solution.py:445
  42.7 3.6 %collective-permute-start.16 = (f32[1,1,640]{2,1,0:T(1,128)S(1)}, f32[1,1,640]{2,1,0:T(1,128)S(1)}, u32[]{:S(2)}, u32[]{:S(2)}) collective-permute-start(f32[1,1,640]{2,1,0:T(1,128)S(1)} %get-tuple-element.245), channel_id=1, source_target_pairs={{0,2},{1,3},{2,0},{3,1},{4,6},{5,7},{6,4},{7,5},{8,10},{9,11},{10,... | collective-permute-start | bytes 7688 | tf_op jit(solution)/shard_map/ppermute | solution.py:445
  43.2 3.6 %collective-permute-start.17 = (f32[1,1,640]{2,1,0:T(1,128)S(1)}, f32[1,1,640]{2,1,0:T(1,128)S(1)}, u32[]{:S(2)}, u32[]{:S(2)}) collective-permute-start(f32[1,1,640]{2,1,0:T(1,128)S(1)} %get-tuple-element.244), channel_id=1, source_target_pairs={{0,4},{1,5},{2,6},{3,7},{4,0},{5,1},{6,2},{7,3},{8,12},{9,13},{10,... | collective-permute-start | bytes 7688 | tf_op jit(solution)/shard_map/ppermute | solution.py:445
  44.4 2.5 %collective-permute-start.14 = (f32[1,1,640]{2,1,0:T(1,128)S(1)}, f32[1,1,640]{2,1,0:T(1,128)S(1)}, u32[]{:S(2)}, u32[]{:S(2)}) collective-permute-start(f32[1,1,640]{2,1,0:T(1,128)S(1)} %get-tuple-element.224), channel_id=1, source_target_pairs={{0,1},{1,0},{2,3},{3,2},{4,8},{5,9},{6,10},{7,11},{8,4},{9,5},{10,... | collective-permute-start | bytes 7688 | tf_op jit(solution)/shard_map/ppermute | solution.py:445
  47.3 0.6 %copy-start.3 = (f32[512]{0:T(512)}, f32[512]{0:T(512)S(1)}, u32[]{:S(2)}) copy-start(f32[512]{0:T(512)S(1)} %get-tuple-element.360) | copy-start | bytes 6148

commit v26 on v25

--- a/solution.py
+++ b/solution.py
@@ -150,7 +150,7 @@
 def prep_kernel(hot, place_ref, cl_ref, st_ref, w_ref, same_ref, other_ref, slot_ref, vectors):
     docs = st_ref.shape[0]
     rest, first, flag, lanes = layout(docs, hot)
-    tile = 128
+    tile = 256
 
     cluster = cl_ref[...]
     group = cluster // CLUS_OWN
@@ -168,11 +168,19 @@
         norm = lax.rsqrt(jnp.sum(projected * projected, axis=1, keepdims=True) + EPS)
         vectors[rows, :] = (projected * (norm * math.sqrt(SCALE))).astype(BF16)
 
+    hot_row = in_hot.astype(F32)
+    runs = [hot_row[:, t:t + 128] for t in range(0, docs, 128)]
     ahead = (
-        lax.broadcasted_iota(jnp.int32, (docs, docs), 0) < lax.broadcasted_iota(jnp.int32, (docs, docs), 1)
+        lax.broadcasted_iota(jnp.int32, (128, 128), 0) < lax.broadcasted_iota(jnp.int32, (128, 128), 1)
     ).astype(F32).astype(BF16)
-    hot_rows = jnp.broadcast_to(in_hot.astype(F32), (8, docs)).astype(BF16)
-    rank = jnp.dot(hot_rows, ahead, preferred_element_type=F32)[0:1, :].astype(jnp.int32)
+    stack = jnp.concatenate(runs + [jnp.zeros((16 - len(runs), 128), F32)], axis=0)
+    within = jnp.dot(stack.astype(BF16), ahead, preferred_element_type=F32)
+    sizes = jnp.sum(stack, axis=1, keepdims=True)
+    ranks, before = [], jnp.zeros((1, 1), F32)
+    for k in range(len(runs)):
+        ranks.append(within[k:k + 1, :] + before)
+        before = before + sizes[k:k + 1, :]
+    rank = jnp.concatenate(ranks, axis=1).astype(jnp.int32)
     place = lax.broadcasted_iota(jnp.int32, (1, docs), 1)
     slot = jnp.where(in_hot, first + rank, place - rank)
     slot_ref[...] = slot

time: 48.1 us -> 48.1 us (level)
  no operation moved by 1% of the time
where the time goes in v26:
time: 48.1 us; the launch traced here: 47.9 us
  waiting for transfers between devices  20.5 us (43%)
  starting transfers between devices  15.2 us (32%)
  Pallas kernels  10.7 us (22%)
  between operations  0.75 us (2%)
  local copies, waits for them, and re-layouts  0.58 us (1%)
    ppermute x15, waiting for transfers between devices, move(): return lax.ppermute(a, ('owner', 'split'), pairs)  20.5 us
    ppermute x15, starting transfers between devices, move(): return lax.ppermute(a, ('owner', 'split'), pairs)  15.2 us
    pallas_call x5, Pallas kernels, score(): pl.pallas_call(lambda *refs: score_kernel(docs, hot, names, given, made,...  6.04 us
    pallas_call x1, Pallas kernels, prep(): pl.pallas_call(lambda *refs: prep_kernel(hot, *refs), out_shape=(shape((r...  3.57 us
  transfers between devices with their start and end apart: 15, of which 6 were waited for; matrix products, arithmetic and copies ran while one was open for 0% of the time, Pallas kernels for 12%

profile of v26, /device:TPU:0, one launch (start us, length us, event | category | flops | bytes accessed | tf_op | source)
XLA Modules:
  0.0 47.9 jit_solution(4089385977018321065)
XLA Ops:
  0.0 0.1 pad_add_fusion.refs_0_
  0.1 3.6 %prep.1 = (bf16[328,768]{1,0:T(8,128)(2,1)S(1)}, bf16[328,768]{1,0:T(8,128)(2,1)S(1)}, s32[1,512]{1,0:T(1,128)S(1)}) custom-call(s32[3]{0:T(128)S(1)} %pad_add_fusion.refs_0_, s32[1,512]{1,0:T(1,128)} %bitcast.16, bf16[512,1024]{1,0:T(8,128)(2,1)} %refs_2_.1, bf16[1024,768]{1,0:T(8,128)(2,1)} %refs_3_.1), custom_call_target="tpu_custom_call" | custom-call | tf_op jit(solution)/shard_map/prep/pallas_call | solution.py:228
  3.7 0.5 %collective-permute-start.3 = (bf16[328,768]{1,0:T(8,128)(2,1)S(1)}, bf16[328,768]{1,0:T(8,128)(2,1)S(1)}, u32[]{:S(2)}, u32[]{:S(2)}) collective-permute-start(bf16[328,768]{1,0:T(8,128)(2,1)S(1)} %get-tuple-element.187.refs_1_), channel_id=1, source_target_pairs={{0,1},{1,0},{2,3},{3,2},{4,5},{5,4},{6,7},{7,6},{8,9},{9,8},{10,11... | collective-permute-start | bytes 1511432 | tf_op jit(solution)/shard_map/ppermute | solution.py:453
  4.2 2.6 %collective-permute-start.7 = (bf16[328,768]{1,0:T(8,128)(2,1)S(1)}, bf16[328,768]{1,0:T(8,128)(2,1)S(1)}, u32[]{:S(2)}, u32[]{:S(2)}) collective-permute-start(bf16[328,768]{1,0:T(8,128)(2,1)S(1)} %get-tuple-element.188), channel_id=1, source_target_pairs={{0,4},{1,5},{2,6},{3,7},{4,0},{5,1},{6,2},{7,3},{8,12},{9,13},{10,... | collective-permute-start | bytes 1511432 | tf_op jit(solution)/shard_map/ppermute | solution.py:453
  6.8 0.0 collective-permute-done.3.refs_2_
  6.8 1.7 %collective-permute-start.4 = (bf16[328,768]{1,0:T(8,128)(2,1)S(1)}, bf16[328,768]{1,0:T(8,128)(2,1)S(1)}, u32[]{:S(2)}, u32[]{:S(2)}) collective-permute-start(bf16[328,768]{1,0:T(8,128)(2,1)S(1)} %get-tuple-element.187.refs_1_), channel_id=1, source_target_pairs={{0,2},{1,3},{2,0},{3,1},{4,6},{5,7},{6,4},{7,5},{8,10},{9,11},{10,... | collective-permute-start | bytes 1511432 | tf_op jit(solution)/shard_map/ppermute | solution.py:453
  8.6 1.4 %own.1 = (f32[4,1,640]{2,1,0:T(1,128)S(1)}, f32[4,1,640]{2,1,0:T(1,128)S(1)}, f32[1,1,640]{2,1,0:T(1,128)S(1)}, f32[1,1,640]{2,1,0:T(1,128)S(1)}, bf16[768,640]{1,0:T(8,128)(2,1)S(1)}, /*index=5*/f32[8,640]{1,0:T(8,128)S(1)}) custom-call(s32[3]{0:T(128)S(1)} %pad_add_fusion.refs_0_, bf16[328,768]{1,0:T(8,128)(2,1)S(1)} %get-tuple-element.187.refs_1_, ...), custom_call_target="tpu_custom_call" | custom-call | flops 8589934592 | bytes 1024 | tf_op jit(solution)/shard_map/own/pallas_call | solution.py:383
  10.0 0.0 collective-permute-start.5
  10.0 8.9 %collective-permute-done.7.refs_1_.refs_3_ = bf16[328,768]{1,0:T(8,128)(2,1)S(1)} collective-permute-done((bf16[328,768]{1,0:T(8,128)(2,1)S(1)}, bf16[328,768]{1,0:T(8,128)(2,1)S(1)}, u32[]{:S(2)}, u32[]{:S(2)}) %collective-permute-start.7) | collective-permute-done | bytes 503840 | tf_op jit(solution)/shard_map/ppermute | solution.py:453
  18.9 0.0 collective-permute-start.10
  18.9 2.8 %collective-permute-start.6 = (bf16[328,768]{1,0:T(8,128)(2,1)S(1)}, bf16[328,768]{1,0:T(8,128)(2,1)S(1)}, u32[]{:S(2)}, u32[]{:S(2)}) collective-permute-start(bf16[328,768]{1,0:T(8,128)(2,1)S(1)} %get-tuple-element.187.refs_1_), channel_id=1, source_target_pairs={{0,8},{1,9},{2,10},{3,11},{4,0},{5,1},{6,2},{7,3},{8,12},{9,13},{1... | collective-permute-start | bytes 1511432 | tf_op jit(solution)/shard_map/ppermute | solution.py:453
  21.7 1.5 %collective-permute-start.8 = (bf16[328,768]{1,0:T(8,128)(2,1)S(1)}, bf16[328,768]{1,0:T(8,128)(2,1)S(1)}, u32[]{:S(2)}, u32[]{:S(2)}) collective-permute-start(bf16[328,768]{1,0:T(8,128)(2,1)S(1)} %collective-permute-done.7.refs_1_.refs_3_), channel_id=1, source_target_pairs={{0,2},{1,3},{2,0},{3,1},{4,6},{5,7},{6,4},{7,5},{8,10},{9,11},{10,... | collective-permute-start | bytes 1511432 | tf_op jit(solution)/shard_map/ppermute | solution.py:453
  23.2 0.0 collective-permute-done.4.refs_1_
  23.2 1.1 %pair.1 = (f32[4,1,640]{2,1,0:T(1,128)S(1)}, f32[4,1,640]{2,1,0:T(1,128)S(1)}, f32[1,1,640]{2,1,0:T(1,128)S(1)}, f32[1,1,640]{2,1,0:T(1,128)S(1)}, bf16[768,640]...) custom-call(s32[3]{0:T(128)S(1)} %pad_add_fusion.refs_0_, ...), custom_call_target="tpu_custom_call" | custom-call | flops 8589934592 | bytes 1024 | tf_op jit(solution)/shard_map/pair/pallas_call | solution.py:383
  24.3 0.8 %collective-permute-done.9.refs_2_ = bf16[328,768]{1,0:T(8,128)(2,1)S(1)} collective-permute-done((bf16[328,768]{1,0:T(8,128)(2,1)S(1)}, bf16[328,768]{1,0:T(8,128)(2,1)S(1)}, u32[]{:S(2)}, u32[]{:S(2)}) %collective-permute-start.9) | collective-permute-done | bytes 503840 | tf_op jit(solution)/shard_map/ppermute | solution.py:453
  25.1 1.8 %row.1 = (f32[4,1,640]{2,1,0:T(1,128)S(1)}, f32[4,1,640]{2,1,0:T(1,128)S(1)}, f32[1,1,640]{2,1,0:T(1,128)S(1)}, f32[1,1,640]{2,1,0:T(1,128)S(1)}, bf16[768,640]{1,0:T(8,128)(2,1)S(1)}, /*index=5*/f32[8,640]{1,0:T(8,128)S(1)}) custom-call(s32[3]{0:T(128)S(1)} %pad_add_fusion.refs_0_, bf16[328,768]{1,0:T(8,128)(2,1)S(1)} %collective-permute-done.4.refs_1_, ...), custom_call_target="tpu_custom_call" | custom-call | flops 1 | bytes 1024 | tf_op jit(solution)/shard_map/row/pallas_call | solution.py:383
  26.9 8.4 %collective-permute-done.8.refs_3_ = bf16[328,768]{1,0:T(8,128)(2,1)S(1)} collective-permute-done((bf16[328,768]{1,0:T(8,128)(2,1)S(1)}, bf16[328,768]{1,0:T(8,128)(2,1)S(1)}, u32[]{:S(2)}, u32[]{:S(2)}) %collective-permute-start.8) | collective-permute-done | bytes 503840 | tf_op jit(solution)/shard_map/ppermute | solution.py:453
  35.3 0.7 %far.1 = (f32[4,1,640]{2,1,0:T(1,128)S(1)}, f32[4,1,640]{2,1,0:T(1,128)S(1)}, f32[1,1,640]{2,1,0:T(1,128)S(1)}, f32[1,1,640]{2,1,0:T(1,128)S(1)}, f32[320,8]{1,0:T(8,128)S(1)}) custom-call(s32[3]{0:T(128)S(1)} %pad_add_fusion.refs_0_, bf16[328,768]{1,0:T(8,128)(2,1)S(1)} %collective-permute-done.6.refs_1_.refs_2_, ...), custom_call_target="tpu_custom_call" | custom-call | flops 1 | bytes 1024 | tf_op jit(solution)/shard_map/far/pallas_call | solution.py:383
  36.0 1.2 %collective-permute-done.11.refs_4_ = bf16[328,768]{1,0:T(8,128)(2,1)S(1)} collective-permute-done((bf16[328,768]{1,0:T(8,128)(2,1)S(1)}, bf16[328,768]{1,0:T(8,128)(2,1)S(1)}, u32[]{:S(2)}, u32[]{:S(2)}) %collective-permute-start.11) | collective-permute-done | bytes 503840 | tf_op jit(solution)/shard_map/ppermute | solution.py:453
  37.2 1.1 %last.1 = (f32[4,1,640]{2,1,0:T(1,128)S(1)}, f32[4,1,640]{2,1,0:T(1,128)S(1)}, f32[1,1,640]{2,1,0:T(1,128)S(1)}, f32[1,1,640]{2,1,0:T(1,128)S(1)}) custom-call(s32[3]{0:T(128)S(1)} %pad_add_fusion.refs_0_, bf16[328,768]{1,0:T(8,128)(2,1)S(1)} %collective-permute-done.5.refs_3_.refs_4_.refs_1_, bf16[328,768]{1,0:T(8,128)(2,1)S(1)} %collective-permute-done.6.refs_1_.refs_2_, ...), custom_call_target="tpu_custom_call" | custom-call | flops 1 | bytes 1024 | tf_op jit(solution)/shard_map/last/pallas_call | solution.py:383
  38.3 0.1 collective-permute-start.13
  38.5 2.3 %collective-permute-start.12 = (f32[1,1,640]{2,1,0:T(1,128)S(1)}, f32[1,1,640]{2,1,0:T(1,128)S(1)}, u32[]{:S(2)}, u32[]{:S(2)}) collective-permute-start(f32[1,1,640]{2,1,0:T(1,128)S(1)} %get-tuple-element.218.refs_0_), channel_id=1, source_target_pairs={{0,8},{1,9},{2,10},{3,11},{4,12},{5,13},{6,14},{7,15},{8,0},{9,1},... | collective-permute-start | bytes 7688 | tf_op jit(solution)/shard_map/ppermute | solution.py:453
  40.8 1.9 %collective-permute-start.15 = (f32[1,1,640]{2,1,0:T(1,128)S(1)}, f32[1,1,640]{2,1,0:T(1,128)S(1)}, u32[]{:S(2)}, u32[]{:S(2)}) collective-permute-start(f32[1,1,640]{2,1,0:T(1,128)S(1)} %get-tuple-element.246), channel_id=1, source_target_pairs={{0,6},{1,7},{2,4},{3,5},{4,2},{5,3},{6,0},{7,1},{8,14},{9,15},{10,... | collective-permute-start | bytes 7688 | tf_op jit(solution)/shard_map/ppermute | solution.py:453
  42.7 0.5 %collective-permute-start.16 = (f32[1,1,640]{2,1,0:T(1,128)S(1)}, f32[1,1,640]{2,1,0:T(1,128)S(1)}, u32[]{:S(2)}, u32[]{:S(2)}) collective-permute-start(f32[1,1,640]{2,1,0:T(1,128)S(1)} %get-tuple-element.245), channel_id=1, source_target_pairs={{0,2},{1,3},{2,0},{3,1},{4,6},{5,7},{6,4},{7,5},{8,10},{9,11},{10,... | collective-permute-start | bytes 7688 | tf_op jit(solution)/shard_map/ppermute | solution.py:453
  43.2 1.1 %collective-permute-start.17 = (f32[1,1,640]{2,1,0:T(1,128)S(1)}, f32[1,1,640]{2,1,0:T(1,128)S(1)}, u32[]{:S(2)}, u32[]{:S(2)}) collective-permute-start(f32[1,1,640]{2,1,0:T(1,128)S(1)} %get-tuple-element.244), channel_id=1, source_target_pairs={{0,4},{1,5},{2,6},{3,7},{4,0},{5,1},{6,2},{7,3},{8,12},{9,13},{10,... | collective-permute-start | bytes 7688 | tf_op jit(solution)/shard_map/ppermute | solution.py:453
  44.4 0.6 %decide.1 = s32[1]{0:T(128)} custom-call(f32[1,1,640]{2,1,0:T(1,128)S(1)} %get-tuple-element.218.refs_0_, f32[1,1,640]{2,1,0:T(1,128)S(1)} %collective-permute-done.12.refs_1_), custom_call_target="tpu_custom_call" | custom-call | tf_op jit(solution)/shard_map/decide/pallas_call | solution.py:425
  45.7 0.7 %collective-permute-done.16 = f32[1,1,640]{2,1,0:T(1,128)S(1)} collective-permute-done((f32[1,1,640]{2,1,0:T(1,128)S(1)}, f32[1,1,640]{2,1,0:T(1,128)S(1)}, u32[]{:S(2)}, u32[]{:S(2)}) %collective-permute-start.16) | collective-permute-done | bytes 2592 | tf_op jit(solution)/shard_map/ppermute | solution.py:453
  46.3 0.5 %collective-permute-done.17 = f32[1,1,640]{2,1,0:T(1,128)S(1)} collective-permute-done((f32[1,1,640]{2,1,0:T(1,128)S(1)}, f32[1,1,640]{2,1,0:T(1,128)S(1)}, u32[]{:S(2)}, u32[]{:S(2)}) %collective-permute-start.17) | collective-permute-done | bytes 2592 | tf_op jit(solution)/shard_map/ppermute | solution.py:453
  46.8 0.5 %conditional.1 = (f32[512]{0:T(512)S(1)}) conditional(s32[]{:T(128)} %bitcast.5, (f32[4,1,640]{2,1,0:T(1,128)S(1)}, f32[4,1,640]{2,1,0:T(1,128)S(1)}, s32[1,512]{1,0:T(1,128)S(1)}, f32[1,1,640]{2,1,0:T(1,128)S(1)}, f32[1,1,640]{2,1,0:T(1,128)S(1)}, /*index=5*/f32[1,1,640]{2,1,0:T(1,128)S(1)}, f32[1,1,640]{2,1,0:T(1,128)S(1)}, ...), branch_computations={%region_0.1_spmd, %region_1.8_spmd} | conditional | flops 1617953280 | bytes 16846124 | solution.py:506
  46.9 0.5 finish.1
  47.4 0.0 copy-start.3
  47.4 0.6 %copy-done.3 = f32[512]{0:T(512)} copy-done((f32[512]{0:T(512)}, f32[512]{0:T(512)S(1)}, u32[]{:S(2)}) %copy-start.3) | copy-done | bytes 2072
  (18 shorter events, 0.1 us)
Async XLA Ops:
  3.7 3.2 %collective-permute-start.3 = (bf16[328,768]{1,0:T(8,128)(2,1)S(1)}, bf16[328,768]{1,0:T(8,128)(2,1)S(1)}, u32[]{:S(2)}, u32[]{:S(2)}) collective-permute-start(bf16[328,768]{1,0:T(8,128)(2,1)S(1)} %get-tuple-element.187.refs_1_), channel_id=1, source_target_pairs={{0,1},{1,0},{2,3},{3,2},{4,5},{5,4},{6,7},{7,6},{8,9},{9,8},{10,11... | collective-permute-start | bytes 1511432 | tf_op jit(solution)/shard_map/ppermute | solution.py:453
  4.2 14.7 %collective-permute-start.7 = (bf16[328,768]{1,0:T(8,128)(2,1)S(1)}, bf16[328,768]{1,0:T(8,128)(2,1)S(1)}, u32[]{:S(2)}, u32[]{:S(2)}) collective-permute-start(bf16[328,768]{1,0:T(8,128)(2,1)S(1)} %get-tuple-element.188), channel_id=1, source_target_pairs={{0,4},{1,5},{2,6},{3,7},{4,0},{5,1},{6,2},{7,3},{8,12},{9,13},{10,... | collective-permute-start | bytes 1511432 | tf_op jit(solution)/shard_map/ppermute | solution.py:453
  6.8 16.4 %collective-permute-start.4 = (bf16[328,768]{1,0:T(8,128)(2,1)S(1)}, bf16[328,768]{1,0:T(8,128)(2,1)S(1)}, u32[]{:S(2)}, u32[]{:S(2)}) collective-permute-start(bf16[328,768]{1,0:T(8,128)(2,1)S(1)} %get-tuple-element.187.refs_1_), channel_id=1, source_target_pairs={{0,2},{1,3},{2,0},{3,1},{4,6},{5,7},{6,4},{7,5},{8,10},{9,11},{10,... | collective-permute-start | bytes 1511432 | tf_op jit(solution)/shard_map/ppermute | solution.py:453
  10.0 13.2 %collective-permute-start.5 = (bf16[328,768]{1,0:T(8,128)(2,1)S(1)}, bf16[328,768]{1,0:T(8,128)(2,1)S(1)}, u32[]{:S(2)}, u32[]{:S(2)}) collective-permute-start(bf16[328,768]{1,0:T(8,128)(2,1)S(1)} %get-tuple-element.188), channel_id=1, source_target_pairs={{0,1},{1,0},{2,3},{3,2},{4,8},{5,9},{6,10},{7,11},{8,4},{9,5},{10,... | collective-permute-start | bytes 1511432 | tf_op jit(solution)/shard_map/ppermute | solution.py:453
  18.9 4.3 %collective-permute-start.10 = (bf16[328,768]{1,0:T(8,128)(2,1)S(1)}, bf16[328,768]{1,0:T(8,128)(2,1)S(1)}, u32[]{:S(2)}, u32[]{:S(2)}) collective-permute-start(bf16[328,768]{1,0:T(8,128)(2,1)S(1)} %collective-permute-done.7.refs_1_.refs_3_), channel_id=1, source_target_pairs={{0,1},{1,0},{2,3},{3,2},{4,5},{5,4},{6,7},{7,6},{8,9},{9,8},{10,11... | collective-permute-start | bytes 1511432 | tf_op jit(solution)/shard_map/ppermute | solution.py:453
  18.9 16.4 %collective-permute-start.6 = (bf16[328,768]{1,0:T(8,128)(2,1)S(1)}, bf16[328,768]{1,0:T(8,128)(2,1)S(1)}, u32[]{:S(2)}, u32[]{:S(2)}) collective-permute-start(bf16[328,768]{1,0:T(8,128)(2,1)S(1)} %get-tuple-element.187.refs_1_), channel_id=1, source_target_pairs={{0,8},{1,9},{2,10},{3,11},{4,0},{5,1},{6,2},{7,3},{8,12},{9,13},{1... | collective-permute-start | bytes 1511432 | tf_op jit(solution)/shard_map/ppermute | solution.py:453
  21.7 13.6 %collective-permute-start.8 = (bf16[328,768]{1,0:T(8,128)(2,1)S(1)}, bf16[328,768]{1,0:T(8,128)(2,1)S(1)}, u32[]{:S(2)}, u32[]{:S(2)}) collective-permute-start(bf16[328,768]{1,0:T(8,128)(2,1)S(1)} %collective-permute-done.7.refs_1_.refs_3_), channel_id=1, source_target_pairs={{0,2},{1,3},{2,0},{3,1},{4,6},{5,7},{6,4},{7,5},{8,10},{9,11},{10,... | collective-permute-start | bytes 1511432 | tf_op jit(solution)/shard_map/ppermute | solution.py:453
  23.2 1.9 %collective-permute-start.9 = (bf16[328,768]{1,0:T(8,128)(2,1)S(1)}, bf16[328,768]{1,0:T(8,128)(2,1)S(1)}, u32[]{:S(2)}, u32[]{:S(2)}) collective-permute-start(bf16[328,768]{1,0:T(8,128)(2,1)S(1)} %collective-permute-done.4.refs_1_), channel_id=1, source_target_pairs={{0,1},{1,0},{2,3},{3,2},{4,5},{5,4},{6,7},{7,6},{8,9},{9,8},{10,11... | collective-permute-start | bytes 1511432 | tf_op jit(solution)/shard_map/ppermute | solution.py:453
  35.3 1.9 %collective-permute-start.11 = (bf16[328,768]{1,0:T(8,128)(2,1)S(1)}, bf16[328,768]{1,0:T(8,128)(2,1)S(1)}, u32[]{:S(2)}, u32[]{:S(2)}) collective-permute-start(bf16[328,768]{1,0:T(8,128)(2,1)S(1)} %collective-permute-done.8.refs_3_), channel_id=1, source_target_pairs={{0,1},{1,0},{2,3},{3,2},{4,5},{5,4},{6,7},{7,6},{8,9},{9,8},{10,11... | collective-permute-start | bytes 1511432 | tf_op jit(solution)/shard_map/ppermute | solution.py:453
  37.2 9.7 %copy-start = (bf16[1024,768]{1,0:T(8,128)(2,1)S(1)}, bf16[1024,768]{1,0:T(8,128)(2,1)}, u32[]{:S(2)}) copy-start(bf16[1024,768]{1,0:T(8,128)(2,1)} %refs_3_.1) | copy-start | bytes 4718596
  37.2 9.7 %copy-start.1 = (bf16[512,1024]{1,0:T(8,128)(2,1)S(1)}, bf16[512,1024]{1,0:T(8,128)(2,1)}, u32[]{:S(2)}) copy-start(bf16[512,1024]{1,0:T(8,128)(2,1)} %refs_2_.1) | copy-start | bytes 3145732
  37.2 9.7 %copy-start.2 = (s32[512]{0:T(512)S(1)}, s32[512]{0:T(512)}, u32[]{:S(2)}) copy-start(s32[512]{0:T(512)} %param.9) | copy-start | bytes 6148
  38.3 2.5 %collective-permute-start.13 = (f32[4,1,640]{2,1,0:T(1,128)S(1)}, f32[4,1,640]{2,1,0:T(1,128)S(1)}, u32[]{:S(2)}, u32[]{:S(2)}) collective-permute-start(f32[4,1,640]{2,1,0:T(1,128)S(1)} %get-tuple-element.220), channel_id=1, source_target_pairs={{0,1},{1,0},{2,3},{3,2},{4,5},{5,4},{6,7},{7,6},{8,9},{9,8},{10,11... | collective-permute-start | bytes 30728 | tf_op jit(solution)/shard_map/ppermute | solution.py:453
  38.5 5.9 %collective-permute-start.12 = (f32[1,1,640]{2,1,0:T(1,128)S(1)}, f32[1,1,640]{2,1,0:T(1,128)S(1)}, u32[]{:S(2)}, u32[]{:S(2)}) collective-permute-start(f32[1,1,640]{2,1,0:T(1,128)S(1)} %get-tuple-element.218.refs_0_), channel_id=1, source_target_pairs={{0,8},{1,9},{2,10},{3,11},{4,12},{5,13},{6,14},{7,15},{8,0},{9,1},... | collective-permute-start | bytes 7688 | tf_op jit(solution)/shard_map/ppermute | solution.py:453
  40.8 4.8 %collective-permute-start.15 = (f32[1,1,640]{2,1,0:T(1,128)S(1)}, f32[1,1,640]{2,1,0:T(1,128)S(1)}, u32[]{:S(2)}, u32[]{:S(2)}) collective-permute-start(f32[1,1,640]{2,1,0:T(1,128)S(1)} %get-tuple-element.246), channel_id=1, source_target_pairs={{0,6},{1,7},{2,4},{3,5},{4,2},{5,3},{6,0},{7,1},{8,14},{9,15},{10,... | collective-permute-start | bytes 7688 | tf_op jit(solution)/shard_map/ppermute | solution.py:453
  42.7 3.6 %collective-permute-start.16 = (f32[1,1,640]{2,1,0:T(1,128)S(1)}, f32[1,1,640]{2,1,0:T(1,128)S(1)}, u32[]{:S(2)}, u32[]{:S(2)}) collective-permute-start(f32[1,1,640]{2,1,0:T(1,128)S(1)} %get-tuple-element.245), channel_id=1, source_target_pairs={{0,2},{1,3},{2,0},{3,1},{4,6},{5,7},{6,4},{7,5},{8,10},{9,11},{10,... | collective-permute-start | bytes 7688 | tf_op jit(solution)/shard_map/ppermute | solution.py:453
  43.2 3.6 %collective-permute-start.17 = (f32[1,1,640]{2,1,0:T(1,128)S(1)}, f32[1,1,640]{2,1,0:T(1,128)S(1)}, u32[]{:S(2)}, u32[]{:S(2)}) collective-permute-start(f32[1,1,640]{2,1,0:T(1,128)S(1)} %get-tuple-element.244), channel_id=1, source_target_pairs={{0,4},{1,5},{2,6},{3,7},{4,0},{5,1},{6,2},{7,3},{8,12},{9,13},{10,... | collective-permute-start | bytes 7688 | tf_op jit(solution)/shard_map/ppermute | solution.py:453
  44.4 2.5 %collective-permute-start.14 = (f32[1,1,640]{2,1,0:T(1,128)S(1)}, f32[1,1,640]{2,1,0:T(1,128)S(1)}, u32[]{:S(2)}, u32[]{:S(2)}) collective-permute-start(f32[1,1,640]{2,1,0:T(1,128)S(1)} %get-tuple-element.224), channel_id=1, source_target_pairs={{0,1},{1,0},{2,3},{3,2},{4,8},{5,9},{6,10},{7,11},{8,4},{9,5},{10,... | collective-permute-start | bytes 7688 | tf_op jit(solution)/shard_map/ppermute | solution.py:453
  47.4 0.6 %copy-start.3 = (f32[512]{0:T(512)}, f32[512]{0:T(512)S(1)}, u32[]{:S(2)}) copy-start(f32[512]{0:T(512)S(1)} %get-tuple-element.360) | copy-start | bytes 6148
